TPU v7x, 32 devices: a whole 2x2x4 slice. The times are simulated.
32 devices in a mesh: clips: 2 (over x), tm: 8 (over z, y), cols: 2 (over core).
Axes of the slice: x: 2, y: 2, z: 4, core: 2. Of those that a mesh axis runs over, the one named last changes fastest.
Arguments:
- video: bfloat16 [64, 32, 32, 512], P(('clips', 'tm'), None, 'cols'), parts along dimension 0, may hold values from -6 to 6
- w_time: bfloat16 [3, 512, 512], replicated, may hold values from -0.15625 to 0.15625
- b_time: float32 [512], replicated, may hold values from -3 to 3
- w_down: bfloat16 [3, 512, 512], replicated, may hold values from -0.15625 to 0.15625
- b_down: float32 [512], replicated, may hold values from -3 to 3
- w_space: bfloat16 [9, 512, 512], replicated, may hold values from -0.09375 to 0.09375
- b_space: float32 [512], replicated, may hold values from -3 to 3
- gain: float32 [512], replicated, may hold values from 0.1 to 1.9
- w_query: bfloat16 [512, 512], replicated, may hold values from -30 to 30
- w_key: bfloat16 [512, 512], replicated, may hold values from -0.25 to 0.25
- w_value: bfloat16 [512, 512], replicated, may hold values from -0.25 to 0.25
- w_out: bfloat16 [512, 512], replicated, may hold values from -0.25 to 0.25
Outputs:
- encoded: bfloat16 [32, 32, 32, 512], P(('clips', 'tm'), None, 'cols'), parts along dimension 0
There are 2 independent parts, one for each index of `clips`. A program takes and returns all parts, laid end to end along the dimension named above; an argument that names none is the same for every part. Nothing has to cross between parts.
All inputs are finite; a program needn't handle non-finite values.
Results may differ from a plain program's by a relative error of at most 0.019.
The roundings to bfloat16 on the way count: a program that leaves them out, or rounds other values in their place, can miss the bound.
Values may be sent and summed in bfloat16 or wider, within the bound.
No kernel may reach another device: no remote copies, remote signals or barrier semaphores. Data moves between devices by JAX's collectives and lax.ppermute only.
A program may use at most 64 MiB of HBM per device.

v0:
```python
from functools import partial

import jax
import jax.numpy as jnp
from jax import lax
from jax.sharding import PartitionSpec as P

epsilon = 1e-06


def passed_along(value, axis, steps):
    count = lax.axis_size(axis)
    first, last = (max(0, -steps), min(count, count - steps))
    return lax.ppermute(value, axis, [(source, source + steps) for source in range(first, last)])


def padded(x, sides, width):
    for axis, dim in sides:
        devices, length = (lax.axis_size(axis), x.shape[dim])
        up = [(i, (i + 1) % devices) for i in range(devices - 1)]
        down = [(j, i) for i, j in up]
        last = lax.slice_in_dim(x, length - width, length, axis=dim)
        first = lax.slice_in_dim(x, 0, width, axis=dim)
        before = lax.ppermute(last, axis, up)
        after = lax.ppermute(first, axis, down)
        x = jnp.concatenate([before, x, after], axis=dim)
    return x


def attend(sequence, gain, w_query, w_key, w_value, w_out):
    frames, pixels, channels = sequence.shape
    wide = sequence.astype(jnp.float32)
    scale = lax.rsqrt(jnp.mean(wide * wide, axis=-1, keepdims=True) + epsilon)
    normed = (wide * scale * gain).astype(jnp.bfloat16).reshape(-1, channels)
    query = (
        jnp.dot(normed, w_query, preferred_element_type=jnp.float32)
        .astype(jnp.bfloat16)
        .reshape(frames, pixels, channels)
    )
    key = (
        jnp.dot(normed, w_key, preferred_element_type=jnp.float32)
        .astype(jnp.bfloat16)
        .reshape(frames, pixels, channels)
    )
    value = (
        jnp.dot(normed, w_value, preferred_element_type=jnp.float32)
        .astype(jnp.bfloat16)
        .reshape(frames, pixels, channels)
    )
    scores = jnp.einsum(
        "spc,tpc->pst", query, key, preferred_element_type=jnp.float32
    ) * channels ** (-0.5)
    steps = jnp.arange(frames)
    allowed = steps[None, :] <= steps[:, None]
    scores = jnp.where(allowed[None], scores, -1e30)
    largest = jnp.max(scores, axis=-1, keepdims=True)
    probs = jnp.exp(scores - largest)
    probs = (probs / jnp.sum(probs, axis=-1, keepdims=True)).astype(jnp.bfloat16)
    context = jnp.einsum("pst,tpc->spc", probs, value, preferred_element_type=jnp.float32).astype(
        jnp.bfloat16
    )
    mixed = jnp.dot(
        context.reshape(-1, channels), w_out, preferred_element_type=jnp.float32
    ).reshape(frames, pixels, channels)
    return (wide + mixed).astype(jnp.bfloat16)


def attend_group(block, attention):
    frames, single, pixels, channels = block.shape
    result = attention(block.reshape(frames, single * pixels, channels))
    return result.reshape(frames, single, pixels, channels)


def temporal(extended, weights, bias, first, count):
    _, height, strip, channels = extended.shape
    summed = jnp.zeros((count * height * strip, channels), jnp.float32) + bias
    for offset in range(3):
        window = extended[first - offset : first - offset + count]
        summed = summed + jnp.dot(
            window.reshape(-1, channels), weights[offset], preferred_element_type=jnp.float32
        )
    return summed.reshape(count, height, strip, channels)


def per_device(
    video, w_time, b_time, w_down, b_down, w_space, b_space, gain, w_query, w_key, w_value, w_out
):
    frames, height, strip, channels = video.shape
    before = passed_along(video[frames - 2 :], "tm", 1)
    extended = jnp.concatenate([before, video], 0)
    summed = temporal(extended, w_time, b_time, 2, frames)
    lifted = (video.astype(jnp.float32) + jax.nn.silu(summed)).astype(jnp.bfloat16)
    carried = passed_along(lifted[frames - 1 :], "tm", 1)
    lifted_ext = jnp.concatenate([carried, lifted], 0)
    halves = frames // 2
    taps = [lifted_ext[2 : frames + 1 : 2], lifted_ext[1:frames:2], lifted_ext[0 : frames - 1 : 2]]
    summed = jnp.zeros((halves * height * strip, channels), jnp.float32) + b_down
    for offset in range(3):
        summed = summed + jnp.dot(
            taps[offset].reshape(-1, channels), w_down[offset], preferred_element_type=jnp.float32
        )
    reduced = summed.reshape(halves, height, strip, channels).astype(jnp.bfloat16)
    framed = padded(reduced, (("cols", 2),), 1)
    framed = jnp.pad(framed, ((0, 0), (1, 1), (0, 0), (0, 0)))
    summed = jnp.zeros((halves * height * strip, channels), jnp.float32) + b_space
    for row_tap in range(3):
        for col_tap in range(3):
            window = framed[:, row_tap : row_tap + height, col_tap : col_tap + strip]
            summed = summed + jnp.dot(
                window.reshape(-1, channels),
                w_space[3 * row_tap + col_tap],
                preferred_element_type=jnp.float32,
            )
    spatial = (
        reduced.astype(jnp.float32) + jax.nn.silu(summed.reshape(halves, height, strip, channels))
    ).astype(jnp.bfloat16)
    flattened = spatial.reshape(halves, height * strip, channels)
    attention = partial(
        attend, gain=gain, w_query=w_query, w_key=w_key, w_value=w_value, w_out=w_out
    )
    owners = lax.axis_size("tm")
    grouped = flattened.reshape(halves, owners, height * strip // owners, channels)
    worker = partial(attend_group, attention=attention)
    attended_four = worker(lax.all_to_all(grouped, "tm", split_axis=1, concat_axis=0, tiled=True))
    attended = attended_four.reshape(halves * owners, height * strip // owners, channels)
    returned = lax.all_to_all(attended, "tm", split_axis=0, concat_axis=1, tiled=True)
    return returned.reshape(halves, height, strip, channels)


def solution(mesh):
    return jax.shard_map(
        per_device,
        mesh=mesh,
        in_specs=(
            P(("clips", "tm"), None, "cols", None),
            P(),
            P(),
            P(),
            P(),
            P(),
            P(),
            P(),
            P(),
            P(),
            P(),
            P(),
        ),
        out_specs=P(("clips", "tm"), None, "cols", None),
        check_vma=False,
    )
```

profile of v0, /device:TPU:0, one launch (start us, length us, event | category | flops | bytes accessed | tf_op | source)
XLA Modules:
  0.0 141.1 jit_solution(7019561361036604672)
XLA Ops:
  0.0 1.4 %slice.103 = bf16[2,32,16,512]{3,2,1,0:T(8,128)(2,1)S(1)} slice(bf16[4,32,16,512]{3,2,1,0:T(8,128)(2,1)} %param.12), slice={[2:4], [0:32], [0:16], [0:512]} | slice | bytes 2097152 | tf_op jit(solution)/shard_map/slice | solution.py:89
  1.5 4.9 %collective-permute-start = (bf16[2,32,16,512]{3,2,1,0:T(8,128)(2,1)S(1)}, bf16[2,32,16,512]{3,2,1,0:T(8,128)(2,1)S(1)}, u32[]{:S(2)}, u32[]{:S(2)}) collective-permute-start(bf16[2,32,16,512]{3,2,1,0:T(8,128)(2,1)S(1)} %slice.103), channel_id=1, source_target_pairs={{0,2},{2,4},{4,6},{6,8},{8,10},{10,12},{12,14},{1,3},{3,5},{5,7},{... | collective-permute-start | bytes 3145736 | tf_op jit(solution)/shard_map/ppermute | solution.py:14
  6.4 2.3 %fusion.46 = f32[2048,512]{1,0:T(8,128)S(1)} fusion(bf16[2048,512]{1,0:T(8,128)(2,1)S(1)} %bitcast.117, bf16[3,512,512]{2,1,0:T(8,128)(2,1)} %param.13), kind=kOutput, calls=%fused_computation.63 | convolution fusion | flops 1073741824 | bytes 6815744 | tf_op jit(solution)/shard_map/dot_general | solution.py:79
  8.7 20.0 %collective-permute-done = bf16[2,32,16,512]{3,2,1,0:T(8,128)(2,1)S(1)} collective-permute-done((bf16[2,32,16,512]{3,2,1,0:T(8,128)(2,1)S(1)}, bf16[2,32,16,512]{3,2,1,0:T(8,128)(2,1)S(1)}, u32[]{:S(2)}, u32[]{:S(2)}) %collective-permute-start) | collective-permute-done | bytes 1048608 | tf_op jit(solution)/shard_map/ppermute | solution.py:14
  29.6 0.8 copy-done.2
  30.4 1.3 fusion.44
  31.7 1.4 %add_add_fusion = f32[2048,512]{1,0:T(8,128)S(1)} fusion(f32[2048,512]{1,0:T(8,128)S(1)} %fusion.44, f32[2048,512]{1,0:T(8,128)S(1)} %fusion.46, bf16[2048,512]{1,0:T(8,128)(2,1)S(1)} %bitcast.124, f32[512]{0:T(512)S(1)} %copy-done.5, bf16[3,512,512]{2,1,0:T(8,128)(2,1)S(1)} %copy-done.2), kind=kOutput, calls=%fused_computation.4 | convolution fusion | flops 1076887552 | bytes 15206400 | tf_op jit(solution)/shard_map/dot_general | solution.py:79
  33.1 1.2 add_convert_fusion
  34.6 4.5 %collective-permute-start.1 = (bf16[1,32,16,512]{3,2,1,0:T(8,128)(2,1)S(1)}, bf16[1,32,16,512]{3,2,1,0:T(8,128)(2,1)S(1)}, u32[]{:S(2)}, u32[]{:S(2)}) collective-permute-start(bf16[1,32,16,512]{3,2,1,0:T(8,128)(2,1)S(1)} %slice.136), channel_id=1, source_target_pairs={{0,2},{2,4},{4,6},{6,8},{8,10},{10,12},{12,14},{1,3},{3,5},{5,7},{... | collective-permute-start | bytes 1572872 | tf_op jit(solution)/shard_map/ppermute | solution.py:14
  39.2 0.7 fusion.39
  40.6 8.8 %collective-permute-done.1 = bf16[1,32,16,512]{3,2,1,0:T(8,128)(2,1)S(1)} collective-permute-done((bf16[1,32,16,512]{3,2,1,0:T(8,128)(2,1)S(1)}, bf16[1,32,16,512]{3,2,1,0:T(8,128)(2,1)S(1)}, u32[]{:S(2)}, u32[]{:S(2)}) %collective-permute-start.1) | collective-permute-done | bytes 524320 | tf_op jit(solution)/shard_map/ppermute | solution.py:14
  50.3 0.8 add_convert_fusion.1
  51.3 1.3 collective-permute-start.2
  52.6 1.5 %collective-permute-start.3 = (bf16[2,32,1,512]{3,2,1,0:T(2,128)(2,1)S(1)}, bf16[2,32,1,512]{3,2,1,0:T(2,128)(2,1)S(1)}, u32[]{:S(2)}, u32[]{:S(2)}) collective-permute-start(bf16[2,32,1,512]{3,2,1,0:T(2,128)(2,1)S(1)} %get-tuple-element.18), channel_id=1, source_target_pairs={{1,0},{3,2},{5,4},{7,6},{9,8},{11,10},{13,12},{15,14},{17,16},{19,... | collective-permute-start | bytes 196616 | tf_op jit(solution)/shard_map/ppermute | solution.py:25
  54.9 1.0 collective-permute-done.3
  55.9 1.1 fusion.10
  56.9 1.0 fusion.67
  59.4 0.7 fusion.32
  60.1 0.7 fusion.34
  60.8 0.7 fusion.36
  61.5 1.0 pad_maximum_fusion.2
  63.9 1.6 %add_add_fusion.1 = f32[1024,512]{1,0:T(8,128)S(1)} fusion(f32[1024,512]{1,0:T(8,128)S(1)} %fusion.22, f32[1024,512]{1,0:T(8,128)S(1)} %fusion.24, f32[1024,512]{1,0:T(8,128)S(1)} %fusion.26, f32[1024,512]{1,0:T(8,128)S(1)} %fusion.28, f32[1024,512]{1,0:T(8,128)S(1)} %fusion.30, f32[1024,512]{1,0:T(8,128)S(1)} %fusion.32, f32[1024,512]{1,0:T(8,128)S(1)} %fusion.34, ...), kind=kOutput, calls=%fused_computation.16 | convolution fusion | flops 541589504 | bytes 20449280 | tf_op jit(solution)/shard_map/dot_general | solution.py:109
  65.5 1.7 %fusion.5 = bf16[2,8,64,512]{3,2,0,1:T(8,128)(2,1)} fusion(f32[2,8,64,512]{3,2,1,0:T(8,128)S(1)} %bitcast.125, bf16[2,8,64,512]{3,2,1,0:T(8,128)(2,1)S(1)} %bitcast.121), kind=kLoop, calls=%fused_computation.14 | loop fusion | flops 3670016 | bytes 4194304 | tf_op jit(solution)/shard_map/convert_element_type | solution.py:116
  67.3 7.8 %all-to-all-start = ((bf16[2,8,64,512]{3,2,0,1:T(8,128)(2,1)}), bf16[2,8,64,512]{3,2,0,1:T(8,128)(2,1)S(1)}, u32[]{:S(2)}, u32[]{:S(2)}) async-start(bf16[2,8,64,512]{3,2,0,1:T(8,128)(2,1)} %fusion.5), calls=%async_computation | async-start | bytes 2097152 | tf_op jit(solution)/shard_map/all_to_all | solution.py:124
  75.1 26.1 %all-to-all-done = bf16[2,8,64,512]{3,2,0,1:T(8,128)(2,1)S(1)} async-done(((bf16[2,8,64,512]{3,2,0,1:T(8,128)(2,1)}), bf16[2,8,64,512]{3,2,0,1:T(8,128)(2,1)S(1)}, u32[]{:S(2)}, u32[]{:S(2)}) %all-to-all-start) | async-done | bytes 1048608 | tf_op jit(solution)/shard_map/all_to_all | solution.py:124
  101.8 0.7 convolution_convert_fusion.1
  103.3 1.3 fusion.13
  104.8 0.7 convolution_convert_fusion.2
  105.5 3.1 %fusion.16 = bf16[64,512,16]{1,2,0:T(8,128)(2,1)} fusion(bf16[16,64,512]{2,1,0:T(8,128)(2,1)S(1)} %bitcast.140, f32[64,16]{1,0:T(8,128)S(1)} %fusion.69, f32[64,16,16]{1,2,0:T(8,128)} %copy-done.11), kind=kOutput, calls=%fused_computation.33 | convolution fusion | flops 16827408 | bytes 2166784 | tf_op jit(solution)/shard_map/pst,tpc->spc/dot_general | solution.py:59
  108.6 2.1 %fusion.4 = bf16[16,64,512]{2,1,0:T(8,128)(2,1)S(1)} fusion(bf16[64,512,16]{1,2,0:T(8,128)(2,1)} %fusion.16, bf16[512,512]{1,0:T(8,128)(2,1)S(1)} %copy-done.10, bf16[2,8,64,512]{3,2,0,1:T(8,128)(2,1)S(1)} %all-to-all-done), kind=kOutput, calls=%fused_computation.11 | convolution fusion | flops 538443776 | bytes 3670016 | tf_op jit(solution)/shard_map/dot_general | solution.py:62
  110.7 29.3 %all_to_all.24 = bf16[16,64,512]{2,1,0:T(8,128)(2,1)S(1)} all-to-all(bf16[16,64,512]{2,1,0:T(8,128)(2,1)S(1)} %fusion.4), channel_id=1, replica_groups=mesh['clips'=2,'tm'=8,'cols'=2] {'tm'}, dimensions={0} | all-to-all | bytes 2097152 | tf_op jit(solution)/shard_map/all_to_all | solution.py:126
  140.0 1.1 copy.22
  (50 shorter events, 8.0 us)
Async XLA Ops:
  0.0 101.8 %copy-start = (bf16[512,512]{1,0:T(8,128)(2,1)S(1)}, bf16[512,512]{1,0:T(8,128)(2,1)}, u32[]{:S(2)}) copy-start(bf16[512,512]{1,0:T(8,128)(2,1)} %param.20) | copy-start | bytes 1572868
  0.0 6.4 %copy-start.1 = (bf16[4,32,16,512]{3,2,1,0:T(8,128)(2,1)S(1)}, bf16[4,32,16,512]{3,2,1,0:T(8,128)(2,1)}, u32[]{:S(2)}) copy-start(bf16[4,32,16,512]{3,2,1,0:T(8,128)(2,1)} %param.12) | copy-start | bytes 6291460
  1.5 27.3 %collective-permute-start = (bf16[2,32,16,512]{3,2,1,0:T(8,128)(2,1)S(1)}, bf16[2,32,16,512]{3,2,1,0:T(8,128)(2,1)S(1)}, u32[]{:S(2)}, u32[]{:S(2)}) collective-permute-start(bf16[2,32,16,512]{3,2,1,0:T(8,128)(2,1)S(1)} %slice.103), channel_id=1, source_target_pairs={{0,2},{2,4},{4,6},{6,8},{8,10},{10,12},{12,14},{1,3},{3,5},{5,7},{... | collective-permute-start | bytes 3145736 | tf_op jit(solution)/shard_map/ppermute | solution.py:14
  29.0 1.4 %copy-start.2 = (bf16[3,512,512]{2,1,0:T(8,128)(2,1)S(1)}, bf16[3,512,512]{2,1,0:T(8,128)(2,1)}, u32[]{:S(2)}) copy-start(bf16[3,512,512]{2,1,0:T(8,128)(2,1)} %param.13) | copy-start | bytes 4718596
  30.4 1.3 copy-start.5
  34.4 4.8 %copy-start.3 = (bf16[3,512,512]{2,1,0:T(8,128)(2,1)S(1)}, bf16[3,512,512]{2,1,0:T(8,128)(2,1)}, u32[]{:S(2)}) copy-start(bf16[3,512,512]{2,1,0:T(8,128)(2,1)} %param.15) | copy-start | bytes 4718596
  34.6 14.8 %collective-permute-start.1 = (bf16[1,32,16,512]{3,2,1,0:T(8,128)(2,1)S(1)}, bf16[1,32,16,512]{3,2,1,0:T(8,128)(2,1)S(1)}, u32[]{:S(2)}, u32[]{:S(2)}) collective-permute-start(bf16[1,32,16,512]{3,2,1,0:T(8,128)(2,1)S(1)} %slice.136), channel_id=1, source_target_pairs={{0,2},{2,4},{4,6},{6,8},{8,10},{10,12},{12,14},{1,3},{3,5},{5,7},{... | collective-permute-start | bytes 1572872 | tf_op jit(solution)/shard_map/ppermute | solution.py:14
  39.9 14.2 %slice-start = ((s8[4718592]{0:T(1024)(128)(4,1)}), s8[4194304]{0:T(1024)(128)(4,1)S(1)}, s32[]{:S(2)}) async-start(s8[4718592]{0:T(1024)(128)(4,1)} %bitcast.126), calls=%async_computation.2 | async-start | bytes 8388608
  49.7 0.7 copy-start.4
  49.7 4.5 %slice-start.1 = ((s8[4718592]{0:T(1024)(128)(4,1)}), s8[524288]{0:T(1024)(128)(4,1)S(1)}, s32[]{:S(2)}) async-start(s8[4718592]{0:T(1024)(128)(4,1)} %bitcast.126), calls=%async_computation.3 | async-start | bytes 1048576
  51.3 3.5 %collective-permute-start.2 = (bf16[2,32,1,512]{3,2,1,0:T(2,128)(2,1)S(1)}, bf16[2,32,1,512]{3,2,1,0:T(2,128)(2,1)S(1)}, u32[]{:S(2)}, u32[]{:S(2)}) collective-permute-start(bf16[2,32,1,512]{3,2,1,0:T(2,128)(2,1)S(1)} %get-tuple-element.17), channel_id=1, source_target_pairs={{0,1},{2,3},{4,5},{6,7},{8,9},{10,11},{12,13},{14,15},{16,17},{18,... | collective-permute-start | bytes 196616 | tf_op jit(solution)/shard_map/ppermute | solution.py:24
  52.6 3.2 %collective-permute-start.3 = (bf16[2,32,1,512]{3,2,1,0:T(2,128)(2,1)S(1)}, bf16[2,32,1,512]{3,2,1,0:T(2,128)(2,1)S(1)}, u32[]{:S(2)}, u32[]{:S(2)}) collective-permute-start(bf16[2,32,1,512]{3,2,1,0:T(2,128)(2,1)S(1)} %get-tuple-element.18), channel_id=1, source_target_pairs={{1,0},{3,2},{5,4},{7,6},{9,8},{11,10},{13,12},{15,14},{17,16},{19,... | collective-permute-start | bytes 196616 | tf_op jit(solution)/shard_map/ppermute | solution.py:25
  63.2 0.7 copy-start.7
  67.3 34.2 %copy-start.6 = (f32[512]{0:T(512)S(1)}, f32[512]{0:T(512)}, u32[]{:S(2)}) copy-start(f32[512]{0:T(512)} %param.19) | copy-start | bytes 6148
  67.3 33.9 %all-to-all-start = ((bf16[2,8,64,512]{3,2,0,1:T(8,128)(2,1)}), bf16[2,8,64,512]{3,2,0,1:T(8,128)(2,1)S(1)}, u32[]{:S(2)}, u32[]{:S(2)}) async-start(bf16[2,8,64,512]{3,2,0,1:T(8,128)(2,1)} %fusion.5), calls=%async_computation | async-start | bytes 2097152 | tf_op jit(solution)/shard_map/all_to_all | solution.py:124
  101.5 1.0 copy-start.8
  103.3 1.5 %copy-start.9 = (bf16[512,512]{1,0:T(8,128)(2,1)S(1)}, bf16[512,512]{1,0:T(8,128)(2,1)}, u32[]{:S(2)}) copy-start(bf16[512,512]{1,0:T(8,128)(2,1)} %param.22) | copy-start | bytes 1572868
  104.5 0.9 copy-start.11
  105.5 3.1 %copy-start.10 = (bf16[512,512]{1,0:T(8,128)(2,1)S(1)}, bf16[512,512]{1,0:T(8,128)(2,1)}, u32[]{:S(2)}) copy-start(bf16[512,512]{1,0:T(8,128)(2,1)} %param.23) | copy-start | bytes 1572868
where the time goes:
time: 142 us; the launch traced here: 141 us
  waiting for transfers between devices  55.9 us (39%)
  blocking collectives  29.3 us (21%)
  matrix products  22.9 us (16%)
  starting transfers between devices  20 us (14%)
  local copies, waits for them, and re-layouts  6.39 us (4%)
  other arithmetic  6.07 us (4%)
    all_to_all x1, blocking collectives, per_device(): lax.all_to_all(attended, 'tm', split_axis=0, concat_axis=1, tiled=True)  29.3 us
    ppermute x2, waiting for transfers between devices, passed_along(): lax.ppermute(value, axis, [(source, source + steps) for source in range(f...  28.9 us
    all_to_all x1, waiting for transfers between devices, per_device(): lax.all_to_all(grouped, 'tm', split_axis=1, concat_axis=0, tiled=True)  26.1 us
    ppermute x2, starting transfers between devices, passed_along(): lax.ppermute(value, axis, [(source, source + steps) for source in range(f...  9.48 us
    all_to_all x1, starting transfers between devices, per_device(): lax.all_to_all(grouped, 'tm', split_axis=1, concat_axis=0, tiled=True)  7.78 us
    dot_general x9, matrix products, per_device(): jnp.dot(window.reshape(-1, channels), w_space[3 * row_tap + col_tap], pre...  7.23 us
    dot_general x3, matrix products, temporal(): jnp.dot(window.reshape(-1, channels), weights[offset], preferred_element_...  4.99 us
    dot_general x1, matrix products, attend(): jnp.einsum('pst,tpc->spc', probs, value, preferred_element_type=jnp.float32)  3.05 us
  transfers between devices with their start and end apart: 5, of which 4 were waited for; matrix products, arithmetic and copies ran while one was open for 3% of the time, Pallas kernels for 0%

commit v1 on v0

v1 whole, which is shorter than its diff:
```python
from functools import partial

import jax
import jax.numpy as jnp
from jax import lax
from jax.experimental import pallas as pl
from jax.experimental.pallas import tpu as pltpu
from jax.sharding import PartitionSpec as P

epsilon = 1e-06
pair = 2
taps = 3
most_direct = 8
vmem_bytes = 48 * 1024 * 1024

VMEM = pl.BlockSpec(memory_space=pltpu.VMEM)
SMEM = pl.BlockSpec(memory_space=pltpu.SMEM)


def silu(v):
    return 0.5 * v * (1.0 + jnp.tanh(0.5 * v))


def dot32(a, b):
    return jnp.dot(a, b, preferred_element_type=jnp.float32)


def cost(flops, *arrays):
    size = sum(a.size * a.dtype.itemsize for a in arrays)
    return pl.CostEstimate(flops=flops, bytes_accessed=size, transcendentals=0)


def lift_kernel(flags, ext, w_time, b_time, w_down, b_down, out, odd, even):
    count, rows, width, channels = ext.shape
    pixels = rows * width
    frames = count - taps
    halves = frames // 2
    lifts = frames + 1
    group = 3 if lifts % 3 == 0 else 1

    def window(first):
        return ext[first : first + group].reshape(group * pixels, channels)

    for j in range(0, lifts, group):
        lhs = jnp.concatenate([window(j + 2 - k) for k in range(taps)], axis=1)
        acc = dot32(lhs, w_time[...]) + b_time[...]
        lifted = window(j + 2).astype(jnp.float32) + silu(acc)
        for g in range(group):
            piece = lifted[g * pixels : (g + 1) * pixels]
            if j + g == 0:
                piece = jnp.where(flags[0] > 0, piece, 0.0)
            (even if (j + g) % 2 else odd)[(j + g) // 2] = piece.astype(jnp.bfloat16)
    parts = [odd[1:], even[...], odd[:halves]]
    lhs = jnp.concatenate([p.reshape(halves * pixels, channels) for p in parts], axis=1)
    acc = dot32(lhs, w_down[...]) + b_down[...]
    out[...] = acc.reshape(halves, rows, width, channels).astype(jnp.bfloat16)

    @pl.when(flags[1] == 0)
    def _():
        out[:, 0] = jnp.zeros_like(out[:, 0])

    @pl.when(flags[2] == 0)
    def _():
        out[:, rows - 1] = jnp.zeros_like(out[:, rows - 1])


def lift(flags, ext, w_time, b_time, w_down, b_down):
    count, rows, width, channels = ext.shape
    frames = count - taps
    halves = frames // 2
    pixels = rows * width
    flops = 2 * taps * channels * channels * pixels * (frames + 1 + halves)
    return pl.pallas_call(
        lift_kernel,
        out_shape=jax.ShapeDtypeStruct((halves, rows, width, channels), jnp.bfloat16),
        in_specs=[SMEM] + [VMEM] * 5,
        out_specs=VMEM,
        scratch_shapes=[
            pltpu.VMEM((halves + 1, pixels, channels), jnp.bfloat16),
            pltpu.VMEM((halves, pixels, channels), jnp.bfloat16),
        ],
        compiler_params=pltpu.CompilerParams(vmem_limit_bytes=vmem_bytes),
        cost_estimate=cost(flops, ext, w_time, w_down),
        name="lift",
    )(flags, ext, w_time, b_time, w_down, b_down)


def space_kernel(left, middle, right, weights, bias, out):
    halves, rows, width, channels = out.shape
    pixels = halves * rows * width
    sources = (left, middle, right)

    def window(source, a):
        return source[:, a : a + rows].reshape(pixels, channels)

    lhs = jnp.concatenate([window(s, a) for a in range(3) for s in sources], axis=1)
    acc = dot32(lhs, weights[...]) + bias[...]
    result = window(middle, 1).astype(jnp.float32) + silu(acc)
    out[...] = result.astype(jnp.bfloat16).reshape(out.shape)


def space(left, middle, right, weights, bias):
    halves, rows, width, channels = middle.shape
    rows = rows - 2
    flops = 2 * 9 * channels * channels * halves * rows * width
    return pl.pallas_call(
        space_kernel,
        out_shape=jax.ShapeDtypeStruct((halves, rows, width, channels), jnp.bfloat16),
        in_specs=[VMEM] * 5,
        out_specs=VMEM,
        compiler_params=pltpu.CompilerParams(vmem_limit_bytes=vmem_bytes),
        cost_estimate=cost(flops, left, middle, right, weights),
        name="space",
    )(left, middle, right, weights, bias)


def attend_kernel(frames_per, lanes, count, first, *refs):
    blocks = refs[:count]
    gain, w_query, w_key, w_value, w_out = refs[count : count + 5]
    outs = refs[count + 5 :]
    channels = gain.shape[-1]
    flat = len(blocks[0].shape) == 2
    groups = 1 if flat else blocks[0].shape[1] // lanes
    each = frames_per * lanes
    size = count * each

    def piece(ref, g):
        if flat:
            return ref[...]
        return ref[:, g * lanes : (g + 1) * lanes].reshape(each, channels)

    def place(index):
        block = index // each
        frame = index // lanes % frames_per
        time = frame
        for j in range(count):
            time = time + jnp.where(block == j, first[j], 0)
        return time, index % lanes

    row_time, row_lane = place(lax.broadcasted_iota(jnp.int32, (size, 1), 0))
    col_time, col_lane = place(lax.broadcasted_iota(jnp.int32, (1, size), 1))
    allowed = (row_lane == col_lane) & (col_time <= row_time)
    x = jnp.concatenate([piece(b, g) for g in range(groups) for b in blocks], axis=0)
    wide = x.astype(jnp.float32)
    scale = lax.rsqrt(jnp.mean(wide * wide, axis=-1, keepdims=True) + epsilon)
    normed = (wide * scale * gain[...]).astype(jnp.bfloat16)
    query = dot32(normed, w_query[...]).astype(jnp.bfloat16)
    key = dot32(normed, w_key[...]).astype(jnp.bfloat16)
    value = dot32(normed, w_value[...]).astype(jnp.bfloat16)
    contexts = []
    for g in range(groups):
        part = slice(g * size, (g + 1) * size)
        scores = lax.dot_general(
            query[part], key[part], (((1,), (1,)), ((), ())), preferred_element_type=jnp.float32
        )
        scores = jnp.where(allowed, scores * channels ** (-0.5), -1e30)
        largest = jnp.max(scores, axis=-1, keepdims=True)
        probs = jnp.exp(scores - largest)
        probs = (probs / jnp.sum(probs, axis=-1, keepdims=True)).astype(jnp.bfloat16)
        contexts.append(dot32(probs, value[part]).astype(jnp.bfloat16))
    mixed = dot32(jnp.concatenate(contexts, axis=0), w_out[...])
    result = (wide + mixed).astype(jnp.bfloat16)
    for g in range(groups):
        for j, out in enumerate(outs):
            begin = g * size + j * each
            rows = result[begin : begin + each]
            if flat:
                out[...] = rows
            else:
                out[:, g * lanes : (g + 1) * lanes] = rows.reshape(frames_per, lanes, channels)


def attend(first, blocks, gain, w_query, w_key, w_value, w_out):
    frames_per, pixels, channels = blocks[0].shape
    lanes = 16 if pixels % 16 == 0 else pixels
    flat = pixels % 16 != 0
    if flat:
        blocks = [b.reshape(frames_per * pixels, channels) for b in blocks]
    count = len(blocks)
    rows = frames_per * pixels * count
    flops = 2 * rows * channels * (4 * channels + 2 * frames_per * count * lanes)
    outs = pl.pallas_call(
        partial(attend_kernel, frames_per, lanes, count),
        out_shape=[jax.ShapeDtypeStruct(b.shape, jnp.bfloat16) for b in blocks],
        in_specs=[SMEM] + [VMEM] * (count + 5),
        out_specs=[VMEM] * count,
        compiler_params=pltpu.CompilerParams(vmem_limit_bytes=vmem_bytes),
        cost_estimate=cost(flops, *blocks, w_query, w_key, w_value, w_out),
        name="attend",
    )(first, *blocks, gain, w_query, w_key, w_value, w_out)
    return [o.reshape(frames_per, pixels, channels) for o in outs]


def after(value, other):
    return lax.optimization_barrier((value, other))[0]


def per_device(
    video, w_time, b_time, w_down, b_down, w_space, b_space, gain, w_query, w_key, w_value, w_out
):
    frames, height, width, channels = video.shape
    devices = lax.axis_size("tm")
    levels = devices // pair
    columns = lax.axis_size("cols")
    place = lax.axis_index("tm")
    side = place % pair
    level = place // pair
    column = lax.axis_index("cols")
    half = height // pair
    halves = frames
    flags_of = lambda top, bottom: jnp.stack(
        [level, 1 if top is None else top, 1 if bottom is None else bottom]
    ).astype(jnp.int32)
    w_time = w_time.reshape(-1, channels)
    w_down = w_down.reshape(-1, channels)
    w_space = w_space.reshape(-1, channels)
    b_time, b_down, b_space, gain = (v.reshape(1, -1) for v in (b_time, b_down, b_space, gain))

    def swap(value):
        return lax.ppermute(value, "tm", [(i, i ^ 1) for i in range(devices)])

    def rows_of(owner, begin, end):
        low, high = owner * half + begin - 1, owner * half + end - 1
        body = video[:, max(low, 0) : min(high, height)]
        return jnp.pad(body, ((0, 0), (max(-low, 0), max(high - height, 0)), (0, 0), (0, 0)))

    def beside(value):
        last, first = value[:, :, -1:], value[:, :, :1]
        if columns == 2:
            other = lax.ppermute(jnp.where(column == 0, last, first), "cols", [(0, 1), (1, 0)])
            return jnp.where(column == 1, other, 0), jnp.where(column == 0, other, 0)
        up = [(i, i + 1) for i in range(columns - 1)]
        return lax.ppermute(last, "cols", up), lax.ppermute(
            first, "cols", [(j, i) for i, j in up]
        )

    if half % 4 == 0:
        sizes = (half // 4, half // 2, half // 4)
    else:
        sizes = (half,)
    direct = levels <= most_direct and levels & (levels - 1) == 0
    encoded = jnp.zeros((halves // pair, height * width, channels), jnp.bfloat16)
    previous = None
    previous_sent = None
    begin = 0
    for index, size in enumerate(sizes):
        end = begin + size
        first_row = 0 if index == 0 else begin + 2
        last_row = end + 2
        mine, others = (
            jnp.where(side == s, rows_of(0, first_row, last_row), rows_of(1, first_row, last_row))
            for s in (0, 1)
        )
        if previous_sent is not None:
            others = after(others, previous_sent)
        received = swap(others)
        previous_sent = received
        lower = jnp.where(side == 0, mine, received)
        upper = jnp.where(side == 0, received, mine)
        halo = lax.ppermute(
            upper[frames - taps :], "tm", [(i, i + pair) for i in range(devices - pair)]
        )
        ext = jnp.concatenate([halo, lower, upper], axis=0)
        flags = flags_of(side if index == 0 else None, 1 - side if end == half else None)
        reduced = lift(flags, ext, w_time, b_time, w_down, b_down)
        left, right = beside(reduced)
        pieces = (left, reduced, right)
        if previous is not None:
            pieces = tuple(jnp.concatenate(pq, axis=1) for pq in zip(previous, pieces))
        previous = tuple(p[:, -2:] for p in pieces)
        left, middle, right = pieces
        to_right = jnp.concatenate([left, middle[:, :, :-1]], axis=2)
        to_left = jnp.concatenate([middle[:, :, 1:], right], axis=2)
        spatial = space(to_right, middle, to_left, w_space, b_space)
        pixels = size * width // levels
        blocks = spatial.reshape(halves, levels, pixels, channels)
        if direct:
            gathered = []
            for j in range(levels):
                block = lax.dynamic_index_in_dim(blocks, level ^ j, 1, keepdims=False)
                if j:
                    route = [(i, (i // pair ^ j) * pair + i % pair) for i in range(devices)]
                    block = lax.ppermute(block, "tm", route)
                gathered.append(block)
            first = jnp.stack([(level ^ j) * halves for j in range(levels)]).astype(jnp.int32)
            results = attend(first, gathered, gain, w_query, w_key, w_value, w_out)
            returned = []
            for j in range(levels):
                block = results[j]
                if j:
                    route = [(i, (i // pair ^ j) * pair + i % pair) for i in range(devices)]
                    block = lax.ppermute(block, "tm", route)
                returned.append(block)
            whole = jnp.zeros((halves, levels, pixels, channels), jnp.bfloat16)
            for j in range(levels):
                whole = lax.dynamic_update_index_in_dim(whole, returned[j], level ^ j, 1)
        else:
            sets = [[s + pair * z for z in range(levels)] for s in range(pair)]
            gathered = lax.all_to_all(blocks, "tm", 1, 0, axis_index_groups=sets, tiled=True)
            gathered = gathered.reshape(halves * levels, pixels, channels)
            first = jnp.zeros((1,), jnp.int32)
            (result,) = attend(first, [gathered], gain, w_query, w_key, w_value, w_out)
            result = result.reshape(halves * levels, 1, pixels, channels)
            whole = lax.all_to_all(result, "tm", 0, 1, axis_index_groups=sets, tiled=True)
        whole = whole.reshape(pair, halves // pair, size * width, channels)
        kept = jnp.where(side == 0, whole[0], whole[1])
        other = swap(jnp.where(side == 0, whole[1], whole[0]))
        encoded = lax.dynamic_update_slice(
            encoded, kept, (0, (side * half + begin) * width, 0)
        )
        encoded = lax.dynamic_update_slice(
            encoded, other, (0, ((1 - side) * half + begin) * width, 0)
        )
        begin = end
    return encoded.reshape(halves // pair, height, width, channels)


def solution(mesh):
    spread = P(("clips", "tm"), None, "cols", None)
    return jax.shard_map(
        per_device,
        mesh=mesh,
        in_specs=(spread,) + (P(),) * 11,
        out_specs=spread,
        check_vma=False,
    )
```

time: 142 us -> 136 us (0.958)
  blocking collectives: 29.3 us -> 0 us
  starting transfers between devices: 20 us -> 47.8 us
  Pallas kernels: 0 us -> 23.5 us
  matrix products: 22.9 us -> 0 us
  waiting for transfers between devices: 55.9 us -> 51.6 us
  local copies, waits for them, and re-layouts: 6.39 us -> 3.92 us
    ppermute x4 -> x30, starting transfers between devices: 12.3 us -> 47.8 us  [the longest x18 30.6 us: per_device(): block = lax.ppermute(block, 'tm', route)]
    all_to_all x1 -> x0, blocking collectives: 29.3 us -> none  [per_device(): lax.all_to_all(attended, 'tm', split_axis=0, concat_axis=1, tiled=True)]
    all_to_all x1 -> x0, waiting for transfers between devices: 26.1 us -> none  [per_device(): lax.all_to_all(grouped, 'tm', split_axis=1, concat_axis=0, tiled=True)]
    pallas_call x0 -> x9, Pallas kernels: none -> 23.5 us  [the longest x3 9.02 us: lift(): pl.pallas_call(lift_kernel, out_shape=jax.ShapeDtypeStruct((halves, rows,...]
    dot_general x21 -> x0, matrix products: 22.9 us -> none  [the longest x9 7.23 us: per_device(): jnp.dot(window.reshape(-1, channels), w_space[3 * row_tap + col_tap], pre...]
    ppermute x4 -> x30, waiting for transfers between devices: 29.9 us -> 51.6 us  [the longest x18 25.2 us: per_device(): block = lax.ppermute(block, 'tm', route)]
    all_to_all x1 -> x0, starting transfers between devices: 7.78 us -> none  [per_device(): lax.all_to_all(grouped, 'tm', split_axis=1, concat_axis=0, tiled=True)]
    select_n x0 -> x15, other arithmetic: none -> 3.63 us  [the longest x3 1.83 us: per_device(): jnp.where(side == s, rows_of(0, first_row, last_row), rows_of(1, first_ro...]
  transfers between devices with their start and end apart: 5 -> 30, of which waited for: 4 -> 19; matrix products, arithmetic and copies ran while one was open for 3% -> 3% of each run, Pallas kernels for 0% -> 11%
where the time goes in v1:
time: 136 us; the launch traced here: 134 us
  waiting for transfers between devices  51.6 us (38%)
  starting transfers between devices  47.8 us (35%)
  Pallas kernels  23.5 us (17%)
  other arithmetic  6.73 us (5%)
  local copies, waits for them, and re-layouts  3.92 us (3%)
    ppermute x18, starting transfers between devices, per_device(): block = lax.ppermute(block, 'tm', route)  30.6 us
    ppermute x18, waiting for transfers between devices, per_device(): block = lax.ppermute(block, 'tm', route)  25.2 us
    ppermute x6, waiting for transfers between devices, swap(): return lax.ppermute(value, 'tm', [(i, i ^ 1) for i in range(devices)])  17.8 us
    pallas_call x3, Pallas kernels, lift(): pl.pallas_call(lift_kernel, out_shape=jax.ShapeDtypeStruct((halves, rows,...  9.02 us
    ppermute x6, starting transfers between devices, swap(): return lax.ppermute(value, 'tm', [(i, i ^ 1) for i in range(devices)])  8.8 us
    ppermute x3, starting transfers between devices, per_device(): lax.ppermute(upper[frames - taps:], 'tm', [(i, i + pair) for i in range(d...  8.07 us
    pallas_call x3, Pallas kernels, space(): pl.pallas_call(space_kernel, out_shape=jax.ShapeDtypeStruct((halves, rows...  8 us
    pallas_call x3, Pallas kernels, attend(): pl.pallas_call(partial(attend_kernel, frames_per, lanes, count), out_shap...  6.44 us
  transfers between devices with their start and end apart: 30, of which 19 were waited for; matrix products, arithmetic and copies ran while one was open for 3% of the time, Pallas kernels for 11%

profile of v1, /device:TPU:0, one launch (start us, length us, event | category | flops | bytes accessed | tf_op | source)
XLA Modules:
  0.0 134.3 jit_solution(12321253755033705943)
XLA Ops:
  2.2 3.0 %collective-permute-start = (bf16[4,6,16,512]{3,2,1,0:T(8,128)(2,1)S(1)}, bf16[4,6,16,512]{3,2,1,0:T(8,128)(2,1)}, u32[]{:S(2)}, u32[]{:S(2)}) collective-permute-start(bf16[4,6,16,512]{3,2,1,0:T(8,128)(2,1)S(1)} %broadcast_select_fusion.4), channel_id=1, source_target_pairs={{0,2},{2,0},{4,6},{6,4},{8,10},{10,8},{12,14},{14,12},{1,3},{3,1},... | collective-permute-start | bytes 1179656 | tf_op jit(solution)/shard_map/ppermute | solution.py:220
  7.0 7.4 %collective-permute-done = bf16[4,6,16,512]{3,2,1,0:T(8,128)(2,1)} collective-permute-done((bf16[4,6,16,512]{3,2,1,0:T(8,128)(2,1)S(1)}, bf16[4,6,16,512]{3,2,1,0:T(8,128)(2,1)}, u32[]{:S(2)}, u32[]{:S(2)}) %collective-permute-start) | collective-permute-done | bytes 393248 | tf_op jit(solution)/shard_map/ppermute | solution.py:220
  15.5 4.4 %collective-permute-start.1 = (bf16[3,6,16,512]{3,2,1,0:T(8,128)(2,1)S(1)}, bf16[3,6,16,512]{3,2,1,0:T(8,128)(2,1)}, u32[]{:S(2)}, u32[]{:S(2)}) collective-permute-start(bf16[3,6,16,512]{3,2,1,0:T(8,128)(2,1)S(1)} %slice.150), channel_id=1, source_target_pairs={{0,4},{2,6},{4,8},{6,10},{8,12},{10,14},{1,5},{3,7},{5,9},{7,11},{... | collective-permute-start | bytes 884744 | tf_op jit(solution)/shard_map/ppermute | solution.py:260
  20.2 4.4 %collective-permute-done.1 = bf16[3,6,16,512]{3,2,1,0:T(8,128)(2,1)} collective-permute-done((bf16[3,6,16,512]{3,2,1,0:T(8,128)(2,1)S(1)}, bf16[3,6,16,512]{3,2,1,0:T(8,128)(2,1)}, u32[]{:S(2)}, u32[]{:S(2)}) %collective-permute-start.1) | collective-permute-done | bytes 294944 | tf_op jit(solution)/shard_map/ppermute | solution.py:260
  25.8 3.0 %lift.3.middle = bf16[4,6,16,512]{3,2,1,0:T(8,128)(2,1)S(1)} custom-call(s32[3]{0:T(128)S(1)} %pad_add_fusion.1.flags, bf16[11,6,16,512]{3,2,1,0:T(8,128)(2,1)S(1)} %pad_maximum_fusion.1.ext, bf16[1536,512]{1,0:T(8,128)(2,1)S(1)} %bitcast.113, f32[1,512]{1,0:T(1,128)S(1)} %bitcast.119, bf16[1536,512]{1,0:T(8,128)(2,1)S(1)} %bitcast.116, f32[1,512]{1,0:T(1,128)S(1)} %bitcast.122), custom_call_target="tpu_custom_call" | custom-call | flops 1962934272 | bytes 4227072 | tf_op jit(solution)/shard_map/lift/pallas_call | solution.py:73
  32.2 2.7 %collective-permute-start.3 = (bf16[4,16,512]{2,1,0:T(8,128)(2,1)S(1)}, bf16[4,16,512]{2,1,0:T(8,128)(2,1)S(1)}, u32[]{:S(2)}, u32[]{:S(2)}) collective-permute-start(bf16[4,16,512]{2,1,0:T(8,128)(2,1)S(1)} %get-tuple-element.61), channel_id=1, source_target_pairs={{0,4},{2,6},{4,0},{6,2},{8,12},{10,14},{12,8},{14,10},{1,5},{3,7},... | collective-permute-start | bytes 196616 | tf_op jit(solution)/shard_map/ppermute | solution.py:283
  34.8 2.6 %collective-permute-start.4 = (bf16[4,16,512]{2,1,0:T(8,128)(2,1)S(1)}, bf16[4,16,512]{2,1,0:T(8,128)(2,1)S(1)}, u32[]{:S(2)}, u32[]{:S(2)}) collective-permute-start(bf16[4,16,512]{2,1,0:T(8,128)(2,1)S(1)} %get-tuple-element.60), channel_id=1, source_target_pairs={{0,8},{2,10},{4,12},{6,14},{8,0},{10,2},{12,4},{14,6},{1,9},{3,11}... | collective-permute-start | bytes 196616 | tf_op jit(solution)/shard_map/ppermute | solution.py:283
  39.1 3.3 %collective-permute-done.4.refs_2_ = bf16[4,16,512]{2,1,0:T(8,128)(2,1)S(1)} collective-permute-done((bf16[4,16,512]{2,1,0:T(8,128)(2,1)S(1)}, bf16[4,16,512]{2,1,0:T(8,128)(2,1)S(1)}, u32[]{:S(2)}, u32[]{:S(2)}) %collective-permute-start.4) | collective-permute-done | bytes 65568 | tf_op jit(solution)/shard_map/ppermute | solution.py:283
  43.6 1.9 %attend.3 = (bf16[4,16,512]{2,1,0:T(8,128)(2,1)S(1)}, bf16[4,16,512]{2,1,0:T(8,128)(2,1)S(1)}, bf16[4,16,512]{2,1,0:T(8,128)(2,1)S(1)}, bf16[4,16,512]{2,1,0:T(8,128)(2,1)S(1)}) custom-call(s32[4]{0:T(128)S(1)} %pad_add_fusion.first, bf16[4,16,512]{2,1,0:T(8,128)(2,1)S(1)} %get-tuple-element.62.refs_0_, ...), custom_call_target="tpu_custom_call" | custom-call | flops 671088640 | bytes 2359296 | tf_op jit(solution)/shard_map/attend/pallas_call | solution.py:182
  46.5 1.7 %collective-permute-start.7 = (bf16[4,16,512]{2,1,0:T(8,128)(2,1)S(1)}, bf16[4,16,512]{2,1,0:T(8,128)(2,1)S(1)}, u32[]{:S(2)}, u32[]{:S(2)}) collective-permute-start(bf16[4,16,512]{2,1,0:T(8,128)(2,1)S(1)} %get-tuple-element.21), channel_id=1, source_target_pairs={{0,8},{2,10},{4,12},{6,14},{8,0},{10,2},{12,4},{14,6},{1,9},{3,11}... | collective-permute-start | bytes 196616 | tf_op jit(solution)/shard_map/ppermute | solution.py:292
  48.2 1.8 %collective-permute-start.8 = (bf16[4,16,512]{2,1,0:T(8,128)(2,1)S(1)}, bf16[4,16,512]{2,1,0:T(8,128)(2,1)S(1)}, u32[]{:S(2)}, u32[]{:S(2)}) collective-permute-start(bf16[4,16,512]{2,1,0:T(8,128)(2,1)S(1)} %get-tuple-element.22), channel_id=1, source_target_pairs={{0,12},{2,14},{4,8},{6,10},{8,4},{10,6},{12,0},{14,2},{1,13},{3,15... | collective-permute-start | bytes 196616 | tf_op jit(solution)/shard_map/ppermute | solution.py:292
  50.1 2.8 %collective-permute-done.7 = bf16[4,16,512]{2,1,0:T(8,128)(2,1)S(1)} collective-permute-done((bf16[4,16,512]{2,1,0:T(8,128)(2,1)S(1)}, bf16[4,16,512]{2,1,0:T(8,128)(2,1)S(1)}, u32[]{:S(2)}, u32[]{:S(2)}) %collective-permute-start.7) | collective-permute-done | bytes 65568 | tf_op jit(solution)/shard_map/ppermute | solution.py:292
  54.3 1.6 %collective-permute-start.9 = (bf16[2,64,512]{2,1,0:T(8,128)(2,1)S(1)}, bf16[2,64,512]{2,1,0:T(8,128)(2,1)S(1)}, u32[]{:S(2)}, u32[]{:S(2)}) collective-permute-start(bf16[2,64,512]{2,1,0:T(8,128)(2,1)S(1)} %bitcast.132), channel_id=1, source_target_pairs={{0,2},{2,0},{4,6},{6,4},{8,10},{10,8},{12,14},{14,12},{1,3},{3,1},... | collective-permute-start | bytes 393224 | tf_op jit(solution)/shard_map/ppermute | solution.py:220
  56.6 1.8 %collective-permute-start.11 = (bf16[3,8,16,512]{3,2,1,0:T(8,128)(2,1)S(1)}, bf16[3,8,16,512]{3,2,1,0:T(8,128)(2,1)S(1)}, u32[]{:S(2)}, u32[]{:S(2)}) collective-permute-start(bf16[3,8,16,512]{3,2,1,0:T(8,128)(2,1)S(1)} %slice.158), channel_id=1, source_target_pairs={{0,4},{2,6},{4,8},{6,10},{8,12},{10,14},{1,5},{3,7},{5,9},{7,11},{... | collective-permute-start | bytes 1179656 | tf_op jit(solution)/shard_map/ppermute | solution.py:260
  58.5 1.8 %collective-permute-done.9 = bf16[2,64,512]{2,1,0:T(8,128)(2,1)S(1)} collective-permute-done((bf16[2,64,512]{2,1,0:T(8,128)(2,1)S(1)}, bf16[2,64,512]{2,1,0:T(8,128)(2,1)S(1)}, u32[]{:S(2)}, u32[]{:S(2)}) %collective-permute-start.9) | collective-permute-done | bytes 131104 | tf_op jit(solution)/shard_map/ppermute | solution.py:220
  60.3 2.8 %collective-permute-done.20 = bf16[4,4,16,512]{3,2,1,0:T(8,128)(2,1)S(1)} collective-permute-done((bf16[4,4,16,512]{3,2,1,0:T(8,128)(2,1)S(1)}, bf16[4,4,16,512]{3,2,1,0:T(8,128)(2,1)S(1)}, u32[]{:S(2)}, u32[]{:S(2)}) %collective-permute-start.20) | collective-permute-done | bytes 262176 | tf_op jit(solution)/shard_map/ppermute | solution.py:220
  63.1 1.8 %collective-permute-start.21 = (bf16[3,4,16,512]{3,2,1,0:T(8,128)(2,1)S(1)}, bf16[3,4,16,512]{3,2,1,0:T(8,128)(2,1)S(1)}, u32[]{:S(2)}, u32[]{:S(2)}) collective-permute-start(bf16[3,4,16,512]{3,2,1,0:T(8,128)(2,1)S(1)} %slice.170), channel_id=1, source_target_pairs={{0,4},{2,6},{4,8},{6,10},{8,12},{10,14},{1,5},{3,7},{5,9},{7,11},{... | collective-permute-start | bytes 589832 | tf_op jit(solution)/shard_map/ppermute | solution.py:260
  66.3 3.8 %lift.4 = bf16[4,8,16,512]{3,2,1,0:T(8,128)(2,1)S(1)} custom-call(s32[3]{0:T(128)S(1)} %stack.53.flags, bf16[11,8,16,512]{3,2,1,0:T(8,128)(2,1)S(1)} %pad_maximum_fusion.ext, bf16[1536,512]{1,0:T(8,128)(2,1)S(1)} %bitcast.114, f32[1,512]{1,0:T(1,128)S(1)} %bitcast.120, bf16[1536,512]{1,0:T(8,128)(2,1)S(1)} %bitcast.117, f32[1,512]{1,0:T(1,128)S(1)} %bitcast.123), custom_call_target="tpu_custom_call" | custom-call | flops 2617245696 | bytes 4587520 | tf_op jit(solution)/shard_map/lift/pallas_call | solution.py:73
  72.2 5.1 %space.4 = bf16[4,8,16,512]{3,2,1,0:T(8,128)(2,1)S(1)} custom-call(bf16[4,10,16,512]{3,2,1,0:T(8,128)(2,1)S(1)} %get-tuple-element.71.left, bf16[4,10,16,512]{3,2,1,0:T(8,128)(2,1)S(1)} %pad_maximum_fusion.2.middle, bf16[4,10,16,512]{3,2,1,0:T(8,128)(2,1)S(1)} %get-tuple-element.72.right, bf16[4608,512]{1,0:T(8,128)(2,1)} %bitcast.102, f32[1,512]{1,0:T(1,128)S(1)} %bitcast.111), custom_call_target="tpu_custom_call" | custom-call | flops 2415919104 | bytes 6684672 | tf_op jit(solution)/shard_map/space/pallas_call | solution.py:106
  77.4 2.2 %lift.5 = bf16[4,4,16,512]{3,2,1,0:T(8,128)(2,1)S(1)} custom-call(s32[3]{0:T(128)S(1)} %pad_add_fusion.2.flags, bf16[11,4,16,512]{3,2,1,0:T(8,128)(2,1)S(1)} %pad_maximum_fusion.3.ext, bf16[1536,512]{1,0:T(8,128)(2,1)S(1)} %bitcast.115, f32[1,512]{1,0:T(1,128)S(1)} %bitcast.121, bf16[1536,512]{1,0:T(8,128)(2,1)S(1)} %bitcast.118, f32[1,512]{1,0:T(1,128)S(1)} %bitcast.124), custom_call_target="tpu_custom_call" | custom-call | flops 1308622848 | bytes 3866624 | tf_op jit(solution)/shard_map/lift/pallas_call | solution.py:73
  83.0 2.6 %collective-permute-start.23 = (bf16[4,16,512]{2,1,0:T(8,128)(2,1)S(1)}, bf16[4,16,512]{2,1,0:T(8,128)(2,1)S(1)}, u32[]{:S(2)}, u32[]{:S(2)}) collective-permute-start(bf16[4,16,512]{2,1,0:T(8,128)(2,1)S(1)} %get-tuple-element.55), channel_id=1, source_target_pairs={{0,4},{2,6},{4,0},{6,2},{8,12},{10,14},{12,8},{14,10},{1,5},{3,7},... | collective-permute-start | bytes 196616 | tf_op jit(solution)/shard_map/ppermute | solution.py:283
  85.6 2.0 %collective-permute-start.24 = (bf16[4,16,512]{2,1,0:T(8,128)(2,1)S(1)}, bf16[4,16,512]{2,1,0:T(8,128)(2,1)S(1)}, u32[]{:S(2)}, u32[]{:S(2)}) collective-permute-start(bf16[4,16,512]{2,1,0:T(8,128)(2,1)S(1)} %get-tuple-element.54), channel_id=1, source_target_pairs={{0,8},{2,10},{4,12},{6,14},{8,0},{10,2},{12,4},{14,6},{1,9},{3,11}... | collective-permute-start | bytes 196616 | tf_op jit(solution)/shard_map/ppermute | solution.py:283
  89.2 2.8 %collective-permute-start.14 = (bf16[4,32,512]{2,1,0:T(8,128)(2,1)S(1)}, bf16[4,32,512]{2,1,0:T(8,128)(2,1)S(1)}, u32[]{:S(2)}, u32[]{:S(2)}) collective-permute-start(bf16[4,32,512]{2,1,0:T(8,128)(2,1)S(1)} %get-tuple-element.44), channel_id=1, source_target_pairs={{0,8},{2,10},{4,12},{6,14},{8,0},{10,2},{12,4},{14,6},{1,9},{3,11}... | collective-permute-start | bytes 393224 | tf_op jit(solution)/shard_map/ppermute | solution.py:283
  94.4 1.9 %attend.5 = (bf16[4,16,512]{2,1,0:T(8,128)(2,1)S(1)}, bf16[4,16,512]{2,1,0:T(8,128)(2,1)S(1)}, bf16[4,16,512]{2,1,0:T(8,128)(2,1)S(1)}, bf16[4,16,512]{2,1,0:T(8,128)(2,1)S(1)}) custom-call(s32[4]{0:T(128)S(1)} %pad_add_fusion.first, bf16[4,16,512]{2,1,0:T(8,128)(2,1)S(1)} %get-tuple-element.56.refs_0_, ...), custom_call_target="tpu_custom_call" | custom-call | flops 671088640 | bytes 2359296 | tf_op jit(solution)/shard_map/attend/pallas_call | solution.py:182
  97.8 2.0 %collective-permute-start.27 = (bf16[4,16,512]{2,1,0:T(8,128)(2,1)S(1)}, bf16[4,16,512]{2,1,0:T(8,128)(2,1)S(1)}, u32[]{:S(2)}, u32[]{:S(2)}) collective-permute-start(bf16[4,16,512]{2,1,0:T(8,128)(2,1)S(1)} %get-tuple-element.31), channel_id=1, source_target_pairs={{0,8},{2,10},{4,12},{6,14},{8,0},{10,2},{12,4},{14,6},{1,9},{3,11}... | collective-permute-start | bytes 196616 | tf_op jit(solution)/shard_map/ppermute | solution.py:292
  101.2 5.3 %collective-permute-done.14.refs_2_ = bf16[4,32,512]{2,1,0:T(8,128)(2,1)S(1)} collective-permute-done((bf16[4,32,512]{2,1,0:T(8,128)(2,1)S(1)}, bf16[4,32,512]{2,1,0:T(8,128)(2,1)S(1)}, u32[]{:S(2)}, u32[]{:S(2)}) %collective-permute-start.14) | collective-permute-done | bytes 131104 | tf_op jit(solution)/shard_map/ppermute | solution.py:283
  106.5 2.6 %attend.4 = (bf16[4,32,512]{2,1,0:T(8,128)(2,1)S(1)}, bf16[4,32,512]{2,1,0:T(8,128)(2,1)S(1)}, bf16[4,32,512]{2,1,0:T(8,128)(2,1)S(1)}, bf16[4,32,512]{2,1,0:T(8,128)(2,1)S(1)}) custom-call(s32[4]{0:T(128)S(1)} %pad_add_fusion.first, bf16[4,32,512]{2,1,0:T(8,128)(2,1)S(1)} %get-tuple-element.46.refs_0_, ...), custom_call_target="tpu_custom_call" | custom-call | flops 1342177280 | bytes 2621440 | tf_op jit(solution)/shard_map/attend/pallas_call | solution.py:182
  109.2 3.4 %collective-permute-start.16 = (bf16[4,32,512]{2,1,0:T(8,128)(2,1)S(1)}, bf16[4,32,512]{2,1,0:T(8,128)(2,1)S(1)}, u32[]{:S(2)}, u32[]{:S(2)}) collective-permute-start(bf16[4,32,512]{2,1,0:T(8,128)(2,1)S(1)} %get-tuple-element.25), channel_id=1, source_target_pairs={{0,4},{2,6},{4,0},{6,2},{8,12},{10,14},{12,8},{14,10},{1,5},{3,7},... | collective-permute-start | bytes 393224 | tf_op jit(solution)/shard_map/ppermute | solution.py:292
  115.4 1.7 %collective-permute-done.16 = bf16[4,32,512]{2,1,0:T(8,128)(2,1)S(1)} collective-permute-done((bf16[4,32,512]{2,1,0:T(8,128)(2,1)S(1)}, bf16[4,32,512]{2,1,0:T(8,128)(2,1)S(1)}, u32[]{:S(2)}, u32[]{:S(2)}) %collective-permute-start.16) | collective-permute-done | bytes 131104 | tf_op jit(solution)/shard_map/ppermute | solution.py:292
  117.1 8.1 %collective-permute-done.17 = bf16[4,32,512]{2,1,0:T(8,128)(2,1)S(1)} collective-permute-done((bf16[4,32,512]{2,1,0:T(8,128)(2,1)S(1)}, bf16[4,32,512]{2,1,0:T(8,128)(2,1)S(1)}, u32[]{:S(2)}, u32[]{:S(2)}) %collective-permute-start.17) | collective-permute-done | bytes 131104 | tf_op jit(solution)/shard_map/ppermute | solution.py:292
  125.3 1.6 %collective-permute-start.19 = (bf16[2,128,512]{2,1,0:T(8,128)(2,1)S(1)}, bf16[2,128,512]{2,1,0:T(8,128)(2,1)S(1)}, u32[]{:S(2)}, u32[]{:S(2)}) collective-permute-start(bf16[2,128,512]{2,1,0:T(8,128)(2,1)S(1)} %bitcast.131), channel_id=1, source_target_pairs={{0,2},{2,0},{4,6},{6,4},{8,10},{10,8},{12,14},{14,12},{1,3},{3,1},... | collective-permute-start | bytes 786440 | tf_op jit(solution)/shard_map/ppermute | solution.py:220
  127.5 4.4 %collective-permute-done.19 = bf16[2,128,512]{2,1,0:T(8,128)(2,1)S(1)} collective-permute-done((bf16[2,128,512]{2,1,0:T(8,128)(2,1)S(1)}, bf16[2,128,512]{2,1,0:T(8,128)(2,1)S(1)}, u32[]{:S(2)}, u32[]{:S(2)}) %collective-permute-start.19) | collective-permute-done | bytes 262176 | tf_op jit(solution)/shard_map/ppermute | solution.py:220
  (139 shorter events, 35.0 us)
Async XLA Ops:
  2.2 12.3 %collective-permute-start = (bf16[4,6,16,512]{3,2,1,0:T(8,128)(2,1)S(1)}, bf16[4,6,16,512]{3,2,1,0:T(8,128)(2,1)}, u32[]{:S(2)}, u32[]{:S(2)}) collective-permute-start(bf16[4,6,16,512]{3,2,1,0:T(8,128)(2,1)S(1)} %broadcast_select_fusion.4), channel_id=1, source_target_pairs={{0,2},{2,0},{4,6},{6,4},{8,10},{10,8},{12,14},{14,12},{1,3},{3,1},... | collective-permute-start | bytes 1179656 | tf_op jit(solution)/shard_map/ppermute | solution.py:220
  15.5 9.1 %collective-permute-start.1 = (bf16[3,6,16,512]{3,2,1,0:T(8,128)(2,1)S(1)}, bf16[3,6,16,512]{3,2,1,0:T(8,128)(2,1)}, u32[]{:S(2)}, u32[]{:S(2)}) collective-permute-start(bf16[3,6,16,512]{3,2,1,0:T(8,128)(2,1)S(1)} %slice.150), channel_id=1, source_target_pairs={{0,4},{2,6},{4,8},{6,10},{8,12},{10,14},{1,5},{3,7},{5,9},{7,11},{... | collective-permute-start | bytes 884744 | tf_op jit(solution)/shard_map/ppermute | solution.py:260
  28.9 1.3 collective-permute-start.2
  30.6 13.0 %copy-start.3 = (bf16[512,512]{1,0:T(8,128)(2,1)S(1)}, bf16[512,512]{1,0:T(8,128)(2,1)}, u32[]{:S(2)}) copy-start(bf16[512,512]{1,0:T(8,128)(2,1)} %refs_5_.5) | copy-start | bytes 1572868
  30.6 13.0 %copy-start.4 = (bf16[512,512]{1,0:T(8,128)(2,1)S(1)}, bf16[512,512]{1,0:T(8,128)(2,1)}, u32[]{:S(2)}) copy-start(bf16[512,512]{1,0:T(8,128)(2,1)} %refs_6_.5) | copy-start | bytes 1572868
  32.2 6.9 %collective-permute-start.3 = (bf16[4,16,512]{2,1,0:T(8,128)(2,1)S(1)}, bf16[4,16,512]{2,1,0:T(8,128)(2,1)S(1)}, u32[]{:S(2)}, u32[]{:S(2)}) collective-permute-start(bf16[4,16,512]{2,1,0:T(8,128)(2,1)S(1)} %get-tuple-element.61), channel_id=1, source_target_pairs={{0,4},{2,6},{4,0},{6,2},{8,12},{10,14},{12,8},{14,10},{1,5},{3,7},... | collective-permute-start | bytes 196616 | tf_op jit(solution)/shard_map/ppermute | solution.py:283
  34.8 7.6 %collective-permute-start.4 = (bf16[4,16,512]{2,1,0:T(8,128)(2,1)S(1)}, bf16[4,16,512]{2,1,0:T(8,128)(2,1)S(1)}, u32[]{:S(2)}, u32[]{:S(2)}) collective-permute-start(bf16[4,16,512]{2,1,0:T(8,128)(2,1)S(1)} %get-tuple-element.60), channel_id=1, source_target_pairs={{0,8},{2,10},{4,12},{6,14},{8,0},{10,2},{12,4},{14,6},{1,9},{3,11}... | collective-permute-start | bytes 196616 | tf_op jit(solution)/shard_map/ppermute | solution.py:283
  37.4 6.2 %collective-permute-start.5 = (bf16[4,16,512]{2,1,0:T(8,128)(2,1)S(1)}, bf16[4,16,512]{2,1,0:T(8,128)(2,1)S(1)}, u32[]{:S(2)}, u32[]{:S(2)}) collective-permute-start(bf16[4,16,512]{2,1,0:T(8,128)(2,1)S(1)} %get-tuple-element.59), channel_id=1, source_target_pairs={{0,12},{2,14},{4,8},{6,10},{8,4},{10,6},{12,0},{14,2},{1,13},{3,15... | collective-permute-start | bytes 196616 | tf_op jit(solution)/shard_map/ppermute | solution.py:283
  37.5 18.4 %collective-permute-start.10 = (bf16[4,8,16,512]{3,2,1,0:T(8,128)(2,1)S(1)}, bf16[4,8,16,512]{3,2,1,0:T(8,128)(2,1)S(1)}, u32[]{:S(2)}, u32[]{:S(2)}) collective-permute-start(bf16[4,8,16,512]{3,2,1,0:T(8,128)(2,1)S(1)} %broadcast_select_fusion), channel_id=1, source_target_pairs={{0,2},{2,0},{4,6},{6,4},{8,10},{10,8},{12,14},{14,12},{1,3},{3,1},... | collective-permute-start | bytes 1572872 | tf_op jit(solution)/shard_map/ppermute | solution.py:220
  45.5 4.5 %collective-permute-start.6 = (bf16[4,16,512]{2,1,0:T(8,128)(2,1)S(1)}, bf16[4,16,512]{2,1,0:T(8,128)(2,1)S(1)}, u32[]{:S(2)}, u32[]{:S(2)}) collective-permute-start(bf16[4,16,512]{2,1,0:T(8,128)(2,1)S(1)} %get-tuple-element.20), channel_id=1, source_target_pairs={{0,4},{2,6},{4,0},{6,2},{8,12},{10,14},{12,8},{14,10},{1,5},{3,7},... | collective-permute-start | bytes 196616 | tf_op jit(solution)/shard_map/ppermute | solution.py:292
  46.5 6.4 %collective-permute-start.7 = (bf16[4,16,512]{2,1,0:T(8,128)(2,1)S(1)}, bf16[4,16,512]{2,1,0:T(8,128)(2,1)S(1)}, u32[]{:S(2)}, u32[]{:S(2)}) collective-permute-start(bf16[4,16,512]{2,1,0:T(8,128)(2,1)S(1)} %get-tuple-element.21), channel_id=1, source_target_pairs={{0,8},{2,10},{4,12},{6,14},{8,0},{10,2},{12,4},{14,6},{1,9},{3,11}... | collective-permute-start | bytes 196616 | tf_op jit(solution)/shard_map/ppermute | solution.py:292
  48.2 6.1 %collective-permute-start.8 = (bf16[4,16,512]{2,1,0:T(8,128)(2,1)S(1)}, bf16[4,16,512]{2,1,0:T(8,128)(2,1)S(1)}, u32[]{:S(2)}, u32[]{:S(2)}) collective-permute-start(bf16[4,16,512]{2,1,0:T(8,128)(2,1)S(1)} %get-tuple-element.22), channel_id=1, source_target_pairs={{0,12},{2,14},{4,8},{6,10},{8,4},{10,6},{12,0},{14,2},{1,13},{3,15... | collective-permute-start | bytes 196616 | tf_op jit(solution)/shard_map/ppermute | solution.py:292
  54.3 5.9 %collective-permute-start.9 = (bf16[2,64,512]{2,1,0:T(8,128)(2,1)S(1)}, bf16[2,64,512]{2,1,0:T(8,128)(2,1)S(1)}, u32[]{:S(2)}, u32[]{:S(2)}) collective-permute-start(bf16[2,64,512]{2,1,0:T(8,128)(2,1)S(1)} %bitcast.132), channel_id=1, source_target_pairs={{0,2},{2,0},{4,6},{6,4},{8,10},{10,8},{12,14},{14,12},{1,3},{3,1},... | collective-permute-start | bytes 393224 | tf_op jit(solution)/shard_map/ppermute | solution.py:220
  55.9 7.2 %collective-permute-start.20 = (bf16[4,4,16,512]{3,2,1,0:T(8,128)(2,1)S(1)}, bf16[4,4,16,512]{3,2,1,0:T(8,128)(2,1)S(1)}, u32[]{:S(2)}, u32[]{:S(2)}) collective-permute-start(bf16[4,4,16,512]{3,2,1,0:T(8,128)(2,1)S(1)} %copy-done.12), channel_id=1, source_target_pairs={{0,2},{2,0},{4,6},{6,4},{8,10},{10,8},{12,14},{14,12},{1,3},{3,1},... | collective-permute-start | bytes 786440 | tf_op jit(solution)/shard_map/ppermute | solution.py:220
  56.6 9.5 %collective-permute-start.11 = (bf16[3,8,16,512]{3,2,1,0:T(8,128)(2,1)S(1)}, bf16[3,8,16,512]{3,2,1,0:T(8,128)(2,1)S(1)}, u32[]{:S(2)}, u32[]{:S(2)}) collective-permute-start(bf16[3,8,16,512]{3,2,1,0:T(8,128)(2,1)S(1)} %slice.158), channel_id=1, source_target_pairs={{0,4},{2,6},{4,8},{6,10},{8,12},{10,14},{1,5},{3,7},{5,9},{7,11},{... | collective-permute-start | bytes 1179656 | tf_op jit(solution)/shard_map/ppermute | solution.py:260
  63.1 14.2 %collective-permute-start.21 = (bf16[3,4,16,512]{3,2,1,0:T(8,128)(2,1)S(1)}, bf16[3,4,16,512]{3,2,1,0:T(8,128)(2,1)S(1)}, u32[]{:S(2)}, u32[]{:S(2)}) collective-permute-start(bf16[3,4,16,512]{3,2,1,0:T(8,128)(2,1)S(1)} %slice.170), channel_id=1, source_target_pairs={{0,4},{2,6},{4,8},{6,10},{8,12},{10,14},{1,5},{3,7},{5,9},{7,11},{... | collective-permute-start | bytes 589832 | tf_op jit(solution)/shard_map/ppermute | solution.py:260
  70.2 1.3 collective-permute-start.12
  79.9 1.3 collective-permute-start.22
  83.0 9.0 %collective-permute-start.23 = (bf16[4,16,512]{2,1,0:T(8,128)(2,1)S(1)}, bf16[4,16,512]{2,1,0:T(8,128)(2,1)S(1)}, u32[]{:S(2)}, u32[]{:S(2)}) collective-permute-start(bf16[4,16,512]{2,1,0:T(8,128)(2,1)S(1)} %get-tuple-element.55), channel_id=1, source_target_pairs={{0,4},{2,6},{4,0},{6,2},{8,12},{10,14},{12,8},{14,10},{1,5},{3,7},... | collective-permute-start | bytes 196616 | tf_op jit(solution)/shard_map/ppermute | solution.py:283
  85.6 7.7 %collective-permute-start.24 = (bf16[4,16,512]{2,1,0:T(8,128)(2,1)S(1)}, bf16[4,16,512]{2,1,0:T(8,128)(2,1)S(1)}, u32[]{:S(2)}, u32[]{:S(2)}) collective-permute-start(bf16[4,16,512]{2,1,0:T(8,128)(2,1)S(1)} %get-tuple-element.54), channel_id=1, source_target_pairs={{0,8},{2,10},{4,12},{6,14},{8,0},{10,2},{12,4},{14,6},{1,9},{3,11}... | collective-permute-start | bytes 196616 | tf_op jit(solution)/shard_map/ppermute | solution.py:283
  87.6 6.8 %collective-permute-start.25 = (bf16[4,16,512]{2,1,0:T(8,128)(2,1)S(1)}, bf16[4,16,512]{2,1,0:T(8,128)(2,1)S(1)}, u32[]{:S(2)}, u32[]{:S(2)}) collective-permute-start(bf16[4,16,512]{2,1,0:T(8,128)(2,1)S(1)} %get-tuple-element.53), channel_id=1, source_target_pairs={{0,12},{2,14},{4,8},{6,10},{8,4},{10,6},{12,0},{14,2},{1,13},{3,15... | collective-permute-start | bytes 196616 | tf_op jit(solution)/shard_map/ppermute | solution.py:283
  88.6 11.2 %collective-permute-start.13 = (bf16[4,32,512]{2,1,0:T(8,128)(2,1)S(1)}, bf16[4,32,512]{2,1,0:T(8,128)(2,1)S(1)}, u32[]{:S(2)}, u32[]{:S(2)}) collective-permute-start(bf16[4,32,512]{2,1,0:T(8,128)(2,1)S(1)} %get-tuple-element.45), channel_id=1, source_target_pairs={{0,4},{2,6},{4,0},{6,2},{8,12},{10,14},{12,8},{14,10},{1,5},{3,7},... | collective-permute-start | bytes 393224 | tf_op jit(solution)/shard_map/ppermute | solution.py:283
  89.2 17.3 %collective-permute-start.14 = (bf16[4,32,512]{2,1,0:T(8,128)(2,1)S(1)}, bf16[4,32,512]{2,1,0:T(8,128)(2,1)S(1)}, u32[]{:S(2)}, u32[]{:S(2)}) collective-permute-start(bf16[4,32,512]{2,1,0:T(8,128)(2,1)S(1)} %get-tuple-element.44), channel_id=1, source_target_pairs={{0,8},{2,10},{4,12},{6,14},{8,0},{10,2},{12,4},{14,6},{1,9},{3,11}... | collective-permute-start | bytes 393224 | tf_op jit(solution)/shard_map/ppermute | solution.py:283
  92.1 14.5 %collective-permute-start.15 = (bf16[4,32,512]{2,1,0:T(8,128)(2,1)S(1)}, bf16[4,32,512]{2,1,0:T(8,128)(2,1)S(1)}, u32[]{:S(2)}, u32[]{:S(2)}) collective-permute-start(bf16[4,32,512]{2,1,0:T(8,128)(2,1)S(1)} %get-tuple-element.43), channel_id=1, source_target_pairs={{0,12},{2,14},{4,8},{6,10},{8,4},{10,6},{12,0},{14,2},{1,13},{3,15... | collective-permute-start | bytes 393224 | tf_op jit(solution)/shard_map/ppermute | solution.py:283
  96.3 17.6 %collective-permute-start.26 = (bf16[4,16,512]{2,1,0:T(8,128)(2,1)S(1)}, bf16[4,16,512]{2,1,0:T(8,128)(2,1)S(1)}, u32[]{:S(2)}, u32[]{:S(2)}) collective-permute-start(bf16[4,16,512]{2,1,0:T(8,128)(2,1)S(1)} %get-tuple-element.30), channel_id=1, source_target_pairs={{0,4},{2,6},{4,0},{6,2},{8,12},{10,14},{12,8},{14,10},{1,5},{3,7},... | collective-permute-start | bytes 196616 | tf_op jit(solution)/shard_map/ppermute | solution.py:292
  97.8 17.5 %collective-permute-start.27 = (bf16[4,16,512]{2,1,0:T(8,128)(2,1)S(1)}, bf16[4,16,512]{2,1,0:T(8,128)(2,1)S(1)}, u32[]{:S(2)}, u32[]{:S(2)}) collective-permute-start(bf16[4,16,512]{2,1,0:T(8,128)(2,1)S(1)} %get-tuple-element.31), channel_id=1, source_target_pairs={{0,8},{2,10},{4,12},{6,14},{8,0},{10,2},{12,4},{14,6},{1,9},{3,11}... | collective-permute-start | bytes 196616 | tf_op jit(solution)/shard_map/ppermute | solution.py:292
  99.8 15.5 %collective-permute-start.28 = (bf16[4,16,512]{2,1,0:T(8,128)(2,1)S(1)}, bf16[4,16,512]{2,1,0:T(8,128)(2,1)S(1)}, u32[]{:S(2)}, u32[]{:S(2)}) collective-permute-start(bf16[4,16,512]{2,1,0:T(8,128)(2,1)S(1)} %get-tuple-element.32), channel_id=1, source_target_pairs={{0,12},{2,14},{4,8},{6,10},{8,4},{10,6},{12,0},{14,2},{1,13},{3,15... | collective-permute-start | bytes 196616 | tf_op jit(solution)/shard_map/ppermute | solution.py:292
  109.2 7.9 %collective-permute-start.16 = (bf16[4,32,512]{2,1,0:T(8,128)(2,1)S(1)}, bf16[4,32,512]{2,1,0:T(8,128)(2,1)S(1)}, u32[]{:S(2)}, u32[]{:S(2)}) collective-permute-start(bf16[4,32,512]{2,1,0:T(8,128)(2,1)S(1)} %get-tuple-element.25), channel_id=1, source_target_pairs={{0,4},{2,6},{4,0},{6,2},{8,12},{10,14},{12,8},{14,10},{1,5},{3,7},... | collective-permute-start | bytes 393224 | tf_op jit(solution)/shard_map/ppermute | solution.py:292
  112.6 12.6 %collective-permute-start.17 = (bf16[4,32,512]{2,1,0:T(8,128)(2,1)S(1)}, bf16[4,32,512]{2,1,0:T(8,128)(2,1)S(1)}, u32[]{:S(2)}, u32[]{:S(2)}) collective-permute-start(bf16[4,32,512]{2,1,0:T(8,128)(2,1)S(1)} %get-tuple-element.26), channel_id=1, source_target_pairs={{0,8},{2,10},{4,12},{6,14},{8,0},{10,2},{12,4},{14,6},{1,9},{3,11}... | collective-permute-start | bytes 393224 | tf_op jit(solution)/shard_map/ppermute | solution.py:292
  113.8 11.4 %collective-permute-start.18 = (bf16[4,32,512]{2,1,0:T(8,128)(2,1)S(1)}, bf16[4,32,512]{2,1,0:T(8,128)(2,1)S(1)}, u32[]{:S(2)}, u32[]{:S(2)}) collective-permute-start(bf16[4,32,512]{2,1,0:T(8,128)(2,1)S(1)} %get-tuple-element.27), channel_id=1, source_target_pairs={{0,12},{2,14},{4,8},{6,10},{8,4},{10,6},{12,0},{14,2},{1,13},{3,15... | collective-permute-start | bytes 393224 | tf_op jit(solution)/shard_map/ppermute | solution.py:292
  125.3 6.6 %collective-permute-start.19 = (bf16[2,128,512]{2,1,0:T(8,128)(2,1)S(1)}, bf16[2,128,512]{2,1,0:T(8,128)(2,1)S(1)}, u32[]{:S(2)}, u32[]{:S(2)}) collective-permute-start(bf16[2,128,512]{2,1,0:T(8,128)(2,1)S(1)} %bitcast.131), channel_id=1, source_target_pairs={{0,2},{2,0},{4,6},{6,4},{8,10},{10,8},{12,14},{14,12},{1,3},{3,1},... | collective-permute-start | bytes 786440 | tf_op jit(solution)/shard_map/ppermute | solution.py:220
  126.9 6.4 %collective-permute-start.29 = (bf16[2,64,512]{2,1,0:T(8,128)(2,1)S(1)}, bf16[2,64,512]{2,1,0:T(8,128)(2,1)S(1)}, u32[]{:S(2)}, u32[]{:S(2)}) collective-permute-start(bf16[2,64,512]{2,1,0:T(8,128)(2,1)S(1)} %bitcast.133), channel_id=1, source_target_pairs={{0,2},{2,0},{4,6},{6,4},{8,10},{10,8},{12,14},{14,12},{1,3},{3,1},... | collective-permute-start | bytes 393224 | tf_op jit(solution)/shard_map/ppermute | solution.py:220
  (15 other events, 100.6 us)

commit v2 on v1

v2 whole, which is shorter than its diff:
```python
from functools import partial

import jax
import jax.numpy as jnp
from jax import lax
from jax.experimental import pallas as pl
from jax.experimental.pallas import tpu as pltpu
from jax.sharding import PartitionSpec as P

epsilon = 1e-06
parts = 2
taps = 3
vmem_bytes = 48 * 1024 * 1024

VMEM = pl.BlockSpec(memory_space=pltpu.VMEM)
SMEM = pl.BlockSpec(memory_space=pltpu.SMEM)


def silu(v):
    return 0.5 * v * (1.0 + jnp.tanh(0.5 * v))


def dot32(a, b):
    return jnp.dot(a, b, preferred_element_type=jnp.float32)


def cost(flops, *arrays):
    size = sum(a.size * a.dtype.itemsize for a in arrays)
    return pl.CostEstimate(flops=flops, bytes_accessed=size, transcendentals=0)


def lift_kernel(started, halo, video, w_time, b_time, w_down, b_down, out, lifted):
    frames, rows, width, channels = video.shape
    pixels = rows * width

    def frame(t):
        ref, index = (halo, t + taps) if t < 0 else (video, t)
        return ref[index].reshape(pixels, channels)

    for t in range(-1, frames):
        lhs = jnp.concatenate([frame(t - k) for k in range(taps)], axis=1)
        acc = dot32(lhs, w_time[...]) + b_time[...]
        result = frame(t).astype(jnp.float32) + silu(acc)
        if t < 0:
            result = jnp.where(started[0] > 0, result, 0.0)
        lifted[t + 1] = result.astype(jnp.bfloat16)
    for s in range(frames // 2):
        lhs = jnp.concatenate([lifted[2 * s + 2 - k] for k in range(taps)], axis=1)
        acc = dot32(lhs, w_down[...]) + b_down[...]
        out[s] = acc.astype(jnp.bfloat16).reshape(rows, width, channels)


def lift(started, halo, video, w_time, b_time, w_down, b_down):
    frames, rows, width, channels = video.shape
    pixels = rows * width
    flops = 2 * taps * channels * channels * pixels * (frames + 1 + frames // 2)
    return pl.pallas_call(
        lift_kernel,
        out_shape=jax.ShapeDtypeStruct((frames // 2, rows, width, channels), jnp.bfloat16),
        in_specs=[SMEM] + [VMEM] * 6,
        out_specs=VMEM,
        scratch_shapes=[pltpu.VMEM((frames + 1, pixels, channels), jnp.bfloat16)],
        compiler_params=pltpu.CompilerParams(vmem_limit_bytes=vmem_bytes),
        cost_estimate=cost(flops, halo, video, w_time, w_down),
        name="lift",
    )(started, halo, video, w_time, b_time, w_down, b_down)


def space_kernel(left, middle, right, weights, bias, out):
    halves, rows, width, channels = out.shape
    pixels = rows * width
    sources = (left, middle, right)
    for s in range(halves):

        def window(source, a):
            return source[s, a : a + rows].reshape(pixels, channels)

        lhs = jnp.concatenate([window(v, a) for a in range(3) for v in sources], axis=1)
        acc = dot32(lhs, weights[...]) + bias[...]
        result = window(middle, 1).astype(jnp.float32) + silu(acc)
        out[s] = result.astype(jnp.bfloat16).reshape(rows, width, channels)


def space(left, middle, right, weights, bias):
    halves, rows, width, channels = middle.shape
    rows = rows - 2
    flops = 2 * 9 * channels * channels * halves * rows * width
    return pl.pallas_call(
        space_kernel,
        out_shape=jax.ShapeDtypeStruct((halves, rows, width, channels), jnp.bfloat16),
        in_specs=[VMEM] * 5,
        out_specs=VMEM,
        compiler_params=pltpu.CompilerParams(vmem_limit_bytes=vmem_bytes),
        cost_estimate=cost(flops, left, middle, right, weights),
        name="space",
    )(left, middle, right, weights, bias)


def attend_kernel(frames_per, lanes, count, first, *refs):
    blocks = refs[:count]
    gain, w_query, w_key, w_value, w_out = refs[count : count + 5]
    outs = refs[count + 5 :]
    channels = gain.shape[-1]
    flat = len(blocks[0].shape) == 2
    groups = 1 if flat else blocks[0].shape[1] // lanes
    each = frames_per * lanes
    size = count * each

    def piece(ref, g):
        if flat:
            return ref[...]
        return ref[:, g * lanes : (g + 1) * lanes].reshape(each, channels)

    def place(index):
        block = index // each
        frame = index // lanes % frames_per
        time = frame
        for j in range(count):
            time = time + jnp.where(block == j, first[j], 0)
        return time, index % lanes

    row_time, row_lane = place(lax.broadcasted_iota(jnp.int32, (size, 1), 0))
    col_time, col_lane = place(lax.broadcasted_iota(jnp.int32, (1, size), 1))
    allowed = (row_lane == col_lane) & (col_time <= row_time)
    x = jnp.concatenate([piece(b, g) for g in range(groups) for b in blocks], axis=0)
    wide = x.astype(jnp.float32)
    scale = lax.rsqrt(jnp.mean(wide * wide, axis=-1, keepdims=True) + epsilon)
    normed = (wide * scale * gain[...]).astype(jnp.bfloat16)
    query = dot32(normed, w_query[...]).astype(jnp.bfloat16)
    key = dot32(normed, w_key[...]).astype(jnp.bfloat16)
    value = dot32(normed, w_value[...]).astype(jnp.bfloat16)
    contexts = []
    for g in range(groups):
        part = slice(g * size, (g + 1) * size)
        scores = lax.dot_general(
            query[part], key[part], (((1,), (1,)), ((), ())), preferred_element_type=jnp.float32
        )
        scores = jnp.where(allowed, scores * channels ** (-0.5), -1e30)
        largest = jnp.max(scores, axis=-1, keepdims=True)
        probs = jnp.exp(scores - largest)
        probs = (probs / jnp.sum(probs, axis=-1, keepdims=True)).astype(jnp.bfloat16)
        contexts.append(dot32(probs, value[part]).astype(jnp.bfloat16))
    mixed = dot32(jnp.concatenate(contexts, axis=0), w_out[...])
    result = (wide + mixed).astype(jnp.bfloat16)
    for g in range(groups):
        for j, out in enumerate(outs):
            begin = g * size + j * each
            rows = result[begin : begin + each]
            if flat:
                out[...] = rows
            else:
                out[:, g * lanes : (g + 1) * lanes] = rows.reshape(frames_per, lanes, channels)


def attend(first, blocks, gain, w_query, w_key, w_value, w_out):
    frames_per, pixels, channels = blocks[0].shape
    lanes = 16 if pixels % 16 == 0 else pixels
    flat = pixels % 16 != 0
    if flat:
        blocks = [b.reshape(frames_per * pixels, channels) for b in blocks]
    count = len(blocks)
    rows = frames_per * pixels * count
    flops = 2 * rows * channels * (4 * channels + 2 * frames_per * count * lanes)
    outs = pl.pallas_call(
        partial(attend_kernel, frames_per, lanes, count),
        out_shape=[jax.ShapeDtypeStruct(b.shape, jnp.bfloat16) for b in blocks],
        in_specs=[SMEM] + [VMEM] * (count + 5),
        out_specs=[VMEM] * count,
        compiler_params=pltpu.CompilerParams(vmem_limit_bytes=vmem_bytes),
        cost_estimate=cost(flops, *blocks, w_query, w_key, w_value, w_out),
        name="attend",
    )(first, *blocks, gain, w_query, w_key, w_value, w_out)
    return [o.reshape(frames_per, pixels, channels) for o in outs]


def after(value, other):
    return lax.optimization_barrier((value, other))[0]


def per_device(
    video, w_time, b_time, w_down, b_down, w_space, b_space, gain, w_query, w_key, w_value, w_out
):
    frames, height, width, channels = video.shape
    devices = lax.axis_size("tm")
    columns = lax.axis_size("cols")
    place = lax.axis_index("tm")
    column = lax.axis_index("cols")
    halves = frames // 2
    started = place.astype(jnp.int32).reshape(1)
    first = jnp.zeros((1,), jnp.int32)
    w_time = w_time.reshape(-1, channels)
    w_down = w_down.reshape(-1, channels)
    w_space = w_space.reshape(-1, channels)
    b_time, b_down, b_space, gain = (v.reshape(1, -1) for v in (b_time, b_down, b_space, gain))
    onward = [(i, i + 1) for i in range(devices - 1)]

    def beside(value):
        last, head = value[:, :, -1:], value[:, :, :1]
        if columns == 2:
            other = lax.ppermute(jnp.where(column == 0, last, head), "cols", [(0, 1), (1, 0)])
            return jnp.where(column == 1, other, 0), jnp.where(column == 0, other, 0)
        up = [(i, i + 1) for i in range(columns - 1)]
        return lax.ppermute(last, "cols", up), lax.ppermute(head, "cols", [(j, i) for i, j in up])

    chunks = parts if height % parts == 0 and height // parts * width % devices == 0 else 1
    size = height // chunks
    halos, newest = [], None
    for index in range(chunks):
        begin = index * size + (1 if index else 0)
        end = min((index + 1) * size + 1, height)
        sent = video[frames - taps :, begin:end]
        if newest is not None:
            sent = after(sent, newest)
        newest = lax.ppermute(sent, "tm", onward)
        halos.append((begin, end, newest))

    spatials, kept = [], None
    for index, (begin, end, halo) in enumerate(halos):
        own = video[:, begin:end]
        if spatials:
            own = after(own, spatials[-1])
        reduced = lift(started, halo, own, w_time, b_time, w_down, b_down)
        left, right = beside(reduced)
        pieces = (left, reduced, right)
        if kept is None:
            kept = tuple(jnp.zeros_like(p[:, :1]) for p in pieces)
        pieces = tuple(jnp.concatenate(pq, axis=1) for pq in zip(kept, pieces))
        if index == chunks - 1:
            pieces = tuple(jnp.pad(p, ((0, 0), (0, 1), (0, 0), (0, 0))) for p in pieces)
        kept = tuple(p[:, -2:] for p in pieces)
        left, middle, right = pieces
        to_right = jnp.concatenate([left, middle[:, :, :-1]], axis=2)
        to_left = jnp.concatenate([middle[:, :, 1:], right], axis=2)
        spatials.append(space(to_right, middle, to_left, w_space, b_space))

    gathers = [
        lax.all_to_all(s.reshape(halves, size * width, channels), "tm", 1, 0, tiled=True)
        for s in spatials
    ]
    returns, newest = [], spatials[-1]
    for block in gathers:
        block = after(block, newest)
        (newest,) = attend(first, [block], gain, w_query, w_key, w_value, w_out)
        returns.append(lax.all_to_all(newest, "tm", 0, 1, tiled=True))
    encoded = jnp.concatenate(returns, axis=1)
    return encoded.reshape(halves, height, width, channels)


def solution(mesh):
    spread = P(("clips", "tm"), None, "cols", None)
    return jax.shard_map(
        per_device,
        mesh=mesh,
        in_specs=(spread,) + (P(),) * 11,
        out_specs=spread,
        check_vma=False,
    )
```

time: 136 us -> 129 us (0.949)
  starting transfers between devices: 47.8 us -> 29.7 us
  local copies, waits for them, and re-layouts: 3.92 us -> 16.2 us
  waiting for transfers between devices: 51.6 us -> 57 us
  other arithmetic: 6.73 us -> 2.61 us
    ppermute x30 -> x4, starting transfers between devices: 47.8 us -> 9.38 us  [the longest x2 9.24 us: per_device(): newest = lax.ppermute(sent, 'tm', onward)]
    all_to_all x0 -> x4, waiting for transfers between devices: none -> 36.5 us  [the longest x2 26.3 us: per_device(): returns.append(lax.all_to_all(newest, 'tm', 0, 1, tiled=True))]
    ppermute x30 -> x4, waiting for transfers between devices: 51.6 us -> 20.5 us  [the longest x2 19.6 us: per_device(): newest = lax.ppermute(sent, 'tm', onward)]
    all_to_all x0 -> x4, starting transfers between devices: none -> 20.4 us  [the longest x2 13.1 us: per_device(): lax.all_to_all(s.reshape(halves, size * width, channels), 'tm', 1, 0, til...]
    slice x11 -> x8, local copies, waits for them, and re-layouts: 2.24 us -> 6.78 us  [the longest x2 4.15 us: per_device(): sent = video[frames - taps:, begin:end]]
    unnamed x34 -> x26, local copies, waits for them, and re-layouts: 1.07 us -> 4.77 us
    select_n x12 -> x2, other arithmetic: 3.36 us -> 0.22 us  [beside(): jnp.where(column == 0, last, head)]
    reshape x0 -> x2, local copies, waits for them, and re-layouts: none -> 2.68 us  [per_device(): s.reshape(halves, size * width, channels)]
  transfers between devices with their start and end apart: 30 -> 8, of which waited for: 19 -> 6; matrix products, arithmetic and copies ran while one was open for 3% -> 8% of each run, Pallas kernels for 11% -> 15%
where the time goes in v2:
time: 129 us; the launch traced here: 128 us
  waiting for transfers between devices  57 us (44%)
  starting transfers between devices  29.7 us (23%)
  Pallas kernels  22.3 us (17%)
  local copies, waits for them, and re-layouts  16.2 us (13%)
  other arithmetic  2.61 us (2%)
    all_to_all x2, waiting for transfers between devices, per_device(): returns.append(lax.all_to_all(newest, 'tm', 0, 1, tiled=True))  26.3 us
    ppermute x2, waiting for transfers between devices, per_device(): newest = lax.ppermute(sent, 'tm', onward)  19.6 us
    all_to_all x2, starting transfers between devices, per_device(): lax.all_to_all(s.reshape(halves, size * width, channels), 'tm', 1, 0, til...  13.1 us
    all_to_all x2, waiting for transfers between devices, per_device(): lax.all_to_all(s.reshape(halves, size * width, channels), 'tm', 1, 0, til...  10.2 us
    pallas_call x2, Pallas kernels, space(): pl.pallas_call(space_kernel, out_shape=jax.ShapeDtypeStruct((halves, rows...  10.1 us
    ppermute x2, starting transfers between devices, per_device(): newest = lax.ppermute(sent, 'tm', onward)  9.24 us
    all_to_all x2, starting transfers between devices, per_device(): returns.append(lax.all_to_all(newest, 'tm', 0, 1, tiled=True))  7.27 us
    pallas_call x2, Pallas kernels, lift(): pl.pallas_call(lift_kernel, out_shape=jax.ShapeDtypeStruct((frames // 2,...  6.45 us
  transfers between devices with their start and end apart: 8, of which 6 were waited for; matrix products, arithmetic and copies ran while one was open for 8% of the time, Pallas kernels for 15%

profile of v2, /device:TPU:0, one launch (start us, length us, event | category | flops | bytes accessed | tf_op | source)
XLA Modules:
  0.0 128.2 jit_solution(12934424178228722278)
XLA Ops:
  0.0 2.1 %slice.45 = bf16[3,17,16,512]{3,2,1,0:T(8,128)(2,1)} slice(bf16[4,32,16,512]{3,2,1,0:T(8,128)(2,1)} %param.12), slice={[1:4], [0:17], [0:16], [0:512]} | slice | bytes 1671168 | tf_op jit(solution)/shard_map/slice | solution.py:211
  2.1 4.9 %collective-permute-start = (bf16[3,17,16,512]{3,2,1,0:T(8,128)(2,1)}, bf16[3,17,16,512]{3,2,1,0:T(8,128)(2,1)S(1)}, u32[]{:S(2)}, u32[]{:S(2)}) collective-permute-start(bf16[3,17,16,512]{3,2,1,0:T(8,128)(2,1)} %slice.45), channel_id=1, source_target_pairs={{0,2},{2,4},{4,6},{6,8},{8,10},{10,12},{12,14},{1,3},{3,5},{5,7},{... | collective-permute-start | bytes 2506760 | tf_op jit(solution)/shard_map/ppermute | solution.py:214
  7.0 1.3 %slice.46.video = bf16[4,17,16,512]{3,2,1,0:T(8,128)(2,1)S(1)} slice(bf16[4,32,16,512]{3,2,1,0:T(8,128)(2,1)} %param.12), slice={[0:4], [0:17], [0:16], [0:512]} | slice | bytes 2228224 | tf_op jit(solution)/shard_map/slice | solution.py:219
  8.4 1.3 slice.53.video
  9.7 2.1 %slice.52 = bf16[3,15,16,512]{3,2,1,0:T(8,128)(2,1)} slice(bf16[4,32,16,512]{3,2,1,0:T(8,128)(2,1)} %param.12), slice={[1:4], [17:32], [0:16], [0:512]} | slice | bytes 1474560 | tf_op jit(solution)/shard_map/slice | solution.py:211
  11.7 13.4 %collective-permute-done.halo = bf16[3,17,16,512]{3,2,1,0:T(8,128)(2,1)S(1)} collective-permute-done((bf16[3,17,16,512]{3,2,1,0:T(8,128)(2,1)}, bf16[3,17,16,512]{3,2,1,0:T(8,128)(2,1)S(1)}, u32[]{:S(2)}, u32[]{:S(2)}) %collective-permute-start) | collective-permute-done | bytes 835616 | tf_op jit(solution)/shard_map/ppermute | solution.py:214
  25.1 1.4 %copy-done.1 = bf16[3,512,512]{2,1,0:T(8,128)(2,1)S(1)} copy-done((bf16[3,512,512]{2,1,0:T(8,128)(2,1)S(1)}, bf16[3,512,512]{2,1,0:T(8,128)(2,1)}, u32[]{:S(2)}) %copy-start.1) | copy-done | bytes 1572888
  26.5 1.4 %copy-done.3 = bf16[3,512,512]{2,1,0:T(8,128)(2,1)S(1)} copy-done((bf16[3,512,512]{2,1,0:T(8,128)(2,1)S(1)}, bf16[3,512,512]{2,1,0:T(8,128)(2,1)}, u32[]{:S(2)}) %copy-start.3) | copy-done | bytes 1572888
  27.9 3.5 %lift.2 = bf16[2,17,16,512]{3,2,1,0:T(8,128)(2,1)S(1)} custom-call(s32[1]{0:T(128)} %bitcast.started, bf16[3,17,16,512]{3,2,1,0:T(8,128)(2,1)S(1)} %collective-permute-done.halo, bf16[4,17,16,512]{3,2,1,0:T(8,128)(2,1)S(1)} %slice.46.video, bf16[1536,512]{1,0:T(8,128)(2,1)S(1)} %bitcast.31, f32[1,512]{1,0:T(1,128)S(1)} %bitcast.35, ...), custom_call_target="tpu_custom_call" | custom-call | flops 2994733056 | bytes 5095424 | tf_op jit(solution)/shard_map/lift/pallas_call | solution.py:57
  31.6 4.3 %collective-permute-start.2 = (bf16[3,15,16,512]{3,2,1,0:T(8,128)(2,1)}, bf16[3,15,16,512]{3,2,1,0:T(8,128)(2,1)S(1)}, u32[]{:S(2)}, u32[]{:S(2)}) collective-permute-start(bf16[3,15,16,512]{3,2,1,0:T(8,128)(2,1)} %slice.52), channel_id=1, source_target_pairs={{0,2},{2,4},{4,6},{6,8},{8,10},{10,12},{12,14},{1,3},{3,5},{5,7},{... | collective-permute-start | bytes 2211848 | tf_op jit(solution)/shard_map/ppermute | solution.py:214
  36.4 0.5 fusion.4
  37.1 5.1 %space.2 = bf16[2,16,16,512]{3,2,1,0:T(8,128)(2,1)S(1)} custom-call(bf16[2,18,16,512]{3,2,1,0:T(8,128)(2,1)S(1)} %get-tuple-element.22.left, bf16[2,18,16,512]{3,2,1,0:T(8,128)(2,1)S(1)} %concatenate.34.middle, bf16[2,18,16,512]{3,2,1,0:T(8,128)(2,1)S(1)} %get-tuple-element.21.right, bf16[4608,512]{1,0:T(8,128)(2,1)} %bitcast.49, f32[1,512]{1,0:T(1,128)S(1)} %bitcast.39), custom_call_target="tpu_custom_call" | custom-call | flops 2415919104 | bytes 6488064 | tf_op jit(solution)/shard_map/space/pallas_call | solution.py:88
  42.2 1.3 %copy.17 = bf16[2,256,512]{2,0,1:T(2,128)(2,1)} copy(bf16[2,256,512]{2,1,0:T(8,128)(2,1)S(1)} %bitcast.27) | data formatting | bytes 1048576 | tf_op jit(solution)/shard_map/reshape | solution.py:237
  43.5 5.7 %all-to-all-start = ((bf16[2,256,512]{2,0,1:T(2,128)(2,1)}), bf16[2,256,512]{2,0,1:T(2,128)(2,1)}, u32[]{:S(2)}, u32[]{:S(2)}) async-start(bf16[2,256,512]{2,0,1:T(2,128)(2,1)} %copy.17), calls=%async_computation | async-start | bytes 1048576 | tf_op jit(solution)/shard_map/all_to_all | solution.py:237
  49.2 6.2 %collective-permute-done.2.halo = bf16[3,15,16,512]{3,2,1,0:T(8,128)(2,1)S(1)} collective-permute-done((bf16[3,15,16,512]{3,2,1,0:T(8,128)(2,1)}, bf16[3,15,16,512]{3,2,1,0:T(8,128)(2,1)S(1)}, u32[]{:S(2)}, u32[]{:S(2)}) %collective-permute-start.2) | collective-permute-done | bytes 737312 | tf_op jit(solution)/shard_map/ppermute | solution.py:214
  55.4 1.4 %copy-done.4 = bf16[3,512,512]{2,1,0:T(8,128)(2,1)S(1)} copy-done((bf16[3,512,512]{2,1,0:T(8,128)(2,1)S(1)}, bf16[3,512,512]{2,1,0:T(8,128)(2,1)}, u32[]{:S(2)}) %copy-start.4) | copy-done | bytes 1572888
  56.8 3.0 %lift.3 = bf16[2,15,16,512]{3,2,1,0:T(8,128)(2,1)S(1)} custom-call(s32[1]{0:T(128)} %bitcast.started, bf16[3,15,16,512]{3,2,1,0:T(8,128)(2,1)S(1)} %collective-permute-done.2.halo, bf16[4,15,16,512]{3,2,1,0:T(8,128)(2,1)S(1)} %slice.53.video, bf16[1536,512]{1,0:T(8,128)(2,1)S(1)} %bitcast.32, f32[1,512]{1,0:T(1,128)S(1)} %bitcast.36, ...), custom_call_target="tpu_custom_call" | custom-call | flops 2642411520 | bytes 4866048 | tf_op jit(solution)/shard_map/lift/pallas_call | solution.py:57
  60.0 0.2 fusion.7
  60.3 0.9 collective-permute-done.3
  61.7 0.3 pad_maximum_fusion.1.left
  61.9 5.0 %space.3 = bf16[2,16,16,512]{3,2,1,0:T(8,128)(2,1)S(1)} custom-call(bf16[2,18,16,512]{3,2,1,0:T(8,128)(2,1)S(1)} %pad_maximum_fusion.1.left, bf16[2,18,16,512]{3,2,1,0:T(8,128)(2,1)S(1)} %fusion.6.middle, bf16[2,18,16,512]{3,2,1,0:T(8,128)(2,1)S(1)} %pad_maximum_fusion.2.right, bf16[4608,512]{1,0:T(8,128)(2,1)} %bitcast.50, f32[1,512]{1,0:T(1,128)S(1)} %bitcast.40), custom_call_target="tpu_custom_call" | custom-call | flops 2415919104 | bytes 6488064 | tf_op jit(solution)/shard_map/space/pallas_call | solution.py:88
  67.0 1.3 %copy.21 = bf16[2,256,512]{2,0,1:T(2,128)(2,1)} copy(bf16[2,256,512]{2,1,0:T(8,128)(2,1)S(1)} %bitcast.28) | data formatting | bytes 1048576 | tf_op jit(solution)/shard_map/reshape | solution.py:237
  68.3 7.4 %all-to-all-start.2 = ((bf16[2,256,512]{2,0,1:T(2,128)(2,1)}), bf16[2,256,512]{2,0,1:T(2,128)(2,1)S(1)}, u32[]{:S(2)}, u32[]{:S(2)}) async-start(bf16[2,256,512]{2,0,1:T(2,128)(2,1)} %copy.21), calls=%async_computation.2 | async-start | bytes 1048576 | tf_op jit(solution)/shard_map/all_to_all | solution.py:237
  75.8 1.2 copy.18
  77.4 2.9 %attend.2 = bf16[16,32,512]{2,1,0:T(8,128)(2,1)} custom-call(s32[1]{0:T(128)} %constant.6.clone.1.first, bf16[16,32,512]{2,1,0:T(8,128)(2,1)S(1)} %bitcast.30, f32[1,512]{1,0:T(1,128)S(1)} %bitcast.41, bf16[512,512]{1,0:T(8,128)(2,1)S(1)} %copy-done.5, bf16[512,512]{1,0:T(8,128)(2,1)S(1)} %copy-done.6, bf16[512,512]{1,0:T(8,128)(2,1)S(1)} %copy-done.7, ...), custom_call_target="tpu_custom_call" | custom-call | flops 1342177280 | bytes 2621440 | tf_op jit(solution)/shard_map/attend/pallas_call | solution.py:164
  80.3 10.2 %all-to-all-done.2 = bf16[2,256,512]{2,0,1:T(2,128)(2,1)S(1)} async-done(((bf16[2,256,512]{2,0,1:T(2,128)(2,1)}), bf16[2,256,512]{2,0,1:T(2,128)(2,1)S(1)}, u32[]{:S(2)}, u32[]{:S(2)}) %all-to-all-start.2) | async-done | bytes 524320 | tf_op jit(solution)/shard_map/all_to_all | solution.py:237
  90.5 3.6 %all-to-all-start.1 = ((bf16[16,32,512]{2,1,0:T(8,128)(2,1)}), bf16[16,32,512]{2,1,0:T(8,128)(2,1)S(1)}, u32[]{:S(2)}, u32[]{:S(2)}) async-start(bf16[16,32,512]{2,1,0:T(8,128)(2,1)} %attend.2), calls=%async_computation.1 | async-start | bytes 1048576 | tf_op jit(solution)/shard_map/all_to_all | solution.py:244
  94.3 2.9 %attend.3 = bf16[16,32,512]{2,1,0:T(8,128)(2,1)} custom-call(s32[1]{0:T(128)} %constant.6.clone.1.first, bf16[16,32,512]{2,1,0:T(8,128)(2,1)S(1)} %bitcast.29, f32[1,512]{1,0:T(1,128)S(1)} %bitcast.42, bf16[512,512]{1,0:T(8,128)(2,1)S(1)} %copy-done.5, bf16[512,512]{1,0:T(8,128)(2,1)S(1)} %copy-done.6, bf16[512,512]{1,0:T(8,128)(2,1)S(1)} %copy-done.7, ...), custom_call_target="tpu_custom_call" | custom-call | flops 1342177280 | bytes 2621440 | tf_op jit(solution)/shard_map/attend/pallas_call | solution.py:164
  97.2 11.7 %all-to-all-done.1 = bf16[16,32,512]{2,1,0:T(8,128)(2,1)S(1)} async-done(((bf16[16,32,512]{2,1,0:T(8,128)(2,1)}), bf16[16,32,512]{2,1,0:T(8,128)(2,1)S(1)}, u32[]{:S(2)}, u32[]{:S(2)}) %all-to-all-start.1) | async-done | bytes 524320 | tf_op jit(solution)/shard_map/all_to_all | solution.py:244
  108.8 3.6 %all-to-all-start.3 = ((bf16[16,32,512]{2,1,0:T(8,128)(2,1)}), bf16[16,32,512]{2,1,0:T(8,128)(2,1)S(1)}, u32[]{:S(2)}, u32[]{:S(2)}) async-start(bf16[16,32,512]{2,1,0:T(8,128)(2,1)} %attend.3), calls=%async_computation.3 | async-start | bytes 1048576 | tf_op jit(solution)/shard_map/all_to_all | solution.py:244
  112.5 14.6 %all-to-all-done.3 = bf16[16,32,512]{2,1,0:T(8,128)(2,1)S(1)} async-done(((bf16[16,32,512]{2,1,0:T(8,128)(2,1)}), bf16[16,32,512]{2,1,0:T(8,128)(2,1)S(1)}, u32[]{:S(2)}, u32[]{:S(2)}) %all-to-all-start.3) | async-done | bytes 524320 | tf_op jit(solution)/shard_map/all_to_all | solution.py:244
  127.2 1.0 pad_maximum_fusion
  (46 shorter events, 2.0 us)
Async XLA Ops:
  2.1 23.0 %collective-permute-start = (bf16[3,17,16,512]{3,2,1,0:T(8,128)(2,1)}, bf16[3,17,16,512]{3,2,1,0:T(8,128)(2,1)S(1)}, u32[]{:S(2)}, u32[]{:S(2)}) collective-permute-start(bf16[3,17,16,512]{3,2,1,0:T(8,128)(2,1)} %slice.45), channel_id=1, source_target_pairs={{0,2},{2,4},{4,6},{6,8},{8,10},{10,12},{12,14},{1,3},{3,5},{5,7},{... | collective-permute-start | bytes 2506760 | tf_op jit(solution)/shard_map/ppermute | solution.py:214
  9.6 15.5 %copy-start.9 = (f32[512]{0:T(512)S(1)}, f32[512]{0:T(512)}, u32[]{:S(2)}) copy-start(f32[512]{0:T(512)} %param.14) | copy-start | bytes 6148
  9.6 15.5 %copy-start.10 = (f32[512]{0:T(512)S(1)}, f32[512]{0:T(512)}, u32[]{:S(2)}) copy-start(f32[512]{0:T(512)} %param.16) | copy-start | bytes 6148
  25.1 1.4 %copy-start.1 = (bf16[3,512,512]{2,1,0:T(8,128)(2,1)S(1)}, bf16[3,512,512]{2,1,0:T(8,128)(2,1)}, u32[]{:S(2)}) copy-start(bf16[3,512,512]{2,1,0:T(8,128)(2,1)} %param.13) | copy-start | bytes 4718596
  26.5 1.4 %copy-start.3 = (bf16[3,512,512]{2,1,0:T(8,128)(2,1)S(1)}, bf16[3,512,512]{2,1,0:T(8,128)(2,1)}, u32[]{:S(2)}) copy-start(bf16[3,512,512]{2,1,0:T(8,128)(2,1)} %param.15) | copy-start | bytes 4718596
  31.4 4.8 %copy-start = (bf16[2,17,16,512]{3,2,1,0:T(8,128)(2,1)}, bf16[2,17,16,512]{3,2,1,0:T(8,128)(2,1)S(1)}, u32[]{:S(2)}) copy-start(bf16[2,17,16,512]{3,2,1,0:T(8,128)(2,1)S(1)} %lift.2) | copy-start | bytes 1671172
  31.6 4.7 %collective-permute-start.1 = (bf16[2,17,1,512]{3,2,1,0:T(2,128)(2,1)S(1)}, bf16[2,17,1,512]{3,2,1,0:T(2,128)(2,1)S(1)}, u32[]{:S(2)}, u32[]{:S(2)}) collective-permute-start(bf16[2,17,1,512]{3,2,1,0:T(2,128)(2,1)S(1)} %broadcast_select_fusion.1), channel_id=1, source_target_pairs={{0,1},{1,0},{2,3},{3,2},{4,5},{5,4},{6,7},{7,6},{8,9},{9,8},{10,11... | collective-permute-start | bytes 104456 | tf_op jit(solution)/shard_map/ppermute | solution.py:200
  31.6 23.8 %collective-permute-start.2 = (bf16[3,15,16,512]{3,2,1,0:T(8,128)(2,1)}, bf16[3,15,16,512]{3,2,1,0:T(8,128)(2,1)S(1)}, u32[]{:S(2)}, u32[]{:S(2)}) collective-permute-start(bf16[3,15,16,512]{3,2,1,0:T(8,128)(2,1)} %slice.52), channel_id=1, source_target_pairs={{0,2},{2,4},{4,6},{6,8},{8,10},{10,12},{12,14},{1,3},{3,5},{5,7},{... | collective-permute-start | bytes 2211848 | tf_op jit(solution)/shard_map/ppermute | solution.py:214
  36.4 0.7 copy-start.11
  42.2 13.2 %copy-start.2 = (bf16[3,512,512]{2,1,0:T(8,128)(2,1)S(1)}, bf16[3,512,512]{2,1,0:T(8,128)(2,1)}, u32[]{:S(2)}) copy-start(bf16[3,512,512]{2,1,0:T(8,128)(2,1)} %param.13) | copy-start | bytes 4718596
  43.5 24.8 %all-to-all-start = ((bf16[2,256,512]{2,0,1:T(2,128)(2,1)}), bf16[2,256,512]{2,0,1:T(2,128)(2,1)}, u32[]{:S(2)}, u32[]{:S(2)}) async-start(bf16[2,256,512]{2,0,1:T(2,128)(2,1)} %copy.17), calls=%async_computation | async-start | bytes 1048576 | tf_op jit(solution)/shard_map/all_to_all | solution.py:237
  49.2 10.8 %slice-start = ((bf16[2,17,16,512]{3,2,1,0:T(8,128)(2,1)}), bf16[2,2,16,512]{3,2,1,0:T(8,128)(2,1)S(1)}, s32[]{:S(2)}) async-start(bf16[2,17,16,512]{3,2,1,0:T(8,128)(2,1)} %copy-done), calls=%async_computation.4 | async-start | bytes 131072 | tf_op jit(solution)/shard_map/slice | solution.py:230
  55.4 1.4 %copy-start.4 = (bf16[3,512,512]{2,1,0:T(8,128)(2,1)S(1)}, bf16[3,512,512]{2,1,0:T(8,128)(2,1)}, u32[]{:S(2)}) copy-start(bf16[3,512,512]{2,1,0:T(8,128)(2,1)} %param.15) | copy-start | bytes 4718596
  59.9 1.3 %collective-permute-start.3 = (bf16[2,15,1,512]{3,2,1,0:T(2,128)(2,1)S(1)}, bf16[2,15,1,512]{3,2,1,0:T(2,128)(2,1)S(1)}, u32[]{:S(2)}, u32[]{:S(2)}) collective-permute-start(bf16[2,15,1,512]{3,2,1,0:T(2,128)(2,1)S(1)} %broadcast_select_fusion.4), channel_id=1, source_target_pairs={{0,1},{1,0},{2,3},{3,2},{4,5},{5,4},{6,7},{7,6},{8,9},{9,8},{10,11... | collective-permute-start | bytes 92168 | tf_op jit(solution)/shard_map/ppermute | solution.py:200
  68.3 22.2 %all-to-all-start.2 = ((bf16[2,256,512]{2,0,1:T(2,128)(2,1)}), bf16[2,256,512]{2,0,1:T(2,128)(2,1)S(1)}, u32[]{:S(2)}, u32[]{:S(2)}) async-start(bf16[2,256,512]{2,0,1:T(2,128)(2,1)} %copy.21), calls=%async_computation.2 | async-start | bytes 1048576 | tf_op jit(solution)/shard_map/all_to_all | solution.py:237
  75.7 1.3 %copy-start.5 = (bf16[512,512]{1,0:T(8,128)(2,1)S(1)}, bf16[512,512]{1,0:T(8,128)(2,1)}, u32[]{:S(2)}) copy-start(bf16[512,512]{1,0:T(8,128)(2,1)} %refs_2_.3) | copy-start | bytes 1572868
  75.7 1.4 %copy-start.6 = (bf16[512,512]{1,0:T(8,128)(2,1)S(1)}, bf16[512,512]{1,0:T(8,128)(2,1)}, u32[]{:S(2)}) copy-start(bf16[512,512]{1,0:T(8,128)(2,1)} %refs_3_.3) | copy-start | bytes 1572868
  75.7 1.5 %copy-start.7 = (bf16[512,512]{1,0:T(8,128)(2,1)S(1)}, bf16[512,512]{1,0:T(8,128)(2,1)}, u32[]{:S(2)}) copy-start(bf16[512,512]{1,0:T(8,128)(2,1)} %refs_4_.3) | copy-start | bytes 1572868
  75.8 1.6 %copy-start.8 = (bf16[512,512]{1,0:T(8,128)(2,1)S(1)}, bf16[512,512]{1,0:T(8,128)(2,1)}, u32[]{:S(2)}) copy-start(bf16[512,512]{1,0:T(8,128)(2,1)} %refs_5_.3) | copy-start | bytes 1572868
  75.8 1.6 %copy-start.12 = (f32[512]{0:T(512)S(1)}, f32[512]{0:T(512)}, u32[]{:S(2)}) copy-start(f32[512]{0:T(512)} %param.19) | copy-start | bytes 6148
  90.5 18.3 %all-to-all-start.1 = ((bf16[16,32,512]{2,1,0:T(8,128)(2,1)}), bf16[16,32,512]{2,1,0:T(8,128)(2,1)S(1)}, u32[]{:S(2)}, u32[]{:S(2)}) async-start(bf16[16,32,512]{2,1,0:T(8,128)(2,1)} %attend.2), calls=%async_computation.1 | async-start | bytes 1048576 | tf_op jit(solution)/shard_map/all_to_all | solution.py:244
  108.8 18.3 %all-to-all-start.3 = ((bf16[16,32,512]{2,1,0:T(8,128)(2,1)}), bf16[16,32,512]{2,1,0:T(8,128)(2,1)S(1)}, u32[]{:S(2)}, u32[]{:S(2)}) async-start(bf16[16,32,512]{2,1,0:T(8,128)(2,1)} %attend.3), calls=%async_computation.3 | async-start | bytes 1048576 | tf_op jit(solution)/shard_map/all_to_all | solution.py:244

commit v3 on v2

--- a/solution.py
+++ b/solution.py
@@ -10,10 +10,12 @@
 epsilon = 1e-06
 parts = 2
 taps = 3
+most_direct = 8
 vmem_bytes = 48 * 1024 * 1024
 
 VMEM = pl.BlockSpec(memory_space=pltpu.VMEM)
 SMEM = pl.BlockSpec(memory_space=pltpu.SMEM)
+ANY = pl.BlockSpec(memory_space=pl.ANY)
 
 
 def silu(v):
@@ -29,71 +31,158 @@
     return pl.CostEstimate(flops=flops, bytes_accessed=size, transcendentals=0)
 
 
-def lift_kernel(started, halo, video, w_time, b_time, w_down, b_down, out, lifted):
-    frames, rows, width, channels = video.shape
+def params():
+    return pltpu.CompilerParams(vmem_limit_bytes=vmem_bytes)
+
+
+def pick_kernel(first, begin, video, out, sem):
+    count, rows = out.shape[:2]
+    copy = pltpu.make_async_copy(video.at[first : first + count, begin : begin + rows], out, sem)
+    copy.start()
+    copy.wait()
+
+
+def pick(video, first, begin, end):
+    frames, _, width, channels = video.shape
+    shape = (frames - first, end - begin, width, channels)
+    return pl.pallas_call(
+        partial(pick_kernel, first, begin),
+        out_shape=jax.ShapeDtypeStruct(shape, video.dtype),
+        in_specs=[ANY],
+        out_specs=ANY,
+        scratch_shapes=[pltpu.SemaphoreType.DMA],
+        compiler_params=params(),
+        name="pick",
+    )(video)
+
+
+def early_kernel(begin, video, w_time, b_time, w_down, b_down, own, part, rows_in, lifted, sem):
+    frames, rows, width, channels = rows_in.shape
     pixels = rows * width
+    copy = pltpu.make_async_copy(video.at[:, begin : begin + rows], rows_in, sem)
+    copy.start()
+    copy.wait()
 
     def frame(t):
-        ref, index = (halo, t + taps) if t < 0 else (video, t)
+        return rows_in[t].reshape(pixels, channels)
+
+    for t in range(taps - 1, frames):
+        lhs = jnp.concatenate([frame(t - k) for k in range(taps)], axis=1)
+        acc = dot32(lhs, w_time[...]) + b_time[...]
+        lifted[t] = (frame(t).astype(jnp.float32) + silu(acc)).astype(jnp.bfloat16)
+    for s in range(1, frames // 2):
+        known = [k for k in range(taps) if 2 * s + 1 - k >= taps - 1]
+        lhs = jnp.concatenate([lifted[2 * s + 1 - k] for k in known], axis=1)
+        part[s - 1] = dot32(lhs, w_down[: len(known) * channels]) + b_down[...]
+    own[...] = rows_in[: taps - 1]
+
+
+def early(video, begin, end, w_time, b_time, w_down, b_down):
+    frames, _, width, channels = video.shape
+    rows = end - begin
+    pixels = rows * width
+    flops = 2 * channels * channels * pixels * (taps * (frames - 2) + 2)
+    return pl.pallas_call(
+        partial(early_kernel, begin),
+        out_shape=[
+            jax.ShapeDtypeStruct((taps - 1, rows, width, channels), jnp.bfloat16),
+            jax.ShapeDtypeStruct((frames // 2 - 1, pixels, channels), jnp.float32),
+        ],
+        in_specs=[ANY] + [VMEM] * 4,
+        out_specs=[VMEM] * 2,
+        scratch_shapes=[
+            pltpu.VMEM((frames, rows, width, channels), jnp.bfloat16),
+            pltpu.VMEM((frames, pixels, channels), jnp.bfloat16),
+            pltpu.SemaphoreType.DMA,
+        ],
+        compiler_params=params(),
+        cost_estimate=cost(flops, w_time, w_down),
+        name="early",
+    )(video, w_time, b_time, w_down, b_down)
+
+
+def lift_kernel(started, halo, own, part, w_time, b_time, w_down, b_down, out, lifted):
+    halves, rows, width, channels = out.shape
+    pixels = rows * width
+
+    def frame(t):
+        ref, index = (halo, t + taps) if t < 0 else (own, t)
         return ref[index].reshape(pixels, channels)
 
-    for t in range(-1, frames):
+    for t in range(-1, taps - 1):
         lhs = jnp.concatenate([frame(t - k) for k in range(taps)], axis=1)
         acc = dot32(lhs, w_time[...]) + b_time[...]
         result = frame(t).astype(jnp.float32) + silu(acc)
         if t < 0:
             result = jnp.where(started[0] > 0, result, 0.0)
         lifted[t + 1] = result.astype(jnp.bfloat16)
-    for s in range(frames // 2):
-        lhs = jnp.concatenate([lifted[2 * s + 2 - k] for k in range(taps)], axis=1)
-        acc = dot32(lhs, w_down[...]) + b_down[...]
+    for s in range(halves):
+        late = [k for k in range(taps) if 2 * s + 1 - k < taps - 1]
+        acc = b_down[...] if s == 0 else part[s - 1]
+        if late:
+            lhs = jnp.concatenate([lifted[2 * s + 2 - k] for k in late], axis=1)
+            acc = dot32(lhs, w_down[late[0] * channels : (late[-1] + 1) * channels]) + acc
         out[s] = acc.astype(jnp.bfloat16).reshape(rows, width, channels)
 
 
-def lift(started, halo, video, w_time, b_time, w_down, b_down):
-    frames, rows, width, channels = video.shape
+def lift(started, halo, own, part, w_time, b_time, w_down, b_down):
+    rows, width, channels = own.shape[1:]
+    halves = part.shape[0] + 1
     pixels = rows * width
-    flops = 2 * taps * channels * channels * pixels * (frames + 1 + frames // 2)
+    flops = 2 * channels * channels * pixels * (taps * taps + 4)
     return pl.pallas_call(
         lift_kernel,
-        out_shape=jax.ShapeDtypeStruct((frames // 2, rows, width, channels), jnp.bfloat16),
-        in_specs=[SMEM] + [VMEM] * 6,
+        out_shape=jax.ShapeDtypeStruct((halves, rows, width, channels), jnp.bfloat16),
+        in_specs=[SMEM] + [VMEM] * 7,
         out_specs=VMEM,
-        scratch_shapes=[pltpu.VMEM((frames + 1, pixels, channels), jnp.bfloat16)],
-        compiler_params=pltpu.CompilerParams(vmem_limit_bytes=vmem_bytes),
-        cost_estimate=cost(flops, halo, video, w_time, w_down),
+        scratch_shapes=[pltpu.VMEM((taps, pixels, channels), jnp.bfloat16)],
+        compiler_params=params(),
+        cost_estimate=cost(flops, halo, own, part, w_time, w_down),
         name="lift",
-    )(started, halo, video, w_time, b_time, w_down, b_down)
-
-
-def space_kernel(left, middle, right, weights, bias, out):
-    halves, rows, width, channels = out.shape
-    pixels = rows * width
+    )(started, halo, own, part, w_time, b_time, w_down, b_down)
+
+
+def space_kernel(owners, order, left, middle, right, weights, bias, *refs):
+    outs, result = refs[:-1], refs[-1]
+    halves, pixels, channels = result.shape
+    rows = middle.shape[1] - 2
     sources = (left, middle, right)
-    for s in range(halves):
-
+
+    @pl.loop(0, halves)
+    def _(s):
         def window(source, a):
             return source[s, a : a + rows].reshape(pixels, channels)
 
         lhs = jnp.concatenate([window(v, a) for a in range(3) for v in sources], axis=1)
         acc = dot32(lhs, weights[...]) + bias[...]
-        result = window(middle, 1).astype(jnp.float32) + silu(acc)
-        out[s] = result.astype(jnp.bfloat16).reshape(rows, width, channels)
-
-
-def space(left, middle, right, weights, bias):
+        value = window(middle, 1).astype(jnp.float32) + silu(acc)
+        result[s] = value.astype(jnp.bfloat16)
+
+    if owners == 1:
+        outs[0][...] = result[...]
+    else:
+        each = pixels // owners
+        for j, out in enumerate(outs):
+            begin = pl.multiple_of(order[j] * each, each)
+            out[...] = result[:, pl.ds(begin, each)]
+
+
+def space(order, left, middle, right, weights, bias):
     halves, rows, width, channels = middle.shape
-    rows = rows - 2
-    flops = 2 * 9 * channels * channels * halves * rows * width
-    return pl.pallas_call(
-        space_kernel,
-        out_shape=jax.ShapeDtypeStruct((halves, rows, width, channels), jnp.bfloat16),
-        in_specs=[VMEM] * 5,
-        out_specs=VMEM,
-        compiler_params=pltpu.CompilerParams(vmem_limit_bytes=vmem_bytes),
+    owners = order.shape[0]
+    pixels = (rows - 2) * width
+    flops = 2 * 9 * channels * channels * halves * pixels
+    block = jax.ShapeDtypeStruct((halves, pixels // owners, channels), jnp.bfloat16)
+    return pl.pallas_call(
+        partial(space_kernel, owners),
+        out_shape=[block] * owners,
+        in_specs=[SMEM] + [VMEM] * 5,
+        out_specs=[VMEM] * owners,
+        scratch_shapes=[pltpu.VMEM((halves, pixels, channels), jnp.bfloat16)],
+        compiler_params=params(),
         cost_estimate=cost(flops, left, middle, right, weights),
         name="space",
-    )(left, middle, right, weights, bias)
+    )(order, left, middle, right, weights, bias)
 
 
 def attend_kernel(frames_per, lanes, count, first, *refs):
@@ -166,11 +255,41 @@
         out_shape=[jax.ShapeDtypeStruct(b.shape, jnp.bfloat16) for b in blocks],
         in_specs=[SMEM] + [VMEM] * (count + 5),
         out_specs=[VMEM] * count,
-        compiler_params=pltpu.CompilerParams(vmem_limit_bytes=vmem_bytes),
+        compiler_params=params(),
         cost_estimate=cost(flops, *blocks, w_query, w_key, w_value, w_out),
         name="attend",
     )(first, *blocks, gain, w_query, w_key, w_value, w_out)
     return [o.reshape(frames_per, pixels, channels) for o in outs]
+
+
+def collect_kernel(count, base, order, *refs):
+    blocks = refs[:count]
+    out, sems = refs[-2:]
+    copies = [
+        pltpu.make_async_copy(block, out.at[:, base + order[j]], sems.at[j])
+        for j, block in enumerate(blocks)
+    ]
+    for copy in copies:
+        copy.start()
+    for copy in copies:
+        copy.wait()
+
+
+def collect(order, blocks, chunk, chunks, whole):
+    count = len(blocks)
+    halves, pixels, channels = blocks[0].shape
+    shape = (halves, chunks * count, pixels, channels)
+    given = [] if whole is None else [whole]
+    return pl.pallas_call(
+        partial(collect_kernel, count, chunk * count),
+        out_shape=jax.ShapeDtypeStruct(shape, jnp.bfloat16),
+        in_specs=[SMEM] + [ANY] * (count + len(given)),
+        out_specs=ANY,
+        input_output_aliases={count + 1: 0} if given else {},
+        scratch_shapes=[pltpu.SemaphoreType.DMA((count,))],
+        compiler_params=params(),
+        name="collect",
+    )(order, *blocks, *given)
 
 
 def after(value, other):
@@ -183,16 +302,21 @@
     frames, height, width, channels = video.shape
     devices = lax.axis_size("tm")
     columns = lax.axis_size("cols")
-    place = lax.axis_index("tm")
+    place = lax.axis_index("tm").astype(jnp.int32)
     column = lax.axis_index("cols")
     halves = frames // 2
-    started = place.astype(jnp.int32).reshape(1)
-    first = jnp.zeros((1,), jnp.int32)
+    started = place.reshape(1)
     w_time = w_time.reshape(-1, channels)
     w_down = w_down.reshape(-1, channels)
     w_space = w_space.reshape(-1, channels)
     b_time, b_down, b_space, gain = (v.reshape(1, -1) for v in (b_time, b_down, b_space, gain))
     onward = [(i, i + 1) for i in range(devices - 1)]
+    chunks = parts if height % parts == 0 and height // parts * width % devices == 0 else 1
+    size = height // chunks
+    each = size * width // devices
+    direct = devices <= most_direct and devices & (devices - 1) == 0 and each % 16 == 0
+    issue = sorted(range(1, devices), key=lambda j: -j)
+    order = place ^ jnp.arange(devices, dtype=jnp.int32) if direct else jnp.zeros(1, jnp.int32)
 
     def beside(value):
         last, head = value[:, :, -1:], value[:, :, :1]
@@ -202,24 +326,31 @@
         up = [(i, i + 1) for i in range(columns - 1)]
         return lax.ppermute(last, "cols", up), lax.ppermute(head, "cols", [(j, i) for i, j in up])
 
-    chunks = parts if height % parts == 0 and height // parts * width % devices == 0 else 1
-    size = height // chunks
-    halos, newest = [], None
+    def exchange(blocks):
+        result = list(blocks)
+        for j in issue:
+            result[j] = lax.ppermute(blocks[j], "tm", [(i, i ^ j) for i in range(devices)])
+        return result
+
+    spans = [
+        (k * size + (1 if k else 0), min((k + 1) * size + 1, height)) for k in range(chunks)
+    ]
+    halos, owns, sums = [], [], []
+    for begin, end in spans:
+        sent = pick(video, frames - taps, begin, end)
+        if sums:
+            sent = after(sent, sums[-1])
+        halos.append(lax.ppermute(sent, "tm", onward))
+        own, part = early(video, begin, end, w_time, b_time, w_down, b_down)
+        owns.append(own)
+        sums.append(part)
+
+    spatials, kept = [], None
     for index in range(chunks):
-        begin = index * size + (1 if index else 0)
-        end = min((index + 1) * size + 1, height)
-        sent = video[frames - taps :, begin:end]
-        if newest is not None:
-            sent = after(sent, newest)
-        newest = lax.ppermute(sent, "tm", onward)
-        halos.append((begin, end, newest))
-
-    spatials, kept = [], None
-    for index, (begin, end, halo) in enumerate(halos):
-        own = video[:, begin:end]
+        halo, own, part = halos[index], owns[index], sums[index]
         if spatials:
-            own = after(own, spatials[-1])
-        reduced = lift(started, halo, own, w_time, b_time, w_down, b_down)
+            own = after(own, spatials[-1][0])
+        reduced = lift(started, halo, own, part, w_time, b_time, w_down, b_down)
         left, right = beside(reduced)
         pieces = (left, reduced, right)
         if kept is None:
@@ -231,19 +362,26 @@
         left, middle, right = pieces
         to_right = jnp.concatenate([left, middle[:, :, :-1]], axis=2)
         to_left = jnp.concatenate([middle[:, :, 1:], right], axis=2)
-        spatials.append(space(to_right, middle, to_left, w_space, b_space))
-
-    gathers = [
-        lax.all_to_all(s.reshape(halves, size * width, channels), "tm", 1, 0, tiled=True)
-        for s in spatials
-    ]
-    returns, newest = [], spatials[-1]
-    for block in gathers:
-        block = after(block, newest)
-        (newest,) = attend(first, [block], gain, w_query, w_key, w_value, w_out)
-        returns.append(lax.all_to_all(newest, "tm", 0, 1, tiled=True))
-    encoded = jnp.concatenate(returns, axis=1)
-    return encoded.reshape(halves, height, width, channels)
+        spatials.append(space(order, to_right, middle, to_left, w_space, b_space))
+
+    newest = spatials[-1][0]
+    if direct:
+        whole = None
+        returns = []
+        for gathered in [exchange(blocks) for blocks in spatials]:
+            gathered[0] = after(gathered[0], newest)
+            results = attend(order * halves, gathered, gain, w_query, w_key, w_value, w_out)
+            newest = results[0]
+            returns.append(exchange(results))
+        for index, blocks in enumerate(returns):
+            whole = collect(order, blocks, index, chunks, whole)
+        return whole.reshape(halves, height, width, channels)
+    returns = []
+    for (block,) in spatials:
+        gathered = lax.all_to_all(block, "tm", 1, 0, tiled=True)
+        (result,) = attend(order, [gathered], gain, w_query, w_key, w_value, w_out)
+        returns.append(lax.all_to_all(result, "tm", 0, 1, tiled=True))
+    return jnp.concatenate(returns, axis=1).reshape(halves, height, width, channels)
 
 
 def solution(mesh):

time: 129 us -> 112 us (0.87)
  waiting for transfers between devices: 57 us -> 17.4 us
  starting transfers between devices: 29.7 us -> 54.2 us
  local copies, waits for them, and re-layouts: 16.2 us -> 4.27 us
  Pallas kernels: 22.3 us -> 33.2 us
    ppermute x2 -> x30, starting transfers between devices: 9.24 us -> 54 us  [the longest x28 44.7 us: exchange(): lax.ppermute(blocks[j], 'tm', [(i, i ^ j) for i in range(devices)])]
    all_to_all x4 -> x0, waiting for transfers between devices: 36.5 us -> none  [the longest x2 26.3 us: per_device(): returns.append(lax.all_to_all(newest, 'tm', 0, 1, tiled=True))]
    all_to_all x4 -> x0, starting transfers between devices: 20.4 us -> none  [the longest x2 13.1 us: per_device(): lax.all_to_all(s.reshape(halves, size * width, channels), 'tm', 1, 0, til...]
    pallas_call x4 -> x10, Pallas kernels: 16.6 us -> 27.8 us  [the longest x2 10.9 us: space(): pl.pallas_call(partial(space_kernel, owners), out_shape=[block] * owners,...]
    slice x4 -> x0, local copies, waits for them, and re-layouts: 6.75 us -> none  [the longest x2 4.15 us: per_device(): sent = video[frames - taps:, begin:end]]
    ppermute x2 -> x30, waiting for transfers between devices: 19.6 us -> 16.8 us  [the longest x2 10.2 us: per_device(): halos.append(lax.ppermute(sent, 'tm', onward))]
    reshape x2 -> x0, local copies, waits for them, and re-layouts: 2.68 us -> none  [per_device(): s.reshape(halves, size * width, channels)]
    all_to_all x6 -> x0, local copies, waits for them, and re-layouts: 1.44 us -> none  [the longest x4 1.37 us: per_device(): lax.all_to_all(s.reshape(halves, size * width, channels), 'tm', 1, 0, til...]
  transfers between devices with their start and end apart: 8 -> 32, of which waited for: 6 -> 9; matrix products, arithmetic and copies ran while one was open for 8% -> 2% of each run, Pallas kernels for 15% -> 25%
where the time goes in v3:
time: 112 us; the launch traced here: 111 us
  starting transfers between devices  54.2 us (48%)
  Pallas kernels  33.2 us (30%)
  waiting for transfers between devices  17.4 us (16%)
  local copies, waits for them, and re-layouts  4.27 us (4%)
  other arithmetic  1.59 us (1%)
    ppermute x28, starting transfers between devices, exchange(): lax.ppermute(blocks[j], 'tm', [(i, i ^ j) for i in range(devices)])  44.7 us
    pallas_call x2, Pallas kernels, space(): pl.pallas_call(partial(space_kernel, owners), out_shape=[block] * owners,...  10.9 us
    ppermute x2, waiting for transfers between devices, per_device(): halos.append(lax.ppermute(sent, 'tm', onward))  10.2 us
    ppermute x2, starting transfers between devices, per_device(): halos.append(lax.ppermute(sent, 'tm', onward))  9.31 us
    pallas_call x2, Pallas kernels, lift(): pl.pallas_call(lift_kernel, out_shape=jax.ShapeDtypeStruct((halves, rows,...  6.77 us
    ppermute x28, waiting for transfers between devices, exchange(): lax.ppermute(blocks[j], 'tm', [(i, i ^ j) for i in range(devices)])  6.55 us
    pallas_call x2, Pallas kernels, early(): pl.pallas_call(partial(early_kernel, begin), out_shape=[jax.ShapeDtypeStr...  5.61 us
    pallas_call x2, Pallas kernels, attend(): pl.pallas_call(partial(attend_kernel, frames_per, lanes, count), out_shap...  5.31 us
  transfers between devices with their start and end apart: 32, of which 9 were waited for; matrix products, arithmetic and copies ran while one was open for 2% of the time, Pallas kernels for 25%

profile of v3, /device:TPU:0, one launch (start us, length us, event | category | flops | bytes accessed | tf_op | source)
XLA Modules:
  0.0 111.2 jit_solution(969397158853242763)
XLA Ops:
  0.0 1.6 %copy-done = bf16[4,32,16,512]{3,2,1,0:T(8,128)(2,1)S(1)} copy-done((bf16[4,32,16,512]{3,2,1,0:T(8,128)(2,1)S(1)}, bf16[4,32,16,512]{3,2,1,0:T(8,128)(2,1)}, u32[]{:S(2)}) %copy-start) | copy-done | bytes 2097176
  2.5 6.0 %collective-permute-start = (bf16[3,17,16,512]{3,2,1,0:T(8,128)(2,1)}, bf16[3,17,16,512]{3,2,1,0:T(8,128)(2,1)}, u32[]{:S(2)}, u32[]{:S(2)}) collective-permute-start(bf16[3,17,16,512]{3,2,1,0:T(8,128)(2,1)} %pick.2), channel_id=1, source_target_pairs={{0,2},{2,4},{4,6},{6,8},{8,10},{10,12},{12,14},{1,3},{3,5},{5,7},{... | collective-permute-start | bytes 2506760 | tf_op jit(solution)/shard_map/ppermute | solution.py:343
  9.4 2.9 %early.2 = (bf16[2,17,16,512]{3,2,1,0:T(8,128)(2,1)S(1)}, f32[1,272,512]{2,1,0:T(8,128)S(1)}) custom-call(bf16[4,32,16,512]{3,2,1,0:T(8,128)(2,1)} %video.7, bf16[1536,512]{1,0:T(8,128)(2,1)S(1)} %bitcast.9, f32[1,512]{1,0:T(1,128)S(1)} %bitcast.17, bf16[1536,512]{1,0:T(8,128)(2,1)S(1)} %bitcast.13, f32[1,512]{1,0:T(1,128)S(1)} %bitcast.21), custom_call_target="tpu_custom_call" | custom-call | flops 1140850688 | bytes 3145728 | tf_op jit(solution)/shard_map/early/pallas_call | solution.py:85
  13.9 3.4 %collective-permute-start.2 = (bf16[3,15,16,512]{3,2,1,0:T(8,128)(2,1)}, bf16[3,15,16,512]{3,2,1,0:T(8,128)(2,1)}, u32[]{:S(2)}, u32[]{:S(2)}) collective-permute-start(bf16[3,15,16,512]{3,2,1,0:T(8,128)(2,1)} %pick.3), channel_id=1, source_target_pairs={{0,2},{2,4},{4,6},{6,8},{8,10},{10,12},{12,14},{1,3},{3,5},{5,7},{... | collective-permute-start | bytes 2211848 | tf_op jit(solution)/shard_map/ppermute | solution.py:343
  17.3 2.8 %early.3 = (bf16[2,15,16,512]{3,2,1,0:T(8,128)(2,1)S(1)}, f32[1,240,512]{2,1,0:T(8,128)S(1)}) custom-call(bf16[4,32,16,512]{3,2,1,0:T(8,128)(2,1)} %video.7, bf16[1536,512]{1,0:T(8,128)(2,1)S(1)} %bitcast.10, f32[1,512]{1,0:T(1,128)S(1)} %bitcast.18, bf16[1536,512]{1,0:T(8,128)(2,1)S(1)} %bitcast.14, f32[1,512]{1,0:T(1,128)S(1)} %bitcast.22), custom_call_target="tpu_custom_call" | custom-call | flops 1006632960 | bytes 3145728 | tf_op jit(solution)/shard_map/early/pallas_call | solution.py:85
  20.0 6.8 %collective-permute-done.halo = bf16[3,17,16,512]{3,2,1,0:T(8,128)(2,1)} collective-permute-done((bf16[3,17,16,512]{3,2,1,0:T(8,128)(2,1)}, bf16[3,17,16,512]{3,2,1,0:T(8,128)(2,1)}, u32[]{:S(2)}, u32[]{:S(2)}) %collective-permute-start) | collective-permute-done | bytes 835616 | tf_op jit(solution)/shard_map/ppermute | solution.py:343
  26.9 3.5 %lift.2 = bf16[2,17,16,512]{3,2,1,0:T(8,128)(2,1)S(1)} custom-call(s32[1]{0:T(128)} %bitcast.started, bf16[3,17,16,512]{3,2,1,0:T(8,128)(2,1)} %collective-permute-done.halo, bf16[2,17,16,512]{3,2,1,0:T(8,128)(2,1)S(1)} %copy-done.7, f32[1,272,512]{2,1,0:T(8,128)S(1)} %copy-done.9, bf16[1536,512]{1,0:T(8,128)(2,1)S(1)} %bitcast.11, f32[1,512]{1,0:T(1,128)S(1)} %bitcast.19, ...), custom_call_target="tpu_custom_call" | custom-call | flops 1853882368 | bytes 5095424 | tf_op jit(solution)/shard_map/lift/pallas_call | solution.py:133
  32.6 5.5 %space.2 = (bf16[2,32,512]{2,1,0:T(8,128)(2,1)S(1)}, bf16[2,32,512]{2,1,0:T(8,128)(2,1)S(1)}, bf16[2,32,512]{2,1,0:T(8,128)(2,1)S(1)}, bf16[2,32,512]{2,1,0:T(8,...) custom-call(s32[8]{0:T(128)S(1)} %iota_xor_fusion.order, ...), custom_call_target="tpu_custom_call" | custom-call | flops 2415919104 | bytes 6488064 | tf_op jit(solution)/shard_map/space/pallas_call | solution.py:176
  38.1 3.4 %collective-permute-done.2.halo = bf16[3,15,16,512]{3,2,1,0:T(8,128)(2,1)} collective-permute-done((bf16[3,15,16,512]{3,2,1,0:T(8,128)(2,1)}, bf16[3,15,16,512]{3,2,1,0:T(8,128)(2,1)}, u32[]{:S(2)}, u32[]{:S(2)}) %collective-permute-start.2) | collective-permute-done | bytes 737312 | tf_op jit(solution)/shard_map/ppermute | solution.py:343
  41.5 3.3 %lift.3 = bf16[2,15,16,512]{3,2,1,0:T(8,128)(2,1)S(1)} custom-call(s32[1]{0:T(128)} %bitcast.started, bf16[3,15,16,512]{3,2,1,0:T(8,128)(2,1)} %collective-permute-done.2.halo, bf16[2,15,16,512]{3,2,1,0:T(8,128)(2,1)S(1)} %get-tuple-element.50.own, f32[1,240,512]{2,1,0:T(8,128)S(1)} %get-tuple-element.51.part, bf16[1536,512]{1,0:T(8,128)(2,1)S(1)} %bitcast.12, ...), custom_call_target="tpu_custom_call" | custom-call | flops 1635778560 | bytes 4866048 | tf_op jit(solution)/shard_map/lift/pallas_call | solution.py:133
  45.3 5.6 %collective-permute-start.10 = (bf16[2,32,512]{2,1,0:T(8,128)(2,1)S(1)}, bf16[2,32,512]{2,1,0:T(8,128)(2,1)S(1)}, u32[]{:S(2)}, u32[]{:S(2)}) collective-permute-start(bf16[2,32,512]{2,1,0:T(8,128)(2,1)S(1)} %get-tuple-element.60), channel_id=1, source_target_pairs={{0,14},{2,12},{4,10},{6,8},{8,6},{10,4},{12,2},{14,0},{1,15},{3,13... | collective-permute-start | bytes 196616 | tf_op jit(solution)/shard_map/ppermute | solution.py:332
  50.9 1.4 %collective-permute-start.4 = (bf16[2,32,512]{2,1,0:T(8,128)(2,1)S(1)}, bf16[2,32,512]{2,1,0:T(8,128)(2,1)S(1)}, u32[]{:S(2)}, u32[]{:S(2)}) collective-permute-start(bf16[2,32,512]{2,1,0:T(8,128)(2,1)S(1)} %get-tuple-element.54), channel_id=1, source_target_pairs={{0,2},{2,0},{4,6},{6,4},{8,10},{10,8},{12,14},{14,12},{1,3},{3,1},... | collective-permute-start | bytes 196616 | tf_op jit(solution)/shard_map/ppermute | solution.py:332
  52.3 2.1 %collective-permute-start.6 = (bf16[2,32,512]{2,1,0:T(8,128)(2,1)S(1)}, bf16[2,32,512]{2,1,0:T(8,128)(2,1)S(1)}, u32[]{:S(2)}, u32[]{:S(2)}) collective-permute-start(bf16[2,32,512]{2,1,0:T(8,128)(2,1)S(1)} %get-tuple-element.56), channel_id=1, source_target_pairs={{0,6},{2,4},{4,2},{6,0},{8,14},{10,12},{12,10},{14,8},{1,7},{3,5},... | collective-permute-start | bytes 196616 | tf_op jit(solution)/shard_map/ppermute | solution.py:332
  55.2 5.4 %space.3 = (bf16[2,32,512]{2,1,0:T(8,128)(2,1)S(1)}, bf16[2,32,512]{2,1,0:T(8,128)(2,1)S(1)}, bf16[2,32,512]{2,1,0:T(8,128)(2,1)S(1)}, bf16[2,32,512]{2,1,0:T(8,...) custom-call(s32[8]{0:T(128)S(1)} %iota_xor_fusion.order, ...), custom_call_target="tpu_custom_call" | custom-call | flops 2415919104 | bytes 6488064 | tf_op jit(solution)/shard_map/space/pallas_call | solution.py:176
  60.6 3.8 %collective-permute-start.8 = (bf16[2,32,512]{2,1,0:T(8,128)(2,1)S(1)}, bf16[2,32,512]{2,1,0:T(8,128)(2,1)S(1)}, u32[]{:S(2)}, u32[]{:S(2)}) collective-permute-start(bf16[2,32,512]{2,1,0:T(8,128)(2,1)S(1)} %get-tuple-element.58), channel_id=1, source_target_pairs={{0,10},{2,8},{4,14},{6,12},{8,2},{10,0},{12,6},{14,4},{1,11},{3,9}... | collective-permute-start | bytes 196616 | tf_op jit(solution)/shard_map/ppermute | solution.py:332
  65.7 2.3 %collective-permute-start.13 = (bf16[2,32,512]{2,1,0:T(8,128)(2,1)S(1)}, bf16[2,32,512]{2,1,0:T(8,128)(2,1)S(1)}, u32[]{:S(2)}, u32[]{:S(2)}) collective-permute-start(bf16[2,32,512]{2,1,0:T(8,128)(2,1)S(1)} %get-tuple-element.65), channel_id=1, source_target_pairs={{0,6},{2,4},{4,2},{6,0},{8,14},{10,12},{12,10},{14,8},{1,7},{3,5},... | collective-permute-start | bytes 196616 | tf_op jit(solution)/shard_map/ppermute | solution.py:332
  68.9 1.5 %collective-permute-start.14 = (bf16[2,32,512]{2,1,0:T(8,128)(2,1)S(1)}, bf16[2,32,512]{2,1,0:T(8,128)(2,1)S(1)}, u32[]{:S(2)}, u32[]{:S(2)}) collective-permute-start(bf16[2,32,512]{2,1,0:T(8,128)(2,1)S(1)} %get-tuple-element.66), channel_id=1, source_target_pairs={{0,8},{2,10},{4,12},{6,14},{8,0},{10,2},{12,4},{14,6},{1,9},{3,11}... | collective-permute-start | bytes 196616 | tf_op jit(solution)/shard_map/ppermute | solution.py:332
  71.6 3.2 %collective-permute-start.16 = (bf16[2,32,512]{2,1,0:T(8,128)(2,1)S(1)}, bf16[2,32,512]{2,1,0:T(8,128)(2,1)S(1)}, u32[]{:S(2)}, u32[]{:S(2)}) collective-permute-start(bf16[2,32,512]{2,1,0:T(8,128)(2,1)S(1)} %get-tuple-element.68), channel_id=1, source_target_pairs={{0,12},{2,14},{4,8},{6,10},{8,4},{10,6},{12,0},{14,2},{1,13},{3,15... | collective-permute-start | bytes 196616 | tf_op jit(solution)/shard_map/ppermute | solution.py:332
  74.8 1.7 %collective-permute-start.17 = (bf16[2,32,512]{2,1,0:T(8,128)(2,1)S(1)}, bf16[2,32,512]{2,1,0:T(8,128)(2,1)S(1)}, u32[]{:S(2)}, u32[]{:S(2)}) collective-permute-start(bf16[2,32,512]{2,1,0:T(8,128)(2,1)S(1)} %get-tuple-element.69), channel_id=1, source_target_pairs={{0,14},{2,12},{4,10},{6,8},{8,6},{10,4},{12,2},{14,0},{1,15},{3,13... | collective-permute-start | bytes 196616 | tf_op jit(solution)/shard_map/ppermute | solution.py:332
  76.6 2.7 %attend.2 = (bf16[2,32,512]{2,1,0:T(8,128)(2,1)S(1)}, bf16[2,32,512]{2,1,0:T(8,128)(2,1)S(1)}, bf16[2,32,512]{2,1,0:T(8,128)(2,1)S(1)}, bf16[2,32,512]{2,1,0:T(8...) custom-call(s32[8]{0:T(128)S(1)} %broadcast_multiply_fusion.first, ...), custom_call_target="tpu_custom_call" | custom-call | flops 1342177280 | bytes 2621440 | tf_op jit(solution)/shard_map/attend/pallas_call | solution.py:253
  80.2 2.6 %collective-permute-start.27 = (bf16[2,32,512]{2,1,0:T(8,128)(2,1)S(1)}, bf16[2,32,512]{2,1,0:T(8,128)(2,1)S(1)}, u32[]{:S(2)}, u32[]{:S(2)}) collective-permute-start(bf16[2,32,512]{2,1,0:T(8,128)(2,1)S(1)} %get-tuple-element.80), channel_id=1, source_target_pairs={{0,6},{2,4},{4,2},{6,0},{8,14},{10,12},{12,10},{14,8},{1,7},{3,5},... | collective-permute-start | bytes 196616 | tf_op jit(solution)/shard_map/ppermute | solution.py:332
  82.8 1.5 %collective-permute-start.28 = (bf16[2,32,512]{2,1,0:T(8,128)(2,1)S(1)}, bf16[2,32,512]{2,1,0:T(8,128)(2,1)S(1)}, u32[]{:S(2)}, u32[]{:S(2)}) collective-permute-start(bf16[2,32,512]{2,1,0:T(8,128)(2,1)S(1)} %get-tuple-element.81), channel_id=1, source_target_pairs={{0,8},{2,10},{4,12},{6,14},{8,0},{10,2},{12,4},{14,6},{1,9},{3,11}... | collective-permute-start | bytes 196616 | tf_op jit(solution)/shard_map/ppermute | solution.py:332
  85.5 2.6 %attend.3 = (bf16[2,32,512]{2,1,0:T(8,128)(2,1)S(1)}, bf16[2,32,512]{2,1,0:T(8,128)(2,1)S(1)}, bf16[2,32,512]{2,1,0:T(8,128)(2,1)S(1)}, bf16[2,32,512]{2,1,0:T(8...) custom-call(s32[8]{0:T(128)S(1)} %broadcast_multiply_fusion.first, ...), custom_call_target="tpu_custom_call" | custom-call | flops 1342177280 | bytes 2621440 | tf_op jit(solution)/shard_map/attend/pallas_call | solution.py:253
  88.2 3.3 %collective-permute-start.30 = (bf16[2,32,512]{2,1,0:T(8,128)(2,1)S(1)}, bf16[2,32,512]{2,1,0:T(8,128)(2,1)S(1)}, u32[]{:S(2)}, u32[]{:S(2)}) collective-permute-start(bf16[2,32,512]{2,1,0:T(8,128)(2,1)S(1)} %get-tuple-element.83), channel_id=1, source_target_pairs={{0,12},{2,14},{4,8},{6,10},{8,4},{10,6},{12,0},{14,2},{1,13},{3,15... | collective-permute-start | bytes 196616 | tf_op jit(solution)/shard_map/ppermute | solution.py:332
  91.5 1.7 %collective-permute-start.31 = (bf16[2,32,512]{2,1,0:T(8,128)(2,1)S(1)}, bf16[2,32,512]{2,1,0:T(8,128)(2,1)S(1)}, u32[]{:S(2)}, u32[]{:S(2)}) collective-permute-start(bf16[2,32,512]{2,1,0:T(8,128)(2,1)S(1)} %get-tuple-element.84), channel_id=1, source_target_pairs={{0,14},{2,12},{4,10},{6,8},{8,6},{10,4},{12,2},{14,0},{1,15},{3,13... | collective-permute-start | bytes 196616 | tf_op jit(solution)/shard_map/ppermute | solution.py:332
  93.6 3.1 %collective-permute-start.20 = (bf16[2,32,512]{2,1,0:T(8,128)(2,1)S(1)}, bf16[2,32,512]{2,1,0:T(8,128)(2,1)S(1)}, u32[]{:S(2)}, u32[]{:S(2)}) collective-permute-start(bf16[2,32,512]{2,1,0:T(8,128)(2,1)S(1)} %get-tuple-element.73), channel_id=1, source_target_pairs={{0,6},{2,4},{4,2},{6,0},{8,14},{10,12},{12,10},{14,8},{1,7},{3,5},... | collective-permute-start | bytes 196616 | tf_op jit(solution)/shard_map/ppermute | solution.py:332
  96.7 1.5 %collective-permute-start.21 = (bf16[2,32,512]{2,1,0:T(8,128)(2,1)S(1)}, bf16[2,32,512]{2,1,0:T(8,128)(2,1)S(1)}, u32[]{:S(2)}, u32[]{:S(2)}) collective-permute-start(bf16[2,32,512]{2,1,0:T(8,128)(2,1)S(1)} %get-tuple-element.74), channel_id=1, source_target_pairs={{0,8},{2,10},{4,12},{6,14},{8,0},{10,2},{12,4},{14,6},{1,9},{3,11}... | collective-permute-start | bytes 196616 | tf_op jit(solution)/shard_map/ppermute | solution.py:332
  99.4 3.2 %collective-permute-start.23 = (bf16[2,32,512]{2,1,0:T(8,128)(2,1)S(1)}, bf16[2,32,512]{2,1,0:T(8,128)(2,1)S(1)}, u32[]{:S(2)}, u32[]{:S(2)}) collective-permute-start(bf16[2,32,512]{2,1,0:T(8,128)(2,1)S(1)} %get-tuple-element.76), channel_id=1, source_target_pairs={{0,12},{2,14},{4,8},{6,10},{8,4},{10,6},{12,0},{14,2},{1,13},{3,15... | collective-permute-start | bytes 196616 | tf_op jit(solution)/shard_map/ppermute | solution.py:332
  102.7 1.7 %collective-permute-start.24 = (bf16[2,32,512]{2,1,0:T(8,128)(2,1)S(1)}, bf16[2,32,512]{2,1,0:T(8,128)(2,1)S(1)}, u32[]{:S(2)}, u32[]{:S(2)}) collective-permute-start(bf16[2,32,512]{2,1,0:T(8,128)(2,1)S(1)} %get-tuple-element.77), channel_id=1, source_target_pairs={{0,14},{2,12},{4,10},{6,8},{8,6},{10,4},{12,2},{14,0},{1,15},{3,13... | collective-permute-start | bytes 196616 | tf_op jit(solution)/shard_map/ppermute | solution.py:332
  104.3 1.4 %collect.2.refs_8_ = bf16[2,16,32,512]{3,2,1,0:T(8,128)(2,1)} custom-call(s32[8]{0:T(128)S(1)} %iota_xor_fusion.order, bf16[2,32,512]{2,1,0:T(8,128)(2,1)S(1)} %get-tuple-element.61.refs_0_, bf16[2,32,512]{2,1,0:T(8,128)(2,1)S(1)} %collective-permute-done.25.refs_1_, bf16[2,32,512]{2,1,0:T(8,128)(2,1)S(1)} %collective-permute-done.26.refs_2_, ...), custom_call_target="tpu_custom_call" | custom-call | tf_op jit(solution)/shard_map/collect/pallas_call | solution.py:283
  105.9 3.7 %collective-permute-done.24.refs_7_ = bf16[2,32,512]{2,1,0:T(8,128)(2,1)S(1)} collective-permute-done((bf16[2,32,512]{2,1,0:T(8,128)(2,1)S(1)}, bf16[2,32,512]{2,1,0:T(8,128)(2,1)S(1)}, u32[]{:S(2)}, u32[]{:S(2)}) %collective-permute-start.24) | collective-permute-done | bytes 65568 | tf_op jit(solution)/shard_map/ppermute | solution.py:332
  109.6 1.4 %collect.3 = bf16[2,16,32,512]{3,2,1,0:T(8,128)(2,1)} custom-call(s32[8]{0:T(128)S(1)} %iota_xor_fusion.order, bf16[2,32,512]{2,1,0:T(8,128)(2,1)S(1)} %get-tuple-element.70.refs_0_, bf16[2,32,512]{2,1,0:T(8,128)(2,1)S(1)} %collective-permute-done.18.refs_1_, ...), custom_call_target="tpu_custom_call", output_to_operand_aliasing={{}: (9, {})} | custom-call | tf_op jit(solution)/shard_map/collect/pallas_call | solution.py:283
  (95 shorter events, 14.0 us)
Async XLA Ops:
  2.5 24.3 %collective-permute-start = (bf16[3,17,16,512]{3,2,1,0:T(8,128)(2,1)}, bf16[3,17,16,512]{3,2,1,0:T(8,128)(2,1)}, u32[]{:S(2)}, u32[]{:S(2)}) collective-permute-start(bf16[3,17,16,512]{3,2,1,0:T(8,128)(2,1)} %pick.2), channel_id=1, source_target_pairs={{0,2},{2,4},{4,6},{6,8},{8,10},{10,12},{12,14},{1,3},{3,5},{5,7},{... | collective-permute-start | bytes 2506760 | tf_op jit(solution)/shard_map/ppermute | solution.py:343
  13.9 27.6 %collective-permute-start.2 = (bf16[3,15,16,512]{3,2,1,0:T(8,128)(2,1)}, bf16[3,15,16,512]{3,2,1,0:T(8,128)(2,1)}, u32[]{:S(2)}, u32[]{:S(2)}) collective-permute-start(bf16[3,15,16,512]{3,2,1,0:T(8,128)(2,1)} %pick.3), channel_id=1, source_target_pairs={{0,2},{2,4},{4,6},{6,8},{8,10},{10,12},{12,14},{1,3},{3,5},{5,7},{... | collective-permute-start | bytes 2211848 | tf_op jit(solution)/shard_map/ppermute | solution.py:343
  30.5 1.3 %collective-permute-start.1 = (bf16[2,17,1,512]{3,2,1,0:T(2,128)(2,1)S(1)}, bf16[2,17,1,512]{3,2,1,0:T(2,128)(2,1)S(1)}, u32[]{:S(2)}, u32[]{:S(2)}) collective-permute-start(bf16[2,17,1,512]{3,2,1,0:T(2,128)(2,1)S(1)} %broadcast_select_fusion.1), channel_id=1, source_target_pairs={{0,1},{1,0},{2,3},{3,2},{4,5},{5,4},{6,7},{7,6},{8,9},{9,8},{10,11... | collective-permute-start | bytes 104456 | tf_op jit(solution)/shard_map/ppermute | solution.py:324
  44.9 9.5 %collective-permute-start.3 = (bf16[2,15,1,512]{3,2,1,0:T(2,128)(2,1)S(1)}, bf16[2,15,1,512]{3,2,1,0:T(2,128)(2,1)S(1)}, u32[]{:S(2)}, u32[]{:S(2)}) collective-permute-start(bf16[2,15,1,512]{3,2,1,0:T(2,128)(2,1)S(1)} %broadcast_select_fusion.4), channel_id=1, source_target_pairs={{0,1},{1,0},{2,3},{3,2},{4,5},{5,4},{6,7},{7,6},{8,9},{9,8},{10,11... | collective-permute-start | bytes 92168 | tf_op jit(solution)/shard_map/ppermute | solution.py:324
  45.3 15.3 %collective-permute-start.10 = (bf16[2,32,512]{2,1,0:T(8,128)(2,1)S(1)}, bf16[2,32,512]{2,1,0:T(8,128)(2,1)S(1)}, u32[]{:S(2)}, u32[]{:S(2)}) collective-permute-start(bf16[2,32,512]{2,1,0:T(8,128)(2,1)S(1)} %get-tuple-element.60), channel_id=1, source_target_pairs={{0,14},{2,12},{4,10},{6,8},{8,6},{10,4},{12,2},{14,0},{1,15},{3,13... | collective-permute-start | bytes 196616 | tf_op jit(solution)/shard_map/ppermute | solution.py:332
  50.9 13.6 %collective-permute-start.4 = (bf16[2,32,512]{2,1,0:T(8,128)(2,1)S(1)}, bf16[2,32,512]{2,1,0:T(8,128)(2,1)S(1)}, u32[]{:S(2)}, u32[]{:S(2)}) collective-permute-start(bf16[2,32,512]{2,1,0:T(8,128)(2,1)S(1)} %get-tuple-element.54), channel_id=1, source_target_pairs={{0,2},{2,0},{4,6},{6,4},{8,10},{10,8},{12,14},{14,12},{1,3},{3,1},... | collective-permute-start | bytes 196616 | tf_op jit(solution)/shard_map/ppermute | solution.py:332
  52.3 12.2 %collective-permute-start.5 = (bf16[2,32,512]{2,1,0:T(8,128)(2,1)S(1)}, bf16[2,32,512]{2,1,0:T(8,128)(2,1)S(1)}, u32[]{:S(2)}, u32[]{:S(2)}) collective-permute-start(bf16[2,32,512]{2,1,0:T(8,128)(2,1)S(1)} %get-tuple-element.55), channel_id=1, source_target_pairs={{0,4},{2,6},{4,0},{6,2},{8,12},{10,14},{12,8},{14,10},{1,5},{3,7},... | collective-permute-start | bytes 196616 | tf_op jit(solution)/shard_map/ppermute | solution.py:332
  52.3 13.0 %collective-permute-start.6 = (bf16[2,32,512]{2,1,0:T(8,128)(2,1)S(1)}, bf16[2,32,512]{2,1,0:T(8,128)(2,1)S(1)}, u32[]{:S(2)}, u32[]{:S(2)}) collective-permute-start(bf16[2,32,512]{2,1,0:T(8,128)(2,1)S(1)} %get-tuple-element.56), channel_id=1, source_target_pairs={{0,6},{2,4},{4,2},{6,0},{8,14},{10,12},{12,10},{14,8},{1,7},{3,5},... | collective-permute-start | bytes 196616 | tf_op jit(solution)/shard_map/ppermute | solution.py:332
  54.4 11.3 %collective-permute-start.7 = (bf16[2,32,512]{2,1,0:T(8,128)(2,1)S(1)}, bf16[2,32,512]{2,1,0:T(8,128)(2,1)S(1)}, u32[]{:S(2)}, u32[]{:S(2)}) collective-permute-start(bf16[2,32,512]{2,1,0:T(8,128)(2,1)S(1)} %get-tuple-element.57), channel_id=1, source_target_pairs={{0,8},{2,10},{4,12},{6,14},{8,0},{10,2},{12,4},{14,6},{1,9},{3,11}... | collective-permute-start | bytes 196616 | tf_op jit(solution)/shard_map/ppermute | solution.py:332
  60.6 8.2 %collective-permute-start.8 = (bf16[2,32,512]{2,1,0:T(8,128)(2,1)S(1)}, bf16[2,32,512]{2,1,0:T(8,128)(2,1)S(1)}, u32[]{:S(2)}, u32[]{:S(2)}) collective-permute-start(bf16[2,32,512]{2,1,0:T(8,128)(2,1)S(1)} %get-tuple-element.58), channel_id=1, source_target_pairs={{0,10},{2,8},{4,14},{6,12},{8,2},{10,0},{12,6},{14,4},{1,11},{3,9}... | collective-permute-start | bytes 196616 | tf_op jit(solution)/shard_map/ppermute | solution.py:332
  64.5 6.4 %collective-permute-start.9 = (bf16[2,32,512]{2,1,0:T(8,128)(2,1)S(1)}, bf16[2,32,512]{2,1,0:T(8,128)(2,1)S(1)}, u32[]{:S(2)}, u32[]{:S(2)}) collective-permute-start(bf16[2,32,512]{2,1,0:T(8,128)(2,1)S(1)} %get-tuple-element.59), channel_id=1, source_target_pairs={{0,12},{2,14},{4,8},{6,10},{8,4},{10,6},{12,0},{14,2},{1,13},{3,15... | collective-permute-start | bytes 196616 | tf_op jit(solution)/shard_map/ppermute | solution.py:332
  64.5 7.2 %collective-permute-start.11 = (bf16[2,32,512]{2,1,0:T(8,128)(2,1)S(1)}, bf16[2,32,512]{2,1,0:T(8,128)(2,1)S(1)}, u32[]{:S(2)}, u32[]{:S(2)}) collective-permute-start(bf16[2,32,512]{2,1,0:T(8,128)(2,1)S(1)} %get-tuple-element.63), channel_id=1, source_target_pairs={{0,2},{2,0},{4,6},{6,4},{8,10},{10,8},{12,14},{14,12},{1,3},{3,1},... | collective-permute-start | bytes 196616 | tf_op jit(solution)/shard_map/ppermute | solution.py:332
  65.3 9.5 %collective-permute-start.12 = (bf16[2,32,512]{2,1,0:T(8,128)(2,1)S(1)}, bf16[2,32,512]{2,1,0:T(8,128)(2,1)S(1)}, u32[]{:S(2)}, u32[]{:S(2)}) collective-permute-start(bf16[2,32,512]{2,1,0:T(8,128)(2,1)S(1)} %get-tuple-element.64), channel_id=1, source_target_pairs={{0,4},{2,6},{4,0},{6,2},{8,12},{10,14},{12,8},{14,10},{1,5},{3,7},... | collective-permute-start | bytes 196616 | tf_op jit(solution)/shard_map/ppermute | solution.py:332
  65.7 13.5 %collective-permute-start.13 = (bf16[2,32,512]{2,1,0:T(8,128)(2,1)S(1)}, bf16[2,32,512]{2,1,0:T(8,128)(2,1)S(1)}, u32[]{:S(2)}, u32[]{:S(2)}) collective-permute-start(bf16[2,32,512]{2,1,0:T(8,128)(2,1)S(1)} %get-tuple-element.65), channel_id=1, source_target_pairs={{0,6},{2,4},{4,2},{6,0},{8,14},{10,12},{12,10},{14,8},{1,7},{3,5},... | collective-permute-start | bytes 196616 | tf_op jit(solution)/shard_map/ppermute | solution.py:332
  68.9 10.8 %collective-permute-start.14 = (bf16[2,32,512]{2,1,0:T(8,128)(2,1)S(1)}, bf16[2,32,512]{2,1,0:T(8,128)(2,1)S(1)}, u32[]{:S(2)}, u32[]{:S(2)}) collective-permute-start(bf16[2,32,512]{2,1,0:T(8,128)(2,1)S(1)} %get-tuple-element.66), channel_id=1, source_target_pairs={{0,8},{2,10},{4,12},{6,14},{8,0},{10,2},{12,4},{14,6},{1,9},{3,11}... | collective-permute-start | bytes 196616 | tf_op jit(solution)/shard_map/ppermute | solution.py:332
  70.8 9.3 %collective-permute-start.15 = (bf16[2,32,512]{2,1,0:T(8,128)(2,1)S(1)}, bf16[2,32,512]{2,1,0:T(8,128)(2,1)S(1)}, u32[]{:S(2)}, u32[]{:S(2)}) collective-permute-start(bf16[2,32,512]{2,1,0:T(8,128)(2,1)S(1)} %get-tuple-element.67), channel_id=1, source_target_pairs={{0,10},{2,8},{4,14},{6,12},{8,2},{10,0},{12,6},{14,4},{1,11},{3,9}... | collective-permute-start | bytes 196616 | tf_op jit(solution)/shard_map/ppermute | solution.py:332
  71.6 11.2 %collective-permute-start.16 = (bf16[2,32,512]{2,1,0:T(8,128)(2,1)S(1)}, bf16[2,32,512]{2,1,0:T(8,128)(2,1)S(1)}, u32[]{:S(2)}, u32[]{:S(2)}) collective-permute-start(bf16[2,32,512]{2,1,0:T(8,128)(2,1)S(1)} %get-tuple-element.68), channel_id=1, source_target_pairs={{0,12},{2,14},{4,8},{6,10},{8,4},{10,6},{12,0},{14,2},{1,13},{3,15... | collective-permute-start | bytes 196616 | tf_op jit(solution)/shard_map/ppermute | solution.py:332
  74.8 9.5 %collective-permute-start.17 = (bf16[2,32,512]{2,1,0:T(8,128)(2,1)S(1)}, bf16[2,32,512]{2,1,0:T(8,128)(2,1)S(1)}, u32[]{:S(2)}, u32[]{:S(2)}) collective-permute-start(bf16[2,32,512]{2,1,0:T(8,128)(2,1)S(1)} %get-tuple-element.69), channel_id=1, source_target_pairs={{0,14},{2,12},{4,10},{6,8},{8,6},{10,4},{12,2},{14,0},{1,15},{3,13... | collective-permute-start | bytes 196616 | tf_op jit(solution)/shard_map/ppermute | solution.py:332
  79.2 9.0 %collective-permute-start.25 = (bf16[2,32,512]{2,1,0:T(8,128)(2,1)S(1)}, bf16[2,32,512]{2,1,0:T(8,128)(2,1)S(1)}, u32[]{:S(2)}, u32[]{:S(2)}) collective-permute-start(bf16[2,32,512]{2,1,0:T(8,128)(2,1)S(1)} %get-tuple-element.78), channel_id=1, source_target_pairs={{0,2},{2,0},{4,6},{6,4},{8,10},{10,8},{12,14},{14,12},{1,3},{3,1},... | collective-permute-start | bytes 196616 | tf_op jit(solution)/shard_map/ppermute | solution.py:332
  79.7 11.8 %collective-permute-start.26 = (bf16[2,32,512]{2,1,0:T(8,128)(2,1)S(1)}, bf16[2,32,512]{2,1,0:T(8,128)(2,1)S(1)}, u32[]{:S(2)}, u32[]{:S(2)}) collective-permute-start(bf16[2,32,512]{2,1,0:T(8,128)(2,1)S(1)} %get-tuple-element.79), channel_id=1, source_target_pairs={{0,4},{2,6},{4,0},{6,2},{8,12},{10,14},{12,8},{14,10},{1,5},{3,7},... | collective-permute-start | bytes 196616 | tf_op jit(solution)/shard_map/ppermute | solution.py:332
  80.2 13.0 %collective-permute-start.27 = (bf16[2,32,512]{2,1,0:T(8,128)(2,1)S(1)}, bf16[2,32,512]{2,1,0:T(8,128)(2,1)S(1)}, u32[]{:S(2)}, u32[]{:S(2)}) collective-permute-start(bf16[2,32,512]{2,1,0:T(8,128)(2,1)S(1)} %get-tuple-element.80), channel_id=1, source_target_pairs={{0,6},{2,4},{4,2},{6,0},{8,14},{10,12},{12,10},{14,8},{1,7},{3,5},... | collective-permute-start | bytes 196616 | tf_op jit(solution)/shard_map/ppermute | solution.py:332
  82.8 10.8 %collective-permute-start.28 = (bf16[2,32,512]{2,1,0:T(8,128)(2,1)S(1)}, bf16[2,32,512]{2,1,0:T(8,128)(2,1)S(1)}, u32[]{:S(2)}, u32[]{:S(2)}) collective-permute-start(bf16[2,32,512]{2,1,0:T(8,128)(2,1)S(1)} %get-tuple-element.81), channel_id=1, source_target_pairs={{0,8},{2,10},{4,12},{6,14},{8,0},{10,2},{12,4},{14,6},{1,9},{3,11}... | collective-permute-start | bytes 196616 | tf_op jit(solution)/shard_map/ppermute | solution.py:332
  84.3 9.2 %collective-permute-start.29 = (bf16[2,32,512]{2,1,0:T(8,128)(2,1)S(1)}, bf16[2,32,512]{2,1,0:T(8,128)(2,1)S(1)}, u32[]{:S(2)}, u32[]{:S(2)}) collective-permute-start(bf16[2,32,512]{2,1,0:T(8,128)(2,1)S(1)} %get-tuple-element.82), channel_id=1, source_target_pairs={{0,10},{2,8},{4,14},{6,12},{8,2},{10,0},{12,6},{14,4},{1,11},{3,9}... | collective-permute-start | bytes 196616 | tf_op jit(solution)/shard_map/ppermute | solution.py:332
  88.2 8.5 %collective-permute-start.30 = (bf16[2,32,512]{2,1,0:T(8,128)(2,1)S(1)}, bf16[2,32,512]{2,1,0:T(8,128)(2,1)S(1)}, u32[]{:S(2)}, u32[]{:S(2)}) collective-permute-start(bf16[2,32,512]{2,1,0:T(8,128)(2,1)S(1)} %get-tuple-element.83), channel_id=1, source_target_pairs={{0,12},{2,14},{4,8},{6,10},{8,4},{10,6},{12,0},{14,2},{1,13},{3,15... | collective-permute-start | bytes 196616 | tf_op jit(solution)/shard_map/ppermute | solution.py:332
  91.5 7.6 %collective-permute-start.31 = (bf16[2,32,512]{2,1,0:T(8,128)(2,1)S(1)}, bf16[2,32,512]{2,1,0:T(8,128)(2,1)S(1)}, u32[]{:S(2)}, u32[]{:S(2)}) collective-permute-start(bf16[2,32,512]{2,1,0:T(8,128)(2,1)S(1)} %get-tuple-element.84), channel_id=1, source_target_pairs={{0,14},{2,12},{4,10},{6,8},{8,6},{10,4},{12,2},{14,0},{1,15},{3,13... | collective-permute-start | bytes 196616 | tf_op jit(solution)/shard_map/ppermute | solution.py:332
  93.2 6.3 %collective-permute-start.18 = (bf16[2,32,512]{2,1,0:T(8,128)(2,1)S(1)}, bf16[2,32,512]{2,1,0:T(8,128)(2,1)S(1)}, u32[]{:S(2)}, u32[]{:S(2)}) collective-permute-start(bf16[2,32,512]{2,1,0:T(8,128)(2,1)S(1)} %get-tuple-element.71), channel_id=1, source_target_pairs={{0,2},{2,0},{4,6},{6,4},{8,10},{10,8},{12,14},{14,12},{1,3},{3,1},... | collective-permute-start | bytes 196616 | tf_op jit(solution)/shard_map/ppermute | solution.py:332
  93.6 9.1 %collective-permute-start.19 = (bf16[2,32,512]{2,1,0:T(8,128)(2,1)S(1)}, bf16[2,32,512]{2,1,0:T(8,128)(2,1)S(1)}, u32[]{:S(2)}, u32[]{:S(2)}) collective-permute-start(bf16[2,32,512]{2,1,0:T(8,128)(2,1)S(1)} %get-tuple-element.72), channel_id=1, source_target_pairs={{0,4},{2,6},{4,0},{6,2},{8,12},{10,14},{12,8},{14,10},{1,5},{3,7},... | collective-permute-start | bytes 196616 | tf_op jit(solution)/shard_map/ppermute | solution.py:332
  93.6 12.2 %collective-permute-start.20 = (bf16[2,32,512]{2,1,0:T(8,128)(2,1)S(1)}, bf16[2,32,512]{2,1,0:T(8,128)(2,1)S(1)}, u32[]{:S(2)}, u32[]{:S(2)}) collective-permute-start(bf16[2,32,512]{2,1,0:T(8,128)(2,1)S(1)} %get-tuple-element.73), channel_id=1, source_target_pairs={{0,6},{2,4},{4,2},{6,0},{8,14},{10,12},{12,10},{14,8},{1,7},{3,5},... | collective-permute-start | bytes 196616 | tf_op jit(solution)/shard_map/ppermute | solution.py:332
  96.7 9.1 %collective-permute-start.21 = (bf16[2,32,512]{2,1,0:T(8,128)(2,1)S(1)}, bf16[2,32,512]{2,1,0:T(8,128)(2,1)S(1)}, u32[]{:S(2)}, u32[]{:S(2)}) collective-permute-start(bf16[2,32,512]{2,1,0:T(8,128)(2,1)S(1)} %get-tuple-element.74), channel_id=1, source_target_pairs={{0,8},{2,10},{4,12},{6,14},{8,0},{10,2},{12,4},{14,6},{1,9},{3,11}... | collective-permute-start | bytes 196616 | tf_op jit(solution)/shard_map/ppermute | solution.py:332
  99.1 6.8 %collective-permute-start.22 = (bf16[2,32,512]{2,1,0:T(8,128)(2,1)S(1)}, bf16[2,32,512]{2,1,0:T(8,128)(2,1)S(1)}, u32[]{:S(2)}, u32[]{:S(2)}) collective-permute-start(bf16[2,32,512]{2,1,0:T(8,128)(2,1)S(1)} %get-tuple-element.75), channel_id=1, source_target_pairs={{0,10},{2,8},{4,14},{6,12},{8,2},{10,0},{12,6},{14,4},{1,11},{3,9}... | collective-permute-start | bytes 196616 | tf_op jit(solution)/shard_map/ppermute | solution.py:332
  99.4 6.4 %collective-permute-start.23 = (bf16[2,32,512]{2,1,0:T(8,128)(2,1)S(1)}, bf16[2,32,512]{2,1,0:T(8,128)(2,1)S(1)}, u32[]{:S(2)}, u32[]{:S(2)}) collective-permute-start(bf16[2,32,512]{2,1,0:T(8,128)(2,1)S(1)} %get-tuple-element.76), channel_id=1, source_target_pairs={{0,12},{2,14},{4,8},{6,10},{8,4},{10,6},{12,0},{14,2},{1,13},{3,15... | collective-permute-start | bytes 196616 | tf_op jit(solution)/shard_map/ppermute | solution.py:332
  102.7 7.0 %collective-permute-start.24 = (bf16[2,32,512]{2,1,0:T(8,128)(2,1)S(1)}, bf16[2,32,512]{2,1,0:T(8,128)(2,1)S(1)}, u32[]{:S(2)}, u32[]{:S(2)}) collective-permute-start(bf16[2,32,512]{2,1,0:T(8,128)(2,1)S(1)} %get-tuple-element.77), channel_id=1, source_target_pairs={{0,14},{2,12},{4,10},{6,8},{8,6},{10,4},{12,2},{14,0},{1,15},{3,13... | collective-permute-start | bytes 196616 | tf_op jit(solution)/shard_map/ppermute | solution.py:332
  (17 other events, 162.8 us)

commit v4 on v3

--- a/solution.py
+++ b/solution.py
@@ -11,7 +11,7 @@
 parts = 2
 taps = 3
 most_direct = 8
-vmem_bytes = 48 * 1024 * 1024
+mebibyte = 1024 * 1024
 
 VMEM = pl.BlockSpec(memory_space=pltpu.VMEM)
 SMEM = pl.BlockSpec(memory_space=pltpu.SMEM)
@@ -31,8 +31,8 @@
     return pl.CostEstimate(flops=flops, bytes_accessed=size, transcendentals=0)
 
 
-def params():
-    return pltpu.CompilerParams(vmem_limit_bytes=vmem_bytes)
+def params(mebibytes):
+    return pltpu.CompilerParams(vmem_limit_bytes=mebibytes * mebibyte)
 
 
 def pick_kernel(first, begin, video, out, sem):
@@ -51,7 +51,7 @@
         in_specs=[ANY],
         out_specs=ANY,
         scratch_shapes=[pltpu.SemaphoreType.DMA],
-        compiler_params=params(),
+        compiler_params=params(56),
         name="pick",
     )(video)
 
@@ -95,7 +95,7 @@
             pltpu.VMEM((frames, pixels, channels), jnp.bfloat16),
             pltpu.SemaphoreType.DMA,
         ],
-        compiler_params=params(),
+        compiler_params=params(20),
         cost_estimate=cost(flops, w_time, w_down),
         name="early",
     )(video, w_time, b_time, w_down, b_down)
@@ -136,13 +136,13 @@
         in_specs=[SMEM] + [VMEM] * 7,
         out_specs=VMEM,
         scratch_shapes=[pltpu.VMEM((taps, pixels, channels), jnp.bfloat16)],
-        compiler_params=params(),
+        compiler_params=params(20),
         cost_estimate=cost(flops, halo, own, part, w_time, w_down),
         name="lift",
     )(started, halo, own, part, w_time, b_time, w_down, b_down)
 
 
-def space_kernel(owners, order, left, middle, right, weights, bias, *refs):
+def space_kernel(owners, joined, order, left, middle, right, weights, bias, *refs):
     outs, result = refs[:-1], refs[-1]
     halves, pixels, channels = result.shape
     rows = middle.shape[1] - 2
@@ -158,28 +158,32 @@
         value = window(middle, 1).astype(jnp.float32) + silu(acc)
         result[s] = value.astype(jnp.bfloat16)
 
+    each = pixels // owners
     if owners == 1:
         outs[0][...] = result[...]
+    elif joined:
+        for j in range(owners):
+            outs[0][j] = result[:, j * each : (j + 1) * each]
     else:
-        each = pixels // owners
         for j, out in enumerate(outs):
             begin = pl.multiple_of(order[j] * each, each)
             out[...] = result[:, pl.ds(begin, each)]
 
 
-def space(order, left, middle, right, weights, bias):
+def space(joined, order, left, middle, right, weights, bias):
     halves, rows, width, channels = middle.shape
     owners = order.shape[0]
     pixels = (rows - 2) * width
     flops = 2 * 9 * channels * channels * halves * pixels
-    block = jax.ShapeDtypeStruct((halves, pixels // owners, channels), jnp.bfloat16)
+    block = (halves, pixels // owners, channels)
+    shapes = [(owners,) + block] if joined else [block] * owners
     return pl.pallas_call(
-        partial(space_kernel, owners),
-        out_shape=[block] * owners,
+        partial(space_kernel, owners, joined),
+        out_shape=[jax.ShapeDtypeStruct(shape, jnp.bfloat16) for shape in shapes],
         in_specs=[SMEM] + [VMEM] * 5,
-        out_specs=[VMEM] * owners,
+        out_specs=[VMEM] * len(shapes),
         scratch_shapes=[pltpu.VMEM((halves, pixels, channels), jnp.bfloat16)],
-        compiler_params=params(),
+        compiler_params=params(20),
         cost_estimate=cost(flops, left, middle, right, weights),
         name="space",
     )(order, left, middle, right, weights, bias)
@@ -249,13 +253,14 @@
         blocks = [b.reshape(frames_per * pixels, channels) for b in blocks]
     count = len(blocks)
     rows = frames_per * pixels * count
+    size = frames_per * count * lanes
     flops = 2 * rows * channels * (4 * channels + 2 * frames_per * count * lanes)
     outs = pl.pallas_call(
         partial(attend_kernel, frames_per, lanes, count),
         out_shape=[jax.ShapeDtypeStruct(b.shape, jnp.bfloat16) for b in blocks],
         in_specs=[SMEM] + [VMEM] * (count + 5),
         out_specs=[VMEM] * count,
-        compiler_params=params(),
+        compiler_params=params(20 if 16 * size * size < 20 * mebibyte else 56),
         cost_estimate=cost(flops, *blocks, w_query, w_key, w_value, w_out),
         name="attend",
     )(first, *blocks, gain, w_query, w_key, w_value, w_out)
@@ -263,12 +268,12 @@
 
 
 def collect_kernel(count, base, order, *refs):
-    blocks = refs[:count]
     out, sems = refs[-2:]
-    copies = [
-        pltpu.make_async_copy(block, out.at[:, base + order[j]], sems.at[j])
-        for j, block in enumerate(blocks)
-    ]
+    joined = len(refs[0].shape) == 4
+    copies = []
+    for j in range(count):
+        block, owner = (refs[0].at[j], j) if joined else (refs[j], order[j])
+        copies.append(pltpu.make_async_copy(block, out.at[:, base + owner], sems.at[j]))
     for copy in copies:
         copy.start()
     for copy in copies:
@@ -276,18 +281,18 @@
 
 
 def collect(order, blocks, chunk, chunks, whole):
-    count = len(blocks)
-    halves, pixels, channels = blocks[0].shape
+    count = order.shape[0]
+    halves, pixels, channels = blocks[0].shape[-3:]
     shape = (halves, chunks * count, pixels, channels)
     given = [] if whole is None else [whole]
     return pl.pallas_call(
         partial(collect_kernel, count, chunk * count),
         out_shape=jax.ShapeDtypeStruct(shape, jnp.bfloat16),
-        in_specs=[SMEM] + [ANY] * (count + len(given)),
+        in_specs=[SMEM] + [ANY] * (len(blocks) + len(given)),
         out_specs=ANY,
-        input_output_aliases={count + 1: 0} if given else {},
+        input_output_aliases={len(blocks) + 1: 0} if given else {},
         scratch_shapes=[pltpu.SemaphoreType.DMA((count,))],
-        compiler_params=params(),
+        compiler_params=params(16),
         name="collect",
     )(order, *blocks, *given)
 
@@ -327,6 +332,10 @@
         return lax.ppermute(last, "cols", up), lax.ppermute(head, "cols", [(j, i) for i, j in up])
 
     def exchange(blocks):
+        if len(blocks) == 1:
+            shape = blocks[0].shape
+            whole = blocks[0].reshape((devices, -1) + shape[-2:])
+            return [lax.all_to_all(whole, "tm", 0, 0, tiled=True).reshape(shape)]
         result = list(blocks)
         for j in issue:
             result[j] = lax.ppermute(blocks[j], "tm", [(i, i ^ j) for i in range(devices)])
@@ -338,8 +347,6 @@
     halos, owns, sums = [], [], []
     for begin, end in spans:
         sent = pick(video, frames - taps, begin, end)
-        if sums:
-            sent = after(sent, sums[-1])
         halos.append(lax.ppermute(sent, "tm", onward))
         own, part = early(video, begin, end, w_time, b_time, w_down, b_down)
         owns.append(own)
@@ -362,7 +369,8 @@
         left, middle, right = pieces
         to_right = jnp.concatenate([left, middle[:, :, :-1]], axis=2)
         to_left = jnp.concatenate([middle[:, :, 1:], right], axis=2)
-        spatials.append(space(order, to_right, middle, to_left, w_space, b_space))
+        joined = direct and index < chunks - 1
+        spatials.append(space(joined, order, to_right, middle, to_left, w_space, b_space))
 
     newest = spatials[-1][0]
     if direct:
@@ -370,8 +378,14 @@
         returns = []
         for gathered in [exchange(blocks) for blocks in spatials]:
             gathered[0] = after(gathered[0], newest)
-            results = attend(order * halves, gathered, gain, w_query, w_key, w_value, w_out)
+            starts = order * halves
+            if len(gathered) == 1:
+                gathered[0] = gathered[0].reshape(devices * halves, each, channels)
+                starts = jnp.zeros(1, jnp.int32)
+            results = attend(starts, gathered, gain, w_query, w_key, w_value, w_out)
             newest = results[0]
+            if len(results) == 1:
+                results = [results[0].reshape(devices, halves, each, channels)]
             returns.append(exchange(results))
         for index, blocks in enumerate(returns):
             whole = collect(order, blocks, index, chunks, whole)

time: 112 us -> 151 us (1.35)
  Pallas kernels: 33.2 us -> 75.2 us
  starting transfers between devices: 54.2 us -> 44.6 us
  local copies, waits for them, and re-layouts: 4.27 us -> 9.82 us
  waiting for transfers between devices: 17.4 us -> 19 us
    pallas_call x2, Pallas kernels: 1.77 us -> 49.9 us  [pick(): pl.pallas_call(partial(pick_kernel, first, begin), out_shape=jax.ShapeDty...]
    ppermute x28 -> x14, starting transfers between devices: 44.7 us -> 26.7 us  [exchange(): lax.ppermute(blocks[j], 'tm', [(i, i ^ j) for i in range(devices)])]
    ppermute x2, waiting for transfers between devices: 10.2 us -> 0.01 us  [per_device(): halos.append(lax.ppermute(sent, 'tm', onward))]
    ppermute x28 -> x14, waiting for transfers between devices: 6.55 us -> 15.9 us  [exchange(): lax.ppermute(blocks[j], 'tm', [(i, i ^ j) for i in range(devices)])]
    all_to_all x0 -> x2, starting transfers between devices: none -> 8.37 us  [exchange(): return [lax.all_to_all(whole, 'tm', 0, 0, tiled=True).reshape(shape)]]
    unnamed x32 -> x46, local copies, waits for them, and re-layouts: 3.72 us -> 9.25 us
    pallas_call x2, Pallas kernels: 10.9 us -> 6.99 us  [space(): pl.pallas_call(partial(space_kernel, owners, joined), out_shape=[jax.Shap...]
    pallas_call x2, Pallas kernels: 5.61 us -> 3.27 us  [early(): pl.pallas_call(partial(early_kernel, begin), out_shape=[jax.ShapeDtypeStr...]
  transfers between devices with their start and end apart: 32 -> 20, of which waited for: 9 -> 8; matrix products, arithmetic and copies ran while one was open for 2% -> 1% of each run, Pallas kernels for 25% -> 29%
where the time goes in v4:
time: 151 us
  Pallas kernels  75.2 us (50%)
  starting transfers between devices  44.6 us (30%)
  waiting for transfers between devices  19 us (13%)
  local copies, waits for them, and re-layouts  9.82 us (7%)
  other arithmetic  1.59 us (1%)
    pallas_call x2, Pallas kernels, pick(): pl.pallas_call(partial(pick_kernel, first, begin), out_shape=jax.ShapeDty...  49.9 us
    ppermute x14, starting transfers between devices, exchange(): lax.ppermute(blocks[j], 'tm', [(i, i ^ j) for i in range(devices)])  26.7 us
    ppermute x14, waiting for transfers between devices, exchange(): lax.ppermute(blocks[j], 'tm', [(i, i ^ j) for i in range(devices)])  15.9 us
    ppermute x2, starting transfers between devices, per_device(): halos.append(lax.ppermute(sent, 'tm', onward))  9.31 us
    unnamed x46, local copies, waits for them, and re-layouts  9.25 us
    all_to_all x2, starting transfers between devices, exchange(): return [lax.all_to_all(whole, 'tm', 0, 0, tiled=True).reshape(shape)]  8.37 us
    pallas_call x2, Pallas kernels, space(): pl.pallas_call(partial(space_kernel, owners, joined), out_shape=[jax.Shap...  6.99 us
    pallas_call x2, Pallas kernels, attend(): pl.pallas_call(partial(attend_kernel, frames_per, lanes, count), out_shap...  6.6 us
  transfers between devices with their start and end apart: 20, of which 8 were waited for; matrix products, arithmetic and copies ran while one was open for 1% of the time, Pallas kernels for 29%

profile of v4, /device:TPU:0, one launch (start us, length us, event | category | flops | bytes accessed | tf_op | source)
XLA Modules:
  0.0 150.8 jit_solution(15472543574787489894)
XLA Ops:
  0.0 26.4 %pick.2 = bf16[3,17,16,512]{3,2,1,0:T(8,128)(2,1)} custom-call(bf16[4,32,16,512]{3,2,1,0:T(8,128)(2,1)} %video.7), custom_call_target="tpu_custom_call" | custom-call | tf_op jit(solution)/shard_map/pick/pallas_call | solution.py:48
  26.5 5.1 %collective-permute-start = (bf16[3,17,16,512]{3,2,1,0:T(8,128)(2,1)}, bf16[3,17,16,512]{3,2,1,0:T(8,128)(2,1)S(1)}, u32[]{:S(2)}, u32[]{:S(2)}) collective-permute-start(bf16[3,17,16,512]{3,2,1,0:T(8,128)(2,1)} %pick.2), channel_id=1, source_target_pairs={{0,2},{2,4},{4,6},{6,8},{8,10},{10,12},{12,14},{1,3},{3,5},{5,7},{... | collective-permute-start | bytes 2506760 | tf_op jit(solution)/shard_map/ppermute | solution.py:350
  31.5 23.4 %pick.3 = bf16[3,15,16,512]{3,2,1,0:T(8,128)(2,1)} custom-call(bf16[4,32,16,512]{3,2,1,0:T(8,128)(2,1)} %video.7), custom_call_target="tpu_custom_call" | custom-call | tf_op jit(solution)/shard_map/pick/pallas_call | solution.py:48
  55.0 4.3 %collective-permute-start.2 = (bf16[3,15,16,512]{3,2,1,0:T(8,128)(2,1)}, bf16[3,15,16,512]{3,2,1,0:T(8,128)(2,1)}, u32[]{:S(2)}, u32[]{:S(2)}) collective-permute-start(bf16[3,15,16,512]{3,2,1,0:T(8,128)(2,1)} %pick.3), channel_id=1, source_target_pairs={{0,2},{2,4},{4,6},{6,8},{8,10},{10,12},{12,14},{1,3},{3,5},{5,7},{... | collective-permute-start | bytes 2211848 | tf_op jit(solution)/shard_map/ppermute | solution.py:350
  59.3 1.4 copy-done.1
  60.7 1.4 copy-done.3
  62.1 1.6 %early.3 = (bf16[2,15,16,512]{3,2,1,0:T(8,128)(2,1)S(1)}, f32[1,240,512]{2,1,0:T(8,128)S(1)}) custom-call(bf16[4,32,16,512]{3,2,1,0:T(8,128)(2,1)S(1)} %copy-done, bf16[1536,512]{1,0:T(8,128)(2,1)S(1)} %bitcast.11, f32[1,512]{1,0:T(1,128)S(1)} %bitcast.19, bf16[1536,512]{1,0:T(8,128)(2,1)S(1)} %bitcast.15, f32[1,512]{1,0:T(1,128)S(1)} %bitcast.23), custom_call_target="tpu_custom_call" | custom-call | flops 1006632960 | bytes 3145728 | tf_op jit(solution)/shard_map/early/pallas_call | solution.py:85
  64.4 1.7 %early.2 = (bf16[2,17,16,512]{3,2,1,0:T(8,128)(2,1)S(1)}, f32[1,272,512]{2,1,0:T(8,128)S(1)}) custom-call(bf16[4,32,16,512]{3,2,1,0:T(8,128)(2,1)S(1)} %copy-done, bf16[1536,512]{1,0:T(8,128)(2,1)S(1)} %bitcast.12, f32[1,512]{1,0:T(1,128)S(1)} %bitcast.20, bf16[1536,512]{1,0:T(8,128)(2,1)S(1)} %bitcast.16, f32[1,512]{1,0:T(1,128)S(1)} %bitcast.24), custom_call_target="tpu_custom_call" | custom-call | flops 1140850688 | bytes 3145728 | tf_op jit(solution)/shard_map/early/pallas_call | solution.py:85
  66.2 2.4 %lift.2 = bf16[2,17,16,512]{3,2,1,0:T(8,128)(2,1)S(1)} custom-call(s32[1]{0:T(128)} %bitcast.started, bf16[3,17,16,512]{3,2,1,0:T(8,128)(2,1)S(1)} %collective-permute-done.halo, bf16[2,17,16,512]{3,2,1,0:T(8,128)(2,1)S(1)} %get-tuple-element.28.own, f32[1,272,512]{2,1,0:T(8,128)S(1)} %get-tuple-element.29.part, bf16[1536,512]{1,0:T(8,128)(2,1)S(1)} %bitcast.13, ...), custom_call_target="tpu_custom_call" | custom-call | flops 1853882368 | bytes 5095424 | tf_op jit(solution)/shard_map/lift/pallas_call | solution.py:133
  70.9 3.5 %space.2 = bf16[8,2,32,512]{3,2,1,0:T(8,128)(2,1)S(1)} custom-call(s32[8]{0:T(128)S(1)} %iota_xor_fusion.order, bf16[2,18,16,512]{3,2,1,0:T(8,128)(2,1)S(1)} %get-tuple-element.60.left, bf16[2,18,16,512]{3,2,1,0:T(8,128)(2,1)S(1)} %concatenate.31.middle, bf16[2,18,16,512]{3,2,1,0:T(8,128)(2,1)S(1)} %get-tuple-element.59.right, ...), custom_call_target="tpu_custom_call" | custom-call | flops 2415919104 | bytes 6488064 | tf_op jit(solution)/shard_map/space/pallas_call | solution.py:180
  75.1 4.1 %all-to-all-start = ((bf16[8,2,32,512]{3,2,1,0:T(8,128)(2,1)}), bf16[8,2,32,512]{3,2,1,0:T(8,128)(2,1)}, u32[]{:S(2)}, u32[]{:S(2)}) async-start(bf16[8,2,32,512]{3,2,1,0:T(8,128)(2,1)} %copy-done.7), calls=%async_computation | async-start | bytes 1048576 | tf_op jit(solution)/shard_map/all_to_all | solution.py:338
  81.4 3.3 %lift.3 = bf16[2,15,16,512]{3,2,1,0:T(8,128)(2,1)S(1)} custom-call(s32[1]{0:T(128)} %bitcast.started, bf16[3,15,16,512]{3,2,1,0:T(8,128)(2,1)} %collective-permute-done.2.halo, bf16[2,15,16,512]{3,2,1,0:T(8,128)(2,1)S(1)} %copy-done.16, f32[1,240,512]{2,1,0:T(8,128)S(1)} %copy-done.18, bf16[1536,512]{1,0:T(8,128)(2,1)S(1)} %bitcast.14, ...), custom_call_target="tpu_custom_call" | custom-call | flops 1635778560 | bytes 4866048 | tf_op jit(solution)/shard_map/lift/pallas_call | solution.py:133
  86.8 2.3 %copy-done.10 = bf16[9,512,512]{2,1,0:T(8,128)(2,1)S(1)} copy-done((bf16[9,512,512]{2,1,0:T(8,128)(2,1)S(1)}, bf16[9,512,512]{2,1,0:T(8,128)(2,1)}, u32[]{:S(2)}) %copy-start.10) | copy-done | bytes 4718616
  89.2 3.5 %space.3 = (bf16[2,32,512]{2,1,0:T(8,128)(2,1)S(1)}, bf16[2,32,512]{2,1,0:T(8,128)(2,1)S(1)}, bf16[2,32,512]{2,1,0:T(8,128)(2,1)S(1)}, bf16[2,32,512]{2,1,0:T(8,...) custom-call(s32[8]{0:T(128)S(1)} %iota_xor_fusion.order, ...), custom_call_target="tpu_custom_call" | custom-call | flops 2415919104 | bytes 6488064 | tf_op jit(solution)/shard_map/space/pallas_call | solution.py:180
  92.7 1.7 %all-to-all-done = bf16[8,2,32,512]{3,2,1,0:T(8,128)(2,1)} async-done(((bf16[8,2,32,512]{3,2,1,0:T(8,128)(2,1)}), bf16[8,2,32,512]{3,2,1,0:T(8,128)(2,1)}, u32[]{:S(2)}, u32[]{:S(2)}) %all-to-all-start) | async-done | bytes 524320 | tf_op jit(solution)/shard_map/all_to_all | solution.py:338
  94.4 3.9 %attend.2 = bf16[16,32,512]{2,1,0:T(8,128)(2,1)} custom-call(s32[1]{0:T(128)} %constant.19.clone.1.first, bf16[16,32,512]{2,1,0:T(8,128)(2,1)} %bitcast.7.refs_0_, f32[1,512]{1,0:T(1,128)S(1)} %bitcast.33, bf16[512,512]{1,0:T(8,128)(2,1)S(1)} %copy-done.11, bf16[512,512]{1,0:T(8,128)(2,1)S(1)} %copy-done.12, bf16[512,512]{1,0:T(8,128)(2,1)S(1)} %copy-done.13, ...), custom_call_target="tpu_custom_call" | custom-call | flops 1342177280 | bytes 2621440 | tf_op jit(solution)/shard_map/attend/pallas_call | solution.py:258
  98.4 4.2 %all-to-all-start.1 = ((bf16[8,2,32,512]{3,2,1,0:T(8,128)(2,1)}), bf16[8,2,32,512]{3,2,1,0:T(8,128)(2,1)S(1)}, u32[]{:S(2)}, u32[]{:S(2)}) async-start(bf16[8,2,32,512]{3,2,1,0:T(8,128)(2,1)} %bitcast.9), calls=%async_computation.1 | async-start | bytes 1048576 | tf_op jit(solution)/shard_map/all_to_all | solution.py:338
  102.6 4.7 %collective-permute-start.10 = (bf16[2,32,512]{2,1,0:T(8,128)(2,1)S(1)}, bf16[2,32,512]{2,1,0:T(8,128)(2,1)S(1)}, u32[]{:S(2)}, u32[]{:S(2)}) collective-permute-start(bf16[2,32,512]{2,1,0:T(8,128)(2,1)S(1)} %get-tuple-element.42), channel_id=1, source_target_pairs={{0,14},{2,12},{4,10},{6,8},{8,6},{10,4},{12,2},{14,0},{1,15},{3,13... | collective-permute-start | bytes 196616 | tf_op jit(solution)/shard_map/ppermute | solution.py:341
  107.9 2.9 %collective-permute-start.6 = (bf16[2,32,512]{2,1,0:T(8,128)(2,1)S(1)}, bf16[2,32,512]{2,1,0:T(8,128)(2,1)S(1)}, u32[]{:S(2)}, u32[]{:S(2)}) collective-permute-start(bf16[2,32,512]{2,1,0:T(8,128)(2,1)S(1)} %get-tuple-element.38), channel_id=1, source_target_pairs={{0,6},{2,4},{4,2},{6,0},{8,14},{10,12},{12,10},{14,8},{1,7},{3,5},... | collective-permute-start | bytes 196616 | tf_op jit(solution)/shard_map/ppermute | solution.py:341
  110.8 8.1 %collective-permute-done.10.refs_7_ = bf16[2,32,512]{2,1,0:T(8,128)(2,1)S(1)} collective-permute-done((bf16[2,32,512]{2,1,0:T(8,128)(2,1)S(1)}, bf16[2,32,512]{2,1,0:T(8,128)(2,1)S(1)}, u32[]{:S(2)}, u32[]{:S(2)}) %collective-permute-start.10) | collective-permute-done | bytes 65568 | tf_op jit(solution)/shard_map/ppermute | solution.py:341
  118.9 4.3 %collective-permute-start.8 = (bf16[2,32,512]{2,1,0:T(8,128)(2,1)S(1)}, bf16[2,32,512]{2,1,0:T(8,128)(2,1)S(1)}, u32[]{:S(2)}, u32[]{:S(2)}) collective-permute-start(bf16[2,32,512]{2,1,0:T(8,128)(2,1)S(1)} %get-tuple-element.40), channel_id=1, source_target_pairs={{0,10},{2,8},{4,14},{6,12},{8,2},{10,0},{12,6},{14,4},{1,11},{3,9}... | collective-permute-start | bytes 196616 | tf_op jit(solution)/shard_map/ppermute | solution.py:341
  123.2 3.0 %collective-permute-start.9 = (bf16[2,32,512]{2,1,0:T(8,128)(2,1)S(1)}, bf16[2,32,512]{2,1,0:T(8,128)(2,1)S(1)}, u32[]{:S(2)}, u32[]{:S(2)}) collective-permute-start(bf16[2,32,512]{2,1,0:T(8,128)(2,1)S(1)} %get-tuple-element.41), channel_id=1, source_target_pairs={{0,12},{2,14},{4,8},{6,10},{8,4},{10,6},{12,0},{14,2},{1,13},{3,15... | collective-permute-start | bytes 196616 | tf_op jit(solution)/shard_map/ppermute | solution.py:341
  126.7 2.6 %collective-permute-done.9.refs_6_ = bf16[2,32,512]{2,1,0:T(8,128)(2,1)S(1)} collective-permute-done((bf16[2,32,512]{2,1,0:T(8,128)(2,1)S(1)}, bf16[2,32,512]{2,1,0:T(8,128)(2,1)S(1)}, u32[]{:S(2)}, u32[]{:S(2)}) %collective-permute-start.9) | collective-permute-done | bytes 65568 | tf_op jit(solution)/shard_map/ppermute | solution.py:341
  129.3 2.7 %attend.3 = (bf16[2,32,512]{2,1,0:T(8,128)(2,1)S(1)}, bf16[2,32,512]{2,1,0:T(8,128)(2,1)S(1)}, bf16[2,32,512]{2,1,0:T(8,128)(2,1)S(1)}, bf16[2,32,512]{2,1,0:T(8...) custom-call(s32[8]{0:T(128)S(1)} %broadcast_multiply_fusion.first, ...), custom_call_target="tpu_custom_call" | custom-call | flops 1342177280 | bytes 2621440 | tf_op jit(solution)/shard_map/attend/pallas_call | solution.py:258
  132.0 1.6 %collective-permute-start.11 = (bf16[2,32,512]{2,1,0:T(8,128)(2,1)S(1)}, bf16[2,32,512]{2,1,0:T(8,128)(2,1)S(1)}, u32[]{:S(2)}, u32[]{:S(2)}) collective-permute-start(bf16[2,32,512]{2,1,0:T(8,128)(2,1)S(1)} %get-tuple-element.44), channel_id=1, source_target_pairs={{0,2},{2,0},{4,6},{6,4},{8,10},{10,8},{12,14},{14,12},{1,3},{3,1},... | collective-permute-start | bytes 196616 | tf_op jit(solution)/shard_map/ppermute | solution.py:341
  133.5 2.0 %collective-permute-start.13 = (bf16[2,32,512]{2,1,0:T(8,128)(2,1)S(1)}, bf16[2,32,512]{2,1,0:T(8,128)(2,1)S(1)}, u32[]{:S(2)}, u32[]{:S(2)}) collective-permute-start(bf16[2,32,512]{2,1,0:T(8,128)(2,1)S(1)} %get-tuple-element.46), channel_id=1, source_target_pairs={{0,6},{2,4},{4,2},{6,0},{8,14},{10,12},{12,10},{14,8},{1,7},{3,5},... | collective-permute-start | bytes 196616 | tf_op jit(solution)/shard_map/ppermute | solution.py:341
  135.5 1.5 collective-permute-start.14
  137.0 2.4 %collective-permute-start.15 = (bf16[2,32,512]{2,1,0:T(8,128)(2,1)S(1)}, bf16[2,32,512]{2,1,0:T(8,128)(2,1)S(1)}, u32[]{:S(2)}, u32[]{:S(2)}) collective-permute-start(bf16[2,32,512]{2,1,0:T(8,128)(2,1)S(1)} %get-tuple-element.48), channel_id=1, source_target_pairs={{0,10},{2,8},{4,14},{6,12},{8,2},{10,0},{12,6},{14,4},{1,11},{3,9}... | collective-permute-start | bytes 196616 | tf_op jit(solution)/shard_map/ppermute | solution.py:341
  139.4 2.9 %collective-permute-start.16 = (bf16[2,32,512]{2,1,0:T(8,128)(2,1)S(1)}, bf16[2,32,512]{2,1,0:T(8,128)(2,1)S(1)}, u32[]{:S(2)}, u32[]{:S(2)}) collective-permute-start(bf16[2,32,512]{2,1,0:T(8,128)(2,1)S(1)} %get-tuple-element.49), channel_id=1, source_target_pairs={{0,12},{2,14},{4,8},{6,10},{8,4},{10,6},{12,0},{14,2},{1,13},{3,15... | collective-permute-start | bytes 196616 | tf_op jit(solution)/shard_map/ppermute | solution.py:341
  144.6 2.1 %collective-permute-done.15.refs_5_ = bf16[2,32,512]{2,1,0:T(8,128)(2,1)S(1)} collective-permute-done((bf16[2,32,512]{2,1,0:T(8,128)(2,1)S(1)}, bf16[2,32,512]{2,1,0:T(8,128)(2,1)S(1)}, u32[]{:S(2)}, u32[]{:S(2)}) %collective-permute-start.15) | collective-permute-done | bytes 65568 | tf_op jit(solution)/shard_map/ppermute | solution.py:341
  146.7 2.5 %collective-permute-done.17.refs_7_ = bf16[2,32,512]{2,1,0:T(8,128)(2,1)S(1)} collective-permute-done((bf16[2,32,512]{2,1,0:T(8,128)(2,1)S(1)}, bf16[2,32,512]{2,1,0:T(8,128)(2,1)S(1)}, u32[]{:S(2)}, u32[]{:S(2)}) %collective-permute-start.17) | collective-permute-done | bytes 65568 | tf_op jit(solution)/shard_map/ppermute | solution.py:341
  149.2 1.4 collect.3
  (86 shorter events, 11.4 us)
Async XLA Ops:
  26.4 32.8 %copy-start = (bf16[4,32,16,512]{3,2,1,0:T(8,128)(2,1)S(1)}, bf16[4,32,16,512]{3,2,1,0:T(8,128)(2,1)}, u32[]{:S(2)}) copy-start(bf16[4,32,16,512]{3,2,1,0:T(8,128)(2,1)} %video.7) | copy-start | bytes 6291460
  26.4 32.8 %copy-start.8 = (f32[512]{0:T(512)S(1)}, f32[512]{0:T(512)}, u32[]{:S(2)}) copy-start(f32[512]{0:T(512)} %param.14) | copy-start | bytes 6148
  26.5 32.8 %copy-start.9 = (f32[512]{0:T(512)S(1)}, f32[512]{0:T(512)}, u32[]{:S(2)}) copy-start(f32[512]{0:T(512)} %param.16) | copy-start | bytes 6148
  26.5 39.7 %collective-permute-start = (bf16[3,17,16,512]{3,2,1,0:T(8,128)(2,1)}, bf16[3,17,16,512]{3,2,1,0:T(8,128)(2,1)S(1)}, u32[]{:S(2)}, u32[]{:S(2)}) collective-permute-start(bf16[3,17,16,512]{3,2,1,0:T(8,128)(2,1)} %pick.2), channel_id=1, source_target_pairs={{0,2},{2,4},{4,6},{6,8},{8,10},{10,12},{12,14},{1,3},{3,5},{5,7},{... | collective-permute-start | bytes 2506760 | tf_op jit(solution)/shard_map/ppermute | solution.py:350
  55.0 24.3 %collective-permute-start.2 = (bf16[3,15,16,512]{3,2,1,0:T(8,128)(2,1)}, bf16[3,15,16,512]{3,2,1,0:T(8,128)(2,1)}, u32[]{:S(2)}, u32[]{:S(2)}) collective-permute-start(bf16[3,15,16,512]{3,2,1,0:T(8,128)(2,1)} %pick.3), channel_id=1, source_target_pairs={{0,2},{2,4},{4,6},{6,8},{8,10},{10,12},{12,14},{1,3},{3,5},{5,7},{... | collective-permute-start | bytes 2211848 | tf_op jit(solution)/shard_map/ppermute | solution.py:350
  64.4 6.3 %slice-start.1 = ((s8[4718592]{0:T(1024)(128)(4,1)}), s8[4194304]{0:T(1024)(128)(4,1)S(1)}, s32[]{:S(2)}) async-start(s8[4718592]{0:T(1024)(128)(4,1)} %bitcast.27), calls=%async_computation.3 | async-start | bytes 8388608
  66.2 4.5 %slice-start.2 = ((s8[4718592]{0:T(1024)(128)(4,1)}), s8[524288]{0:T(1024)(128)(4,1)S(1)}, s32[]{:S(2)}) async-start(s8[4718592]{0:T(1024)(128)(4,1)} %bitcast.27), calls=%async_computation.4 | async-start | bytes 1048576
  68.7 1.3 collective-permute-start.1
  70.8 8.5 %copy-start.2 = (bf16[3,512,512]{2,1,0:T(8,128)(2,1)S(1)}, bf16[3,512,512]{2,1,0:T(8,128)(2,1)}, u32[]{:S(2)}) copy-start(bf16[3,512,512]{2,1,0:T(8,128)(2,1)} %param.13) | copy-start | bytes 4718596
  70.8 8.5 %copy-start.5 = (bf16[3,512,512]{2,1,0:T(8,128)(2,1)S(1)}, bf16[3,512,512]{2,1,0:T(8,128)(2,1)}, u32[]{:S(2)}) copy-start(bf16[3,512,512]{2,1,0:T(8,128)(2,1)} %param.15) | copy-start | bytes 4718596
  75.1 19.2 %all-to-all-start = ((bf16[8,2,32,512]{3,2,1,0:T(8,128)(2,1)}), bf16[8,2,32,512]{3,2,1,0:T(8,128)(2,1)}, u32[]{:S(2)}, u32[]{:S(2)}) async-start(bf16[8,2,32,512]{3,2,1,0:T(8,128)(2,1)} %copy-done.7), calls=%async_computation | async-start | bytes 1048576 | tf_op jit(solution)/shard_map/all_to_all | solution.py:338
  84.8 1.3 collective-permute-start.3
  89.2 5.2 %copy-start.11 = (bf16[512,512]{1,0:T(8,128)(2,1)S(1)}, bf16[512,512]{1,0:T(8,128)(2,1)}, u32[]{:S(2)}) copy-start(bf16[512,512]{1,0:T(8,128)(2,1)} %refs_9_.1) | copy-start | bytes 1572868
  89.2 5.2 %copy-start.12 = (bf16[512,512]{1,0:T(8,128)(2,1)S(1)}, bf16[512,512]{1,0:T(8,128)(2,1)}, u32[]{:S(2)}) copy-start(bf16[512,512]{1,0:T(8,128)(2,1)} %refs_10_.1) | copy-start | bytes 1572868
  89.2 5.2 %copy-start.13 = (bf16[512,512]{1,0:T(8,128)(2,1)S(1)}, bf16[512,512]{1,0:T(8,128)(2,1)}, u32[]{:S(2)}) copy-start(bf16[512,512]{1,0:T(8,128)(2,1)} %refs_11_.1) | copy-start | bytes 1572868
  89.2 5.2 %copy-start.14 = (bf16[512,512]{1,0:T(8,128)(2,1)S(1)}, bf16[512,512]{1,0:T(8,128)(2,1)}, u32[]{:S(2)}) copy-start(bf16[512,512]{1,0:T(8,128)(2,1)} %refs_12_.1) | copy-start | bytes 1572868
  89.2 5.2 %copy-start.20 = (f32[512]{0:T(512)S(1)}, f32[512]{0:T(512)}, u32[]{:S(2)}) copy-start(f32[512]{0:T(512)} %param.19) | copy-start | bytes 6148
  98.4 44.8 %all-to-all-start.1 = ((bf16[8,2,32,512]{3,2,1,0:T(8,128)(2,1)}), bf16[8,2,32,512]{3,2,1,0:T(8,128)(2,1)S(1)}, u32[]{:S(2)}, u32[]{:S(2)}) async-start(bf16[8,2,32,512]{3,2,1,0:T(8,128)(2,1)} %bitcast.9), calls=%async_computation.1 | async-start | bytes 1048576 | tf_op jit(solution)/shard_map/all_to_all | solution.py:338
  102.6 16.3 %collective-permute-start.10 = (bf16[2,32,512]{2,1,0:T(8,128)(2,1)S(1)}, bf16[2,32,512]{2,1,0:T(8,128)(2,1)S(1)}, u32[]{:S(2)}, u32[]{:S(2)}) collective-permute-start(bf16[2,32,512]{2,1,0:T(8,128)(2,1)S(1)} %get-tuple-element.42), channel_id=1, source_target_pairs={{0,14},{2,12},{4,10},{6,8},{8,6},{10,4},{12,2},{14,0},{1,15},{3,13... | collective-permute-start | bytes 196616 | tf_op jit(solution)/shard_map/ppermute | solution.py:341
  107.3 15.9 %collective-permute-start.4 = (bf16[2,32,512]{2,1,0:T(8,128)(2,1)S(1)}, bf16[2,32,512]{2,1,0:T(8,128)(2,1)S(1)}, u32[]{:S(2)}, u32[]{:S(2)}) collective-permute-start(bf16[2,32,512]{2,1,0:T(8,128)(2,1)S(1)} %get-tuple-element.36), channel_id=1, source_target_pairs={{0,2},{2,0},{4,6},{6,4},{8,10},{10,8},{12,14},{14,12},{1,3},{3,1},... | collective-permute-start | bytes 196616 | tf_op jit(solution)/shard_map/ppermute | solution.py:341
  107.9 18.3 %collective-permute-start.5 = (bf16[2,32,512]{2,1,0:T(8,128)(2,1)S(1)}, bf16[2,32,512]{2,1,0:T(8,128)(2,1)S(1)}, u32[]{:S(2)}, u32[]{:S(2)}) collective-permute-start(bf16[2,32,512]{2,1,0:T(8,128)(2,1)S(1)} %get-tuple-element.37), channel_id=1, source_target_pairs={{0,4},{2,6},{4,0},{6,2},{8,12},{10,14},{12,8},{14,10},{1,5},{3,7},... | collective-permute-start | bytes 196616 | tf_op jit(solution)/shard_map/ppermute | solution.py:341
  107.9 18.3 %collective-permute-start.6 = (bf16[2,32,512]{2,1,0:T(8,128)(2,1)S(1)}, bf16[2,32,512]{2,1,0:T(8,128)(2,1)S(1)}, u32[]{:S(2)}, u32[]{:S(2)}) collective-permute-start(bf16[2,32,512]{2,1,0:T(8,128)(2,1)S(1)} %get-tuple-element.38), channel_id=1, source_target_pairs={{0,6},{2,4},{4,2},{6,0},{8,14},{10,12},{12,10},{14,8},{1,7},{3,5},... | collective-permute-start | bytes 196616 | tf_op jit(solution)/shard_map/ppermute | solution.py:341
  110.8 15.4 %collective-permute-start.7 = (bf16[2,32,512]{2,1,0:T(8,128)(2,1)S(1)}, bf16[2,32,512]{2,1,0:T(8,128)(2,1)S(1)}, u32[]{:S(2)}, u32[]{:S(2)}) collective-permute-start(bf16[2,32,512]{2,1,0:T(8,128)(2,1)S(1)} %get-tuple-element.39), channel_id=1, source_target_pairs={{0,8},{2,10},{4,12},{6,14},{8,0},{10,2},{12,4},{14,6},{1,9},{3,11}... | collective-permute-start | bytes 196616 | tf_op jit(solution)/shard_map/ppermute | solution.py:341
  118.9 7.8 %collective-permute-start.8 = (bf16[2,32,512]{2,1,0:T(8,128)(2,1)S(1)}, bf16[2,32,512]{2,1,0:T(8,128)(2,1)S(1)}, u32[]{:S(2)}, u32[]{:S(2)}) collective-permute-start(bf16[2,32,512]{2,1,0:T(8,128)(2,1)S(1)} %get-tuple-element.40), channel_id=1, source_target_pairs={{0,10},{2,8},{4,14},{6,12},{8,2},{10,0},{12,6},{14,4},{1,11},{3,9}... | collective-permute-start | bytes 196616 | tf_op jit(solution)/shard_map/ppermute | solution.py:341
  123.2 6.1 %collective-permute-start.9 = (bf16[2,32,512]{2,1,0:T(8,128)(2,1)S(1)}, bf16[2,32,512]{2,1,0:T(8,128)(2,1)S(1)}, u32[]{:S(2)}, u32[]{:S(2)}) collective-permute-start(bf16[2,32,512]{2,1,0:T(8,128)(2,1)S(1)} %get-tuple-element.41), channel_id=1, source_target_pairs={{0,12},{2,14},{4,8},{6,10},{8,4},{10,6},{12,0},{14,2},{1,13},{3,15... | collective-permute-start | bytes 196616 | tf_op jit(solution)/shard_map/ppermute | solution.py:341
  132.0 7.4 %collective-permute-start.11 = (bf16[2,32,512]{2,1,0:T(8,128)(2,1)S(1)}, bf16[2,32,512]{2,1,0:T(8,128)(2,1)S(1)}, u32[]{:S(2)}, u32[]{:S(2)}) collective-permute-start(bf16[2,32,512]{2,1,0:T(8,128)(2,1)S(1)} %get-tuple-element.44), channel_id=1, source_target_pairs={{0,2},{2,0},{4,6},{6,4},{8,10},{10,8},{12,14},{14,12},{1,3},{3,1},... | collective-permute-start | bytes 196616 | tf_op jit(solution)/shard_map/ppermute | solution.py:341
  133.5 8.7 %collective-permute-start.12 = (bf16[2,32,512]{2,1,0:T(8,128)(2,1)S(1)}, bf16[2,32,512]{2,1,0:T(8,128)(2,1)S(1)}, u32[]{:S(2)}, u32[]{:S(2)}) collective-permute-start(bf16[2,32,512]{2,1,0:T(8,128)(2,1)S(1)} %get-tuple-element.45), channel_id=1, source_target_pairs={{0,4},{2,6},{4,0},{6,2},{8,12},{10,14},{12,8},{14,10},{1,5},{3,7},... | collective-permute-start | bytes 196616 | tf_op jit(solution)/shard_map/ppermute | solution.py:341
  133.5 11.0 %collective-permute-start.13 = (bf16[2,32,512]{2,1,0:T(8,128)(2,1)S(1)}, bf16[2,32,512]{2,1,0:T(8,128)(2,1)S(1)}, u32[]{:S(2)}, u32[]{:S(2)}) collective-permute-start(bf16[2,32,512]{2,1,0:T(8,128)(2,1)S(1)} %get-tuple-element.46), channel_id=1, source_target_pairs={{0,6},{2,4},{4,2},{6,0},{8,14},{10,12},{12,10},{14,8},{1,7},{3,5},... | collective-permute-start | bytes 196616 | tf_op jit(solution)/shard_map/ppermute | solution.py:341
  135.5 9.1 %collective-permute-start.14 = (bf16[2,32,512]{2,1,0:T(8,128)(2,1)S(1)}, bf16[2,32,512]{2,1,0:T(8,128)(2,1)S(1)}, u32[]{:S(2)}, u32[]{:S(2)}) collective-permute-start(bf16[2,32,512]{2,1,0:T(8,128)(2,1)S(1)} %get-tuple-element.47), channel_id=1, source_target_pairs={{0,8},{2,10},{4,12},{6,14},{8,0},{10,2},{12,4},{14,6},{1,9},{3,11}... | collective-permute-start | bytes 196616 | tf_op jit(solution)/shard_map/ppermute | solution.py:341
  137.0 9.7 %collective-permute-start.15 = (bf16[2,32,512]{2,1,0:T(8,128)(2,1)S(1)}, bf16[2,32,512]{2,1,0:T(8,128)(2,1)S(1)}, u32[]{:S(2)}, u32[]{:S(2)}) collective-permute-start(bf16[2,32,512]{2,1,0:T(8,128)(2,1)S(1)} %get-tuple-element.48), channel_id=1, source_target_pairs={{0,10},{2,8},{4,14},{6,12},{8,2},{10,0},{12,6},{14,4},{1,11},{3,9}... | collective-permute-start | bytes 196616 | tf_op jit(solution)/shard_map/ppermute | solution.py:341
  139.4 7.3 %collective-permute-start.16 = (bf16[2,32,512]{2,1,0:T(8,128)(2,1)S(1)}, bf16[2,32,512]{2,1,0:T(8,128)(2,1)S(1)}, u32[]{:S(2)}, u32[]{:S(2)}) collective-permute-start(bf16[2,32,512]{2,1,0:T(8,128)(2,1)S(1)} %get-tuple-element.49), channel_id=1, source_target_pairs={{0,12},{2,14},{4,8},{6,10},{8,4},{10,6},{12,0},{14,2},{1,13},{3,15... | collective-permute-start | bytes 196616 | tf_op jit(solution)/shard_map/ppermute | solution.py:341
  142.3 7.0 %collective-permute-start.17 = (bf16[2,32,512]{2,1,0:T(8,128)(2,1)S(1)}, bf16[2,32,512]{2,1,0:T(8,128)(2,1)S(1)}, u32[]{:S(2)}, u32[]{:S(2)}) collective-permute-start(bf16[2,32,512]{2,1,0:T(8,128)(2,1)S(1)} %get-tuple-element.50), channel_id=1, source_target_pairs={{0,14},{2,12},{4,10},{6,8},{8,6},{10,4},{12,2},{14,0},{1,15},{3,13... | collective-permute-start | bytes 196616 | tf_op jit(solution)/shard_map/ppermute | solution.py:341
  (12 other events, 17.3 us)

commit v5 on v1

--- a/solution.py
+++ b/solution.py
@@ -216,8 +216,13 @@
     w_space = w_space.reshape(-1, channels)
     b_time, b_down, b_space, gain = (v.reshape(1, -1) for v in (b_time, b_down, b_space, gain))
 
+    def exchange(value, bit):
+        sets = [[i, i ^ bit] for i in range(devices) if i < i ^ bit]
+        both = lax.all_gather(value, "tm", axis_index_groups=sets)
+        return lax.dynamic_index_in_dim(both, (place < place ^ bit).astype(jnp.int32), keepdims=False)
+
     def swap(value):
-        return lax.ppermute(value, "tm", [(i, i ^ 1) for i in range(devices)])
+        return exchange(value, 1)
 
     def rows_of(owner, begin, end):
         low, high = owner * half + begin - 1, owner * half + end - 1
@@ -279,8 +284,7 @@
             for j in range(levels):
                 block = lax.dynamic_index_in_dim(blocks, level ^ j, 1, keepdims=False)
                 if j:
-                    route = [(i, (i // pair ^ j) * pair + i % pair) for i in range(devices)]
-                    block = lax.ppermute(block, "tm", route)
+                    block = exchange(block, j * pair)
                 gathered.append(block)
             first = jnp.stack([(level ^ j) * halves for j in range(levels)]).astype(jnp.int32)
             results = attend(first, gathered, gain, w_query, w_key, w_value, w_out)
@@ -288,8 +292,7 @@
             for j in range(levels):
                 block = results[j]
                 if j:
-                    route = [(i, (i // pair ^ j) * pair + i % pair) for i in range(devices)]
-                    block = lax.ppermute(block, "tm", route)
+                    block = exchange(block, j * pair)
                 returned.append(block)
             whole = jnp.zeros((halves, levels, pixels, channels), jnp.bfloat16)
             for j in range(levels):

time: 136 us -> 232 us (1.71)
  blocking collectives: 0 us -> 158 us
  waiting for transfers between devices: 51.6 us -> 5.18 us
  starting transfers between devices: 47.8 us -> 8.31 us
  between operations: 0.82 us -> 14.2 us
  local copies, waits for them, and re-layouts: 3.92 us -> 10 us
  other arithmetic: 6.73 us -> 11.6 us
    all_gather x0 -> x23, blocking collectives: none -> 158 us  [exchange(): both = lax.all_gather(value, 'tm', axis_index_groups=sets)]
    ppermute x24 -> x0, waiting for transfers between devices: 43 us -> none  [the longest x18 25.2 us: per_device(): block = lax.ppermute(block, 'tm', route)]
    ppermute x24 -> x0, starting transfers between devices: 39.4 us -> none  [the longest x18 30.6 us: per_device(): block = lax.ppermute(block, 'tm', route)]
    ppermute x3, waiting for transfers between devices: 5.55 us -> 2.9 us  [per_device(): lax.ppermute(upper[frames - taps:], 'tm', [(i, i + pair) for i in range(d...]
  transfers between devices with their start and end apart: 30 -> 7, of which waited for: 19 -> 5; matrix products, arithmetic and copies ran while one was open for 3% -> 5% of each run, Pallas kernels for 11% -> 4%
where the time goes in v5:
time: 232 us; the launch traced here: 231 us
  blocking collectives  158 us (68%)
  Pallas kernels  23.6 us (10%)
  between operations  14.2 us (6%)
  other arithmetic  11.6 us (5%)
  local copies, waits for them, and re-layouts  10 us (4%)
  starting transfers between devices  8.31 us (4%)
  waiting for transfers between devices  5.18 us (2%)
    all_gather x23, blocking collectives, exchange(): both = lax.all_gather(value, 'tm', axis_index_groups=sets)  158 us
    pallas_call x3, Pallas kernels, lift(): pl.pallas_call(lift_kernel, out_shape=jax.ShapeDtypeStruct((halves, rows,...  9.12 us
    ppermute x3, starting transfers between devices, per_device(): lax.ppermute(upper[frames - taps:], 'tm', [(i, i + pair) for i in range(d...  8.08 us
    pallas_call x3, Pallas kernels, space(): pl.pallas_call(space_kernel, out_shape=jax.ShapeDtypeStruct((halves, rows...  8 us
    pallas_call x3, Pallas kernels, attend(): pl.pallas_call(partial(attend_kernel, frames_per, lanes, count), out_shap...  6.45 us
  transfers between devices with their start and end apart: 7, of which 5 were waited for; matrix products, arithmetic and copies ran while one was open for 5% of the time, Pallas kernels for 4%

profile of v5, /device:TPU:0, one launch (start us, length us, event | category | flops | bytes accessed | tf_op | source)
XLA Modules:
  0.0 231.4 jit_solution(11652120630477848497)
XLA Ops:
  7.7 2.1 broadcast_select_fusion
  9.8 12.8 %all-gather = bf16[8,6,16,512]{3,2,1,0:T(8,128)(2,1)S(1)} all-gather(bf16[4,6,16,512]{3,2,1,0:T(8,128)(2,1)S(1)} %broadcast_select_fusion.4), channel_id=2, replica_groups={{0,2},{4,6},{8,10},{12,14},{1,3},{5,7},{9,11},{13,15},{16,18},{20,22},{..., dimensions={0}, use_global_device_ids=true | all-gather | bytes 1179648 | tf_op jit(solution)/shard_map/all_gather | solution.py:221
  25.4 4.4 %collective-permute-start = (bf16[3,6,16,512]{3,2,1,0:T(8,128)(2,1)}, bf16[3,6,16,512]{3,2,1,0:T(8,128)(2,1)}, u32[]{:S(2)}, u32[]{:S(2)}) collective-permute-start(bf16[3,6,16,512]{3,2,1,0:T(8,128)(2,1)} %slice.150), channel_id=1, source_target_pairs={{0,4},{2,6},{4,8},{6,10},{8,12},{10,14},{1,5},{3,7},{5,9},{7,11},{... | collective-permute-start | bytes 884744 | tf_op jit(solution)/shard_map/ppermute | solution.py:265
  36.2 3.0 %lift.3.middle = bf16[4,6,16,512]{3,2,1,0:T(8,128)(2,1)S(1)} custom-call(s32[3]{0:T(128)S(1)} %pad_add_fusion.1.flags, bf16[11,6,16,512]{3,2,1,0:T(8,128)(2,1)S(1)} %pad_maximum_fusion.1.ext, bf16[1536,512]{1,0:T(8,128)(2,1)S(1)} %bitcast.123, f32[1,512]{1,0:T(1,128)S(1)} %bitcast.129, bf16[1536,512]{1,0:T(8,128)(2,1)S(1)} %bitcast.126, f32[1,512]{1,0:T(1,128)S(1)} %bitcast.132), custom_call_target="tpu_custom_call" | custom-call | flops 1962934272 | bytes 4227072 | tf_op jit(solution)/shard_map/lift/pallas_call | solution.py:73
  42.9 7.8 %all-gather.3 = bf16[8,1,16,512]{3,2,1,0:T(8,128)(2,1)S(1)} all-gather(bf16[4,1,16,512]{3,2,1,0:T(8,128)(2,1)S(1)} %get-tuple-element.59), channel_id=5, replica_groups={{0,12},{2,14},{4,8},{6,10},{1,13},{3,15},{5,9},{7,11},{16,28},{18,30},{..., dimensions={0}, use_global_device_ids=true | all-gather | bytes 196608 | tf_op jit(solution)/shard_map/all_gather | solution.py:221
  50.7 5.8 %all-gather.2 = bf16[8,1,16,512]{3,2,1,0:T(8,128)(2,1)S(1)} all-gather(bf16[4,1,16,512]{3,2,1,0:T(8,128)(2,1)S(1)} %get-tuple-element.60), channel_id=4, replica_groups={{0,8},{2,10},{4,12},{6,14},{1,9},{3,11},{5,13},{7,15},{16,24},{18,26},{..., dimensions={0}, use_global_device_ids=true | all-gather | bytes 196608 | tf_op jit(solution)/shard_map/all_gather | solution.py:221
  56.6 4.9 %all-gather.1 = bf16[8,1,16,512]{3,2,1,0:T(8,128)(2,1)S(1)} all-gather(bf16[4,1,16,512]{3,2,1,0:T(8,128)(2,1)S(1)} %get-tuple-element.61), channel_id=3, replica_groups={{0,4},{2,6},{8,12},{10,14},{1,5},{3,7},{9,13},{11,15},{16,20},{18,22},{..., dimensions={0}, use_global_device_ids=true | all-gather | bytes 196608 | tf_op jit(solution)/shard_map/all_gather | solution.py:221
  63.5 4.9 %all-gather.4 = bf16[8,16,512]{2,1,0:T(8,128)(2,1)S(1)} all-gather(bf16[4,16,512]{2,1,0:T(8,128)(2,1)S(1)} %get-tuple-element.20), channel_id=6, replica_groups={{0,4},{2,6},{8,12},{10,14},{1,5},{3,7},{9,13},{11,15},{16,20},{18,22},{..., dimensions={0}, use_global_device_ids=true | all-gather | bytes 196608 | tf_op jit(solution)/shard_map/all_gather | solution.py:221
  68.4 7.1 %all-gather.5 = bf16[8,16,512]{2,1,0:T(8,128)(2,1)S(1)} all-gather(bf16[4,16,512]{2,1,0:T(8,128)(2,1)S(1)} %get-tuple-element.21), channel_id=7, replica_groups={{0,8},{2,10},{4,12},{6,14},{1,9},{3,11},{5,13},{7,15},{16,24},{18,26},{..., dimensions={0}, use_global_device_ids=true | all-gather | bytes 196608 | tf_op jit(solution)/shard_map/all_gather | solution.py:221
  75.5 6.7 %all-gather.6 = bf16[8,16,512]{2,1,0:T(8,128)(2,1)S(1)} all-gather(bf16[4,16,512]{2,1,0:T(8,128)(2,1)S(1)} %get-tuple-element.22), channel_id=8, replica_groups={{0,12},{2,14},{4,8},{6,10},{1,13},{3,15},{5,9},{7,11},{16,28},{18,30},{..., dimensions={0}, use_global_device_ids=true | all-gather | bytes 196608 | tf_op jit(solution)/shard_map/all_gather | solution.py:221
  82.3 6.0 %all_gather.152 = bf16[2,2,64,512]{3,2,1,0:T(8,128)(2,1)} all-gather(bf16[1,2,64,512]{3,2,1,0:T(8,128)(2,1)S(1)} %bitcast.149), channel_id=1, replica_groups={{0,2},{4,6},{8,10},{12,14},{1,3},{5,7},{9,11},{13,15},{16,18},{20,22},{..., dimensions={0}, use_global_device_ids=true | all-gather | bytes 393216 | tf_op jit(solution)/shard_map/all_gather | solution.py:221
  91.7 7.0 %all-gather.14 = bf16[8,4,16,512]{3,2,1,0:T(8,128)(2,1)S(1)} all-gather(bf16[4,4,16,512]{3,2,1,0:T(8,128)(2,1)S(1)} %copy-done.17), channel_id=16, replica_groups={{0,2},{4,6},{8,10},{12,14},{1,3},{5,7},{9,11},{13,15},{16,18},{20,22},{..., dimensions={0}, use_global_device_ids=true | all-gather | bytes 786432 | tf_op jit(solution)/shard_map/all_gather | solution.py:221
  100.3 2.3 %collective-permute-start.2 = (bf16[3,8,16,512]{3,2,1,0:T(8,128)(2,1)S(1)}, bf16[3,8,16,512]{3,2,1,0:T(8,128)(2,1)S(1)}, u32[]{:S(2)}, u32[]{:S(2)}) collective-permute-start(bf16[3,8,16,512]{3,2,1,0:T(8,128)(2,1)S(1)} %slice.158), channel_id=1, source_target_pairs={{0,4},{2,6},{4,8},{6,10},{8,12},{10,14},{1,5},{3,7},{5,9},{7,11},{... | collective-permute-start | bytes 1179656 | tf_op jit(solution)/shard_map/ppermute | solution.py:265
  103.4 2.3 lift.5
  108.0 3.8 %lift.4 = bf16[4,8,16,512]{3,2,1,0:T(8,128)(2,1)S(1)} custom-call(s32[3]{0:T(128)S(1)} %stack.53.flags, bf16[11,8,16,512]{3,2,1,0:T(8,128)(2,1)S(1)} %pad_maximum_fusion.ext, bf16[1536,512]{1,0:T(8,128)(2,1)S(1)} %bitcast.125, f32[1,512]{1,0:T(1,128)S(1)} %bitcast.131, bf16[1536,512]{1,0:T(8,128)(2,1)S(1)} %bitcast.128, f32[1,512]{1,0:T(1,128)S(1)} %bitcast.134), custom_call_target="tpu_custom_call" | custom-call | flops 2617245696 | bytes 4587520 | tf_op jit(solution)/shard_map/lift/pallas_call | solution.py:73
  115.8 9.0 %all-gather.17 = bf16[8,1,16,512]{3,2,1,0:T(8,128)(2,1)S(1)} all-gather(bf16[4,1,16,512]{3,2,1,0:T(8,128)(2,1)S(1)} %get-tuple-element.53), channel_id=19, replica_groups={{0,12},{2,14},{4,8},{6,10},{1,13},{3,15},{5,9},{7,11},{16,28},{18,30},{..., dimensions={0}, use_global_device_ids=true | all-gather | bytes 196608 | tf_op jit(solution)/shard_map/all_gather | solution.py:221
  124.8 7.6 %all-gather.16 = bf16[8,1,16,512]{3,2,1,0:T(8,128)(2,1)S(1)} all-gather(bf16[4,1,16,512]{3,2,1,0:T(8,128)(2,1)S(1)} %get-tuple-element.54), channel_id=18, replica_groups={{0,8},{2,10},{4,12},{6,14},{1,9},{3,11},{5,13},{7,15},{16,24},{18,26},{..., dimensions={0}, use_global_device_ids=true | all-gather | bytes 196608 | tf_op jit(solution)/shard_map/all_gather | solution.py:221
  132.4 4.9 %all-gather.15 = bf16[8,1,16,512]{3,2,1,0:T(8,128)(2,1)S(1)} all-gather(bf16[4,1,16,512]{3,2,1,0:T(8,128)(2,1)S(1)} %get-tuple-element.55), channel_id=17, replica_groups={{0,4},{2,6},{8,12},{10,14},{1,5},{3,7},{9,13},{11,15},{16,20},{18,22},{..., dimensions={0}, use_global_device_ids=true | all-gather | bytes 196608 | tf_op jit(solution)/shard_map/all_gather | solution.py:221
  137.4 1.9 attend.5
  139.3 5.5 %all-gather.18 = bf16[8,16,512]{2,1,0:T(8,128)(2,1)S(1)} all-gather(bf16[4,16,512]{2,1,0:T(8,128)(2,1)S(1)} %get-tuple-element.30), channel_id=20, replica_groups={{0,4},{2,6},{8,12},{10,14},{1,5},{3,7},{9,13},{11,15},{16,20},{18,22},{..., dimensions={0}, use_global_device_ids=true | all-gather | bytes 196608 | tf_op jit(solution)/shard_map/all_gather | solution.py:221
  144.8 7.0 %all-gather.19 = bf16[8,16,512]{2,1,0:T(8,128)(2,1)S(1)} all-gather(bf16[4,16,512]{2,1,0:T(8,128)(2,1)S(1)} %get-tuple-element.31), channel_id=21, replica_groups={{0,8},{2,10},{4,12},{6,14},{1,9},{3,11},{5,13},{7,15},{16,24},{18,26},{..., dimensions={0}, use_global_device_ids=true | all-gather | bytes 196608 | tf_op jit(solution)/shard_map/all_gather | solution.py:221
  151.8 6.7 %all-gather.20 = bf16[8,16,512]{2,1,0:T(8,128)(2,1)S(1)} all-gather(bf16[4,16,512]{2,1,0:T(8,128)(2,1)S(1)} %get-tuple-element.32), channel_id=22, replica_groups={{0,12},{2,14},{4,8},{6,10},{1,13},{3,15},{5,9},{7,11},{16,28},{18,30},{..., dimensions={0}, use_global_device_ids=true | all-gather | bytes 196608 | tf_op jit(solution)/shard_map/all_gather | solution.py:221
  159.2 5.1 %space.4 = bf16[4,8,16,512]{3,2,1,0:T(8,128)(2,1)S(1)} custom-call(bf16[4,10,16,512]{3,2,1,0:T(8,128)(2,1)S(1)} %get-tuple-element.71.left, bf16[4,10,16,512]{3,2,1,0:T(8,128)(2,1)S(1)} %pad_maximum_fusion.2.middle, bf16[4,10,16,512]{3,2,1,0:T(8,128)(2,1)S(1)} %get-tuple-element.72.right, bf16[4608,512]{1,0:T(8,128)(2,1)} %bitcast.112, f32[1,512]{1,0:T(1,128)S(1)} %bitcast.122), custom_call_target="tpu_custom_call" | custom-call | flops 2415919104 | bytes 6684672 | tf_op jit(solution)/shard_map/space/pallas_call | solution.py:106
  164.3 7.5 %all-gather.10 = bf16[8,1,32,512]{3,2,1,0:T(8,128)(2,1)S(1)} all-gather(bf16[4,1,32,512]{3,2,1,0:T(8,128)(2,1)S(1)} %get-tuple-element.43), channel_id=12, replica_groups={{0,12},{2,14},{4,8},{6,10},{1,13},{3,15},{5,9},{7,11},{16,28},{18,30},{..., dimensions={0}, use_global_device_ids=true | all-gather | bytes 393216 | tf_op jit(solution)/shard_map/all_gather | solution.py:221
  171.9 7.2 %all-gather.9 = bf16[8,1,32,512]{3,2,1,0:T(8,128)(2,1)S(1)} all-gather(bf16[4,1,32,512]{3,2,1,0:T(8,128)(2,1)S(1)} %get-tuple-element.44), channel_id=11, replica_groups={{0,8},{2,10},{4,12},{6,14},{1,9},{3,11},{5,13},{7,15},{16,24},{18,26},{..., dimensions={0}, use_global_device_ids=true | all-gather | bytes 393216 | tf_op jit(solution)/shard_map/all_gather | solution.py:221
  179.1 6.1 %all-gather.8 = bf16[8,1,32,512]{3,2,1,0:T(8,128)(2,1)S(1)} all-gather(bf16[4,1,32,512]{3,2,1,0:T(8,128)(2,1)S(1)} %get-tuple-element.45), channel_id=10, replica_groups={{0,4},{2,6},{8,12},{10,14},{1,5},{3,7},{9,13},{11,15},{16,20},{18,22},{..., dimensions={0}, use_global_device_ids=true | all-gather | bytes 393216 | tf_op jit(solution)/shard_map/all_gather | solution.py:221
  185.2 2.7 %attend.4 = (bf16[4,32,512]{2,1,0:T(8,128)(2,1)S(1)}, bf16[4,32,512]{2,1,0:T(8,128)(2,1)S(1)}, bf16[4,32,512]{2,1,0:T(8,128)(2,1)S(1)}, bf16[4,32,512]{2,1,0:T(8,128)(2,1)S(1)}) custom-call(s32[4]{0:T(128)S(1)} %pad_add_fusion.first, bf16[4,32,512]{2,1,0:T(8,128)(2,1)S(1)} %get-tuple-element.46.refs_0_, ...), custom_call_target="tpu_custom_call" | custom-call | flops 1342177280 | bytes 2621440 | tf_op jit(solution)/shard_map/attend/pallas_call | solution.py:182
  187.9 5.6 %all-gather.11 = bf16[8,32,512]{2,1,0:T(8,128)(2,1)S(1)} all-gather(bf16[4,32,512]{2,1,0:T(8,128)(2,1)S(1)} %get-tuple-element.25), channel_id=13, replica_groups={{0,4},{2,6},{8,12},{10,14},{1,5},{3,7},{9,13},{11,15},{16,20},{18,22},{..., dimensions={0}, use_global_device_ids=true | all-gather | bytes 393216 | tf_op jit(solution)/shard_map/all_gather | solution.py:221
  193.5 7.9 %all-gather.12 = bf16[8,32,512]{2,1,0:T(8,128)(2,1)S(1)} all-gather(bf16[4,32,512]{2,1,0:T(8,128)(2,1)S(1)} %get-tuple-element.26), channel_id=14, replica_groups={{0,8},{2,10},{4,12},{6,14},{1,9},{3,11},{5,13},{7,15},{16,24},{18,26},{..., dimensions={0}, use_global_device_ids=true | all-gather | bytes 393216 | tf_op jit(solution)/shard_map/all_gather | solution.py:221
  201.5 7.4 %all-gather.13 = bf16[8,32,512]{2,1,0:T(8,128)(2,1)S(1)} all-gather(bf16[4,32,512]{2,1,0:T(8,128)(2,1)S(1)} %get-tuple-element.27), channel_id=15, replica_groups={{0,12},{2,14},{4,8},{6,10},{1,13},{3,15},{5,9},{7,11},{16,28},{18,30},{..., dimensions={0}, use_global_device_ids=true | all-gather | bytes 393216 | tf_op jit(solution)/shard_map/all_gather | solution.py:221
  209.1 7.0 %all_gather.167 = bf16[2,2,128,512]{3,2,1,0:T(8,128)(2,1)S(1)} all-gather(bf16[1,2,128,512]{3,2,1,0:T(8,128)(2,1)S(1)} %bitcast.140), channel_id=1, replica_groups={{0,2},{4,6},{8,10},{12,14},{1,3},{5,7},{9,11},{13,15},{16,18},{20,22},{..., dimensions={0}, use_global_device_ids=true | all-gather | bytes 786432 | tf_op jit(solution)/shard_map/all_gather | solution.py:221
  216.1 5.6 %all_gather.182 = bf16[2,2,64,512]{3,2,1,0:T(8,128)(2,1)S(1)} all-gather(bf16[1,2,64,512]{3,2,1,0:T(8,128)(2,1)S(1)} %bitcast.148), channel_id=1, replica_groups={{0,2},{4,6},{8,10},{12,14},{1,3},{5,7},{9,11},{13,15},{16,18},{20,22},{..., dimensions={0}, use_global_device_ids=true | all-gather | bytes 393216 | tf_op jit(solution)/shard_map/all_gather | solution.py:221
  (142 shorter events, 31.1 us)
Async XLA Ops:
  6.5 3.2 %copy-start.14 = (bf16[4,32,16,512]{3,2,1,0:T(8,128)(2,1)S(1)}, bf16[4,32,16,512]{3,2,1,0:T(8,128)(2,1)}, u32[]{:S(2)}) copy-start(bf16[4,32,16,512]{3,2,1,0:T(8,128)(2,1)} %param.12) | copy-start | bytes 6291460
  6.5 83.5 %all-gather.23.cloned.1.call-start = ((), (), s32[]{:S(2)}) async-start(), calls=%async_computation | async-start | bytes 1572864 | tf_op jit(solution)/shard_map/all_gather | solution.py:221
  24.6 0.9 copy-start.16
  25.4 9.4 %collective-permute-start = (bf16[3,6,16,512]{3,2,1,0:T(8,128)(2,1)}, bf16[3,6,16,512]{3,2,1,0:T(8,128)(2,1)}, u32[]{:S(2)}, u32[]{:S(2)}) collective-permute-start(bf16[3,6,16,512]{3,2,1,0:T(8,128)(2,1)} %slice.150), channel_id=1, source_target_pairs={{0,4},{2,6},{4,8},{6,10},{8,12},{10,14},{1,5},{3,7},{5,9},{7,11},{... | collective-permute-start | bytes 884744 | tf_op jit(solution)/shard_map/ppermute | solution.py:265
  29.9 6.3 %copy-start.2 = (bf16[3,512,512]{2,1,0:T(8,128)(2,1)S(1)}, bf16[3,512,512]{2,1,0:T(8,128)(2,1)}, u32[]{:S(2)}) copy-start(bf16[3,512,512]{2,1,0:T(8,128)(2,1)} %param.15) | copy-start | bytes 4718596
  31.3 4.9 %copy-start.1 = (bf16[3,512,512]{2,1,0:T(8,128)(2,1)S(1)}, bf16[3,512,512]{2,1,0:T(8,128)(2,1)}, u32[]{:S(2)}) copy-start(bf16[3,512,512]{2,1,0:T(8,128)(2,1)} %param.13) | copy-start | bytes 4718596
  31.3 4.9 %copy-start.11 = (f32[512]{0:T(512)S(1)}, f32[512]{0:T(512)}, u32[]{:S(2)}) copy-start(f32[512]{0:T(512)} %param.14) | copy-start | bytes 6148
  31.3 4.9 %copy-start.12 = (f32[512]{0:T(512)S(1)}, f32[512]{0:T(512)}, u32[]{:S(2)}) copy-start(f32[512]{0:T(512)} %param.16) | copy-start | bytes 6148
  36.2 5.2 %slice-start = ((s8[4718592]{0:T(1024)(128)(4,1)}), s8[4194304]{0:T(1024)(128)(4,1)S(1)}, s32[]{:S(2)}) async-start(s8[4718592]{0:T(1024)(128)(4,1)} %bitcast.113), calls=%async_computation.1 | async-start | bytes 8388608
  36.2 5.1 %slice-start.1 = ((s8[4718592]{0:T(1024)(128)(4,1)}), s8[524288]{0:T(1024)(128)(4,1)S(1)}, s32[]{:S(2)}) async-start(s8[4718592]{0:T(1024)(128)(4,1)} %bitcast.113), calls=%async_computation.2 | async-start | bytes 1048576
  39.3 1.3 collective-permute-start.1
  39.5 1.8 copy-start
  40.7 0.6 copy-start.19
  41.3 20.2 %copy-start.7 = (bf16[512,512]{1,0:T(8,128)(2,1)S(1)}, bf16[512,512]{1,0:T(8,128)(2,1)}, u32[]{:S(2)}) copy-start(bf16[512,512]{1,0:T(8,128)(2,1)} %refs_7_.5) | copy-start | bytes 1572868
  41.3 20.2 %copy-start.9 = (bf16[512,512]{1,0:T(8,128)(2,1)S(1)}, bf16[512,512]{1,0:T(8,128)(2,1)}, u32[]{:S(2)}) copy-start(bf16[512,512]{1,0:T(8,128)(2,1)} %refs_8_.5) | copy-start | bytes 1572868
  42.8 18.7 %copy-start.3 = (bf16[512,512]{1,0:T(8,128)(2,1)S(1)}, bf16[512,512]{1,0:T(8,128)(2,1)}, u32[]{:S(2)}) copy-start(bf16[512,512]{1,0:T(8,128)(2,1)} %refs_5_.5) | copy-start | bytes 1572868
  42.8 18.7 %copy-start.5 = (bf16[512,512]{1,0:T(8,128)(2,1)S(1)}, bf16[512,512]{1,0:T(8,128)(2,1)}, u32[]{:S(2)}) copy-start(bf16[512,512]{1,0:T(8,128)(2,1)} %refs_6_.5) | copy-start | bytes 1572868
  42.8 18.7 %copy-start.13 = (f32[512]{0:T(512)S(1)}, f32[512]{0:T(512)}, u32[]{:S(2)}) copy-start(f32[512]{0:T(512)} %param.19) | copy-start | bytes 6148
  90.1 1.6 copy-start.17
  90.1 8.7 %copy-start.15 = (bf16[4,32,16,512]{3,2,1,0:T(8,128)(2,1)S(1)}, bf16[4,32,16,512]{3,2,1,0:T(8,128)(2,1)}, u32[]{:S(2)}) copy-start(bf16[4,32,16,512]{3,2,1,0:T(8,128)(2,1)} %param.12) | copy-start | bytes 6291460
  98.8 4.5 %collective-permute-start.4 = (bf16[3,4,16,512]{3,2,1,0:T(8,128)(2,1)S(1)}, bf16[3,4,16,512]{3,2,1,0:T(8,128)(2,1)S(1)}, u32[]{:S(2)}, u32[]{:S(2)}) collective-permute-start(bf16[3,4,16,512]{3,2,1,0:T(8,128)(2,1)S(1)} %slice.170), channel_id=1, source_target_pairs={{0,4},{2,6},{4,8},{6,10},{8,12},{10,14},{1,5},{3,7},{5,9},{7,11},{... | collective-permute-start | bytes 589832 | tf_op jit(solution)/shard_map/ppermute | solution.py:265
  100.3 7.6 %collective-permute-start.2 = (bf16[3,8,16,512]{3,2,1,0:T(8,128)(2,1)S(1)}, bf16[3,8,16,512]{3,2,1,0:T(8,128)(2,1)S(1)}, u32[]{:S(2)}, u32[]{:S(2)}) collective-permute-start(bf16[3,8,16,512]{3,2,1,0:T(8,128)(2,1)S(1)} %slice.158), channel_id=1, source_target_pairs={{0,4},{2,6},{4,8},{6,10},{8,12},{10,14},{1,5},{3,7},{5,9},{7,11},{... | collective-permute-start | bytes 1179656 | tf_op jit(solution)/shard_map/ppermute | solution.py:265
  103.4 2.5 %copy-start.18 = (bf16[2,2,64,512]{3,2,1,0:T(8,128)(2,1)S(1)}, bf16[2,2,64,512]{3,2,1,0:T(8,128)(2,1)}, u32[]{:S(2)}) copy-start(bf16[2,2,64,512]{3,2,1,0:T(8,128)(2,1)} %all_gather.152) | copy-start | bytes 786436
  105.7 1.5 collective-permute-start.5
  107.8 6.4 %slice-start.2 = ((s8[4718592]{0:T(1024)(128)(4,1)}), s8[4194304]{0:T(1024)(128)(4,1)S(1)}, s32[]{:S(2)}) async-start(s8[4718592]{0:T(1024)(128)(4,1)} %bitcast.116), calls=%async_computation.3 | async-start | bytes 8388608
  108.0 6.2 %slice-start.3 = ((s8[4718592]{0:T(1024)(128)(4,1)}), s8[524288]{0:T(1024)(128)(4,1)S(1)}, s32[]{:S(2)}) async-start(s8[4718592]{0:T(1024)(128)(4,1)} %bitcast.116), calls=%async_computation.4 | async-start | bytes 1048576
  112.4 1.3 collective-permute-start.3
  114.2 23.1 %copy-start.8 = (bf16[512,512]{1,0:T(8,128)(2,1)S(1)}, bf16[512,512]{1,0:T(8,128)(2,1)}, u32[]{:S(2)}) copy-start(bf16[512,512]{1,0:T(8,128)(2,1)} %refs_7_.5) | copy-start | bytes 1572868
  114.2 23.1 %copy-start.10 = (bf16[512,512]{1,0:T(8,128)(2,1)S(1)}, bf16[512,512]{1,0:T(8,128)(2,1)}, u32[]{:S(2)}) copy-start(bf16[512,512]{1,0:T(8,128)(2,1)} %refs_8_.5) | copy-start | bytes 1572868
  115.7 21.6 %copy-start.4 = (bf16[512,512]{1,0:T(8,128)(2,1)S(1)}, bf16[512,512]{1,0:T(8,128)(2,1)}, u32[]{:S(2)}) copy-start(bf16[512,512]{1,0:T(8,128)(2,1)} %refs_5_.5) | copy-start | bytes 1572868
  115.7 21.6 %copy-start.6 = (bf16[512,512]{1,0:T(8,128)(2,1)S(1)}, bf16[512,512]{1,0:T(8,128)(2,1)}, u32[]{:S(2)}) copy-start(bf16[512,512]{1,0:T(8,128)(2,1)} %refs_6_.5) | copy-start | bytes 1572868
Sparse Core Ops, SparseCore 0:
  23.6 22.7 all-gather.22

commit v6 on v3

--- a/solution.py
+++ b/solution.py
@@ -11,7 +11,7 @@
 parts = 2
 taps = 3
 most_direct = 8
-vmem_bytes = 48 * 1024 * 1024
+mebibyte = 1024 * 1024
 
 VMEM = pl.BlockSpec(memory_space=pltpu.VMEM)
 SMEM = pl.BlockSpec(memory_space=pltpu.SMEM)
@@ -31,8 +31,8 @@
     return pl.CostEstimate(flops=flops, bytes_accessed=size, transcendentals=0)
 
 
-def params():
-    return pltpu.CompilerParams(vmem_limit_bytes=vmem_bytes)
+def params(mebibytes):
+    return pltpu.CompilerParams(vmem_limit_bytes=mebibytes * mebibyte)
 
 
 def pick_kernel(first, begin, video, out, sem):
@@ -49,14 +49,14 @@
         partial(pick_kernel, first, begin),
         out_shape=jax.ShapeDtypeStruct(shape, video.dtype),
         in_specs=[ANY],
-        out_specs=ANY,
+        out_specs=VMEM,
         scratch_shapes=[pltpu.SemaphoreType.DMA],
-        compiler_params=params(),
+        compiler_params=params(56),
         name="pick",
     )(video)
 
 
-def early_kernel(begin, video, w_time, b_time, w_down, b_down, own, part, rows_in, lifted, sem):
+def early_kernel(begin, video, edge, w_time, b_time, w_down, b_down, own, part, rows_in, lifted, sem):
     frames, rows, width, channels = rows_in.shape
     pixels = rows * width
     copy = pltpu.make_async_copy(video.at[:, begin : begin + rows], rows_in, sem)
@@ -64,7 +64,7 @@
     copy.wait()
 
     def frame(t):
-        return rows_in[t].reshape(pixels, channels)
+        return jnp.concatenate([rows_in[t].reshape(pixels, channels), edge[t]], axis=0)
 
     for t in range(taps - 1, frames):
         lhs = jnp.concatenate([frame(t - k) for k in range(taps)], axis=1)
@@ -74,115 +74,149 @@
         known = [k for k in range(taps) if 2 * s + 1 - k >= taps - 1]
         lhs = jnp.concatenate([lifted[2 * s + 1 - k] for k in known], axis=1)
         part[s - 1] = dot32(lhs, w_down[: len(known) * channels]) + b_down[...]
-    own[...] = rows_in[: taps - 1]
-
-
-def early(video, begin, end, w_time, b_time, w_down, b_down):
+    for t in range(taps - 1):
+        own[t] = frame(t)
+
+
+def early(video, edge, begin, end, w_time, b_time, w_down, b_down):
     frames, _, width, channels = video.shape
     rows = end - begin
-    pixels = rows * width
+    pixels = rows * width + edge.shape[1]
     flops = 2 * channels * channels * pixels * (taps * (frames - 2) + 2)
     return pl.pallas_call(
         partial(early_kernel, begin),
         out_shape=[
-            jax.ShapeDtypeStruct((taps - 1, rows, width, channels), jnp.bfloat16),
+            jax.ShapeDtypeStruct((taps - 1, pixels, channels), jnp.bfloat16),
             jax.ShapeDtypeStruct((frames // 2 - 1, pixels, channels), jnp.float32),
         ],
-        in_specs=[ANY] + [VMEM] * 4,
+        in_specs=[ANY] + [VMEM] * 5,
         out_specs=[VMEM] * 2,
         scratch_shapes=[
             pltpu.VMEM((frames, rows, width, channels), jnp.bfloat16),
             pltpu.VMEM((frames, pixels, channels), jnp.bfloat16),
             pltpu.SemaphoreType.DMA,
         ],
-        compiler_params=params(),
+        compiler_params=params(24),
         cost_estimate=cost(flops, w_time, w_down),
         name="early",
-    )(video, w_time, b_time, w_down, b_down)
-
-
-def lift_kernel(started, halo, own, part, w_time, b_time, w_down, b_down, out, lifted):
-    halves, rows, width, channels = out.shape
+    )(video, edge, w_time, b_time, w_down, b_down)
+
+
+def conv_kernel(
+    owners, size, fresh, last, scalars, halo, halo_edge, own, part, w_time, b_time, w_down, b_down,
+    w_space, b_space, *refs
+):
+    refs = list(refs)
+    kept = None if fresh else refs.pop(0)
+    lifted, buffers, result, weights, sem = refs[-5:]
+    outs = refs[:owners]
+    keeps = None if last else refs[owners]
+    _, rows, width, channels = halo.shape
+    halves = result.shape[0]
     pixels = rows * width
+    edges = halo_edge.shape[1]
+    fetch = pltpu.make_async_copy(w_space, weights, sem)
+    fetch.start()
+    column = scalars[1]
 
     def frame(t):
-        ref, index = (halo, t + taps) if t < 0 else (own, t)
-        return ref[index].reshape(pixels, channels)
+        if t >= 0:
+            return own[t]
+        return jnp.concatenate([halo[t + taps].reshape(pixels, channels), halo_edge[t + taps]], 0)
 
     for t in range(-1, taps - 1):
         lhs = jnp.concatenate([frame(t - k) for k in range(taps)], axis=1)
         acc = dot32(lhs, w_time[...]) + b_time[...]
-        result = frame(t).astype(jnp.float32) + silu(acc)
+        value = frame(t).astype(jnp.float32) + silu(acc)
         if t < 0:
-            result = jnp.where(started[0] > 0, result, 0.0)
-        lifted[t + 1] = result.astype(jnp.bfloat16)
+            value = jnp.where(scalars[0] > 0, value, 0.0)
+        lifted[t + 1] = value.astype(jnp.bfloat16)
+
+    top = 1 if fresh else 2
+    row_of = lax.broadcasted_iota(jnp.int32, (pixels, edges), 0) // width
+    spread = (row_of == lax.broadcasted_iota(jnp.int32, (pixels, edges), 1)).astype(jnp.bfloat16)
+    across = lax.broadcasted_iota(jnp.int32, (pixels, channels), 0) % width
     for s in range(halves):
         late = [k for k in range(taps) if 2 * s + 1 - k < taps - 1]
         acc = b_down[...] if s == 0 else part[s - 1]
         if late:
             lhs = jnp.concatenate([lifted[2 * s + 2 - k] for k in late], axis=1)
             acc = dot32(lhs, w_down[late[0] * channels : (late[-1] + 1) * channels]) + acc
-        out[s] = acc.astype(jnp.bfloat16).reshape(rows, width, channels)
-
-
-def lift(started, halo, own, part, w_time, b_time, w_down, b_down):
-    rows, width, channels = own.shape[1:]
-    halves = part.shape[0] + 1
-    pixels = rows * width
-    flops = 2 * channels * channels * pixels * (taps * taps + 4)
-    return pl.pallas_call(
-        lift_kernel,
-        out_shape=jax.ShapeDtypeStruct((halves, rows, width, channels), jnp.bfloat16),
-        in_specs=[SMEM] + [VMEM] * 7,
-        out_specs=VMEM,
-        scratch_shapes=[pltpu.VMEM((taps, pixels, channels), jnp.bfloat16)],
-        compiler_params=params(),
-        cost_estimate=cost(flops, halo, own, part, w_time, w_down),
-        name="lift",
-    )(started, halo, own, part, w_time, b_time, w_down, b_down)
-
-
-def space_kernel(owners, order, left, middle, right, weights, bias, *refs):
-    outs, result = refs[:-1], refs[-1]
-    halves, pixels, channels = result.shape
-    rows = middle.shape[1] - 2
-    sources = (left, middle, right)
+        reduced = acc.astype(jnp.bfloat16)
+        wide = reduced[:pixels].astype(jnp.float32)
+        beside = dot32(spread, reduced[pixels:])
+        before = jnp.where(column == 1, beside, 0.0)
+        behind = jnp.where(column == 0, beside, 0.0)
+        shifted = (
+            jnp.where(across == 0, before, pltpu.roll(wide, 1, 0)),
+            wide,
+            jnp.where(across == width - 1, behind, pltpu.roll(wide, pixels - 1, 0)),
+        )
+        for b in range(3):
+            value = shifted[b].astype(jnp.bfloat16).reshape(rows, width, channels)
+            buffers[b, s, top : top + rows] = value
+    blank = jnp.zeros((3, halves, 1, width, channels), jnp.bfloat16)
+    if fresh:
+        buffers[:, :, :1] = blank
+    else:
+        buffers[:, :, :2] = kept[...]
+    if last:
+        buffers[:, :, size + 1 :] = blank
+    else:
+        keeps[...] = buffers[:, :, size:]
+    fetch.wait()
 
     @pl.loop(0, halves)
     def _(s):
-        def window(source, a):
-            return source[s, a : a + rows].reshape(pixels, channels)
-
-        lhs = jnp.concatenate([window(v, a) for a in range(3) for v in sources], axis=1)
-        acc = dot32(lhs, weights[...]) + bias[...]
-        value = window(middle, 1).astype(jnp.float32) + silu(acc)
+        def window(b, a):
+            return buffers[b, s, a : a + size].reshape(size * width, channels)
+
+        lhs = jnp.concatenate([window(b, a) for a in range(3) for b in range(3)], axis=1)
+        acc = dot32(lhs, weights[...]) + b_space[...]
+        value = window(1, 1).astype(jnp.float32) + silu(acc)
         result[s] = value.astype(jnp.bfloat16)
 
+    each = size * width // owners
     if owners == 1:
         outs[0][...] = result[...]
     else:
-        each = pixels // owners
         for j, out in enumerate(outs):
-            begin = pl.multiple_of(order[j] * each, each)
+            begin = pl.multiple_of(scalars[2 + j] * each, each)
             out[...] = result[:, pl.ds(begin, each)]
 
 
-def space(order, left, middle, right, weights, bias):
-    halves, rows, width, channels = middle.shape
-    owners = order.shape[0]
-    pixels = (rows - 2) * width
-    flops = 2 * 9 * channels * channels * halves * pixels
-    block = jax.ShapeDtypeStruct((halves, pixels // owners, channels), jnp.bfloat16)
+def conv(
+    owners, size, kept, last, scalars, halo, halo_edge, own, part, w_time, b_time, w_down, b_down,
+    w_space, b_space
+):
+    _, rows, width, channels = halo.shape
+    halves = part.shape[0] + 1
+    pixels = own.shape[1]
+    fresh = kept is None
+    flops = 2 * channels * channels * (pixels * (taps * taps + 4) + 9 * halves * size * width)
+    shapes = [(halves, size * width // owners, channels)] * owners
+    if not last:
+        shapes.append((3, halves, 2, width, channels))
+    given = [] if fresh else [kept]
     return pl.pallas_call(
-        partial(space_kernel, owners),
-        out_shape=[block] * owners,
-        in_specs=[SMEM] + [VMEM] * 5,
-        out_specs=[VMEM] * owners,
-        scratch_shapes=[pltpu.VMEM((halves, pixels, channels), jnp.bfloat16)],
-        compiler_params=params(),
-        cost_estimate=cost(flops, left, middle, right, weights),
-        name="space",
-    )(order, left, middle, right, weights, bias)
+        partial(conv_kernel, owners, size, fresh, last),
+        out_shape=[jax.ShapeDtypeStruct(shape, jnp.bfloat16) for shape in shapes],
+        in_specs=[SMEM] + [VMEM] * 8 + [ANY] + [VMEM] * (1 + len(given)),
+        out_specs=[VMEM] * len(shapes),
+        scratch_shapes=[
+            pltpu.VMEM((taps, pixels, channels), jnp.bfloat16),
+            pltpu.VMEM((3, halves, size + 2, width, channels), jnp.bfloat16),
+            pltpu.VMEM((halves, size * width, channels), jnp.bfloat16),
+            pltpu.VMEM(w_space.shape, jnp.bfloat16),
+            pltpu.SemaphoreType.DMA,
+        ],
+        compiler_params=params(36),
+        cost_estimate=cost(flops, halo, own, part, w_time, w_down, w_space),
+        name="conv",
+    )(
+        scalars, halo, halo_edge, own, part, w_time, b_time, w_down, b_down, w_space, b_space,
+        *given
+    )
 
 
 def attend_kernel(frames_per, lanes, count, first, *refs):
@@ -249,13 +283,14 @@
         blocks = [b.reshape(frames_per * pixels, channels) for b in blocks]
     count = len(blocks)
     rows = frames_per * pixels * count
+    size = frames_per * count * lanes
     flops = 2 * rows * channels * (4 * channels + 2 * frames_per * count * lanes)
     outs = pl.pallas_call(
         partial(attend_kernel, frames_per, lanes, count),
         out_shape=[jax.ShapeDtypeStruct(b.shape, jnp.bfloat16) for b in blocks],
         in_specs=[SMEM] + [VMEM] * (count + 5),
         out_specs=[VMEM] * count,
-        compiler_params=params(),
+        compiler_params=params(20 if 16 * size * size < 20 * mebibyte else 56),
         cost_estimate=cost(flops, *blocks, w_query, w_key, w_value, w_out),
         name="attend",
     )(first, *blocks, gain, w_query, w_key, w_value, w_out)
@@ -287,7 +322,7 @@
         out_specs=ANY,
         input_output_aliases={count + 1: 0} if given else {},
         scratch_shapes=[pltpu.SemaphoreType.DMA((count,))],
-        compiler_params=params(),
+        compiler_params=params(16),
         name="collect",
     )(order, *blocks, *given)
 
@@ -302,29 +337,22 @@
     frames, height, width, channels = video.shape
     devices = lax.axis_size("tm")
     columns = lax.axis_size("cols")
+    assert columns == 2
     place = lax.axis_index("tm").astype(jnp.int32)
-    column = lax.axis_index("cols")
+    column = lax.axis_index("cols").astype(jnp.int32)
     halves = frames // 2
-    started = place.reshape(1)
     w_time = w_time.reshape(-1, channels)
     w_down = w_down.reshape(-1, channels)
     w_space = w_space.reshape(-1, channels)
     b_time, b_down, b_space, gain = (v.reshape(1, -1) for v in (b_time, b_down, b_space, gain))
-    onward = [(i, i + 1) for i in range(devices - 1)]
     chunks = parts if height % parts == 0 and height // parts * width % devices == 0 else 1
     size = height // chunks
     each = size * width // devices
     direct = devices <= most_direct and devices & (devices - 1) == 0 and each % 16 == 0
     issue = sorted(range(1, devices), key=lambda j: -j)
     order = place ^ jnp.arange(devices, dtype=jnp.int32) if direct else jnp.zeros(1, jnp.int32)
-
-    def beside(value):
-        last, head = value[:, :, -1:], value[:, :, :1]
-        if columns == 2:
-            other = lax.ppermute(jnp.where(column == 0, last, head), "cols", [(0, 1), (1, 0)])
-            return jnp.where(column == 1, other, 0), jnp.where(column == 0, other, 0)
-        up = [(i, i + 1) for i in range(columns - 1)]
-        return lax.ppermute(last, "cols", up), lax.ppermute(head, "cols", [(j, i) for i, j in up])
+    scalars = jnp.concatenate([jnp.stack([place, column]), order])
+    owners = order.shape[0]
 
     def exchange(blocks):
         result = list(blocks)
@@ -335,34 +363,38 @@
     spans = [
         (k * size + (1 if k else 0), min((k + 1) * size + 1, height)) for k in range(chunks)
     ]
-    halos, owns, sums = [], [], []
-    for begin, end in spans:
-        sent = pick(video, frames - taps, begin, end)
-        if sums:
-            sent = after(sent, sums[-1])
-        halos.append(lax.ppermute(sent, "tm", onward))
-        own, part = early(video, begin, end, w_time, b_time, w_down, b_down)
-        owns.append(own)
-        sums.append(part)
-
+    onward = [(i, i + 1) for i in range(devices - 1)]
+    aslant = [
+        (i * columns + c, (i + 1) * columns + 1 - c)
+        for i in range(devices - 1)
+        for c in range(columns)
+    ]
+    sent = [pick(video, frames - taps, begin, end) for begin, end in spans]
+    border = jnp.where(column == 0, video[:, :, -1], video[:, :, 0])
+    border = after(border, sent[0])
+    halos = [lax.ppermute(value, "tm", onward) for value in sent]
+    own_edge = lax.ppermute(border, "cols", [(0, 1), (1, 0)])
+    halo_edge = lax.ppermute(border[frames - taps :], ("tm", "cols"), aslant)
+
+    def edge_rows(edge, begin, end):
+        return jnp.pad(edge[:, begin:end], ((0, 0), (0, -(end - begin) % 16), (0, 0)))
+
+    ahead = [
+        early(video, edge_rows(own_edge, begin, end), begin, end, w_time, b_time, w_down, b_down)
+        for begin, end in spans
+    ]
     spatials, kept = [], None
-    for index in range(chunks):
-        halo, own, part = halos[index], owns[index], sums[index]
+    for index, (begin, end) in enumerate(spans):
+        own, part = ahead[index]
         if spatials:
             own = after(own, spatials[-1][0])
-        reduced = lift(started, halo, own, part, w_time, b_time, w_down, b_down)
-        left, right = beside(reduced)
-        pieces = (left, reduced, right)
-        if kept is None:
-            kept = tuple(jnp.zeros_like(p[:, :1]) for p in pieces)
-        pieces = tuple(jnp.concatenate(pq, axis=1) for pq in zip(kept, pieces))
-        if index == chunks - 1:
-            pieces = tuple(jnp.pad(p, ((0, 0), (0, 1), (0, 0), (0, 0))) for p in pieces)
-        kept = tuple(p[:, -2:] for p in pieces)
-        left, middle, right = pieces
-        to_right = jnp.concatenate([left, middle[:, :, :-1]], axis=2)
-        to_left = jnp.concatenate([middle[:, :, 1:], right], axis=2)
-        spatials.append(space(order, to_right, middle, to_left, w_space, b_space))
+        last = index == chunks - 1
+        made = conv(
+            owners, size, kept, last, scalars, halos[index], edge_rows(halo_edge, begin, end), own,
+            part, w_time, b_time, w_down, b_down, w_space, b_space
+        )
+        spatials.append(made[:owners])
+        kept = None if last else made[owners]
 
     newest = spatials[-1][0]
     if direct:

time: 112 us -> 111 us (level)
  local copies, waits for them, and re-layouts: 4.27 us -> 8.28 us
  waiting for transfers between devices: 17.4 us -> 13.9 us
  Pallas kernels: 33.2 us -> 29.9 us
  starting transfers between devices: 54.2 us -> 57.3 us
    pallas_call x4 -> x2, Pallas kernels: 17.7 us -> 14.3 us  [conv(): pl.pallas_call(partial(conv_kernel, owners, size, fresh, last), out_shape...]
    ppermute x4, starting transfers between devices: 9.45 us -> 12.7 us  [the longest x2 9.25 us: per_device(): halos = [lax.ppermute(value, 'tm', onward) for value in sent]]
    ppermute x4, waiting for transfers between devices: 10.9 us -> 7.76 us  [the longest x1 7.75 us: per_device(): halo_edge = lax.ppermute(border[frames - taps:], ('tm', 'cols'), aslant)]
    slice x6 -> x4, local copies, waits for them, and re-layouts: 0.51 us -> 2.89 us  [the longest x1 1.95 us: per_device(): border = jnp.where(column == 0, video[:, :, -1], video[:, :, 0])]
    pallas_call x2, Pallas kernels: 1.77 us -> 4.05 us  [pick(): pl.pallas_call(partial(pick_kernel, first, begin), out_shape=jax.ShapeDty...]
    pallas_call x2, Pallas kernels: 5.61 us -> 3.43 us  [early(): pl.pallas_call(partial(early_kernel, begin), out_shape=[jax.ShapeDtypeStr...]
    unnamed x32 -> x34, local copies, waits for them, and re-layouts: 3.72 us -> 5.37 us
  transfers between devices with their start and end apart: 32 -> 32, of which waited for: 9 -> 6; matrix products, arithmetic and copies ran while one was open for 2% -> 3% of each run, Pallas kernels for 25% -> 24%
where the time goes in v6:
time: 111 us
  starting transfers between devices  57.3 us (52%)
  Pallas kernels  29.9 us (27%)
  waiting for transfers between devices  13.9 us (13%)
  local copies, waits for them, and re-layouts  8.28 us (7%)
    ppermute x28, starting transfers between devices, exchange(): lax.ppermute(blocks[j], 'tm', [(i, i ^ j) for i in range(devices)])  44.6 us
    pallas_call x2, Pallas kernels, conv(): pl.pallas_call(partial(conv_kernel, owners, size, fresh, last), out_shape...  14.3 us
    ppermute x2, starting transfers between devices, per_device(): halos = [lax.ppermute(value, 'tm', onward) for value in sent]  9.25 us
    ppermute x1, waiting for transfers between devices, per_device(): halo_edge = lax.ppermute(border[frames - taps:], ('tm', 'cols'), aslant)  7.75 us
    ppermute x28, waiting for transfers between devices, exchange(): lax.ppermute(blocks[j], 'tm', [(i, i ^ j) for i in range(devices)])  6.18 us
    unnamed x34, local copies, waits for them, and re-layouts  5.37 us
    pallas_call x2, Pallas kernels, attend(): pl.pallas_call(partial(attend_kernel, frames_per, lanes, count), out_shap...  5.32 us
    pallas_call x2, Pallas kernels, pick(): pl.pallas_call(partial(pick_kernel, first, begin), out_shape=jax.ShapeDty...  4.05 us
  transfers between devices with their start and end apart: 32, of which 6 were waited for; matrix products, arithmetic and copies ran while one was open for 3% of the time, Pallas kernels for 24%

profile of v6, /device:TPU:0, one launch (start us, length us, event | category | flops | bytes accessed | tf_op | source)
XLA Modules:
  0.0 110.8 jit_solution(14927831935242404688)
XLA Ops:
  0.0 2.1 %pick.3 = bf16[3,17,16,512]{3,2,1,0:T(8,128)(2,1)} custom-call(bf16[4,32,16,512]{3,2,1,0:T(8,128)(2,1)} %video.7), custom_call_target="tpu_custom_call" | custom-call | tf_op jit(solution)/shard_map/pick/pallas_call | solution.py:48
  2.1 4.9 %collective-permute-start.3 = (bf16[3,17,16,512]{3,2,1,0:T(8,128)(2,1)}, bf16[3,17,16,512]{3,2,1,0:T(8,128)(2,1)S(1)}, u32[]{:S(2)}, u32[]{:S(2)}) collective-permute-start(bf16[3,17,16,512]{3,2,1,0:T(8,128)(2,1)} %pick.3), channel_id=1, source_target_pairs={{0,2},{2,4},{4,6},{6,8},{8,10},{10,12},{12,14},{1,3},{3,5},{5,7},{... | collective-permute-start | bytes 2506760 | tf_op jit(solution)/shard_map/ppermute | solution.py:375
  7.0 2.0 %fusion.1 = (bf16[4,32,1,512]{3,2,1,0:T(2,128)(2,1)S(1)}, bf16[4,32,1,512]{3,2,1,0:T(2,128)(2,1)S(1)}) fusion(bf16[4,32,16,512]{3,2,1,0:T(8,128)(2,1)} %video.7), kind=kLoop, calls=%fused_computation.7 | loop fusion | bytes 524288 | tf_op jit(solution)/shard_map/slice | solution.py:373
  10.6 3.5 %collective-permute-start.1 = (bf16[3,32,512]{2,1,0:T(8,128)(2,1)S(1)}, bf16[3,32,512]{2,1,0:T(8,128)(2,1)S(1)}, u32[]{:S(2)}, u32[]{:S(2)}) collective-permute-start(bf16[3,32,512]{2,1,0:T(8,128)(2,1)S(1)} %slice.21), channel_id=1, source_target_pairs={{0,3},{1,2},{2,5},{3,4},{4,7},{5,6},{6,9},{7,8},{8,11},{9,10},{10,... | collective-permute-start | bytes 294920 | tf_op jit(solution)/shard_map/ppermute | solution.py:377
  14.1 2.0 %pick.2 = bf16[3,15,16,512]{3,2,1,0:T(8,128)(2,1)} custom-call(bf16[4,32,16,512]{3,2,1,0:T(8,128)(2,1)} %video.7), custom_call_target="tpu_custom_call" | custom-call | tf_op jit(solution)/shard_map/pick/pallas_call | solution.py:48
  16.1 4.3 %collective-permute-start = (bf16[3,15,16,512]{3,2,1,0:T(8,128)(2,1)}, bf16[3,15,16,512]{3,2,1,0:T(8,128)(2,1)}, u32[]{:S(2)}, u32[]{:S(2)}) collective-permute-start(bf16[3,15,16,512]{3,2,1,0:T(8,128)(2,1)} %pick.2), channel_id=1, source_target_pairs={{0,2},{2,4},{4,6},{6,8},{8,10},{10,12},{12,14},{1,3},{3,5},{5,7},{... | collective-permute-start | bytes 2211848 | tf_op jit(solution)/shard_map/ppermute | solution.py:375
  20.5 7.7 %collective-permute-done.1 = bf16[3,32,512]{2,1,0:T(8,128)(2,1)S(1)} collective-permute-done((bf16[3,32,512]{2,1,0:T(8,128)(2,1)S(1)}, bf16[3,32,512]{2,1,0:T(8,128)(2,1)S(1)}, u32[]{:S(2)}, u32[]{:S(2)}) %collective-permute-start.1) | collective-permute-done | bytes 98336 | tf_op jit(solution)/shard_map/ppermute | solution.py:377
  28.5 1.4 %copy-done.1 = bf16[3,512,512]{2,1,0:T(8,128)(2,1)S(1)} copy-done((bf16[3,512,512]{2,1,0:T(8,128)(2,1)S(1)}, bf16[3,512,512]{2,1,0:T(8,128)(2,1)}, u32[]{:S(2)}) %copy-start.1) | copy-done | bytes 1572888
  29.9 1.4 %copy-done.3 = bf16[3,512,512]{2,1,0:T(8,128)(2,1)S(1)} copy-done((bf16[3,512,512]{2,1,0:T(8,128)(2,1)S(1)}, bf16[3,512,512]{2,1,0:T(8,128)(2,1)}, u32[]{:S(2)}) %copy-start.3) | copy-done | bytes 1572888
  31.3 1.6 %early.2 = (bf16[2,256,512]{2,1,0:T(8,128)(2,1)S(1)}, f32[1,256,512]{2,1,0:T(8,128)S(1)}) custom-call(bf16[4,32,16,512]{3,2,1,0:T(8,128)(2,1)S(1)} %copy-done, bf16[4,16,512]{2,1,0:T(8,128)(2,1)S(1)} %pad.17.edge, bf16[1536,512]{1,0:T(8,128)(2,1)S(1)} %bitcast.12, f32[1,512]{1,0:T(1,128)S(1)} %bitcast.20, bf16[1536,512]{1,0:T(8,128)(2,1)S(1)} %bitcast.16, ...), custom_call_target="tpu_custom_call" | custom-call | flops 1073741824 | bytes 3145728 | tf_op jit(solution)/shard_map/early/pallas_call | solution.py:86
  33.1 1.8 %early.3 = (bf16[2,304,512]{2,1,0:T(8,128)(2,1)S(1)}, f32[1,304,512]{2,1,0:T(8,128)S(1)}) custom-call(bf16[4,32,16,512]{3,2,1,0:T(8,128)(2,1)S(1)} %copy-done, bf16[4,32,512]{2,1,0:T(8,128)(2,1)S(1)} %broadcast_select_fusion.edge, bf16[1536,512]{1,0:T(8,128)(2,1)S(1)} %bitcast.13, f32[1,512]{1,0:T(1,128)S(1)} %bitcast.21, bf16[1536,512]{1,0:T(8,128)(2,1)S(1)} %bitcast.17, ...), custom_call_target="tpu_custom_call" | custom-call | flops 1275068416 | bytes 3145728 | tf_op jit(solution)/shard_map/early/pallas_call | solution.py:86
  35.0 2.3 %copy-done.7 = bf16[9,512,512]{2,1,0:T(8,128)(2,1)S(1)} copy-done((bf16[9,512,512]{2,1,0:T(8,128)(2,1)S(1)}, bf16[9,512,512]{2,1,0:T(8,128)(2,1)}, u32[]{:S(2)}) %copy-start.7) | copy-done | bytes 4718616
  37.3 6.9 %conv.2 = (bf16[2,32,512]{2,1,0:T(8,128)(2,1)S(1)}, bf16[2,32,512]{2,1,0:T(8,128)(2,1)S(1)}, bf16[2,32,512]{2,1,0:T(8,128)(2,1)S(1)}, bf16[2,32,512]{2,1,0:T(8,1...) custom-call(s32[10]{0:T(128)S(1)} %pad_add_fusion.scalars, ...), custom_call_target="tpu_custom_call" | custom-call | flops 4487905280 | bytes 9945088 | tf_op jit(solution)/shard_map/conv/pallas_call | solution.py:201
  44.2 3.3 %collective-permute-start.10 = (bf16[2,32,512]{2,1,0:T(8,128)(2,1)S(1)}, bf16[2,32,512]{2,1,0:T(8,128)(2,1)S(1)}, u32[]{:S(2)}, u32[]{:S(2)}) collective-permute-start(bf16[2,32,512]{2,1,0:T(8,128)(2,1)S(1)} %get-tuple-element.62), channel_id=1, source_target_pairs={{0,14},{2,12},{4,10},{6,8},{8,6},{10,4},{12,2},{14,0},{1,15},{3,13... | collective-permute-start | bytes 196616 | tf_op jit(solution)/shard_map/ppermute | solution.py:360
  47.5 1.8 %collective-permute-start.4 = (bf16[2,32,512]{2,1,0:T(8,128)(2,1)S(1)}, bf16[2,32,512]{2,1,0:T(8,128)(2,1)S(1)}, u32[]{:S(2)}, u32[]{:S(2)}) collective-permute-start(bf16[2,32,512]{2,1,0:T(8,128)(2,1)S(1)} %get-tuple-element.56), channel_id=1, source_target_pairs={{0,2},{2,0},{4,6},{6,4},{8,10},{10,8},{12,14},{14,12},{1,3},{3,1},... | collective-permute-start | bytes 196616 | tf_op jit(solution)/shard_map/ppermute | solution.py:360
  49.3 1.6 %collective-permute-start.6 = (bf16[2,32,512]{2,1,0:T(8,128)(2,1)S(1)}, bf16[2,32,512]{2,1,0:T(8,128)(2,1)S(1)}, u32[]{:S(2)}, u32[]{:S(2)}) collective-permute-start(bf16[2,32,512]{2,1,0:T(8,128)(2,1)S(1)} %get-tuple-element.58), channel_id=1, source_target_pairs={{0,6},{2,4},{4,2},{6,0},{8,14},{10,12},{12,10},{14,8},{1,7},{3,5},... | collective-permute-start | bytes 196616 | tf_op jit(solution)/shard_map/ppermute | solution.py:360
  51.8 7.5 %conv.3 = (bf16[2,32,512]{2,1,0:T(8,128)(2,1)S(1)}, bf16[2,32,512]{2,1,0:T(8,128)(2,1)S(1)}, bf16[2,32,512]{2,1,0:T(8,128)(2,1)S(1)}, bf16[2,32,512]{2,1,0:T(8,1...) custom-call(s32[10]{0:T(128)S(1)} %pad_add_fusion.scalars, ...), custom_call_target="tpu_custom_call" | custom-call | flops 4160749568 | bytes 9650176 | tf_op jit(solution)/shard_map/conv/pallas_call | solution.py:201
  59.3 3.5 %collective-permute-start.8 = (bf16[2,32,512]{2,1,0:T(8,128)(2,1)S(1)}, bf16[2,32,512]{2,1,0:T(8,128)(2,1)S(1)}, u32[]{:S(2)}, u32[]{:S(2)}) collective-permute-start(bf16[2,32,512]{2,1,0:T(8,128)(2,1)S(1)} %get-tuple-element.60), channel_id=1, source_target_pairs={{0,10},{2,8},{4,14},{6,12},{8,2},{10,0},{12,6},{14,4},{1,11},{3,9}... | collective-permute-start | bytes 196616 | tf_op jit(solution)/shard_map/ppermute | solution.py:360
  63.0 1.5 %collective-permute-start.11 = (bf16[2,32,512]{2,1,0:T(8,128)(2,1)S(1)}, bf16[2,32,512]{2,1,0:T(8,128)(2,1)S(1)}, u32[]{:S(2)}, u32[]{:S(2)}) collective-permute-start(bf16[2,32,512]{2,1,0:T(8,128)(2,1)S(1)} %get-tuple-element.65), channel_id=1, source_target_pairs={{0,2},{2,0},{4,6},{6,4},{8,10},{10,8},{12,14},{14,12},{1,3},{3,1},... | collective-permute-start | bytes 196616 | tf_op jit(solution)/shard_map/ppermute | solution.py:360
  64.6 2.0 %collective-permute-start.13 = (bf16[2,32,512]{2,1,0:T(8,128)(2,1)S(1)}, bf16[2,32,512]{2,1,0:T(8,128)(2,1)S(1)}, u32[]{:S(2)}, u32[]{:S(2)}) collective-permute-start(bf16[2,32,512]{2,1,0:T(8,128)(2,1)S(1)} %get-tuple-element.67), channel_id=1, source_target_pairs={{0,6},{2,4},{4,2},{6,0},{8,14},{10,12},{12,10},{14,8},{1,7},{3,5},... | collective-permute-start | bytes 196616 | tf_op jit(solution)/shard_map/ppermute | solution.py:360
  66.9 1.9 %collective-permute-start.14 = (bf16[2,32,512]{2,1,0:T(8,128)(2,1)S(1)}, bf16[2,32,512]{2,1,0:T(8,128)(2,1)S(1)}, u32[]{:S(2)}, u32[]{:S(2)}) collective-permute-start(bf16[2,32,512]{2,1,0:T(8,128)(2,1)S(1)} %get-tuple-element.68), channel_id=1, source_target_pairs={{0,8},{2,10},{4,12},{6,14},{8,0},{10,2},{12,4},{14,6},{1,9},{3,11}... | collective-permute-start | bytes 196616 | tf_op jit(solution)/shard_map/ppermute | solution.py:360
  69.3 1.8 %collective-permute-start.15 = (bf16[2,32,512]{2,1,0:T(8,128)(2,1)S(1)}, bf16[2,32,512]{2,1,0:T(8,128)(2,1)S(1)}, u32[]{:S(2)}, u32[]{:S(2)}) collective-permute-start(bf16[2,32,512]{2,1,0:T(8,128)(2,1)S(1)} %get-tuple-element.69), channel_id=1, source_target_pairs={{0,10},{2,8},{4,14},{6,12},{8,2},{10,0},{12,6},{14,4},{1,11},{3,9}... | collective-permute-start | bytes 196616 | tf_op jit(solution)/shard_map/ppermute | solution.py:360
  71.1 3.4 %collective-permute-start.16 = (bf16[2,32,512]{2,1,0:T(8,128)(2,1)S(1)}, bf16[2,32,512]{2,1,0:T(8,128)(2,1)S(1)}, u32[]{:S(2)}, u32[]{:S(2)}) collective-permute-start(bf16[2,32,512]{2,1,0:T(8,128)(2,1)S(1)} %get-tuple-element.70), channel_id=1, source_target_pairs={{0,12},{2,14},{4,8},{6,10},{8,4},{10,6},{12,0},{14,2},{1,13},{3,15... | collective-permute-start | bytes 196616 | tf_op jit(solution)/shard_map/ppermute | solution.py:360
  75.7 2.7 %attend.2 = (bf16[2,32,512]{2,1,0:T(8,128)(2,1)S(1)}, bf16[2,32,512]{2,1,0:T(8,128)(2,1)S(1)}, bf16[2,32,512]{2,1,0:T(8,128)(2,1)S(1)}, bf16[2,32,512]{2,1,0:T(8...) custom-call(s32[8]{0:T(128)S(1)} %broadcast_multiply_fusion.first, ...), custom_call_target="tpu_custom_call" | custom-call | flops 1342177280 | bytes 2621440 | tf_op jit(solution)/shard_map/attend/pallas_call | solution.py:288
  79.2 2.8 %collective-permute-start.27 = (bf16[2,32,512]{2,1,0:T(8,128)(2,1)S(1)}, bf16[2,32,512]{2,1,0:T(8,128)(2,1)S(1)}, u32[]{:S(2)}, u32[]{:S(2)}) collective-permute-start(bf16[2,32,512]{2,1,0:T(8,128)(2,1)S(1)} %get-tuple-element.82), channel_id=1, source_target_pairs={{0,6},{2,4},{4,2},{6,0},{8,14},{10,12},{12,10},{14,8},{1,7},{3,5},... | collective-permute-start | bytes 196616 | tf_op jit(solution)/shard_map/ppermute | solution.py:360
  82.0 1.9 %collective-permute-start.28 = (bf16[2,32,512]{2,1,0:T(8,128)(2,1)S(1)}, bf16[2,32,512]{2,1,0:T(8,128)(2,1)S(1)}, u32[]{:S(2)}, u32[]{:S(2)}) collective-permute-start(bf16[2,32,512]{2,1,0:T(8,128)(2,1)S(1)} %get-tuple-element.83), channel_id=1, source_target_pairs={{0,8},{2,10},{4,12},{6,14},{8,0},{10,2},{12,4},{14,6},{1,9},{3,11}... | collective-permute-start | bytes 196616 | tf_op jit(solution)/shard_map/ppermute | solution.py:360
  85.0 2.6 %attend.3 = (bf16[2,32,512]{2,1,0:T(8,128)(2,1)S(1)}, bf16[2,32,512]{2,1,0:T(8,128)(2,1)S(1)}, bf16[2,32,512]{2,1,0:T(8,128)(2,1)S(1)}, bf16[2,32,512]{2,1,0:T(8...) custom-call(s32[8]{0:T(128)S(1)} %broadcast_multiply_fusion.first, ...), custom_call_target="tpu_custom_call" | custom-call | flops 1342177280 | bytes 2621440 | tf_op jit(solution)/shard_map/attend/pallas_call | solution.py:288
  87.7 3.5 %collective-permute-start.30 = (bf16[2,32,512]{2,1,0:T(8,128)(2,1)S(1)}, bf16[2,32,512]{2,1,0:T(8,128)(2,1)S(1)}, u32[]{:S(2)}, u32[]{:S(2)}) collective-permute-start(bf16[2,32,512]{2,1,0:T(8,128)(2,1)S(1)} %get-tuple-element.85), channel_id=1, source_target_pairs={{0,12},{2,14},{4,8},{6,10},{8,4},{10,6},{12,0},{14,2},{1,13},{3,15... | collective-permute-start | bytes 196616 | tf_op jit(solution)/shard_map/ppermute | solution.py:360
  93.0 2.8 %collective-permute-start.20 = (bf16[2,32,512]{2,1,0:T(8,128)(2,1)S(1)}, bf16[2,32,512]{2,1,0:T(8,128)(2,1)S(1)}, u32[]{:S(2)}, u32[]{:S(2)}) collective-permute-start(bf16[2,32,512]{2,1,0:T(8,128)(2,1)S(1)} %get-tuple-element.75), channel_id=1, source_target_pairs={{0,6},{2,4},{4,2},{6,0},{8,14},{10,12},{12,10},{14,8},{1,7},{3,5},... | collective-permute-start | bytes 196616 | tf_op jit(solution)/shard_map/ppermute | solution.py:360
  95.9 1.9 %collective-permute-start.21 = (bf16[2,32,512]{2,1,0:T(8,128)(2,1)S(1)}, bf16[2,32,512]{2,1,0:T(8,128)(2,1)S(1)}, u32[]{:S(2)}, u32[]{:S(2)}) collective-permute-start(bf16[2,32,512]{2,1,0:T(8,128)(2,1)S(1)} %get-tuple-element.76), channel_id=1, source_target_pairs={{0,8},{2,10},{4,12},{6,14},{8,0},{10,2},{12,4},{14,6},{1,9},{3,11}... | collective-permute-start | bytes 196616 | tf_op jit(solution)/shard_map/ppermute | solution.py:360
  98.9 3.4 %collective-permute-start.23 = (bf16[2,32,512]{2,1,0:T(8,128)(2,1)S(1)}, bf16[2,32,512]{2,1,0:T(8,128)(2,1)S(1)}, u32[]{:S(2)}, u32[]{:S(2)}) collective-permute-start(bf16[2,32,512]{2,1,0:T(8,128)(2,1)S(1)} %get-tuple-element.78), channel_id=1, source_target_pairs={{0,12},{2,14},{4,8},{6,10},{8,4},{10,6},{12,0},{14,2},{1,13},{3,15... | collective-permute-start | bytes 196616 | tf_op jit(solution)/shard_map/ppermute | solution.py:360
  106.1 3.2 %collective-permute-done.24.refs_7_ = bf16[2,32,512]{2,1,0:T(8,128)(2,1)S(1)} collective-permute-done((bf16[2,32,512]{2,1,0:T(8,128)(2,1)S(1)}, bf16[2,32,512]{2,1,0:T(8,128)(2,1)S(1)}, u32[]{:S(2)}, u32[]{:S(2)}) %collective-permute-start.24) | collective-permute-done | bytes 65568 | tf_op jit(solution)/shard_map/ppermute | solution.py:360
  (89 shorter events, 15.3 us)
Async XLA Ops:
  2.1 32.9 %collective-permute-start.3 = (bf16[3,17,16,512]{3,2,1,0:T(8,128)(2,1)}, bf16[3,17,16,512]{3,2,1,0:T(8,128)(2,1)S(1)}, u32[]{:S(2)}, u32[]{:S(2)}) collective-permute-start(bf16[3,17,16,512]{3,2,1,0:T(8,128)(2,1)} %pick.3), channel_id=1, source_target_pairs={{0,2},{2,4},{4,6},{6,8},{8,10},{10,12},{12,14},{1,3},{3,5},{5,7},{... | collective-permute-start | bytes 2506760 | tf_op jit(solution)/shard_map/ppermute | solution.py:375
  9.7 18.7 %collective-permute-start.2 = (bf16[4,32,512]{2,1,0:T(8,128)(2,1)}, bf16[4,32,512]{2,1,0:T(8,128)(2,1)S(1)}, u32[]{:S(2)}, u32[]{:S(2)}) collective-permute-start(bf16[4,32,512]{2,1,0:T(8,128)(2,1)} %fusion), channel_id=1, source_target_pairs={{0,1},{1,0},{2,3},{3,2},{4,5},{5,4},{6,7},{7,6},{8,9},{9,8},{10,11... | collective-permute-start | bytes 393224 | tf_op jit(solution)/shard_map/ppermute | solution.py:376
  10.6 17.7 %collective-permute-start.1 = (bf16[3,32,512]{2,1,0:T(8,128)(2,1)S(1)}, bf16[3,32,512]{2,1,0:T(8,128)(2,1)S(1)}, u32[]{:S(2)}, u32[]{:S(2)}) collective-permute-start(bf16[3,32,512]{2,1,0:T(8,128)(2,1)S(1)} %slice.21), channel_id=1, source_target_pairs={{0,3},{1,2},{2,5},{3,4},{4,7},{5,6},{6,9},{7,8},{8,11},{9,10},{10,... | collective-permute-start | bytes 294920 | tf_op jit(solution)/shard_map/ppermute | solution.py:377
  16.1 34.9 %collective-permute-start = (bf16[3,15,16,512]{3,2,1,0:T(8,128)(2,1)}, bf16[3,15,16,512]{3,2,1,0:T(8,128)(2,1)}, u32[]{:S(2)}, u32[]{:S(2)}) collective-permute-start(bf16[3,15,16,512]{3,2,1,0:T(8,128)(2,1)} %pick.2), channel_id=1, source_target_pairs={{0,2},{2,4},{4,6},{6,8},{8,10},{10,12},{12,14},{1,3},{3,5},{5,7},{... | collective-permute-start | bytes 2211848 | tf_op jit(solution)/shard_map/ppermute | solution.py:375
  44.2 15.1 %collective-permute-start.10 = (bf16[2,32,512]{2,1,0:T(8,128)(2,1)S(1)}, bf16[2,32,512]{2,1,0:T(8,128)(2,1)S(1)}, u32[]{:S(2)}, u32[]{:S(2)}) collective-permute-start(bf16[2,32,512]{2,1,0:T(8,128)(2,1)S(1)} %get-tuple-element.62), channel_id=1, source_target_pairs={{0,14},{2,12},{4,10},{6,8},{8,6},{10,4},{12,2},{14,0},{1,15},{3,13... | collective-permute-start | bytes 196616 | tf_op jit(solution)/shard_map/ppermute | solution.py:360
  47.5 15.3 %collective-permute-start.4 = (bf16[2,32,512]{2,1,0:T(8,128)(2,1)S(1)}, bf16[2,32,512]{2,1,0:T(8,128)(2,1)S(1)}, u32[]{:S(2)}, u32[]{:S(2)}) collective-permute-start(bf16[2,32,512]{2,1,0:T(8,128)(2,1)S(1)} %get-tuple-element.56), channel_id=1, source_target_pairs={{0,2},{2,0},{4,6},{6,4},{8,10},{10,8},{12,14},{14,12},{1,3},{3,1},... | collective-permute-start | bytes 196616 | tf_op jit(solution)/shard_map/ppermute | solution.py:360
  49.3 13.7 %collective-permute-start.5 = (bf16[2,32,512]{2,1,0:T(8,128)(2,1)S(1)}, bf16[2,32,512]{2,1,0:T(8,128)(2,1)S(1)}, u32[]{:S(2)}, u32[]{:S(2)}) collective-permute-start(bf16[2,32,512]{2,1,0:T(8,128)(2,1)S(1)} %get-tuple-element.57), channel_id=1, source_target_pairs={{0,4},{2,6},{4,0},{6,2},{8,12},{10,14},{12,8},{14,10},{1,5},{3,7},... | collective-permute-start | bytes 196616 | tf_op jit(solution)/shard_map/ppermute | solution.py:360
  49.3 15.2 %collective-permute-start.6 = (bf16[2,32,512]{2,1,0:T(8,128)(2,1)S(1)}, bf16[2,32,512]{2,1,0:T(8,128)(2,1)S(1)}, u32[]{:S(2)}, u32[]{:S(2)}) collective-permute-start(bf16[2,32,512]{2,1,0:T(8,128)(2,1)S(1)} %get-tuple-element.58), channel_id=1, source_target_pairs={{0,6},{2,4},{4,2},{6,0},{8,14},{10,12},{12,10},{14,8},{1,7},{3,5},... | collective-permute-start | bytes 196616 | tf_op jit(solution)/shard_map/ppermute | solution.py:360
  51.0 13.6 %collective-permute-start.7 = (bf16[2,32,512]{2,1,0:T(8,128)(2,1)S(1)}, bf16[2,32,512]{2,1,0:T(8,128)(2,1)S(1)}, u32[]{:S(2)}, u32[]{:S(2)}) collective-permute-start(bf16[2,32,512]{2,1,0:T(8,128)(2,1)S(1)} %get-tuple-element.59), channel_id=1, source_target_pairs={{0,8},{2,10},{4,12},{6,14},{8,0},{10,2},{12,4},{14,6},{1,9},{3,11}... | collective-permute-start | bytes 196616 | tf_op jit(solution)/shard_map/ppermute | solution.py:360
  59.3 7.6 %collective-permute-start.8 = (bf16[2,32,512]{2,1,0:T(8,128)(2,1)S(1)}, bf16[2,32,512]{2,1,0:T(8,128)(2,1)S(1)}, u32[]{:S(2)}, u32[]{:S(2)}) collective-permute-start(bf16[2,32,512]{2,1,0:T(8,128)(2,1)S(1)} %get-tuple-element.60), channel_id=1, source_target_pairs={{0,10},{2,8},{4,14},{6,12},{8,2},{10,0},{12,6},{14,4},{1,11},{3,9}... | collective-permute-start | bytes 196616 | tf_op jit(solution)/shard_map/ppermute | solution.py:360
  62.8 6.5 %collective-permute-start.9 = (bf16[2,32,512]{2,1,0:T(8,128)(2,1)S(1)}, bf16[2,32,512]{2,1,0:T(8,128)(2,1)S(1)}, u32[]{:S(2)}, u32[]{:S(2)}) collective-permute-start(bf16[2,32,512]{2,1,0:T(8,128)(2,1)S(1)} %get-tuple-element.61), channel_id=1, source_target_pairs={{0,12},{2,14},{4,8},{6,10},{8,4},{10,6},{12,0},{14,2},{1,13},{3,15... | collective-permute-start | bytes 196616 | tf_op jit(solution)/shard_map/ppermute | solution.py:360
  63.0 8.1 %collective-permute-start.11 = (bf16[2,32,512]{2,1,0:T(8,128)(2,1)S(1)}, bf16[2,32,512]{2,1,0:T(8,128)(2,1)S(1)}, u32[]{:S(2)}, u32[]{:S(2)}) collective-permute-start(bf16[2,32,512]{2,1,0:T(8,128)(2,1)S(1)} %get-tuple-element.65), channel_id=1, source_target_pairs={{0,2},{2,0},{4,6},{6,4},{8,10},{10,8},{12,14},{14,12},{1,3},{3,1},... | collective-permute-start | bytes 196616 | tf_op jit(solution)/shard_map/ppermute | solution.py:360
  64.5 10.0 %collective-permute-start.12 = (bf16[2,32,512]{2,1,0:T(8,128)(2,1)S(1)}, bf16[2,32,512]{2,1,0:T(8,128)(2,1)S(1)}, u32[]{:S(2)}, u32[]{:S(2)}) collective-permute-start(bf16[2,32,512]{2,1,0:T(8,128)(2,1)S(1)} %get-tuple-element.66), channel_id=1, source_target_pairs={{0,4},{2,6},{4,0},{6,2},{8,12},{10,14},{12,8},{14,10},{1,5},{3,7},... | collective-permute-start | bytes 196616 | tf_op jit(solution)/shard_map/ppermute | solution.py:360
  64.6 13.9 %collective-permute-start.13 = (bf16[2,32,512]{2,1,0:T(8,128)(2,1)S(1)}, bf16[2,32,512]{2,1,0:T(8,128)(2,1)S(1)}, u32[]{:S(2)}, u32[]{:S(2)}) collective-permute-start(bf16[2,32,512]{2,1,0:T(8,128)(2,1)S(1)} %get-tuple-element.67), channel_id=1, source_target_pairs={{0,6},{2,4},{4,2},{6,0},{8,14},{10,12},{12,10},{14,8},{1,7},{3,5},... | collective-permute-start | bytes 196616 | tf_op jit(solution)/shard_map/ppermute | solution.py:360
  66.9 12.3 %collective-permute-start.14 = (bf16[2,32,512]{2,1,0:T(8,128)(2,1)S(1)}, bf16[2,32,512]{2,1,0:T(8,128)(2,1)S(1)}, u32[]{:S(2)}, u32[]{:S(2)}) collective-permute-start(bf16[2,32,512]{2,1,0:T(8,128)(2,1)S(1)} %get-tuple-element.68), channel_id=1, source_target_pairs={{0,8},{2,10},{4,12},{6,14},{8,0},{10,2},{12,4},{14,6},{1,9},{3,11}... | collective-permute-start | bytes 196616 | tf_op jit(solution)/shard_map/ppermute | solution.py:360
  69.3 9.9 %collective-permute-start.15 = (bf16[2,32,512]{2,1,0:T(8,128)(2,1)S(1)}, bf16[2,32,512]{2,1,0:T(8,128)(2,1)S(1)}, u32[]{:S(2)}, u32[]{:S(2)}) collective-permute-start(bf16[2,32,512]{2,1,0:T(8,128)(2,1)S(1)} %get-tuple-element.69), channel_id=1, source_target_pairs={{0,10},{2,8},{4,14},{6,12},{8,2},{10,0},{12,6},{14,4},{1,11},{3,9}... | collective-permute-start | bytes 196616 | tf_op jit(solution)/shard_map/ppermute | solution.py:360
  71.1 10.9 %collective-permute-start.16 = (bf16[2,32,512]{2,1,0:T(8,128)(2,1)S(1)}, bf16[2,32,512]{2,1,0:T(8,128)(2,1)S(1)}, u32[]{:S(2)}, u32[]{:S(2)}) collective-permute-start(bf16[2,32,512]{2,1,0:T(8,128)(2,1)S(1)} %get-tuple-element.70), channel_id=1, source_target_pairs={{0,12},{2,14},{4,8},{6,10},{8,4},{10,6},{12,0},{14,2},{1,13},{3,15... | collective-permute-start | bytes 196616 | tf_op jit(solution)/shard_map/ppermute | solution.py:360
  74.5 9.4 %collective-permute-start.17 = (bf16[2,32,512]{2,1,0:T(8,128)(2,1)S(1)}, bf16[2,32,512]{2,1,0:T(8,128)(2,1)S(1)}, u32[]{:S(2)}, u32[]{:S(2)}) collective-permute-start(bf16[2,32,512]{2,1,0:T(8,128)(2,1)S(1)} %get-tuple-element.71), channel_id=1, source_target_pairs={{0,14},{2,12},{4,10},{6,8},{8,6},{10,4},{12,2},{14,0},{1,15},{3,13... | collective-permute-start | bytes 196616 | tf_op jit(solution)/shard_map/ppermute | solution.py:360
  78.4 9.2 %collective-permute-start.25 = (bf16[2,32,512]{2,1,0:T(8,128)(2,1)S(1)}, bf16[2,32,512]{2,1,0:T(8,128)(2,1)S(1)}, u32[]{:S(2)}, u32[]{:S(2)}) collective-permute-start(bf16[2,32,512]{2,1,0:T(8,128)(2,1)S(1)} %get-tuple-element.80), channel_id=1, source_target_pairs={{0,2},{2,0},{4,6},{6,4},{8,10},{10,8},{12,14},{14,12},{1,3},{3,1},... | collective-permute-start | bytes 196616 | tf_op jit(solution)/shard_map/ppermute | solution.py:360
  79.1 12.0 %collective-permute-start.26 = (bf16[2,32,512]{2,1,0:T(8,128)(2,1)S(1)}, bf16[2,32,512]{2,1,0:T(8,128)(2,1)S(1)}, u32[]{:S(2)}, u32[]{:S(2)}) collective-permute-start(bf16[2,32,512]{2,1,0:T(8,128)(2,1)S(1)} %get-tuple-element.81), channel_id=1, source_target_pairs={{0,4},{2,6},{4,0},{6,2},{8,12},{10,14},{12,8},{14,10},{1,5},{3,7},... | collective-permute-start | bytes 196616 | tf_op jit(solution)/shard_map/ppermute | solution.py:360
  79.2 13.2 %collective-permute-start.27 = (bf16[2,32,512]{2,1,0:T(8,128)(2,1)S(1)}, bf16[2,32,512]{2,1,0:T(8,128)(2,1)S(1)}, u32[]{:S(2)}, u32[]{:S(2)}) collective-permute-start(bf16[2,32,512]{2,1,0:T(8,128)(2,1)S(1)} %get-tuple-element.82), channel_id=1, source_target_pairs={{0,6},{2,4},{4,2},{6,0},{8,14},{10,12},{12,10},{14,8},{1,7},{3,5},... | collective-permute-start | bytes 196616 | tf_op jit(solution)/shard_map/ppermute | solution.py:360
  82.0 11.0 %collective-permute-start.28 = (bf16[2,32,512]{2,1,0:T(8,128)(2,1)S(1)}, bf16[2,32,512]{2,1,0:T(8,128)(2,1)S(1)}, u32[]{:S(2)}, u32[]{:S(2)}) collective-permute-start(bf16[2,32,512]{2,1,0:T(8,128)(2,1)S(1)} %get-tuple-element.83), channel_id=1, source_target_pairs={{0,8},{2,10},{4,12},{6,14},{8,0},{10,2},{12,4},{14,6},{1,9},{3,11}... | collective-permute-start | bytes 196616 | tf_op jit(solution)/shard_map/ppermute | solution.py:360
  83.9 9.2 %collective-permute-start.29 = (bf16[2,32,512]{2,1,0:T(8,128)(2,1)S(1)}, bf16[2,32,512]{2,1,0:T(8,128)(2,1)S(1)}, u32[]{:S(2)}, u32[]{:S(2)}) collective-permute-start(bf16[2,32,512]{2,1,0:T(8,128)(2,1)S(1)} %get-tuple-element.84), channel_id=1, source_target_pairs={{0,10},{2,8},{4,14},{6,12},{8,2},{10,0},{12,6},{14,4},{1,11},{3,9}... | collective-permute-start | bytes 196616 | tf_op jit(solution)/shard_map/ppermute | solution.py:360
  87.7 8.2 %collective-permute-start.30 = (bf16[2,32,512]{2,1,0:T(8,128)(2,1)S(1)}, bf16[2,32,512]{2,1,0:T(8,128)(2,1)S(1)}, u32[]{:S(2)}, u32[]{:S(2)}) collective-permute-start(bf16[2,32,512]{2,1,0:T(8,128)(2,1)S(1)} %get-tuple-element.85), channel_id=1, source_target_pairs={{0,12},{2,14},{4,8},{6,10},{8,4},{10,6},{12,0},{14,2},{1,13},{3,15... | collective-permute-start | bytes 196616 | tf_op jit(solution)/shard_map/ppermute | solution.py:360
  91.2 7.5 %collective-permute-start.31 = (bf16[2,32,512]{2,1,0:T(8,128)(2,1)S(1)}, bf16[2,32,512]{2,1,0:T(8,128)(2,1)S(1)}, u32[]{:S(2)}, u32[]{:S(2)}) collective-permute-start(bf16[2,32,512]{2,1,0:T(8,128)(2,1)S(1)} %get-tuple-element.86), channel_id=1, source_target_pairs={{0,14},{2,12},{4,10},{6,8},{8,6},{10,4},{12,2},{14,0},{1,15},{3,13... | collective-permute-start | bytes 196616 | tf_op jit(solution)/shard_map/ppermute | solution.py:360
  92.4 6.5 %collective-permute-start.18 = (bf16[2,32,512]{2,1,0:T(8,128)(2,1)S(1)}, bf16[2,32,512]{2,1,0:T(8,128)(2,1)S(1)}, u32[]{:S(2)}, u32[]{:S(2)}) collective-permute-start(bf16[2,32,512]{2,1,0:T(8,128)(2,1)S(1)} %get-tuple-element.73), channel_id=1, source_target_pairs={{0,2},{2,0},{4,6},{6,4},{8,10},{10,8},{12,14},{14,12},{1,3},{3,1},... | collective-permute-start | bytes 196616 | tf_op jit(solution)/shard_map/ppermute | solution.py:360
  93.0 9.3 %collective-permute-start.19 = (bf16[2,32,512]{2,1,0:T(8,128)(2,1)S(1)}, bf16[2,32,512]{2,1,0:T(8,128)(2,1)S(1)}, u32[]{:S(2)}, u32[]{:S(2)}) collective-permute-start(bf16[2,32,512]{2,1,0:T(8,128)(2,1)S(1)} %get-tuple-element.74), channel_id=1, source_target_pairs={{0,4},{2,6},{4,0},{6,2},{8,12},{10,14},{12,8},{14,10},{1,5},{3,7},... | collective-permute-start | bytes 196616 | tf_op jit(solution)/shard_map/ppermute | solution.py:360
  93.0 11.9 %collective-permute-start.20 = (bf16[2,32,512]{2,1,0:T(8,128)(2,1)S(1)}, bf16[2,32,512]{2,1,0:T(8,128)(2,1)S(1)}, u32[]{:S(2)}, u32[]{:S(2)}) collective-permute-start(bf16[2,32,512]{2,1,0:T(8,128)(2,1)S(1)} %get-tuple-element.75), channel_id=1, source_target_pairs={{0,6},{2,4},{4,2},{6,0},{8,14},{10,12},{12,10},{14,8},{1,7},{3,5},... | collective-permute-start | bytes 196616 | tf_op jit(solution)/shard_map/ppermute | solution.py:360
  95.9 9.1 %collective-permute-start.21 = (bf16[2,32,512]{2,1,0:T(8,128)(2,1)S(1)}, bf16[2,32,512]{2,1,0:T(8,128)(2,1)S(1)}, u32[]{:S(2)}, u32[]{:S(2)}) collective-permute-start(bf16[2,32,512]{2,1,0:T(8,128)(2,1)S(1)} %get-tuple-element.76), channel_id=1, source_target_pairs={{0,8},{2,10},{4,12},{6,14},{8,0},{10,2},{12,4},{14,6},{1,9},{3,11}... | collective-permute-start | bytes 196616 | tf_op jit(solution)/shard_map/ppermute | solution.py:360
  98.7 7.5 %collective-permute-start.22 = (bf16[2,32,512]{2,1,0:T(8,128)(2,1)S(1)}, bf16[2,32,512]{2,1,0:T(8,128)(2,1)S(1)}, u32[]{:S(2)}, u32[]{:S(2)}) collective-permute-start(bf16[2,32,512]{2,1,0:T(8,128)(2,1)S(1)} %get-tuple-element.77), channel_id=1, source_target_pairs={{0,10},{2,8},{4,14},{6,12},{8,2},{10,0},{12,6},{14,4},{1,11},{3,9}... | collective-permute-start | bytes 196616 | tf_op jit(solution)/shard_map/ppermute | solution.py:360
  98.9 7.2 %collective-permute-start.23 = (bf16[2,32,512]{2,1,0:T(8,128)(2,1)S(1)}, bf16[2,32,512]{2,1,0:T(8,128)(2,1)S(1)}, u32[]{:S(2)}, u32[]{:S(2)}) collective-permute-start(bf16[2,32,512]{2,1,0:T(8,128)(2,1)S(1)} %get-tuple-element.78), channel_id=1, source_target_pairs={{0,12},{2,14},{4,8},{6,10},{8,4},{10,6},{12,0},{14,2},{1,13},{3,15... | collective-permute-start | bytes 196616 | tf_op jit(solution)/shard_map/ppermute | solution.py:360
  102.3 7.0 %collective-permute-start.24 = (bf16[2,32,512]{2,1,0:T(8,128)(2,1)S(1)}, bf16[2,32,512]{2,1,0:T(8,128)(2,1)S(1)}, u32[]{:S(2)}, u32[]{:S(2)}) collective-permute-start(bf16[2,32,512]{2,1,0:T(8,128)(2,1)S(1)} %get-tuple-element.79), channel_id=1, source_target_pairs={{0,14},{2,12},{4,10},{6,8},{8,6},{10,4},{12,2},{14,0},{1,15},{3,13... | collective-permute-start | bytes 196616 | tf_op jit(solution)/shard_map/ppermute | solution.py:360
  (17 other events, 242.9 us)

commit v7 on v6

--- a/solution.py
+++ b/solution.py
@@ -15,6 +15,7 @@
 
 VMEM = pl.BlockSpec(memory_space=pltpu.VMEM)
 SMEM = pl.BlockSpec(memory_space=pltpu.SMEM)
+HBM = pl.BlockSpec(memory_space=pltpu.HBM)
 ANY = pl.BlockSpec(memory_space=pl.ANY)
 
 
@@ -37,9 +38,14 @@
 
 def pick_kernel(first, begin, video, out, sem):
     count, rows = out.shape[:2]
-    copy = pltpu.make_async_copy(video.at[first : first + count, begin : begin + rows], out, sem)
-    copy.start()
-    copy.wait()
+    copies = [
+        pltpu.make_async_copy(video.at[first + t, begin : begin + rows], out.at[t], sem.at[t])
+        for t in range(count)
+    ]
+    for copy in copies:
+        copy.start()
+    for copy in copies:
+        copy.wait()
 
 
 def pick(video, first, begin, end):
@@ -48,10 +54,10 @@
     return pl.pallas_call(
         partial(pick_kernel, first, begin),
         out_shape=jax.ShapeDtypeStruct(shape, video.dtype),
-        in_specs=[ANY],
+        in_specs=[HBM],
         out_specs=VMEM,
-        scratch_shapes=[pltpu.SemaphoreType.DMA],
-        compiler_params=params(56),
+        scratch_shapes=[pltpu.SemaphoreType.DMA((frames - first,))],
+        compiler_params=params(8),
         name="pick",
     )(video)
 
@@ -59,9 +65,14 @@
 def early_kernel(begin, video, edge, w_time, b_time, w_down, b_down, own, part, rows_in, lifted, sem):
     frames, rows, width, channels = rows_in.shape
     pixels = rows * width
-    copy = pltpu.make_async_copy(video.at[:, begin : begin + rows], rows_in, sem)
-    copy.start()
-    copy.wait()
+    copies = [
+        pltpu.make_async_copy(video.at[t, begin : begin + rows], rows_in.at[t], sem.at[t])
+        for t in range(frames)
+    ]
+    for copy in copies:
+        copy.start()
+    for copy in copies:
+        copy.wait()
 
     def frame(t):
         return jnp.concatenate([rows_in[t].reshape(pixels, channels), edge[t]], axis=0)
@@ -89,14 +100,14 @@
             jax.ShapeDtypeStruct((taps - 1, pixels, channels), jnp.bfloat16),
             jax.ShapeDtypeStruct((frames // 2 - 1, pixels, channels), jnp.float32),
         ],
-        in_specs=[ANY] + [VMEM] * 5,
+        in_specs=[HBM] + [VMEM] * 5,
         out_specs=[VMEM] * 2,
         scratch_shapes=[
             pltpu.VMEM((frames, rows, width, channels), jnp.bfloat16),
             pltpu.VMEM((frames, pixels, channels), jnp.bfloat16),
-            pltpu.SemaphoreType.DMA,
+            pltpu.SemaphoreType.DMA((frames,)),
         ],
-        compiler_params=params(24),
+        compiler_params=params(16),
         cost_estimate=cost(flops, w_time, w_down),
         name="early",
     )(video, edge, w_time, b_time, w_down, b_down)
@@ -115,8 +126,12 @@
     halves = result.shape[0]
     pixels = rows * width
     edges = halo_edge.shape[1]
-    fetch = pltpu.make_async_copy(w_space, weights, sem)
-    fetch.start()
+    fetches = [
+        pltpu.make_async_copy(w_space.at[tap], weights.at[tap], sem.at[tap])
+        for tap in range(w_space.shape[0])
+    ]
+    for fetch in fetches:
+        fetch.start()
     column = scalars[1]
 
     def frame(t):
@@ -164,7 +179,8 @@
         buffers[:, :, size + 1 :] = blank
     else:
         keeps[...] = buffers[:, :, size:]
-    fetch.wait()
+    for fetch in fetches:
+        fetch.wait()
 
     @pl.loop(0, halves)
     def _(s):
@@ -172,7 +188,7 @@
             return buffers[b, s, a : a + size].reshape(size * width, channels)
 
         lhs = jnp.concatenate([window(b, a) for a in range(3) for b in range(3)], axis=1)
-        acc = dot32(lhs, weights[...]) + b_space[...]
+        acc = dot32(lhs, weights[...].reshape(-1, channels)) + b_space[...]
         value = window(1, 1).astype(jnp.float32) + silu(acc)
         result[s] = value.astype(jnp.bfloat16)
 
@@ -201,16 +217,16 @@
     return pl.pallas_call(
         partial(conv_kernel, owners, size, fresh, last),
         out_shape=[jax.ShapeDtypeStruct(shape, jnp.bfloat16) for shape in shapes],
-        in_specs=[SMEM] + [VMEM] * 8 + [ANY] + [VMEM] * (1 + len(given)),
+        in_specs=[SMEM] + [VMEM] * 8 + [HBM] + [VMEM] * (1 + len(given)),
         out_specs=[VMEM] * len(shapes),
         scratch_shapes=[
             pltpu.VMEM((taps, pixels, channels), jnp.bfloat16),
             pltpu.VMEM((3, halves, size + 2, width, channels), jnp.bfloat16),
             pltpu.VMEM((halves, size * width, channels), jnp.bfloat16),
             pltpu.VMEM(w_space.shape, jnp.bfloat16),
-            pltpu.SemaphoreType.DMA,
+            pltpu.SemaphoreType.DMA(w_space.shape[:1]),
         ],
-        compiler_params=params(36),
+        compiler_params=params(24),
         cost_estimate=cost(flops, halo, own, part, w_time, w_down, w_space),
         name="conv",
     )(
@@ -343,7 +359,6 @@
     halves = frames // 2
     w_time = w_time.reshape(-1, channels)
     w_down = w_down.reshape(-1, channels)
-    w_space = w_space.reshape(-1, channels)
     b_time, b_down, b_space, gain = (v.reshape(1, -1) for v in (b_time, b_down, b_space, gain))
     chunks = parts if height % parts == 0 and height // parts * width % devices == 0 else 1
     size = height // chunks
@@ -383,6 +398,7 @@
         early(video, edge_rows(own_edge, begin, end), begin, end, w_time, b_time, w_down, b_down)
         for begin, end in spans
     ]
+    halo_edge = after(halo_edge, [part for _, part in ahead])
     spatials, kept = [], None
     for index, (begin, end) in enumerate(spans):
         own, part = ahead[index]

time: 111 us -> 107 us (0.964)
  waiting for transfers between devices: 13.9 us -> 4.99 us
  starting transfers between devices: 57.3 us -> 62.7 us
    ppermute x1, waiting for transfers between devices: 7.75 us -> 1.58 us  [per_device(): halo_edge = lax.ppermute(border[frames - taps:], ('tm', 'cols'), aslant)]
    ppermute x28, starting transfers between devices: 44.6 us -> 49.8 us  [exchange(): lax.ppermute(blocks[j], 'tm', [(i, i ^ j) for i in range(devices)])]
    ppermute x28, waiting for transfers between devices: 6.18 us -> 3.4 us  [exchange(): lax.ppermute(blocks[j], 'tm', [(i, i ^ j) for i in range(devices)])]
    pallas_call x2, Pallas kernels: 4.05 us -> 1.99 us  [pick(): pl.pallas_call(partial(pick_kernel, first, begin), out_shape=jax.ShapeDty...]
    slice x1, local copies, waits for them, and re-layouts: 1.95 us -> 0.41 us  [per_device(): border = jnp.where(column == 0, video[:, :, -1], video[:, :, 0])]
    unnamed x34 -> x36, local copies, waits for them, and re-layouts: 5.37 us -> 6.81 us
    pallas_call x2, Pallas kernels: 3.43 us -> 4.64 us  [early(): pl.pallas_call(partial(early_kernel, begin), out_shape=[jax.ShapeDtypeStr...]
  transfers between devices with their start and end apart: 32 -> 32, of which waited for: 6 -> 5; matrix products, arithmetic and copies ran while one was open for 3% -> 2% of each run, Pallas kernels for 24% -> 26%
where the time goes in v7:
time: 107 us
  starting transfers between devices  62.7 us (59%)
  Pallas kernels  29.8 us (28%)
  local copies, waits for them, and re-layouts  8.17 us (8%)
  waiting for transfers between devices  4.99 us (5%)
    ppermute x28, starting transfers between devices, exchange(): lax.ppermute(blocks[j], 'tm', [(i, i ^ j) for i in range(devices)])  49.8 us
    pallas_call x2, Pallas kernels, conv(): pl.pallas_call(partial(conv_kernel, owners, size, fresh, last), out_shape...  15 us
    ppermute x2, starting transfers between devices, per_device(): halos = [lax.ppermute(value, 'tm', onward) for value in sent]  10.2 us
    unnamed x36, local copies, waits for them, and re-layouts  6.81 us
    pallas_call x2, Pallas kernels, attend(): pl.pallas_call(partial(attend_kernel, frames_per, lanes, count), out_shap...  5.29 us
    pallas_call x2, Pallas kernels, early(): pl.pallas_call(partial(early_kernel, begin), out_shape=[jax.ShapeDtypeStr...  4.64 us
    ppermute x28, waiting for transfers between devices, exchange(): lax.ppermute(blocks[j], 'tm', [(i, i ^ j) for i in range(devices)])  3.4 us
    pallas_call x2, Pallas kernels, collect(): pl.pallas_call(partial(collect_kernel, count, chunk * count), out_shape=j...  2.78 us
  transfers between devices with their start and end apart: 32, of which 5 were waited for; matrix products, arithmetic and copies ran while one was open for 2% of the time, Pallas kernels for 26%

profile of v7, /device:TPU:0, one launch (start us, length us, event | category | flops | bytes accessed | tf_op | source)
XLA Modules:
  0.0 107.0 jit_solution(6405308726763292675)
XLA Ops:
  0.0 1.6 %copy-done = bf16[4,32,16,512]{3,2,1,0:T(8,128)(2,1)S(1)} copy-done((bf16[4,32,16,512]{3,2,1,0:T(8,128)(2,1)S(1)}, bf16[4,32,16,512]{3,2,1,0:T(8,128)(2,1)}, u32[]{:S(2)}) %copy-start) | copy-done | bytes 2097176
  1.7 5.9 %collective-permute-start.3 = (bf16[3,17,16,512]{3,2,1,0:T(8,128)(2,1)S(1)}, bf16[3,17,16,512]{3,2,1,0:T(8,128)(2,1)}, u32[]{:S(2)}, u32[]{:S(2)}) collective-permute-start(bf16[3,17,16,512]{3,2,1,0:T(8,128)(2,1)S(1)} %pick.3), channel_id=1, source_target_pairs={{0,2},{2,4},{4,6},{6,8},{8,10},{10,12},{12,14},{1,3},{3,5},{5,7},{... | collective-permute-start | bytes 2506760 | tf_op jit(solution)/shard_map/ppermute | solution.py:390
  9.7 2.6 %collective-permute-start.1 = (bf16[3,32,512]{2,1,0:T(8,128)(2,1)S(1)}, bf16[3,32,512]{2,1,0:T(8,128)(2,1)S(1)}, u32[]{:S(2)}, u32[]{:S(2)}) collective-permute-start(bf16[3,32,512]{2,1,0:T(8,128)(2,1)S(1)} %slice.21), channel_id=1, source_target_pairs={{0,3},{1,2},{2,5},{3,4},{4,7},{5,6},{6,9},{7,8},{8,11},{9,10},{10,... | collective-permute-start | bytes 294920 | tf_op jit(solution)/shard_map/ppermute | solution.py:392
  12.4 1.8 %pick.2 = bf16[3,15,16,512]{3,2,1,0:T(8,128)(2,1)} custom-call(bf16[4,32,16,512]{3,2,1,0:T(8,128)(2,1)S(1)} %copy-done.1), custom_call_target="tpu_custom_call" | custom-call | tf_op jit(solution)/shard_map/pick/pallas_call | solution.py:54
  14.2 4.3 %collective-permute-start = (bf16[3,15,16,512]{3,2,1,0:T(8,128)(2,1)}, bf16[3,15,16,512]{3,2,1,0:T(8,128)(2,1)}, u32[]{:S(2)}, u32[]{:S(2)}) collective-permute-start(bf16[3,15,16,512]{3,2,1,0:T(8,128)(2,1)} %pick.2), channel_id=1, source_target_pairs={{0,2},{2,4},{4,6},{6,8},{8,10},{10,12},{12,14},{1,3},{3,5},{5,7},{... | collective-permute-start | bytes 2211848 | tf_op jit(solution)/shard_map/ppermute | solution.py:390
  18.8 1.4 %copy-done.2 = bf16[3,512,512]{2,1,0:T(8,128)(2,1)S(1)} copy-done((bf16[3,512,512]{2,1,0:T(8,128)(2,1)S(1)}, bf16[3,512,512]{2,1,0:T(8,128)(2,1)}, u32[]{:S(2)}) %copy-start.2) | copy-done | bytes 1572888
  20.2 1.4 %copy-done.4 = bf16[3,512,512]{2,1,0:T(8,128)(2,1)S(1)} copy-done((bf16[3,512,512]{2,1,0:T(8,128)(2,1)S(1)}, bf16[3,512,512]{2,1,0:T(8,128)(2,1)}, u32[]{:S(2)}) %copy-start.4) | copy-done | bytes 1572888
  21.6 1.9 %early.2 = (bf16[2,304,512]{2,1,0:T(8,128)(2,1)S(1)}, f32[1,304,512]{2,1,0:T(8,128)S(1)}) custom-call(bf16[4,32,16,512]{3,2,1,0:T(8,128)(2,1)S(1)} %copy-done.1, bf16[4,32,512]{2,1,0:T(8,128)(2,1)S(1)} %broadcast_select_fusion.edge, bf16[1536,512]{1,0:T(8,128)(2,1)S(1)} %bitcast.11, f32[1,512]{1,0:T(1,128)S(1)} %bitcast.19, bf16[1536,512]{1,0:T(8,128)(2,1)S(1)} %bitcast.15, ...), custom_call_target="tpu_custom_call" | custom-call | flops 1275068416 | bytes 3145728 | tf_op jit(solution)/shard_map/early/pallas_call | solution.py:97
  23.5 2.8 %early.3 = (bf16[2,256,512]{2,1,0:T(8,128)(2,1)S(1)}, f32[1,256,512]{2,1,0:T(8,128)S(1)}) custom-call(bf16[4,32,16,512]{3,2,1,0:T(8,128)(2,1)S(1)} %copy-done.1, bf16[4,16,512]{2,1,0:T(8,128)(2,1)S(1)} %pad.17.edge, bf16[1536,512]{1,0:T(8,128)(2,1)S(1)} %bitcast.12, f32[1,512]{1,0:T(1,128)S(1)} %bitcast.20, bf16[1536,512]{1,0:T(8,128)(2,1)S(1)} %bitcast.16, ...), custom_call_target="tpu_custom_call" | custom-call | flops 1073741824 | bytes 3145728 | tf_op jit(solution)/shard_map/early/pallas_call | solution.py:97
  26.3 1.6 %collective-permute-done.1 = bf16[3,32,512]{2,1,0:T(8,128)(2,1)S(1)} collective-permute-done((bf16[3,32,512]{2,1,0:T(8,128)(2,1)S(1)}, bf16[3,32,512]{2,1,0:T(8,128)(2,1)S(1)}, u32[]{:S(2)}, u32[]{:S(2)}) %collective-permute-start.1) | collective-permute-done | bytes 98336 | tf_op jit(solution)/shard_map/ppermute | solution.py:392
  28.0 2.3 %copy-done.8 = bf16[9,512,512]{2,1,0:T(8,128)(2,1)S(1)} copy-done((bf16[9,512,512]{2,1,0:T(8,128)(2,1)S(1)}, bf16[9,512,512]{2,1,0:T(8,128)(2,1)}, u32[]{:S(2)}) %copy-start.8) | copy-done | bytes 4718616
  30.3 7.6 %conv.2 = (bf16[2,32,512]{2,1,0:T(8,128)(2,1)S(1)}, bf16[2,32,512]{2,1,0:T(8,128)(2,1)S(1)}, bf16[2,32,512]{2,1,0:T(8,128)(2,1)S(1)}, bf16[2,32,512]{2,1,0:T(8,1...) custom-call(s32[10]{0:T(128)S(1)} %pad_add_fusion.scalars, ...), custom_call_target="tpu_custom_call" | custom-call | flops 4487905280 | bytes 9945088 | tf_op jit(solution)/shard_map/conv/pallas_call | solution.py:217
  37.9 3.4 %collective-permute-start.10 = (bf16[2,32,512]{2,1,0:T(8,128)(2,1)S(1)}, bf16[2,32,512]{2,1,0:T(8,128)(2,1)S(1)}, u32[]{:S(2)}, u32[]{:S(2)}) collective-permute-start(bf16[2,32,512]{2,1,0:T(8,128)(2,1)S(1)} %get-tuple-element.64), channel_id=1, source_target_pairs={{0,14},{2,12},{4,10},{6,8},{8,6},{10,4},{12,2},{14,0},{1,15},{3,13... | collective-permute-start | bytes 196616 | tf_op jit(solution)/shard_map/ppermute | solution.py:375
  41.4 1.7 %collective-permute-start.4 = (bf16[2,32,512]{2,1,0:T(8,128)(2,1)S(1)}, bf16[2,32,512]{2,1,0:T(8,128)(2,1)S(1)}, u32[]{:S(2)}, u32[]{:S(2)}) collective-permute-start(bf16[2,32,512]{2,1,0:T(8,128)(2,1)S(1)} %get-tuple-element.58), channel_id=1, source_target_pairs={{0,2},{2,0},{4,6},{6,4},{8,10},{10,8},{12,14},{14,12},{1,3},{3,1},... | collective-permute-start | bytes 196616 | tf_op jit(solution)/shard_map/ppermute | solution.py:375
  43.0 1.8 %collective-permute-start.6 = (bf16[2,32,512]{2,1,0:T(8,128)(2,1)S(1)}, bf16[2,32,512]{2,1,0:T(8,128)(2,1)S(1)}, u32[]{:S(2)}, u32[]{:S(2)}) collective-permute-start(bf16[2,32,512]{2,1,0:T(8,128)(2,1)S(1)} %get-tuple-element.60), channel_id=1, source_target_pairs={{0,6},{2,4},{4,2},{6,0},{8,14},{10,12},{12,10},{14,8},{1,7},{3,5},... | collective-permute-start | bytes 196616 | tf_op jit(solution)/shard_map/ppermute | solution.py:375
  44.8 3.9 %collective-permute-start.7 = (bf16[2,32,512]{2,1,0:T(8,128)(2,1)S(1)}, bf16[2,32,512]{2,1,0:T(8,128)(2,1)S(1)}, u32[]{:S(2)}, u32[]{:S(2)}) collective-permute-start(bf16[2,32,512]{2,1,0:T(8,128)(2,1)S(1)} %get-tuple-element.61), channel_id=1, source_target_pairs={{0,8},{2,10},{4,12},{6,14},{8,0},{10,2},{12,4},{14,6},{1,9},{3,11}... | collective-permute-start | bytes 196616 | tf_op jit(solution)/shard_map/ppermute | solution.py:375
  48.8 7.5 %conv.3 = (bf16[2,32,512]{2,1,0:T(8,128)(2,1)S(1)}, bf16[2,32,512]{2,1,0:T(8,128)(2,1)S(1)}, bf16[2,32,512]{2,1,0:T(8,128)(2,1)S(1)}, bf16[2,32,512]{2,1,0:T(8,1...) custom-call(s32[10]{0:T(128)S(1)} %pad_add_fusion.scalars, ...), custom_call_target="tpu_custom_call" | custom-call | flops 4160749568 | bytes 9650176 | tf_op jit(solution)/shard_map/conv/pallas_call | solution.py:217
  56.3 2.0 %collective-permute-start.8 = (bf16[2,32,512]{2,1,0:T(8,128)(2,1)S(1)}, bf16[2,32,512]{2,1,0:T(8,128)(2,1)S(1)}, u32[]{:S(2)}, u32[]{:S(2)}) collective-permute-start(bf16[2,32,512]{2,1,0:T(8,128)(2,1)S(1)} %get-tuple-element.62), channel_id=1, source_target_pairs={{0,10},{2,8},{4,14},{6,12},{8,2},{10,0},{12,6},{14,4},{1,11},{3,9}... | collective-permute-start | bytes 196616 | tf_op jit(solution)/shard_map/ppermute | solution.py:375
  58.3 3.9 %collective-permute-start.9 = (bf16[2,32,512]{2,1,0:T(8,128)(2,1)S(1)}, bf16[2,32,512]{2,1,0:T(8,128)(2,1)S(1)}, u32[]{:S(2)}, u32[]{:S(2)}) collective-permute-start(bf16[2,32,512]{2,1,0:T(8,128)(2,1)S(1)} %get-tuple-element.63), channel_id=1, source_target_pairs={{0,12},{2,14},{4,8},{6,10},{8,4},{10,6},{12,0},{14,2},{1,13},{3,15... | collective-permute-start | bytes 196616 | tf_op jit(solution)/shard_map/ppermute | solution.py:375
  62.3 3.4 %collective-permute-start.13 = (bf16[2,32,512]{2,1,0:T(8,128)(2,1)S(1)}, bf16[2,32,512]{2,1,0:T(8,128)(2,1)S(1)}, u32[]{:S(2)}, u32[]{:S(2)}) collective-permute-start(bf16[2,32,512]{2,1,0:T(8,128)(2,1)S(1)} %get-tuple-element.69), channel_id=1, source_target_pairs={{0,6},{2,4},{4,2},{6,0},{8,14},{10,12},{12,10},{14,8},{1,7},{3,5},... | collective-permute-start | bytes 196616 | tf_op jit(solution)/shard_map/ppermute | solution.py:375
  66.6 1.6 %collective-permute-start.15 = (bf16[2,32,512]{2,1,0:T(8,128)(2,1)S(1)}, bf16[2,32,512]{2,1,0:T(8,128)(2,1)S(1)}, u32[]{:S(2)}, u32[]{:S(2)}) collective-permute-start(bf16[2,32,512]{2,1,0:T(8,128)(2,1)S(1)} %get-tuple-element.71), channel_id=1, source_target_pairs={{0,10},{2,8},{4,14},{6,12},{8,2},{10,0},{12,6},{14,4},{1,11},{3,9}... | collective-permute-start | bytes 196616 | tf_op jit(solution)/shard_map/ppermute | solution.py:375
  69.1 4.3 %collective-permute-start.17 = (bf16[2,32,512]{2,1,0:T(8,128)(2,1)S(1)}, bf16[2,32,512]{2,1,0:T(8,128)(2,1)S(1)}, u32[]{:S(2)}, u32[]{:S(2)}) collective-permute-start(bf16[2,32,512]{2,1,0:T(8,128)(2,1)S(1)} %get-tuple-element.73), channel_id=1, source_target_pairs={{0,14},{2,12},{4,10},{6,8},{8,6},{10,4},{12,2},{14,0},{1,15},{3,13... | collective-permute-start | bytes 196616 | tf_op jit(solution)/shard_map/ppermute | solution.py:375
  73.4 2.7 %attend.2 = (bf16[2,32,512]{2,1,0:T(8,128)(2,1)S(1)}, bf16[2,32,512]{2,1,0:T(8,128)(2,1)S(1)}, bf16[2,32,512]{2,1,0:T(8,128)(2,1)S(1)}, bf16[2,32,512]{2,1,0:T(8...) custom-call(s32[8]{0:T(128)S(1)} %broadcast_multiply_fusion.first, ...), custom_call_target="tpu_custom_call" | custom-call | flops 1342177280 | bytes 2621440 | tf_op jit(solution)/shard_map/attend/pallas_call | solution.py:304
  76.3 3.4 %collective-permute-start.27 = (bf16[2,32,512]{2,1,0:T(8,128)(2,1)S(1)}, bf16[2,32,512]{2,1,0:T(8,128)(2,1)S(1)}, u32[]{:S(2)}, u32[]{:S(2)}) collective-permute-start(bf16[2,32,512]{2,1,0:T(8,128)(2,1)S(1)} %get-tuple-element.84), channel_id=1, source_target_pairs={{0,6},{2,4},{4,2},{6,0},{8,14},{10,12},{12,10},{14,8},{1,7},{3,5},... | collective-permute-start | bytes 196616 | tf_op jit(solution)/shard_map/ppermute | solution.py:375
  82.1 2.6 %attend.3 = (bf16[2,32,512]{2,1,0:T(8,128)(2,1)S(1)}, bf16[2,32,512]{2,1,0:T(8,128)(2,1)S(1)}, bf16[2,32,512]{2,1,0:T(8,128)(2,1)S(1)}, bf16[2,32,512]{2,1,0:T(8...) custom-call(s32[8]{0:T(128)S(1)} %broadcast_multiply_fusion.first, ...), custom_call_target="tpu_custom_call" | custom-call | flops 1342177280 | bytes 2621440 | tf_op jit(solution)/shard_map/attend/pallas_call | solution.py:304
  84.8 2.6 %collective-permute-start.30 = (bf16[2,32,512]{2,1,0:T(8,128)(2,1)S(1)}, bf16[2,32,512]{2,1,0:T(8,128)(2,1)S(1)}, u32[]{:S(2)}, u32[]{:S(2)}) collective-permute-start(bf16[2,32,512]{2,1,0:T(8,128)(2,1)S(1)} %get-tuple-element.87), channel_id=1, source_target_pairs={{0,12},{2,14},{4,8},{6,10},{8,4},{10,6},{12,0},{14,2},{1,13},{3,15... | collective-permute-start | bytes 196616 | tf_op jit(solution)/shard_map/ppermute | solution.py:375
  87.3 2.7 %collective-permute-start.31 = (bf16[2,32,512]{2,1,0:T(8,128)(2,1)S(1)}, bf16[2,32,512]{2,1,0:T(8,128)(2,1)S(1)}, u32[]{:S(2)}, u32[]{:S(2)}) collective-permute-start(bf16[2,32,512]{2,1,0:T(8,128)(2,1)S(1)} %get-tuple-element.88), channel_id=1, source_target_pairs={{0,14},{2,12},{4,10},{6,8},{8,6},{10,4},{12,2},{14,0},{1,15},{3,13... | collective-permute-start | bytes 196616 | tf_op jit(solution)/shard_map/ppermute | solution.py:375
  90.1 3.4 %collective-permute-start.20 = (bf16[2,32,512]{2,1,0:T(8,128)(2,1)S(1)}, bf16[2,32,512]{2,1,0:T(8,128)(2,1)S(1)}, u32[]{:S(2)}, u32[]{:S(2)}) collective-permute-start(bf16[2,32,512]{2,1,0:T(8,128)(2,1)S(1)} %get-tuple-element.77), channel_id=1, source_target_pairs={{0,6},{2,4},{4,2},{6,0},{8,14},{10,12},{12,10},{14,8},{1,7},{3,5},... | collective-permute-start | bytes 196616 | tf_op jit(solution)/shard_map/ppermute | solution.py:375
  94.8 2.4 %collective-permute-start.22 = (bf16[2,32,512]{2,1,0:T(8,128)(2,1)S(1)}, bf16[2,32,512]{2,1,0:T(8,128)(2,1)S(1)}, u32[]{:S(2)}, u32[]{:S(2)}) collective-permute-start(bf16[2,32,512]{2,1,0:T(8,128)(2,1)S(1)} %get-tuple-element.79), channel_id=1, source_target_pairs={{0,10},{2,8},{4,14},{6,12},{8,2},{10,0},{12,6},{14,4},{1,11},{3,9}... | collective-permute-start | bytes 196616 | tf_op jit(solution)/shard_map/ppermute | solution.py:375
  98.5 3.2 %collective-permute-start.24 = (bf16[2,32,512]{2,1,0:T(8,128)(2,1)S(1)}, bf16[2,32,512]{2,1,0:T(8,128)(2,1)S(1)}, u32[]{:S(2)}, u32[]{:S(2)}) collective-permute-start(bf16[2,32,512]{2,1,0:T(8,128)(2,1)S(1)} %get-tuple-element.81), channel_id=1, source_target_pairs={{0,14},{2,12},{4,10},{6,8},{8,6},{10,4},{12,2},{14,0},{1,15},{3,13... | collective-permute-start | bytes 196616 | tf_op jit(solution)/shard_map/ppermute | solution.py:375
  103.4 2.1 %collective-permute-done.24.refs_7_ = bf16[2,32,512]{2,1,0:T(8,128)(2,1)S(1)} collective-permute-done((bf16[2,32,512]{2,1,0:T(8,128)(2,1)S(1)}, bf16[2,32,512]{2,1,0:T(8,128)(2,1)S(1)}, u32[]{:S(2)}, u32[]{:S(2)}) %collective-permute-start.24) | collective-permute-done | bytes 65568 | tf_op jit(solution)/shard_map/ppermute | solution.py:375
  105.5 1.4 %collect.3 = bf16[2,16,32,512]{3,2,1,0:T(8,128)(2,1)} custom-call(s32[8]{0:T(128)S(1)} %iota_xor_fusion.order, bf16[2,32,512]{2,1,0:T(8,128)(2,1)S(1)} %get-tuple-element.74.refs_0_, bf16[2,32,512]{2,1,0:T(8,128)(2,1)S(1)} %collective-permute-done.18.refs_1_, ...), custom_call_target="tpu_custom_call", output_to_operand_aliasing={{}: (9, {})} | custom-call | tf_op jit(solution)/shard_map/collect/pallas_call | solution.py:334
  (91 shorter events, 11.5 us)
Async XLA Ops:
  1.7 26.2 %collective-permute-start.3 = (bf16[3,17,16,512]{3,2,1,0:T(8,128)(2,1)S(1)}, bf16[3,17,16,512]{3,2,1,0:T(8,128)(2,1)}, u32[]{:S(2)}, u32[]{:S(2)}) collective-permute-start(bf16[3,17,16,512]{3,2,1,0:T(8,128)(2,1)S(1)} %pick.3), channel_id=1, source_target_pairs={{0,2},{2,4},{4,6},{6,8},{8,10},{10,12},{12,14},{1,3},{3,5},{5,7},{... | collective-permute-start | bytes 2506760 | tf_op jit(solution)/shard_map/ppermute | solution.py:390
  8.8 9.7 %collective-permute-start.2 = (bf16[4,32,512]{2,1,0:T(8,128)(2,1)}, bf16[4,32,512]{2,1,0:T(8,128)(2,1)S(1)}, u32[]{:S(2)}, u32[]{:S(2)}) collective-permute-start(bf16[4,32,512]{2,1,0:T(8,128)(2,1)} %fusion), channel_id=1, source_target_pairs={{0,1},{1,0},{2,3},{3,2},{4,5},{5,4},{6,7},{7,6},{8,9},{9,8},{10,11... | collective-permute-start | bytes 393224 | tf_op jit(solution)/shard_map/ppermute | solution.py:391
  9.7 18.1 %collective-permute-start.1 = (bf16[3,32,512]{2,1,0:T(8,128)(2,1)S(1)}, bf16[3,32,512]{2,1,0:T(8,128)(2,1)S(1)}, u32[]{:S(2)}, u32[]{:S(2)}) collective-permute-start(bf16[3,32,512]{2,1,0:T(8,128)(2,1)S(1)} %slice.21), channel_id=1, source_target_pairs={{0,3},{1,2},{2,5},{3,4},{4,7},{5,6},{6,9},{7,8},{8,11},{9,10},{10,... | collective-permute-start | bytes 294920 | tf_op jit(solution)/shard_map/ppermute | solution.py:392
  14.2 30.6 %collective-permute-start = (bf16[3,15,16,512]{3,2,1,0:T(8,128)(2,1)}, bf16[3,15,16,512]{3,2,1,0:T(8,128)(2,1)}, u32[]{:S(2)}, u32[]{:S(2)}) collective-permute-start(bf16[3,15,16,512]{3,2,1,0:T(8,128)(2,1)} %pick.2), channel_id=1, source_target_pairs={{0,2},{2,4},{4,6},{6,8},{8,10},{10,12},{12,14},{1,3},{3,5},{5,7},{... | collective-permute-start | bytes 2211848 | tf_op jit(solution)/shard_map/ppermute | solution.py:390
  37.9 18.4 %collective-permute-start.10 = (bf16[2,32,512]{2,1,0:T(8,128)(2,1)S(1)}, bf16[2,32,512]{2,1,0:T(8,128)(2,1)S(1)}, u32[]{:S(2)}, u32[]{:S(2)}) collective-permute-start(bf16[2,32,512]{2,1,0:T(8,128)(2,1)S(1)} %get-tuple-element.64), channel_id=1, source_target_pairs={{0,14},{2,12},{4,10},{6,8},{8,6},{10,4},{12,2},{14,0},{1,15},{3,13... | collective-permute-start | bytes 196616 | tf_op jit(solution)/shard_map/ppermute | solution.py:375
  41.4 16.9 %collective-permute-start.4 = (bf16[2,32,512]{2,1,0:T(8,128)(2,1)S(1)}, bf16[2,32,512]{2,1,0:T(8,128)(2,1)S(1)}, u32[]{:S(2)}, u32[]{:S(2)}) collective-permute-start(bf16[2,32,512]{2,1,0:T(8,128)(2,1)S(1)} %get-tuple-element.58), channel_id=1, source_target_pairs={{0,2},{2,0},{4,6},{6,4},{8,10},{10,8},{12,14},{14,12},{1,3},{3,1},... | collective-permute-start | bytes 196616 | tf_op jit(solution)/shard_map/ppermute | solution.py:375
  43.0 19.2 %collective-permute-start.5 = (bf16[2,32,512]{2,1,0:T(8,128)(2,1)S(1)}, bf16[2,32,512]{2,1,0:T(8,128)(2,1)S(1)}, u32[]{:S(2)}, u32[]{:S(2)}) collective-permute-start(bf16[2,32,512]{2,1,0:T(8,128)(2,1)S(1)} %get-tuple-element.59), channel_id=1, source_target_pairs={{0,4},{2,6},{4,0},{6,2},{8,12},{10,14},{12,8},{14,10},{1,5},{3,7},... | collective-permute-start | bytes 196616 | tf_op jit(solution)/shard_map/ppermute | solution.py:375
  43.0 19.3 %collective-permute-start.6 = (bf16[2,32,512]{2,1,0:T(8,128)(2,1)S(1)}, bf16[2,32,512]{2,1,0:T(8,128)(2,1)S(1)}, u32[]{:S(2)}, u32[]{:S(2)}) collective-permute-start(bf16[2,32,512]{2,1,0:T(8,128)(2,1)S(1)} %get-tuple-element.60), channel_id=1, source_target_pairs={{0,6},{2,4},{4,2},{6,0},{8,14},{10,12},{12,10},{14,8},{1,7},{3,5},... | collective-permute-start | bytes 196616 | tf_op jit(solution)/shard_map/ppermute | solution.py:375
  44.8 17.5 %collective-permute-start.7 = (bf16[2,32,512]{2,1,0:T(8,128)(2,1)S(1)}, bf16[2,32,512]{2,1,0:T(8,128)(2,1)S(1)}, u32[]{:S(2)}, u32[]{:S(2)}) collective-permute-start(bf16[2,32,512]{2,1,0:T(8,128)(2,1)S(1)} %get-tuple-element.61), channel_id=1, source_target_pairs={{0,8},{2,10},{4,12},{6,14},{8,0},{10,2},{12,4},{14,6},{1,9},{3,11}... | collective-permute-start | bytes 196616 | tf_op jit(solution)/shard_map/ppermute | solution.py:375
  56.3 9.4 %collective-permute-start.8 = (bf16[2,32,512]{2,1,0:T(8,128)(2,1)S(1)}, bf16[2,32,512]{2,1,0:T(8,128)(2,1)S(1)}, u32[]{:S(2)}, u32[]{:S(2)}) collective-permute-start(bf16[2,32,512]{2,1,0:T(8,128)(2,1)S(1)} %get-tuple-element.62), channel_id=1, source_target_pairs={{0,10},{2,8},{4,14},{6,12},{8,2},{10,0},{12,6},{14,4},{1,11},{3,9}... | collective-permute-start | bytes 196616 | tf_op jit(solution)/shard_map/ppermute | solution.py:375
  58.3 8.4 %collective-permute-start.9 = (bf16[2,32,512]{2,1,0:T(8,128)(2,1)S(1)}, bf16[2,32,512]{2,1,0:T(8,128)(2,1)S(1)}, u32[]{:S(2)}, u32[]{:S(2)}) collective-permute-start(bf16[2,32,512]{2,1,0:T(8,128)(2,1)S(1)} %get-tuple-element.63), channel_id=1, source_target_pairs={{0,12},{2,14},{4,8},{6,10},{8,4},{10,6},{12,0},{14,2},{1,13},{3,15... | collective-permute-start | bytes 196616 | tf_op jit(solution)/shard_map/ppermute | solution.py:375
  62.2 6.0 %collective-permute-start.11 = (bf16[2,32,512]{2,1,0:T(8,128)(2,1)S(1)}, bf16[2,32,512]{2,1,0:T(8,128)(2,1)S(1)}, u32[]{:S(2)}, u32[]{:S(2)}) collective-permute-start(bf16[2,32,512]{2,1,0:T(8,128)(2,1)S(1)} %get-tuple-element.67), channel_id=1, source_target_pairs={{0,2},{2,0},{4,6},{6,4},{8,10},{10,8},{12,14},{14,12},{1,3},{3,1},... | collective-permute-start | bytes 196616 | tf_op jit(solution)/shard_map/ppermute | solution.py:375
  62.3 6.7 %collective-permute-start.12 = (bf16[2,32,512]{2,1,0:T(8,128)(2,1)S(1)}, bf16[2,32,512]{2,1,0:T(8,128)(2,1)S(1)}, u32[]{:S(2)}, u32[]{:S(2)}) collective-permute-start(bf16[2,32,512]{2,1,0:T(8,128)(2,1)S(1)} %get-tuple-element.68), channel_id=1, source_target_pairs={{0,4},{2,6},{4,0},{6,2},{8,12},{10,14},{12,8},{14,10},{1,5},{3,7},... | collective-permute-start | bytes 196616 | tf_op jit(solution)/shard_map/ppermute | solution.py:375
  62.3 13.7 %collective-permute-start.13 = (bf16[2,32,512]{2,1,0:T(8,128)(2,1)S(1)}, bf16[2,32,512]{2,1,0:T(8,128)(2,1)S(1)}, u32[]{:S(2)}, u32[]{:S(2)}) collective-permute-start(bf16[2,32,512]{2,1,0:T(8,128)(2,1)S(1)} %get-tuple-element.69), channel_id=1, source_target_pairs={{0,6},{2,4},{4,2},{6,0},{8,14},{10,12},{12,10},{14,8},{1,7},{3,5},... | collective-permute-start | bytes 196616 | tf_op jit(solution)/shard_map/ppermute | solution.py:375
  65.7 10.5 %collective-permute-start.14 = (bf16[2,32,512]{2,1,0:T(8,128)(2,1)S(1)}, bf16[2,32,512]{2,1,0:T(8,128)(2,1)S(1)}, u32[]{:S(2)}, u32[]{:S(2)}) collective-permute-start(bf16[2,32,512]{2,1,0:T(8,128)(2,1)S(1)} %get-tuple-element.70), channel_id=1, source_target_pairs={{0,8},{2,10},{4,12},{6,14},{8,0},{10,2},{12,4},{14,6},{1,9},{3,11}... | collective-permute-start | bytes 196616 | tf_op jit(solution)/shard_map/ppermute | solution.py:375
  66.6 9.6 %collective-permute-start.15 = (bf16[2,32,512]{2,1,0:T(8,128)(2,1)S(1)}, bf16[2,32,512]{2,1,0:T(8,128)(2,1)S(1)}, u32[]{:S(2)}, u32[]{:S(2)}) collective-permute-start(bf16[2,32,512]{2,1,0:T(8,128)(2,1)S(1)} %get-tuple-element.71), channel_id=1, source_target_pairs={{0,10},{2,8},{4,14},{6,12},{8,2},{10,0},{12,6},{14,4},{1,11},{3,9}... | collective-permute-start | bytes 196616 | tf_op jit(solution)/shard_map/ppermute | solution.py:375
  68.2 11.4 %collective-permute-start.16 = (bf16[2,32,512]{2,1,0:T(8,128)(2,1)S(1)}, bf16[2,32,512]{2,1,0:T(8,128)(2,1)S(1)}, u32[]{:S(2)}, u32[]{:S(2)}) collective-permute-start(bf16[2,32,512]{2,1,0:T(8,128)(2,1)S(1)} %get-tuple-element.72), channel_id=1, source_target_pairs={{0,12},{2,14},{4,8},{6,10},{8,4},{10,6},{12,0},{14,2},{1,13},{3,15... | collective-permute-start | bytes 196616 | tf_op jit(solution)/shard_map/ppermute | solution.py:375
  69.1 11.7 %collective-permute-start.17 = (bf16[2,32,512]{2,1,0:T(8,128)(2,1)S(1)}, bf16[2,32,512]{2,1,0:T(8,128)(2,1)S(1)}, u32[]{:S(2)}, u32[]{:S(2)}) collective-permute-start(bf16[2,32,512]{2,1,0:T(8,128)(2,1)S(1)} %get-tuple-element.73), channel_id=1, source_target_pairs={{0,14},{2,12},{4,10},{6,8},{8,6},{10,4},{12,2},{14,0},{1,15},{3,13... | collective-permute-start | bytes 196616 | tf_op jit(solution)/shard_map/ppermute | solution.py:375
  76.1 8.7 %collective-permute-start.25 = (bf16[2,32,512]{2,1,0:T(8,128)(2,1)S(1)}, bf16[2,32,512]{2,1,0:T(8,128)(2,1)S(1)}, u32[]{:S(2)}, u32[]{:S(2)}) collective-permute-start(bf16[2,32,512]{2,1,0:T(8,128)(2,1)S(1)} %get-tuple-element.82), channel_id=1, source_target_pairs={{0,2},{2,0},{4,6},{6,4},{8,10},{10,8},{12,14},{14,12},{1,3},{3,1},... | collective-permute-start | bytes 196616 | tf_op jit(solution)/shard_map/ppermute | solution.py:375
  76.3 11.1 %collective-permute-start.26 = (bf16[2,32,512]{2,1,0:T(8,128)(2,1)S(1)}, bf16[2,32,512]{2,1,0:T(8,128)(2,1)S(1)}, u32[]{:S(2)}, u32[]{:S(2)}) collective-permute-start(bf16[2,32,512]{2,1,0:T(8,128)(2,1)S(1)} %get-tuple-element.83), channel_id=1, source_target_pairs={{0,4},{2,6},{4,0},{6,2},{8,12},{10,14},{12,8},{14,10},{1,5},{3,7},... | collective-permute-start | bytes 196616 | tf_op jit(solution)/shard_map/ppermute | solution.py:375
  76.3 13.7 %collective-permute-start.27 = (bf16[2,32,512]{2,1,0:T(8,128)(2,1)S(1)}, bf16[2,32,512]{2,1,0:T(8,128)(2,1)S(1)}, u32[]{:S(2)}, u32[]{:S(2)}) collective-permute-start(bf16[2,32,512]{2,1,0:T(8,128)(2,1)S(1)} %get-tuple-element.84), channel_id=1, source_target_pairs={{0,6},{2,4},{4,2},{6,0},{8,14},{10,12},{12,10},{14,8},{1,7},{3,5},... | collective-permute-start | bytes 196616 | tf_op jit(solution)/shard_map/ppermute | solution.py:375
  79.6 10.5 %collective-permute-start.28 = (bf16[2,32,512]{2,1,0:T(8,128)(2,1)S(1)}, bf16[2,32,512]{2,1,0:T(8,128)(2,1)S(1)}, u32[]{:S(2)}, u32[]{:S(2)}) collective-permute-start(bf16[2,32,512]{2,1,0:T(8,128)(2,1)S(1)} %get-tuple-element.85), channel_id=1, source_target_pairs={{0,8},{2,10},{4,12},{6,14},{8,0},{10,2},{12,4},{14,6},{1,9},{3,11}... | collective-permute-start | bytes 196616 | tf_op jit(solution)/shard_map/ppermute | solution.py:375
  80.8 9.4 %collective-permute-start.29 = (bf16[2,32,512]{2,1,0:T(8,128)(2,1)S(1)}, bf16[2,32,512]{2,1,0:T(8,128)(2,1)S(1)}, u32[]{:S(2)}, u32[]{:S(2)}) collective-permute-start(bf16[2,32,512]{2,1,0:T(8,128)(2,1)S(1)} %get-tuple-element.86), channel_id=1, source_target_pairs={{0,10},{2,8},{4,14},{6,12},{8,2},{10,0},{12,6},{14,4},{1,11},{3,9}... | collective-permute-start | bytes 196616 | tf_op jit(solution)/shard_map/ppermute | solution.py:375
  84.8 8.7 %collective-permute-start.30 = (bf16[2,32,512]{2,1,0:T(8,128)(2,1)S(1)}, bf16[2,32,512]{2,1,0:T(8,128)(2,1)S(1)}, u32[]{:S(2)}, u32[]{:S(2)}) collective-permute-start(bf16[2,32,512]{2,1,0:T(8,128)(2,1)S(1)} %get-tuple-element.87), channel_id=1, source_target_pairs={{0,12},{2,14},{4,8},{6,10},{8,4},{10,6},{12,0},{14,2},{1,13},{3,15... | collective-permute-start | bytes 196616 | tf_op jit(solution)/shard_map/ppermute | solution.py:375
  87.3 7.4 %collective-permute-start.31 = (bf16[2,32,512]{2,1,0:T(8,128)(2,1)S(1)}, bf16[2,32,512]{2,1,0:T(8,128)(2,1)S(1)}, u32[]{:S(2)}, u32[]{:S(2)}) collective-permute-start(bf16[2,32,512]{2,1,0:T(8,128)(2,1)S(1)} %get-tuple-element.88), channel_id=1, source_target_pairs={{0,14},{2,12},{4,10},{6,8},{8,6},{10,4},{12,2},{14,0},{1,15},{3,13... | collective-permute-start | bytes 196616 | tf_op jit(solution)/shard_map/ppermute | solution.py:375
  90.0 7.2 %collective-permute-start.18 = (bf16[2,32,512]{2,1,0:T(8,128)(2,1)S(1)}, bf16[2,32,512]{2,1,0:T(8,128)(2,1)S(1)}, u32[]{:S(2)}, u32[]{:S(2)}) collective-permute-start(bf16[2,32,512]{2,1,0:T(8,128)(2,1)S(1)} %get-tuple-element.75), channel_id=1, source_target_pairs={{0,2},{2,0},{4,6},{6,4},{8,10},{10,8},{12,14},{14,12},{1,3},{3,1},... | collective-permute-start | bytes 196616 | tf_op jit(solution)/shard_map/ppermute | solution.py:375
  90.1 8.4 %collective-permute-start.19 = (bf16[2,32,512]{2,1,0:T(8,128)(2,1)S(1)}, bf16[2,32,512]{2,1,0:T(8,128)(2,1)S(1)}, u32[]{:S(2)}, u32[]{:S(2)}) collective-permute-start(bf16[2,32,512]{2,1,0:T(8,128)(2,1)S(1)} %get-tuple-element.76), channel_id=1, source_target_pairs={{0,4},{2,6},{4,0},{6,2},{8,12},{10,14},{12,8},{14,10},{1,5},{3,7},... | collective-permute-start | bytes 196616 | tf_op jit(solution)/shard_map/ppermute | solution.py:375
  90.1 13.0 %collective-permute-start.20 = (bf16[2,32,512]{2,1,0:T(8,128)(2,1)S(1)}, bf16[2,32,512]{2,1,0:T(8,128)(2,1)S(1)}, u32[]{:S(2)}, u32[]{:S(2)}) collective-permute-start(bf16[2,32,512]{2,1,0:T(8,128)(2,1)S(1)} %get-tuple-element.77), channel_id=1, source_target_pairs={{0,6},{2,4},{4,2},{6,0},{8,14},{10,12},{12,10},{14,8},{1,7},{3,5},... | collective-permute-start | bytes 196616 | tf_op jit(solution)/shard_map/ppermute | solution.py:375
  93.5 9.7 %collective-permute-start.21 = (bf16[2,32,512]{2,1,0:T(8,128)(2,1)S(1)}, bf16[2,32,512]{2,1,0:T(8,128)(2,1)S(1)}, u32[]{:S(2)}, u32[]{:S(2)}) collective-permute-start(bf16[2,32,512]{2,1,0:T(8,128)(2,1)S(1)} %get-tuple-element.78), channel_id=1, source_target_pairs={{0,8},{2,10},{4,12},{6,14},{8,0},{10,2},{12,4},{14,6},{1,9},{3,11}... | collective-permute-start | bytes 196616 | tf_op jit(solution)/shard_map/ppermute | solution.py:375
  94.8 8.4 %collective-permute-start.22 = (bf16[2,32,512]{2,1,0:T(8,128)(2,1)S(1)}, bf16[2,32,512]{2,1,0:T(8,128)(2,1)S(1)}, u32[]{:S(2)}, u32[]{:S(2)}) collective-permute-start(bf16[2,32,512]{2,1,0:T(8,128)(2,1)S(1)} %get-tuple-element.79), channel_id=1, source_target_pairs={{0,10},{2,8},{4,14},{6,12},{8,2},{10,0},{12,6},{14,4},{1,11},{3,9}... | collective-permute-start | bytes 196616 | tf_op jit(solution)/shard_map/ppermute | solution.py:375
  97.2 6.2 %collective-permute-start.23 = (bf16[2,32,512]{2,1,0:T(8,128)(2,1)S(1)}, bf16[2,32,512]{2,1,0:T(8,128)(2,1)S(1)}, u32[]{:S(2)}, u32[]{:S(2)}) collective-permute-start(bf16[2,32,512]{2,1,0:T(8,128)(2,1)S(1)} %get-tuple-element.80), channel_id=1, source_target_pairs={{0,12},{2,14},{4,8},{6,10},{8,4},{10,6},{12,0},{14,2},{1,13},{3,15... | collective-permute-start | bytes 196616 | tf_op jit(solution)/shard_map/ppermute | solution.py:375
  98.5 7.0 %collective-permute-start.24 = (bf16[2,32,512]{2,1,0:T(8,128)(2,1)S(1)}, bf16[2,32,512]{2,1,0:T(8,128)(2,1)S(1)}, u32[]{:S(2)}, u32[]{:S(2)}) collective-permute-start(bf16[2,32,512]{2,1,0:T(8,128)(2,1)S(1)} %get-tuple-element.81), channel_id=1, source_target_pairs={{0,14},{2,12},{4,10},{6,8},{8,6},{10,4},{12,2},{14,0},{1,15},{3,13... | collective-permute-start | bytes 196616 | tf_op jit(solution)/shard_map/ppermute | solution.py:375
  (18 other events, 224.1 us)

commit v8 on v7

--- a/solution.py
+++ b/solution.py
@@ -15,7 +15,6 @@
 
 VMEM = pl.BlockSpec(memory_space=pltpu.VMEM)
 SMEM = pl.BlockSpec(memory_space=pltpu.SMEM)
-HBM = pl.BlockSpec(memory_space=pltpu.HBM)
 ANY = pl.BlockSpec(memory_space=pl.ANY)
 
 
@@ -36,33 +35,36 @@
     return pltpu.CompilerParams(vmem_limit_bytes=mebibytes * mebibyte)
 
 
-def pick_kernel(first, begin, video, out, sem):
-    count, rows = out.shape[:2]
-    copies = [
-        pltpu.make_async_copy(video.at[first + t, begin : begin + rows], out.at[t], sem.at[t])
-        for t in range(count)
-    ]
+def pick_kernel(first, spans, video, *refs):
+    outs, sem = refs[:-1], refs[-1]
+    copies = []
+    for (begin, end), out in zip(spans, outs):
+        for t in range(out.shape[0]):
+            source = video.at[first + t, begin:end]
+            copies.append(pltpu.make_async_copy(source, out.at[t], sem.at[len(copies)]))
     for copy in copies:
         copy.start()
     for copy in copies:
         copy.wait()
 
 
-def pick(video, first, begin, end):
+def pick(video, first, spans):
     frames, _, width, channels = video.shape
-    shape = (frames - first, end - begin, width, channels)
+    shapes = [(frames - first, end - begin, width, channels) for begin, end in spans]
     return pl.pallas_call(
-        partial(pick_kernel, first, begin),
-        out_shape=jax.ShapeDtypeStruct(shape, video.dtype),
-        in_specs=[HBM],
-        out_specs=VMEM,
-        scratch_shapes=[pltpu.SemaphoreType.DMA((frames - first,))],
+        partial(pick_kernel, first, spans),
+        out_shape=[jax.ShapeDtypeStruct(shape, video.dtype) for shape in shapes],
+        in_specs=[ANY],
+        out_specs=[VMEM] * len(shapes),
+        scratch_shapes=[pltpu.SemaphoreType.DMA((len(spans) * (frames - first),))],
         compiler_params=params(8),
         name="pick",
     )(video)
 
 
-def early_kernel(begin, video, edge, w_time, b_time, w_down, b_down, own, part, rows_in, lifted, sem):
+def early_kernel(
+    begin, video, edge, w_time, b_time, w_down, b_down, own, part, rows_in, lifted, sem
+):
     frames, rows, width, channels = rows_in.shape
     pixels = rows * width
     copies = [
@@ -100,7 +102,7 @@
             jax.ShapeDtypeStruct((taps - 1, pixels, channels), jnp.bfloat16),
             jax.ShapeDtypeStruct((frames // 2 - 1, pixels, channels), jnp.float32),
         ],
-        in_specs=[HBM] + [VMEM] * 5,
+        in_specs=[ANY] + [VMEM] * 5,
         out_specs=[VMEM] * 2,
         scratch_shapes=[
             pltpu.VMEM((frames, rows, width, channels), jnp.bfloat16),
@@ -114,24 +116,18 @@
 
 
 def conv_kernel(
-    owners, size, fresh, last, scalars, halo, halo_edge, own, part, w_time, b_time, w_down, b_down,
+    owners, joined, size, fresh, last, scalars, halo, halo_edge, own, part, w_time, b_time, w_down, b_down,
     w_space, b_space, *refs
 ):
     refs = list(refs)
     kept = None if fresh else refs.pop(0)
-    lifted, buffers, result, weights, sem = refs[-5:]
-    outs = refs[:owners]
-    keeps = None if last else refs[owners]
+    lifted, buffers, result = refs[-3:]
+    outs = refs[: 1 if joined else owners]
+    keeps = None if last else refs[-4]
     _, rows, width, channels = halo.shape
     halves = result.shape[0]
     pixels = rows * width
     edges = halo_edge.shape[1]
-    fetches = [
-        pltpu.make_async_copy(w_space.at[tap], weights.at[tap], sem.at[tap])
-        for tap in range(w_space.shape[0])
-    ]
-    for fetch in fetches:
-        fetch.start()
     column = scalars[1]
 
     def frame(t):
@@ -179,8 +175,6 @@
         buffers[:, :, size + 1 :] = blank
     else:
         keeps[...] = buffers[:, :, size:]
-    for fetch in fetches:
-        fetch.wait()
 
     @pl.loop(0, halves)
     def _(s):
@@ -188,13 +182,16 @@
             return buffers[b, s, a : a + size].reshape(size * width, channels)
 
         lhs = jnp.concatenate([window(b, a) for a in range(3) for b in range(3)], axis=1)
-        acc = dot32(lhs, weights[...].reshape(-1, channels)) + b_space[...]
+        acc = dot32(lhs, w_space[...].reshape(-1, channels)) + b_space[...]
         value = window(1, 1).astype(jnp.float32) + silu(acc)
         result[s] = value.astype(jnp.bfloat16)
 
     each = size * width // owners
     if owners == 1:
         outs[0][...] = result[...]
+    elif joined:
+        for j in range(owners):
+            outs[0][j] = result[:, j * each : (j + 1) * each]
     else:
         for j, out in enumerate(outs):
             begin = pl.multiple_of(scalars[2 + j] * each, each)
@@ -202,7 +199,7 @@
 
 
 def conv(
-    owners, size, kept, last, scalars, halo, halo_edge, own, part, w_time, b_time, w_down, b_down,
+    owners, joined, size, kept, last, scalars, halo, halo_edge, own, part, w_time, b_time, w_down, b_down,
     w_space, b_space
 ):
     _, rows, width, channels = halo.shape
@@ -210,21 +207,20 @@
     pixels = own.shape[1]
     fresh = kept is None
     flops = 2 * channels * channels * (pixels * (taps * taps + 4) + 9 * halves * size * width)
-    shapes = [(halves, size * width // owners, channels)] * owners
+    block = (halves, size * width // owners, channels)
+    shapes = [(owners,) + block] if joined else [block] * owners
     if not last:
         shapes.append((3, halves, 2, width, channels))
     given = [] if fresh else [kept]
     return pl.pallas_call(
-        partial(conv_kernel, owners, size, fresh, last),
+        partial(conv_kernel, owners, joined, size, fresh, last),
         out_shape=[jax.ShapeDtypeStruct(shape, jnp.bfloat16) for shape in shapes],
-        in_specs=[SMEM] + [VMEM] * 8 + [HBM] + [VMEM] * (1 + len(given)),
+        in_specs=[SMEM] + [VMEM] * 9 + [VMEM] * (1 + len(given)),
         out_specs=[VMEM] * len(shapes),
         scratch_shapes=[
             pltpu.VMEM((taps, pixels, channels), jnp.bfloat16),
             pltpu.VMEM((3, halves, size + 2, width, channels), jnp.bfloat16),
             pltpu.VMEM((halves, size * width, channels), jnp.bfloat16),
-            pltpu.VMEM(w_space.shape, jnp.bfloat16),
-            pltpu.SemaphoreType.DMA(w_space.shape[:1]),
         ],
         compiler_params=params(24),
         cost_estimate=cost(flops, halo, own, part, w_time, w_down, w_space),
@@ -235,33 +231,34 @@
     )
 
 
-def attend_kernel(frames_per, lanes, count, first, *refs):
-    blocks = refs[:count]
-    gain, w_query, w_key, w_value, w_out = refs[count : count + 5]
-    outs = refs[count + 5 :]
+def attend_kernel(frames_per, lanes, count, taken, order, *refs):
+    blocks = refs[:taken]
+    gain, w_query, w_key, w_value, w_out = refs[taken : taken + 5]
+    outs = refs[taken + 5 :]
     channels = gain.shape[-1]
     flat = len(blocks[0].shape) == 2
-    groups = 1 if flat else blocks[0].shape[1] // lanes
+    groups = 1 if flat else blocks[0].shape[-2] // lanes
     each = frames_per * lanes
     size = count * each
 
-    def piece(ref, g):
+    def piece(j, g):
         if flat:
-            return ref[...]
-        return ref[:, g * lanes : (g + 1) * lanes].reshape(each, channels)
+            return blocks[0][...]
+        part = slice(g * lanes, (g + 1) * lanes)
+        rows = blocks[j][:, part] if taken == count else blocks[0][order[j], :, part]
+        return rows.reshape(each, channels)
 
     def place(index):
         block = index // each
-        frame = index // lanes % frames_per
-        time = frame
+        time = index // lanes % frames_per
         for j in range(count):
-            time = time + jnp.where(block == j, first[j], 0)
+            time = time + jnp.where(block == j, order[j] * frames_per, 0)
         return time, index % lanes
 
     row_time, row_lane = place(lax.broadcasted_iota(jnp.int32, (size, 1), 0))
     col_time, col_lane = place(lax.broadcasted_iota(jnp.int32, (1, size), 1))
     allowed = (row_lane == col_lane) & (col_time <= row_time)
-    x = jnp.concatenate([piece(b, g) for g in range(groups) for b in blocks], axis=0)
+    x = jnp.concatenate([piece(j, g) for g in range(groups) for j in range(count)], axis=0)
     wide = x.astype(jnp.float32)
     scale = lax.rsqrt(jnp.mean(wide * wide, axis=-1, keepdims=True) + epsilon)
     normed = (wide * scale * gain[...]).astype(jnp.bfloat16)
@@ -281,45 +278,49 @@
         contexts.append(dot32(probs, value[part]).astype(jnp.bfloat16))
     mixed = dot32(jnp.concatenate(contexts, axis=0), w_out[...])
     result = (wide + mixed).astype(jnp.bfloat16)
+    if flat:
+        outs[0][...] = result
+        return
     for g in range(groups):
-        for j, out in enumerate(outs):
+        part = slice(g * lanes, (g + 1) * lanes)
+        for j in range(count):
             begin = g * size + j * each
-            rows = result[begin : begin + each]
-            if flat:
-                out[...] = rows
+            rows = result[begin : begin + each].reshape(frames_per, lanes, channels)
+            if len(outs) == count:
+                outs[j][:, part] = rows
             else:
-                out[:, g * lanes : (g + 1) * lanes] = rows.reshape(frames_per, lanes, channels)
-
-
-def attend(first, blocks, gain, w_query, w_key, w_value, w_out):
-    frames_per, pixels, channels = blocks[0].shape
-    lanes = 16 if pixels % 16 == 0 else pixels
+                outs[0][order[j], :, part] = rows
+
+
+def attend(order, joined, blocks, gain, w_query, w_key, w_value, w_out):
+    count = order.shape[0]
+    frames_per, pixels, channels = blocks[0].shape[-3:]
     flat = pixels % 16 != 0
+    lanes = pixels if flat else 16
     if flat:
         blocks = [b.reshape(frames_per * pixels, channels) for b in blocks]
-    count = len(blocks)
-    rows = frames_per * pixels * count
     size = frames_per * count * lanes
-    flops = 2 * rows * channels * (4 * channels + 2 * frames_per * count * lanes)
+    block = (frames_per, pixels, channels)
+    shapes = [blocks[0].shape] if flat else [(count,) + block] if joined else [block] * count
+    flops = 2 * frames_per * pixels * count * channels * (4 * channels + 2 * size)
     outs = pl.pallas_call(
-        partial(attend_kernel, frames_per, lanes, count),
-        out_shape=[jax.ShapeDtypeStruct(b.shape, jnp.bfloat16) for b in blocks],
-        in_specs=[SMEM] + [VMEM] * (count + 5),
-        out_specs=[VMEM] * count,
+        partial(attend_kernel, frames_per, lanes, count, len(blocks)),
+        out_shape=[jax.ShapeDtypeStruct(shape, jnp.bfloat16) for shape in shapes],
+        in_specs=[SMEM] + [VMEM] * (len(blocks) + 5),
+        out_specs=[VMEM] * len(shapes),
         compiler_params=params(20 if 16 * size * size < 20 * mebibyte else 56),
         cost_estimate=cost(flops, *blocks, w_query, w_key, w_value, w_out),
         name="attend",
-    )(first, *blocks, gain, w_query, w_key, w_value, w_out)
-    return [o.reshape(frames_per, pixels, channels) for o in outs]
-
-
-def collect_kernel(count, base, order, *refs):
-    blocks = refs[:count]
+    )(order, *blocks, gain, w_query, w_key, w_value, w_out)
+    return [o.reshape(block) for o in outs] if flat else outs
+
+
+def collect_kernel(base, joined, order, *refs):
     out, sems = refs[-2:]
-    copies = [
-        pltpu.make_async_copy(block, out.at[:, base + order[j]], sems.at[j])
-        for j, block in enumerate(blocks)
-    ]
+    copies = []
+    for j in range(sems.shape[0]):
+        block, owner = (refs[0].at[j], j) if joined else (refs[j], order[j])
+        copies.append(pltpu.make_async_copy(block, out.at[:, base + owner], sems.at[j]))
     for copy in copies:
         copy.start()
     for copy in copies:
@@ -327,16 +328,16 @@
 
 
 def collect(order, blocks, chunk, chunks, whole):
-    count = len(blocks)
-    halves, pixels, channels = blocks[0].shape
+    count = order.shape[0]
+    halves, pixels, channels = blocks[0].shape[-3:]
     shape = (halves, chunks * count, pixels, channels)
     given = [] if whole is None else [whole]
     return pl.pallas_call(
-        partial(collect_kernel, count, chunk * count),
+        partial(collect_kernel, chunk * count, len(blocks) != count),
         out_shape=jax.ShapeDtypeStruct(shape, jnp.bfloat16),
-        in_specs=[SMEM] + [ANY] * (count + len(given)),
+        in_specs=[SMEM] + [ANY] * (len(blocks) + len(given)),
         out_specs=ANY,
-        input_output_aliases={count + 1: 0} if given else {},
+        input_output_aliases={len(blocks) + 1: 0} if given else {},
         scratch_shapes=[pltpu.SemaphoreType.DMA((count,))],
         compiler_params=params(16),
         name="collect",
@@ -370,6 +371,8 @@
     owners = order.shape[0]
 
     def exchange(blocks):
+        if len(blocks) == 1:
+            return [lax.all_to_all(blocks[0], "tm", 0, 0, tiled=True)]
         result = list(blocks)
         for j in issue:
             result[j] = lax.ppermute(blocks[j], "tm", [(i, i ^ j) for i in range(devices)])
@@ -384,7 +387,7 @@
         for i in range(devices - 1)
         for c in range(columns)
     ]
-    sent = [pick(video, frames - taps, begin, end) for begin, end in spans]
+    sent = pick(video, frames - taps, spans)
     border = jnp.where(column == 0, video[:, :, -1], video[:, :, 0])
     border = after(border, sent[0])
     halos = [lax.ppermute(value, "tm", onward) for value in sent]
@@ -398,19 +401,21 @@
         early(video, edge_rows(own_edge, begin, end), begin, end, w_time, b_time, w_down, b_down)
         for begin, end in spans
     ]
-    halo_edge = after(halo_edge, [part for _, part in ahead])
+    w_space = jnp.where(after(place, own_edge) >= 0, w_space, 0)
+    halo_edge = after(halo_edge, [w_space] + [part for _, part in ahead])
     spatials, kept = [], None
     for index, (begin, end) in enumerate(spans):
         own, part = ahead[index]
         if spatials:
             own = after(own, spatials[-1][0])
         last = index == chunks - 1
+        joined = direct and index == 0 and chunks > 1
         made = conv(
-            owners, size, kept, last, scalars, halos[index], edge_rows(halo_edge, begin, end), own,
+            owners, joined, size, kept, last, scalars, halos[index], edge_rows(halo_edge, begin, end), own,
             part, w_time, b_time, w_down, b_down, w_space, b_space
         )
-        spatials.append(made[:owners])
-        kept = None if last else made[owners]
+        spatials.append(made if last else made[:-1])
+        kept = None if last else made[-1]
 
     newest = spatials[-1][0]
     if direct:
@@ -418,7 +423,8 @@
         returns = []
         for gathered in [exchange(blocks) for blocks in spatials]:
             gathered[0] = after(gathered[0], newest)
-            results = attend(order * halves, gathered, gain, w_query, w_key, w_value, w_out)
+            joined = len(returns) == chunks - 1
+            results = attend(order, joined, gathered, gain, w_query, w_key, w_value, w_out)
             newest = results[0]
             returns.append(exchange(results))
         for index, blocks in enumerate(returns):
@@ -427,7 +433,7 @@
     returns = []
     for (block,) in spatials:
         gathered = lax.all_to_all(block, "tm", 1, 0, tiled=True)
-        (result,) = attend(order, [gathered], gain, w_query, w_key, w_value, w_out)
+        (result,) = attend(order, True, [gathered], gain, w_query, w_key, w_value, w_out)
         returns.append(lax.all_to_all(result, "tm", 0, 1, tiled=True))
     return jnp.concatenate(returns, axis=1).reshape(halves, height, width, channels)
 

time: 107 us -> 121 us (1.13)
  local copies, waits for them, and re-layouts: 8.17 us -> 28.4 us
  starting transfers between devices: 62.7 us -> 49.4 us
  other arithmetic: 0.94 us -> 4.38 us
  waiting for transfers between devices: 4.99 us -> 7.4 us
    ppermute x28 -> x14, starting transfers between devices: 49.8 us -> 26.7 us  [exchange(): lax.ppermute(blocks[j], 'tm', [(i, i ^ j) for i in range(devices)])]
    unnamed x36 -> x76, local copies, waits for them, and re-layouts: 6.81 us -> 25.5 us
    all_to_all x0 -> x2, starting transfers between devices: none -> 10.1 us  [exchange(): return [lax.all_to_all(blocks[0], 'tm', 0, 0, tiled=True)]]
    ppermute x28 -> x14, waiting for transfers between devices: 3.4 us -> 7.39 us  [exchange(): lax.ppermute(blocks[j], 'tm', [(i, i ^ j) for i in range(devices)])]
    select_n x0 -> x1, other arithmetic: none -> 2.8 us  [per_device(): w_space = jnp.where(after(place, own_edge) >= 0, w_space, 0)]
    ppermute x1, waiting for transfers between devices: 1.58 us -> 0.01 us  [per_device(): halo_edge = lax.ppermute(border[frames - taps:], ('tm', 'cols'), aslant)]
    slice x1, local copies, waits for them, and re-layouts: 0.41 us -> 1.95 us  [per_device(): border = jnp.where(column == 0, video[:, :, -1], video[:, :, 0])]
    pallas_call x8 -> x7, Pallas kernels: 25.1 us -> 25.3 us  [the longest x2 13.9 us: conv(): pl.pallas_call(partial(conv_kernel, owners, joined, size, fresh, last), o...]
  transfers between devices with their start and end apart: 32 -> 20, of which waited for: 5 -> 3; matrix products, arithmetic and copies ran while one was open for 2% -> 6% of each run, Pallas kernels for 26% -> 19%
where the time goes in v8:
time: 121 us; the launch traced here: 120 us
  starting transfers between devices  49.4 us (41%)
  Pallas kernels  30 us (25%)
  local copies, waits for them, and re-layouts  28.4 us (23%)
  waiting for transfers between devices  7.4 us (6%)
  other arithmetic  4.38 us (4%)
    ppermute x14, starting transfers between devices, exchange(): lax.ppermute(blocks[j], 'tm', [(i, i ^ j) for i in range(devices)])  26.7 us
    unnamed x76, local copies, waits for them, and re-layouts  25.5 us
    pallas_call x2, Pallas kernels, conv(): pl.pallas_call(partial(conv_kernel, owners, joined, size, fresh, last), o...  13.9 us
    all_to_all x2, starting transfers between devices, exchange(): return [lax.all_to_all(blocks[0], 'tm', 0, 0, tiled=True)]  10.1 us
    ppermute x2, starting transfers between devices, per_device(): halos = [lax.ppermute(value, 'tm', onward) for value in sent]  9.21 us
    ppermute x14, waiting for transfers between devices, exchange(): lax.ppermute(blocks[j], 'tm', [(i, i ^ j) for i in range(devices)])  7.39 us
    pallas_call x2, Pallas kernels, attend(): pl.pallas_call(partial(attend_kernel, frames_per, lanes, count, len(block...  6.63 us
    pallas_call x2, Pallas kernels, early(): pl.pallas_call(partial(early_kernel, begin), out_shape=[jax.ShapeDtypeStr...  4.66 us
  transfers between devices with their start and end apart: 20, of which 3 were waited for; matrix products, arithmetic and copies ran while one was open for 6% of the time, Pallas kernels for 19%

profile of v8, /device:TPU:0, one launch (start us, length us, event | category | flops | bytes accessed | tf_op | source)
XLA Modules:
  0.0 120.1 jit_solution(13791701617612017016)
XLA Ops:
  0.0 1.6 %copy-done = bf16[4,32,16,512]{3,2,1,0:T(8,128)(2,1)S(1)} copy-done((bf16[4,32,16,512]{3,2,1,0:T(8,128)(2,1)S(1)}, bf16[4,32,16,512]{3,2,1,0:T(8,128)(2,1)}, u32[]{:S(2)}) %copy-start) | copy-done | bytes 2097176
  1.6 2.0 %pick.1 = (bf16[3,17,16,512]{3,2,1,0:T(8,128)(2,1)}, bf16[3,15,16,512]{3,2,1,0:T(8,128)(2,1)S(1)}) custom-call(bf16[4,32,16,512]{3,2,1,0:T(8,128)(2,1)S(1)} %copy-done), custom_call_target="tpu_custom_call" | custom-call | tf_op jit(solution)/shard_map/pick/pallas_call | solution.py:54
  4.5 4.9 %collective-permute-start.3 = (bf16[3,17,16,512]{3,2,1,0:T(8,128)(2,1)}, bf16[3,17,16,512]{3,2,1,0:T(8,128)(2,1)S(1)}, u32[]{:S(2)}, u32[]{:S(2)}) collective-permute-start(bf16[3,17,16,512]{3,2,1,0:T(8,128)(2,1)} %get-tuple-element.36), channel_id=1, source_target_pairs={{0,2},{2,4},{4,6},{6,8},{8,10},{10,12},{12,14},{1,3},{3,5},{5,7},{... | collective-permute-start | bytes 2506760 | tf_op jit(solution)/shard_map/ppermute | solution.py:393
  9.4 2.0 %fusion.1 = (bf16[4,32,1,512]{3,2,1,0:T(2,128)(2,1)S(1)}, bf16[4,32,1,512]{3,2,1,0:T(2,128)(2,1)S(1)}) fusion(bf16[4,32,16,512]{3,2,1,0:T(8,128)(2,1)} %video.5), kind=kLoop, calls=%fused_computation.7 | loop fusion | bytes 524288 | tf_op jit(solution)/shard_map/slice | solution.py:391
  13.0 3.5 %collective-permute-start.1 = (bf16[3,32,512]{2,1,0:T(8,128)(2,1)S(1)}, bf16[3,32,512]{2,1,0:T(8,128)(2,1)S(1)}, u32[]{:S(2)}, u32[]{:S(2)}) collective-permute-start(bf16[3,32,512]{2,1,0:T(8,128)(2,1)S(1)} %slice.21), channel_id=1, source_target_pairs={{0,3},{1,2},{2,5},{3,4},{4,7},{5,6},{6,9},{7,8},{8,11},{9,10},{10,... | collective-permute-start | bytes 294920 | tf_op jit(solution)/shard_map/ppermute | solution.py:395
  16.5 4.3 %collective-permute-start = (bf16[3,15,16,512]{3,2,1,0:T(8,128)(2,1)}, bf16[3,15,16,512]{3,2,1,0:T(8,128)(2,1)}, u32[]{:S(2)}, u32[]{:S(2)}) collective-permute-start(bf16[3,15,16,512]{3,2,1,0:T(8,128)(2,1)} %copy-done.17), channel_id=1, source_target_pairs={{0,2},{2,4},{4,6},{6,8},{8,10},{10,12},{12,14},{1,3},{3,5},{5,7},{... | collective-permute-start | bytes 2211848 | tf_op jit(solution)/shard_map/ppermute | solution.py:393
  21.6 1.4 %copy-done.2 = bf16[3,512,512]{2,1,0:T(8,128)(2,1)S(1)} copy-done((bf16[3,512,512]{2,1,0:T(8,128)(2,1)S(1)}, bf16[3,512,512]{2,1,0:T(8,128)(2,1)}, u32[]{:S(2)}) %copy-start.2) | copy-done | bytes 1572888
  23.0 1.4 %copy-done.5 = bf16[3,512,512]{2,1,0:T(8,128)(2,1)S(1)} copy-done((bf16[3,512,512]{2,1,0:T(8,128)(2,1)S(1)}, bf16[3,512,512]{2,1,0:T(8,128)(2,1)}, u32[]{:S(2)}) %copy-start.5) | copy-done | bytes 1572888
  25.8 1.9 %early.2 = (bf16[2,304,512]{2,1,0:T(8,128)(2,1)S(1)}, f32[1,304,512]{2,1,0:T(8,128)S(1)}) custom-call(bf16[4,32,16,512]{3,2,1,0:T(8,128)(2,1)S(1)} %copy-done.1, bf16[4,32,512]{2,1,0:T(8,128)(2,1)S(1)} %broadcast_select_fusion.1.edge, bf16[1536,512]{1,0:T(8,128)(2,1)S(1)} %bitcast.11, f32[1,512]{1,0:T(1,128)S(1)} %bitcast.19, ...), custom_call_target="tpu_custom_call" | custom-call | flops 1275068416 | bytes 3145728 | tf_op jit(solution)/shard_map/early/pallas_call | solution.py:99
  29.5 2.8 %broadcast_select_fusion.w_space = bf16[9,512,512]{2,1,0:T(8,128)(2,1)S(1)} fusion(bf16[9,512,512]{2,1,0:T(8,128)(2,1)} %param.17, pred[]{:T(512)S(6)} %ge.3), kind=kLoop, calls=%fused_computation | loop fusion | flops 2359296 | bytes 9437185 | tf_op jit(solution)/shard_map/jit(_where)/select_n | solution.py:404
  32.8 2.8 %early.3 = (bf16[2,256,512]{2,1,0:T(8,128)(2,1)S(1)}, f32[1,256,512]{2,1,0:T(8,128)S(1)}) custom-call(bf16[4,32,16,512]{3,2,1,0:T(8,128)(2,1)S(1)} %copy-done.1, bf16[4,16,512]{2,1,0:T(8,128)(2,1)S(1)} %pad.17.edge, bf16[1536,512]{1,0:T(8,128)(2,1)S(1)} %bitcast.12, f32[1,512]{1,0:T(1,128)S(1)} %bitcast.20, bf16[1536,512]{1,0:T(8,128)(2,1)S(1)} %bitcast.16, ...), custom_call_target="tpu_custom_call" | custom-call | flops 1073741824 | bytes 3145728 | tf_op jit(solution)/shard_map/early/pallas_call | solution.py:99
  39.4 6.5 %conv.2 = (bf16[8,2,32,512]{3,2,1,0:T(8,128)(2,1)S(1)}, bf16[3,2,2,16,512]{4,3,2,1,0:T(8,128)(2,1)S(1)}) custom-call(s32[10]{0:T(128)S(1)} %pad_add_fusion.scalars, bf16[3,17,16,512]{3,2,1,0:T(8,128)(2,1)S(1)} %copy-done.16, bf16[3,32,512]{2,1,0:T(8,128)(2,1)S(1)} %broadcast_select_fusion.2.halo_edge, bf16[2,304,512]{2,1,0:T(8,128)(2,1)S(1)} %copy-done.19, ...), custom_call_target="tpu_custom_call" | custom-call | flops 4487905280 | bytes 9945088 | tf_op jit(solution)/shard_map/conv/pallas_call | solution.py:215
  47.4 4.3 %all-to-all-start = ((bf16[8,2,32,512]{3,2,1,0:T(8,128)(2,1)}), bf16[8,2,32,512]{3,2,1,0:T(8,128)(2,1)}, u32[]{:S(2)}, u32[]{:S(2)}) async-start(bf16[8,2,32,512]{3,2,1,0:T(8,128)(2,1)} %copy-done.10), calls=%async_computation | async-start | bytes 1048576 | tf_op jit(solution)/shard_map/all_to_all | solution.py:375
  51.8 2.3 %copy-done.9 = bf16[9,512,512]{2,1,0:T(8,128)(2,1)S(1)} copy-done((bf16[9,512,512]{2,1,0:T(8,128)(2,1)S(1)}, bf16[9,512,512]{2,1,0:T(8,128)(2,1)}, u32[]{:S(2)}) %copy-start.9) | copy-done | bytes 4718616
  57.9 7.4 %conv.3 = (bf16[2,32,512]{2,1,0:T(8,128)(2,1)S(1)}, bf16[2,32,512]{2,1,0:T(8,128)(2,1)}, bf16[2,32,512]{2,1,0:T(8,128)(2,1)S(1)}, bf16[2,32,512]{2,1,0:T(8,128)(...) custom-call(s32[10]{0:T(128)S(1)} %pad_add_fusion.scalars, ...), custom_call_target="tpu_custom_call" | custom-call | flops 4160749568 | bytes 9650176 | tf_op jit(solution)/shard_map/conv/pallas_call | solution.py:215
  65.8 1.7 %collective-permute-start.4 = (bf16[2,32,512]{2,1,0:T(8,128)(2,1)}, bf16[2,32,512]{2,1,0:T(8,128)(2,1)S(1)}, u32[]{:S(2)}, u32[]{:S(2)}) collective-permute-start(bf16[2,32,512]{2,1,0:T(8,128)(2,1)} %get-tuple-element.51), channel_id=1, source_target_pairs={{0,2},{2,0},{4,6},{6,4},{8,10},{10,8},{12,14},{14,12},{1,3},{3,1},... | collective-permute-start | bytes 196616 | tf_op jit(solution)/shard_map/ppermute | solution.py:378
  67.5 1.5 %collective-permute-start.5 = (bf16[2,32,512]{2,1,0:T(8,128)(2,1)S(1)}, bf16[2,32,512]{2,1,0:T(8,128)(2,1)S(1)}, u32[]{:S(2)}, u32[]{:S(2)}) collective-permute-start(bf16[2,32,512]{2,1,0:T(8,128)(2,1)S(1)} %get-tuple-element.52), channel_id=1, source_target_pairs={{0,4},{2,6},{4,0},{6,2},{8,12},{10,14},{12,8},{14,10},{1,5},{3,7},... | collective-permute-start | bytes 196616 | tf_op jit(solution)/shard_map/ppermute | solution.py:378
  69.3 2.6 %collective-permute-start.7 = (bf16[2,32,512]{2,1,0:T(8,128)(2,1)S(1)}, bf16[2,32,512]{2,1,0:T(8,128)(2,1)S(1)}, u32[]{:S(2)}, u32[]{:S(2)}) collective-permute-start(bf16[2,32,512]{2,1,0:T(8,128)(2,1)S(1)} %get-tuple-element.54), channel_id=1, source_target_pairs={{0,8},{2,10},{4,12},{6,14},{8,0},{10,2},{12,4},{14,6},{1,9},{3,11}... | collective-permute-start | bytes 196616 | tf_op jit(solution)/shard_map/ppermute | solution.py:378
  72.0 1.4 %collective-permute-start.8 = (bf16[2,32,512]{2,1,0:T(8,128)(2,1)S(1)}, bf16[2,32,512]{2,1,0:T(8,128)(2,1)S(1)}, u32[]{:S(2)}, u32[]{:S(2)}) collective-permute-start(bf16[2,32,512]{2,1,0:T(8,128)(2,1)S(1)} %get-tuple-element.55), channel_id=1, source_target_pairs={{0,10},{2,8},{4,14},{6,12},{8,2},{10,0},{12,6},{14,4},{1,11},{3,9}... | collective-permute-start | bytes 196616 | tf_op jit(solution)/shard_map/ppermute | solution.py:378
  73.4 3.3 %collective-permute-start.9 = (bf16[2,32,512]{2,1,0:T(8,128)(2,1)S(1)}, bf16[2,32,512]{2,1,0:T(8,128)(2,1)S(1)}, u32[]{:S(2)}, u32[]{:S(2)}) collective-permute-start(bf16[2,32,512]{2,1,0:T(8,128)(2,1)S(1)} %get-tuple-element.56), channel_id=1, source_target_pairs={{0,12},{2,14},{4,8},{6,10},{8,4},{10,6},{12,0},{14,2},{1,13},{3,15... | collective-permute-start | bytes 196616 | tf_op jit(solution)/shard_map/ppermute | solution.py:378
  81.8 3.2 %attend.2 = (bf16[2,32,512]{2,1,0:T(8,128)(2,1)S(1)}, bf16[2,32,512]{2,1,0:T(8,128)(2,1)S(1)}, bf16[2,32,512]{2,1,0:T(8,128)(2,1)S(1)}, bf16[2,32,512]{2,1,0:T(8...) custom-call(s32[8]{0:T(128)S(1)} %iota_xor_fusion.order, ...), custom_call_target="tpu_custom_call" | custom-call | flops 1342177280 | bytes 2621440 | tf_op jit(solution)/shard_map/attend/pallas_call | solution.py:306
  85.1 3.4 %attend.3 = bf16[8,2,32,512]{3,2,1,0:T(8,128)(2,1)} custom-call(s32[8]{0:T(128)S(1)} %iota_xor_fusion.order, bf16[2,32,512]{2,1,0:T(8,128)(2,1)S(1)} %copy-done.34, bf16[2,32,512]{2,1,0:T(8,128)(2,1)S(1)} %collective-permute-done.4.refs_1_, bf16[2,32,512]{2,1,0:T(8,128)(2,1)S(1)} %collective-permute-done.5.refs_2_, ...), custom_call_target="tpu_custom_call" | custom-call | flops 1342177280 | bytes 2621440 | tf_op jit(solution)/shard_map/attend/pallas_call | solution.py:306
  88.5 5.7 %all-to-all-start.1 = ((bf16[8,2,32,512]{3,2,1,0:T(8,128)(2,1)}), bf16[8,2,32,512]{3,2,1,0:T(8,128)(2,1)S(1)}, u32[]{:S(2)}, u32[]{:S(2)}) async-start(bf16[8,2,32,512]{3,2,1,0:T(8,128)(2,1)} %attend.3), calls=%async_computation.1 | async-start | bytes 1048576 | tf_op jit(solution)/shard_map/all_to_all | solution.py:375
  94.3 2.0 %collective-permute-start.11 = (bf16[2,32,512]{2,1,0:T(8,128)(2,1)S(1)}, bf16[2,32,512]{2,1,0:T(8,128)(2,1)S(1)}, u32[]{:S(2)}, u32[]{:S(2)}) collective-permute-start(bf16[2,32,512]{2,1,0:T(8,128)(2,1)S(1)} %get-tuple-element.58), channel_id=1, source_target_pairs={{0,2},{2,0},{4,6},{6,4},{8,10},{10,8},{12,14},{14,12},{1,3},{3,1},... | collective-permute-start | bytes 196616 | tf_op jit(solution)/shard_map/ppermute | solution.py:378
  96.3 1.5 %collective-permute-start.12 = (bf16[2,32,512]{2,1,0:T(8,128)(2,1)S(1)}, bf16[2,32,512]{2,1,0:T(8,128)(2,1)S(1)}, u32[]{:S(2)}, u32[]{:S(2)}) collective-permute-start(bf16[2,32,512]{2,1,0:T(8,128)(2,1)S(1)} %get-tuple-element.59), channel_id=1, source_target_pairs={{0,4},{2,6},{4,0},{6,2},{8,12},{10,14},{12,8},{14,10},{1,5},{3,7},... | collective-permute-start | bytes 196616 | tf_op jit(solution)/shard_map/ppermute | solution.py:378
  97.8 2.9 %collective-permute-start.14 = (bf16[2,32,512]{2,1,0:T(8,128)(2,1)S(1)}, bf16[2,32,512]{2,1,0:T(8,128)(2,1)S(1)}, u32[]{:S(2)}, u32[]{:S(2)}) collective-permute-start(bf16[2,32,512]{2,1,0:T(8,128)(2,1)S(1)} %get-tuple-element.61), channel_id=1, source_target_pairs={{0,8},{2,10},{4,12},{6,14},{8,0},{10,2},{12,4},{14,6},{1,9},{3,11}... | collective-permute-start | bytes 196616 | tf_op jit(solution)/shard_map/ppermute | solution.py:378
  100.7 1.5 %collective-permute-start.15 = (bf16[2,32,512]{2,1,0:T(8,128)(2,1)S(1)}, bf16[2,32,512]{2,1,0:T(8,128)(2,1)S(1)}, u32[]{:S(2)}, u32[]{:S(2)}) collective-permute-start(bf16[2,32,512]{2,1,0:T(8,128)(2,1)S(1)} %get-tuple-element.62), channel_id=1, source_target_pairs={{0,10},{2,8},{4,14},{6,12},{8,2},{10,0},{12,6},{14,4},{1,11},{3,9}... | collective-permute-start | bytes 196616 | tf_op jit(solution)/shard_map/ppermute | solution.py:378
  102.1 3.3 %collective-permute-start.16 = (bf16[2,32,512]{2,1,0:T(8,128)(2,1)S(1)}, bf16[2,32,512]{2,1,0:T(8,128)(2,1)S(1)}, u32[]{:S(2)}, u32[]{:S(2)}) collective-permute-start(bf16[2,32,512]{2,1,0:T(8,128)(2,1)S(1)} %get-tuple-element.63), channel_id=1, source_target_pairs={{0,12},{2,14},{4,8},{6,10},{8,4},{10,6},{12,0},{14,2},{1,13},{3,15... | collective-permute-start | bytes 196616 | tf_op jit(solution)/shard_map/ppermute | solution.py:378
  105.5 4.4 %collective-permute-start.17 = (bf16[2,32,512]{2,1,0:T(8,128)(2,1)S(1)}, bf16[2,32,512]{2,1,0:T(8,128)(2,1)S(1)}, u32[]{:S(2)}, u32[]{:S(2)}) collective-permute-start(bf16[2,32,512]{2,1,0:T(8,128)(2,1)S(1)} %get-tuple-element.64), channel_id=1, source_target_pairs={{0,14},{2,12},{4,10},{6,8},{8,6},{10,4},{12,2},{14,0},{1,15},{3,13... | collective-permute-start | bytes 196616 | tf_op jit(solution)/shard_map/ppermute | solution.py:378
  109.9 5.7 %collective-permute-done.14.refs_4_ = bf16[2,32,512]{2,1,0:T(8,128)(2,1)S(1)} collective-permute-done((bf16[2,32,512]{2,1,0:T(8,128)(2,1)S(1)}, bf16[2,32,512]{2,1,0:T(8,128)(2,1)S(1)}, u32[]{:S(2)}, u32[]{:S(2)}) %collective-permute-start.14) | collective-permute-done | bytes 65568 | tf_op jit(solution)/shard_map/ppermute | solution.py:378
  115.6 1.6 %collective-permute-done.15.refs_5_ = bf16[2,32,512]{2,1,0:T(8,128)(2,1)S(1)} collective-permute-done((bf16[2,32,512]{2,1,0:T(8,128)(2,1)S(1)}, bf16[2,32,512]{2,1,0:T(8,128)(2,1)S(1)}, u32[]{:S(2)}, u32[]{:S(2)}) %collective-permute-start.15) | collective-permute-done | bytes 65568 | tf_op jit(solution)/shard_map/ppermute | solution.py:378
  117.2 1.4 %collect.2.refs_1_ = bf16[2,16,32,512]{3,2,1,0:T(8,128)(2,1)} custom-call(s32[8]{0:T(128)S(1)} %iota_xor_fusion.order, bf16[2,32,512]{2,1,0:T(8,128)(2,1)S(1)} %get-tuple-element.49.refs_0_, bf16[2,32,512]{2,1,0:T(8,128)(2,1)S(1)} %collective-permute-done.11.refs_1_, bf16[2,32,512]{2,1,0:T(8,128)(2,1)S(1)} %collective-permute-done.12.refs_2_, ...), custom_call_target="tpu_custom_call" | custom-call | tf_op jit(solution)/shard_map/collect/pallas_call | solution.py:335
  (105 shorter events, 23.5 us)
Async XLA Ops:
  1.6 20.0 %copy-start.1 = (bf16[4,32,16,512]{3,2,1,0:T(8,128)(2,1)S(1)}, bf16[4,32,16,512]{3,2,1,0:T(8,128)(2,1)}, u32[]{:S(2)}) copy-start(bf16[4,32,16,512]{3,2,1,0:T(8,128)(2,1)} %video.5) | copy-start | bytes 6291460
  4.5 32.8 %collective-permute-start.3 = (bf16[3,17,16,512]{3,2,1,0:T(8,128)(2,1)}, bf16[3,17,16,512]{3,2,1,0:T(8,128)(2,1)S(1)}, u32[]{:S(2)}, u32[]{:S(2)}) collective-permute-start(bf16[3,17,16,512]{3,2,1,0:T(8,128)(2,1)} %get-tuple-element.36), channel_id=1, source_target_pairs={{0,2},{2,4},{4,6},{6,8},{8,10},{10,12},{12,14},{1,3},{3,5},{5,7},{... | collective-permute-start | bytes 2506760 | tf_op jit(solution)/shard_map/ppermute | solution.py:393
  12.1 8.8 %collective-permute-start.2 = (bf16[4,32,512]{2,1,0:T(8,128)(2,1)}, bf16[4,32,512]{2,1,0:T(8,128)(2,1)S(1)}, u32[]{:S(2)}, u32[]{:S(2)}) collective-permute-start(bf16[4,32,512]{2,1,0:T(8,128)(2,1)} %fusion), channel_id=1, source_target_pairs={{0,1},{1,0},{2,3},{3,2},{4,5},{5,4},{6,7},{7,6},{8,9},{9,8},{10,11... | collective-permute-start | bytes 393224 | tf_op jit(solution)/shard_map/ppermute | solution.py:394
  13.0 24.3 %collective-permute-start.1 = (bf16[3,32,512]{2,1,0:T(8,128)(2,1)S(1)}, bf16[3,32,512]{2,1,0:T(8,128)(2,1)S(1)}, u32[]{:S(2)}, u32[]{:S(2)}) collective-permute-start(bf16[3,32,512]{2,1,0:T(8,128)(2,1)S(1)} %slice.21), channel_id=1, source_target_pairs={{0,3},{1,2},{2,5},{3,4},{4,7},{5,6},{6,9},{7,8},{8,11},{9,10},{10,... | collective-permute-start | bytes 294920 | tf_op jit(solution)/shard_map/ppermute | solution.py:395
  16.5 35.3 %collective-permute-start = (bf16[3,15,16,512]{3,2,1,0:T(8,128)(2,1)}, bf16[3,15,16,512]{3,2,1,0:T(8,128)(2,1)}, u32[]{:S(2)}, u32[]{:S(2)}) collective-permute-start(bf16[3,15,16,512]{3,2,1,0:T(8,128)(2,1)} %copy-done.17), channel_id=1, source_target_pairs={{0,2},{2,4},{4,6},{6,8},{8,10},{10,12},{12,14},{1,3},{3,5},{5,7},{... | collective-permute-start | bytes 2211848 | tf_op jit(solution)/shard_map/ppermute | solution.py:393
  29.4 3.3 %copy-start.6 = (bf16[3,512,512]{2,1,0:T(8,128)(2,1)S(1)}, bf16[3,512,512]{2,1,0:T(8,128)(2,1)}, u32[]{:S(2)}) copy-start(bf16[3,512,512]{2,1,0:T(8,128)(2,1)} %param.15) | copy-start | bytes 4718596
  29.4 3.3 %copy-start.12 = (f32[512]{0:T(512)S(1)}, f32[512]{0:T(512)}, u32[]{:S(2)}) copy-start(f32[512]{0:T(512)} %param.14) | copy-start | bytes 6148
  29.4 3.3 %copy-start.14 = (f32[512]{0:T(512)S(1)}, f32[512]{0:T(512)}, u32[]{:S(2)}) copy-start(f32[512]{0:T(512)} %param.16) | copy-start | bytes 6148
  32.7 13.2 %copy-start.8 = (bf16[9,512,512]{2,1,0:T(8,128)(2,1)}, bf16[9,512,512]{2,1,0:T(8,128)(2,1)S(1)}, u32[]{:S(2)}) copy-start(bf16[9,512,512]{2,1,0:T(8,128)(2,1)S(1)} %broadcast_select_fusion.w_space) | copy-start | bytes 14155780
  32.7 4.5 %copy-start.37 = (pred[32]{0:T(512)(128)(4,1)S(1)}, pred[32]{0:T(512)(128)(4,1)}, u32[]{:S(2)}) copy-start(pred[32]{0:T(512)(128)(4,1)} %constant.14.clone.1) | copy-start | bytes 100
  32.7 5.5 %copy-start.19 = (bf16[2,304,512]{2,1,0:T(8,128)(2,1)S(1)}, bf16[2,304,512]{2,1,0:T(8,128)(2,1)}, u32[]{:S(2)}) copy-start(bf16[2,304,512]{2,1,0:T(8,128)(2,1)} %copy-done.18) | copy-start | bytes 1867780
  32.7 5.5 %copy-start.21 = (f32[1,304,512]{2,1,0:T(8,128)S(1)}, f32[1,304,512]{2,1,0:T(8,128)}, u32[]{:S(2)}) copy-start(f32[1,304,512]{2,1,0:T(8,128)} %copy-done.20) | copy-start | bytes 1867780
  32.8 5.5 %copy-start.30 = (f32[512]{0:T(512)S(1)}, f32[512]{0:T(512)}, u32[]{:S(2)}) copy-start(f32[512]{0:T(512)} %param.18) | copy-start | bytes 6148
  39.4 12.4 %copy-start.4 = (bf16[3,512,512]{2,1,0:T(8,128)(2,1)S(1)}, bf16[3,512,512]{2,1,0:T(8,128)(2,1)}, u32[]{:S(2)}) copy-start(bf16[3,512,512]{2,1,0:T(8,128)(2,1)} %param.13) | copy-start | bytes 4718596
  39.4 12.4 %copy-start.7 = (bf16[3,512,512]{2,1,0:T(8,128)(2,1)S(1)}, bf16[3,512,512]{2,1,0:T(8,128)(2,1)}, u32[]{:S(2)}) copy-start(bf16[3,512,512]{2,1,0:T(8,128)(2,1)} %param.15) | copy-start | bytes 4718596
  47.4 26.0 %all-to-all-start = ((bf16[8,2,32,512]{3,2,1,0:T(8,128)(2,1)}), bf16[8,2,32,512]{3,2,1,0:T(8,128)(2,1)}, u32[]{:S(2)}, u32[]{:S(2)}) async-start(bf16[8,2,32,512]{3,2,1,0:T(8,128)(2,1)} %copy-done.10), calls=%async_computation | async-start | bytes 1048576 | tf_op jit(solution)/shard_map/all_to_all | solution.py:375
  65.8 7.6 %collective-permute-start.4 = (bf16[2,32,512]{2,1,0:T(8,128)(2,1)}, bf16[2,32,512]{2,1,0:T(8,128)(2,1)S(1)}, u32[]{:S(2)}, u32[]{:S(2)}) collective-permute-start(bf16[2,32,512]{2,1,0:T(8,128)(2,1)} %get-tuple-element.51), channel_id=1, source_target_pairs={{0,2},{2,0},{4,6},{6,4},{8,10},{10,8},{12,14},{14,12},{1,3},{3,1},... | collective-permute-start | bytes 196616 | tf_op jit(solution)/shard_map/ppermute | solution.py:378
  67.5 9.2 %collective-permute-start.5 = (bf16[2,32,512]{2,1,0:T(8,128)(2,1)S(1)}, bf16[2,32,512]{2,1,0:T(8,128)(2,1)S(1)}, u32[]{:S(2)}, u32[]{:S(2)}) collective-permute-start(bf16[2,32,512]{2,1,0:T(8,128)(2,1)S(1)} %get-tuple-element.52), channel_id=1, source_target_pairs={{0,4},{2,6},{4,0},{6,2},{8,12},{10,14},{12,8},{14,10},{1,5},{3,7},... | collective-permute-start | bytes 196616 | tf_op jit(solution)/shard_map/ppermute | solution.py:378
  69.0 16.0 %collective-permute-start.6 = (bf16[2,32,512]{2,1,0:T(8,128)(2,1)S(1)}, bf16[2,32,512]{2,1,0:T(8,128)(2,1)S(1)}, u32[]{:S(2)}, u32[]{:S(2)}) collective-permute-start(bf16[2,32,512]{2,1,0:T(8,128)(2,1)S(1)} %get-tuple-element.53), channel_id=1, source_target_pairs={{0,6},{2,4},{4,2},{6,0},{8,14},{10,12},{12,10},{14,8},{1,7},{3,5},... | collective-permute-start | bytes 196616 | tf_op jit(solution)/shard_map/ppermute | solution.py:378
  69.3 15.7 %collective-permute-start.7 = (bf16[2,32,512]{2,1,0:T(8,128)(2,1)S(1)}, bf16[2,32,512]{2,1,0:T(8,128)(2,1)S(1)}, u32[]{:S(2)}, u32[]{:S(2)}) collective-permute-start(bf16[2,32,512]{2,1,0:T(8,128)(2,1)S(1)} %get-tuple-element.54), channel_id=1, source_target_pairs={{0,8},{2,10},{4,12},{6,14},{8,0},{10,2},{12,4},{14,6},{1,9},{3,11}... | collective-permute-start | bytes 196616 | tf_op jit(solution)/shard_map/ppermute | solution.py:378
  72.0 13.1 %collective-permute-start.8 = (bf16[2,32,512]{2,1,0:T(8,128)(2,1)S(1)}, bf16[2,32,512]{2,1,0:T(8,128)(2,1)S(1)}, u32[]{:S(2)}, u32[]{:S(2)}) collective-permute-start(bf16[2,32,512]{2,1,0:T(8,128)(2,1)S(1)} %get-tuple-element.55), channel_id=1, source_target_pairs={{0,10},{2,8},{4,14},{6,12},{8,2},{10,0},{12,6},{14,4},{1,11},{3,9}... | collective-permute-start | bytes 196616 | tf_op jit(solution)/shard_map/ppermute | solution.py:378
  73.4 11.7 %collective-permute-start.9 = (bf16[2,32,512]{2,1,0:T(8,128)(2,1)S(1)}, bf16[2,32,512]{2,1,0:T(8,128)(2,1)S(1)}, u32[]{:S(2)}, u32[]{:S(2)}) collective-permute-start(bf16[2,32,512]{2,1,0:T(8,128)(2,1)S(1)} %get-tuple-element.56), channel_id=1, source_target_pairs={{0,12},{2,14},{4,8},{6,10},{8,4},{10,6},{12,0},{14,2},{1,13},{3,15... | collective-permute-start | bytes 196616 | tf_op jit(solution)/shard_map/ppermute | solution.py:378
  76.7 8.4 %collective-permute-start.10 = (bf16[2,32,512]{2,1,0:T(8,128)(2,1)S(1)}, bf16[2,32,512]{2,1,0:T(8,128)(2,1)S(1)}, u32[]{:S(2)}, u32[]{:S(2)}) collective-permute-start(bf16[2,32,512]{2,1,0:T(8,128)(2,1)S(1)} %get-tuple-element.57), channel_id=1, source_target_pairs={{0,14},{2,12},{4,10},{6,8},{8,6},{10,4},{12,2},{14,0},{1,15},{3,13... | collective-permute-start | bytes 196616 | tf_op jit(solution)/shard_map/ppermute | solution.py:378
  81.8 3.2 %copy-start.34 = (bf16[2,32,512]{2,1,0:T(8,128)(2,1)S(1)}, bf16[2,32,512]{2,1,0:T(8,128)(2,1)}, u32[]{:S(2)}) copy-start(bf16[2,32,512]{2,1,0:T(8,128)(2,1)} %copy-done.33) | copy-start | bytes 196612
  88.5 30.0 %all-to-all-start.1 = ((bf16[8,2,32,512]{3,2,1,0:T(8,128)(2,1)}), bf16[8,2,32,512]{3,2,1,0:T(8,128)(2,1)S(1)}, u32[]{:S(2)}, u32[]{:S(2)}) async-start(bf16[8,2,32,512]{3,2,1,0:T(8,128)(2,1)} %attend.3), calls=%async_computation.1 | async-start | bytes 1048576 | tf_op jit(solution)/shard_map/all_to_all | solution.py:375
  94.3 7.9 %collective-permute-start.11 = (bf16[2,32,512]{2,1,0:T(8,128)(2,1)S(1)}, bf16[2,32,512]{2,1,0:T(8,128)(2,1)S(1)}, u32[]{:S(2)}, u32[]{:S(2)}) collective-permute-start(bf16[2,32,512]{2,1,0:T(8,128)(2,1)S(1)} %get-tuple-element.58), channel_id=1, source_target_pairs={{0,2},{2,0},{4,6},{6,4},{8,10},{10,8},{12,14},{14,12},{1,3},{3,1},... | collective-permute-start | bytes 196616 | tf_op jit(solution)/shard_map/ppermute | solution.py:378
  96.3 9.2 %collective-permute-start.12 = (bf16[2,32,512]{2,1,0:T(8,128)(2,1)S(1)}, bf16[2,32,512]{2,1,0:T(8,128)(2,1)S(1)}, u32[]{:S(2)}, u32[]{:S(2)}) collective-permute-start(bf16[2,32,512]{2,1,0:T(8,128)(2,1)S(1)} %get-tuple-element.59), channel_id=1, source_target_pairs={{0,4},{2,6},{4,0},{6,2},{8,12},{10,14},{12,8},{14,10},{1,5},{3,7},... | collective-permute-start | bytes 196616 | tf_op jit(solution)/shard_map/ppermute | solution.py:378
  97.7 12.2 %collective-permute-start.13 = (bf16[2,32,512]{2,1,0:T(8,128)(2,1)S(1)}, bf16[2,32,512]{2,1,0:T(8,128)(2,1)S(1)}, u32[]{:S(2)}, u32[]{:S(2)}) collective-permute-start(bf16[2,32,512]{2,1,0:T(8,128)(2,1)S(1)} %get-tuple-element.60), channel_id=1, source_target_pairs={{0,6},{2,4},{4,2},{6,0},{8,14},{10,12},{12,10},{14,8},{1,7},{3,5},... | collective-permute-start | bytes 196616 | tf_op jit(solution)/shard_map/ppermute | solution.py:378
  97.8 17.8 %collective-permute-start.14 = (bf16[2,32,512]{2,1,0:T(8,128)(2,1)S(1)}, bf16[2,32,512]{2,1,0:T(8,128)(2,1)S(1)}, u32[]{:S(2)}, u32[]{:S(2)}) collective-permute-start(bf16[2,32,512]{2,1,0:T(8,128)(2,1)S(1)} %get-tuple-element.61), channel_id=1, source_target_pairs={{0,8},{2,10},{4,12},{6,14},{8,0},{10,2},{12,4},{14,6},{1,9},{3,11}... | collective-permute-start | bytes 196616 | tf_op jit(solution)/shard_map/ppermute | solution.py:378
  100.7 16.5 %collective-permute-start.15 = (bf16[2,32,512]{2,1,0:T(8,128)(2,1)S(1)}, bf16[2,32,512]{2,1,0:T(8,128)(2,1)S(1)}, u32[]{:S(2)}, u32[]{:S(2)}) collective-permute-start(bf16[2,32,512]{2,1,0:T(8,128)(2,1)S(1)} %get-tuple-element.62), channel_id=1, source_target_pairs={{0,10},{2,8},{4,14},{6,12},{8,2},{10,0},{12,6},{14,4},{1,11},{3,9}... | collective-permute-start | bytes 196616 | tf_op jit(solution)/shard_map/ppermute | solution.py:378
  102.1 15.0 %collective-permute-start.16 = (bf16[2,32,512]{2,1,0:T(8,128)(2,1)S(1)}, bf16[2,32,512]{2,1,0:T(8,128)(2,1)S(1)}, u32[]{:S(2)}, u32[]{:S(2)}) collective-permute-start(bf16[2,32,512]{2,1,0:T(8,128)(2,1)S(1)} %get-tuple-element.63), channel_id=1, source_target_pairs={{0,12},{2,14},{4,8},{6,10},{8,4},{10,6},{12,0},{14,2},{1,13},{3,15... | collective-permute-start | bytes 196616 | tf_op jit(solution)/shard_map/ppermute | solution.py:378
  105.5 11.7 %collective-permute-start.17 = (bf16[2,32,512]{2,1,0:T(8,128)(2,1)S(1)}, bf16[2,32,512]{2,1,0:T(8,128)(2,1)S(1)}, u32[]{:S(2)}, u32[]{:S(2)}) collective-permute-start(bf16[2,32,512]{2,1,0:T(8,128)(2,1)S(1)} %get-tuple-element.64), channel_id=1, source_target_pairs={{0,14},{2,12},{4,10},{6,8},{8,6},{10,4},{12,2},{14,0},{1,15},{3,13... | collective-permute-start | bytes 196616 | tf_op jit(solution)/shard_map/ppermute | solution.py:378
  (26 other events, 27.9 us)

commit v9 on v2

v9 whole, which is shorter than its diff:
```python
from functools import partial

import jax
import jax.numpy as jnp
from jax import lax
from jax.experimental import pallas as pl
from jax.experimental.pallas import tpu as pltpu
from jax.sharding import PartitionSpec as P

epsilon = 1e-06
parts = 2
pair = 2
taps = 3
most_direct = 8
mebibyte = 1024 * 1024

VMEM = pl.BlockSpec(memory_space=pltpu.VMEM)
SMEM = pl.BlockSpec(memory_space=pltpu.SMEM)
ANY = pl.BlockSpec(memory_space=pl.ANY)


def silu(v):
    return 0.5 * v * (1.0 + jnp.tanh(0.5 * v))


def dot32(a, b):
    return jnp.dot(a, b, preferred_element_type=jnp.float32)


def cost(flops, *arrays):
    size = sum(a.size * a.dtype.itemsize for a in arrays)
    return pl.CostEstimate(flops=flops, bytes_accessed=size, transcendentals=0)


def params(mebibytes):
    return pltpu.CompilerParams(vmem_limit_bytes=mebibytes * mebibyte)


def rows_of(owner, begin, end, half, height):
    low, high = max(begin, 1), min(end, half + 1)
    pieces = [(owner * half + low - 1, low - begin, high - low)]
    if begin == 0:
        pieces.append((jnp.maximum(owner * half - 1, 0), 0, 1))
    if end == half + 2:
        pieces.append((jnp.minimum((owner + 1) * half, height - 1), end - 1 - begin, 1))
    return pieces


def run(copies):
    for copy in copies:
        copy.start()
    for copy in copies:
        copy.wait()


def send_kernel(spans, half, scalars, video, *refs):
    outs, sems = refs[:-1], refs[-1]
    frames, height = video.shape[:2]
    copies = []
    for (begin, end), out in zip(spans, outs):
        for source, here, count in rows_of(1 - scalars[0], begin, end, half, height):
            copies.append(
                pltpu.make_async_copy(
                    video.at[:, pl.ds(source, count)],
                    out.at[:, here : here + count],
                    sems.at[len(copies)],
                )
            )
    run(copies)


def send(scalars, video, spans, half):
    frames, _, width, channels = video.shape
    shapes = [(frames, end - begin, width, channels) for begin, end in spans]
    return pl.pallas_call(
        partial(send_kernel, spans, half),
        out_shape=[jax.ShapeDtypeStruct(shape, video.dtype) for shape in shapes],
        in_specs=[SMEM, ANY],
        out_specs=[VMEM] * len(shapes),
        scratch_shapes=[pltpu.SemaphoreType.DMA((3 * len(spans),))],
        compiler_params=params(8),
        name="send",
    )(scalars, video)


def join_kernel(begin, end, half, scalars, video, received, own_edge, other_edge, first, last, sems):
    frames, height = video.shape[:2]
    rows = end - begin
    split = first.shape[0]

    def at(f):
        return first.at[f] if f < split else last.at[f - split]

    def copies(side):
        made = []

        def add(source, target):
            made.append(pltpu.make_async_copy(source, target, sems.at[len(made)]))

        for t in range(frames):
            mine, others = at(side * frames + t), at((1 - side) * frames + t)
            for source, here, count in rows_of(side, begin, end, half, height):
                add(video.at[t, pl.ds(source, count)], mine.at[here : here + count])
            add(received.at[t], others.at[:rows])
            add(own_edge.at[t], mine.at[rows:])
            add(other_edge.at[t], others.at[rows:])
        return made

    for side in range(pair):

        @pl.when(scalars[0] == side)
        def _():
            run(copies(side))


def join(scalars, video, received, own_edge, other_edge, begin, end, half):
    frames, _, width, channels = video.shape
    rows = end - begin + own_edge.shape[1]
    lasting = pair * frames - taps
    return pl.pallas_call(
        partial(join_kernel, begin, end, half),
        out_shape=[
            jax.ShapeDtypeStruct((count, rows, width, channels), jnp.bfloat16)
            for count in (lasting, taps)
        ],
        in_specs=[SMEM] + [ANY] * 4,
        out_specs=[VMEM] * 2,
        scratch_shapes=[pltpu.SemaphoreType.DMA((6 * frames,))],
        compiler_params=params(8),
        name="join",
    )(scalars, video, received, own_edge, other_edge)


def place_rows(buffers, index, top, reduced, rows, width, column):
    pixels, channels = rows * width, reduced.shape[-1]
    edges = reduced.shape[0] - pixels
    row_of = lax.broadcasted_iota(jnp.int32, (pixels, edges), 0) // width
    spread = (row_of == lax.broadcasted_iota(jnp.int32, (pixels, edges), 1)).astype(jnp.bfloat16)
    across = lax.broadcasted_iota(jnp.int32, (pixels, channels), 0) % width
    wide = reduced[:pixels].astype(jnp.float32)
    beside = dot32(spread, reduced[pixels:])
    before = jnp.where(column == 1, beside, 0.0)
    behind = jnp.where(column == 0, beside, 0.0)
    shifted = (
        jnp.where(across == 0, before, pltpu.roll(wide, 1, 0)),
        wide,
        jnp.where(across == width - 1, behind, pltpu.roll(wide, pixels - 1, 0)),
    )
    for b in range(3):
        value = shifted[b].astype(jnp.bfloat16).reshape(rows, width, channels)
        buffers[b, index, top : top + rows] = value


def convolve(buffers, fresh, last, side, kept, keeps, w_space, b_space):
    _, frames, rows, width, channels = buffers.shape
    size = rows - 2
    if fresh:

        @pl.when(side == 0)
        def _():
            buffers[:, :, :1] = jnp.zeros((3, frames, 1, width, channels), jnp.bfloat16)

    else:
        buffers[:, :, :2] = kept[...]
    if last:

        @pl.when(side == pair - 1)
        def _():
            buffers[:, :, size + 1 :] = jnp.zeros((3, frames, 1, width, channels), jnp.bfloat16)

    else:
        keeps[...] = buffers[:, :, size:]

    def window(b, a):
        return buffers[b, :, a : a + size].reshape(frames * size * width, channels)

    lhs = jnp.concatenate([window(b, a) for a in range(3) for b in range(3)], axis=1)
    acc = dot32(lhs, w_space[...].reshape(-1, channels)) + b_space[...]
    value = window(1, 1).astype(jnp.float32) + silu(acc)
    return value.astype(jnp.bfloat16).reshape(frames, size * width, channels)


def early_kernel(
    fresh, final, rows, scalars, first, last, w_time, b_time, w_down, b_down, w_space, b_space, *refs
):
    refs = list(refs)
    kept = None if fresh else refs.pop(0)
    part, spatial = refs[:2]
    keeps = None if final else refs[2]
    lifted, buffers = refs[-2:]
    split, depth, width, channels = first.shape
    count = split + taps
    halves = count // 2
    pixels = depth * width

    def frame(t):
        return (first[t] if t < split else last[t - split]).reshape(pixels, channels)

    starts = list(range(taps - 1, count))
    for low in range(0, len(starts), 3):
        group = starts[low : low + 3]
        lhs = jnp.concatenate(
            [jnp.concatenate([frame(t - k) for t in group], axis=0) for k in range(taps)], axis=1
        )
        acc = dot32(lhs, w_time[...]) + b_time[...]
        held = jnp.concatenate([frame(t) for t in group], axis=0).astype(jnp.float32)
        value = (held + silu(acc)).astype(jnp.bfloat16)
        for g, t in enumerate(group):
            lifted[t] = value[g * pixels : (g + 1) * pixels]
    lhs = jnp.concatenate([lifted[3], lifted[2]], axis=1)
    part[...] = dot32(lhs, w_down[: 2 * channels]) + b_down[...]
    whole = range(2, halves)
    lhs = jnp.concatenate(
        [jnp.concatenate([lifted[2 * s + 1 - k] for s in whole], axis=0) for k in range(taps)],
        axis=1,
    )
    reduced = (dot32(lhs, w_down[...]) + b_down[...]).astype(jnp.bfloat16)
    for index in range(len(whole)):
        value = reduced[index * pixels : (index + 1) * pixels]
        place_rows(buffers, index, 0 if fresh else 2, value, rows, width, scalars[1])
    spatial[...] = convolve(buffers, fresh, final, scalars[0], kept, keeps, w_space, b_space)


def early(scalars, first, last, kept, final, size, rows, *weights):
    split, depth, width, channels = first.shape
    halves = (split + taps) // 2
    pixels = depth * width
    later = halves - 2
    given = [] if kept is None else [kept]
    shapes = [
        jax.ShapeDtypeStruct((pixels, channels), jnp.float32),
        jax.ShapeDtypeStruct((later, size * width, channels), jnp.bfloat16),
    ]
    if not final:
        shapes.append(jax.ShapeDtypeStruct((3, later, 2, width, channels), jnp.bfloat16))
    flops = 2 * channels * channels * (pixels * 26 + 9 * later * size * width)
    return pl.pallas_call(
        partial(early_kernel, kept is None, final, rows),
        out_shape=shapes,
        in_specs=[SMEM] + [VMEM] * (2 + len(weights) + len(given)),
        out_specs=[VMEM] * len(shapes),
        scratch_shapes=[
            pltpu.VMEM((2 * halves, pixels, channels), jnp.bfloat16),
            pltpu.VMEM((3, later, size + 2, width, channels), jnp.bfloat16),
        ],
        compiler_params=params(24),
        cost_estimate=cost(flops, first, last, *weights),
        name="early",
    )(scalars, first, last, *weights, *given)


def late_kernel(
    owners, fresh, final, rows, scalars, halo, first, part, spatial, w_time, b_time, w_down, b_down,
    w_space, b_space, *refs
):
    refs = list(refs)
    kept = None if fresh else refs.pop(0)
    outs = refs[:owners]
    keeps = None if final else refs[owners]
    lifted, buffers, result = refs[-3:]
    _, depth, width, channels = first.shape
    pixels = depth * width

    def frame(t):
        return (halo[t + taps] if t < 0 else first[t]).reshape(pixels, channels)

    group = range(-1, taps - 1)
    lhs = jnp.concatenate(
        [jnp.concatenate([frame(t - k) for t in group], axis=0) for k in range(taps)], axis=1
    )
    acc = dot32(lhs, w_time[...]) + b_time[...]
    held = jnp.concatenate([frame(t) for t in group], axis=0).astype(jnp.float32)
    value = held + silu(acc)
    for index in range(taps):
        piece = value[index * pixels : (index + 1) * pixels]
        if index == 0:
            piece = jnp.where(scalars[2] > 0, piece, 0.0)
        lifted[index] = piece.astype(jnp.bfloat16)
    lhs = jnp.concatenate([lifted[2], lifted[1], lifted[0]], axis=1)
    reduced = (
        dot32(lhs, w_down[...]) + b_down[...],
        dot32(lifted[2], w_down[2 * channels :]) + part[...],
    )
    for index, value in enumerate(reduced):
        value = value.astype(jnp.bfloat16)
        place_rows(buffers, index, 0 if fresh else 2, value, rows, width, scalars[1])
    result[:2] = convolve(buffers, fresh, final, scalars[0], kept, keeps, w_space, b_space)
    result[2:] = spatial[...]
    each = result.shape[1] // owners
    if owners == 1:
        outs[0][...] = result[...]
    else:
        for j, out in enumerate(outs):
            begin = pl.multiple_of((scalars[2] ^ j) * each, each)
            out[...] = result[:, pl.ds(begin, each)]


def late(owners, scalars, halo, first, part, spatial, kept, final, rows, *weights):
    _, depth, width, channels = first.shape
    later, pixels = spatial.shape[:2]
    halves = later + 2
    size = pixels // width
    given = [] if kept is None else [kept]
    shapes = [(halves, pixels // owners, channels)] * owners
    if not final:
        shapes.append((3, 2, 2, width, channels))
    flops = 2 * channels * channels * (depth * width * 13 + 18 * pixels)
    return pl.pallas_call(
        partial(late_kernel, owners, kept is None, final, rows),
        out_shape=[jax.ShapeDtypeStruct(shape, jnp.bfloat16) for shape in shapes],
        in_specs=[SMEM] + [VMEM] * (4 + len(weights) + len(given)),
        out_specs=[VMEM] * len(shapes),
        scratch_shapes=[
            pltpu.VMEM((taps, depth * width, channels), jnp.bfloat16),
            pltpu.VMEM((3, 2, size + 2, width, channels), jnp.bfloat16),
            pltpu.VMEM((halves, pixels, channels), jnp.bfloat16),
        ],
        compiler_params=params(24),
        cost_estimate=cost(flops, halo, first, part, *weights),
        name="late",
    )(scalars, halo, first, part, spatial, *weights, *given)


def attend_kernel(frames_per, lanes, count, scalars, *refs):
    blocks = refs[:count]
    gain, w_query, w_key, w_value, w_out = refs[count : count + 5]
    outs = refs[count + 5 :]
    channels = gain.shape[-1]
    flat = len(blocks[0].shape) == 2
    groups = 1 if flat else blocks[0].shape[1] // lanes
    each = frames_per * lanes
    size = count * each

    def piece(j, g):
        if flat:
            return blocks[0][...]
        return blocks[j][:, g * lanes : (g + 1) * lanes].reshape(each, channels)

    def place(index):
        block = index // each
        time = index // lanes % frames_per
        for j in range(count):
            level = 0 if flat else scalars[2] ^ j
            time = time + jnp.where(block == j, level * frames_per, 0)
        return time, index % lanes

    row_time, row_lane = place(lax.broadcasted_iota(jnp.int32, (size, 1), 0))
    col_time, col_lane = place(lax.broadcasted_iota(jnp.int32, (1, size), 1))
    allowed = (row_lane == col_lane) & (col_time <= row_time)
    x = jnp.concatenate([piece(j, g) for g in range(groups) for j in range(count)], axis=0)
    wide = x.astype(jnp.float32)
    scale = lax.rsqrt(jnp.mean(wide * wide, axis=-1, keepdims=True) + epsilon)
    normed = (wide * scale * gain[...]).astype(jnp.bfloat16)
    query = dot32(normed, w_query[...]).astype(jnp.bfloat16)
    key = dot32(normed, w_key[...]).astype(jnp.bfloat16)
    value = dot32(normed, w_value[...]).astype(jnp.bfloat16)
    contexts = []
    for g in range(groups):
        part = slice(g * size, (g + 1) * size)
        scores = lax.dot_general(
            query[part], key[part], (((1,), (1,)), ((), ())), preferred_element_type=jnp.float32
        )
        scores = jnp.where(allowed, scores * channels ** (-0.5), -1e30)
        largest = jnp.max(scores, axis=-1, keepdims=True)
        probs = jnp.exp(scores - largest)
        probs = (probs / jnp.sum(probs, axis=-1, keepdims=True)).astype(jnp.bfloat16)
        contexts.append(dot32(probs, value[part]).astype(jnp.bfloat16))
    mixed = dot32(jnp.concatenate(contexts, axis=0), w_out[...])
    result = (wide + mixed).astype(jnp.bfloat16)
    if flat:
        outs[0][...] = result
        return
    short = frames_per // pair
    for g in range(groups):
        for j in range(count):
            begin = g * size + j * each
            rows = result[begin : begin + each].reshape(pair, short, lanes, channels)
            for side in range(pair):

                @pl.when(scalars[0] == side)
                def _():
                    for x in range(pair):
                        outs[pair * j + x][:, g * lanes : (g + 1) * lanes] = rows[side ^ x]


def attend(scalars, blocks, gain, w_query, w_key, w_value, w_out):
    frames_per, pixels, channels = blocks[0].shape
    flat = pixels % 16 != 0
    lanes = pixels if flat else 16
    if flat:
        blocks = [b.reshape(frames_per * pixels, channels) for b in blocks]
    count = len(blocks)
    size = frames_per * count * lanes
    shapes = [(frames_per // pair, pixels, channels)] * (pair * count)
    if flat:
        shapes = [blocks[0].shape]
    flops = 2 * frames_per * pixels * count * channels * (4 * channels + 2 * size)
    outs = pl.pallas_call(
        partial(attend_kernel, frames_per, lanes, count),
        out_shape=[jax.ShapeDtypeStruct(shape, jnp.bfloat16) for shape in shapes],
        in_specs=[SMEM] + [VMEM] * (count + 5),
        out_specs=[VMEM] * len(shapes),
        compiler_params=params(20 if 16 * size * size < 20 * mebibyte else 56),
        cost_estimate=cost(flops, *blocks, w_query, w_key, w_value, w_out),
        name="attend",
    )(scalars, *blocks, gain, w_query, w_key, w_value, w_out)
    return [o.reshape(frames_per, pixels, channels) for o in outs] if flat else outs


def collect_kernel(base, stride, scalars, *refs):
    out, sems = refs[-2:]
    copies = []
    for m in range(sems.shape[0]):
        index = base + (scalars[0] ^ m % pair) * stride + (scalars[2] ^ m // pair)
        copies.append(pltpu.make_async_copy(refs[m], out.at[:, index], sems.at[m]))
    run(copies)


def collect(scalars, blocks, chunk, chunks, whole):
    count = len(blocks)
    halves, pixels, channels = blocks[0].shape
    levels = count // pair
    given = [] if whole is None else [whole]
    return pl.pallas_call(
        partial(collect_kernel, chunk * levels, chunks * levels),
        out_shape=jax.ShapeDtypeStruct((halves, chunks * count, pixels, channels), jnp.bfloat16),
        in_specs=[SMEM] + [ANY] * (count + len(given)),
        out_specs=ANY,
        input_output_aliases={count + 1: 0} if given else {},
        scratch_shapes=[pltpu.SemaphoreType.DMA((count,))],
        compiler_params=params(16),
        name="collect",
    )(scalars, *blocks, *given)


def after(value, other):
    return lax.optimization_barrier((value, other))[0]


def per_device(
    video, w_time, b_time, w_down, b_down, w_space, b_space, gain, w_query, w_key, w_value, w_out
):
    frames, height, width, channels = video.shape
    devices = lax.axis_size("tm")
    levels = devices // pair
    columns = lax.axis_size("cols")
    assert columns == 2 and devices % pair == 0 and height % pair == 0 and frames >= taps
    place = lax.axis_index("tm").astype(jnp.int32)
    column = lax.axis_index("cols").astype(jnp.int32)
    side, level = place % pair, place // pair
    scalars = jnp.stack([side, column, level])
    half = height // pair
    gain = gain.reshape(1, -1)
    weights = [
        w_time.reshape(-1, channels), b_time.reshape(1, -1), w_down.reshape(-1, channels),
        b_down.reshape(1, -1), w_space, b_space.reshape(1, -1),
    ]
    attention = [gain, w_query, w_key, w_value, w_out]
    chunks = parts if half % parts == 0 and half // parts * width % levels == 0 else 1
    size = half // chunks
    each = size * width // levels
    direct = devices <= most_direct and levels & (levels - 1) == 0 and each % 16 == 0
    spans = [
        (k * size + (2 if k else 0), (k + 1) * size + 2) for k in range(chunks)
    ]

    def tm_permute(value, move):
        return lax.ppermute(value, "tm", [(i, move(i)) for i in range(devices) if move(i) < devices])

    sent = send(scalars, video, spans, half)
    received = [tm_permute(value, lambda i: i ^ 1) for value in sent]
    border = jnp.where(column == 0, video[:, :, -1], video[:, :, 0])
    border = jnp.pad(after(border, sent[0]), ((0, 0), (1, 1), (0, 0)))
    own_edge, other_edge = (
        lax.dynamic_slice_in_dim(border, s * half, half + 2, axis=1) for s in (side, 1 - side)
    )
    own_edge = lax.ppermute(own_edge, "cols", [(0, 1), (1, 0)])
    aslant = [
        (i * columns + c, (i ^ 1) * columns + 1 - c)
        for i in range(devices)
        for c in range(columns)
    ]
    other_edge = lax.ppermute(other_edge, ("tm", "cols"), aslant)

    def edge_rows(edge, begin, end):
        cut = jnp.pad(edge[:, begin:end], ((0, 0), (0, -(end - begin) % width), (0, 0)))
        return cut.reshape(frames, -1, width, channels)

    ahead, halos = [], []
    kept = None
    for k, (begin, end) in enumerate(spans):
        arrived = after(received[k], ahead[-1][1]) if ahead else received[k]
        first, last = join(
            scalars, video, arrived, edge_rows(own_edge, begin, end),
            edge_rows(other_edge, begin, end), begin, end, half
        )
        halos.append(tm_permute(last, lambda i: i + pair))
        final = k == chunks - 1
        made = early(scalars, first, last, kept, final, size, end - begin, *weights)
        kept = None if final else made[2]
        ahead.append((first, made[0], made[1]))

    spatials = []
    kept = None
    owners = levels if direct else 1
    for k, (begin, end) in enumerate(spans):
        first, part, spatial = ahead[k]
        if spatials:
            part = after(part, spatials[-1][0])
        final = k == chunks - 1
        made = late(
            owners, scalars, halos[k], first, part, spatial, kept, final, end - begin, *weights
        )
        spatials.append(made[:owners])
        kept = None if final else made[owners]

    newest = spatials[-1][0]
    if direct:
        gathers = [
            [blocks[0]]
            + [tm_permute(blocks[j], lambda i: i ^ (pair * j)) for j in range(1, levels)]
            for blocks in spatials
        ]
        returns = []
        for gathered in gathers:
            gathered[0] = after(gathered[0], newest)
            results = attend(scalars, gathered, *attention)
            newest = results[0]
            returns.append(
                [results[0]]
                + [tm_permute(results[m], lambda i: i ^ m) for m in range(1, devices)]
            )
        whole = None
        for k, blocks in enumerate(returns):
            whole = collect(scalars, blocks, k, chunks, whole)
        return whole.reshape(frames // 2, height, width, channels)
    sets = [[pair * z + s for z in range(levels)] for s in range(pair)]
    returns = []
    for (block,) in spatials:
        gathered = lax.all_to_all(block, "tm", 1, 0, axis_index_groups=sets, tiled=True)
        (result,) = attend(scalars, [gathered], *attention)
        result = lax.all_to_all(result, "tm", 0, 1, tiled=True)
        result = result.reshape(frames // 2, levels, pair, each, channels)
        returns.append(result.transpose(0, 2, 1, 3, 4).reshape(frames // 2, pair, -1, channels))
    return jnp.concatenate(returns, axis=2).reshape(frames // 2, height, width, channels)


def solution(mesh):
    spread = P(("clips", "tm"), None, "cols", None)
    return jax.shard_map(
        per_device,
        mesh=mesh,
        in_specs=(spread,) + (P(),) * 11,
        out_specs=spread,
        check_vma=False,
    )
```

time: 129 us -> 112 us (0.87)
  waiting for transfers between devices: 57 us -> 19.3 us
  starting transfers between devices: 29.7 us -> 49.8 us
  Pallas kernels: 22.3 us -> 31.4 us
  local copies, waits for them, and re-layouts: 16.2 us -> 9.98 us
  other arithmetic: 2.61 us -> 0.85 us
    ppermute x4 -> x26, starting transfers between devices: 9.38 us -> 49.8 us  [the longest x24 49.6 us: tm_permute(): lax.ppermute(value, 'tm', [(i, move(i)) for i in range(devices) if move(i...]
    all_to_all x4 -> x0, waiting for transfers between devices: 36.5 us -> none  [the longest x2 26.3 us: per_device(): returns.append(lax.all_to_all(newest, 'tm', 0, 1, tiled=True))]
    all_to_all x4 -> x0, starting transfers between devices: 20.4 us -> none  [the longest x2 13.1 us: per_device(): lax.all_to_all(s.reshape(halves, size * width, channels), 'tm', 1, 0, til...]
    pallas_call x4 -> x9, Pallas kernels: 16.6 us -> 25.8 us  [the longest x2 9.55 us: early(): pl.pallas_call(partial(early_kernel, kept is None, final, rows), out_shap...]
    slice x10 -> x3, local copies, waits for them, and re-layouts: 7.23 us -> 0.44 us  [the longest x1 0.41 us: per_device(): border = jnp.where(column == 0, video[:, :, -1], video[:, :, 0])]
    unnamed x26 -> x36, local copies, waits for them, and re-layouts: 4.77 us -> 9.45 us
    reshape x2, local copies, waits for them, and re-layouts: 2.68 us -> 0.01 us  [edge_rows(): return cut.reshape(frames, -1, width, channels)]
    concatenate x7 -> x0, other arithmetic: 2.17 us -> none  [the longest x1 1.04 us: per_device(): encoded = jnp.concatenate(returns, axis=1)]
  transfers between devices with their start and end apart: 8 -> 26, of which waited for: 6 -> 5; matrix products, arithmetic and copies ran while one was open for 8% -> 1% of each run, Pallas kernels for 15% -> 26%
where the time goes in v9:
time: 112 us
  starting transfers between devices  49.8 us (44%)
  Pallas kernels  31.4 us (28%)
  waiting for transfers between devices  19.3 us (17%)
  local copies, waits for them, and re-layouts  9.98 us (9%)
    ppermute x24, starting transfers between devices, tm_permute(): lax.ppermute(value, 'tm', [(i, move(i)) for i in range(devices) if move(i...  49.6 us
    ppermute x1, waiting for transfers between devices, per_device(): other_edge = lax.ppermute(other_edge, ('tm', 'cols'), aslant)  14.4 us
    pallas_call x2, Pallas kernels, early(): pl.pallas_call(partial(early_kernel, kept is None, final, rows), out_shap...  9.55 us
    unnamed x36, local copies, waits for them, and re-layouts  9.45 us
    pallas_call x2, Pallas kernels, late(): pl.pallas_call(partial(late_kernel, owners, kept is None, final, rows), o...  7.71 us
    pallas_call x2, Pallas kernels, attend(): pl.pallas_call(partial(attend_kernel, frames_per, lanes, count), out_shap...  5.57 us
    pallas_call x2, Pallas kernels, join(): pl.pallas_call(partial(join_kernel, begin, end, half), out_shape=[jax.Sha...  4.98 us
    ppermute x24, waiting for transfers between devices, tm_permute(): lax.ppermute(value, 'tm', [(i, move(i)) for i in range(devices) if move(i...  4.85 us
  transfers between devices with their start and end apart: 26, of which 5 were waited for; matrix products, arithmetic and copies ran while one was open for 1% of the time, Pallas kernels for 26%

profile of v9, /device:TPU:0, one launch (start us, length us, event | category | flops | bytes accessed | tf_op | source)
XLA Modules:
  0.0 111.9 jit_solution(5677323760162916599)
XLA Ops:
  0.1 1.6 %copy-done = bf16[4,32,16,512]{3,2,1,0:T(8,128)(2,1)S(1)} copy-done((bf16[4,32,16,512]{3,2,1,0:T(8,128)(2,1)S(1)}, bf16[4,32,16,512]{3,2,1,0:T(8,128)(2,1)}, u32[]{:S(2)}) %copy-start) | copy-done | bytes 2097176
  3.3 3.0 %collective-permute-start.1 = (bf16[4,10,16,512]{3,2,1,0:T(8,128)(2,1)S(1)}, bf16[4,10,16,512]{3,2,1,0:T(8,128)(2,1)S(1)}, u32[]{:S(2)}, u32[]{:S(2)}) collective-permute-start(bf16[4,10,16,512]{3,2,1,0:T(8,128)(2,1)S(1)} %get-tuple-element.47), channel_id=1, source_target_pairs={{0,2},{2,0},{4,6},{6,4},{8,10},{10,8},{12,14},{14,12},{1,3},{3,1},... | collective-permute-start | bytes 1966088 | tf_op jit(solution)/shard_map/ppermute | solution.py:468
  7.0 2.0 %collective-permute-start = (bf16[4,8,16,512]{3,2,1,0:T(8,128)(2,1)}, bf16[4,8,16,512]{3,2,1,0:T(8,128)(2,1)S(1)}, u32[]{:S(2)}, u32[]{:S(2)}) collective-permute-start(bf16[4,8,16,512]{3,2,1,0:T(8,128)(2,1)} %copy-done.14), channel_id=1, source_target_pairs={{0,2},{2,0},{4,6},{6,4},{8,10},{10,8},{12,14},{14,12},{1,3},{3,1},... | collective-permute-start | bytes 1572872 | tf_op jit(solution)/shard_map/ppermute | solution.py:468
  9.1 14.4 %collective-permute-done.3 = bf16[4,18,512]{2,1,0:T(8,128)(2,1)S(1)} collective-permute-done((bf16[4,18,512]{2,1,0:T(8,128)(2,1)S(1)}, bf16[4,18,512]{2,1,0:T(8,128)(2,1)S(1)}, u32[]{:S(2)}, u32[]{:S(2)}) %collective-permute-start.3) | collective-permute-done | bytes 73760 | tf_op jit(solution)/shard_map/ppermute | solution.py:483
  24.3 2.7 %join.2 = (bf16[5,11,16,512]{3,2,1,0:T(8,128)(2,1)S(1)}, bf16[3,11,16,512]{3,2,1,0:T(8,128)(2,1)S(1)}) custom-call(s32[3]{0:T(128)S(1)} %pad_add_fusion.scalars, bf16[4,32,16,512]{3,2,1,0:T(8,128)(2,1)S(1)} %copy-done.1, bf16[4,10,16,512]{3,2,1,0:T(8,128)(2,1)S(1)} %collective-permute-done.1.received, ...), custom_call_target="tpu_custom_call" | custom-call | tf_op jit(solution)/shard_map/join/pallas_call | solution.py:120
  27.0 3.5 %collective-permute-start.5 = (bf16[3,11,16,512]{3,2,1,0:T(8,128)(2,1)S(1)}, bf16[3,11,16,512]{3,2,1,0:T(8,128)(2,1)S(1)}, u32[]{:S(2)}, u32[]{:S(2)}) collective-permute-start(bf16[3,11,16,512]{3,2,1,0:T(8,128)(2,1)S(1)} %get-tuple-element.50.last), channel_id=1, source_target_pairs={{0,4},{2,6},{4,8},{6,10},{8,12},{10,14},{1,5},{3,7},{5,9},{7,11},{... | collective-permute-start | bytes 1622024 | tf_op jit(solution)/shard_map/ppermute | solution.py:468
  30.6 2.3 %copy-done.2 = bf16[9,512,512]{2,1,0:T(8,128)(2,1)S(1)} copy-done((bf16[9,512,512]{2,1,0:T(8,128)(2,1)S(1)}, bf16[9,512,512]{2,1,0:T(8,128)(2,1)}, u32[]{:S(2)}) %copy-start.2) | copy-done | bytes 4718616
  32.9 5.0 %early.2 = (f32[176,512]{1,0:T(8,128)S(1)}, bf16[2,128,512]{2,1,0:T(8,128)(2,1)S(1)}, bf16[3,2,2,16,512]{4,3,2,1,0:T(8,128)(2,1)S(1)}) custom-call(s32[3]{0:T(128)S(1)} %pad_add_fusion.scalars, bf16[5,11,16,512]{3,2,1,0:T(8,128)(2,1)S(1)} %get-tuple-element.49.first, bf16[3,11,16,512]{3,2,1,0:T(8,128)(2,1)S(1)} %get-tuple-element.50.last, ...), custom_call_target="tpu_custom_call" | custom-call | flops 3607101440 | bytes 9312256 | tf_op jit(solution)/shard_map/early/pallas_call | solution.py:237
  37.9 2.3 %join.3 = (bf16[5,9,16,512]{3,2,1,0:T(8,128)(2,1)S(1)}, bf16[3,9,16,512]{3,2,1,0:T(8,128)(2,1)S(1)}) custom-call(s32[3]{0:T(128)S(1)} %pad_add_fusion.scalars, bf16[4,32,16,512]{3,2,1,0:T(8,128)(2,1)S(1)} %copy-done.1, bf16[4,8,16,512]{3,2,1,0:T(8,128)(2,1)S(1)} %collective-permute-done.received, bf16[4,1,16,512]{3,2,1,0:T(8,128)(2,1)S(1)} %pad_bitcast_fusion.1.own_edge, ...), custom_call_target="tpu_custom_call" | custom-call | tf_op jit(solution)/shard_map/join/pallas_call | solution.py:120
  40.2 3.5 %collective-permute-start.4 = (bf16[3,9,16,512]{3,2,1,0:T(8,128)(2,1)S(1)}, bf16[3,9,16,512]{3,2,1,0:T(8,128)(2,1)S(1)}, u32[]{:S(2)}, u32[]{:S(2)}) collective-permute-start(bf16[3,9,16,512]{3,2,1,0:T(8,128)(2,1)S(1)} %get-tuple-element.53.last), channel_id=1, source_target_pairs={{0,4},{2,6},{4,8},{6,10},{8,12},{10,14},{1,5},{3,7},{5,9},{7,11},{... | collective-permute-start | bytes 1327112 | tf_op jit(solution)/shard_map/ppermute | solution.py:468
  43.7 2.3 %copy-done.3 = bf16[9,512,512]{2,1,0:T(8,128)(2,1)S(1)} copy-done((bf16[9,512,512]{2,1,0:T(8,128)(2,1)S(1)}, bf16[9,512,512]{2,1,0:T(8,128)(2,1)}, u32[]{:S(2)}) %copy-start.3) | copy-done | bytes 4718616
  46.0 4.6 %early.3 = (f32[144,512]{1,0:T(8,128)S(1)}, bf16[2,128,512]{2,1,0:T(8,128)(2,1)S(1)}) custom-call(s32[3]{0:T(128)S(1)} %pad_add_fusion.scalars, bf16[5,9,16,512]{3,2,1,0:T(8,128)(2,1)S(1)} %get-tuple-element.54.first, bf16[3,9,16,512]{3,2,1,0:T(8,128)(2,1)S(1)} %get-tuple-element.53.last, bf16[1536,512]{1,0:T(8,128)(2,1)S(1)} %bitcast.29, ...), custom_call_target="tpu_custom_call" | custom-call | flops 3170893824 | bytes 9050112 | tf_op jit(solution)/shard_map/early/pallas_call | solution.py:237
  50.6 2.3 %copy-done.4 = bf16[9,512,512]{2,1,0:T(8,128)(2,1)S(1)} copy-done((bf16[9,512,512]{2,1,0:T(8,128)(2,1)S(1)}, bf16[9,512,512]{2,1,0:T(8,128)(2,1)}, u32[]{:S(2)}) %copy-start.4) | copy-done | bytes 4718616
  53.0 3.9 %late.2 = (bf16[4,32,512]{2,1,0:T(8,128)(2,1)S(1)}, bf16[4,32,512]{2,1,0:T(8,128)(2,1)S(1)}, bf16[4,32,512]{2,1,0:T(8,128)(2,1)S(1)}, bf16[4,32,512]{2,1,0:T(8,128)(2,1)S(1)}, bf16[3,2,2,16,512]{4,3,2,1,0:T(8,128)(2,1)S(1)}) custom-call(s32[3]{0:T(128)S(1)} %pad_add_fusion.scalars, bf16[3,11,16,512]{3,2,1,0:T(8,128)(2,1)S(1)} %collective-permute-done.5.halo, ...), custom_call_target="tpu_custom_call" | custom-call | flops 2407530496 | bytes 9672704 | tf_op jit(solution)/shard_map/late/pallas_call | solution.py:308
  56.9 1.6 %collective-permute-start.6 = (bf16[4,32,512]{2,1,0:T(8,128)(2,1)S(1)}, bf16[4,32,512]{2,1,0:T(8,128)(2,1)S(1)}, u32[]{:S(2)}, u32[]{:S(2)}) collective-permute-start(bf16[4,32,512]{2,1,0:T(8,128)(2,1)S(1)} %get-tuple-element.64), channel_id=1, source_target_pairs={{0,4},{2,6},{4,0},{6,2},{8,12},{10,14},{12,8},{14,10},{1,5},{3,7},... | collective-permute-start | bytes 393224 | tf_op jit(solution)/shard_map/ppermute | solution.py:468
  58.5 2.8 %collective-permute-start.8 = (bf16[4,32,512]{2,1,0:T(8,128)(2,1)S(1)}, bf16[4,32,512]{2,1,0:T(8,128)(2,1)S(1)}, u32[]{:S(2)}, u32[]{:S(2)}) collective-permute-start(bf16[4,32,512]{2,1,0:T(8,128)(2,1)S(1)} %get-tuple-element.66), channel_id=1, source_target_pairs={{0,12},{2,14},{4,8},{6,10},{8,4},{10,6},{12,0},{14,2},{1,13},{3,15... | collective-permute-start | bytes 393224 | tf_op jit(solution)/shard_map/ppermute | solution.py:468
  61.4 3.8 %late.3 = (bf16[4,32,512]{2,1,0:T(8,128)(2,1)S(1)}, bf16[4,32,512]{2,1,0:T(8,128)(2,1)S(1)}, bf16[4,32,512]{2,1,0:T(8,128)(2,1)S(1)}, bf16[4,32,512]{2,1,0:T(8,128)(2,1)S(1)}) custom-call(s32[3]{0:T(128)S(1)} %pad_add_fusion.scalars, bf16[3,9,16,512]{3,2,1,0:T(8,128)(2,1)S(1)} %collective-permute-done.4.halo, ...), custom_call_target="tpu_custom_call" | custom-call | flops 2189426688 | bytes 9345024 | tf_op jit(solution)/shard_map/late/pallas_call | solution.py:308
  66.9 2.8 %collective-permute-start.11 = (bf16[4,32,512]{2,1,0:T(8,128)(2,1)S(1)}, bf16[4,32,512]{2,1,0:T(8,128)(2,1)S(1)}, u32[]{:S(2)}, u32[]{:S(2)}) collective-permute-start(bf16[4,32,512]{2,1,0:T(8,128)(2,1)S(1)} %get-tuple-element.71), channel_id=1, source_target_pairs={{0,12},{2,14},{4,8},{6,10},{8,4},{10,6},{12,0},{14,2},{1,13},{3,15... | collective-permute-start | bytes 393224 | tf_op jit(solution)/shard_map/ppermute | solution.py:468
  69.7 1.8 %collective-permute-done.7.refs_2_ = bf16[4,32,512]{2,1,0:T(8,128)(2,1)S(1)} collective-permute-done((bf16[4,32,512]{2,1,0:T(8,128)(2,1)S(1)}, bf16[4,32,512]{2,1,0:T(8,128)(2,1)S(1)}, u32[]{:S(2)}, u32[]{:S(2)}) %collective-permute-start.7) | collective-permute-done | bytes 131104 | tf_op jit(solution)/shard_map/ppermute | solution.py:468
  71.5 2.8 %attend.2 = (bf16[2,32,512]{2,1,0:T(8,128)(2,1)S(1)}, bf16[2,32,512]{2,1,0:T(8,128)(2,1)S(1)}, bf16[2,32,512]{2,1,0:T(8,128)(2,1)S(1)}, bf16[2,32,512]{2,1,0:T(8...) custom-call(s32[3]{0:T(128)S(1)} %pad_add_fusion.scalars, ...), custom_call_target="tpu_custom_call" | custom-call | flops 1342177280 | bytes 2621440 | tf_op jit(solution)/shard_map/attend/pallas_call | solution.py:398
  74.9 8.9 %collective-permute-start.20 = (bf16[2,32,512]{2,1,0:T(8,128)(2,1)S(1)}, bf16[2,32,512]{2,1,0:T(8,128)(2,1)S(1)}, u32[]{:S(2)}, u32[]{:S(2)}) collective-permute-start(bf16[2,32,512]{2,1,0:T(8,128)(2,1)S(1)} %get-tuple-element.81), channel_id=1, source_target_pairs={{0,4},{2,6},{4,0},{6,2},{8,12},{10,14},{12,8},{14,10},{1,5},{3,7},... | collective-permute-start | bytes 196616 | tf_op jit(solution)/shard_map/ppermute | solution.py:468
  84.8 1.5 %collective-permute-start.22 = (bf16[2,32,512]{2,1,0:T(8,128)(2,1)S(1)}, bf16[2,32,512]{2,1,0:T(8,128)(2,1)S(1)}, u32[]{:S(2)}, u32[]{:S(2)}) collective-permute-start(bf16[2,32,512]{2,1,0:T(8,128)(2,1)S(1)} %get-tuple-element.83), channel_id=1, source_target_pairs={{0,8},{2,10},{4,12},{6,14},{8,0},{10,2},{12,4},{14,6},{1,9},{3,11}... | collective-permute-start | bytes 196616 | tf_op jit(solution)/shard_map/ppermute | solution.py:468
  86.3 1.5 %collective-permute-start.23 = (bf16[2,32,512]{2,1,0:T(8,128)(2,1)S(1)}, bf16[2,32,512]{2,1,0:T(8,128)(2,1)S(1)}, u32[]{:S(2)}, u32[]{:S(2)}) collective-permute-start(bf16[2,32,512]{2,1,0:T(8,128)(2,1)S(1)} %get-tuple-element.84), channel_id=1, source_target_pairs={{0,10},{2,8},{4,14},{6,12},{8,2},{10,0},{12,6},{14,4},{1,11},{3,9}... | collective-permute-start | bytes 196616 | tf_op jit(solution)/shard_map/ppermute | solution.py:468
  87.8 2.8 %attend.3 = (bf16[2,32,512]{2,1,0:T(8,128)(2,1)S(1)}, bf16[2,32,512]{2,1,0:T(8,128)(2,1)S(1)}, bf16[2,32,512]{2,1,0:T(8,128)(2,1)S(1)}, bf16[2,32,512]{2,1,0:T(8...) custom-call(s32[3]{0:T(128)S(1)} %pad_add_fusion.scalars, ...), custom_call_target="tpu_custom_call" | custom-call | flops 1342177280 | bytes 2621440 | tf_op jit(solution)/shard_map/attend/pallas_call | solution.py:398
  90.6 1.5 %collective-permute-start.24 = (bf16[2,32,512]{2,1,0:T(8,128)(2,1)S(1)}, bf16[2,32,512]{2,1,0:T(8,128)(2,1)S(1)}, u32[]{:S(2)}, u32[]{:S(2)}) collective-permute-start(bf16[2,32,512]{2,1,0:T(8,128)(2,1)S(1)} %get-tuple-element.85), channel_id=1, source_target_pairs={{0,12},{2,14},{4,8},{6,10},{8,4},{10,6},{12,0},{14,2},{1,13},{3,15... | collective-permute-start | bytes 196616 | tf_op jit(solution)/shard_map/ppermute | solution.py:468
  92.1 3.2 %collective-permute-start.25 = (bf16[2,32,512]{2,1,0:T(8,128)(2,1)S(1)}, bf16[2,32,512]{2,1,0:T(8,128)(2,1)S(1)}, u32[]{:S(2)}, u32[]{:S(2)}) collective-permute-start(bf16[2,32,512]{2,1,0:T(8,128)(2,1)S(1)} %get-tuple-element.86), channel_id=1, source_target_pairs={{0,14},{2,12},{4,10},{6,8},{8,6},{10,4},{12,2},{14,0},{1,15},{3,13... | collective-permute-start | bytes 196616 | tf_op jit(solution)/shard_map/ppermute | solution.py:468
  96.1 2.7 %collective-permute-start.14 = (bf16[2,32,512]{2,1,0:T(8,128)(2,1)S(1)}, bf16[2,32,512]{2,1,0:T(8,128)(2,1)S(1)}, u32[]{:S(2)}, u32[]{:S(2)}) collective-permute-start(bf16[2,32,512]{2,1,0:T(8,128)(2,1)S(1)} %get-tuple-element.75), channel_id=1, source_target_pairs={{0,6},{2,4},{4,2},{6,0},{8,14},{10,12},{12,10},{14,8},{1,7},{3,5},... | collective-permute-start | bytes 196616 | tf_op jit(solution)/shard_map/ppermute | solution.py:468
  99.5 2.3 %collective-permute-start.16 = (bf16[2,32,512]{2,1,0:T(8,128)(2,1)S(1)}, bf16[2,32,512]{2,1,0:T(8,128)(2,1)S(1)}, u32[]{:S(2)}, u32[]{:S(2)}) collective-permute-start(bf16[2,32,512]{2,1,0:T(8,128)(2,1)S(1)} %get-tuple-element.77), channel_id=1, source_target_pairs={{0,10},{2,8},{4,14},{6,12},{8,2},{10,0},{12,6},{14,4},{1,11},{3,9}... | collective-permute-start | bytes 196616 | tf_op jit(solution)/shard_map/ppermute | solution.py:468
  101.8 1.4 %collective-permute-start.17 = (bf16[2,32,512]{2,1,0:T(8,128)(2,1)S(1)}, bf16[2,32,512]{2,1,0:T(8,128)(2,1)S(1)}, u32[]{:S(2)}, u32[]{:S(2)}) collective-permute-start(bf16[2,32,512]{2,1,0:T(8,128)(2,1)S(1)} %get-tuple-element.78), channel_id=1, source_target_pairs={{0,12},{2,14},{4,8},{6,10},{8,4},{10,6},{12,0},{14,2},{1,13},{3,15... | collective-permute-start | bytes 196616 | tf_op jit(solution)/shard_map/ppermute | solution.py:468
  103.2 3.2 %collective-permute-start.18 = (bf16[2,32,512]{2,1,0:T(8,128)(2,1)S(1)}, bf16[2,32,512]{2,1,0:T(8,128)(2,1)S(1)}, u32[]{:S(2)}, u32[]{:S(2)}) collective-permute-start(bf16[2,32,512]{2,1,0:T(8,128)(2,1)S(1)} %get-tuple-element.79), channel_id=1, source_target_pairs={{0,14},{2,12},{4,10},{6,8},{8,6},{10,4},{12,2},{14,0},{1,15},{3,13... | collective-permute-start | bytes 196616 | tf_op jit(solution)/shard_map/ppermute | solution.py:468
  106.4 1.4 %collect.2.refs_8_ = bf16[2,16,32,512]{3,2,1,0:T(8,128)(2,1)} custom-call(s32[3]{0:T(128)S(1)} %pad_add_fusion.scalars, bf16[2,32,512]{2,1,0:T(8,128)(2,1)S(1)} %get-tuple-element.67.refs_0_, bf16[2,32,512]{2,1,0:T(8,128)(2,1)S(1)} %collective-permute-done.19.refs_1_, bf16[2,32,512]{2,1,0:T(8,128)(2,1)S(1)} %collective-permute-done.20.refs_2_, ...), custom_call_target="tpu_custom_call" | custom-call | tf_op jit(solution)/shard_map/collect/pallas_call | solution.py:424
  110.3 1.4 %collect.3 = bf16[2,16,32,512]{3,2,1,0:T(8,128)(2,1)} custom-call(s32[3]{0:T(128)S(1)} %pad_add_fusion.scalars, bf16[2,32,512]{2,1,0:T(8,128)(2,1)S(1)} %get-tuple-element.72.refs_0_, bf16[2,32,512]{2,1,0:T(8,128)(2,1)S(1)} %collective-permute-done.12.refs_1_, ...), custom_call_target="tpu_custom_call", output_to_operand_aliasing={{}: (9, {})} | custom-call | tf_op jit(solution)/shard_map/collect/pallas_call | solution.py:424
  (77 shorter events, 10.3 us)
Async XLA Ops:
  3.3 21.0 %collective-permute-start.1 = (bf16[4,10,16,512]{3,2,1,0:T(8,128)(2,1)S(1)}, bf16[4,10,16,512]{3,2,1,0:T(8,128)(2,1)S(1)}, u32[]{:S(2)}, u32[]{:S(2)}) collective-permute-start(bf16[4,10,16,512]{3,2,1,0:T(8,128)(2,1)S(1)} %get-tuple-element.47), channel_id=1, source_target_pairs={{0,2},{2,0},{4,6},{6,4},{8,10},{10,8},{12,14},{14,12},{1,3},{3,1},... | collective-permute-start | bytes 1966088 | tf_op jit(solution)/shard_map/ppermute | solution.py:468
  6.6 23.8 %copy-start.7 = (f32[512]{0:T(512)S(1)}, f32[512]{0:T(512)}, u32[]{:S(2)}) copy-start(f32[512]{0:T(512)} %param.14) | copy-start | bytes 6148
  6.7 23.8 %copy-start.8 = (f32[512]{0:T(512)S(1)}, f32[512]{0:T(512)}, u32[]{:S(2)}) copy-start(f32[512]{0:T(512)} %param.16) | copy-start | bytes 6148
  6.7 23.8 %copy-start.9 = (f32[512]{0:T(512)S(1)}, f32[512]{0:T(512)}, u32[]{:S(2)}) copy-start(f32[512]{0:T(512)} %param.18) | copy-start | bytes 6148
  6.7 23.8 %copy-start.5 = (bf16[3,512,512]{2,1,0:T(8,128)(2,1)S(1)}, bf16[3,512,512]{2,1,0:T(8,128)(2,1)}, u32[]{:S(2)}) copy-start(bf16[3,512,512]{2,1,0:T(8,128)(2,1)} %param.13) | copy-start | bytes 4718596
  6.7 23.8 %copy-start.6 = (bf16[3,512,512]{2,1,0:T(8,128)(2,1)S(1)}, bf16[3,512,512]{2,1,0:T(8,128)(2,1)}, u32[]{:S(2)}) copy-start(bf16[3,512,512]{2,1,0:T(8,128)(2,1)} %param.15) | copy-start | bytes 4718596
  6.9 16.6 %collective-permute-start.3 = (bf16[4,18,512]{2,1,0:T(8,128)(2,1)S(1)}, bf16[4,18,512]{2,1,0:T(8,128)(2,1)S(1)}, u32[]{:S(2)}, u32[]{:S(2)}) collective-permute-start(bf16[4,18,512]{2,1,0:T(8,128)(2,1)S(1)} %get-tuple-element.89), channel_id=1, source_target_pairs={{0,3},{1,2},{2,1},{3,0},{4,7},{5,6},{6,5},{7,4},{8,11},{9,10},{10,... | collective-permute-start | bytes 221192 | tf_op jit(solution)/shard_map/ppermute | solution.py:483
  6.9 16.6 %collective-permute-start.2 = (bf16[4,18,512]{2,1,0:T(8,128)(2,1)S(1)}, bf16[4,18,512]{2,1,0:T(8,128)(2,1)S(1)}, u32[]{:S(2)}, u32[]{:S(2)}) collective-permute-start(bf16[4,18,512]{2,1,0:T(8,128)(2,1)S(1)} %get-tuple-element.90), channel_id=1, source_target_pairs={{0,1},{1,0},{2,3},{3,2},{4,5},{5,4},{6,7},{7,6},{8,9},{9,8},{10,11... | collective-permute-start | bytes 221192 | tf_op jit(solution)/shard_map/ppermute | solution.py:477
  7.0 30.8 %collective-permute-start = (bf16[4,8,16,512]{3,2,1,0:T(8,128)(2,1)}, bf16[4,8,16,512]{3,2,1,0:T(8,128)(2,1)S(1)}, u32[]{:S(2)}, u32[]{:S(2)}) collective-permute-start(bf16[4,8,16,512]{3,2,1,0:T(8,128)(2,1)} %copy-done.14), channel_id=1, source_target_pairs={{0,2},{2,0},{4,6},{6,4},{8,10},{10,8},{12,14},{14,12},{1,3},{3,1},... | collective-permute-start | bytes 1572872 | tf_op jit(solution)/shard_map/ppermute | solution.py:468
  27.0 23.7 %collective-permute-start.5 = (bf16[3,11,16,512]{3,2,1,0:T(8,128)(2,1)S(1)}, bf16[3,11,16,512]{3,2,1,0:T(8,128)(2,1)S(1)}, u32[]{:S(2)}, u32[]{:S(2)}) collective-permute-start(bf16[3,11,16,512]{3,2,1,0:T(8,128)(2,1)S(1)} %get-tuple-element.50.last), channel_id=1, source_target_pairs={{0,4},{2,6},{4,8},{6,10},{8,12},{10,14},{1,5},{3,7},{5,9},{7,11},{... | collective-permute-start | bytes 1622024 | tf_op jit(solution)/shard_map/ppermute | solution.py:468
  32.9 28.5 %slice-start = ((s8[4718592]{0:T(1024)(128)(4,1)}), s8[4194304]{0:T(1024)(128)(4,1)S(1)}, s32[]{:S(2)}) async-start(s8[4718592]{0:T(1024)(128)(4,1)} %bitcast.26), calls=%async_computation | async-start | bytes 8388608
  40.2 21.1 %collective-permute-start.4 = (bf16[3,9,16,512]{3,2,1,0:T(8,128)(2,1)S(1)}, bf16[3,9,16,512]{3,2,1,0:T(8,128)(2,1)S(1)}, u32[]{:S(2)}, u32[]{:S(2)}) collective-permute-start(bf16[3,9,16,512]{3,2,1,0:T(8,128)(2,1)S(1)} %get-tuple-element.53.last), channel_id=1, source_target_pairs={{0,4},{2,6},{4,8},{6,10},{8,12},{10,14},{1,5},{3,7},{5,9},{7,11},{... | collective-permute-start | bytes 1327112 | tf_op jit(solution)/shard_map/ppermute | solution.py:468
  56.9 10.0 %collective-permute-start.6 = (bf16[4,32,512]{2,1,0:T(8,128)(2,1)S(1)}, bf16[4,32,512]{2,1,0:T(8,128)(2,1)S(1)}, u32[]{:S(2)}, u32[]{:S(2)}) collective-permute-start(bf16[4,32,512]{2,1,0:T(8,128)(2,1)S(1)} %get-tuple-element.64), channel_id=1, source_target_pairs={{0,4},{2,6},{4,0},{6,2},{8,12},{10,14},{12,8},{14,10},{1,5},{3,7},... | collective-permute-start | bytes 393224 | tf_op jit(solution)/shard_map/ppermute | solution.py:468
  58.5 13.0 %collective-permute-start.7 = (bf16[4,32,512]{2,1,0:T(8,128)(2,1)S(1)}, bf16[4,32,512]{2,1,0:T(8,128)(2,1)S(1)}, u32[]{:S(2)}, u32[]{:S(2)}) collective-permute-start(bf16[4,32,512]{2,1,0:T(8,128)(2,1)S(1)} %get-tuple-element.65), channel_id=1, source_target_pairs={{0,8},{2,10},{4,12},{6,14},{8,0},{10,2},{12,4},{14,6},{1,9},{3,11}... | collective-permute-start | bytes 393224 | tf_op jit(solution)/shard_map/ppermute | solution.py:468
  58.5 13.0 %collective-permute-start.8 = (bf16[4,32,512]{2,1,0:T(8,128)(2,1)S(1)}, bf16[4,32,512]{2,1,0:T(8,128)(2,1)S(1)}, u32[]{:S(2)}, u32[]{:S(2)}) collective-permute-start(bf16[4,32,512]{2,1,0:T(8,128)(2,1)S(1)} %get-tuple-element.66), channel_id=1, source_target_pairs={{0,12},{2,14},{4,8},{6,10},{8,4},{10,6},{12,0},{14,2},{1,13},{3,15... | collective-permute-start | bytes 393224 | tf_op jit(solution)/shard_map/ppermute | solution.py:468
  65.2 18.6 %collective-permute-start.9 = (bf16[4,32,512]{2,1,0:T(8,128)(2,1)S(1)}, bf16[4,32,512]{2,1,0:T(8,128)(2,1)S(1)}, u32[]{:S(2)}, u32[]{:S(2)}) collective-permute-start(bf16[4,32,512]{2,1,0:T(8,128)(2,1)S(1)} %get-tuple-element.69), channel_id=1, source_target_pairs={{0,4},{2,6},{4,0},{6,2},{8,12},{10,14},{12,8},{14,10},{1,5},{3,7},... | collective-permute-start | bytes 393224 | tf_op jit(solution)/shard_map/ppermute | solution.py:468
  65.9 18.8 %collective-permute-start.10 = (bf16[4,32,512]{2,1,0:T(8,128)(2,1)S(1)}, bf16[4,32,512]{2,1,0:T(8,128)(2,1)S(1)}, u32[]{:S(2)}, u32[]{:S(2)}) collective-permute-start(bf16[4,32,512]{2,1,0:T(8,128)(2,1)S(1)} %get-tuple-element.70), channel_id=1, source_target_pairs={{0,8},{2,10},{4,12},{6,14},{8,0},{10,2},{12,4},{14,6},{1,9},{3,11}... | collective-permute-start | bytes 393224 | tf_op jit(solution)/shard_map/ppermute | solution.py:468
  66.9 19.4 %collective-permute-start.11 = (bf16[4,32,512]{2,1,0:T(8,128)(2,1)S(1)}, bf16[4,32,512]{2,1,0:T(8,128)(2,1)S(1)}, u32[]{:S(2)}, u32[]{:S(2)}) collective-permute-start(bf16[4,32,512]{2,1,0:T(8,128)(2,1)S(1)} %get-tuple-element.71), channel_id=1, source_target_pairs={{0,12},{2,14},{4,8},{6,10},{8,4},{10,6},{12,0},{14,2},{1,13},{3,15... | collective-permute-start | bytes 393224 | tf_op jit(solution)/shard_map/ppermute | solution.py:468
  74.3 16.2 %collective-permute-start.19 = (bf16[2,32,512]{2,1,0:T(8,128)(2,1)S(1)}, bf16[2,32,512]{2,1,0:T(8,128)(2,1)S(1)}, u32[]{:S(2)}, u32[]{:S(2)}) collective-permute-start(bf16[2,32,512]{2,1,0:T(8,128)(2,1)S(1)} %get-tuple-element.80), channel_id=1, source_target_pairs={{0,2},{2,0},{4,6},{6,4},{8,10},{10,8},{12,14},{14,12},{1,3},{3,1},... | collective-permute-start | bytes 196616 | tf_op jit(solution)/shard_map/ppermute | solution.py:468
  74.9 17.2 %collective-permute-start.20 = (bf16[2,32,512]{2,1,0:T(8,128)(2,1)S(1)}, bf16[2,32,512]{2,1,0:T(8,128)(2,1)S(1)}, u32[]{:S(2)}, u32[]{:S(2)}) collective-permute-start(bf16[2,32,512]{2,1,0:T(8,128)(2,1)S(1)} %get-tuple-element.81), channel_id=1, source_target_pairs={{0,4},{2,6},{4,0},{6,2},{8,12},{10,14},{12,8},{14,10},{1,5},{3,7},... | collective-permute-start | bytes 196616 | tf_op jit(solution)/shard_map/ppermute | solution.py:468
  83.8 11.5 %collective-permute-start.21 = (bf16[2,32,512]{2,1,0:T(8,128)(2,1)S(1)}, bf16[2,32,512]{2,1,0:T(8,128)(2,1)S(1)}, u32[]{:S(2)}, u32[]{:S(2)}) collective-permute-start(bf16[2,32,512]{2,1,0:T(8,128)(2,1)S(1)} %get-tuple-element.82), channel_id=1, source_target_pairs={{0,6},{2,4},{4,2},{6,0},{8,14},{10,12},{12,10},{14,8},{1,7},{3,5},... | collective-permute-start | bytes 196616 | tf_op jit(solution)/shard_map/ppermute | solution.py:468
  84.8 11.2 %collective-permute-start.22 = (bf16[2,32,512]{2,1,0:T(8,128)(2,1)S(1)}, bf16[2,32,512]{2,1,0:T(8,128)(2,1)S(1)}, u32[]{:S(2)}, u32[]{:S(2)}) collective-permute-start(bf16[2,32,512]{2,1,0:T(8,128)(2,1)S(1)} %get-tuple-element.83), channel_id=1, source_target_pairs={{0,8},{2,10},{4,12},{6,14},{8,0},{10,2},{12,4},{14,6},{1,9},{3,11}... | collective-permute-start | bytes 196616 | tf_op jit(solution)/shard_map/ppermute | solution.py:468
  86.3 9.8 %collective-permute-start.23 = (bf16[2,32,512]{2,1,0:T(8,128)(2,1)S(1)}, bf16[2,32,512]{2,1,0:T(8,128)(2,1)S(1)}, u32[]{:S(2)}, u32[]{:S(2)}) collective-permute-start(bf16[2,32,512]{2,1,0:T(8,128)(2,1)S(1)} %get-tuple-element.84), channel_id=1, source_target_pairs={{0,10},{2,8},{4,14},{6,12},{8,2},{10,0},{12,6},{14,4},{1,11},{3,9}... | collective-permute-start | bytes 196616 | tf_op jit(solution)/shard_map/ppermute | solution.py:468
  90.6 8.2 %collective-permute-start.24 = (bf16[2,32,512]{2,1,0:T(8,128)(2,1)S(1)}, bf16[2,32,512]{2,1,0:T(8,128)(2,1)S(1)}, u32[]{:S(2)}, u32[]{:S(2)}) collective-permute-start(bf16[2,32,512]{2,1,0:T(8,128)(2,1)S(1)} %get-tuple-element.85), channel_id=1, source_target_pairs={{0,12},{2,14},{4,8},{6,10},{8,4},{10,6},{12,0},{14,2},{1,13},{3,15... | collective-permute-start | bytes 196616 | tf_op jit(solution)/shard_map/ppermute | solution.py:468
  92.1 7.4 %collective-permute-start.25 = (bf16[2,32,512]{2,1,0:T(8,128)(2,1)S(1)}, bf16[2,32,512]{2,1,0:T(8,128)(2,1)S(1)}, u32[]{:S(2)}, u32[]{:S(2)}) collective-permute-start(bf16[2,32,512]{2,1,0:T(8,128)(2,1)S(1)} %get-tuple-element.86), channel_id=1, source_target_pairs={{0,14},{2,12},{4,10},{6,8},{8,6},{10,4},{12,2},{14,0},{1,15},{3,13... | collective-permute-start | bytes 196616 | tf_op jit(solution)/shard_map/ppermute | solution.py:468
  95.3 6.5 %collective-permute-start.12 = (bf16[2,32,512]{2,1,0:T(8,128)(2,1)S(1)}, bf16[2,32,512]{2,1,0:T(8,128)(2,1)S(1)}, u32[]{:S(2)}, u32[]{:S(2)}) collective-permute-start(bf16[2,32,512]{2,1,0:T(8,128)(2,1)S(1)} %get-tuple-element.73), channel_id=1, source_target_pairs={{0,2},{2,0},{4,6},{6,4},{8,10},{10,8},{12,14},{14,12},{1,3},{3,1},... | collective-permute-start | bytes 196616 | tf_op jit(solution)/shard_map/ppermute | solution.py:468
  95.9 7.3 %collective-permute-start.13 = (bf16[2,32,512]{2,1,0:T(8,128)(2,1)S(1)}, bf16[2,32,512]{2,1,0:T(8,128)(2,1)S(1)}, u32[]{:S(2)}, u32[]{:S(2)}) collective-permute-start(bf16[2,32,512]{2,1,0:T(8,128)(2,1)S(1)} %get-tuple-element.74), channel_id=1, source_target_pairs={{0,4},{2,6},{4,0},{6,2},{8,12},{10,14},{12,8},{14,10},{1,5},{3,7},... | collective-permute-start | bytes 196616 | tf_op jit(solution)/shard_map/ppermute | solution.py:468
  96.1 11.8 %collective-permute-start.14 = (bf16[2,32,512]{2,1,0:T(8,128)(2,1)S(1)}, bf16[2,32,512]{2,1,0:T(8,128)(2,1)S(1)}, u32[]{:S(2)}, u32[]{:S(2)}) collective-permute-start(bf16[2,32,512]{2,1,0:T(8,128)(2,1)S(1)} %get-tuple-element.75), channel_id=1, source_target_pairs={{0,6},{2,4},{4,2},{6,0},{8,14},{10,12},{12,10},{14,8},{1,7},{3,5},... | collective-permute-start | bytes 196616 | tf_op jit(solution)/shard_map/ppermute | solution.py:468
  98.8 9.1 %collective-permute-start.15 = (bf16[2,32,512]{2,1,0:T(8,128)(2,1)S(1)}, bf16[2,32,512]{2,1,0:T(8,128)(2,1)S(1)}, u32[]{:S(2)}, u32[]{:S(2)}) collective-permute-start(bf16[2,32,512]{2,1,0:T(8,128)(2,1)S(1)} %get-tuple-element.76), channel_id=1, source_target_pairs={{0,8},{2,10},{4,12},{6,14},{8,0},{10,2},{12,4},{14,6},{1,9},{3,11}... | collective-permute-start | bytes 196616 | tf_op jit(solution)/shard_map/ppermute | solution.py:468
  99.5 9.7 %collective-permute-start.16 = (bf16[2,32,512]{2,1,0:T(8,128)(2,1)S(1)}, bf16[2,32,512]{2,1,0:T(8,128)(2,1)S(1)}, u32[]{:S(2)}, u32[]{:S(2)}) collective-permute-start(bf16[2,32,512]{2,1,0:T(8,128)(2,1)S(1)} %get-tuple-element.77), channel_id=1, source_target_pairs={{0,10},{2,8},{4,14},{6,12},{8,2},{10,0},{12,6},{14,4},{1,11},{3,9}... | collective-permute-start | bytes 196616 | tf_op jit(solution)/shard_map/ppermute | solution.py:468
  101.8 7.4 %collective-permute-start.17 = (bf16[2,32,512]{2,1,0:T(8,128)(2,1)S(1)}, bf16[2,32,512]{2,1,0:T(8,128)(2,1)S(1)}, u32[]{:S(2)}, u32[]{:S(2)}) collective-permute-start(bf16[2,32,512]{2,1,0:T(8,128)(2,1)S(1)} %get-tuple-element.78), channel_id=1, source_target_pairs={{0,12},{2,14},{4,8},{6,10},{8,4},{10,6},{12,0},{14,2},{1,13},{3,15... | collective-permute-start | bytes 196616 | tf_op jit(solution)/shard_map/ppermute | solution.py:468
  103.2 7.1 %collective-permute-start.18 = (bf16[2,32,512]{2,1,0:T(8,128)(2,1)S(1)}, bf16[2,32,512]{2,1,0:T(8,128)(2,1)S(1)}, u32[]{:S(2)}, u32[]{:S(2)}) collective-permute-start(bf16[2,32,512]{2,1,0:T(8,128)(2,1)S(1)} %get-tuple-element.79), channel_id=1, source_target_pairs={{0,14},{2,12},{4,10},{6,8},{8,6},{10,4},{12,2},{14,0},{1,15},{3,13... | collective-permute-start | bytes 196616 | tf_op jit(solution)/shard_map/ppermute | solution.py:468
  (12 other events, 79.9 us)

commit v10 on v9

--- a/solution.py
+++ b/solution.py
@@ -53,82 +53,90 @@
         copy.wait()
 
 
-def send_kernel(spans, half, scalars, video, *refs):
-    outs, sems = refs[:-1], refs[-1]
-    frames, height = video.shape[:2]
-    copies = []
-    for (begin, end), out in zip(spans, outs):
-        for source, here, count in rows_of(1 - scalars[0], begin, end, half, height):
-            copies.append(
-                pltpu.make_async_copy(
-                    video.at[:, pl.ds(source, count)],
-                    out.at[:, here : here + count],
-                    sems.at[len(copies)],
-                )
-            )
-    run(copies)
+def cut(target, video, frame, owner, begin, end, half):
+    for source, here, count in rows_of(owner, begin, end, half, video.shape[1]):
+        target[here : here + count] = video[frame, pl.ds(source, count)]
+
+
+def send_kernel(spans, half, scalars, video, *outs):
+    frames = video.shape[0]
+    rest = frames - taps
+    for k, (begin, end) in enumerate(spans):
+        for t in range(frames):
+            if k == 0:
+                target = outs[0].at[t - rest] if t >= rest else outs[1].at[t]
+            else:
+                target = outs[k + 1].at[t]
+            cut(target, video, t, 1 - scalars[0], begin, end, half)
 
 
 def send(scalars, video, spans, half):
     frames, _, width, channels = video.shape
-    shapes = [(frames, end - begin, width, channels) for begin, end in spans]
+    counts = [taps, frames - taps] + [frames] * (len(spans) - 1)
+    shapes = [
+        (count, end - begin, width, channels)
+        for count, (begin, end) in zip(counts, spans[:1] + spans)
+    ]
     return pl.pallas_call(
         partial(send_kernel, spans, half),
         out_shape=[jax.ShapeDtypeStruct(shape, video.dtype) for shape in shapes],
-        in_specs=[SMEM, ANY],
+        in_specs=[SMEM, VMEM],
         out_specs=[VMEM] * len(shapes),
-        scratch_shapes=[pltpu.SemaphoreType.DMA((3 * len(spans),))],
-        compiler_params=params(8),
+        compiler_params=params(12),
         name="send",
     )(scalars, video)
 
 
-def join_kernel(begin, end, half, scalars, video, received, own_edge, other_edge, first, last, sems):
-    frames, height = video.shape[:2]
-    rows = end - begin
-    split = first.shape[0]
-
-    def at(f):
-        return first.at[f] if f < split else last.at[f - split]
-
-    def copies(side):
-        made = []
-
-        def add(source, target):
-            made.append(pltpu.make_async_copy(source, target, sems.at[len(made)]))
-
+def join_last_kernel(begin, end, half, scalars, video, received, own_edge, other_edge, out):
+    frames, rows = video.shape[0], end - begin
+
+    @pl.when(scalars[0] == 0)
+    def _():
+        out[:, :rows] = received[received.shape[0] - taps :]
+        out[:, rows:] = other_edge[frames - taps :]
+
+    @pl.when(scalars[0] == 1)
+    def _():
+        for t in range(taps):
+            cut(out.at[t], video, frames - taps + t, 1, begin, end, half)
+        out[:, rows:] = own_edge[frames - taps :]
+
+
+def join_first_kernel(
+    begin, end, half, scalars, video, received, others, own_edge, other_edge, out
+):
+    frames, rows = video.shape[0], end - begin
+    rest = frames - taps
+
+    @pl.when(scalars[0] == 0)
+    def _():
         for t in range(frames):
-            mine, others = at(side * frames + t), at((1 - side) * frames + t)
-            for source, here, count in rows_of(side, begin, end, half, height):
-                add(video.at[t, pl.ds(source, count)], mine.at[here : here + count])
-            add(received.at[t], others.at[:rows])
-            add(own_edge.at[t], mine.at[rows:])
-            add(other_edge.at[t], others.at[rows:])
-        return made
-
-    for side in range(pair):
-
-        @pl.when(scalars[0] == side)
-        def _():
-            run(copies(side))
-
-
-def join(scalars, video, received, own_edge, other_edge, begin, end, half):
-    frames, _, width, channels = video.shape
-    rows = end - begin + own_edge.shape[1]
-    lasting = pair * frames - taps
+            cut(out.at[t], video, t, 0, begin, end, half)
+        out[:frames, rows:] = own_edge[...]
+        out[frames:, :rows] = others[:rest]
+        out[frames:, rows:] = other_edge[:rest]
+
+    @pl.when(scalars[0] == 1)
+    def _():
+        out[:rest, :rows] = others[:rest]
+        out[rest:frames, :rows] = received[received.shape[0] - taps :]
+        out[:frames, rows:] = other_edge[...]
+        for t in range(rest):
+            cut(out.at[frames + t], video, t, 1, begin, end, half)
+        out[frames:, rows:] = own_edge[:rest]
+
+
+def join(kernel, count, name, begin, end, half, scalars, video, *parts):
+    _, _, width, channels = video.shape
+    rows = end - begin + parts[-1].shape[1]
     return pl.pallas_call(
-        partial(join_kernel, begin, end, half),
-        out_shape=[
-            jax.ShapeDtypeStruct((count, rows, width, channels), jnp.bfloat16)
-            for count in (lasting, taps)
-        ],
-        in_specs=[SMEM] + [ANY] * 4,
-        out_specs=[VMEM] * 2,
-        scratch_shapes=[pltpu.SemaphoreType.DMA((6 * frames,))],
-        compiler_params=params(8),
-        name="join",
-    )(scalars, video, received, own_edge, other_edge)
+        partial(kernel, begin, end, half),
+        out_shape=jax.ShapeDtypeStruct((count, rows, width, channels), jnp.bfloat16),
+        in_specs=[SMEM] + [VMEM] * (1 + len(parts)),
+        out_specs=VMEM,
+        compiler_params=params(12),
+        name=name,
+    )(scalars, video, *parts)
 
 
 def place_rows(buffers, index, top, reduced, rows, width, column):
@@ -451,6 +459,7 @@
     scalars = jnp.stack([side, column, level])
     half = height // pair
     gain = gain.reshape(1, -1)
+    w_space = jnp.where(after(place, video) >= 0, w_space, 0)
     weights = [
         w_time.reshape(-1, channels), b_time.reshape(1, -1), w_down.reshape(-1, channels),
         b_down.reshape(1, -1), w_space, b_space.reshape(1, -1),
@@ -489,10 +498,14 @@
     ahead, halos = [], []
     kept = None
     for k, (begin, end) in enumerate(spans):
-        arrived = after(received[k], ahead[-1][1]) if ahead else received[k]
-        first, last = join(
-            scalars, video, arrived, edge_rows(own_edge, begin, end),
-            edge_rows(other_edge, begin, end), begin, end, half
+        edges = [edge_rows(edge, begin, end) for edge in (own_edge, other_edge)]
+        arrived, others = received[:2] if k == 0 else (received[k + 1], received[k + 1])
+        arrived = after(arrived, ahead[-1][1] if ahead else w_space)
+        place_of = (begin, end, half, scalars, video)
+        last = join(join_last_kernel, taps, "join_last", *place_of, arrived, *edges)
+        others = after(others, last) if k == 0 else arrived
+        first = join(
+            join_first_kernel, pair * frames - taps, "join_first", *place_of, arrived, others, *edges
         )
         halos.append(tm_permute(last, lambda i: i + pair))
         final = k == chunks - 1

time: 112 us -> 103 us (0.920)
  local copies, waits for them, and re-layouts: 9.98 us -> 3.73 us
  Pallas kernels: 31.4 us -> 28.7 us
  waiting for transfers between devices: 19.3 us -> 17 us
  other arithmetic: 0.85 us -> 2.99 us
    ppermute x1, waiting for transfers between devices: 14.4 us -> 6.52 us  [per_device(): other_edge = lax.ppermute(other_edge, ('tm', 'cols'), aslant)]
    unnamed x36 -> x26, local copies, waits for them, and re-layouts: 9.45 us -> 1.65 us
    ppermute x24 -> x25, waiting for transfers between devices: 4.85 us -> 10.5 us  [tm_permute(): lax.ppermute(value, 'tm', [(i, move(i)) for i in range(devices) if move(i...]
    select_n x0 -> x1, other arithmetic: none -> 2.79 us  [per_device(): w_space = jnp.where(after(place, video) >= 0, w_space, 0)]
    pallas_call x2 -> x4, Pallas kernels: 4.98 us -> 2.38 us  [join(): pl.pallas_call(partial(kernel, begin, end, half), out_shape=jax.ShapeDtyp...]
    slice x1, local copies, waits for them, and re-layouts: 0.41 us -> 1.95 us  [per_device(): border = jnp.where(column == 0, video[:, :, -1], video[:, :, 0])]
    ppermute x24 -> x25, starting transfers between devices: 49.6 us -> 49.4 us  [tm_permute(): lax.ppermute(value, 'tm', [(i, move(i)) for i in range(devices) if move(i...]
  transfers between devices with their start and end apart: 26 -> 27, of which waited for: 5 -> 6; matrix products, arithmetic and copies ran while one was open for 1% -> 5% of each run, Pallas kernels for 26% -> 26%
where the time goes in v10:
time: 103 us
  starting transfers between devices  49.6 us (48%)
  Pallas kernels  28.7 us (28%)
  waiting for transfers between devices  17 us (17%)
  local copies, waits for them, and re-layouts  3.73 us (4%)
  other arithmetic  2.99 us (3%)
    ppermute x25, starting transfers between devices, tm_permute(): lax.ppermute(value, 'tm', [(i, move(i)) for i in range(devices) if move(i...  49.4 us
    ppermute x25, waiting for transfers between devices, tm_permute(): lax.ppermute(value, 'tm', [(i, move(i)) for i in range(devices) if move(i...  10.5 us
    pallas_call x2, Pallas kernels, early(): pl.pallas_call(partial(early_kernel, kept is None, final, rows), out_shap...  9.6 us
    pallas_call x2, Pallas kernels, late(): pl.pallas_call(partial(late_kernel, owners, kept is None, final, rows), o...  7.72 us
    ppermute x1, waiting for transfers between devices, per_device(): other_edge = lax.ppermute(other_edge, ('tm', 'cols'), aslant)  6.52 us
    pallas_call x2, Pallas kernels, attend(): pl.pallas_call(partial(attend_kernel, frames_per, lanes, count), out_shap...  5.57 us
    select_n x1, other arithmetic, per_device(): w_space = jnp.where(after(place, video) >= 0, w_space, 0)  2.79 us
    pallas_call x2, Pallas kernels, collect(): pl.pallas_call(partial(collect_kernel, chunk * levels, chunks * levels),...  2.78 us
  transfers between devices with their start and end apart: 27, of which 6 were waited for; matrix products, arithmetic and copies ran while one was open for 5% of the time, Pallas kernels for 26%

profile of v10, /device:TPU:0, one launch (start us, length us, event | category | flops | bytes accessed | tf_op | source)
XLA Modules:
  0.0 102.6 jit_solution(445118804598303411)
XLA Ops:
  0.1 1.6 %copy-done = bf16[4,32,16,512]{3,2,1,0:T(8,128)(2,1)S(1)} copy-done((bf16[4,32,16,512]{3,2,1,0:T(8,128)(2,1)S(1)}, bf16[4,32,16,512]{3,2,1,0:T(8,128)(2,1)}, u32[]{:S(2)}) %copy-start) | copy-done | bytes 2097176
  2.3 3.0 %collective-permute-start.1 = (bf16[3,10,16,512]{3,2,1,0:T(8,128)(2,1)S(1)}, bf16[3,10,16,512]{3,2,1,0:T(8,128)(2,1)S(1)}, u32[]{:S(2)}, u32[]{:S(2)}) collective-permute-start(bf16[3,10,16,512]{3,2,1,0:T(8,128)(2,1)S(1)} %get-tuple-element.47), channel_id=1, source_target_pairs={{0,2},{2,0},{4,6},{6,4},{8,10},{10,8},{12,14},{14,12},{1,3},{3,1},... | collective-permute-start | bytes 1474568 | tf_op jit(solution)/shard_map/ppermute | solution.py:477
  5.3 1.9 %fusion.3 = (bf16[4,32,1,512]{3,2,1,0:T(2,128)(2,1)S(1)}, bf16[4,32,1,512]{3,2,1,0:T(2,128)(2,1)S(1)}) fusion(bf16[4,32,16,512]{3,2,1,0:T(8,128)(2,1)} %video.9), kind=kLoop, calls=%fused_computation.12 | loop fusion | bytes 524288 | tf_op jit(solution)/shard_map/slice | solution.py:481
  7.6 2.0 %collective-permute-start.2 = (bf16[1,10,16,512]{3,2,1,0:T(8,128)(2,1)S(1)}, bf16[1,10,16,512]{3,2,1,0:T(8,128)(2,1)S(1)}, u32[]{:S(2)}, u32[]{:S(2)}) collective-permute-start(bf16[1,10,16,512]{3,2,1,0:T(8,128)(2,1)S(1)} %get-tuple-element.50), channel_id=1, source_target_pairs={{0,2},{2,0},{4,6},{6,4},{8,10},{10,8},{12,14},{14,12},{1,3},{3,1},... | collective-permute-start | bytes 491528 | tf_op jit(solution)/shard_map/ppermute | solution.py:477
  9.7 2.8 %broadcast_select_fusion.w_space = bf16[9,512,512]{2,1,0:T(8,128)(2,1)S(1)} fusion(bf16[9,512,512]{2,1,0:T(8,128)(2,1)} %param.17, pred[]{:T(512)S(6)} %ge.3), kind=kLoop, calls=%fused_computation | loop fusion | flops 2359296 | bytes 9437185 | tf_op jit(solution)/shard_map/jit(_where)/select_n | solution.py:462
  12.5 6.5 %collective-permute-done.4 = bf16[4,18,512]{2,1,0:T(8,128)(2,1)S(1)} collective-permute-done((bf16[4,18,512]{2,1,0:T(8,128)(2,1)S(1)}, bf16[4,18,512]{2,1,0:T(8,128)(2,1)S(1)}, u32[]{:S(2)}, u32[]{:S(2)}) %collective-permute-start.4) | collective-permute-done | bytes 73760 | tf_op jit(solution)/shard_map/ppermute | solution.py:492
  19.9 3.5 %collective-permute-start.6 = (bf16[3,11,16,512]{3,2,1,0:T(8,128)(2,1)S(1)}, bf16[3,11,16,512]{3,2,1,0:T(8,128)(2,1)S(1)}, u32[]{:S(2)}, u32[]{:S(2)}) collective-permute-start(bf16[3,11,16,512]{3,2,1,0:T(8,128)(2,1)S(1)} %join_last.2.last), channel_id=1, source_target_pairs={{0,4},{2,6},{4,8},{6,10},{8,12},{10,14},{1,5},{3,7},{5,9},{7,11},{... | collective-permute-start | bytes 1622024 | tf_op jit(solution)/shard_map/ppermute | solution.py:477
  24.1 5.0 %early.2 = (f32[176,512]{1,0:T(8,128)S(1)}, bf16[2,128,512]{2,1,0:T(8,128)(2,1)S(1)}, bf16[3,2,2,16,512]{4,3,2,1,0:T(8,128)(2,1)S(1)}) custom-call(s32[3]{0:T(128)S(1)} %pad_add_fusion.scalars, bf16[5,11,16,512]{3,2,1,0:T(8,128)(2,1)S(1)} %join_first.2.first, bf16[3,11,16,512]{3,2,1,0:T(8,128)(2,1)S(1)} %join_last.2.last, bf16[1536,512]{1,0:T(8,128)(2,1)S(1)} %bitcast.26, ...), custom_call_target="tpu_custom_call" | custom-call | flops 3607101440 | bytes 9312256 | tf_op jit(solution)/shard_map/early/pallas_call | solution.py:245
  29.1 4.3 %collective-permute-done.received.others = bf16[4,8,16,512]{3,2,1,0:T(8,128)(2,1)S(1)} collective-permute-done((bf16[4,8,16,512]{3,2,1,0:T(8,128)(2,1)S(1)}, bf16[4,8,16,512]{3,2,1,0:T(8,128)(2,1)S(1)}, u32[]{:S(2)}, u32[]{:S(2)}) %collective-permute-start) | collective-permute-done | bytes 524320 | tf_op jit(solution)/shard_map/ppermute | solution.py:477
  34.6 3.7 %collective-permute-start.5 = (bf16[3,9,16,512]{3,2,1,0:T(8,128)(2,1)S(1)}, bf16[3,9,16,512]{3,2,1,0:T(8,128)(2,1)S(1)}, u32[]{:S(2)}, u32[]{:S(2)}) collective-permute-start(bf16[3,9,16,512]{3,2,1,0:T(8,128)(2,1)S(1)} %join_last.3.last), channel_id=1, source_target_pairs={{0,4},{2,6},{4,8},{6,10},{8,12},{10,14},{1,5},{3,7},{5,9},{7,11},{... | collective-permute-start | bytes 1327112 | tf_op jit(solution)/shard_map/ppermute | solution.py:477
  38.3 4.6 %early.3 = (f32[144,512]{1,0:T(8,128)S(1)}, bf16[2,128,512]{2,1,0:T(8,128)(2,1)S(1)}) custom-call(s32[3]{0:T(128)S(1)} %pad_add_fusion.scalars, bf16[5,9,16,512]{3,2,1,0:T(8,128)(2,1)S(1)} %join_first.3.first, bf16[3,9,16,512]{3,2,1,0:T(8,128)(2,1)S(1)} %join_last.3.last, bf16[1536,512]{1,0:T(8,128)(2,1)S(1)} %bitcast.27, f32[1,512]{1,0:T(1,128)S(1)} %bitcast.35, ...), custom_call_target="tpu_custom_call" | custom-call | flops 3170893824 | bytes 9050112 | tf_op jit(solution)/shard_map/early/pallas_call | solution.py:245
  43.0 3.9 %late.2 = (bf16[4,32,512]{2,1,0:T(8,128)(2,1)S(1)}, bf16[4,32,512]{2,1,0:T(8,128)(2,1)S(1)}, bf16[4,32,512]{2,1,0:T(8,128)(2,1)S(1)}, bf16[4,32,512]{2,1,0:T(8,128)(2,1)S(1)}, bf16[3,2,2,16,512]{4,3,2,1,0:T(8,128)(2,1)S(1)}) custom-call(s32[3]{0:T(128)S(1)} %pad_add_fusion.scalars, bf16[3,11,16,512]{3,2,1,0:T(8,128)(2,1)S(1)} %collective-permute-done.6.halo, ...), custom_call_target="tpu_custom_call" | custom-call | flops 2407530496 | bytes 9672704 | tf_op jit(solution)/shard_map/late/pallas_call | solution.py:316
  46.9 1.6 %collective-permute-start.7 = (bf16[4,32,512]{2,1,0:T(8,128)(2,1)S(1)}, bf16[4,32,512]{2,1,0:T(8,128)(2,1)S(1)}, u32[]{:S(2)}, u32[]{:S(2)}) collective-permute-start(bf16[4,32,512]{2,1,0:T(8,128)(2,1)S(1)} %get-tuple-element.64), channel_id=1, source_target_pairs={{0,4},{2,6},{4,0},{6,2},{8,12},{10,14},{12,8},{14,10},{1,5},{3,7},... | collective-permute-start | bytes 393224 | tf_op jit(solution)/shard_map/ppermute | solution.py:477
  49.6 1.7 %collective-permute-start.9 = (bf16[4,32,512]{2,1,0:T(8,128)(2,1)S(1)}, bf16[4,32,512]{2,1,0:T(8,128)(2,1)S(1)}, u32[]{:S(2)}, u32[]{:S(2)}) collective-permute-start(bf16[4,32,512]{2,1,0:T(8,128)(2,1)S(1)} %get-tuple-element.66), channel_id=1, source_target_pairs={{0,12},{2,14},{4,8},{6,10},{8,4},{10,6},{12,0},{14,2},{1,13},{3,15... | collective-permute-start | bytes 393224 | tf_op jit(solution)/shard_map/ppermute | solution.py:477
  51.4 3.8 %late.3 = (bf16[4,32,512]{2,1,0:T(8,128)(2,1)S(1)}, bf16[4,32,512]{2,1,0:T(8,128)(2,1)S(1)}, bf16[4,32,512]{2,1,0:T(8,128)(2,1)S(1)}, bf16[4,32,512]{2,1,0:T(8,128)(2,1)S(1)}) custom-call(s32[3]{0:T(128)S(1)} %pad_add_fusion.scalars, bf16[3,9,16,512]{3,2,1,0:T(8,128)(2,1)S(1)} %collective-permute-done.5.halo, bf16[5,9,16,512]{3,2,1,0:T(8,128)(2,1)S(1)} %join_first.3.first, ...), custom_call_target="tpu_custom_call" | custom-call | flops 2189426688 | bytes 9345024 | tf_op jit(solution)/shard_map/late/pallas_call | solution.py:316
  55.9 2.0 %collective-permute-start.11 = (bf16[4,32,512]{2,1,0:T(8,128)(2,1)S(1)}, bf16[4,32,512]{2,1,0:T(8,128)(2,1)S(1)}, u32[]{:S(2)}, u32[]{:S(2)}) collective-permute-start(bf16[4,32,512]{2,1,0:T(8,128)(2,1)S(1)} %get-tuple-element.70), channel_id=1, source_target_pairs={{0,8},{2,10},{4,12},{6,14},{8,0},{10,2},{12,4},{14,6},{1,9},{3,11}... | collective-permute-start | bytes 393224 | tf_op jit(solution)/shard_map/ppermute | solution.py:477
  57.9 1.7 %collective-permute-start.12 = (bf16[4,32,512]{2,1,0:T(8,128)(2,1)S(1)}, bf16[4,32,512]{2,1,0:T(8,128)(2,1)S(1)}, u32[]{:S(2)}, u32[]{:S(2)}) collective-permute-start(bf16[4,32,512]{2,1,0:T(8,128)(2,1)S(1)} %get-tuple-element.71), channel_id=1, source_target_pairs={{0,12},{2,14},{4,8},{6,10},{8,4},{10,6},{12,0},{14,2},{1,13},{3,15... | collective-permute-start | bytes 393224 | tf_op jit(solution)/shard_map/ppermute | solution.py:477
  61.0 2.8 %attend.2 = (bf16[2,32,512]{2,1,0:T(8,128)(2,1)S(1)}, bf16[2,32,512]{2,1,0:T(8,128)(2,1)S(1)}, bf16[2,32,512]{2,1,0:T(8,128)(2,1)S(1)}, bf16[2,32,512]{2,1,0:T(8...) custom-call(s32[3]{0:T(128)S(1)} %pad_add_fusion.scalars, ...), custom_call_target="tpu_custom_call" | custom-call | flops 1342177280 | bytes 2621440 | tf_op jit(solution)/shard_map/attend/pallas_call | solution.py:406
  63.8 1.6 %collective-permute-start.20 = (bf16[2,32,512]{2,1,0:T(8,128)(2,1)S(1)}, bf16[2,32,512]{2,1,0:T(8,128)(2,1)S(1)}, u32[]{:S(2)}, u32[]{:S(2)}) collective-permute-start(bf16[2,32,512]{2,1,0:T(8,128)(2,1)S(1)} %get-tuple-element.80), channel_id=1, source_target_pairs={{0,2},{2,0},{4,6},{6,4},{8,10},{10,8},{12,14},{14,12},{1,3},{3,1},... | collective-permute-start | bytes 196616 | tf_op jit(solution)/shard_map/ppermute | solution.py:477
  65.4 8.3 %collective-permute-start.21 = (bf16[2,32,512]{2,1,0:T(8,128)(2,1)S(1)}, bf16[2,32,512]{2,1,0:T(8,128)(2,1)S(1)}, u32[]{:S(2)}, u32[]{:S(2)}) collective-permute-start(bf16[2,32,512]{2,1,0:T(8,128)(2,1)S(1)} %get-tuple-element.81), channel_id=1, source_target_pairs={{0,4},{2,6},{4,0},{6,2},{8,12},{10,14},{12,8},{14,10},{1,5},{3,7},... | collective-permute-start | bytes 196616 | tf_op jit(solution)/shard_map/ppermute | solution.py:477
  73.7 2.4 %collective-permute-start.23 = (bf16[2,32,512]{2,1,0:T(8,128)(2,1)S(1)}, bf16[2,32,512]{2,1,0:T(8,128)(2,1)S(1)}, u32[]{:S(2)}, u32[]{:S(2)}) collective-permute-start(bf16[2,32,512]{2,1,0:T(8,128)(2,1)S(1)} %get-tuple-element.83), channel_id=1, source_target_pairs={{0,8},{2,10},{4,12},{6,14},{8,0},{10,2},{12,4},{14,6},{1,9},{3,11}... | collective-permute-start | bytes 196616 | tf_op jit(solution)/shard_map/ppermute | solution.py:477
  76.2 1.4 %collective-permute-start.24 = (bf16[2,32,512]{2,1,0:T(8,128)(2,1)S(1)}, bf16[2,32,512]{2,1,0:T(8,128)(2,1)S(1)}, u32[]{:S(2)}, u32[]{:S(2)}) collective-permute-start(bf16[2,32,512]{2,1,0:T(8,128)(2,1)S(1)} %get-tuple-element.84), channel_id=1, source_target_pairs={{0,10},{2,8},{4,14},{6,12},{8,2},{10,0},{12,6},{14,4},{1,11},{3,9}... | collective-permute-start | bytes 196616 | tf_op jit(solution)/shard_map/ppermute | solution.py:477
  77.6 2.8 %attend.3 = (bf16[2,32,512]{2,1,0:T(8,128)(2,1)S(1)}, bf16[2,32,512]{2,1,0:T(8,128)(2,1)S(1)}, bf16[2,32,512]{2,1,0:T(8,128)(2,1)S(1)}, bf16[2,32,512]{2,1,0:T(8...) custom-call(s32[3]{0:T(128)S(1)} %pad_add_fusion.scalars, ...), custom_call_target="tpu_custom_call" | custom-call | flops 1342177280 | bytes 2621440 | tf_op jit(solution)/shard_map/attend/pallas_call | solution.py:406
  80.4 2.0 %collective-permute-start.25 = (bf16[2,32,512]{2,1,0:T(8,128)(2,1)S(1)}, bf16[2,32,512]{2,1,0:T(8,128)(2,1)S(1)}, u32[]{:S(2)}, u32[]{:S(2)}) collective-permute-start(bf16[2,32,512]{2,1,0:T(8,128)(2,1)S(1)} %get-tuple-element.85), channel_id=1, source_target_pairs={{0,12},{2,14},{4,8},{6,10},{8,4},{10,6},{12,0},{14,2},{1,13},{3,15... | collective-permute-start | bytes 196616 | tf_op jit(solution)/shard_map/ppermute | solution.py:477
  82.4 2.0 %collective-permute-start.26 = (bf16[2,32,512]{2,1,0:T(8,128)(2,1)S(1)}, bf16[2,32,512]{2,1,0:T(8,128)(2,1)S(1)}, u32[]{:S(2)}, u32[]{:S(2)}) collective-permute-start(bf16[2,32,512]{2,1,0:T(8,128)(2,1)S(1)} %get-tuple-element.86), channel_id=1, source_target_pairs={{0,14},{2,12},{4,10},{6,8},{8,6},{10,4},{12,2},{14,0},{1,15},{3,13... | collective-permute-start | bytes 196616 | tf_op jit(solution)/shard_map/ppermute | solution.py:477
  84.3 1.4 %collective-permute-start.13 = (bf16[2,32,512]{2,1,0:T(8,128)(2,1)S(1)}, bf16[2,32,512]{2,1,0:T(8,128)(2,1)S(1)}, u32[]{:S(2)}, u32[]{:S(2)}) collective-permute-start(bf16[2,32,512]{2,1,0:T(8,128)(2,1)S(1)} %get-tuple-element.73), channel_id=1, source_target_pairs={{0,2},{2,0},{4,6},{6,4},{8,10},{10,8},{12,14},{14,12},{1,3},{3,1},... | collective-permute-start | bytes 196616 | tf_op jit(solution)/shard_map/ppermute | solution.py:477
  86.0 1.9 %collective-permute-start.15 = (bf16[2,32,512]{2,1,0:T(8,128)(2,1)S(1)}, bf16[2,32,512]{2,1,0:T(8,128)(2,1)S(1)}, u32[]{:S(2)}, u32[]{:S(2)}) collective-permute-start(bf16[2,32,512]{2,1,0:T(8,128)(2,1)S(1)} %get-tuple-element.75), channel_id=1, source_target_pairs={{0,6},{2,4},{4,2},{6,0},{8,14},{10,12},{12,10},{14,8},{1,7},{3,5},... | collective-permute-start | bytes 196616 | tf_op jit(solution)/shard_map/ppermute | solution.py:477
  89.3 2.2 %collective-permute-start.17 = (bf16[2,32,512]{2,1,0:T(8,128)(2,1)S(1)}, bf16[2,32,512]{2,1,0:T(8,128)(2,1)S(1)}, u32[]{:S(2)}, u32[]{:S(2)}) collective-permute-start(bf16[2,32,512]{2,1,0:T(8,128)(2,1)S(1)} %get-tuple-element.77), channel_id=1, source_target_pairs={{0,10},{2,8},{4,14},{6,12},{8,2},{10,0},{12,6},{14,4},{1,11},{3,9}... | collective-permute-start | bytes 196616 | tf_op jit(solution)/shard_map/ppermute | solution.py:477
  91.6 2.5 %collective-permute-start.18 = (bf16[2,32,512]{2,1,0:T(8,128)(2,1)S(1)}, bf16[2,32,512]{2,1,0:T(8,128)(2,1)S(1)}, u32[]{:S(2)}, u32[]{:S(2)}) collective-permute-start(bf16[2,32,512]{2,1,0:T(8,128)(2,1)S(1)} %get-tuple-element.78), channel_id=1, source_target_pairs={{0,12},{2,14},{4,8},{6,10},{8,4},{10,6},{12,0},{14,2},{1,13},{3,15... | collective-permute-start | bytes 196616 | tf_op jit(solution)/shard_map/ppermute | solution.py:477
  94.1 1.7 %collective-permute-start.19 = (bf16[2,32,512]{2,1,0:T(8,128)(2,1)S(1)}, bf16[2,32,512]{2,1,0:T(8,128)(2,1)S(1)}, u32[]{:S(2)}, u32[]{:S(2)}) collective-permute-start(bf16[2,32,512]{2,1,0:T(8,128)(2,1)S(1)} %get-tuple-element.79), channel_id=1, source_target_pairs={{0,14},{2,12},{4,10},{6,8},{8,6},{10,4},{12,2},{14,0},{1,15},{3,13... | collective-permute-start | bytes 196616 | tf_op jit(solution)/shard_map/ppermute | solution.py:477
  97.8 3.3 %collective-permute-done.19.refs_7_ = bf16[2,32,512]{2,1,0:T(8,128)(2,1)S(1)} collective-permute-done((bf16[2,32,512]{2,1,0:T(8,128)(2,1)S(1)}, bf16[2,32,512]{2,1,0:T(8,128)(2,1)S(1)}, u32[]{:S(2)}, u32[]{:S(2)}) %collective-permute-start.19) | collective-permute-done | bytes 65568 | tf_op jit(solution)/shard_map/ppermute | solution.py:477
  101.0 1.4 %collect.3 = bf16[2,16,32,512]{3,2,1,0:T(8,128)(2,1)} custom-call(s32[3]{0:T(128)S(1)} %pad_add_fusion.scalars, bf16[2,32,512]{2,1,0:T(8,128)(2,1)S(1)} %get-tuple-element.72.refs_0_, bf16[2,32,512]{2,1,0:T(8,128)(2,1)S(1)} %collective-permute-done.13.refs_1_, ...), custom_call_target="tpu_custom_call", output_to_operand_aliasing={{}: (9, {})} | custom-call | tf_op jit(solution)/shard_map/collect/pallas_call | solution.py:432
  (71 shorter events, 10.5 us)
Async XLA Ops:
  2.3 16.9 %collective-permute-start.1 = (bf16[3,10,16,512]{3,2,1,0:T(8,128)(2,1)S(1)}, bf16[3,10,16,512]{3,2,1,0:T(8,128)(2,1)S(1)}, u32[]{:S(2)}, u32[]{:S(2)}) collective-permute-start(bf16[3,10,16,512]{3,2,1,0:T(8,128)(2,1)S(1)} %get-tuple-element.47), channel_id=1, source_target_pairs={{0,2},{2,0},{4,6},{6,4},{8,10},{10,8},{12,14},{14,12},{1,3},{3,1},... | collective-permute-start | bytes 1474568 | tf_op jit(solution)/shard_map/ppermute | solution.py:477
  7.4 11.6 %collective-permute-start.4 = (bf16[4,18,512]{2,1,0:T(8,128)(2,1)S(1)}, bf16[4,18,512]{2,1,0:T(8,128)(2,1)S(1)}, u32[]{:S(2)}, u32[]{:S(2)}) collective-permute-start(bf16[4,18,512]{2,1,0:T(8,128)(2,1)S(1)} %get-tuple-element.89), channel_id=1, source_target_pairs={{0,3},{1,2},{2,1},{3,0},{4,7},{5,6},{6,5},{7,4},{8,11},{9,10},{10,... | collective-permute-start | bytes 221192 | tf_op jit(solution)/shard_map/ppermute | solution.py:492
  7.5 11.6 %collective-permute-start.3 = (bf16[4,18,512]{2,1,0:T(8,128)(2,1)S(1)}, bf16[4,18,512]{2,1,0:T(8,128)(2,1)S(1)}, u32[]{:S(2)}, u32[]{:S(2)}) collective-permute-start(bf16[4,18,512]{2,1,0:T(8,128)(2,1)S(1)} %get-tuple-element.90), channel_id=1, source_target_pairs={{0,1},{1,0},{2,3},{3,2},{4,5},{5,4},{6,7},{7,6},{8,9},{9,8},{10,11... | collective-permute-start | bytes 221192 | tf_op jit(solution)/shard_map/ppermute | solution.py:486
  7.6 15.7 %collective-permute-start.2 = (bf16[1,10,16,512]{3,2,1,0:T(8,128)(2,1)S(1)}, bf16[1,10,16,512]{3,2,1,0:T(8,128)(2,1)S(1)}, u32[]{:S(2)}, u32[]{:S(2)}) collective-permute-start(bf16[1,10,16,512]{3,2,1,0:T(8,128)(2,1)S(1)} %get-tuple-element.50), channel_id=1, source_target_pairs={{0,2},{2,0},{4,6},{6,4},{8,10},{10,8},{12,14},{14,12},{1,3},{3,1},... | collective-permute-start | bytes 491528 | tf_op jit(solution)/shard_map/ppermute | solution.py:477
  9.6 23.8 %collective-permute-start = (bf16[4,8,16,512]{3,2,1,0:T(8,128)(2,1)S(1)}, bf16[4,8,16,512]{3,2,1,0:T(8,128)(2,1)S(1)}, u32[]{:S(2)}, u32[]{:S(2)}) collective-permute-start(bf16[4,8,16,512]{3,2,1,0:T(8,128)(2,1)S(1)} %get-tuple-element.46), channel_id=1, source_target_pairs={{0,2},{2,0},{4,6},{6,4},{8,10},{10,8},{12,14},{14,12},{1,3},{3,1},... | collective-permute-start | bytes 1572872 | tf_op jit(solution)/shard_map/ppermute | solution.py:477
  12.5 11.5 %copy-start.2 = (bf16[3,512,512]{2,1,0:T(8,128)(2,1)S(1)}, bf16[3,512,512]{2,1,0:T(8,128)(2,1)}, u32[]{:S(2)}) copy-start(bf16[3,512,512]{2,1,0:T(8,128)(2,1)} %param.13) | copy-start | bytes 4718596
  12.5 11.5 %copy-start.3 = (bf16[3,512,512]{2,1,0:T(8,128)(2,1)S(1)}, bf16[3,512,512]{2,1,0:T(8,128)(2,1)}, u32[]{:S(2)}) copy-start(bf16[3,512,512]{2,1,0:T(8,128)(2,1)} %param.15) | copy-start | bytes 4718596
  12.5 11.5 %copy-start.4 = (f32[512]{0:T(512)S(1)}, f32[512]{0:T(512)}, u32[]{:S(2)}) copy-start(f32[512]{0:T(512)} %param.14) | copy-start | bytes 6148
  12.5 11.5 %copy-start.5 = (f32[512]{0:T(512)S(1)}, f32[512]{0:T(512)}, u32[]{:S(2)}) copy-start(f32[512]{0:T(512)} %param.16) | copy-start | bytes 6148
  12.5 11.5 %copy-start.6 = (f32[512]{0:T(512)S(1)}, f32[512]{0:T(512)}, u32[]{:S(2)}) copy-start(f32[512]{0:T(512)} %param.18) | copy-start | bytes 6148
  19.9 23.1 %collective-permute-start.6 = (bf16[3,11,16,512]{3,2,1,0:T(8,128)(2,1)S(1)}, bf16[3,11,16,512]{3,2,1,0:T(8,128)(2,1)S(1)}, u32[]{:S(2)}, u32[]{:S(2)}) collective-permute-start(bf16[3,11,16,512]{3,2,1,0:T(8,128)(2,1)S(1)} %join_last.2.last), channel_id=1, source_target_pairs={{0,4},{2,6},{4,8},{6,10},{8,12},{10,14},{1,5},{3,7},{5,9},{7,11},{... | collective-permute-start | bytes 1622024 | tf_op jit(solution)/shard_map/ppermute | solution.py:477
  34.6 16.7 %collective-permute-start.5 = (bf16[3,9,16,512]{3,2,1,0:T(8,128)(2,1)S(1)}, bf16[3,9,16,512]{3,2,1,0:T(8,128)(2,1)S(1)}, u32[]{:S(2)}, u32[]{:S(2)}) collective-permute-start(bf16[3,9,16,512]{3,2,1,0:T(8,128)(2,1)S(1)} %join_last.3.last), channel_id=1, source_target_pairs={{0,4},{2,6},{4,8},{6,10},{8,12},{10,14},{1,5},{3,7},{5,9},{7,11},{... | collective-permute-start | bytes 1327112 | tf_op jit(solution)/shard_map/ppermute | solution.py:477
  46.9 11.0 %collective-permute-start.7 = (bf16[4,32,512]{2,1,0:T(8,128)(2,1)S(1)}, bf16[4,32,512]{2,1,0:T(8,128)(2,1)S(1)}, u32[]{:S(2)}, u32[]{:S(2)}) collective-permute-start(bf16[4,32,512]{2,1,0:T(8,128)(2,1)S(1)} %get-tuple-element.64), channel_id=1, source_target_pairs={{0,4},{2,6},{4,0},{6,2},{8,12},{10,14},{12,8},{14,10},{1,5},{3,7},... | collective-permute-start | bytes 393224 | tf_op jit(solution)/shard_map/ppermute | solution.py:477
  48.5 12.5 %collective-permute-start.8 = (bf16[4,32,512]{2,1,0:T(8,128)(2,1)S(1)}, bf16[4,32,512]{2,1,0:T(8,128)(2,1)S(1)}, u32[]{:S(2)}, u32[]{:S(2)}) collective-permute-start(bf16[4,32,512]{2,1,0:T(8,128)(2,1)S(1)} %get-tuple-element.65), channel_id=1, source_target_pairs={{0,8},{2,10},{4,12},{6,14},{8,0},{10,2},{12,4},{14,6},{1,9},{3,11}... | collective-permute-start | bytes 393224 | tf_op jit(solution)/shard_map/ppermute | solution.py:477
  49.6 11.4 %collective-permute-start.9 = (bf16[4,32,512]{2,1,0:T(8,128)(2,1)S(1)}, bf16[4,32,512]{2,1,0:T(8,128)(2,1)S(1)}, u32[]{:S(2)}, u32[]{:S(2)}) collective-permute-start(bf16[4,32,512]{2,1,0:T(8,128)(2,1)S(1)} %get-tuple-element.66), channel_id=1, source_target_pairs={{0,12},{2,14},{4,8},{6,10},{8,4},{10,6},{12,0},{14,2},{1,13},{3,15... | collective-permute-start | bytes 393224 | tf_op jit(solution)/shard_map/ppermute | solution.py:477
  55.2 18.5 %collective-permute-start.10 = (bf16[4,32,512]{2,1,0:T(8,128)(2,1)S(1)}, bf16[4,32,512]{2,1,0:T(8,128)(2,1)S(1)}, u32[]{:S(2)}, u32[]{:S(2)}) collective-permute-start(bf16[4,32,512]{2,1,0:T(8,128)(2,1)S(1)} %get-tuple-element.69), channel_id=1, source_target_pairs={{0,4},{2,6},{4,0},{6,2},{8,12},{10,14},{12,8},{14,10},{1,5},{3,7},... | collective-permute-start | bytes 393224 | tf_op jit(solution)/shard_map/ppermute | solution.py:477
  55.9 17.8 %collective-permute-start.11 = (bf16[4,32,512]{2,1,0:T(8,128)(2,1)S(1)}, bf16[4,32,512]{2,1,0:T(8,128)(2,1)S(1)}, u32[]{:S(2)}, u32[]{:S(2)}) collective-permute-start(bf16[4,32,512]{2,1,0:T(8,128)(2,1)S(1)} %get-tuple-element.70), channel_id=1, source_target_pairs={{0,8},{2,10},{4,12},{6,14},{8,0},{10,2},{12,4},{14,6},{1,9},{3,11}... | collective-permute-start | bytes 393224 | tf_op jit(solution)/shard_map/ppermute | solution.py:477
  57.9 18.3 %collective-permute-start.12 = (bf16[4,32,512]{2,1,0:T(8,128)(2,1)S(1)}, bf16[4,32,512]{2,1,0:T(8,128)(2,1)S(1)}, u32[]{:S(2)}, u32[]{:S(2)}) collective-permute-start(bf16[4,32,512]{2,1,0:T(8,128)(2,1)S(1)} %get-tuple-element.71), channel_id=1, source_target_pairs={{0,12},{2,14},{4,8},{6,10},{8,4},{10,6},{12,0},{14,2},{1,13},{3,15... | collective-permute-start | bytes 393224 | tf_op jit(solution)/shard_map/ppermute | solution.py:477
  63.8 16.5 %collective-permute-start.20 = (bf16[2,32,512]{2,1,0:T(8,128)(2,1)S(1)}, bf16[2,32,512]{2,1,0:T(8,128)(2,1)S(1)}, u32[]{:S(2)}, u32[]{:S(2)}) collective-permute-start(bf16[2,32,512]{2,1,0:T(8,128)(2,1)S(1)} %get-tuple-element.80), channel_id=1, source_target_pairs={{0,2},{2,0},{4,6},{6,4},{8,10},{10,8},{12,14},{14,12},{1,3},{3,1},... | collective-permute-start | bytes 196616 | tf_op jit(solution)/shard_map/ppermute | solution.py:477
  65.4 17.0 %collective-permute-start.21 = (bf16[2,32,512]{2,1,0:T(8,128)(2,1)S(1)}, bf16[2,32,512]{2,1,0:T(8,128)(2,1)S(1)}, u32[]{:S(2)}, u32[]{:S(2)}) collective-permute-start(bf16[2,32,512]{2,1,0:T(8,128)(2,1)S(1)} %get-tuple-element.81), channel_id=1, source_target_pairs={{0,4},{2,6},{4,0},{6,2},{8,12},{10,14},{12,8},{14,10},{1,5},{3,7},... | collective-permute-start | bytes 196616 | tf_op jit(solution)/shard_map/ppermute | solution.py:477
  73.7 10.6 %collective-permute-start.22 = (bf16[2,32,512]{2,1,0:T(8,128)(2,1)S(1)}, bf16[2,32,512]{2,1,0:T(8,128)(2,1)S(1)}, u32[]{:S(2)}, u32[]{:S(2)}) collective-permute-start(bf16[2,32,512]{2,1,0:T(8,128)(2,1)S(1)} %get-tuple-element.82), channel_id=1, source_target_pairs={{0,6},{2,4},{4,2},{6,0},{8,14},{10,12},{12,10},{14,8},{1,7},{3,5},... | collective-permute-start | bytes 196616 | tf_op jit(solution)/shard_map/ppermute | solution.py:477
  73.7 12.0 %collective-permute-start.23 = (bf16[2,32,512]{2,1,0:T(8,128)(2,1)S(1)}, bf16[2,32,512]{2,1,0:T(8,128)(2,1)S(1)}, u32[]{:S(2)}, u32[]{:S(2)}) collective-permute-start(bf16[2,32,512]{2,1,0:T(8,128)(2,1)S(1)} %get-tuple-element.83), channel_id=1, source_target_pairs={{0,8},{2,10},{4,12},{6,14},{8,0},{10,2},{12,4},{14,6},{1,9},{3,11}... | collective-permute-start | bytes 196616 | tf_op jit(solution)/shard_map/ppermute | solution.py:477
  76.2 9.8 %collective-permute-start.24 = (bf16[2,32,512]{2,1,0:T(8,128)(2,1)S(1)}, bf16[2,32,512]{2,1,0:T(8,128)(2,1)S(1)}, u32[]{:S(2)}, u32[]{:S(2)}) collective-permute-start(bf16[2,32,512]{2,1,0:T(8,128)(2,1)S(1)} %get-tuple-element.84), channel_id=1, source_target_pairs={{0,10},{2,8},{4,14},{6,12},{8,2},{10,0},{12,6},{14,4},{1,11},{3,9}... | collective-permute-start | bytes 196616 | tf_op jit(solution)/shard_map/ppermute | solution.py:477
  80.4 7.5 %collective-permute-start.25 = (bf16[2,32,512]{2,1,0:T(8,128)(2,1)S(1)}, bf16[2,32,512]{2,1,0:T(8,128)(2,1)S(1)}, u32[]{:S(2)}, u32[]{:S(2)}) collective-permute-start(bf16[2,32,512]{2,1,0:T(8,128)(2,1)S(1)} %get-tuple-element.85), channel_id=1, source_target_pairs={{0,12},{2,14},{4,8},{6,10},{8,4},{10,6},{12,0},{14,2},{1,13},{3,15... | collective-permute-start | bytes 196616 | tf_op jit(solution)/shard_map/ppermute | solution.py:477
  82.4 7.0 %collective-permute-start.26 = (bf16[2,32,512]{2,1,0:T(8,128)(2,1)S(1)}, bf16[2,32,512]{2,1,0:T(8,128)(2,1)S(1)}, u32[]{:S(2)}, u32[]{:S(2)}) collective-permute-start(bf16[2,32,512]{2,1,0:T(8,128)(2,1)S(1)} %get-tuple-element.86), channel_id=1, source_target_pairs={{0,14},{2,12},{4,10},{6,8},{8,6},{10,4},{12,2},{14,0},{1,15},{3,13... | collective-permute-start | bytes 196616 | tf_op jit(solution)/shard_map/ppermute | solution.py:477
  84.3 7.3 %collective-permute-start.13 = (bf16[2,32,512]{2,1,0:T(8,128)(2,1)S(1)}, bf16[2,32,512]{2,1,0:T(8,128)(2,1)S(1)}, u32[]{:S(2)}, u32[]{:S(2)}) collective-permute-start(bf16[2,32,512]{2,1,0:T(8,128)(2,1)S(1)} %get-tuple-element.73), channel_id=1, source_target_pairs={{0,2},{2,0},{4,6},{6,4},{8,10},{10,8},{12,14},{14,12},{1,3},{3,1},... | collective-permute-start | bytes 196616 | tf_op jit(solution)/shard_map/ppermute | solution.py:477
  85.7 8.3 %collective-permute-start.14 = (bf16[2,32,512]{2,1,0:T(8,128)(2,1)S(1)}, bf16[2,32,512]{2,1,0:T(8,128)(2,1)S(1)}, u32[]{:S(2)}, u32[]{:S(2)}) collective-permute-start(bf16[2,32,512]{2,1,0:T(8,128)(2,1)S(1)} %get-tuple-element.74), channel_id=1, source_target_pairs={{0,4},{2,6},{4,0},{6,2},{8,12},{10,14},{12,8},{14,10},{1,5},{3,7},... | collective-permute-start | bytes 196616 | tf_op jit(solution)/shard_map/ppermute | solution.py:477
  86.0 11.2 %collective-permute-start.15 = (bf16[2,32,512]{2,1,0:T(8,128)(2,1)S(1)}, bf16[2,32,512]{2,1,0:T(8,128)(2,1)S(1)}, u32[]{:S(2)}, u32[]{:S(2)}) collective-permute-start(bf16[2,32,512]{2,1,0:T(8,128)(2,1)S(1)} %get-tuple-element.75), channel_id=1, source_target_pairs={{0,6},{2,4},{4,2},{6,0},{8,14},{10,12},{12,10},{14,8},{1,7},{3,5},... | collective-permute-start | bytes 196616 | tf_op jit(solution)/shard_map/ppermute | solution.py:477
  87.8 9.4 %collective-permute-start.16 = (bf16[2,32,512]{2,1,0:T(8,128)(2,1)S(1)}, bf16[2,32,512]{2,1,0:T(8,128)(2,1)S(1)}, u32[]{:S(2)}, u32[]{:S(2)}) collective-permute-start(bf16[2,32,512]{2,1,0:T(8,128)(2,1)S(1)} %get-tuple-element.76), channel_id=1, source_target_pairs={{0,8},{2,10},{4,12},{6,14},{8,0},{10,2},{12,4},{14,6},{1,9},{3,11}... | collective-permute-start | bytes 196616 | tf_op jit(solution)/shard_map/ppermute | solution.py:477
  89.3 7.9 %collective-permute-start.17 = (bf16[2,32,512]{2,1,0:T(8,128)(2,1)S(1)}, bf16[2,32,512]{2,1,0:T(8,128)(2,1)S(1)}, u32[]{:S(2)}, u32[]{:S(2)}) collective-permute-start(bf16[2,32,512]{2,1,0:T(8,128)(2,1)S(1)} %get-tuple-element.77), channel_id=1, source_target_pairs={{0,10},{2,8},{4,14},{6,12},{8,2},{10,0},{12,6},{14,4},{1,11},{3,9}... | collective-permute-start | bytes 196616 | tf_op jit(solution)/shard_map/ppermute | solution.py:477
  91.6 6.2 %collective-permute-start.18 = (bf16[2,32,512]{2,1,0:T(8,128)(2,1)S(1)}, bf16[2,32,512]{2,1,0:T(8,128)(2,1)S(1)}, u32[]{:S(2)}, u32[]{:S(2)}) collective-permute-start(bf16[2,32,512]{2,1,0:T(8,128)(2,1)S(1)} %get-tuple-element.78), channel_id=1, source_target_pairs={{0,12},{2,14},{4,8},{6,10},{8,4},{10,6},{12,0},{14,2},{1,13},{3,15... | collective-permute-start | bytes 196616 | tf_op jit(solution)/shard_map/ppermute | solution.py:477
  94.1 7.0 %collective-permute-start.19 = (bf16[2,32,512]{2,1,0:T(8,128)(2,1)S(1)}, bf16[2,32,512]{2,1,0:T(8,128)(2,1)S(1)}, u32[]{:S(2)}, u32[]{:S(2)}) collective-permute-start(bf16[2,32,512]{2,1,0:T(8,128)(2,1)S(1)} %get-tuple-element.79), channel_id=1, source_target_pairs={{0,14},{2,12},{4,10},{6,8},{8,6},{10,4},{12,2},{14,0},{1,15},{3,13... | collective-permute-start | bytes 196616 | tf_op jit(solution)/shard_map/ppermute | solution.py:477
  (8 other events, 68.8 us)

commit v11 on v10

--- a/solution.py
+++ b/solution.py
@@ -63,19 +63,16 @@
     rest = frames - taps
     for k, (begin, end) in enumerate(spans):
         for t in range(frames):
-            if k == 0:
-                target = outs[0].at[t - rest] if t >= rest else outs[1].at[t]
-            else:
-                target = outs[k + 1].at[t]
+            target = outs[k].at[t - rest] if t >= rest else outs[len(spans) + k].at[t]
             cut(target, video, t, 1 - scalars[0], begin, end, half)
 
 
 def send(scalars, video, spans, half):
     frames, _, width, channels = video.shape
-    counts = [taps, frames - taps] + [frames] * (len(spans) - 1)
     shapes = [
         (count, end - begin, width, channels)
-        for count, (begin, end) in zip(counts, spans[:1] + spans)
+        for count in (taps, frames - taps)
+        for begin, end in spans
     ]
     return pl.pallas_call(
         partial(send_kernel, spans, half),
@@ -92,7 +89,7 @@
 
     @pl.when(scalars[0] == 0)
     def _():
-        out[:, :rows] = received[received.shape[0] - taps :]
+        out[:, :rows] = received[...]
         out[:, rows:] = other_edge[frames - taps :]
 
     @pl.when(scalars[0] == 1)
@@ -113,13 +110,13 @@
         for t in range(frames):
             cut(out.at[t], video, t, 0, begin, end, half)
         out[:frames, rows:] = own_edge[...]
-        out[frames:, :rows] = others[:rest]
+        out[frames:, :rows] = others[...]
         out[frames:, rows:] = other_edge[:rest]
 
     @pl.when(scalars[0] == 1)
     def _():
-        out[:rest, :rows] = others[:rest]
-        out[rest:frames, :rows] = received[received.shape[0] - taps :]
+        out[:rest, :rows] = others[...]
+        out[rest:frames, :rows] = received[...]
         out[:frames, rows:] = other_edge[...]
         for t in range(rest):
             cut(out.at[frames + t], video, t, 1, begin, end, half)
@@ -169,7 +166,7 @@
             buffers[:, :, :1] = jnp.zeros((3, frames, 1, width, channels), jnp.bfloat16)
 
     else:
-        buffers[:, :, :2] = kept[...]
+        buffers[:, :, :2] = kept
     if last:
 
         @pl.when(side == pair - 1)
@@ -177,7 +174,7 @@
             buffers[:, :, size + 1 :] = jnp.zeros((3, frames, 1, width, channels), jnp.bfloat16)
 
     else:
-        keeps[...] = buffers[:, :, size:]
+        keeps(buffers[:, :, size:])
 
     def window(b, a):
         return buffers[b, :, a : a + size].reshape(frames * size * width, channels)
@@ -189,13 +186,11 @@
 
 
 def early_kernel(
-    fresh, final, rows, scalars, first, last, w_time, b_time, w_down, b_down, w_space, b_space, *refs
+    final, rows, scalars, first, last, w_time, b_time, w_down, b_down, w_space, b_space, *refs
 ):
-    refs = list(refs)
-    kept = None if fresh else refs.pop(0)
     part, spatial = refs[:2]
-    keeps = None if final else refs[2]
     lifted, buffers = refs[-2:]
+    keeps = None if final else (lambda value: refs[2].__setitem__(..., value))
     split, depth, width, channels = first.shape
     count = split + taps
     halves = count // 2
@@ -225,16 +220,15 @@
     reduced = (dot32(lhs, w_down[...]) + b_down[...]).astype(jnp.bfloat16)
     for index in range(len(whole)):
         value = reduced[index * pixels : (index + 1) * pixels]
-        place_rows(buffers, index, 0 if fresh else 2, value, rows, width, scalars[1])
-    spatial[...] = convolve(buffers, fresh, final, scalars[0], kept, keeps, w_space, b_space)
-
-
-def early(scalars, first, last, kept, final, size, rows, *weights):
+        place_rows(buffers, index, 0, value, rows, width, scalars[1])
+    spatial[...] = convolve(buffers, True, final, scalars[0], None, keeps, w_space, b_space)
+
+
+def early(scalars, first, last, final, size, rows, *weights):
     split, depth, width, channels = first.shape
     halves = (split + taps) // 2
     pixels = depth * width
     later = halves - 2
-    given = [] if kept is None else [kept]
     shapes = [
         jax.ShapeDtypeStruct((pixels, channels), jnp.float32),
         jax.ShapeDtypeStruct((later, size * width, channels), jnp.bfloat16),
@@ -243,9 +237,9 @@
         shapes.append(jax.ShapeDtypeStruct((3, later, 2, width, channels), jnp.bfloat16))
     flops = 2 * channels * channels * (pixels * 26 + 9 * later * size * width)
     return pl.pallas_call(
-        partial(early_kernel, kept is None, final, rows),
+        partial(early_kernel, final, rows),
         out_shape=shapes,
-        in_specs=[SMEM] + [VMEM] * (2 + len(weights) + len(given)),
+        in_specs=[SMEM] + [VMEM] * (2 + len(weights)),
         out_specs=[VMEM] * len(shapes),
         scratch_shapes=[
             pltpu.VMEM((2 * halves, pixels, channels), jnp.bfloat16),
@@ -254,23 +248,111 @@
         compiler_params=params(24),
         cost_estimate=cost(flops, first, last, *weights),
         name="early",
-    )(scalars, first, last, *weights, *given)
+    )(scalars, first, last, *weights)
+
+
+def full_kernel(
+    owners, final, rows, scalars, halo, first, last, kept_late, kept_early, w_time, b_time, w_down,
+    b_down, w_space, b_space, *refs
+):
+    outs = refs[:owners]
+    keeps = None if final else refs[owners : owners + 2]
+    lifted, buffers = refs[-2:]
+    split, depth, width, channels = first.shape
+    count = split + taps
+    halves = count // 2
+    pixels = depth * width
+
+    def frame(t):
+        if t < 0:
+            value = halo[t + taps].reshape(pixels, channels)
+            return jnp.where(scalars[2] > 0, value, jnp.zeros_like(value))
+        return (first[t] if t < split else last[t - split]).reshape(pixels, channels)
+
+    starts = list(range(-1, count))
+    for low in range(0, len(starts), 3):
+        group = starts[low : low + 3]
+        lhs = jnp.concatenate(
+            [jnp.concatenate([frame(t - k) for t in group], axis=0) for k in range(taps)], axis=1
+        )
+        acc = dot32(lhs, w_time[...]) + b_time[...]
+        held = jnp.concatenate([frame(t) for t in group], axis=0).astype(jnp.float32)
+        value = held + silu(acc)
+        for g, t in enumerate(group):
+            piece = value[g * pixels : (g + 1) * pixels]
+            if t < 0:
+                piece = jnp.where(scalars[2] > 0, piece, 0.0)
+            lifted[t + 1] = piece.astype(jnp.bfloat16)
+    lhs = jnp.concatenate(
+        [
+            jnp.concatenate([lifted[2 * s + 2 - k] for s in range(halves)], axis=0)
+            for k in range(taps)
+        ],
+        axis=1,
+    )
+    reduced = (dot32(lhs, w_down[...]) + b_down[...]).astype(jnp.bfloat16)
+    for index in range(halves):
+        value = reduced[index * pixels : (index + 1) * pixels]
+        place_rows(buffers, index, 2, value, rows, width, scalars[1])
+    kept = jnp.concatenate([kept_late[...], kept_early[...]], axis=1)
+    keep = None if final else (lambda value: keep_both(keeps, value))
+    result = convolve(buffers, False, final, scalars[0], kept, keep, w_space, b_space)
+    each = result.shape[1] // owners
+    if owners == 1:
+        outs[0][...] = result
+    else:
+        for j in range(owners):
+            part = result[:, j * each : (j + 1) * each]
+            for m in range(owners):
+
+                @pl.when((scalars[2] ^ m) == j)
+                def _():
+                    outs[m][...] = part
+
+
+def keep_both(keeps, value):
+    keeps[0][...] = value[:, :2]
+    keeps[1][...] = value[:, 2:]
+
+
+def full(owners, scalars, halo, first, last, kept, final, size, rows, *weights):
+    split, depth, width, channels = first.shape
+    halves = (split + taps) // 2
+    pixels = depth * width
+    shapes = [(halves, size * width // owners, channels)] * owners
+    if not final:
+        shapes += [(3, count, 2, width, channels) for count in (2, halves - 2)]
+    flops = 2 * channels * channels * (pixels * 39 + 9 * halves * size * width)
+    return pl.pallas_call(
+        partial(full_kernel, owners, final, rows),
+        out_shape=[jax.ShapeDtypeStruct(shape, jnp.bfloat16) for shape in shapes],
+        in_specs=[SMEM] + [VMEM] * (5 + len(weights)),
+        out_specs=[VMEM] * len(shapes),
+        scratch_shapes=[
+            pltpu.VMEM((2 * halves + 1, pixels, channels), jnp.bfloat16),
+            pltpu.VMEM((3, halves, size + 2, width, channels), jnp.bfloat16),
+        ],
+        compiler_params=params(28),
+        cost_estimate=cost(flops, halo, first, last, *weights),
+        name="full",
+    )(scalars, halo, first, last, *kept, *weights)
 
 
 def late_kernel(
-    owners, fresh, final, rows, scalars, halo, first, part, spatial, w_time, b_time, w_down, b_down,
+    owners, final, rows, scalars, halo, first, part, spatial, w_time, b_time, w_down, b_down,
     w_space, b_space, *refs
 ):
-    refs = list(refs)
-    kept = None if fresh else refs.pop(0)
     outs = refs[:owners]
-    keeps = None if final else refs[owners]
+    keeps = None if final else (lambda value: refs[owners].__setitem__(..., value))
     lifted, buffers, result = refs[-3:]
     _, depth, width, channels = first.shape
     pixels = depth * width
 
     def frame(t):
-        return (halo[t + taps] if t < 0 else first[t]).reshape(pixels, channels)
+        if t < 0:
+            value = halo[t + taps].reshape(pixels, channels)
+            return jnp.where(scalars[2] > 0, value, jnp.zeros_like(value))
+        return first[t].reshape(pixels, channels)
 
     group = range(-1, taps - 1)
     lhs = jnp.concatenate(
@@ -291,8 +373,8 @@
     )
     for index, value in enumerate(reduced):
         value = value.astype(jnp.bfloat16)
-        place_rows(buffers, index, 0 if fresh else 2, value, rows, width, scalars[1])
-    result[:2] = convolve(buffers, fresh, final, scalars[0], kept, keeps, w_space, b_space)
+        place_rows(buffers, index, 0, value, rows, width, scalars[1])
+    result[:2] = convolve(buffers, True, final, scalars[0], None, keeps, w_space, b_space)
     result[2:] = spatial[...]
     each = result.shape[1] // owners
     if owners == 1:
@@ -303,20 +385,19 @@
             out[...] = result[:, pl.ds(begin, each)]
 
 
-def late(owners, scalars, halo, first, part, spatial, kept, final, rows, *weights):
+def late(owners, scalars, halo, first, part, spatial, final, rows, *weights):
     _, depth, width, channels = first.shape
     later, pixels = spatial.shape[:2]
     halves = later + 2
     size = pixels // width
-    given = [] if kept is None else [kept]
     shapes = [(halves, pixels // owners, channels)] * owners
     if not final:
         shapes.append((3, 2, 2, width, channels))
     flops = 2 * channels * channels * (depth * width * 13 + 18 * pixels)
     return pl.pallas_call(
-        partial(late_kernel, owners, kept is None, final, rows),
+        partial(late_kernel, owners, final, rows),
         out_shape=[jax.ShapeDtypeStruct(shape, jnp.bfloat16) for shape in shapes],
-        in_specs=[SMEM] + [VMEM] * (4 + len(weights) + len(given)),
+        in_specs=[SMEM] + [VMEM] * (4 + len(weights)),
         out_specs=[VMEM] * len(shapes),
         scratch_shapes=[
             pltpu.VMEM((taps, depth * width, channels), jnp.bfloat16),
@@ -326,7 +407,7 @@
         compiler_params=params(24),
         cost_estimate=cost(flops, halo, first, part, *weights),
         name="late",
-    )(scalars, halo, first, part, spatial, *weights, *given)
+    )(scalars, halo, first, part, spatial, *weights)
 
 
 def attend_kernel(frames_per, lanes, count, scalars, *refs):
@@ -495,37 +576,40 @@
         cut = jnp.pad(edge[:, begin:end], ((0, 0), (0, -(end - begin) % width), (0, 0)))
         return cut.reshape(frames, -1, width, channels)
 
-    ahead, halos = [], []
+    owners = levels if direct else 1
+    edges = [[edge_rows(e, begin, end) for e in (own_edge, other_edge)] for begin, end in spans]
+    lasts, halos = [], []
+    newest = w_space
+    for k, (begin, end) in enumerate(spans):
+        newest = join(
+            join_last_kernel, taps, "join_last", begin, end, half, scalars, video,
+            after(received[k], newest), *edges[k]
+        )
+        lasts.append(newest)
+        halos.append(tm_permute(newest, lambda i: (i + pair) % devices))
+
+    spatials = []
     kept = None
     for k, (begin, end) in enumerate(spans):
-        edges = [edge_rows(edge, begin, end) for edge in (own_edge, other_edge)]
-        arrived, others = received[:2] if k == 0 else (received[k + 1], received[k + 1])
-        arrived = after(arrived, ahead[-1][1] if ahead else w_space)
-        place_of = (begin, end, half, scalars, video)
-        last = join(join_last_kernel, taps, "join_last", *place_of, arrived, *edges)
-        others = after(others, last) if k == 0 else arrived
+        rows, final = end - begin, k == chunks - 1
+        others = after(received[chunks + k], newest)
         first = join(
-            join_first_kernel, pair * frames - taps, "join_first", *place_of, arrived, others, *edges
+            join_first_kernel, pair * frames - taps, "join_first", begin, end, half, scalars,
+            video, received[k], others, *edges[k]
         )
-        halos.append(tm_permute(last, lambda i: i + pair))
-        final = k == chunks - 1
-        made = early(scalars, first, last, kept, final, size, end - begin, *weights)
-        kept = None if final else made[2]
-        ahead.append((first, made[0], made[1]))
-
-    spatials = []
-    kept = None
-    owners = levels if direct else 1
-    for k, (begin, end) in enumerate(spans):
-        first, part, spatial = ahead[k]
-        if spatials:
-            part = after(part, spatials[-1][0])
-        final = k == chunks - 1
-        made = late(
-            owners, scalars, halos[k], first, part, spatial, kept, final, end - begin, *weights
-        )
+        if k == 0:
+            part, spatial, *kept = early(scalars, first, lasts[k], final, size, rows, *weights)
+            made = late(
+                owners, scalars, halos[k], first, part, spatial, final, rows, *weights
+            )
+            kept = [*made[owners:], *kept]
+        else:
+            made = full(
+                owners, scalars, halos[k], first, lasts[k], kept, final, size, rows, *weights
+            )
+            kept = made[owners:]
         spatials.append(made[:owners])
-        kept = None if final else made[owners]
+        newest = made[0]
 
     newest = spatials[-1][0]
     if direct:

time: 103 us -> 98.3 us (0.954)
  starting transfers between devices: 49.6 us -> 44.4 us
  waiting for transfers between devices: 17 us -> 18.8 us
  Pallas kernels: 28.7 us -> 27.6 us
    ppermute x25 -> x26, starting transfers between devices: 49.4 us -> 44.2 us  [tm_permute(): lax.ppermute(value, 'tm', [(i, move(i)) for i in range(devices) if move(i...]
    ppermute x25 -> x26, waiting for transfers between devices: 10.5 us -> 12.2 us  [tm_permute(): lax.ppermute(value, 'tm', [(i, move(i)) for i in range(devices) if move(i...]
    pallas_call x4 -> x3, Pallas kernels: 17.3 us -> 16.3 us  [the longest x1 7.32 us: full(): pl.pallas_call(partial(full_kernel, owners, final, rows), out_shape=[jax....]
  transfers between devices with their start and end apart: 27 -> 28, of which waited for: 6 -> 6; matrix products, arithmetic and copies ran while one was open for 5% -> 5% of each run, Pallas kernels for 26% -> 26%
where the time goes in v11:
time: 98.3 us; the launch traced here: 98.1 us
  starting transfers between devices  44.4 us (45%)
  Pallas kernels  27.6 us (28%)
  waiting for transfers between devices  18.8 us (19%)
  local copies, waits for them, and re-layouts  3.74 us (4%)
  other arithmetic  2.99 us (3%)
    ppermute x26, starting transfers between devices, tm_permute(): lax.ppermute(value, 'tm', [(i, move(i)) for i in range(devices) if move(i...  44.2 us
    ppermute x26, waiting for transfers between devices, tm_permute(): lax.ppermute(value, 'tm', [(i, move(i)) for i in range(devices) if move(i...  12.2 us
    pallas_call x1, Pallas kernels, full(): pl.pallas_call(partial(full_kernel, owners, final, rows), out_shape=[jax....  7.32 us
    ppermute x1, waiting for transfers between devices, per_device(): other_edge = lax.ppermute(other_edge, ('tm', 'cols'), aslant)  6.56 us
    pallas_call x2, Pallas kernels, attend(): pl.pallas_call(partial(attend_kernel, frames_per, lanes, count), out_shap...  5.57 us
    pallas_call x1, Pallas kernels, early(): pl.pallas_call(partial(early_kernel, final, rows), out_shape=shapes, in_s...  5.02 us
    pallas_call x1, Pallas kernels, late(): pl.pallas_call(partial(late_kernel, owners, final, rows), out_shape=[jax....  3.92 us
    select_n x1, other arithmetic, per_device(): w_space = jnp.where(after(place, video) >= 0, w_space, 0)  2.79 us
  transfers between devices with their start and end apart: 28, of which 6 were waited for; matrix products, arithmetic and copies ran while one was open for 5% of the time, Pallas kernels for 26%

profile of v11, /device:TPU:0, one launch (start us, length us, event | category | flops | bytes accessed | tf_op | source)
XLA Modules:
  0.0 98.1 jit_solution(3593015821242584570)
XLA Ops:
  0.1 1.6 %copy-done = bf16[4,32,16,512]{3,2,1,0:T(8,128)(2,1)S(1)} copy-done((bf16[4,32,16,512]{3,2,1,0:T(8,128)(2,1)S(1)}, bf16[4,32,16,512]{3,2,1,0:T(8,128)(2,1)}, u32[]{:S(2)}) %copy-start) | copy-done | bytes 2097176
  1.7 0.6 send.1
  2.3 3.0 %collective-permute-start.1 = (bf16[3,10,16,512]{3,2,1,0:T(8,128)(2,1)S(1)}, bf16[3,10,16,512]{3,2,1,0:T(8,128)(2,1)S(1)}, u32[]{:S(2)}, u32[]{:S(2)}) collective-permute-start(bf16[3,10,16,512]{3,2,1,0:T(8,128)(2,1)S(1)} %get-tuple-element.46), channel_id=1, source_target_pairs={{0,2},{2,0},{4,6},{6,4},{8,10},{10,8},{12,14},{14,12},{1,3},{3,1},... | collective-permute-start | bytes 1474568 | tf_op jit(solution)/shard_map/ppermute | solution.py:558
  5.3 1.9 %fusion.3 = (bf16[4,32,1,512]{3,2,1,0:T(2,128)(2,1)S(1)}, bf16[4,32,1,512]{3,2,1,0:T(2,128)(2,1)S(1)}) fusion(bf16[4,32,16,512]{3,2,1,0:T(8,128)(2,1)} %video.9), kind=kLoop, calls=%fused_computation.12 | loop fusion | bytes 524288 | tf_op jit(solution)/shard_map/slice | solution.py:562
  7.7 2.0 %collective-permute-start = (bf16[3,8,16,512]{3,2,1,0:T(8,128)(2,1)S(1)}, bf16[3,8,16,512]{3,2,1,0:T(8,128)(2,1)S(1)}, u32[]{:S(2)}, u32[]{:S(2)}) collective-permute-start(bf16[3,8,16,512]{3,2,1,0:T(8,128)(2,1)S(1)} %get-tuple-element.45), channel_id=1, source_target_pairs={{0,2},{2,0},{4,6},{6,4},{8,10},{10,8},{12,14},{14,12},{1,3},{3,1},... | collective-permute-start | bytes 1179656 | tf_op jit(solution)/shard_map/ppermute | solution.py:558
  9.7 2.8 %broadcast_select_fusion.w_space = bf16[9,512,512]{2,1,0:T(8,128)(2,1)S(1)} fusion(bf16[9,512,512]{2,1,0:T(8,128)(2,1)} %param.17, pred[]{:T(512)S(6)} %ge.3), kind=kLoop, calls=%fused_computation | loop fusion | flops 2359296 | bytes 9437185 | tf_op jit(solution)/shard_map/jit(_where)/select_n | solution.py:543
  12.5 6.6 %collective-permute-done.3 = bf16[4,18,512]{2,1,0:T(8,128)(2,1)S(1)} collective-permute-done((bf16[4,18,512]{2,1,0:T(8,128)(2,1)S(1)}, bf16[4,18,512]{2,1,0:T(8,128)(2,1)S(1)}, u32[]{:S(2)}, u32[]{:S(2)}) %collective-permute-start.3) | collective-permute-done | bytes 73760 | tf_op jit(solution)/shard_map/ppermute | solution.py:573
  20.0 2.0 %collective-permute-start.6 = (bf16[3,11,16,512]{3,2,1,0:T(8,128)(2,1)S(1)}, bf16[3,11,16,512]{3,2,1,0:T(8,128)(2,1)S(1)}, u32[]{:S(2)}, u32[]{:S(2)}) collective-permute-start(bf16[3,11,16,512]{3,2,1,0:T(8,128)(2,1)S(1)} %join_last.2.last), channel_id=1, source_target_pairs={{0,4},{2,6},{4,8},{6,10},{8,12},{10,14},{12,0},{14,2},{1,5},{3,7},... | collective-permute-start | bytes 1622024 | tf_op jit(solution)/shard_map/ppermute | solution.py:558
  22.0 5.9 %collective-permute-done.received = bf16[3,8,16,512]{3,2,1,0:T(8,128)(2,1)S(1)} collective-permute-done((bf16[3,8,16,512]{3,2,1,0:T(8,128)(2,1)S(1)}, bf16[3,8,16,512]{3,2,1,0:T(8,128)(2,1)S(1)}, u32[]{:S(2)}, u32[]{:S(2)}) %collective-permute-start) | collective-permute-done | bytes 393248 | tf_op jit(solution)/shard_map/ppermute | solution.py:558
  28.5 2.2 %collective-permute-start.4 = (bf16[3,9,16,512]{3,2,1,0:T(8,128)(2,1)S(1)}, bf16[3,9,16,512]{3,2,1,0:T(8,128)(2,1)S(1)}, u32[]{:S(2)}, u32[]{:S(2)}) collective-permute-start(bf16[3,9,16,512]{3,2,1,0:T(8,128)(2,1)S(1)} %join_last.3.last), channel_id=1, source_target_pairs={{0,4},{2,6},{4,8},{6,10},{8,12},{10,14},{12,0},{14,2},{1,5},{3,7},... | collective-permute-start | bytes 1327112 | tf_op jit(solution)/shard_map/ppermute | solution.py:558
  30.7 0.8 collective-permute-done.7.others
  32.1 5.0 %early.1 = (f32[176,512]{1,0:T(8,128)S(1)}, bf16[2,128,512]{2,1,0:T(8,128)(2,1)S(1)}, bf16[3,2,2,16,512]{4,3,2,1,0:T(8,128)(2,1)S(1)}) custom-call(s32[3]{0:T(128)S(1)} %pad_add_fusion.scalars, bf16[5,11,16,512]{3,2,1,0:T(8,128)(2,1)S(1)} %join_first.2.first, bf16[3,11,16,512]{3,2,1,0:T(8,128)(2,1)S(1)} %join_last.2.last, bf16[1536,512]{1,0:T(8,128)(2,1)S(1)} %bitcast.26, ...), custom_call_target="tpu_custom_call" | custom-call | flops 3607101440 | bytes 9312256 | tf_op jit(solution)/shard_map/early/pallas_call | solution.py:239
  37.1 3.9 %late.1 = (bf16[4,32,512]{2,1,0:T(8,128)(2,1)S(1)}, bf16[4,32,512]{2,1,0:T(8,128)(2,1)S(1)}, bf16[4,32,512]{2,1,0:T(8,128)(2,1)S(1)}, bf16[4,32,512]{2,1,0:T(8,128)(2,1)S(1)}, bf16[3,2,2,16,512]{4,3,2,1,0:T(8,128)(2,1)S(1)}) custom-call(s32[3]{0:T(128)S(1)} %pad_add_fusion.scalars, bf16[3,11,16,512]{3,2,1,0:T(8,128)(2,1)S(1)} %collective-permute-done.6.halo, ...), custom_call_target="tpu_custom_call" | custom-call | flops 2407530496 | bytes 9672704 | tf_op jit(solution)/shard_map/late/pallas_call | solution.py:397
  41.1 4.2 %collective-permute-start.10 = (bf16[4,32,512]{2,1,0:T(8,128)(2,1)S(1)}, bf16[4,32,512]{2,1,0:T(8,128)(2,1)S(1)}, u32[]{:S(2)}, u32[]{:S(2)}) collective-permute-start(bf16[4,32,512]{2,1,0:T(8,128)(2,1)S(1)} %get-tuple-element.64), channel_id=1, source_target_pairs={{0,12},{2,14},{4,8},{6,10},{8,4},{10,6},{12,0},{14,2},{1,13},{3,15... | collective-permute-start | bytes 393224 | tf_op jit(solution)/shard_map/ppermute | solution.py:558
  45.3 0.6 collective-permute-start.9
  46.6 7.3 %full.1 = (bf16[4,32,512]{2,1,0:T(8,128)(2,1)S(1)}, bf16[4,32,512]{2,1,0:T(8,128)(2,1)S(1)}, bf16[4,32,512]{2,1,0:T(8,128)(2,1)S(1)}, bf16[4,32,512]{2,1,0:T(8,128)(2,1)S(1)}) custom-call(s32[3]{0:T(128)S(1)} %pad_add_fusion.scalars, bf16[3,9,16,512]{3,2,1,0:T(8,128)(2,1)S(1)} %collective-permute-done.4.halo, bf16[5,9,16,512]{3,2,1,0:T(8,128)(2,1)S(1)} %join_first.3.first, ...), custom_call_target="tpu_custom_call" | custom-call | flops 5360320512 | bytes 9492480 | tf_op jit(solution)/shard_map/full/pallas_call | solution.py:326
  53.9 1.5 %collective-permute-start.11 = (bf16[4,32,512]{2,1,0:T(8,128)(2,1)S(1)}, bf16[4,32,512]{2,1,0:T(8,128)(2,1)S(1)}, u32[]{:S(2)}, u32[]{:S(2)}) collective-permute-start(bf16[4,32,512]{2,1,0:T(8,128)(2,1)S(1)} %get-tuple-element.67), channel_id=1, source_target_pairs={{0,4},{2,6},{4,0},{6,2},{8,12},{10,14},{12,8},{14,10},{1,5},{3,7},... | collective-permute-start | bytes 393224 | tf_op jit(solution)/shard_map/ppermute | solution.py:558
  55.4 2.9 %collective-permute-start.12 = (bf16[4,32,512]{2,1,0:T(8,128)(2,1)S(1)}, bf16[4,32,512]{2,1,0:T(8,128)(2,1)S(1)}, u32[]{:S(2)}, u32[]{:S(2)}) collective-permute-start(bf16[4,32,512]{2,1,0:T(8,128)(2,1)S(1)} %get-tuple-element.68), channel_id=1, source_target_pairs={{0,8},{2,10},{4,12},{6,14},{8,0},{10,2},{12,4},{14,6},{1,9},{3,11}... | collective-permute-start | bytes 393224 | tf_op jit(solution)/shard_map/ppermute | solution.py:558
  58.4 2.8 %attend.2 = (bf16[2,32,512]{2,1,0:T(8,128)(2,1)S(1)}, bf16[2,32,512]{2,1,0:T(8,128)(2,1)S(1)}, bf16[2,32,512]{2,1,0:T(8,128)(2,1)S(1)}, bf16[2,32,512]{2,1,0:T(8...) custom-call(s32[3]{0:T(128)S(1)} %pad_add_fusion.scalars, ...), custom_call_target="tpu_custom_call" | custom-call | flops 1342177280 | bytes 2621440 | tf_op jit(solution)/shard_map/attend/pallas_call | solution.py:487
  61.2 2.0 %collective-permute-start.21 = (bf16[2,32,512]{2,1,0:T(8,128)(2,1)S(1)}, bf16[2,32,512]{2,1,0:T(8,128)(2,1)S(1)}, u32[]{:S(2)}, u32[]{:S(2)}) collective-permute-start(bf16[2,32,512]{2,1,0:T(8,128)(2,1)S(1)} %get-tuple-element.78), channel_id=1, source_target_pairs={{0,2},{2,0},{4,6},{6,4},{8,10},{10,8},{12,14},{14,12},{1,3},{3,1},... | collective-permute-start | bytes 196616 | tf_op jit(solution)/shard_map/ppermute | solution.py:558
  63.3 1.5 %collective-permute-start.23 = (bf16[2,32,512]{2,1,0:T(8,128)(2,1)S(1)}, bf16[2,32,512]{2,1,0:T(8,128)(2,1)S(1)}, u32[]{:S(2)}, u32[]{:S(2)}) collective-permute-start(bf16[2,32,512]{2,1,0:T(8,128)(2,1)S(1)} %get-tuple-element.80), channel_id=1, source_target_pairs={{0,6},{2,4},{4,2},{6,0},{8,14},{10,12},{12,10},{14,8},{1,7},{3,5},... | collective-permute-start | bytes 196616 | tf_op jit(solution)/shard_map/ppermute | solution.py:558
  64.8 3.5 %collective-permute-done.12.refs_2_ = bf16[4,32,512]{2,1,0:T(8,128)(2,1)S(1)} collective-permute-done((bf16[4,32,512]{2,1,0:T(8,128)(2,1)S(1)}, bf16[4,32,512]{2,1,0:T(8,128)(2,1)S(1)}, u32[]{:S(2)}, u32[]{:S(2)}) %collective-permute-start.12) | collective-permute-done | bytes 131104 | tf_op jit(solution)/shard_map/ppermute | solution.py:558
  68.3 3.7 %collective-permute-start.25 = (bf16[2,32,512]{2,1,0:T(8,128)(2,1)S(1)}, bf16[2,32,512]{2,1,0:T(8,128)(2,1)S(1)}, u32[]{:S(2)}, u32[]{:S(2)}) collective-permute-start(bf16[2,32,512]{2,1,0:T(8,128)(2,1)S(1)} %get-tuple-element.82), channel_id=1, source_target_pairs={{0,10},{2,8},{4,14},{6,12},{8,2},{10,0},{12,6},{14,4},{1,11},{3,9}... | collective-permute-start | bytes 196616 | tf_op jit(solution)/shard_map/ppermute | solution.py:558
  72.1 2.8 %attend.3 = (bf16[2,32,512]{2,1,0:T(8,128)(2,1)S(1)}, bf16[2,32,512]{2,1,0:T(8,128)(2,1)S(1)}, bf16[2,32,512]{2,1,0:T(8,128)(2,1)S(1)}, bf16[2,32,512]{2,1,0:T(8...) custom-call(s32[3]{0:T(128)S(1)} %pad_add_fusion.scalars, ...), custom_call_target="tpu_custom_call" | custom-call | flops 1342177280 | bytes 2621440 | tf_op jit(solution)/shard_map/attend/pallas_call | solution.py:487
  74.8 2.6 %collective-permute-start.26 = (bf16[2,32,512]{2,1,0:T(8,128)(2,1)S(1)}, bf16[2,32,512]{2,1,0:T(8,128)(2,1)S(1)}, u32[]{:S(2)}, u32[]{:S(2)}) collective-permute-start(bf16[2,32,512]{2,1,0:T(8,128)(2,1)S(1)} %get-tuple-element.83), channel_id=1, source_target_pairs={{0,12},{2,14},{4,8},{6,10},{8,4},{10,6},{12,0},{14,2},{1,13},{3,15... | collective-permute-start | bytes 196616 | tf_op jit(solution)/shard_map/ppermute | solution.py:558
  77.5 4.9 %collective-permute-start.27 = (bf16[2,32,512]{2,1,0:T(8,128)(2,1)S(1)}, bf16[2,32,512]{2,1,0:T(8,128)(2,1)S(1)}, u32[]{:S(2)}, u32[]{:S(2)}) collective-permute-start(bf16[2,32,512]{2,1,0:T(8,128)(2,1)S(1)} %get-tuple-element.84), channel_id=1, source_target_pairs={{0,14},{2,12},{4,10},{6,8},{8,6},{10,4},{12,2},{14,0},{1,15},{3,13... | collective-permute-start | bytes 196616 | tf_op jit(solution)/shard_map/ppermute | solution.py:558
  82.5 3.4 %collective-permute-start.16 = (bf16[2,32,512]{2,1,0:T(8,128)(2,1)S(1)}, bf16[2,32,512]{2,1,0:T(8,128)(2,1)S(1)}, u32[]{:S(2)}, u32[]{:S(2)}) collective-permute-start(bf16[2,32,512]{2,1,0:T(8,128)(2,1)S(1)} %get-tuple-element.73), channel_id=1, source_target_pairs={{0,6},{2,4},{4,2},{6,0},{8,14},{10,12},{12,10},{14,8},{1,7},{3,5},... | collective-permute-start | bytes 196616 | tf_op jit(solution)/shard_map/ppermute | solution.py:558
  86.3 2.0 %collective-permute-start.18 = (bf16[2,32,512]{2,1,0:T(8,128)(2,1)S(1)}, bf16[2,32,512]{2,1,0:T(8,128)(2,1)S(1)}, u32[]{:S(2)}, u32[]{:S(2)}) collective-permute-start(bf16[2,32,512]{2,1,0:T(8,128)(2,1)S(1)} %get-tuple-element.75), channel_id=1, source_target_pairs={{0,10},{2,8},{4,14},{6,12},{8,2},{10,0},{12,6},{14,4},{1,11},{3,9}... | collective-permute-start | bytes 196616 | tf_op jit(solution)/shard_map/ppermute | solution.py:558
  88.9 4.7 %collective-permute-start.20 = (bf16[2,32,512]{2,1,0:T(8,128)(2,1)S(1)}, bf16[2,32,512]{2,1,0:T(8,128)(2,1)S(1)}, u32[]{:S(2)}, u32[]{:S(2)}) collective-permute-start(bf16[2,32,512]{2,1,0:T(8,128)(2,1)S(1)} %get-tuple-element.77), channel_id=1, source_target_pairs={{0,14},{2,12},{4,10},{6,8},{8,6},{10,4},{12,2},{14,0},{1,15},{3,13... | collective-permute-start | bytes 196616 | tf_op jit(solution)/shard_map/ppermute | solution.py:558
  93.5 1.4 %collect.2.refs_8_ = bf16[2,16,32,512]{3,2,1,0:T(8,128)(2,1)} custom-call(s32[3]{0:T(128)S(1)} %pad_add_fusion.scalars, bf16[2,32,512]{2,1,0:T(8,128)(2,1)S(1)} %get-tuple-element.65.refs_0_, bf16[2,32,512]{2,1,0:T(8,128)(2,1)S(1)} %collective-permute-done.21.refs_1_, bf16[2,32,512]{2,1,0:T(8,128)(2,1)S(1)} %collective-permute-done.22.refs_2_, ...), custom_call_target="tpu_custom_call" | custom-call | tf_op jit(solution)/shard_map/collect/pallas_call | solution.py:513
  95.0 1.6 %collective-permute-done.20.refs_7_ = bf16[2,32,512]{2,1,0:T(8,128)(2,1)S(1)} collective-permute-done((bf16[2,32,512]{2,1,0:T(8,128)(2,1)S(1)}, bf16[2,32,512]{2,1,0:T(8,128)(2,1)S(1)}, u32[]{:S(2)}, u32[]{:S(2)}) %collective-permute-start.20) | collective-permute-done | bytes 65568 | tf_op jit(solution)/shard_map/ppermute | solution.py:558
  96.6 1.4 %collect.3 = bf16[2,16,32,512]{3,2,1,0:T(8,128)(2,1)} custom-call(s32[3]{0:T(128)S(1)} %pad_add_fusion.scalars, bf16[2,32,512]{2,1,0:T(8,128)(2,1)S(1)} %get-tuple-element.70.refs_0_, bf16[2,32,512]{2,1,0:T(8,128)(2,1)S(1)} %collective-permute-done.14.refs_1_, ...), custom_call_target="tpu_custom_call", output_to_operand_aliasing={{}: (9, {})} | custom-call | tf_op jit(solution)/shard_map/collect/pallas_call | solution.py:513
  (72 shorter events, 4.5 us)
Async XLA Ops:
  2.3 17.1 %collective-permute-start.1 = (bf16[3,10,16,512]{3,2,1,0:T(8,128)(2,1)S(1)}, bf16[3,10,16,512]{3,2,1,0:T(8,128)(2,1)S(1)}, u32[]{:S(2)}, u32[]{:S(2)}) collective-permute-start(bf16[3,10,16,512]{3,2,1,0:T(8,128)(2,1)S(1)} %get-tuple-element.46), channel_id=1, source_target_pairs={{0,2},{2,0},{4,6},{6,4},{8,10},{10,8},{12,14},{14,12},{1,3},{3,1},... | collective-permute-start | bytes 1474568 | tf_op jit(solution)/shard_map/ppermute | solution.py:558
  7.4 11.8 %collective-permute-start.2 = (bf16[4,18,512]{2,1,0:T(8,128)(2,1)S(1)}, bf16[4,18,512]{2,1,0:T(8,128)(2,1)S(1)}, u32[]{:S(2)}, u32[]{:S(2)}) collective-permute-start(bf16[4,18,512]{2,1,0:T(8,128)(2,1)S(1)} %get-tuple-element.88), channel_id=1, source_target_pairs={{0,1},{1,0},{2,3},{3,2},{4,5},{5,4},{6,7},{7,6},{8,9},{9,8},{10,11... | collective-permute-start | bytes 221192 | tf_op jit(solution)/shard_map/ppermute | solution.py:567
  7.5 11.5 %collective-permute-start.3 = (bf16[4,18,512]{2,1,0:T(8,128)(2,1)S(1)}, bf16[4,18,512]{2,1,0:T(8,128)(2,1)S(1)}, u32[]{:S(2)}, u32[]{:S(2)}) collective-permute-start(bf16[4,18,512]{2,1,0:T(8,128)(2,1)S(1)} %get-tuple-element.87), channel_id=1, source_target_pairs={{0,3},{1,2},{2,1},{3,0},{4,7},{5,6},{6,5},{7,4},{8,11},{9,10},{10,... | collective-permute-start | bytes 221192 | tf_op jit(solution)/shard_map/ppermute | solution.py:573
  7.7 20.3 %collective-permute-start = (bf16[3,8,16,512]{3,2,1,0:T(8,128)(2,1)S(1)}, bf16[3,8,16,512]{3,2,1,0:T(8,128)(2,1)S(1)}, u32[]{:S(2)}, u32[]{:S(2)}) collective-permute-start(bf16[3,8,16,512]{3,2,1,0:T(8,128)(2,1)S(1)} %get-tuple-element.45), channel_id=1, source_target_pairs={{0,2},{2,0},{4,6},{6,4},{8,10},{10,8},{12,14},{14,12},{1,3},{3,1},... | collective-permute-start | bytes 1179656 | tf_op jit(solution)/shard_map/ppermute | solution.py:558
  9.7 21.8 %collective-permute-start.7 = (bf16[1,10,16,512]{3,2,1,0:T(8,128)(2,1)S(1)}, bf16[1,10,16,512]{3,2,1,0:T(8,128)(2,1)S(1)}, u32[]{:S(2)}, u32[]{:S(2)}) collective-permute-start(bf16[1,10,16,512]{3,2,1,0:T(8,128)(2,1)S(1)} %get-tuple-element.52), channel_id=1, source_target_pairs={{0,2},{2,0},{4,6},{6,4},{8,10},{10,8},{12,14},{14,12},{1,3},{3,1},... | collective-permute-start | bytes 491528 | tf_op jit(solution)/shard_map/ppermute | solution.py:558
  19.1 22.0 %collective-permute-start.5 = (bf16[1,8,16,512]{3,2,1,0:T(8,128)(2,1)S(1)}, bf16[1,8,16,512]{3,2,1,0:T(8,128)(2,1)S(1)}, u32[]{:S(2)}, u32[]{:S(2)}) collective-permute-start(bf16[1,8,16,512]{3,2,1,0:T(8,128)(2,1)S(1)} %get-tuple-element.51), channel_id=1, source_target_pairs={{0,2},{2,0},{4,6},{6,4},{8,10},{10,8},{12,14},{14,12},{1,3},{3,1},... | collective-permute-start | bytes 393224 | tf_op jit(solution)/shard_map/ppermute | solution.py:558
  19.4 12.7 %copy-start.2 = (bf16[3,512,512]{2,1,0:T(8,128)(2,1)S(1)}, bf16[3,512,512]{2,1,0:T(8,128)(2,1)}, u32[]{:S(2)}) copy-start(bf16[3,512,512]{2,1,0:T(8,128)(2,1)} %param.13) | copy-start | bytes 4718596
  19.4 12.7 %copy-start.3 = (bf16[3,512,512]{2,1,0:T(8,128)(2,1)S(1)}, bf16[3,512,512]{2,1,0:T(8,128)(2,1)}, u32[]{:S(2)}) copy-start(bf16[3,512,512]{2,1,0:T(8,128)(2,1)} %param.15) | copy-start | bytes 4718596
  19.4 12.6 %copy-start.4 = (f32[512]{0:T(512)S(1)}, f32[512]{0:T(512)}, u32[]{:S(2)}) copy-start(f32[512]{0:T(512)} %param.14) | copy-start | bytes 6148
  19.4 12.6 %copy-start.5 = (f32[512]{0:T(512)S(1)}, f32[512]{0:T(512)}, u32[]{:S(2)}) copy-start(f32[512]{0:T(512)} %param.16) | copy-start | bytes 6148
  20.0 17.1 %collective-permute-start.6 = (bf16[3,11,16,512]{3,2,1,0:T(8,128)(2,1)S(1)}, bf16[3,11,16,512]{3,2,1,0:T(8,128)(2,1)S(1)}, u32[]{:S(2)}, u32[]{:S(2)}) collective-permute-start(bf16[3,11,16,512]{3,2,1,0:T(8,128)(2,1)S(1)} %join_last.2.last), channel_id=1, source_target_pairs={{0,4},{2,6},{4,8},{6,10},{8,12},{10,14},{12,0},{14,2},{1,5},{3,7},... | collective-permute-start | bytes 1622024 | tf_op jit(solution)/shard_map/ppermute | solution.py:558
  28.5 18.0 %collective-permute-start.4 = (bf16[3,9,16,512]{3,2,1,0:T(8,128)(2,1)S(1)}, bf16[3,9,16,512]{3,2,1,0:T(8,128)(2,1)S(1)}, u32[]{:S(2)}, u32[]{:S(2)}) collective-permute-start(bf16[3,9,16,512]{3,2,1,0:T(8,128)(2,1)S(1)} %join_last.3.last), channel_id=1, source_target_pairs={{0,4},{2,6},{4,8},{6,10},{8,12},{10,14},{12,0},{14,2},{1,5},{3,7},... | collective-permute-start | bytes 1327112 | tf_op jit(solution)/shard_map/ppermute | solution.py:558
  41.1 17.3 %collective-permute-start.10 = (bf16[4,32,512]{2,1,0:T(8,128)(2,1)S(1)}, bf16[4,32,512]{2,1,0:T(8,128)(2,1)S(1)}, u32[]{:S(2)}, u32[]{:S(2)}) collective-permute-start(bf16[4,32,512]{2,1,0:T(8,128)(2,1)S(1)} %get-tuple-element.64), channel_id=1, source_target_pairs={{0,12},{2,14},{4,8},{6,10},{8,4},{10,6},{12,0},{14,2},{1,13},{3,15... | collective-permute-start | bytes 393224 | tf_op jit(solution)/shard_map/ppermute | solution.py:558
  45.3 13.1 %collective-permute-start.8 = (bf16[4,32,512]{2,1,0:T(8,128)(2,1)S(1)}, bf16[4,32,512]{2,1,0:T(8,128)(2,1)S(1)}, u32[]{:S(2)}, u32[]{:S(2)}) collective-permute-start(bf16[4,32,512]{2,1,0:T(8,128)(2,1)S(1)} %get-tuple-element.62), channel_id=1, source_target_pairs={{0,4},{2,6},{4,0},{6,2},{8,12},{10,14},{12,8},{14,10},{1,5},{3,7},... | collective-permute-start | bytes 393224 | tf_op jit(solution)/shard_map/ppermute | solution.py:558
  45.3 13.1 %collective-permute-start.9 = (bf16[4,32,512]{2,1,0:T(8,128)(2,1)S(1)}, bf16[4,32,512]{2,1,0:T(8,128)(2,1)S(1)}, u32[]{:S(2)}, u32[]{:S(2)}) collective-permute-start(bf16[4,32,512]{2,1,0:T(8,128)(2,1)S(1)} %get-tuple-element.63), channel_id=1, source_target_pairs={{0,8},{2,10},{4,12},{6,14},{8,0},{10,2},{12,4},{14,6},{1,9},{3,11}... | collective-permute-start | bytes 393224 | tf_op jit(solution)/shard_map/ppermute | solution.py:558
  53.9 9.4 %collective-permute-start.11 = (bf16[4,32,512]{2,1,0:T(8,128)(2,1)S(1)}, bf16[4,32,512]{2,1,0:T(8,128)(2,1)S(1)}, u32[]{:S(2)}, u32[]{:S(2)}) collective-permute-start(bf16[4,32,512]{2,1,0:T(8,128)(2,1)S(1)} %get-tuple-element.67), channel_id=1, source_target_pairs={{0,4},{2,6},{4,0},{6,2},{8,12},{10,14},{12,8},{14,10},{1,5},{3,7},... | collective-permute-start | bytes 393224 | tf_op jit(solution)/shard_map/ppermute | solution.py:558
  55.4 12.9 %collective-permute-start.12 = (bf16[4,32,512]{2,1,0:T(8,128)(2,1)S(1)}, bf16[4,32,512]{2,1,0:T(8,128)(2,1)S(1)}, u32[]{:S(2)}, u32[]{:S(2)}) collective-permute-start(bf16[4,32,512]{2,1,0:T(8,128)(2,1)S(1)} %get-tuple-element.68), channel_id=1, source_target_pairs={{0,8},{2,10},{4,12},{6,14},{8,0},{10,2},{12,4},{14,6},{1,9},{3,11}... | collective-permute-start | bytes 393224 | tf_op jit(solution)/shard_map/ppermute | solution.py:558
  58.3 10.0 %collective-permute-start.13 = (bf16[4,32,512]{2,1,0:T(8,128)(2,1)S(1)}, bf16[4,32,512]{2,1,0:T(8,128)(2,1)S(1)}, u32[]{:S(2)}, u32[]{:S(2)}) collective-permute-start(bf16[4,32,512]{2,1,0:T(8,128)(2,1)S(1)} %get-tuple-element.69), channel_id=1, source_target_pairs={{0,12},{2,14},{4,8},{6,10},{8,4},{10,6},{12,0},{14,2},{1,13},{3,15... | collective-permute-start | bytes 393224 | tf_op jit(solution)/shard_map/ppermute | solution.py:558
  61.2 13.6 %collective-permute-start.21 = (bf16[2,32,512]{2,1,0:T(8,128)(2,1)S(1)}, bf16[2,32,512]{2,1,0:T(8,128)(2,1)S(1)}, u32[]{:S(2)}, u32[]{:S(2)}) collective-permute-start(bf16[2,32,512]{2,1,0:T(8,128)(2,1)S(1)} %get-tuple-element.78), channel_id=1, source_target_pairs={{0,2},{2,0},{4,6},{6,4},{8,10},{10,8},{12,14},{14,12},{1,3},{3,1},... | collective-permute-start | bytes 196616 | tf_op jit(solution)/shard_map/ppermute | solution.py:558
  63.2 14.3 %collective-permute-start.22 = (bf16[2,32,512]{2,1,0:T(8,128)(2,1)S(1)}, bf16[2,32,512]{2,1,0:T(8,128)(2,1)S(1)}, u32[]{:S(2)}, u32[]{:S(2)}) collective-permute-start(bf16[2,32,512]{2,1,0:T(8,128)(2,1)S(1)} %get-tuple-element.79), channel_id=1, source_target_pairs={{0,4},{2,6},{4,0},{6,2},{8,12},{10,14},{12,8},{14,10},{1,5},{3,7},... | collective-permute-start | bytes 196616 | tf_op jit(solution)/shard_map/ppermute | solution.py:558
  63.3 19.0 %collective-permute-start.23 = (bf16[2,32,512]{2,1,0:T(8,128)(2,1)S(1)}, bf16[2,32,512]{2,1,0:T(8,128)(2,1)S(1)}, u32[]{:S(2)}, u32[]{:S(2)}) collective-permute-start(bf16[2,32,512]{2,1,0:T(8,128)(2,1)S(1)} %get-tuple-element.80), channel_id=1, source_target_pairs={{0,6},{2,4},{4,2},{6,0},{8,14},{10,12},{12,10},{14,8},{1,7},{3,5},... | collective-permute-start | bytes 196616 | tf_op jit(solution)/shard_map/ppermute | solution.py:558
  68.3 14.0 %collective-permute-start.24 = (bf16[2,32,512]{2,1,0:T(8,128)(2,1)S(1)}, bf16[2,32,512]{2,1,0:T(8,128)(2,1)S(1)}, u32[]{:S(2)}, u32[]{:S(2)}) collective-permute-start(bf16[2,32,512]{2,1,0:T(8,128)(2,1)S(1)} %get-tuple-element.81), channel_id=1, source_target_pairs={{0,8},{2,10},{4,12},{6,14},{8,0},{10,2},{12,4},{14,6},{1,9},{3,11}... | collective-permute-start | bytes 196616 | tf_op jit(solution)/shard_map/ppermute | solution.py:558
  68.3 14.1 %collective-permute-start.25 = (bf16[2,32,512]{2,1,0:T(8,128)(2,1)S(1)}, bf16[2,32,512]{2,1,0:T(8,128)(2,1)S(1)}, u32[]{:S(2)}, u32[]{:S(2)}) collective-permute-start(bf16[2,32,512]{2,1,0:T(8,128)(2,1)S(1)} %get-tuple-element.82), channel_id=1, source_target_pairs={{0,10},{2,8},{4,14},{6,12},{8,2},{10,0},{12,6},{14,4},{1,11},{3,9}... | collective-permute-start | bytes 196616 | tf_op jit(solution)/shard_map/ppermute | solution.py:558
  74.8 11.0 %collective-permute-start.26 = (bf16[2,32,512]{2,1,0:T(8,128)(2,1)S(1)}, bf16[2,32,512]{2,1,0:T(8,128)(2,1)S(1)}, u32[]{:S(2)}, u32[]{:S(2)}) collective-permute-start(bf16[2,32,512]{2,1,0:T(8,128)(2,1)S(1)} %get-tuple-element.83), channel_id=1, source_target_pairs={{0,12},{2,14},{4,8},{6,10},{8,4},{10,6},{12,0},{14,2},{1,13},{3,15... | collective-permute-start | bytes 196616 | tf_op jit(solution)/shard_map/ppermute | solution.py:558
  77.5 8.8 %collective-permute-start.27 = (bf16[2,32,512]{2,1,0:T(8,128)(2,1)S(1)}, bf16[2,32,512]{2,1,0:T(8,128)(2,1)S(1)}, u32[]{:S(2)}, u32[]{:S(2)}) collective-permute-start(bf16[2,32,512]{2,1,0:T(8,128)(2,1)S(1)} %get-tuple-element.84), channel_id=1, source_target_pairs={{0,14},{2,12},{4,10},{6,8},{8,6},{10,4},{12,2},{14,0},{1,15},{3,13... | collective-permute-start | bytes 196616 | tf_op jit(solution)/shard_map/ppermute | solution.py:558
  82.4 5.9 %collective-permute-start.14 = (bf16[2,32,512]{2,1,0:T(8,128)(2,1)S(1)}, bf16[2,32,512]{2,1,0:T(8,128)(2,1)S(1)}, u32[]{:S(2)}, u32[]{:S(2)}) collective-permute-start(bf16[2,32,512]{2,1,0:T(8,128)(2,1)S(1)} %get-tuple-element.71), channel_id=1, source_target_pairs={{0,2},{2,0},{4,6},{6,4},{8,10},{10,8},{12,14},{14,12},{1,3},{3,1},... | collective-permute-start | bytes 196616 | tf_op jit(solution)/shard_map/ppermute | solution.py:558
  82.4 6.5 %collective-permute-start.15 = (bf16[2,32,512]{2,1,0:T(8,128)(2,1)S(1)}, bf16[2,32,512]{2,1,0:T(8,128)(2,1)S(1)}, u32[]{:S(2)}, u32[]{:S(2)}) collective-permute-start(bf16[2,32,512]{2,1,0:T(8,128)(2,1)S(1)} %get-tuple-element.72), channel_id=1, source_target_pairs={{0,4},{2,6},{4,0},{6,2},{8,12},{10,14},{12,8},{14,10},{1,5},{3,7},... | collective-permute-start | bytes 196616 | tf_op jit(solution)/shard_map/ppermute | solution.py:558
  82.5 12.5 %collective-permute-start.16 = (bf16[2,32,512]{2,1,0:T(8,128)(2,1)S(1)}, bf16[2,32,512]{2,1,0:T(8,128)(2,1)S(1)}, u32[]{:S(2)}, u32[]{:S(2)}) collective-permute-start(bf16[2,32,512]{2,1,0:T(8,128)(2,1)S(1)} %get-tuple-element.73), channel_id=1, source_target_pairs={{0,6},{2,4},{4,2},{6,0},{8,14},{10,12},{12,10},{14,8},{1,7},{3,5},... | collective-permute-start | bytes 196616 | tf_op jit(solution)/shard_map/ppermute | solution.py:558
  85.9 9.1 %collective-permute-start.17 = (bf16[2,32,512]{2,1,0:T(8,128)(2,1)S(1)}, bf16[2,32,512]{2,1,0:T(8,128)(2,1)S(1)}, u32[]{:S(2)}, u32[]{:S(2)}) collective-permute-start(bf16[2,32,512]{2,1,0:T(8,128)(2,1)S(1)} %get-tuple-element.74), channel_id=1, source_target_pairs={{0,8},{2,10},{4,12},{6,14},{8,0},{10,2},{12,4},{14,6},{1,9},{3,11}... | collective-permute-start | bytes 196616 | tf_op jit(solution)/shard_map/ppermute | solution.py:558
  86.3 8.7 %collective-permute-start.18 = (bf16[2,32,512]{2,1,0:T(8,128)(2,1)S(1)}, bf16[2,32,512]{2,1,0:T(8,128)(2,1)S(1)}, u32[]{:S(2)}, u32[]{:S(2)}) collective-permute-start(bf16[2,32,512]{2,1,0:T(8,128)(2,1)S(1)} %get-tuple-element.75), channel_id=1, source_target_pairs={{0,10},{2,8},{4,14},{6,12},{8,2},{10,0},{12,6},{14,4},{1,11},{3,9}... | collective-permute-start | bytes 196616 | tf_op jit(solution)/shard_map/ppermute | solution.py:558
  88.3 6.7 %collective-permute-start.19 = (bf16[2,32,512]{2,1,0:T(8,128)(2,1)S(1)}, bf16[2,32,512]{2,1,0:T(8,128)(2,1)S(1)}, u32[]{:S(2)}, u32[]{:S(2)}) collective-permute-start(bf16[2,32,512]{2,1,0:T(8,128)(2,1)S(1)} %get-tuple-element.76), channel_id=1, source_target_pairs={{0,12},{2,14},{4,8},{6,10},{8,4},{10,6},{12,0},{14,2},{1,13},{3,15... | collective-permute-start | bytes 196616 | tf_op jit(solution)/shard_map/ppermute | solution.py:558
  88.9 7.7 %collective-permute-start.20 = (bf16[2,32,512]{2,1,0:T(8,128)(2,1)S(1)}, bf16[2,32,512]{2,1,0:T(8,128)(2,1)S(1)}, u32[]{:S(2)}, u32[]{:S(2)}) collective-permute-start(bf16[2,32,512]{2,1,0:T(8,128)(2,1)S(1)} %get-tuple-element.77), channel_id=1, source_target_pairs={{0,14},{2,12},{4,10},{6,8},{8,6},{10,4},{12,2},{14,0},{1,15},{3,13... | collective-permute-start | bytes 196616 | tf_op jit(solution)/shard_map/ppermute | solution.py:558
  (9 other events, 92.7 us)

commit v12 on v11

--- a/solution.py
+++ b/solution.py
@@ -410,7 +410,8 @@
     )(scalars, halo, first, part, spatial, *weights)
 
 
-def attend_kernel(frames_per, lanes, count, scalars, *refs):
+def attend_kernel(frames_per, lanes, turns, scalars, *refs):
+    count = len(turns)
     blocks = refs[:count]
     gain, w_query, w_key, w_value, w_out = refs[count : count + 5]
     outs = refs[count + 5 :]
@@ -428,8 +429,8 @@
     def place(index):
         block = index // each
         time = index // lanes % frames_per
-        for j in range(count):
-            level = 0 if flat else scalars[2] ^ j
+        for j, turn in enumerate(turns):
+            level = 0 if flat else scalars[2] ^ turn
             time = time + jnp.where(block == j, level * frames_per, 0)
         return time, index % lanes
 
@@ -472,7 +473,7 @@
                         outs[pair * j + x][:, g * lanes : (g + 1) * lanes] = rows[side ^ x]
 
 
-def attend(scalars, blocks, gain, w_query, w_key, w_value, w_out):
+def attend(scalars, turns, blocks, gain, w_query, w_key, w_value, w_out):
     frames_per, pixels, channels = blocks[0].shape
     flat = pixels % 16 != 0
     lanes = pixels if flat else 16
@@ -485,7 +486,7 @@
         shapes = [blocks[0].shape]
     flops = 2 * frames_per * pixels * count * channels * (4 * channels + 2 * size)
     outs = pl.pallas_call(
-        partial(attend_kernel, frames_per, lanes, count),
+        partial(attend_kernel, frames_per, lanes, turns),
         out_shape=[jax.ShapeDtypeStruct(shape, jnp.bfloat16) for shape in shapes],
         in_specs=[SMEM] + [VMEM] * (count + 5),
         out_specs=[VMEM] * len(shapes),
@@ -496,26 +497,28 @@
     return [o.reshape(frames_per, pixels, channels) for o in outs] if flat else outs
 
 
-def collect_kernel(base, stride, scalars, *refs):
+def collect_kernel(base, stride, turns, scalars, *refs):
     out, sems = refs[-2:]
     copies = []
-    for m in range(sems.shape[0]):
-        index = base + (scalars[0] ^ m % pair) * stride + (scalars[2] ^ m // pair)
-        copies.append(pltpu.make_async_copy(refs[m], out.at[:, index], sems.at[m]))
+    for j, level in enumerate(turns):
+        for x in range(pair):
+            block = refs[pair * j + x]
+            index = base + (scalars[0] ^ x) * stride + (scalars[2] ^ level)
+            copies.append(pltpu.make_async_copy(block, out.at[:, index], sems.at[len(copies)]))
     run(copies)
 
 
-def collect(scalars, blocks, chunk, chunks, whole):
-    count = len(blocks)
+def collect(scalars, turns, blocks, chunk, chunks, whole):
+    levels = len(turns)
+    count = pair * levels
     halves, pixels, channels = blocks[0].shape
-    levels = count // pair
     given = [] if whole is None else [whole]
     return pl.pallas_call(
-        partial(collect_kernel, chunk * levels, chunks * levels),
+        partial(collect_kernel, chunk * levels, chunks * levels, turns),
         out_shape=jax.ShapeDtypeStruct((halves, chunks * count, pixels, channels), jnp.bfloat16),
-        in_specs=[SMEM] + [ANY] * (count + len(given)),
+        in_specs=[SMEM] + [ANY] * (len(blocks) + len(given)),
         out_specs=ANY,
-        input_output_aliases={count + 1: 0} if given else {},
+        input_output_aliases={len(blocks) + 1: 0} if given else {},
         scratch_shapes=[pltpu.SemaphoreType.DMA((count,))],
         compiler_params=params(16),
         name="collect",
@@ -613,29 +616,33 @@
 
     newest = spatials[-1][0]
     if direct:
+        turns = tuple(range(levels // 2, levels)) + tuple(range(levels // 2))[::-1]
+
+        def exchange(blocks, moves):
+            return [
+                tm_permute(block, lambda i: i ^ move) if move else block
+                for block, move in zip(blocks, moves)
+            ]
+
         gathers = [
-            [blocks[0]]
-            + [tm_permute(blocks[j], lambda i: i ^ (pair * j)) for j in range(1, levels)]
-            for blocks in spatials
+            exchange([blocks[j] for j in turns], [pair * j for j in turns]) for blocks in spatials
         ]
         returns = []
         for gathered in gathers:
-            gathered[0] = after(gathered[0], newest)
-            results = attend(scalars, gathered, *attention)
+            gathered[-1] = after(gathered[-1], newest)
+            results = attend(scalars, turns, gathered, *attention)
             newest = results[0]
-            returns.append(
-                [results[0]]
-                + [tm_permute(results[m], lambda i: i ^ m) for m in range(1, devices)]
-            )
+            moves = [pair * j + x for j in turns for x in range(pair)]
+            returns.append(exchange(results, moves))
         whole = None
         for k, blocks in enumerate(returns):
-            whole = collect(scalars, blocks, k, chunks, whole)
+            whole = collect(scalars, turns, blocks, k, chunks, whole)
         return whole.reshape(frames // 2, height, width, channels)
     sets = [[pair * z + s for z in range(levels)] for s in range(pair)]
     returns = []
     for (block,) in spatials:
         gathered = lax.all_to_all(block, "tm", 1, 0, axis_index_groups=sets, tiled=True)
-        (result,) = attend(scalars, [gathered], *attention)
+        (result,) = attend(scalars, (0,), [gathered], *attention)
         result = lax.all_to_all(result, "tm", 0, 1, tiled=True)
         result = result.reshape(frames // 2, levels, pair, each, channels)
         returns.append(result.transpose(0, 2, 1, 3, 4).reshape(frames // 2, pair, -1, channels))

time: 98.3 us -> 99.8 us (1.015)
  starting transfers between devices: 44.4 us -> 46.8 us
    ppermute x26, starting transfers between devices: 44.2 us -> 46.6 us  [tm_permute(): lax.ppermute(value, 'tm', [(i, move(i)) for i in range(devices) if move(i...]
  transfers between devices with their start and end apart: 28 -> 28, of which waited for: 6 -> 7; matrix products, arithmetic and copies ran while one was open for 5% -> 5% of each run, Pallas kernels for 26% -> 26%
where the time goes in v12:
time: 99.8 us; the launch traced here: 99.7 us
  starting transfers between devices  46.8 us (47%)
  Pallas kernels  27.6 us (28%)
  waiting for transfers between devices  17.9 us (18%)
  local copies, waits for them, and re-layouts  3.74 us (4%)
  other arithmetic  2.99 us (3%)
    ppermute x26, starting transfers between devices, tm_permute(): lax.ppermute(value, 'tm', [(i, move(i)) for i in range(devices) if move(i...  46.6 us
    ppermute x26, waiting for transfers between devices, tm_permute(): lax.ppermute(value, 'tm', [(i, move(i)) for i in range(devices) if move(i...  11.4 us
    pallas_call x1, Pallas kernels, full(): pl.pallas_call(partial(full_kernel, owners, final, rows), out_shape=[jax....  7.32 us
    ppermute x1, waiting for transfers between devices, per_device(): other_edge = lax.ppermute(other_edge, ('tm', 'cols'), aslant)  6.56 us
    pallas_call x2, Pallas kernels, attend(): pl.pallas_call(partial(attend_kernel, frames_per, lanes, turns), out_shap...  5.58 us
    pallas_call x1, Pallas kernels, early(): pl.pallas_call(partial(early_kernel, final, rows), out_shape=shapes, in_s...  5.02 us
    pallas_call x1, Pallas kernels, late(): pl.pallas_call(partial(late_kernel, owners, final, rows), out_shape=[jax....  3.92 us
    select_n x1, other arithmetic, per_device(): w_space = jnp.where(after(place, video) >= 0, w_space, 0)  2.79 us
  transfers between devices with their start and end apart: 28, of which 7 were waited for; matrix products, arithmetic and copies ran while one was open for 5% of the time, Pallas kernels for 26%

profile of v12, /device:TPU:0, one launch (start us, length us, event | category | flops | bytes accessed | tf_op | source)
XLA Modules:
  0.0 99.7 jit_solution(5167846290709042334)
XLA Ops:
  0.1 1.6 %copy-done = bf16[4,32,16,512]{3,2,1,0:T(8,128)(2,1)S(1)} copy-done((bf16[4,32,16,512]{3,2,1,0:T(8,128)(2,1)S(1)}, bf16[4,32,16,512]{3,2,1,0:T(8,128)(2,1)}, u32[]{:S(2)}) %copy-start) | copy-done | bytes 2097176
  2.3 3.0 %collective-permute-start.1 = (bf16[3,10,16,512]{3,2,1,0:T(8,128)(2,1)S(1)}, bf16[3,10,16,512]{3,2,1,0:T(8,128)(2,1)S(1)}, u32[]{:S(2)}, u32[]{:S(2)}) collective-permute-start(bf16[3,10,16,512]{3,2,1,0:T(8,128)(2,1)S(1)} %get-tuple-element.46), channel_id=1, source_target_pairs={{0,2},{2,0},{4,6},{6,4},{8,10},{10,8},{12,14},{14,12},{1,3},{3,1},... | collective-permute-start | bytes 1474568 | tf_op jit(solution)/shard_map/ppermute | solution.py:561
  5.3 1.9 %fusion.3 = (bf16[4,32,1,512]{3,2,1,0:T(2,128)(2,1)S(1)}, bf16[4,32,1,512]{3,2,1,0:T(2,128)(2,1)S(1)}) fusion(bf16[4,32,16,512]{3,2,1,0:T(8,128)(2,1)} %video.9), kind=kLoop, calls=%fused_computation.12 | loop fusion | bytes 524288 | tf_op jit(solution)/shard_map/slice | solution.py:565
  7.7 2.0 %collective-permute-start = (bf16[3,8,16,512]{3,2,1,0:T(8,128)(2,1)S(1)}, bf16[3,8,16,512]{3,2,1,0:T(8,128)(2,1)S(1)}, u32[]{:S(2)}, u32[]{:S(2)}) collective-permute-start(bf16[3,8,16,512]{3,2,1,0:T(8,128)(2,1)S(1)} %get-tuple-element.45), channel_id=1, source_target_pairs={{0,2},{2,0},{4,6},{6,4},{8,10},{10,8},{12,14},{14,12},{1,3},{3,1},... | collective-permute-start | bytes 1179656 | tf_op jit(solution)/shard_map/ppermute | solution.py:561
  9.7 2.8 %broadcast_select_fusion.w_space = bf16[9,512,512]{2,1,0:T(8,128)(2,1)S(1)} fusion(bf16[9,512,512]{2,1,0:T(8,128)(2,1)} %param.17, pred[]{:T(512)S(6)} %ge.3), kind=kLoop, calls=%fused_computation | loop fusion | flops 2359296 | bytes 9437185 | tf_op jit(solution)/shard_map/jit(_where)/select_n | solution.py:546
  12.5 6.6 %collective-permute-done.3 = bf16[4,18,512]{2,1,0:T(8,128)(2,1)S(1)} collective-permute-done((bf16[4,18,512]{2,1,0:T(8,128)(2,1)S(1)}, bf16[4,18,512]{2,1,0:T(8,128)(2,1)S(1)}, u32[]{:S(2)}, u32[]{:S(2)}) %collective-permute-start.3) | collective-permute-done | bytes 73760 | tf_op jit(solution)/shard_map/ppermute | solution.py:576
  20.0 2.0 %collective-permute-start.6 = (bf16[3,11,16,512]{3,2,1,0:T(8,128)(2,1)S(1)}, bf16[3,11,16,512]{3,2,1,0:T(8,128)(2,1)S(1)}, u32[]{:S(2)}, u32[]{:S(2)}) collective-permute-start(bf16[3,11,16,512]{3,2,1,0:T(8,128)(2,1)S(1)} %join_last.2.last), channel_id=1, source_target_pairs={{0,4},{2,6},{4,8},{6,10},{8,12},{10,14},{12,0},{14,2},{1,5},{3,7},... | collective-permute-start | bytes 1622024 | tf_op jit(solution)/shard_map/ppermute | solution.py:561
  22.0 5.9 %collective-permute-done.received = bf16[3,8,16,512]{3,2,1,0:T(8,128)(2,1)S(1)} collective-permute-done((bf16[3,8,16,512]{3,2,1,0:T(8,128)(2,1)S(1)}, bf16[3,8,16,512]{3,2,1,0:T(8,128)(2,1)S(1)}, u32[]{:S(2)}, u32[]{:S(2)}) %collective-permute-start) | collective-permute-done | bytes 393248 | tf_op jit(solution)/shard_map/ppermute | solution.py:561
  28.5 2.2 %collective-permute-start.4 = (bf16[3,9,16,512]{3,2,1,0:T(8,128)(2,1)S(1)}, bf16[3,9,16,512]{3,2,1,0:T(8,128)(2,1)S(1)}, u32[]{:S(2)}, u32[]{:S(2)}) collective-permute-start(bf16[3,9,16,512]{3,2,1,0:T(8,128)(2,1)S(1)} %join_last.3.last), channel_id=1, source_target_pairs={{0,4},{2,6},{4,8},{6,10},{8,12},{10,14},{12,0},{14,2},{1,5},{3,7},... | collective-permute-start | bytes 1327112 | tf_op jit(solution)/shard_map/ppermute | solution.py:561
  32.1 5.0 %early.1 = (f32[176,512]{1,0:T(8,128)S(1)}, bf16[2,128,512]{2,1,0:T(8,128)(2,1)S(1)}, bf16[3,2,2,16,512]{4,3,2,1,0:T(8,128)(2,1)S(1)}) custom-call(s32[3]{0:T(128)S(1)} %pad_add_fusion.scalars, bf16[5,11,16,512]{3,2,1,0:T(8,128)(2,1)S(1)} %join_first.2.first, bf16[3,11,16,512]{3,2,1,0:T(8,128)(2,1)S(1)} %join_last.2.last, bf16[1536,512]{1,0:T(8,128)(2,1)S(1)} %bitcast.26, ...), custom_call_target="tpu_custom_call" | custom-call | flops 3607101440 | bytes 9312256 | tf_op jit(solution)/shard_map/early/pallas_call | solution.py:239
  37.1 3.9 %late.1 = (bf16[4,32,512]{2,1,0:T(8,128)(2,1)S(1)}, bf16[4,32,512]{2,1,0:T(8,128)(2,1)S(1)}, bf16[4,32,512]{2,1,0:T(8,128)(2,1)S(1)}, bf16[4,32,512]{2,1,0:T(8,128)(2,1)S(1)}, bf16[3,2,2,16,512]{4,3,2,1,0:T(8,128)(2,1)S(1)}) custom-call(s32[3]{0:T(128)S(1)} %pad_add_fusion.scalars, bf16[3,11,16,512]{3,2,1,0:T(8,128)(2,1)S(1)} %collective-permute-done.6.halo, ...), custom_call_target="tpu_custom_call" | custom-call | flops 2407530496 | bytes 9672704 | tf_op jit(solution)/shard_map/late/pallas_call | solution.py:397
  41.1 3.2 %collective-permute-start.11 = (bf16[4,32,512]{2,1,0:T(8,128)(2,1)S(1)}, bf16[4,32,512]{2,1,0:T(8,128)(2,1)S(1)}, u32[]{:S(2)}, u32[]{:S(2)}) collective-permute-start(bf16[4,32,512]{2,1,0:T(8,128)(2,1)S(1)} %get-tuple-element.64), channel_id=1, source_target_pairs={{0,8},{2,10},{4,12},{6,14},{8,0},{10,2},{12,4},{14,6},{1,9},{3,11}... | collective-permute-start | bytes 393224 | tf_op jit(solution)/shard_map/ppermute | solution.py:561
  44.3 1.3 %collective-permute-start.12 = (bf16[4,32,512]{2,1,0:T(8,128)(2,1)S(1)}, bf16[4,32,512]{2,1,0:T(8,128)(2,1)S(1)}, u32[]{:S(2)}, u32[]{:S(2)}) collective-permute-start(bf16[4,32,512]{2,1,0:T(8,128)(2,1)S(1)} %get-tuple-element.65), channel_id=1, source_target_pairs={{0,12},{2,14},{4,8},{6,10},{8,4},{10,6},{12,0},{14,2},{1,13},{3,15... | collective-permute-start | bytes 393224 | tf_op jit(solution)/shard_map/ppermute | solution.py:561
  46.5 7.3 %full.1 = (bf16[4,32,512]{2,1,0:T(8,128)(2,1)S(1)}, bf16[4,32,512]{2,1,0:T(8,128)(2,1)S(1)}, bf16[4,32,512]{2,1,0:T(8,128)(2,1)S(1)}, bf16[4,32,512]{2,1,0:T(8,128)(2,1)S(1)}) custom-call(s32[3]{0:T(128)S(1)} %pad_add_fusion.scalars, bf16[3,9,16,512]{3,2,1,0:T(8,128)(2,1)S(1)} %collective-permute-done.4.halo, bf16[5,9,16,512]{3,2,1,0:T(8,128)(2,1)S(1)} %join_first.3.first, ...), custom_call_target="tpu_custom_call" | custom-call | flops 5360320512 | bytes 9492480 | tf_op jit(solution)/shard_map/full/pallas_call | solution.py:326
  53.9 1.9 %collective-permute-start.10 = (bf16[4,32,512]{2,1,0:T(8,128)(2,1)S(1)}, bf16[4,32,512]{2,1,0:T(8,128)(2,1)S(1)}, u32[]{:S(2)}, u32[]{:S(2)}) collective-permute-start(bf16[4,32,512]{2,1,0:T(8,128)(2,1)S(1)} %get-tuple-element.62), channel_id=1, source_target_pairs={{0,4},{2,6},{4,0},{6,2},{8,12},{10,14},{12,8},{14,10},{1,5},{3,7},... | collective-permute-start | bytes 393224 | tf_op jit(solution)/shard_map/ppermute | solution.py:561
  55.7 1.7 %collective-permute-start.8 = (bf16[4,32,512]{2,1,0:T(8,128)(2,1)S(1)}, bf16[4,32,512]{2,1,0:T(8,128)(2,1)S(1)}, u32[]{:S(2)}, u32[]{:S(2)}) collective-permute-start(bf16[4,32,512]{2,1,0:T(8,128)(2,1)S(1)} %get-tuple-element.60), channel_id=1, source_target_pairs={{0,8},{2,10},{4,12},{6,14},{8,0},{10,2},{12,4},{14,6},{1,9},{3,11}... | collective-permute-start | bytes 393224 | tf_op jit(solution)/shard_map/ppermute | solution.py:561
  58.4 2.8 %attend.2 = (bf16[2,32,512]{2,1,0:T(8,128)(2,1)S(1)}, bf16[2,32,512]{2,1,0:T(8,128)(2,1)S(1)}, bf16[2,32,512]{2,1,0:T(8,128)(2,1)S(1)}, bf16[2,32,512]{2,1,0:T(8...) custom-call(s32[3]{0:T(128)S(1)} %pad_add_fusion.scalars, ...), custom_call_target="tpu_custom_call" | custom-call | flops 1342177280 | bytes 2621440 | tf_op jit(solution)/shard_map/attend/pallas_call | solution.py:488
  61.2 2.0 %collective-permute-start.21 = (bf16[2,32,512]{2,1,0:T(8,128)(2,1)S(1)}, bf16[2,32,512]{2,1,0:T(8,128)(2,1)S(1)}, u32[]{:S(2)}, u32[]{:S(2)}) collective-permute-start(bf16[2,32,512]{2,1,0:T(8,128)(2,1)S(1)} %get-tuple-element.68), channel_id=1, source_target_pairs={{0,8},{2,10},{4,12},{6,14},{8,0},{10,2},{12,4},{14,6},{1,9},{3,11}... | collective-permute-start | bytes 196616 | tf_op jit(solution)/shard_map/ppermute | solution.py:561
  63.1 4.5 %collective-permute-start.22 = (bf16[2,32,512]{2,1,0:T(8,128)(2,1)S(1)}, bf16[2,32,512]{2,1,0:T(8,128)(2,1)S(1)}, u32[]{:S(2)}, u32[]{:S(2)}) collective-permute-start(bf16[2,32,512]{2,1,0:T(8,128)(2,1)S(1)} %get-tuple-element.78), channel_id=1, source_target_pairs={{0,10},{2,8},{4,14},{6,12},{8,2},{10,0},{12,6},{14,4},{1,11},{3,9}... | collective-permute-start | bytes 196616 | tf_op jit(solution)/shard_map/ppermute | solution.py:561
  67.7 2.4 %collective-permute-start.23 = (bf16[2,32,512]{2,1,0:T(8,128)(2,1)S(1)}, bf16[2,32,512]{2,1,0:T(8,128)(2,1)S(1)}, u32[]{:S(2)}, u32[]{:S(2)}) collective-permute-start(bf16[2,32,512]{2,1,0:T(8,128)(2,1)S(1)} %get-tuple-element.79), channel_id=1, source_target_pairs={{0,12},{2,14},{4,8},{6,10},{8,4},{10,6},{12,0},{14,2},{1,13},{3,15... | collective-permute-start | bytes 196616 | tf_op jit(solution)/shard_map/ppermute | solution.py:561
  71.3 4.4 %collective-permute-start.24 = (bf16[2,32,512]{2,1,0:T(8,128)(2,1)S(1)}, bf16[2,32,512]{2,1,0:T(8,128)(2,1)S(1)}, u32[]{:S(2)}, u32[]{:S(2)}) collective-permute-start(bf16[2,32,512]{2,1,0:T(8,128)(2,1)S(1)} %get-tuple-element.80), channel_id=1, source_target_pairs={{0,14},{2,12},{4,10},{6,8},{8,6},{10,4},{12,2},{14,0},{1,15},{3,13... | collective-permute-start | bytes 196616 | tf_op jit(solution)/shard_map/ppermute | solution.py:561
  76.1 2.8 %attend.3 = (bf16[2,32,512]{2,1,0:T(8,128)(2,1)S(1)}, bf16[2,32,512]{2,1,0:T(8,128)(2,1)S(1)}, bf16[2,32,512]{2,1,0:T(8,128)(2,1)S(1)}, bf16[2,32,512]{2,1,0:T(8...) custom-call(s32[3]{0:T(128)S(1)} %pad_add_fusion.scalars, ...), custom_call_target="tpu_custom_call" | custom-call | flops 1342177280 | bytes 2621440 | tf_op jit(solution)/shard_map/attend/pallas_call | solution.py:488
  78.9 1.3 %collective-permute-start.26 = (bf16[2,32,512]{2,1,0:T(8,128)(2,1)S(1)}, bf16[2,32,512]{2,1,0:T(8,128)(2,1)S(1)}, u32[]{:S(2)}, u32[]{:S(2)}) collective-permute-start(bf16[2,32,512]{2,1,0:T(8,128)(2,1)S(1)} %get-tuple-element.82), channel_id=1, source_target_pairs={{0,6},{2,4},{4,2},{6,0},{8,14},{10,12},{12,10},{14,8},{1,7},{3,5},... | collective-permute-start | bytes 196616 | tf_op jit(solution)/shard_map/ppermute | solution.py:561
  80.2 1.9 %collective-permute-start.27 = (bf16[2,32,512]{2,1,0:T(8,128)(2,1)S(1)}, bf16[2,32,512]{2,1,0:T(8,128)(2,1)S(1)}, u32[]{:S(2)}, u32[]{:S(2)}) collective-permute-start(bf16[2,32,512]{2,1,0:T(8,128)(2,1)S(1)} %get-tuple-element.84), channel_id=1, source_target_pairs={{0,2},{2,0},{4,6},{6,4},{8,10},{10,8},{12,14},{14,12},{1,3},{3,1},... | collective-permute-start | bytes 196616 | tf_op jit(solution)/shard_map/ppermute | solution.py:561
  82.1 2.0 %collective-permute-start.14 = (bf16[2,32,512]{2,1,0:T(8,128)(2,1)S(1)}, bf16[2,32,512]{2,1,0:T(8,128)(2,1)S(1)}, u32[]{:S(2)}, u32[]{:S(2)}) collective-permute-start(bf16[2,32,512]{2,1,0:T(8,128)(2,1)S(1)} %get-tuple-element.70), channel_id=1, source_target_pairs={{0,8},{2,10},{4,12},{6,14},{8,0},{10,2},{12,4},{14,6},{1,9},{3,11}... | collective-permute-start | bytes 196616 | tf_op jit(solution)/shard_map/ppermute | solution.py:561
  84.1 1.5 %collective-permute-start.15 = (bf16[2,32,512]{2,1,0:T(8,128)(2,1)S(1)}, bf16[2,32,512]{2,1,0:T(8,128)(2,1)S(1)}, u32[]{:S(2)}, u32[]{:S(2)}) collective-permute-start(bf16[2,32,512]{2,1,0:T(8,128)(2,1)S(1)} %get-tuple-element.71), channel_id=1, source_target_pairs={{0,10},{2,8},{4,14},{6,12},{8,2},{10,0},{12,6},{14,4},{1,11},{3,9}... | collective-permute-start | bytes 196616 | tf_op jit(solution)/shard_map/ppermute | solution.py:561
  86.5 3.2 %collective-permute-start.17 = (bf16[2,32,512]{2,1,0:T(8,128)(2,1)S(1)}, bf16[2,32,512]{2,1,0:T(8,128)(2,1)S(1)}, u32[]{:S(2)}, u32[]{:S(2)}) collective-permute-start(bf16[2,32,512]{2,1,0:T(8,128)(2,1)S(1)} %get-tuple-element.73), channel_id=1, source_target_pairs={{0,14},{2,12},{4,10},{6,8},{8,6},{10,4},{12,2},{14,0},{1,15},{3,13... | collective-permute-start | bytes 196616 | tf_op jit(solution)/shard_map/ppermute | solution.py:561
  90.9 1.4 %collective-permute-start.19 = (bf16[2,32,512]{2,1,0:T(8,128)(2,1)S(1)}, bf16[2,32,512]{2,1,0:T(8,128)(2,1)S(1)}, u32[]{:S(2)}, u32[]{:S(2)}) collective-permute-start(bf16[2,32,512]{2,1,0:T(8,128)(2,1)S(1)} %get-tuple-element.75), channel_id=1, source_target_pairs={{0,6},{2,4},{4,2},{6,0},{8,14},{10,12},{12,10},{14,8},{1,7},{3,5},... | collective-permute-start | bytes 196616 | tf_op jit(solution)/shard_map/ppermute | solution.py:561
  92.4 1.5 %collective-permute-done.15.refs_1_ = bf16[2,32,512]{2,1,0:T(8,128)(2,1)S(1)} collective-permute-done((bf16[2,32,512]{2,1,0:T(8,128)(2,1)S(1)}, bf16[2,32,512]{2,1,0:T(8,128)(2,1)S(1)}, u32[]{:S(2)}, u32[]{:S(2)}) %collective-permute-start.15) | collective-permute-done | bytes 65568 | tf_op jit(solution)/shard_map/ppermute | solution.py:561
  93.8 2.0 %collective-permute-start.20 = (bf16[2,32,512]{2,1,0:T(8,128)(2,1)S(1)}, bf16[2,32,512]{2,1,0:T(8,128)(2,1)S(1)}, u32[]{:S(2)}, u32[]{:S(2)}) collective-permute-start(bf16[2,32,512]{2,1,0:T(8,128)(2,1)S(1)} %get-tuple-element.77), channel_id=1, source_target_pairs={{0,2},{2,0},{4,6},{6,4},{8,10},{10,8},{12,14},{14,12},{1,3},{3,1},... | collective-permute-start | bytes 196616 | tf_op jit(solution)/shard_map/ppermute | solution.py:561
  95.9 1.4 %collect.2.refs_8_ = bf16[2,16,32,512]{3,2,1,0:T(8,128)(2,1)} custom-call(s32[3]{0:T(128)S(1)} %pad_add_fusion.scalars, bf16[2,32,512]{2,1,0:T(8,128)(2,1)S(1)} %collective-permute-done.21.refs_0_, bf16[2,32,512]{2,1,0:T(8,128)(2,1)S(1)} %collective-permute-done.22.refs_1_, bf16[2,32,512]{2,1,0:T(8,128)(2,1)S(1)} %collective-permute-done.23.refs_2_, ...), custom_call_target="tpu_custom_call" | custom-call | tf_op jit(solution)/shard_map/collect/pallas_call | solution.py:516
  98.1 1.4 %collect.3 = bf16[2,16,32,512]{3,2,1,0:T(8,128)(2,1)} custom-call(s32[3]{0:T(128)S(1)} %pad_add_fusion.scalars, bf16[2,32,512]{2,1,0:T(8,128)(2,1)S(1)} %collective-permute-done.14.refs_0_, bf16[2,32,512]{2,1,0:T(8,128)(2,1)S(1)} %collective-permute-done.15.refs_1_, ...), custom_call_target="tpu_custom_call", output_to_operand_aliasing={{}: (9, {})} | custom-call | tf_op jit(solution)/shard_map/collect/pallas_call | solution.py:516
  (72 shorter events, 10.3 us)
Async XLA Ops:
  2.3 17.1 %collective-permute-start.1 = (bf16[3,10,16,512]{3,2,1,0:T(8,128)(2,1)S(1)}, bf16[3,10,16,512]{3,2,1,0:T(8,128)(2,1)S(1)}, u32[]{:S(2)}, u32[]{:S(2)}) collective-permute-start(bf16[3,10,16,512]{3,2,1,0:T(8,128)(2,1)S(1)} %get-tuple-element.46), channel_id=1, source_target_pairs={{0,2},{2,0},{4,6},{6,4},{8,10},{10,8},{12,14},{14,12},{1,3},{3,1},... | collective-permute-start | bytes 1474568 | tf_op jit(solution)/shard_map/ppermute | solution.py:561
  7.4 11.8 %collective-permute-start.2 = (bf16[4,18,512]{2,1,0:T(8,128)(2,1)S(1)}, bf16[4,18,512]{2,1,0:T(8,128)(2,1)S(1)}, u32[]{:S(2)}, u32[]{:S(2)}) collective-permute-start(bf16[4,18,512]{2,1,0:T(8,128)(2,1)S(1)} %get-tuple-element.88), channel_id=1, source_target_pairs={{0,1},{1,0},{2,3},{3,2},{4,5},{5,4},{6,7},{7,6},{8,9},{9,8},{10,11... | collective-permute-start | bytes 221192 | tf_op jit(solution)/shard_map/ppermute | solution.py:570
  7.5 11.5 %collective-permute-start.3 = (bf16[4,18,512]{2,1,0:T(8,128)(2,1)S(1)}, bf16[4,18,512]{2,1,0:T(8,128)(2,1)S(1)}, u32[]{:S(2)}, u32[]{:S(2)}) collective-permute-start(bf16[4,18,512]{2,1,0:T(8,128)(2,1)S(1)} %get-tuple-element.87), channel_id=1, source_target_pairs={{0,3},{1,2},{2,1},{3,0},{4,7},{5,6},{6,5},{7,4},{8,11},{9,10},{10,... | collective-permute-start | bytes 221192 | tf_op jit(solution)/shard_map/ppermute | solution.py:576
  7.7 20.3 %collective-permute-start = (bf16[3,8,16,512]{3,2,1,0:T(8,128)(2,1)S(1)}, bf16[3,8,16,512]{3,2,1,0:T(8,128)(2,1)S(1)}, u32[]{:S(2)}, u32[]{:S(2)}) collective-permute-start(bf16[3,8,16,512]{3,2,1,0:T(8,128)(2,1)S(1)} %get-tuple-element.45), channel_id=1, source_target_pairs={{0,2},{2,0},{4,6},{6,4},{8,10},{10,8},{12,14},{14,12},{1,3},{3,1},... | collective-permute-start | bytes 1179656 | tf_op jit(solution)/shard_map/ppermute | solution.py:561
  9.7 21.8 %collective-permute-start.7 = (bf16[1,10,16,512]{3,2,1,0:T(8,128)(2,1)S(1)}, bf16[1,10,16,512]{3,2,1,0:T(8,128)(2,1)S(1)}, u32[]{:S(2)}, u32[]{:S(2)}) collective-permute-start(bf16[1,10,16,512]{3,2,1,0:T(8,128)(2,1)S(1)} %get-tuple-element.52), channel_id=1, source_target_pairs={{0,2},{2,0},{4,6},{6,4},{8,10},{10,8},{12,14},{14,12},{1,3},{3,1},... | collective-permute-start | bytes 491528 | tf_op jit(solution)/shard_map/ppermute | solution.py:561
  19.1 22.0 %collective-permute-start.5 = (bf16[1,8,16,512]{3,2,1,0:T(8,128)(2,1)S(1)}, bf16[1,8,16,512]{3,2,1,0:T(8,128)(2,1)S(1)}, u32[]{:S(2)}, u32[]{:S(2)}) collective-permute-start(bf16[1,8,16,512]{3,2,1,0:T(8,128)(2,1)S(1)} %get-tuple-element.51), channel_id=1, source_target_pairs={{0,2},{2,0},{4,6},{6,4},{8,10},{10,8},{12,14},{14,12},{1,3},{3,1},... | collective-permute-start | bytes 393224 | tf_op jit(solution)/shard_map/ppermute | solution.py:561
  19.4 12.7 %copy-start.2 = (bf16[3,512,512]{2,1,0:T(8,128)(2,1)S(1)}, bf16[3,512,512]{2,1,0:T(8,128)(2,1)}, u32[]{:S(2)}) copy-start(bf16[3,512,512]{2,1,0:T(8,128)(2,1)} %param.13) | copy-start | bytes 4718596
  19.4 12.7 %copy-start.3 = (bf16[3,512,512]{2,1,0:T(8,128)(2,1)S(1)}, bf16[3,512,512]{2,1,0:T(8,128)(2,1)}, u32[]{:S(2)}) copy-start(bf16[3,512,512]{2,1,0:T(8,128)(2,1)} %param.15) | copy-start | bytes 4718596
  19.4 12.6 %copy-start.4 = (f32[512]{0:T(512)S(1)}, f32[512]{0:T(512)}, u32[]{:S(2)}) copy-start(f32[512]{0:T(512)} %param.14) | copy-start | bytes 6148
  19.4 12.6 %copy-start.5 = (f32[512]{0:T(512)S(1)}, f32[512]{0:T(512)}, u32[]{:S(2)}) copy-start(f32[512]{0:T(512)} %param.16) | copy-start | bytes 6148
  20.0 17.1 %collective-permute-start.6 = (bf16[3,11,16,512]{3,2,1,0:T(8,128)(2,1)S(1)}, bf16[3,11,16,512]{3,2,1,0:T(8,128)(2,1)S(1)}, u32[]{:S(2)}, u32[]{:S(2)}) collective-permute-start(bf16[3,11,16,512]{3,2,1,0:T(8,128)(2,1)S(1)} %join_last.2.last), channel_id=1, source_target_pairs={{0,4},{2,6},{4,8},{6,10},{8,12},{10,14},{12,0},{14,2},{1,5},{3,7},... | collective-permute-start | bytes 1622024 | tf_op jit(solution)/shard_map/ppermute | solution.py:561
  28.5 18.0 %collective-permute-start.4 = (bf16[3,9,16,512]{3,2,1,0:T(8,128)(2,1)S(1)}, bf16[3,9,16,512]{3,2,1,0:T(8,128)(2,1)S(1)}, u32[]{:S(2)}, u32[]{:S(2)}) collective-permute-start(bf16[3,9,16,512]{3,2,1,0:T(8,128)(2,1)S(1)} %join_last.3.last), channel_id=1, source_target_pairs={{0,4},{2,6},{4,8},{6,10},{8,12},{10,14},{12,0},{14,2},{1,5},{3,7},... | collective-permute-start | bytes 1327112 | tf_op jit(solution)/shard_map/ppermute | solution.py:561
  41.1 16.3 %collective-permute-start.11 = (bf16[4,32,512]{2,1,0:T(8,128)(2,1)S(1)}, bf16[4,32,512]{2,1,0:T(8,128)(2,1)S(1)}, u32[]{:S(2)}, u32[]{:S(2)}) collective-permute-start(bf16[4,32,512]{2,1,0:T(8,128)(2,1)S(1)} %get-tuple-element.64), channel_id=1, source_target_pairs={{0,8},{2,10},{4,12},{6,14},{8,0},{10,2},{12,4},{14,6},{1,9},{3,11}... | collective-permute-start | bytes 393224 | tf_op jit(solution)/shard_map/ppermute | solution.py:561
  44.3 14.0 %collective-permute-start.12 = (bf16[4,32,512]{2,1,0:T(8,128)(2,1)S(1)}, bf16[4,32,512]{2,1,0:T(8,128)(2,1)S(1)}, u32[]{:S(2)}, u32[]{:S(2)}) collective-permute-start(bf16[4,32,512]{2,1,0:T(8,128)(2,1)S(1)} %get-tuple-element.65), channel_id=1, source_target_pairs={{0,12},{2,14},{4,8},{6,10},{8,4},{10,6},{12,0},{14,2},{1,13},{3,15... | collective-permute-start | bytes 393224 | tf_op jit(solution)/shard_map/ppermute | solution.py:561
  45.6 12.7 %collective-permute-start.13 = (bf16[4,32,512]{2,1,0:T(8,128)(2,1)S(1)}, bf16[4,32,512]{2,1,0:T(8,128)(2,1)S(1)}, u32[]{:S(2)}, u32[]{:S(2)}) collective-permute-start(bf16[4,32,512]{2,1,0:T(8,128)(2,1)S(1)} %get-tuple-element.66), channel_id=1, source_target_pairs={{0,4},{2,6},{4,0},{6,2},{8,12},{10,14},{12,8},{14,10},{1,5},{3,7},... | collective-permute-start | bytes 393224 | tf_op jit(solution)/shard_map/ppermute | solution.py:561
  53.9 13.8 %collective-permute-start.10 = (bf16[4,32,512]{2,1,0:T(8,128)(2,1)S(1)}, bf16[4,32,512]{2,1,0:T(8,128)(2,1)S(1)}, u32[]{:S(2)}, u32[]{:S(2)}) collective-permute-start(bf16[4,32,512]{2,1,0:T(8,128)(2,1)S(1)} %get-tuple-element.62), channel_id=1, source_target_pairs={{0,4},{2,6},{4,0},{6,2},{8,12},{10,14},{12,8},{14,10},{1,5},{3,7},... | collective-permute-start | bytes 393224 | tf_op jit(solution)/shard_map/ppermute | solution.py:561
  55.7 15.6 %collective-permute-start.8 = (bf16[4,32,512]{2,1,0:T(8,128)(2,1)S(1)}, bf16[4,32,512]{2,1,0:T(8,128)(2,1)S(1)}, u32[]{:S(2)}, u32[]{:S(2)}) collective-permute-start(bf16[4,32,512]{2,1,0:T(8,128)(2,1)S(1)} %get-tuple-element.60), channel_id=1, source_target_pairs={{0,8},{2,10},{4,12},{6,14},{8,0},{10,2},{12,4},{14,6},{1,9},{3,11}... | collective-permute-start | bytes 393224 | tf_op jit(solution)/shard_map/ppermute | solution.py:561
  57.4 18.3 %collective-permute-start.9 = (bf16[4,32,512]{2,1,0:T(8,128)(2,1)S(1)}, bf16[4,32,512]{2,1,0:T(8,128)(2,1)S(1)}, u32[]{:S(2)}, u32[]{:S(2)}) collective-permute-start(bf16[4,32,512]{2,1,0:T(8,128)(2,1)S(1)} %get-tuple-element.61), channel_id=1, source_target_pairs={{0,12},{2,14},{4,8},{6,10},{8,4},{10,6},{12,0},{14,2},{1,13},{3,15... | collective-permute-start | bytes 393224 | tf_op jit(solution)/shard_map/ppermute | solution.py:561
  61.2 17.7 %collective-permute-start.21 = (bf16[2,32,512]{2,1,0:T(8,128)(2,1)S(1)}, bf16[2,32,512]{2,1,0:T(8,128)(2,1)S(1)}, u32[]{:S(2)}, u32[]{:S(2)}) collective-permute-start(bf16[2,32,512]{2,1,0:T(8,128)(2,1)S(1)} %get-tuple-element.68), channel_id=1, source_target_pairs={{0,8},{2,10},{4,12},{6,14},{8,0},{10,2},{12,4},{14,6},{1,9},{3,11}... | collective-permute-start | bytes 196616 | tf_op jit(solution)/shard_map/ppermute | solution.py:561
  63.1 17.0 %collective-permute-start.22 = (bf16[2,32,512]{2,1,0:T(8,128)(2,1)S(1)}, bf16[2,32,512]{2,1,0:T(8,128)(2,1)S(1)}, u32[]{:S(2)}, u32[]{:S(2)}) collective-permute-start(bf16[2,32,512]{2,1,0:T(8,128)(2,1)S(1)} %get-tuple-element.78), channel_id=1, source_target_pairs={{0,10},{2,8},{4,14},{6,12},{8,2},{10,0},{12,6},{14,4},{1,11},{3,9}... | collective-permute-start | bytes 196616 | tf_op jit(solution)/shard_map/ppermute | solution.py:561
  67.7 14.4 %collective-permute-start.23 = (bf16[2,32,512]{2,1,0:T(8,128)(2,1)S(1)}, bf16[2,32,512]{2,1,0:T(8,128)(2,1)S(1)}, u32[]{:S(2)}, u32[]{:S(2)}) collective-permute-start(bf16[2,32,512]{2,1,0:T(8,128)(2,1)S(1)} %get-tuple-element.79), channel_id=1, source_target_pairs={{0,12},{2,14},{4,8},{6,10},{8,4},{10,6},{12,0},{14,2},{1,13},{3,15... | collective-permute-start | bytes 196616 | tf_op jit(solution)/shard_map/ppermute | solution.py:561
  71.3 12.7 %collective-permute-start.24 = (bf16[2,32,512]{2,1,0:T(8,128)(2,1)S(1)}, bf16[2,32,512]{2,1,0:T(8,128)(2,1)S(1)}, u32[]{:S(2)}, u32[]{:S(2)}) collective-permute-start(bf16[2,32,512]{2,1,0:T(8,128)(2,1)S(1)} %get-tuple-element.80), channel_id=1, source_target_pairs={{0,14},{2,12},{4,10},{6,8},{8,6},{10,4},{12,2},{14,0},{1,15},{3,13... | collective-permute-start | bytes 196616 | tf_op jit(solution)/shard_map/ppermute | solution.py:561
  75.7 9.9 %collective-permute-start.25 = (bf16[2,32,512]{2,1,0:T(8,128)(2,1)S(1)}, bf16[2,32,512]{2,1,0:T(8,128)(2,1)S(1)}, u32[]{:S(2)}, u32[]{:S(2)}) collective-permute-start(bf16[2,32,512]{2,1,0:T(8,128)(2,1)S(1)} %get-tuple-element.81), channel_id=1, source_target_pairs={{0,4},{2,6},{4,0},{6,2},{8,12},{10,14},{12,8},{14,10},{1,5},{3,7},... | collective-permute-start | bytes 196616 | tf_op jit(solution)/shard_map/ppermute | solution.py:561
  78.9 7.6 %collective-permute-start.26 = (bf16[2,32,512]{2,1,0:T(8,128)(2,1)S(1)}, bf16[2,32,512]{2,1,0:T(8,128)(2,1)S(1)}, u32[]{:S(2)}, u32[]{:S(2)}) collective-permute-start(bf16[2,32,512]{2,1,0:T(8,128)(2,1)S(1)} %get-tuple-element.82), channel_id=1, source_target_pairs={{0,6},{2,4},{4,2},{6,0},{8,14},{10,12},{12,10},{14,8},{1,7},{3,5},... | collective-permute-start | bytes 196616 | tf_op jit(solution)/shard_map/ppermute | solution.py:561
  80.2 9.6 %collective-permute-start.27 = (bf16[2,32,512]{2,1,0:T(8,128)(2,1)S(1)}, bf16[2,32,512]{2,1,0:T(8,128)(2,1)S(1)}, u32[]{:S(2)}, u32[]{:S(2)}) collective-permute-start(bf16[2,32,512]{2,1,0:T(8,128)(2,1)S(1)} %get-tuple-element.84), channel_id=1, source_target_pairs={{0,2},{2,0},{4,6},{6,4},{8,10},{10,8},{12,14},{14,12},{1,3},{3,1},... | collective-permute-start | bytes 196616 | tf_op jit(solution)/shard_map/ppermute | solution.py:561
  82.1 8.9 %collective-permute-start.14 = (bf16[2,32,512]{2,1,0:T(8,128)(2,1)S(1)}, bf16[2,32,512]{2,1,0:T(8,128)(2,1)S(1)}, u32[]{:S(2)}, u32[]{:S(2)}) collective-permute-start(bf16[2,32,512]{2,1,0:T(8,128)(2,1)S(1)} %get-tuple-element.70), channel_id=1, source_target_pairs={{0,8},{2,10},{4,12},{6,14},{8,0},{10,2},{12,4},{14,6},{1,9},{3,11}... | collective-permute-start | bytes 196616 | tf_op jit(solution)/shard_map/ppermute | solution.py:561
  84.1 9.8 %collective-permute-start.15 = (bf16[2,32,512]{2,1,0:T(8,128)(2,1)S(1)}, bf16[2,32,512]{2,1,0:T(8,128)(2,1)S(1)}, u32[]{:S(2)}, u32[]{:S(2)}) collective-permute-start(bf16[2,32,512]{2,1,0:T(8,128)(2,1)S(1)} %get-tuple-element.71), channel_id=1, source_target_pairs={{0,10},{2,8},{4,14},{6,12},{8,2},{10,0},{12,6},{14,4},{1,11},{3,9}... | collective-permute-start | bytes 196616 | tf_op jit(solution)/shard_map/ppermute | solution.py:561
  85.6 11.7 %collective-permute-start.16 = (bf16[2,32,512]{2,1,0:T(8,128)(2,1)S(1)}, bf16[2,32,512]{2,1,0:T(8,128)(2,1)S(1)}, u32[]{:S(2)}, u32[]{:S(2)}) collective-permute-start(bf16[2,32,512]{2,1,0:T(8,128)(2,1)S(1)} %get-tuple-element.72), channel_id=1, source_target_pairs={{0,12},{2,14},{4,8},{6,10},{8,4},{10,6},{12,0},{14,2},{1,13},{3,15... | collective-permute-start | bytes 196616 | tf_op jit(solution)/shard_map/ppermute | solution.py:561
  86.5 10.8 %collective-permute-start.17 = (bf16[2,32,512]{2,1,0:T(8,128)(2,1)S(1)}, bf16[2,32,512]{2,1,0:T(8,128)(2,1)S(1)}, u32[]{:S(2)}, u32[]{:S(2)}) collective-permute-start(bf16[2,32,512]{2,1,0:T(8,128)(2,1)S(1)} %get-tuple-element.73), channel_id=1, source_target_pairs={{0,14},{2,12},{4,10},{6,8},{8,6},{10,4},{12,2},{14,0},{1,15},{3,13... | collective-permute-start | bytes 196616 | tf_op jit(solution)/shard_map/ppermute | solution.py:561
  89.8 7.5 %collective-permute-start.18 = (bf16[2,32,512]{2,1,0:T(8,128)(2,1)S(1)}, bf16[2,32,512]{2,1,0:T(8,128)(2,1)S(1)}, u32[]{:S(2)}, u32[]{:S(2)}) collective-permute-start(bf16[2,32,512]{2,1,0:T(8,128)(2,1)S(1)} %get-tuple-element.74), channel_id=1, source_target_pairs={{0,4},{2,6},{4,0},{6,2},{8,12},{10,14},{12,8},{14,10},{1,5},{3,7},... | collective-permute-start | bytes 196616 | tf_op jit(solution)/shard_map/ppermute | solution.py:561
  90.9 6.4 %collective-permute-start.19 = (bf16[2,32,512]{2,1,0:T(8,128)(2,1)S(1)}, bf16[2,32,512]{2,1,0:T(8,128)(2,1)S(1)}, u32[]{:S(2)}, u32[]{:S(2)}) collective-permute-start(bf16[2,32,512]{2,1,0:T(8,128)(2,1)S(1)} %get-tuple-element.75), channel_id=1, source_target_pairs={{0,6},{2,4},{4,2},{6,0},{8,14},{10,12},{12,10},{14,8},{1,7},{3,5},... | collective-permute-start | bytes 196616 | tf_op jit(solution)/shard_map/ppermute | solution.py:561
  93.8 4.3 %collective-permute-start.20 = (bf16[2,32,512]{2,1,0:T(8,128)(2,1)S(1)}, bf16[2,32,512]{2,1,0:T(8,128)(2,1)S(1)}, u32[]{:S(2)}, u32[]{:S(2)}) collective-permute-start(bf16[2,32,512]{2,1,0:T(8,128)(2,1)S(1)} %get-tuple-element.77), channel_id=1, source_target_pairs={{0,2},{2,0},{4,6},{6,4},{8,10},{10,8},{12,14},{14,12},{1,3},{3,1},... | collective-permute-start | bytes 196616 | tf_op jit(solution)/shard_map/ppermute | solution.py:561
  (9 other events, 92.7 us)

commit v13 on v11

--- a/solution.py
+++ b/solution.py
@@ -63,7 +63,7 @@
     rest = frames - taps
     for k, (begin, end) in enumerate(spans):
         for t in range(frames):
-            target = outs[k].at[t - rest] if t >= rest else outs[len(spans) + k].at[t]
+            target = outs[2 * k].at[t - rest] if t >= rest else outs[2 * k + 1].at[t]
             cut(target, video, t, 1 - scalars[0], begin, end, half)
 
 
@@ -71,8 +71,8 @@
     frames, _, width, channels = video.shape
     shapes = [
         (count, end - begin, width, channels)
+        for begin, end in spans
         for count in (taps, frames - taps)
-        for begin, end in spans
     ]
     return pl.pallas_call(
         partial(send_kernel, spans, half),
@@ -578,38 +578,46 @@
 
     owners = levels if direct else 1
     edges = [[edge_rows(e, begin, end) for e in (own_edge, other_edge)] for begin, end in spans]
-    lasts, halos = [], []
+    lasts, firsts, halos = [], [], []
     newest = w_space
     for k, (begin, end) in enumerate(spans):
-        newest = join(
-            join_last_kernel, taps, "join_last", begin, end, half, scalars, video,
-            after(received[k], newest), *edges[k]
-        )
-        lasts.append(newest)
-        halos.append(tm_permute(newest, lambda i: (i + pair) % devices))
+        span = (begin, end, half, scalars, video)
+        arrived = after(received[2 * k], newest)
+        last = join(join_last_kernel, taps, "join_last", *span, arrived, *edges[k])
+        lasts.append(last)
+        halos.append(tm_permute(last, lambda i: (i + pair) % devices))
+        if k == 0:
+            others = after(received[1], last)
+            firsts.append(join(
+                join_first_kernel, pair * frames - taps, "join_first", *span, arrived, others,
+                *edges[k]
+            ))
+            part, spatial, *kept = early(
+                scalars, firsts[0], last, chunks == 1, size, end - begin, *weights
+            )
+            newest = part
 
     spatials = []
-    kept = None
     for k, (begin, end) in enumerate(spans):
         rows, final = end - begin, k == chunks - 1
-        others = after(received[chunks + k], newest)
-        first = join(
-            join_first_kernel, pair * frames - taps, "join_first", begin, end, half, scalars,
-            video, received[k], others, *edges[k]
-        )
         if k == 0:
-            part, spatial, *kept = early(scalars, first, lasts[k], final, size, rows, *weights)
+            part = after(part, lasts[-1])
             made = late(
-                owners, scalars, halos[k], first, part, spatial, final, rows, *weights
+                owners, scalars, halos[k], firsts[0], part, spatial, final, rows, *weights
             )
             kept = [*made[owners:], *kept]
         else:
+            span = (begin, end, half, scalars, video)
+            others = after(received[2 * k + 1], spatials[-1][0])
+            first = join(
+                join_first_kernel, pair * frames - taps, "join_first", *span, received[2 * k],
+                others, *edges[k]
+            )
             made = full(
                 owners, scalars, halos[k], first, lasts[k], kept, final, size, rows, *weights
             )
             kept = made[owners:]
         spatials.append(made[:owners])
-        newest = made[0]
 
     newest = spatials[-1][0]
     if direct:

time: 98.3 us -> 95.9 us (0.976)
  starting transfers between devices: 44.4 us -> 42.1 us
    ppermute x26, starting transfers between devices: 44.2 us -> 41.9 us  [tm_permute(): lax.ppermute(value, 'tm', [(i, move(i)) for i in range(devices) if move(i...]
  transfers between devices with their start and end apart: 28 -> 28, of which waited for: 6 -> 9; matrix products, arithmetic and copies ran while one was open for 5% -> 5% of each run, Pallas kernels for 26% -> 27%
where the time goes in v13:
time: 95.9 us; the launch traced here: 95.7 us
  starting transfers between devices  42.1 us (44%)
  Pallas kernels  27.6 us (29%)
  waiting for transfers between devices  18.7 us (19%)
  local copies, waits for them, and re-layouts  3.73 us (4%)
  other arithmetic  2.99 us (3%)
    ppermute x26, starting transfers between devices, tm_permute(): lax.ppermute(value, 'tm', [(i, move(i)) for i in range(devices) if move(i...  41.9 us
    ppermute x26, waiting for transfers between devices, tm_permute(): lax.ppermute(value, 'tm', [(i, move(i)) for i in range(devices) if move(i...  12.2 us
    pallas_call x1, Pallas kernels, full(): pl.pallas_call(partial(full_kernel, owners, final, rows), out_shape=[jax....  7.33 us
    ppermute x1, waiting for transfers between devices, per_device(): other_edge = lax.ppermute(other_edge, ('tm', 'cols'), aslant)  6.52 us
    pallas_call x2, Pallas kernels, attend(): pl.pallas_call(partial(attend_kernel, frames_per, lanes, count), out_shap...  5.58 us
    pallas_call x1, Pallas kernels, early(): pl.pallas_call(partial(early_kernel, final, rows), out_shape=shapes, in_s...  5.03 us
    pallas_call x1, Pallas kernels, late(): pl.pallas_call(partial(late_kernel, owners, final, rows), out_shape=[jax....  3.91 us
    select_n x1, other arithmetic, per_device(): w_space = jnp.where(after(place, video) >= 0, w_space, 0)  2.79 us
  transfers between devices with their start and end apart: 28, of which 9 were waited for; matrix products, arithmetic and copies ran while one was open for 5% of the time, Pallas kernels for 27%

profile of v13, /device:TPU:0, one launch (start us, length us, event | category | flops | bytes accessed | tf_op | source)
XLA Modules:
  0.0 95.7 jit_solution(1357750714841507485)
XLA Ops:
  0.1 1.6 %copy-done = bf16[4,32,16,512]{3,2,1,0:T(8,128)(2,1)S(1)} copy-done((bf16[4,32,16,512]{3,2,1,0:T(8,128)(2,1)S(1)}, bf16[4,32,16,512]{3,2,1,0:T(8,128)(2,1)}, u32[]{:S(2)}) %copy-start) | copy-done | bytes 2097176
  2.3 3.0 %collective-permute-start.1 = (bf16[3,10,16,512]{3,2,1,0:T(8,128)(2,1)S(1)}, bf16[3,10,16,512]{3,2,1,0:T(8,128)(2,1)S(1)}, u32[]{:S(2)}, u32[]{:S(2)}) collective-permute-start(bf16[3,10,16,512]{3,2,1,0:T(8,128)(2,1)S(1)} %get-tuple-element.47), channel_id=1, source_target_pairs={{0,2},{2,0},{4,6},{6,4},{8,10},{10,8},{12,14},{14,12},{1,3},{3,1},... | collective-permute-start | bytes 1474568 | tf_op jit(solution)/shard_map/ppermute | solution.py:558
  5.3 1.9 %fusion.3 = (bf16[4,32,1,512]{3,2,1,0:T(2,128)(2,1)S(1)}, bf16[4,32,1,512]{3,2,1,0:T(2,128)(2,1)S(1)}) fusion(bf16[4,32,16,512]{3,2,1,0:T(8,128)(2,1)} %video.9), kind=kLoop, calls=%fused_computation.12 | loop fusion | bytes 524288 | tf_op jit(solution)/shard_map/slice | solution.py:562
  7.6 2.0 %collective-permute-start.2 = (bf16[1,10,16,512]{3,2,1,0:T(8,128)(2,1)S(1)}, bf16[1,10,16,512]{3,2,1,0:T(8,128)(2,1)S(1)}, u32[]{:S(2)}, u32[]{:S(2)}) collective-permute-start(bf16[1,10,16,512]{3,2,1,0:T(8,128)(2,1)S(1)} %get-tuple-element.50), channel_id=1, source_target_pairs={{0,2},{2,0},{4,6},{6,4},{8,10},{10,8},{12,14},{14,12},{1,3},{3,1},... | collective-permute-start | bytes 491528 | tf_op jit(solution)/shard_map/ppermute | solution.py:558
  9.7 2.8 %broadcast_select_fusion.w_space = bf16[9,512,512]{2,1,0:T(8,128)(2,1)S(1)} fusion(bf16[9,512,512]{2,1,0:T(8,128)(2,1)} %param.17, pred[]{:T(512)S(6)} %ge.3), kind=kLoop, calls=%fused_computation | loop fusion | flops 2359296 | bytes 9437185 | tf_op jit(solution)/shard_map/jit(_where)/select_n | solution.py:543
  12.5 6.5 %collective-permute-done.4 = bf16[4,18,512]{2,1,0:T(8,128)(2,1)S(1)} collective-permute-done((bf16[4,18,512]{2,1,0:T(8,128)(2,1)S(1)}, bf16[4,18,512]{2,1,0:T(8,128)(2,1)S(1)}, u32[]{:S(2)}, u32[]{:S(2)}) %collective-permute-start.4) | collective-permute-done | bytes 73760 | tf_op jit(solution)/shard_map/ppermute | solution.py:573
  19.9 1.6 %collective-permute-start.7 = (bf16[3,11,16,512]{3,2,1,0:T(8,128)(2,1)S(1)}, bf16[3,11,16,512]{3,2,1,0:T(8,128)(2,1)S(1)}, u32[]{:S(2)}, u32[]{:S(2)}) collective-permute-start(bf16[3,11,16,512]{3,2,1,0:T(8,128)(2,1)S(1)} %join_last.2.last), channel_id=1, source_target_pairs={{0,4},{2,6},{4,8},{6,10},{8,12},{10,14},{12,0},{14,2},{1,5},{3,7},... | collective-permute-start | bytes 1622024 | tf_op jit(solution)/shard_map/ppermute | solution.py:558
  21.5 1.5 %collective-permute-done.2.others = bf16[1,10,16,512]{3,2,1,0:T(8,128)(2,1)S(1)} collective-permute-done((bf16[1,10,16,512]{3,2,1,0:T(8,128)(2,1)S(1)}, bf16[1,10,16,512]{3,2,1,0:T(8,128)(2,1)S(1)}, u32[]{:S(2)}, u32[]{:S(2)}) %collective-permute-start.2) | collective-permute-done | bytes 163872 | tf_op jit(solution)/shard_map/ppermute | solution.py:558
  23.7 5.0 %early.1 = (f32[176,512]{1,0:T(8,128)S(1)}, bf16[2,128,512]{2,1,0:T(8,128)(2,1)S(1)}, bf16[3,2,2,16,512]{4,3,2,1,0:T(8,128)(2,1)S(1)}) custom-call(s32[3]{0:T(128)S(1)} %pad_add_fusion.scalars, bf16[5,11,16,512]{3,2,1,0:T(8,128)(2,1)S(1)} %join_first.2.first, bf16[3,11,16,512]{3,2,1,0:T(8,128)(2,1)S(1)} %join_last.2.last, bf16[1536,512]{1,0:T(8,128)(2,1)S(1)} %bitcast.26, ...), custom_call_target="tpu_custom_call" | custom-call | flops 3607101440 | bytes 9312256 | tf_op jit(solution)/shard_map/early/pallas_call | solution.py:239
  28.7 1.9 %collective-permute-done.received = bf16[3,8,16,512]{3,2,1,0:T(8,128)(2,1)S(1)} collective-permute-done((bf16[3,8,16,512]{3,2,1,0:T(8,128)(2,1)S(1)}, bf16[3,8,16,512]{3,2,1,0:T(8,128)(2,1)S(1)}, u32[]{:S(2)}, u32[]{:S(2)}) %collective-permute-start) | collective-permute-done | bytes 393248 | tf_op jit(solution)/shard_map/ppermute | solution.py:558
  31.2 1.8 %collective-permute-start.5 = (bf16[3,9,16,512]{3,2,1,0:T(8,128)(2,1)S(1)}, bf16[3,9,16,512]{3,2,1,0:T(8,128)(2,1)S(1)}, u32[]{:S(2)}, u32[]{:S(2)}) collective-permute-start(bf16[3,9,16,512]{3,2,1,0:T(8,128)(2,1)S(1)} %join_last.3.last), channel_id=1, source_target_pairs={{0,4},{2,6},{4,8},{6,10},{8,12},{10,14},{12,0},{14,2},{1,5},{3,7},... | collective-permute-start | bytes 1327112 | tf_op jit(solution)/shard_map/ppermute | solution.py:558
  33.0 1.5 %collective-permute-start.6 = (bf16[1,8,16,512]{3,2,1,0:T(8,128)(2,1)S(1)}, bf16[1,8,16,512]{3,2,1,0:T(8,128)(2,1)S(1)}, u32[]{:S(2)}, u32[]{:S(2)}) collective-permute-start(bf16[1,8,16,512]{3,2,1,0:T(8,128)(2,1)S(1)} %get-tuple-element.55), channel_id=1, source_target_pairs={{0,2},{2,0},{4,6},{6,4},{8,10},{10,8},{12,14},{14,12},{1,3},{3,1},... | collective-permute-start | bytes 393224 | tf_op jit(solution)/shard_map/ppermute | solution.py:558
  34.6 2.3 %collective-permute-done.7.halo = bf16[3,11,16,512]{3,2,1,0:T(8,128)(2,1)S(1)} collective-permute-done((bf16[3,11,16,512]{3,2,1,0:T(8,128)(2,1)S(1)}, bf16[3,11,16,512]{3,2,1,0:T(8,128)(2,1)S(1)}, u32[]{:S(2)}, u32[]{:S(2)}) %collective-permute-start.7) | collective-permute-done | bytes 540704 | tf_op jit(solution)/shard_map/ppermute | solution.py:558
  36.9 3.9 %late.1 = (bf16[4,32,512]{2,1,0:T(8,128)(2,1)S(1)}, bf16[4,32,512]{2,1,0:T(8,128)(2,1)S(1)}, bf16[4,32,512]{2,1,0:T(8,128)(2,1)S(1)}, bf16[4,32,512]{2,1,0:T(8,128)(2,1)S(1)}, bf16[3,2,2,16,512]{4,3,2,1,0:T(8,128)(2,1)S(1)}) custom-call(s32[3]{0:T(128)S(1)} %pad_add_fusion.scalars, bf16[3,11,16,512]{3,2,1,0:T(8,128)(2,1)S(1)} %collective-permute-done.7.halo, ...), custom_call_target="tpu_custom_call" | custom-call | flops 2407530496 | bytes 9672704 | tf_op jit(solution)/shard_map/late/pallas_call | solution.py:397
  40.9 2.4 %collective-permute-start.9 = (bf16[4,32,512]{2,1,0:T(8,128)(2,1)S(1)}, bf16[4,32,512]{2,1,0:T(8,128)(2,1)S(1)}, u32[]{:S(2)}, u32[]{:S(2)}) collective-permute-start(bf16[4,32,512]{2,1,0:T(8,128)(2,1)S(1)} %get-tuple-element.65), channel_id=1, source_target_pairs={{0,8},{2,10},{4,12},{6,14},{8,0},{10,2},{12,4},{14,6},{1,9},{3,11}... | collective-permute-start | bytes 393224 | tf_op jit(solution)/shard_map/ppermute | solution.py:558
  43.2 2.0 %collective-permute-start.10 = (bf16[4,32,512]{2,1,0:T(8,128)(2,1)S(1)}, bf16[4,32,512]{2,1,0:T(8,128)(2,1)S(1)}, u32[]{:S(2)}, u32[]{:S(2)}) collective-permute-start(bf16[4,32,512]{2,1,0:T(8,128)(2,1)S(1)} %get-tuple-element.66), channel_id=1, source_target_pairs={{0,12},{2,14},{4,8},{6,10},{8,4},{10,6},{12,0},{14,2},{1,13},{3,15... | collective-permute-start | bytes 393224 | tf_op jit(solution)/shard_map/ppermute | solution.py:558
  46.5 7.3 %full.1 = (bf16[4,32,512]{2,1,0:T(8,128)(2,1)S(1)}, bf16[4,32,512]{2,1,0:T(8,128)(2,1)S(1)}, bf16[4,32,512]{2,1,0:T(8,128)(2,1)S(1)}, bf16[4,32,512]{2,1,0:T(8,128)(2,1)S(1)}) custom-call(s32[3]{0:T(128)S(1)} %pad_add_fusion.scalars, bf16[3,9,16,512]{3,2,1,0:T(8,128)(2,1)S(1)} %collective-permute-done.5.halo, bf16[5,9,16,512]{3,2,1,0:T(8,128)(2,1)S(1)} %join_first.3.first, ...), custom_call_target="tpu_custom_call" | custom-call | flops 5360320512 | bytes 9492480 | tf_op jit(solution)/shard_map/full/pallas_call | solution.py:326
  53.9 4.9 %collective-permute-start.12 = (bf16[4,32,512]{2,1,0:T(8,128)(2,1)S(1)}, bf16[4,32,512]{2,1,0:T(8,128)(2,1)S(1)}, u32[]{:S(2)}, u32[]{:S(2)}) collective-permute-start(bf16[4,32,512]{2,1,0:T(8,128)(2,1)S(1)} %get-tuple-element.70), channel_id=1, source_target_pairs={{0,8},{2,10},{4,12},{6,14},{8,0},{10,2},{12,4},{14,6},{1,9},{3,11}... | collective-permute-start | bytes 393224 | tf_op jit(solution)/shard_map/ppermute | solution.py:558
  58.9 2.8 %attend.2 = (bf16[2,32,512]{2,1,0:T(8,128)(2,1)S(1)}, bf16[2,32,512]{2,1,0:T(8,128)(2,1)S(1)}, bf16[2,32,512]{2,1,0:T(8,128)(2,1)S(1)}, bf16[2,32,512]{2,1,0:T(8...) custom-call(s32[3]{0:T(128)S(1)} %pad_add_fusion.scalars, ...), custom_call_target="tpu_custom_call" | custom-call | flops 1342177280 | bytes 2621440 | tf_op jit(solution)/shard_map/attend/pallas_call | solution.py:487
  63.3 2.0 %collective-permute-start.23 = (bf16[2,32,512]{2,1,0:T(8,128)(2,1)S(1)}, bf16[2,32,512]{2,1,0:T(8,128)(2,1)S(1)}, u32[]{:S(2)}, u32[]{:S(2)}) collective-permute-start(bf16[2,32,512]{2,1,0:T(8,128)(2,1)S(1)} %get-tuple-element.82), channel_id=1, source_target_pairs={{0,6},{2,4},{4,2},{6,0},{8,14},{10,12},{12,10},{14,8},{1,7},{3,5},... | collective-permute-start | bytes 196616 | tf_op jit(solution)/shard_map/ppermute | solution.py:558
  65.2 2.7 %collective-permute-done.12.refs_2_ = bf16[4,32,512]{2,1,0:T(8,128)(2,1)S(1)} collective-permute-done((bf16[4,32,512]{2,1,0:T(8,128)(2,1)S(1)}, bf16[4,32,512]{2,1,0:T(8,128)(2,1)S(1)}, u32[]{:S(2)}, u32[]{:S(2)}) %collective-permute-start.12) | collective-permute-done | bytes 131104 | tf_op jit(solution)/shard_map/ppermute | solution.py:558
  67.9 3.0 %collective-permute-start.25 = (bf16[2,32,512]{2,1,0:T(8,128)(2,1)S(1)}, bf16[2,32,512]{2,1,0:T(8,128)(2,1)S(1)}, u32[]{:S(2)}, u32[]{:S(2)}) collective-permute-start(bf16[2,32,512]{2,1,0:T(8,128)(2,1)S(1)} %get-tuple-element.84), channel_id=1, source_target_pairs={{0,10},{2,8},{4,14},{6,12},{8,2},{10,0},{12,6},{14,4},{1,11},{3,9}... | collective-permute-start | bytes 196616 | tf_op jit(solution)/shard_map/ppermute | solution.py:558
  70.9 2.8 %attend.3 = (bf16[2,32,512]{2,1,0:T(8,128)(2,1)S(1)}, bf16[2,32,512]{2,1,0:T(8,128)(2,1)S(1)}, bf16[2,32,512]{2,1,0:T(8,128)(2,1)S(1)}, bf16[2,32,512]{2,1,0:T(8...) custom-call(s32[3]{0:T(128)S(1)} %pad_add_fusion.scalars, ...), custom_call_target="tpu_custom_call" | custom-call | flops 1342177280 | bytes 2621440 | tf_op jit(solution)/shard_map/attend/pallas_call | solution.py:487
  73.7 2.0 %collective-permute-start.26 = (bf16[2,32,512]{2,1,0:T(8,128)(2,1)S(1)}, bf16[2,32,512]{2,1,0:T(8,128)(2,1)S(1)}, u32[]{:S(2)}, u32[]{:S(2)}) collective-permute-start(bf16[2,32,512]{2,1,0:T(8,128)(2,1)S(1)} %get-tuple-element.85), channel_id=1, source_target_pairs={{0,12},{2,14},{4,8},{6,10},{8,4},{10,6},{12,0},{14,2},{1,13},{3,15... | collective-permute-start | bytes 196616 | tf_op jit(solution)/shard_map/ppermute | solution.py:558
  75.8 2.7 %collective-permute-start.27 = (bf16[2,32,512]{2,1,0:T(8,128)(2,1)S(1)}, bf16[2,32,512]{2,1,0:T(8,128)(2,1)S(1)}, u32[]{:S(2)}, u32[]{:S(2)}) collective-permute-start(bf16[2,32,512]{2,1,0:T(8,128)(2,1)S(1)} %get-tuple-element.86), channel_id=1, source_target_pairs={{0,14},{2,12},{4,10},{6,8},{8,6},{10,4},{12,2},{14,0},{1,15},{3,13... | collective-permute-start | bytes 196616 | tf_op jit(solution)/shard_map/ppermute | solution.py:558
  79.1 2.9 %collective-permute-start.16 = (bf16[2,32,512]{2,1,0:T(8,128)(2,1)S(1)}, bf16[2,32,512]{2,1,0:T(8,128)(2,1)S(1)}, u32[]{:S(2)}, u32[]{:S(2)}) collective-permute-start(bf16[2,32,512]{2,1,0:T(8,128)(2,1)S(1)} %get-tuple-element.75), channel_id=1, source_target_pairs={{0,6},{2,4},{4,2},{6,0},{8,14},{10,12},{12,10},{14,8},{1,7},{3,5},... | collective-permute-start | bytes 196616 | tf_op jit(solution)/shard_map/ppermute | solution.py:558
  83.5 1.5 %collective-permute-start.18 = (bf16[2,32,512]{2,1,0:T(8,128)(2,1)S(1)}, bf16[2,32,512]{2,1,0:T(8,128)(2,1)S(1)}, u32[]{:S(2)}, u32[]{:S(2)}) collective-permute-start(bf16[2,32,512]{2,1,0:T(8,128)(2,1)S(1)} %get-tuple-element.77), channel_id=1, source_target_pairs={{0,10},{2,8},{4,14},{6,12},{8,2},{10,0},{12,6},{14,4},{1,11},{3,9}... | collective-permute-start | bytes 196616 | tf_op jit(solution)/shard_map/ppermute | solution.py:558
  85.0 2.2 %collective-permute-start.19 = (bf16[2,32,512]{2,1,0:T(8,128)(2,1)S(1)}, bf16[2,32,512]{2,1,0:T(8,128)(2,1)S(1)}, u32[]{:S(2)}, u32[]{:S(2)}) collective-permute-start(bf16[2,32,512]{2,1,0:T(8,128)(2,1)S(1)} %get-tuple-element.78), channel_id=1, source_target_pairs={{0,12},{2,14},{4,8},{6,10},{8,4},{10,6},{12,0},{14,2},{1,13},{3,15... | collective-permute-start | bytes 196616 | tf_op jit(solution)/shard_map/ppermute | solution.py:558
  87.2 2.5 %collective-permute-start.20 = (bf16[2,32,512]{2,1,0:T(8,128)(2,1)S(1)}, bf16[2,32,512]{2,1,0:T(8,128)(2,1)S(1)}, u32[]{:S(2)}, u32[]{:S(2)}) collective-permute-start(bf16[2,32,512]{2,1,0:T(8,128)(2,1)S(1)} %get-tuple-element.79), channel_id=1, source_target_pairs={{0,14},{2,12},{4,10},{6,8},{8,6},{10,4},{12,2},{14,0},{1,15},{3,13... | collective-permute-start | bytes 196616 | tf_op jit(solution)/shard_map/ppermute | solution.py:558
  89.7 1.4 %collect.2.refs_8_ = bf16[2,16,32,512]{3,2,1,0:T(8,128)(2,1)} custom-call(s32[3]{0:T(128)S(1)} %pad_add_fusion.scalars, bf16[2,32,512]{2,1,0:T(8,128)(2,1)S(1)} %get-tuple-element.67.refs_0_, bf16[2,32,512]{2,1,0:T(8,128)(2,1)S(1)} %collective-permute-done.21.refs_1_, bf16[2,32,512]{2,1,0:T(8,128)(2,1)S(1)} %collective-permute-done.22.refs_2_, ...), custom_call_target="tpu_custom_call" | custom-call | tf_op jit(solution)/shard_map/collect/pallas_call | solution.py:513
  92.0 2.1 %collective-permute-done.20.refs_7_ = bf16[2,32,512]{2,1,0:T(8,128)(2,1)S(1)} collective-permute-done((bf16[2,32,512]{2,1,0:T(8,128)(2,1)S(1)}, bf16[2,32,512]{2,1,0:T(8,128)(2,1)S(1)}, u32[]{:S(2)}, u32[]{:S(2)}) %collective-permute-start.20) | collective-permute-done | bytes 65568 | tf_op jit(solution)/shard_map/ppermute | solution.py:558
  94.1 1.4 %collect.3 = bf16[2,16,32,512]{3,2,1,0:T(8,128)(2,1)} custom-call(s32[3]{0:T(128)S(1)} %pad_add_fusion.scalars, bf16[2,32,512]{2,1,0:T(8,128)(2,1)S(1)} %get-tuple-element.72.refs_0_, bf16[2,32,512]{2,1,0:T(8,128)(2,1)S(1)} %collective-permute-done.14.refs_1_, ...), custom_call_target="tpu_custom_call", output_to_operand_aliasing={{}: (9, {})} | custom-call | tf_op jit(solution)/shard_map/collect/pallas_call | solution.py:513
  (72 shorter events, 9.0 us)
Async XLA Ops:
  2.3 16.9 %collective-permute-start.1 = (bf16[3,10,16,512]{3,2,1,0:T(8,128)(2,1)S(1)}, bf16[3,10,16,512]{3,2,1,0:T(8,128)(2,1)S(1)}, u32[]{:S(2)}, u32[]{:S(2)}) collective-permute-start(bf16[3,10,16,512]{3,2,1,0:T(8,128)(2,1)S(1)} %get-tuple-element.47), channel_id=1, source_target_pairs={{0,2},{2,0},{4,6},{6,4},{8,10},{10,8},{12,14},{14,12},{1,3},{3,1},... | collective-permute-start | bytes 1474568 | tf_op jit(solution)/shard_map/ppermute | solution.py:558
  7.4 11.6 %collective-permute-start.4 = (bf16[4,18,512]{2,1,0:T(8,128)(2,1)S(1)}, bf16[4,18,512]{2,1,0:T(8,128)(2,1)S(1)}, u32[]{:S(2)}, u32[]{:S(2)}) collective-permute-start(bf16[4,18,512]{2,1,0:T(8,128)(2,1)S(1)} %get-tuple-element.89), channel_id=1, source_target_pairs={{0,3},{1,2},{2,1},{3,0},{4,7},{5,6},{6,5},{7,4},{8,11},{9,10},{10,... | collective-permute-start | bytes 221192 | tf_op jit(solution)/shard_map/ppermute | solution.py:573
  7.5 11.6 %collective-permute-start.3 = (bf16[4,18,512]{2,1,0:T(8,128)(2,1)S(1)}, bf16[4,18,512]{2,1,0:T(8,128)(2,1)S(1)}, u32[]{:S(2)}, u32[]{:S(2)}) collective-permute-start(bf16[4,18,512]{2,1,0:T(8,128)(2,1)S(1)} %get-tuple-element.90), channel_id=1, source_target_pairs={{0,1},{1,0},{2,3},{3,2},{4,5},{5,4},{6,7},{7,6},{8,9},{9,8},{10,11... | collective-permute-start | bytes 221192 | tf_op jit(solution)/shard_map/ppermute | solution.py:567
  7.6 15.4 %collective-permute-start.2 = (bf16[1,10,16,512]{3,2,1,0:T(8,128)(2,1)S(1)}, bf16[1,10,16,512]{3,2,1,0:T(8,128)(2,1)S(1)}, u32[]{:S(2)}, u32[]{:S(2)}) collective-permute-start(bf16[1,10,16,512]{3,2,1,0:T(8,128)(2,1)S(1)} %get-tuple-element.50), channel_id=1, source_target_pairs={{0,2},{2,0},{4,6},{6,4},{8,10},{10,8},{12,14},{14,12},{1,3},{3,1},... | collective-permute-start | bytes 491528 | tf_op jit(solution)/shard_map/ppermute | solution.py:558
  9.6 21.0 %collective-permute-start = (bf16[3,8,16,512]{3,2,1,0:T(8,128)(2,1)S(1)}, bf16[3,8,16,512]{3,2,1,0:T(8,128)(2,1)S(1)}, u32[]{:S(2)}, u32[]{:S(2)}) collective-permute-start(bf16[3,8,16,512]{3,2,1,0:T(8,128)(2,1)S(1)} %get-tuple-element.46), channel_id=1, source_target_pairs={{0,2},{2,0},{4,6},{6,4},{8,10},{10,8},{12,14},{14,12},{1,3},{3,1},... | collective-permute-start | bytes 1179656 | tf_op jit(solution)/shard_map/ppermute | solution.py:558
  19.9 17.0 %collective-permute-start.7 = (bf16[3,11,16,512]{3,2,1,0:T(8,128)(2,1)S(1)}, bf16[3,11,16,512]{3,2,1,0:T(8,128)(2,1)S(1)}, u32[]{:S(2)}, u32[]{:S(2)}) collective-permute-start(bf16[3,11,16,512]{3,2,1,0:T(8,128)(2,1)S(1)} %join_last.2.last), channel_id=1, source_target_pairs={{0,4},{2,6},{4,8},{6,10},{8,12},{10,14},{12,0},{14,2},{1,5},{3,7},... | collective-permute-start | bytes 1622024 | tf_op jit(solution)/shard_map/ppermute | solution.py:558
  31.2 15.3 %collective-permute-start.5 = (bf16[3,9,16,512]{3,2,1,0:T(8,128)(2,1)S(1)}, bf16[3,9,16,512]{3,2,1,0:T(8,128)(2,1)S(1)}, u32[]{:S(2)}, u32[]{:S(2)}) collective-permute-start(bf16[3,9,16,512]{3,2,1,0:T(8,128)(2,1)S(1)} %join_last.3.last), channel_id=1, source_target_pairs={{0,4},{2,6},{4,8},{6,10},{8,12},{10,14},{12,0},{14,2},{1,5},{3,7},... | collective-permute-start | bytes 1327112 | tf_op jit(solution)/shard_map/ppermute | solution.py:558
  33.0 7.7 %collective-permute-start.6 = (bf16[1,8,16,512]{3,2,1,0:T(8,128)(2,1)S(1)}, bf16[1,8,16,512]{3,2,1,0:T(8,128)(2,1)S(1)}, u32[]{:S(2)}, u32[]{:S(2)}) collective-permute-start(bf16[1,8,16,512]{3,2,1,0:T(8,128)(2,1)S(1)} %get-tuple-element.55), channel_id=1, source_target_pairs={{0,2},{2,0},{4,6},{6,4},{8,10},{10,8},{12,14},{14,12},{1,3},{3,1},... | collective-permute-start | bytes 393224 | tf_op jit(solution)/shard_map/ppermute | solution.py:558
  40.8 18.0 %collective-permute-start.8 = (bf16[4,32,512]{2,1,0:T(8,128)(2,1)S(1)}, bf16[4,32,512]{2,1,0:T(8,128)(2,1)S(1)}, u32[]{:S(2)}, u32[]{:S(2)}) collective-permute-start(bf16[4,32,512]{2,1,0:T(8,128)(2,1)S(1)} %get-tuple-element.64), channel_id=1, source_target_pairs={{0,4},{2,6},{4,0},{6,2},{8,12},{10,14},{12,8},{14,10},{1,5},{3,7},... | collective-permute-start | bytes 393224 | tf_op jit(solution)/shard_map/ppermute | solution.py:558
  40.9 18.0 %collective-permute-start.9 = (bf16[4,32,512]{2,1,0:T(8,128)(2,1)S(1)}, bf16[4,32,512]{2,1,0:T(8,128)(2,1)S(1)}, u32[]{:S(2)}, u32[]{:S(2)}) collective-permute-start(bf16[4,32,512]{2,1,0:T(8,128)(2,1)S(1)} %get-tuple-element.65), channel_id=1, source_target_pairs={{0,8},{2,10},{4,12},{6,14},{8,0},{10,2},{12,4},{14,6},{1,9},{3,11}... | collective-permute-start | bytes 393224 | tf_op jit(solution)/shard_map/ppermute | solution.py:558
  43.2 15.6 %collective-permute-start.10 = (bf16[4,32,512]{2,1,0:T(8,128)(2,1)S(1)}, bf16[4,32,512]{2,1,0:T(8,128)(2,1)S(1)}, u32[]{:S(2)}, u32[]{:S(2)}) collective-permute-start(bf16[4,32,512]{2,1,0:T(8,128)(2,1)S(1)} %get-tuple-element.66), channel_id=1, source_target_pairs={{0,12},{2,14},{4,8},{6,10},{8,4},{10,6},{12,0},{14,2},{1,13},{3,15... | collective-permute-start | bytes 393224 | tf_op jit(solution)/shard_map/ppermute | solution.py:558
  46.5 12.4 %copy-start.8 = (bf16[512,512]{1,0:T(8,128)(2,1)S(1)}, bf16[512,512]{1,0:T(8,128)(2,1)}, u32[]{:S(2)}) copy-start(bf16[512,512]{1,0:T(8,128)(2,1)} %refs_6_.3) | copy-start | bytes 1572868
  46.5 12.4 %copy-start.9 = (bf16[512,512]{1,0:T(8,128)(2,1)S(1)}, bf16[512,512]{1,0:T(8,128)(2,1)}, u32[]{:S(2)}) copy-start(bf16[512,512]{1,0:T(8,128)(2,1)} %refs_7_.3) | copy-start | bytes 1572868
  46.5 12.4 %copy-start.10 = (bf16[512,512]{1,0:T(8,128)(2,1)S(1)}, bf16[512,512]{1,0:T(8,128)(2,1)}, u32[]{:S(2)}) copy-start(bf16[512,512]{1,0:T(8,128)(2,1)} %refs_8_.3) | copy-start | bytes 1572868
  46.5 12.4 %copy-start.11 = (f32[512]{0:T(512)S(1)}, f32[512]{0:T(512)}, u32[]{:S(2)}) copy-start(f32[512]{0:T(512)} %param.19) | copy-start | bytes 6148
  53.8 9.5 %collective-permute-start.11 = (bf16[4,32,512]{2,1,0:T(8,128)(2,1)S(1)}, bf16[4,32,512]{2,1,0:T(8,128)(2,1)S(1)}, u32[]{:S(2)}, u32[]{:S(2)}) collective-permute-start(bf16[4,32,512]{2,1,0:T(8,128)(2,1)S(1)} %get-tuple-element.69), channel_id=1, source_target_pairs={{0,4},{2,6},{4,0},{6,2},{8,12},{10,14},{12,8},{14,10},{1,5},{3,7},... | collective-permute-start | bytes 393224 | tf_op jit(solution)/shard_map/ppermute | solution.py:558
  53.9 14.0 %collective-permute-start.12 = (bf16[4,32,512]{2,1,0:T(8,128)(2,1)S(1)}, bf16[4,32,512]{2,1,0:T(8,128)(2,1)S(1)}, u32[]{:S(2)}, u32[]{:S(2)}) collective-permute-start(bf16[4,32,512]{2,1,0:T(8,128)(2,1)S(1)} %get-tuple-element.70), channel_id=1, source_target_pairs={{0,8},{2,10},{4,12},{6,14},{8,0},{10,2},{12,4},{14,6},{1,9},{3,11}... | collective-permute-start | bytes 393224 | tf_op jit(solution)/shard_map/ppermute | solution.py:558
  58.8 9.1 %collective-permute-start.13 = (bf16[4,32,512]{2,1,0:T(8,128)(2,1)S(1)}, bf16[4,32,512]{2,1,0:T(8,128)(2,1)S(1)}, u32[]{:S(2)}, u32[]{:S(2)}) collective-permute-start(bf16[4,32,512]{2,1,0:T(8,128)(2,1)S(1)} %get-tuple-element.71), channel_id=1, source_target_pairs={{0,12},{2,14},{4,8},{6,10},{8,4},{10,6},{12,0},{14,2},{1,13},{3,15... | collective-permute-start | bytes 393224 | tf_op jit(solution)/shard_map/ppermute | solution.py:558
  61.7 12.1 %collective-permute-start.21 = (bf16[2,32,512]{2,1,0:T(8,128)(2,1)S(1)}, bf16[2,32,512]{2,1,0:T(8,128)(2,1)S(1)}, u32[]{:S(2)}, u32[]{:S(2)}) collective-permute-start(bf16[2,32,512]{2,1,0:T(8,128)(2,1)S(1)} %get-tuple-element.80), channel_id=1, source_target_pairs={{0,2},{2,0},{4,6},{6,4},{8,10},{10,8},{12,14},{14,12},{1,3},{3,1},... | collective-permute-start | bytes 196616 | tf_op jit(solution)/shard_map/ppermute | solution.py:558
  62.7 13.1 %collective-permute-start.22 = (bf16[2,32,512]{2,1,0:T(8,128)(2,1)S(1)}, bf16[2,32,512]{2,1,0:T(8,128)(2,1)S(1)}, u32[]{:S(2)}, u32[]{:S(2)}) collective-permute-start(bf16[2,32,512]{2,1,0:T(8,128)(2,1)S(1)} %get-tuple-element.81), channel_id=1, source_target_pairs={{0,4},{2,6},{4,0},{6,2},{8,12},{10,14},{12,8},{14,10},{1,5},{3,7},... | collective-permute-start | bytes 196616 | tf_op jit(solution)/shard_map/ppermute | solution.py:558
  63.3 15.2 %collective-permute-start.23 = (bf16[2,32,512]{2,1,0:T(8,128)(2,1)S(1)}, bf16[2,32,512]{2,1,0:T(8,128)(2,1)S(1)}, u32[]{:S(2)}, u32[]{:S(2)}) collective-permute-start(bf16[2,32,512]{2,1,0:T(8,128)(2,1)S(1)} %get-tuple-element.82), channel_id=1, source_target_pairs={{0,6},{2,4},{4,2},{6,0},{8,14},{10,12},{12,10},{14,8},{1,7},{3,5},... | collective-permute-start | bytes 196616 | tf_op jit(solution)/shard_map/ppermute | solution.py:558
  67.9 11.2 %collective-permute-start.24 = (bf16[2,32,512]{2,1,0:T(8,128)(2,1)S(1)}, bf16[2,32,512]{2,1,0:T(8,128)(2,1)S(1)}, u32[]{:S(2)}, u32[]{:S(2)}) collective-permute-start(bf16[2,32,512]{2,1,0:T(8,128)(2,1)S(1)} %get-tuple-element.83), channel_id=1, source_target_pairs={{0,8},{2,10},{4,12},{6,14},{8,0},{10,2},{12,4},{14,6},{1,9},{3,11}... | collective-permute-start | bytes 196616 | tf_op jit(solution)/shard_map/ppermute | solution.py:558
  67.9 11.2 %collective-permute-start.25 = (bf16[2,32,512]{2,1,0:T(8,128)(2,1)S(1)}, bf16[2,32,512]{2,1,0:T(8,128)(2,1)S(1)}, u32[]{:S(2)}, u32[]{:S(2)}) collective-permute-start(bf16[2,32,512]{2,1,0:T(8,128)(2,1)S(1)} %get-tuple-element.84), channel_id=1, source_target_pairs={{0,10},{2,8},{4,14},{6,12},{8,2},{10,0},{12,6},{14,4},{1,11},{3,9}... | collective-permute-start | bytes 196616 | tf_op jit(solution)/shard_map/ppermute | solution.py:558
  73.7 8.3 %collective-permute-start.26 = (bf16[2,32,512]{2,1,0:T(8,128)(2,1)S(1)}, bf16[2,32,512]{2,1,0:T(8,128)(2,1)S(1)}, u32[]{:S(2)}, u32[]{:S(2)}) collective-permute-start(bf16[2,32,512]{2,1,0:T(8,128)(2,1)S(1)} %get-tuple-element.85), channel_id=1, source_target_pairs={{0,12},{2,14},{4,8},{6,10},{8,4},{10,6},{12,0},{14,2},{1,13},{3,15... | collective-permute-start | bytes 196616 | tf_op jit(solution)/shard_map/ppermute | solution.py:558
  75.8 7.7 %collective-permute-start.27 = (bf16[2,32,512]{2,1,0:T(8,128)(2,1)S(1)}, bf16[2,32,512]{2,1,0:T(8,128)(2,1)S(1)}, u32[]{:S(2)}, u32[]{:S(2)}) collective-permute-start(bf16[2,32,512]{2,1,0:T(8,128)(2,1)S(1)} %get-tuple-element.86), channel_id=1, source_target_pairs={{0,14},{2,12},{4,10},{6,8},{8,6},{10,4},{12,2},{14,0},{1,15},{3,13... | collective-permute-start | bytes 196616 | tf_op jit(solution)/shard_map/ppermute | solution.py:558
  78.5 6.5 %collective-permute-start.14 = (bf16[2,32,512]{2,1,0:T(8,128)(2,1)S(1)}, bf16[2,32,512]{2,1,0:T(8,128)(2,1)S(1)}, u32[]{:S(2)}, u32[]{:S(2)}) collective-permute-start(bf16[2,32,512]{2,1,0:T(8,128)(2,1)S(1)} %get-tuple-element.73), channel_id=1, source_target_pairs={{0,2},{2,0},{4,6},{6,4},{8,10},{10,8},{12,14},{14,12},{1,3},{3,1},... | collective-permute-start | bytes 196616 | tf_op jit(solution)/shard_map/ppermute | solution.py:558
  79.1 8.1 %collective-permute-start.15 = (bf16[2,32,512]{2,1,0:T(8,128)(2,1)S(1)}, bf16[2,32,512]{2,1,0:T(8,128)(2,1)S(1)}, u32[]{:S(2)}, u32[]{:S(2)}) collective-permute-start(bf16[2,32,512]{2,1,0:T(8,128)(2,1)S(1)} %get-tuple-element.74), channel_id=1, source_target_pairs={{0,4},{2,6},{4,0},{6,2},{8,12},{10,14},{12,8},{14,10},{1,5},{3,7},... | collective-permute-start | bytes 196616 | tf_op jit(solution)/shard_map/ppermute | solution.py:558
  79.1 12.0 %collective-permute-start.16 = (bf16[2,32,512]{2,1,0:T(8,128)(2,1)S(1)}, bf16[2,32,512]{2,1,0:T(8,128)(2,1)S(1)}, u32[]{:S(2)}, u32[]{:S(2)}) collective-permute-start(bf16[2,32,512]{2,1,0:T(8,128)(2,1)S(1)} %get-tuple-element.75), channel_id=1, source_target_pairs={{0,6},{2,4},{4,2},{6,0},{8,14},{10,12},{12,10},{14,8},{1,7},{3,5},... | collective-permute-start | bytes 196616 | tf_op jit(solution)/shard_map/ppermute | solution.py:558
  82.0 9.1 %collective-permute-start.17 = (bf16[2,32,512]{2,1,0:T(8,128)(2,1)S(1)}, bf16[2,32,512]{2,1,0:T(8,128)(2,1)S(1)}, u32[]{:S(2)}, u32[]{:S(2)}) collective-permute-start(bf16[2,32,512]{2,1,0:T(8,128)(2,1)S(1)} %get-tuple-element.76), channel_id=1, source_target_pairs={{0,8},{2,10},{4,12},{6,14},{8,0},{10,2},{12,4},{14,6},{1,9},{3,11}... | collective-permute-start | bytes 196616 | tf_op jit(solution)/shard_map/ppermute | solution.py:558
  83.5 8.6 %collective-permute-start.18 = (bf16[2,32,512]{2,1,0:T(8,128)(2,1)S(1)}, bf16[2,32,512]{2,1,0:T(8,128)(2,1)S(1)}, u32[]{:S(2)}, u32[]{:S(2)}) collective-permute-start(bf16[2,32,512]{2,1,0:T(8,128)(2,1)S(1)} %get-tuple-element.77), channel_id=1, source_target_pairs={{0,10},{2,8},{4,14},{6,12},{8,2},{10,0},{12,6},{14,4},{1,11},{3,9}... | collective-permute-start | bytes 196616 | tf_op jit(solution)/shard_map/ppermute | solution.py:558
  85.0 7.1 %collective-permute-start.19 = (bf16[2,32,512]{2,1,0:T(8,128)(2,1)S(1)}, bf16[2,32,512]{2,1,0:T(8,128)(2,1)S(1)}, u32[]{:S(2)}, u32[]{:S(2)}) collective-permute-start(bf16[2,32,512]{2,1,0:T(8,128)(2,1)S(1)} %get-tuple-element.78), channel_id=1, source_target_pairs={{0,12},{2,14},{4,8},{6,10},{8,4},{10,6},{12,0},{14,2},{1,13},{3,15... | collective-permute-start | bytes 196616 | tf_op jit(solution)/shard_map/ppermute | solution.py:558
  87.2 7.0 %collective-permute-start.20 = (bf16[2,32,512]{2,1,0:T(8,128)(2,1)S(1)}, bf16[2,32,512]{2,1,0:T(8,128)(2,1)S(1)}, u32[]{:S(2)}, u32[]{:S(2)}) collective-permute-start(bf16[2,32,512]{2,1,0:T(8,128)(2,1)S(1)} %get-tuple-element.79), channel_id=1, source_target_pairs={{0,14},{2,12},{4,10},{6,8},{8,6},{10,4},{12,2},{14,0},{1,15},{3,13... | collective-permute-start | bytes 196616 | tf_op jit(solution)/shard_map/ppermute | solution.py:558
  (9 other events, 88.6 us)

commit v14 on v11

--- a/solution.py
+++ b/solution.py
@@ -58,24 +58,31 @@
         target[here : here + count] = video[frame, pl.ds(source, count)]
 
 
-def send_kernel(spans, half, scalars, video, *outs):
-    frames = video.shape[0]
-    rest = frames - taps
-    for k, (begin, end) in enumerate(spans):
-        for t in range(frames):
-            target = outs[k].at[t - rest] if t >= rest else outs[len(spans) + k].at[t]
-            cut(target, video, t, 1 - scalars[0], begin, end, half)
-
-
-def send(scalars, video, spans, half):
-    frames, _, width, channels = video.shape
+def cuts(k, frames):
+    first = frames - taps
+    return ((first + 1, frames), (first, first + 1)) if k == 0 else ((first, frames),)
+
+
+def frame_of(refs, pieces, t):
+    for ref, (low, high) in zip(refs, pieces):
+        if low <= t < high:
+            return ref[t - low]
+
+
+def send_kernel(spans, pieces, half, scalars, video, *outs):
+    for out, (k, low, high) in zip(outs, pieces):
+        begin, end = spans[k]
+        for t in range(low, high):
+            cut(out.at[t - low], video, t, 1 - scalars[0], begin, end, half)
+
+
+def send(scalars, video, spans, pieces, half):
+    width, channels = video.shape[2:]
     shapes = [
-        (count, end - begin, width, channels)
-        for count in (taps, frames - taps)
-        for begin, end in spans
+        (high - low, spans[k][1] - spans[k][0], width, channels) for k, low, high in pieces
     ]
     return pl.pallas_call(
-        partial(send_kernel, spans, half),
+        partial(send_kernel, spans, pieces, half),
         out_shape=[jax.ShapeDtypeStruct(shape, video.dtype) for shape in shapes],
         in_specs=[SMEM, VMEM],
         out_specs=[VMEM] * len(shapes),
@@ -84,24 +91,25 @@
     )(scalars, video)
 
 
-def join_last_kernel(begin, end, half, scalars, video, received, own_edge, other_edge, out):
-    frames, rows = video.shape[0], end - begin
+def join_last_kernel(begin, end, half, pieces, scalars, video, received, own_edge, other_edge, out):
+    rows = end - begin
+    ((low, high),) = pieces
 
     @pl.when(scalars[0] == 0)
     def _():
         out[:, :rows] = received[...]
-        out[:, rows:] = other_edge[frames - taps :]
+        out[:, rows:] = other_edge[low:high]
 
     @pl.when(scalars[0] == 1)
     def _():
-        for t in range(taps):
-            cut(out.at[t], video, frames - taps + t, 1, begin, end, half)
-        out[:, rows:] = own_edge[frames - taps :]
-
-
-def join_first_kernel(
-    begin, end, half, scalars, video, received, others, own_edge, other_edge, out
-):
+        for t in range(low, high):
+            cut(out.at[t - low], video, t, 1, begin, end, half)
+        out[:, rows:] = own_edge[low:high]
+
+
+def join_first_kernel(begin, end, half, pieces, scalars, video, *refs):
+    received, others = refs[: len(pieces)], refs[len(pieces)]
+    own_edge, other_edge, out = refs[-3:]
     frames, rows = video.shape[0], end - begin
     rest = frames - taps
 
@@ -116,18 +124,19 @@
     @pl.when(scalars[0] == 1)
     def _():
         out[:rest, :rows] = others[...]
-        out[rest:frames, :rows] = received[...]
+        for ref, (low, high) in zip(received, pieces):
+            out[low:high, :rows] = ref[...]
         out[:frames, rows:] = other_edge[...]
         for t in range(rest):
             cut(out.at[frames + t], video, t, 1, begin, end, half)
         out[frames:, rows:] = own_edge[:rest]
 
 
-def join(kernel, count, name, begin, end, half, scalars, video, *parts):
-    _, _, width, channels = video.shape
+def join(kernel, count, name, begin, end, half, pieces, scalars, video, *parts):
+    width, channels = video.shape[2:]
     rows = end - begin + parts[-1].shape[1]
     return pl.pallas_call(
-        partial(kernel, begin, end, half),
+        partial(kernel, begin, end, half, pieces),
         out_shape=jax.ShapeDtypeStruct((count, rows, width, channels), jnp.bfloat16),
         in_specs=[SMEM] + [VMEM] * (1 + len(parts)),
         out_specs=VMEM,
@@ -186,8 +195,11 @@
 
 
 def early_kernel(
-    final, rows, scalars, first, last, w_time, b_time, w_down, b_down, w_space, b_space, *refs
+    final, rows, pieces, scalars, first, *refs
 ):
+    lasts, refs = refs[: len(pieces)], refs[len(pieces) :]
+    w_time, b_time, w_down, b_down, w_space, b_space = refs[:6]
+    refs = refs[6:]
     part, spatial = refs[:2]
     lifted, buffers = refs[-2:]
     keeps = None if final else (lambda value: refs[2].__setitem__(..., value))
@@ -197,7 +209,7 @@
     pixels = depth * width
 
     def frame(t):
-        return (first[t] if t < split else last[t - split]).reshape(pixels, channels)
+        return (first[t] if t < split else frame_of(lasts, pieces, t - halves)).reshape(pixels, channels)
 
     starts = list(range(taps - 1, count))
     for low in range(0, len(starts), 3):
@@ -224,7 +236,7 @@
     spatial[...] = convolve(buffers, True, final, scalars[0], None, keeps, w_space, b_space)
 
 
-def early(scalars, first, last, final, size, rows, *weights):
+def early(scalars, first, lasts, pieces, final, size, rows, *weights):
     split, depth, width, channels = first.shape
     halves = (split + taps) // 2
     pixels = depth * width
@@ -237,23 +249,23 @@
         shapes.append(jax.ShapeDtypeStruct((3, later, 2, width, channels), jnp.bfloat16))
     flops = 2 * channels * channels * (pixels * 26 + 9 * later * size * width)
     return pl.pallas_call(
-        partial(early_kernel, final, rows),
+        partial(early_kernel, final, rows, pieces),
         out_shape=shapes,
-        in_specs=[SMEM] + [VMEM] * (2 + len(weights)),
+        in_specs=[SMEM] + [VMEM] * (1 + len(lasts) + len(weights)),
         out_specs=[VMEM] * len(shapes),
         scratch_shapes=[
             pltpu.VMEM((2 * halves, pixels, channels), jnp.bfloat16),
             pltpu.VMEM((3, later, size + 2, width, channels), jnp.bfloat16),
         ],
         compiler_params=params(24),
-        cost_estimate=cost(flops, first, last, *weights),
+        cost_estimate=cost(flops, first, *lasts, *weights),
         name="early",
-    )(scalars, first, last, *weights)
+    )(scalars, first, *lasts, *weights)
 
 
 def full_kernel(
-    owners, final, rows, scalars, halo, first, last, kept_late, kept_early, w_time, b_time, w_down,
-    b_down, w_space, b_space, *refs
+    owners, final, rows, pieces, scalars, halo, first, last, kept_late, kept_early, w_time, b_time,
+    w_down, b_down, w_space, b_space, *refs
 ):
     outs = refs[:owners]
     keeps = None if final else refs[owners : owners + 2]
@@ -265,9 +277,9 @@
 
     def frame(t):
         if t < 0:
-            value = halo[t + taps].reshape(pixels, channels)
+            value = frame_of([halo], pieces, halves + t).reshape(pixels, channels)
             return jnp.where(scalars[2] > 0, value, jnp.zeros_like(value))
-        return (first[t] if t < split else last[t - split]).reshape(pixels, channels)
+        return (first[t] if t < split else frame_of([last], pieces, t - halves)).reshape(pixels, channels)
 
     starts = list(range(-1, count))
     for low in range(0, len(starts), 3):
@@ -315,7 +327,7 @@
     keeps[1][...] = value[:, 2:]
 
 
-def full(owners, scalars, halo, first, last, kept, final, size, rows, *weights):
+def full(owners, scalars, halo, first, last, pieces, kept, final, size, rows, *weights):
     split, depth, width, channels = first.shape
     halves = (split + taps) // 2
     pixels = depth * width
@@ -324,7 +336,7 @@
         shapes += [(3, count, 2, width, channels) for count in (2, halves - 2)]
     flops = 2 * channels * channels * (pixels * 39 + 9 * halves * size * width)
     return pl.pallas_call(
-        partial(full_kernel, owners, final, rows),
+        partial(full_kernel, owners, final, rows, pieces),
         out_shape=[jax.ShapeDtypeStruct(shape, jnp.bfloat16) for shape in shapes],
         in_specs=[SMEM] + [VMEM] * (5 + len(weights)),
         out_specs=[VMEM] * len(shapes),
@@ -339,9 +351,11 @@
 
 
 def late_kernel(
-    owners, final, rows, scalars, halo, first, part, spatial, w_time, b_time, w_down, b_down,
-    w_space, b_space, *refs
+    owners, final, rows, pieces, scalars, *refs
 ):
+    halos, refs = refs[: len(pieces)], refs[len(pieces) :]
+    first, part, spatial, w_time, b_time, w_down, b_down, w_space, b_space = refs[:9]
+    refs = refs[9:]
     outs = refs[:owners]
     keeps = None if final else (lambda value: refs[owners].__setitem__(..., value))
     lifted, buffers, result = refs[-3:]
@@ -350,7 +364,7 @@
 
     def frame(t):
         if t < 0:
-            value = halo[t + taps].reshape(pixels, channels)
+            value = frame_of(halos, pieces, result.shape[0] + t).reshape(pixels, channels)
             return jnp.where(scalars[2] > 0, value, jnp.zeros_like(value))
         return first[t].reshape(pixels, channels)
 
@@ -385,7 +399,7 @@
             out[...] = result[:, pl.ds(begin, each)]
 
 
-def late(owners, scalars, halo, first, part, spatial, final, rows, *weights):
+def late(owners, scalars, halos, pieces, first, part, spatial, final, rows, *weights):
     _, depth, width, channels = first.shape
     later, pixels = spatial.shape[:2]
     halves = later + 2
@@ -395,9 +409,9 @@
         shapes.append((3, 2, 2, width, channels))
     flops = 2 * channels * channels * (depth * width * 13 + 18 * pixels)
     return pl.pallas_call(
-        partial(late_kernel, owners, final, rows),
+        partial(late_kernel, owners, final, rows, pieces),
         out_shape=[jax.ShapeDtypeStruct(shape, jnp.bfloat16) for shape in shapes],
-        in_specs=[SMEM] + [VMEM] * (4 + len(weights)),
+        in_specs=[SMEM] + [VMEM] * (3 + len(halos) + len(weights)),
         out_specs=[VMEM] * len(shapes),
         scratch_shapes=[
             pltpu.VMEM((taps, depth * width, channels), jnp.bfloat16),
@@ -405,9 +419,9 @@
             pltpu.VMEM((halves, pixels, channels), jnp.bfloat16),
         ],
         compiler_params=params(24),
-        cost_estimate=cost(flops, halo, first, part, *weights),
+        cost_estimate=cost(flops, *halos, first, part, *weights),
         name="late",
-    )(scalars, halo, first, part, spatial, *weights)
+    )(scalars, *halos, first, part, spatial, *weights)
 
 
 def attend_kernel(frames_per, lanes, count, scalars, *refs):
@@ -557,8 +571,15 @@
     def tm_permute(value, move):
         return lax.ppermute(value, "tm", [(i, move(i)) for i in range(devices) if move(i) < devices])
 
-    sent = send(scalars, video, spans, half)
-    received = [tm_permute(value, lambda i: i ^ 1) for value in sent]
+    rest = frames - taps
+    pieces = [(k, low, high) for k in range(chunks) for low, high in cuts(k, frames)]
+    pieces += [(k, 0, rest) for k in range(chunks)]
+    sent = send(scalars, video, spans, pieces, half)
+    received = {}
+    for key, value in zip(pieces, sent):
+        if key[2] == rest and key[1] == 0:
+            value = after(value, received[(key[0],) + cuts(key[0], frames)[0]])
+        received[key] = tm_permute(value, lambda i: i ^ 1)
     border = jnp.where(column == 0, video[:, :, -1], video[:, :, 0])
     border = jnp.pad(after(border, sent[0]), ((0, 0), (1, 1), (0, 0)))
     own_edge, other_edge = (
@@ -578,34 +599,41 @@
 
     owners = levels if direct else 1
     edges = [[edge_rows(e, begin, end) for e in (own_edge, other_edge)] for begin, end in spans]
-    lasts, halos = [], []
+    lasts, halos = {}, {}
     newest = w_space
-    for k, (begin, end) in enumerate(spans):
+    for k, low, high in pieces[: len(pieces) - chunks]:
+        begin, end = spans[k]
         newest = join(
-            join_last_kernel, taps, "join_last", begin, end, half, scalars, video,
-            after(received[k], newest), *edges[k]
+            join_last_kernel, high - low, "join_last", begin, end, half, ((low, high),), scalars,
+            video, after(received[k, low, high], newest), *edges[k]
         )
-        lasts.append(newest)
-        halos.append(tm_permute(newest, lambda i: (i + pair) % devices))
+        lasts[k, low, high] = newest
+        halos[k, low, high] = tm_permute(newest, lambda i: (i + pair) % devices)
 
     spatials = []
     kept = None
     for k, (begin, end) in enumerate(spans):
         rows, final = end - begin, k == chunks - 1
-        others = after(received[chunks + k], newest)
+        ranges = cuts(k, frames)
+        keys = [(k,) + piece for piece in ranges]
         first = join(
-            join_first_kernel, pair * frames - taps, "join_first", begin, end, half, scalars,
-            video, received[k], others, *edges[k]
+            join_first_kernel, pair * frames - taps, "join_first", begin, end, half, ranges, scalars,
+            video, *[received[key] for key in keys], after(received[k, 0, rest], newest), *edges[k]
         )
         if k == 0:
-            part, spatial, *kept = early(scalars, first, lasts[k], final, size, rows, *weights)
+            part, spatial, *kept = early(
+                scalars, first, [lasts[key] for key in keys], ranges, final, size, rows, *weights
+            )
             made = late(
-                owners, scalars, halos[k], first, part, spatial, final, rows, *weights
+                owners, scalars, [halos[key] for key in keys], ranges, first, part, spatial, final,
+                rows, *weights
             )
             kept = [*made[owners:], *kept]
         else:
+            (key,) = keys
             made = full(
-                owners, scalars, halos[k], first, lasts[k], kept, final, size, rows, *weights
+                owners, scalars, halos[key], first, lasts[key], ranges, kept, final, size, rows,
+                *weights
             )
             kept = made[owners:]
         spatials.append(made[:owners])

time: 98.3 us -> 96.8 us (0.985)
  waiting for transfers between devices: 18.8 us -> 14.2 us
  starting transfers between devices: 44.4 us -> 46.9 us
    ppermute x1, waiting for transfers between devices: 6.56 us -> 3.07 us  [per_device(): other_edge = lax.ppermute(other_edge, ('tm', 'cols'), aslant)]
    ppermute x26 -> x28, starting transfers between devices: 44.2 us -> 46.7 us  [tm_permute(): lax.ppermute(value, 'tm', [(i, move(i)) for i in range(devices) if move(i...]
    ppermute x26 -> x28, waiting for transfers between devices: 12.2 us -> 11.2 us  [tm_permute(): lax.ppermute(value, 'tm', [(i, move(i)) for i in range(devices) if move(i...]
    pallas_call x8 -> x9, Pallas kernels: 19.3 us -> 19.8 us  [the longest x1 7.32 us: full(): pl.pallas_call(partial(full_kernel, owners, final, rows, pieces), out_sha...]
  transfers between devices with their start and end apart: 28 -> 30, of which waited for: 6 -> 7; matrix products, arithmetic and copies ran while one was open for 5% -> 5% of each run, Pallas kernels for 26% -> 27%
where the time goes in v14:
time: 96.8 us; the launch traced here: 96.6 us
  starting transfers between devices  46.9 us (48%)
  Pallas kernels  28.2 us (29%)
  waiting for transfers between devices  14.2 us (15%)
  local copies, waits for them, and re-layouts  3.73 us (4%)
  other arithmetic  2.99 us (3%)
    ppermute x28, starting transfers between devices, tm_permute(): lax.ppermute(value, 'tm', [(i, move(i)) for i in range(devices) if move(i...  46.7 us
    ppermute x28, waiting for transfers between devices, tm_permute(): lax.ppermute(value, 'tm', [(i, move(i)) for i in range(devices) if move(i...  11.2 us
    pallas_call x1, Pallas kernels, full(): pl.pallas_call(partial(full_kernel, owners, final, rows, pieces), out_sha...  7.32 us
    pallas_call x2, Pallas kernels, attend(): pl.pallas_call(partial(attend_kernel, frames_per, lanes, count), out_shap...  5.57 us
    pallas_call x1, Pallas kernels, early(): pl.pallas_call(partial(early_kernel, final, rows, pieces), out_shape=shap...  5.02 us
    pallas_call x1, Pallas kernels, late(): pl.pallas_call(partial(late_kernel, owners, final, rows, pieces), out_sha...  3.92 us
    ppermute x1, waiting for transfers between devices, per_device(): other_edge = lax.ppermute(other_edge, ('tm', 'cols'), aslant)  3.07 us
    pallas_call x5, Pallas kernels, join(): pl.pallas_call(partial(kernel, begin, end, half, pieces), out_shape=jax.S...  2.93 us
  transfers between devices with their start and end apart: 30, of which 7 were waited for; matrix products, arithmetic and copies ran while one was open for 5% of the time, Pallas kernels for 27%

profile of v14, /device:TPU:0, one launch (start us, length us, event | category | flops | bytes accessed | tf_op | source)
XLA Modules:
  0.0 96.6 jit_solution(11493933297001926890)
XLA Ops:
  0.1 1.6 %copy-done = bf16[4,32,16,512]{3,2,1,0:T(8,128)(2,1)S(1)} copy-done((bf16[4,32,16,512]{3,2,1,0:T(8,128)(2,1)S(1)}, bf16[4,32,16,512]{3,2,1,0:T(8,128)(2,1)}, u32[]{:S(2)}) %copy-start) | copy-done | bytes 2097176
  2.3 3.0 %collective-permute-start.2 = (bf16[2,10,16,512]{3,2,1,0:T(8,128)(2,1)S(1)}, bf16[2,10,16,512]{3,2,1,0:T(8,128)(2,1)S(1)}, u32[]{:S(2)}, u32[]{:S(2)}) collective-permute-start(bf16[2,10,16,512]{3,2,1,0:T(8,128)(2,1)S(1)} %get-tuple-element.51), channel_id=1, source_target_pairs={{0,2},{2,0},{4,6},{6,4},{8,10},{10,8},{12,14},{14,12},{1,3},{3,1},... | collective-permute-start | bytes 983048 | tf_op jit(solution)/shard_map/ppermute | solution.py:572
  5.3 1.9 %fusion.3 = (bf16[4,32,1,512]{3,2,1,0:T(2,128)(2,1)S(1)}, bf16[4,32,1,512]{3,2,1,0:T(2,128)(2,1)S(1)}) fusion(bf16[4,32,16,512]{3,2,1,0:T(8,128)(2,1)} %video.11), kind=kLoop, calls=%fused_computation.12 | loop fusion | bytes 524288 | tf_op jit(solution)/shard_map/slice | solution.py:583
  7.6 2.0 %collective-permute-start.1 = (bf16[1,10,16,512]{3,2,1,0:T(8,128)(2,1)S(1)}, bf16[1,10,16,512]{3,2,1,0:T(8,128)(2,1)S(1)}, u32[]{:S(2)}, u32[]{:S(2)}) collective-permute-start(bf16[1,10,16,512]{3,2,1,0:T(8,128)(2,1)S(1)} %get-tuple-element.50), channel_id=1, source_target_pairs={{0,2},{2,0},{4,6},{6,4},{8,10},{10,8},{12,14},{14,12},{1,3},{3,1},... | collective-permute-start | bytes 491528 | tf_op jit(solution)/shard_map/ppermute | solution.py:572
  9.7 2.8 %broadcast_select_fusion.refs_6_.refs_9_.w_space = bf16[9,512,512]{2,1,0:T(8,128)(2,1)S(1)} fusion(bf16[9,512,512]{2,1,0:T(8,128)(2,1)} %param.17, pred[]{:T(512)S(6)} %ge.3), kind=kLoop, calls=%fused_computation | loop fusion | flops 2359296 | bytes 9437185 | tf_op jit(solution)/shard_map/jit(_where)/select_n | solution.py:557
  12.5 3.1 %collective-permute-done.4 = bf16[4,18,512]{2,1,0:T(8,128)(2,1)S(1)} collective-permute-done((bf16[4,18,512]{2,1,0:T(8,128)(2,1)S(1)}, bf16[4,18,512]{2,1,0:T(8,128)(2,1)S(1)}, u32[]{:S(2)}, u32[]{:S(2)}) %collective-permute-start.4) | collective-permute-done | bytes 73760 | tf_op jit(solution)/shard_map/ppermute | solution.py:594
  16.6 2.0 %collective-permute-start.7 = (bf16[2,11,16,512]{3,2,1,0:T(8,128)(2,1)S(1)}, bf16[2,11,16,512]{3,2,1,0:T(8,128)(2,1)S(1)}, u32[]{:S(2)}, u32[]{:S(2)}) collective-permute-start(bf16[2,11,16,512]{3,2,1,0:T(8,128)(2,1)S(1)} %join_last.3.refs_0_), channel_id=1, source_target_pairs={{0,4},{2,6},{4,8},{6,10},{8,12},{10,14},{12,0},{14,2},{1,5},{3,7},... | collective-permute-start | bytes 1081352 | tf_op jit(solution)/shard_map/ppermute | solution.py:572
  20.1 2.2 %collective-permute-start.8 = (bf16[1,11,16,512]{3,2,1,0:T(8,128)(2,1)S(1)}, bf16[1,11,16,512]{3,2,1,0:T(8,128)(2,1)S(1)}, u32[]{:S(2)}, u32[]{:S(2)}) collective-permute-start(bf16[1,11,16,512]{3,2,1,0:T(8,128)(2,1)S(1)} %join_last.4.refs_1_), channel_id=1, source_target_pairs={{0,4},{2,6},{4,8},{6,10},{8,12},{10,14},{12,0},{14,2},{1,5},{3,7},... | collective-permute-start | bytes 540680 | tf_op jit(solution)/shard_map/ppermute | solution.py:572
  22.2 5.7 %collective-permute-done.received.refs_0_ = bf16[3,8,16,512]{3,2,1,0:T(8,128)(2,1)S(1)} collective-permute-done((bf16[3,8,16,512]{3,2,1,0:T(8,128)(2,1)S(1)}, bf16[3,8,16,512]{3,2,1,0:T(8,128)(2,1)S(1)}, u32[]{:S(2)}, u32[]{:S(2)}) %collective-permute-start) | collective-permute-done | bytes 393248 | tf_op jit(solution)/shard_map/ppermute | solution.py:572
  27.9 2.1 %collective-permute-start.6 = (bf16[1,8,16,512]{3,2,1,0:T(8,128)(2,1)S(1)}, bf16[1,8,16,512]{3,2,1,0:T(8,128)(2,1)S(1)}, u32[]{:S(2)}, u32[]{:S(2)}) collective-permute-start(bf16[1,8,16,512]{3,2,1,0:T(8,128)(2,1)S(1)} %get-tuple-element.58), channel_id=1, source_target_pairs={{0,2},{2,0},{4,6},{6,4},{8,10},{10,8},{12,14},{14,12},{1,3},{3,1},... | collective-permute-start | bytes 393224 | tf_op jit(solution)/shard_map/ppermute | solution.py:572
  30.6 1.6 %collective-permute-start.5 = (bf16[3,9,16,512]{3,2,1,0:T(8,128)(2,1)S(1)}, bf16[3,9,16,512]{3,2,1,0:T(8,128)(2,1)S(1)}, u32[]{:S(2)}, u32[]{:S(2)}) collective-permute-start(bf16[3,9,16,512]{3,2,1,0:T(8,128)(2,1)S(1)} %join_last.5.last), channel_id=1, source_target_pairs={{0,4},{2,6},{4,8},{6,10},{8,12},{10,14},{12,0},{14,2},{1,5},{3,7},... | collective-permute-start | bytes 1327112 | tf_op jit(solution)/shard_map/ppermute | solution.py:572
  32.9 5.0 %early.1 = (f32[176,512]{1,0:T(8,128)S(1)}, bf16[2,128,512]{2,1,0:T(8,128)(2,1)S(1)}, bf16[3,2,2,16,512]{4,3,2,1,0:T(8,128)(2,1)S(1)}) custom-call(s32[3]{0:T(128)S(1)} %pad_add_fusion.scalars, bf16[5,11,16,512]{3,2,1,0:T(8,128)(2,1)S(1)} %join_first.2.first.refs_2_, bf16[2,11,16,512]{3,2,1,0:T(8,128)(2,1)S(1)} %join_last.3.refs_0_, ...), custom_call_target="tpu_custom_call" | custom-call | flops 3607101440 | bytes 9312256 | tf_op jit(solution)/shard_map/early/pallas_call | solution.py:251
  37.9 3.9 %late.1 = (bf16[4,32,512]{2,1,0:T(8,128)(2,1)S(1)}, bf16[4,32,512]{2,1,0:T(8,128)(2,1)S(1)}, bf16[4,32,512]{2,1,0:T(8,128)(2,1)S(1)}, bf16[4,32,512]{2,1,0:T(8,128)(2,1)S(1)}, bf16[3,2,2,16,512]{4,3,2,1,0:T(8,128)(2,1)S(1)}) custom-call(s32[3]{0:T(128)S(1)} %pad_add_fusion.scalars, bf16[2,11,16,512]{3,2,1,0:T(8,128)(2,1)S(1)} %collective-permute-done.7.refs_0_, ...), custom_call_target="tpu_custom_call" | custom-call | flops 2407530496 | bytes 9672704 | tf_op jit(solution)/shard_map/late/pallas_call | solution.py:411
  41.9 1.6 %collective-permute-start.10 = (bf16[4,32,512]{2,1,0:T(8,128)(2,1)S(1)}, bf16[4,32,512]{2,1,0:T(8,128)(2,1)S(1)}, u32[]{:S(2)}, u32[]{:S(2)}) collective-permute-start(bf16[4,32,512]{2,1,0:T(8,128)(2,1)S(1)} %get-tuple-element.70), channel_id=1, source_target_pairs={{0,4},{2,6},{4,0},{6,2},{8,12},{10,14},{12,8},{14,10},{1,5},{3,7},... | collective-permute-start | bytes 393224 | tf_op jit(solution)/shard_map/ppermute | solution.py:572
  43.5 2.4 %collective-permute-start.11 = (bf16[4,32,512]{2,1,0:T(8,128)(2,1)S(1)}, bf16[4,32,512]{2,1,0:T(8,128)(2,1)S(1)}, u32[]{:S(2)}, u32[]{:S(2)}) collective-permute-start(bf16[4,32,512]{2,1,0:T(8,128)(2,1)S(1)} %get-tuple-element.71), channel_id=1, source_target_pairs={{0,8},{2,10},{4,12},{6,14},{8,0},{10,2},{12,4},{14,6},{1,9},{3,11}... | collective-permute-start | bytes 393224 | tf_op jit(solution)/shard_map/ppermute | solution.py:572
  47.0 7.3 %full.1 = (bf16[4,32,512]{2,1,0:T(8,128)(2,1)S(1)}, bf16[4,32,512]{2,1,0:T(8,128)(2,1)S(1)}, bf16[4,32,512]{2,1,0:T(8,128)(2,1)S(1)}, bf16[4,32,512]{2,1,0:T(8,128)(2,1)S(1)}) custom-call(s32[3]{0:T(128)S(1)} %pad_add_fusion.scalars, bf16[3,9,16,512]{3,2,1,0:T(8,128)(2,1)S(1)} %collective-permute-done.5.halo, bf16[5,9,16,512]{3,2,1,0:T(8,128)(2,1)S(1)} %join_first.3.first, ...), custom_call_target="tpu_custom_call" | custom-call | flops 5360320512 | bytes 9492480 | tf_op jit(solution)/shard_map/full/pallas_call | solution.py:338
  55.1 3.3 %collective-permute-start.14 = (bf16[4,32,512]{2,1,0:T(8,128)(2,1)S(1)}, bf16[4,32,512]{2,1,0:T(8,128)(2,1)S(1)}, u32[]{:S(2)}, u32[]{:S(2)}) collective-permute-start(bf16[4,32,512]{2,1,0:T(8,128)(2,1)S(1)} %get-tuple-element.76), channel_id=1, source_target_pairs={{0,8},{2,10},{4,12},{6,14},{8,0},{10,2},{12,4},{14,6},{1,9},{3,11}... | collective-permute-start | bytes 393224 | tf_op jit(solution)/shard_map/ppermute | solution.py:572
  58.8 2.8 %attend.2 = (bf16[2,32,512]{2,1,0:T(8,128)(2,1)S(1)}, bf16[2,32,512]{2,1,0:T(8,128)(2,1)S(1)}, bf16[2,32,512]{2,1,0:T(8,128)(2,1)S(1)}, bf16[2,32,512]{2,1,0:T(8...) custom-call(s32[3]{0:T(128)S(1)} %pad_add_fusion.scalars, ...), custom_call_target="tpu_custom_call" | custom-call | flops 1342177280 | bytes 2621440 | tf_op jit(solution)/shard_map/attend/pallas_call | solution.py:501
  61.6 1.4 %collective-permute-start.23 = (bf16[2,32,512]{2,1,0:T(8,128)(2,1)S(1)}, bf16[2,32,512]{2,1,0:T(8,128)(2,1)S(1)}, u32[]{:S(2)}, u32[]{:S(2)}) collective-permute-start(bf16[2,32,512]{2,1,0:T(8,128)(2,1)S(1)} %get-tuple-element.86), channel_id=1, source_target_pairs={{0,2},{2,0},{4,6},{6,4},{8,10},{10,8},{12,14},{14,12},{1,3},{3,1},... | collective-permute-start | bytes 196616 | tf_op jit(solution)/shard_map/ppermute | solution.py:572
  63.3 1.9 %collective-permute-start.25 = (bf16[2,32,512]{2,1,0:T(8,128)(2,1)S(1)}, bf16[2,32,512]{2,1,0:T(8,128)(2,1)S(1)}, u32[]{:S(2)}, u32[]{:S(2)}) collective-permute-start(bf16[2,32,512]{2,1,0:T(8,128)(2,1)S(1)} %get-tuple-element.88), channel_id=1, source_target_pairs={{0,6},{2,4},{4,2},{6,0},{8,14},{10,12},{12,10},{14,8},{1,7},{3,5},... | collective-permute-start | bytes 196616 | tf_op jit(solution)/shard_map/ppermute | solution.py:572
  66.1 1.1 %collective-permute-start.26 = (bf16[2,32,512]{2,1,0:T(8,128)(2,1)S(1)}, bf16[2,32,512]{2,1,0:T(8,128)(2,1)S(1)}, u32[]{:S(2)}, u32[]{:S(2)}) collective-permute-start(bf16[2,32,512]{2,1,0:T(8,128)(2,1)S(1)} %get-tuple-element.89), channel_id=1, source_target_pairs={{0,8},{2,10},{4,12},{6,14},{8,0},{10,2},{12,4},{14,6},{1,9},{3,11}... | collective-permute-start | bytes 196616 | tf_op jit(solution)/shard_map/ppermute | solution.py:572
  67.2 6.2 %collective-permute-start.27 = (bf16[2,32,512]{2,1,0:T(8,128)(2,1)S(1)}, bf16[2,32,512]{2,1,0:T(8,128)(2,1)S(1)}, u32[]{:S(2)}, u32[]{:S(2)}) collective-permute-start(bf16[2,32,512]{2,1,0:T(8,128)(2,1)S(1)} %get-tuple-element.90), channel_id=1, source_target_pairs={{0,10},{2,8},{4,14},{6,12},{8,2},{10,0},{12,6},{14,4},{1,11},{3,9}... | collective-permute-start | bytes 196616 | tf_op jit(solution)/shard_map/ppermute | solution.py:572
  73.4 2.8 %attend.3 = (bf16[2,32,512]{2,1,0:T(8,128)(2,1)S(1)}, bf16[2,32,512]{2,1,0:T(8,128)(2,1)S(1)}, bf16[2,32,512]{2,1,0:T(8,128)(2,1)S(1)}, bf16[2,32,512]{2,1,0:T(8...) custom-call(s32[3]{0:T(128)S(1)} %pad_add_fusion.scalars, ...), custom_call_target="tpu_custom_call" | custom-call | flops 1342177280 | bytes 2621440 | tf_op jit(solution)/shard_map/attend/pallas_call | solution.py:501
  76.8 2.3 %collective-permute-start.29 = (bf16[2,32,512]{2,1,0:T(8,128)(2,1)S(1)}, bf16[2,32,512]{2,1,0:T(8,128)(2,1)S(1)}, u32[]{:S(2)}, u32[]{:S(2)}) collective-permute-start(bf16[2,32,512]{2,1,0:T(8,128)(2,1)S(1)} %get-tuple-element.92), channel_id=1, source_target_pairs={{0,14},{2,12},{4,10},{6,8},{8,6},{10,4},{12,2},{14,0},{1,15},{3,13... | collective-permute-start | bytes 196616 | tf_op jit(solution)/shard_map/ppermute | solution.py:572
  79.1 2.5 %collective-permute-start.16 = (bf16[2,32,512]{2,1,0:T(8,128)(2,1)S(1)}, bf16[2,32,512]{2,1,0:T(8,128)(2,1)S(1)}, u32[]{:S(2)}, u32[]{:S(2)}) collective-permute-start(bf16[2,32,512]{2,1,0:T(8,128)(2,1)S(1)} %get-tuple-element.79), channel_id=1, source_target_pairs={{0,2},{2,0},{4,6},{6,4},{8,10},{10,8},{12,14},{14,12},{1,3},{3,1},... | collective-permute-start | bytes 196616 | tf_op jit(solution)/shard_map/ppermute | solution.py:572
  81.6 1.5 %collective-permute-start.18 = (bf16[2,32,512]{2,1,0:T(8,128)(2,1)S(1)}, bf16[2,32,512]{2,1,0:T(8,128)(2,1)S(1)}, u32[]{:S(2)}, u32[]{:S(2)}) collective-permute-start(bf16[2,32,512]{2,1,0:T(8,128)(2,1)S(1)} %get-tuple-element.81), channel_id=1, source_target_pairs={{0,6},{2,4},{4,2},{6,0},{8,14},{10,12},{12,10},{14,8},{1,7},{3,5},... | collective-permute-start | bytes 196616 | tf_op jit(solution)/shard_map/ppermute | solution.py:572
  83.9 3.6 %collective-permute-start.20 = (bf16[2,32,512]{2,1,0:T(8,128)(2,1)S(1)}, bf16[2,32,512]{2,1,0:T(8,128)(2,1)S(1)}, u32[]{:S(2)}, u32[]{:S(2)}) collective-permute-start(bf16[2,32,512]{2,1,0:T(8,128)(2,1)S(1)} %get-tuple-element.83), channel_id=1, source_target_pairs={{0,10},{2,8},{4,14},{6,12},{8,2},{10,0},{12,6},{14,4},{1,11},{3,9}... | collective-permute-start | bytes 196616 | tf_op jit(solution)/shard_map/ppermute | solution.py:572
  88.0 2.8 %collective-permute-start.22 = (bf16[2,32,512]{2,1,0:T(8,128)(2,1)S(1)}, bf16[2,32,512]{2,1,0:T(8,128)(2,1)S(1)}, u32[]{:S(2)}, u32[]{:S(2)}) collective-permute-start(bf16[2,32,512]{2,1,0:T(8,128)(2,1)S(1)} %get-tuple-element.85), channel_id=1, source_target_pairs={{0,14},{2,12},{4,10},{6,8},{8,6},{10,4},{12,2},{14,0},{1,15},{3,13... | collective-permute-start | bytes 196616 | tf_op jit(solution)/shard_map/ppermute | solution.py:572
  90.8 1.4 %collect.2.refs_8_ = bf16[2,16,32,512]{3,2,1,0:T(8,128)(2,1)} custom-call(s32[3]{0:T(128)S(1)} %pad_add_fusion.scalars, bf16[2,32,512]{2,1,0:T(8,128)(2,1)S(1)} %get-tuple-element.73.refs_0_, bf16[2,32,512]{2,1,0:T(8,128)(2,1)S(1)} %collective-permute-done.23.refs_1_, bf16[2,32,512]{2,1,0:T(8,128)(2,1)S(1)} %collective-permute-done.24.refs_2_, ...), custom_call_target="tpu_custom_call" | custom-call | tf_op jit(solution)/shard_map/collect/pallas_call | solution.py:527
  92.2 1.4 %collective-permute-done.21.refs_6_ = bf16[2,32,512]{2,1,0:T(8,128)(2,1)S(1)} collective-permute-done((bf16[2,32,512]{2,1,0:T(8,128)(2,1)S(1)}, bf16[2,32,512]{2,1,0:T(8,128)(2,1)S(1)}, u32[]{:S(2)}, u32[]{:S(2)}) %collective-permute-start.21) | collective-permute-done | bytes 65568 | tf_op jit(solution)/shard_map/ppermute | solution.py:572
  93.6 1.4 %collective-permute-done.22.refs_7_ = bf16[2,32,512]{2,1,0:T(8,128)(2,1)S(1)} collective-permute-done((bf16[2,32,512]{2,1,0:T(8,128)(2,1)S(1)}, bf16[2,32,512]{2,1,0:T(8,128)(2,1)S(1)}, u32[]{:S(2)}, u32[]{:S(2)}) %collective-permute-start.22) | collective-permute-done | bytes 65568 | tf_op jit(solution)/shard_map/ppermute | solution.py:572
  95.1 1.4 %collect.3 = bf16[2,16,32,512]{3,2,1,0:T(8,128)(2,1)} custom-call(s32[3]{0:T(128)S(1)} %pad_add_fusion.scalars, bf16[2,32,512]{2,1,0:T(8,128)(2,1)S(1)} %get-tuple-element.78.refs_0_, bf16[2,32,512]{2,1,0:T(8,128)(2,1)S(1)} %collective-permute-done.16.refs_1_, ...), custom_call_target="tpu_custom_call", output_to_operand_aliasing={{}: (9, {})} | custom-call | tf_op jit(solution)/shard_map/collect/pallas_call | solution.py:527
  (77 shorter events, 10.2 us)
Async XLA Ops:
  2.3 13.4 %collective-permute-start.2 = (bf16[2,10,16,512]{3,2,1,0:T(8,128)(2,1)S(1)}, bf16[2,10,16,512]{3,2,1,0:T(8,128)(2,1)S(1)}, u32[]{:S(2)}, u32[]{:S(2)}) collective-permute-start(bf16[2,10,16,512]{3,2,1,0:T(8,128)(2,1)S(1)} %get-tuple-element.51), channel_id=1, source_target_pairs={{0,2},{2,0},{4,6},{6,4},{8,10},{10,8},{12,14},{14,12},{1,3},{3,1},... | collective-permute-start | bytes 983048 | tf_op jit(solution)/shard_map/ppermute | solution.py:572
  7.4 8.1 %collective-permute-start.4 = (bf16[4,18,512]{2,1,0:T(8,128)(2,1)S(1)}, bf16[4,18,512]{2,1,0:T(8,128)(2,1)S(1)}, u32[]{:S(2)}, u32[]{:S(2)}) collective-permute-start(bf16[4,18,512]{2,1,0:T(8,128)(2,1)S(1)} %get-tuple-element.95), channel_id=1, source_target_pairs={{0,3},{1,2},{2,1},{3,0},{4,7},{5,6},{6,5},{7,4},{8,11},{9,10},{10,... | collective-permute-start | bytes 221192 | tf_op jit(solution)/shard_map/ppermute | solution.py:594
  7.5 8.1 %collective-permute-start.3 = (bf16[4,18,512]{2,1,0:T(8,128)(2,1)S(1)}, bf16[4,18,512]{2,1,0:T(8,128)(2,1)S(1)}, u32[]{:S(2)}, u32[]{:S(2)}) collective-permute-start(bf16[4,18,512]{2,1,0:T(8,128)(2,1)S(1)} %get-tuple-element.96), channel_id=1, source_target_pairs={{0,1},{1,0},{2,3},{3,2},{4,5},{5,4},{6,7},{7,6},{8,9},{9,8},{10,11... | collective-permute-start | bytes 221192 | tf_op jit(solution)/shard_map/ppermute | solution.py:588
  7.6 11.8 %collective-permute-start.1 = (bf16[1,10,16,512]{3,2,1,0:T(8,128)(2,1)S(1)}, bf16[1,10,16,512]{3,2,1,0:T(8,128)(2,1)S(1)}, u32[]{:S(2)}, u32[]{:S(2)}) collective-permute-start(bf16[1,10,16,512]{3,2,1,0:T(8,128)(2,1)S(1)} %get-tuple-element.50), channel_id=1, source_target_pairs={{0,2},{2,0},{4,6},{6,4},{8,10},{10,8},{12,14},{14,12},{1,3},{3,1},... | collective-permute-start | bytes 491528 | tf_op jit(solution)/shard_map/ppermute | solution.py:572
  9.6 18.3 %collective-permute-start = (bf16[3,8,16,512]{3,2,1,0:T(8,128)(2,1)S(1)}, bf16[3,8,16,512]{3,2,1,0:T(8,128)(2,1)S(1)}, u32[]{:S(2)}, u32[]{:S(2)}) collective-permute-start(bf16[3,8,16,512]{3,2,1,0:T(8,128)(2,1)S(1)} %get-tuple-element.49), channel_id=1, source_target_pairs={{0,2},{2,0},{4,6},{6,4},{8,10},{10,8},{12,14},{14,12},{1,3},{3,1},... | collective-permute-start | bytes 1179656 | tf_op jit(solution)/shard_map/ppermute | solution.py:572
  15.7 16.5 %collective-permute-start.9 = (bf16[1,10,16,512]{3,2,1,0:T(8,128)(2,1)S(1)}, bf16[1,10,16,512]{3,2,1,0:T(8,128)(2,1)S(1)}, u32[]{:S(2)}, u32[]{:S(2)}) collective-permute-start(bf16[1,10,16,512]{3,2,1,0:T(8,128)(2,1)S(1)} %get-tuple-element.60), channel_id=1, source_target_pairs={{0,2},{2,0},{4,6},{6,4},{8,10},{10,8},{12,14},{14,12},{1,3},{3,1},... | collective-permute-start | bytes 491528 | tf_op jit(solution)/shard_map/ppermute | solution.py:572
  16.6 21.4 %collective-permute-start.7 = (bf16[2,11,16,512]{3,2,1,0:T(8,128)(2,1)S(1)}, bf16[2,11,16,512]{3,2,1,0:T(8,128)(2,1)S(1)}, u32[]{:S(2)}, u32[]{:S(2)}) collective-permute-start(bf16[2,11,16,512]{3,2,1,0:T(8,128)(2,1)S(1)} %join_last.3.refs_0_), channel_id=1, source_target_pairs={{0,4},{2,6},{4,8},{6,10},{8,12},{10,14},{12,0},{14,2},{1,5},{3,7},... | collective-permute-start | bytes 1081352 | tf_op jit(solution)/shard_map/ppermute | solution.py:572
  18.5 14.3 %copy-start.4 = (f32[512]{0:T(512)S(1)}, f32[512]{0:T(512)}, u32[]{:S(2)}) copy-start(f32[512]{0:T(512)} %param.14) | copy-start | bytes 6148
  18.5 14.3 %copy-start.5 = (f32[512]{0:T(512)S(1)}, f32[512]{0:T(512)}, u32[]{:S(2)}) copy-start(f32[512]{0:T(512)} %param.16) | copy-start | bytes 6148
  20.1 17.8 %collective-permute-start.8 = (bf16[1,11,16,512]{3,2,1,0:T(8,128)(2,1)S(1)}, bf16[1,11,16,512]{3,2,1,0:T(8,128)(2,1)S(1)}, u32[]{:S(2)}, u32[]{:S(2)}) collective-permute-start(bf16[1,11,16,512]{3,2,1,0:T(8,128)(2,1)S(1)} %join_last.4.refs_1_), channel_id=1, source_target_pairs={{0,4},{2,6},{4,8},{6,10},{8,12},{10,14},{12,0},{14,2},{1,5},{3,7},... | collective-permute-start | bytes 540680 | tf_op jit(solution)/shard_map/ppermute | solution.py:572
  27.9 13.9 %collective-permute-start.6 = (bf16[1,8,16,512]{3,2,1,0:T(8,128)(2,1)S(1)}, bf16[1,8,16,512]{3,2,1,0:T(8,128)(2,1)S(1)}, u32[]{:S(2)}, u32[]{:S(2)}) collective-permute-start(bf16[1,8,16,512]{3,2,1,0:T(8,128)(2,1)S(1)} %get-tuple-element.58), channel_id=1, source_target_pairs={{0,2},{2,0},{4,6},{6,4},{8,10},{10,8},{12,14},{14,12},{1,3},{3,1},... | collective-permute-start | bytes 393224 | tf_op jit(solution)/shard_map/ppermute | solution.py:572
  30.6 16.4 %collective-permute-start.5 = (bf16[3,9,16,512]{3,2,1,0:T(8,128)(2,1)S(1)}, bf16[3,9,16,512]{3,2,1,0:T(8,128)(2,1)S(1)}, u32[]{:S(2)}, u32[]{:S(2)}) collective-permute-start(bf16[3,9,16,512]{3,2,1,0:T(8,128)(2,1)S(1)} %join_last.5.last), channel_id=1, source_target_pairs={{0,4},{2,6},{4,8},{6,10},{8,12},{10,14},{12,0},{14,2},{1,5},{3,7},... | collective-permute-start | bytes 1327112 | tf_op jit(solution)/shard_map/ppermute | solution.py:572
  41.9 16.5 %collective-permute-start.10 = (bf16[4,32,512]{2,1,0:T(8,128)(2,1)S(1)}, bf16[4,32,512]{2,1,0:T(8,128)(2,1)S(1)}, u32[]{:S(2)}, u32[]{:S(2)}) collective-permute-start(bf16[4,32,512]{2,1,0:T(8,128)(2,1)S(1)} %get-tuple-element.70), channel_id=1, source_target_pairs={{0,4},{2,6},{4,0},{6,2},{8,12},{10,14},{12,8},{14,10},{1,5},{3,7},... | collective-permute-start | bytes 393224 | tf_op jit(solution)/shard_map/ppermute | solution.py:572
  43.5 15.3 %collective-permute-start.11 = (bf16[4,32,512]{2,1,0:T(8,128)(2,1)S(1)}, bf16[4,32,512]{2,1,0:T(8,128)(2,1)S(1)}, u32[]{:S(2)}, u32[]{:S(2)}) collective-permute-start(bf16[4,32,512]{2,1,0:T(8,128)(2,1)S(1)} %get-tuple-element.71), channel_id=1, source_target_pairs={{0,8},{2,10},{4,12},{6,14},{8,0},{10,2},{12,4},{14,6},{1,9},{3,11}... | collective-permute-start | bytes 393224 | tf_op jit(solution)/shard_map/ppermute | solution.py:572
  45.8 12.9 %collective-permute-start.12 = (bf16[4,32,512]{2,1,0:T(8,128)(2,1)S(1)}, bf16[4,32,512]{2,1,0:T(8,128)(2,1)S(1)}, u32[]{:S(2)}, u32[]{:S(2)}) collective-permute-start(bf16[4,32,512]{2,1,0:T(8,128)(2,1)S(1)} %get-tuple-element.72), channel_id=1, source_target_pairs={{0,12},{2,14},{4,8},{6,10},{8,4},{10,6},{12,0},{14,2},{1,13},{3,15... | collective-permute-start | bytes 393224 | tf_op jit(solution)/shard_map/ppermute | solution.py:572
  54.3 9.0 %collective-permute-start.13 = (bf16[4,32,512]{2,1,0:T(8,128)(2,1)S(1)}, bf16[4,32,512]{2,1,0:T(8,128)(2,1)S(1)}, u32[]{:S(2)}, u32[]{:S(2)}) collective-permute-start(bf16[4,32,512]{2,1,0:T(8,128)(2,1)S(1)} %get-tuple-element.75), channel_id=1, source_target_pairs={{0,4},{2,6},{4,0},{6,2},{8,12},{10,14},{12,8},{14,10},{1,5},{3,7},... | collective-permute-start | bytes 393224 | tf_op jit(solution)/shard_map/ppermute | solution.py:572
  55.1 11.1 %collective-permute-start.14 = (bf16[4,32,512]{2,1,0:T(8,128)(2,1)S(1)}, bf16[4,32,512]{2,1,0:T(8,128)(2,1)S(1)}, u32[]{:S(2)}, u32[]{:S(2)}) collective-permute-start(bf16[4,32,512]{2,1,0:T(8,128)(2,1)S(1)} %get-tuple-element.76), channel_id=1, source_target_pairs={{0,8},{2,10},{4,12},{6,14},{8,0},{10,2},{12,4},{14,6},{1,9},{3,11}... | collective-permute-start | bytes 393224 | tf_op jit(solution)/shard_map/ppermute | solution.py:572
  58.3 8.9 %collective-permute-start.15 = (bf16[4,32,512]{2,1,0:T(8,128)(2,1)S(1)}, bf16[4,32,512]{2,1,0:T(8,128)(2,1)S(1)}, u32[]{:S(2)}, u32[]{:S(2)}) collective-permute-start(bf16[4,32,512]{2,1,0:T(8,128)(2,1)S(1)} %get-tuple-element.77), channel_id=1, source_target_pairs={{0,12},{2,14},{4,8},{6,10},{8,4},{10,6},{12,0},{14,2},{1,13},{3,15... | collective-permute-start | bytes 393224 | tf_op jit(solution)/shard_map/ppermute | solution.py:572
  61.6 14.6 %collective-permute-start.23 = (bf16[2,32,512]{2,1,0:T(8,128)(2,1)S(1)}, bf16[2,32,512]{2,1,0:T(8,128)(2,1)S(1)}, u32[]{:S(2)}, u32[]{:S(2)}) collective-permute-start(bf16[2,32,512]{2,1,0:T(8,128)(2,1)S(1)} %get-tuple-element.86), channel_id=1, source_target_pairs={{0,2},{2,0},{4,6},{6,4},{8,10},{10,8},{12,14},{14,12},{1,3},{3,1},... | collective-permute-start | bytes 196616 | tf_op jit(solution)/shard_map/ppermute | solution.py:572
  63.0 13.8 %collective-permute-start.24 = (bf16[2,32,512]{2,1,0:T(8,128)(2,1)S(1)}, bf16[2,32,512]{2,1,0:T(8,128)(2,1)S(1)}, u32[]{:S(2)}, u32[]{:S(2)}) collective-permute-start(bf16[2,32,512]{2,1,0:T(8,128)(2,1)S(1)} %get-tuple-element.87), channel_id=1, source_target_pairs={{0,4},{2,6},{4,0},{6,2},{8,12},{10,14},{12,8},{14,10},{1,5},{3,7},... | collective-permute-start | bytes 196616 | tf_op jit(solution)/shard_map/ppermute | solution.py:572
  63.3 15.8 %collective-permute-start.25 = (bf16[2,32,512]{2,1,0:T(8,128)(2,1)S(1)}, bf16[2,32,512]{2,1,0:T(8,128)(2,1)S(1)}, u32[]{:S(2)}, u32[]{:S(2)}) collective-permute-start(bf16[2,32,512]{2,1,0:T(8,128)(2,1)S(1)} %get-tuple-element.88), channel_id=1, source_target_pairs={{0,6},{2,4},{4,2},{6,0},{8,14},{10,12},{12,10},{14,8},{1,7},{3,5},... | collective-permute-start | bytes 196616 | tf_op jit(solution)/shard_map/ppermute | solution.py:572
  66.1 15.5 %collective-permute-start.26 = (bf16[2,32,512]{2,1,0:T(8,128)(2,1)S(1)}, bf16[2,32,512]{2,1,0:T(8,128)(2,1)S(1)}, u32[]{:S(2)}, u32[]{:S(2)}) collective-permute-start(bf16[2,32,512]{2,1,0:T(8,128)(2,1)S(1)} %get-tuple-element.89), channel_id=1, source_target_pairs={{0,8},{2,10},{4,12},{6,14},{8,0},{10,2},{12,4},{14,6},{1,9},{3,11}... | collective-permute-start | bytes 196616 | tf_op jit(solution)/shard_map/ppermute | solution.py:572
  67.2 14.4 %collective-permute-start.27 = (bf16[2,32,512]{2,1,0:T(8,128)(2,1)S(1)}, bf16[2,32,512]{2,1,0:T(8,128)(2,1)S(1)}, u32[]{:S(2)}, u32[]{:S(2)}) collective-permute-start(bf16[2,32,512]{2,1,0:T(8,128)(2,1)S(1)} %get-tuple-element.90), channel_id=1, source_target_pairs={{0,10},{2,8},{4,14},{6,12},{8,2},{10,0},{12,6},{14,4},{1,11},{3,9}... | collective-permute-start | bytes 196616 | tf_op jit(solution)/shard_map/ppermute | solution.py:572
  76.2 6.9 %collective-permute-start.28 = (bf16[2,32,512]{2,1,0:T(8,128)(2,1)S(1)}, bf16[2,32,512]{2,1,0:T(8,128)(2,1)S(1)}, u32[]{:S(2)}, u32[]{:S(2)}) collective-permute-start(bf16[2,32,512]{2,1,0:T(8,128)(2,1)S(1)} %get-tuple-element.91), channel_id=1, source_target_pairs={{0,12},{2,14},{4,8},{6,10},{8,4},{10,6},{12,0},{14,2},{1,13},{3,15... | collective-permute-start | bytes 196616 | tf_op jit(solution)/shard_map/ppermute | solution.py:572
  76.8 7.0 %collective-permute-start.29 = (bf16[2,32,512]{2,1,0:T(8,128)(2,1)S(1)}, bf16[2,32,512]{2,1,0:T(8,128)(2,1)S(1)}, u32[]{:S(2)}, u32[]{:S(2)}) collective-permute-start(bf16[2,32,512]{2,1,0:T(8,128)(2,1)S(1)} %get-tuple-element.92), channel_id=1, source_target_pairs={{0,14},{2,12},{4,10},{6,8},{8,6},{10,4},{12,2},{14,0},{1,15},{3,13... | collective-permute-start | bytes 196616 | tf_op jit(solution)/shard_map/ppermute | solution.py:572
  79.1 8.4 %collective-permute-start.16 = (bf16[2,32,512]{2,1,0:T(8,128)(2,1)S(1)}, bf16[2,32,512]{2,1,0:T(8,128)(2,1)S(1)}, u32[]{:S(2)}, u32[]{:S(2)}) collective-permute-start(bf16[2,32,512]{2,1,0:T(8,128)(2,1)S(1)} %get-tuple-element.79), channel_id=1, source_target_pairs={{0,2},{2,0},{4,6},{6,4},{8,10},{10,8},{12,14},{14,12},{1,3},{3,1},... | collective-permute-start | bytes 196616 | tf_op jit(solution)/shard_map/ppermute | solution.py:572
  81.6 6.4 %collective-permute-start.17 = (bf16[2,32,512]{2,1,0:T(8,128)(2,1)S(1)}, bf16[2,32,512]{2,1,0:T(8,128)(2,1)S(1)}, u32[]{:S(2)}, u32[]{:S(2)}) collective-permute-start(bf16[2,32,512]{2,1,0:T(8,128)(2,1)S(1)} %get-tuple-element.80), channel_id=1, source_target_pairs={{0,4},{2,6},{4,0},{6,2},{8,12},{10,14},{12,8},{14,10},{1,5},{3,7},... | collective-permute-start | bytes 196616 | tf_op jit(solution)/shard_map/ppermute | solution.py:572
  81.6 10.6 %collective-permute-start.18 = (bf16[2,32,512]{2,1,0:T(8,128)(2,1)S(1)}, bf16[2,32,512]{2,1,0:T(8,128)(2,1)S(1)}, u32[]{:S(2)}, u32[]{:S(2)}) collective-permute-start(bf16[2,32,512]{2,1,0:T(8,128)(2,1)S(1)} %get-tuple-element.81), channel_id=1, source_target_pairs={{0,6},{2,4},{4,2},{6,0},{8,14},{10,12},{12,10},{14,8},{1,7},{3,5},... | collective-permute-start | bytes 196616 | tf_op jit(solution)/shard_map/ppermute | solution.py:572
  83.1 9.1 %collective-permute-start.19 = (bf16[2,32,512]{2,1,0:T(8,128)(2,1)S(1)}, bf16[2,32,512]{2,1,0:T(8,128)(2,1)S(1)}, u32[]{:S(2)}, u32[]{:S(2)}) collective-permute-start(bf16[2,32,512]{2,1,0:T(8,128)(2,1)S(1)} %get-tuple-element.82), channel_id=1, source_target_pairs={{0,8},{2,10},{4,12},{6,14},{8,0},{10,2},{12,4},{14,6},{1,9},{3,11}... | collective-permute-start | bytes 196616 | tf_op jit(solution)/shard_map/ppermute | solution.py:572
  83.9 8.3 %collective-permute-start.20 = (bf16[2,32,512]{2,1,0:T(8,128)(2,1)S(1)}, bf16[2,32,512]{2,1,0:T(8,128)(2,1)S(1)}, u32[]{:S(2)}, u32[]{:S(2)}) collective-permute-start(bf16[2,32,512]{2,1,0:T(8,128)(2,1)S(1)} %get-tuple-element.83), channel_id=1, source_target_pairs={{0,10},{2,8},{4,14},{6,12},{8,2},{10,0},{12,6},{14,4},{1,11},{3,9}... | collective-permute-start | bytes 196616 | tf_op jit(solution)/shard_map/ppermute | solution.py:572
  87.5 6.2 %collective-permute-start.21 = (bf16[2,32,512]{2,1,0:T(8,128)(2,1)S(1)}, bf16[2,32,512]{2,1,0:T(8,128)(2,1)S(1)}, u32[]{:S(2)}, u32[]{:S(2)}) collective-permute-start(bf16[2,32,512]{2,1,0:T(8,128)(2,1)S(1)} %get-tuple-element.84), channel_id=1, source_target_pairs={{0,12},{2,14},{4,8},{6,10},{8,4},{10,6},{12,0},{14,2},{1,13},{3,15... | collective-permute-start | bytes 196616 | tf_op jit(solution)/shard_map/ppermute | solution.py:572
  88.0 7.1 %collective-permute-start.22 = (bf16[2,32,512]{2,1,0:T(8,128)(2,1)S(1)}, bf16[2,32,512]{2,1,0:T(8,128)(2,1)S(1)}, u32[]{:S(2)}, u32[]{:S(2)}) collective-permute-start(bf16[2,32,512]{2,1,0:T(8,128)(2,1)S(1)} %get-tuple-element.85), channel_id=1, source_target_pairs={{0,14},{2,12},{4,10},{6,8},{8,6},{10,4},{12,2},{14,0},{1,15},{3,13... | collective-permute-start | bytes 196616 | tf_op jit(solution)/shard_map/ppermute | solution.py:572
  (11 other events, 115.9 us)

commit v15 on v13

--- a/solution.py
+++ b/solution.py
@@ -410,10 +410,12 @@
     )(scalars, halo, first, part, spatial, *weights)
 
 
-def attend_kernel(frames_per, lanes, count, scalars, *refs):
-    blocks = refs[:count]
-    gain, w_query, w_key, w_value, w_out = refs[count : count + 5]
-    outs = refs[count + 5 :]
+def attend_kernel(frames_per, lanes, count, near, chunks, scalars, *refs):
+    blocks, refs = refs[:count], refs[count:]
+    gain, w_query, w_key, w_value, w_out = refs[:5]
+    waiting, outs = refs[5 : 5 + near * (chunks - 1)], refs[5 + near * (chunks - 1) :]
+    for index, block in enumerate(waiting):
+        outs[1 + index % near][index // near] = block[...]
     channels = gain.shape[-1]
     flat = len(blocks[0].shape) == 2
     groups = 1 if flat else blocks[0].shape[1] // lanes
@@ -468,11 +470,16 @@
 
                 @pl.when(scalars[0] == side)
                 def _():
+                    part = slice(g * lanes, (g + 1) * lanes)
                     for x in range(pair):
-                        outs[pair * j + x][:, g * lanes : (g + 1) * lanes] = rows[side ^ x]
-
-
-def attend(scalars, blocks, gain, w_query, w_key, w_value, w_out):
+                        m = pair * j + x
+                        if 0 < m <= near:
+                            outs[m][chunks - 1, :, part] = rows[side ^ x]
+                        else:
+                            outs[m][:, part] = rows[side ^ x]
+
+
+def attend(scalars, blocks, near, waiting, gain, w_query, w_key, w_value, w_out):
     frames_per, pixels, channels = blocks[0].shape
     flat = pixels % 16 != 0
     lanes = pixels if flat else 16
@@ -480,43 +487,47 @@
         blocks = [b.reshape(frames_per * pixels, channels) for b in blocks]
     count = len(blocks)
     size = frames_per * count * lanes
-    shapes = [(frames_per // pair, pixels, channels)] * (pair * count)
+    block = (frames_per // pair, pixels, channels)
+    chunks = 1 + len(waiting) // near if near else 1
+    shapes = [
+        (chunks,) + block if 0 < m <= near else block for m in range(pair * count)
+    ]
     if flat:
         shapes = [blocks[0].shape]
     flops = 2 * frames_per * pixels * count * channels * (4 * channels + 2 * size)
     outs = pl.pallas_call(
-        partial(attend_kernel, frames_per, lanes, count),
+        partial(attend_kernel, frames_per, lanes, count, near, chunks),
         out_shape=[jax.ShapeDtypeStruct(shape, jnp.bfloat16) for shape in shapes],
-        in_specs=[SMEM] + [VMEM] * (count + 5),
+        in_specs=[SMEM] + [VMEM] * (count + 5 + len(waiting)),
         out_specs=[VMEM] * len(shapes),
         compiler_params=params(20 if 16 * size * size < 20 * mebibyte else 56),
         cost_estimate=cost(flops, *blocks, w_query, w_key, w_value, w_out),
         name="attend",
-    )(scalars, *blocks, gain, w_query, w_key, w_value, w_out)
+    )(scalars, *blocks, gain, w_query, w_key, w_value, w_out, *waiting)
     return [o.reshape(frames_per, pixels, channels) for o in outs] if flat else outs
 
 
-def collect_kernel(base, stride, scalars, *refs):
+def collect_kernel(entries, levels, chunks, scalars, *refs):
     out, sems = refs[-2:]
     copies = []
-    for m in range(sems.shape[0]):
-        index = base + (scalars[0] ^ m % pair) * stride + (scalars[2] ^ m // pair)
-        copies.append(pltpu.make_async_copy(refs[m], out.at[:, index], sems.at[m]))
+    for index, (ref, sub, k, m) in enumerate(entries):
+        block = refs[ref] if sub is None else refs[ref].at[sub]
+        place = ((scalars[0] ^ m % pair) * chunks + k) * levels + (scalars[2] ^ m // pair)
+        copies.append(pltpu.make_async_copy(block, out.at[:, place], sems.at[index]))
     run(copies)
 
 
-def collect(scalars, blocks, chunk, chunks, whole):
-    count = len(blocks)
-    halves, pixels, channels = blocks[0].shape
-    levels = count // pair
+def collect(scalars, blocks, entries, levels, chunks, whole):
+    halves, pixels, channels = blocks[0].shape[-3:]
     given = [] if whole is None else [whole]
+    shape = (halves, chunks * pair * levels, pixels, channels)
     return pl.pallas_call(
-        partial(collect_kernel, chunk * levels, chunks * levels),
-        out_shape=jax.ShapeDtypeStruct((halves, chunks * count, pixels, channels), jnp.bfloat16),
-        in_specs=[SMEM] + [ANY] * (count + len(given)),
+        partial(collect_kernel, entries, levels, chunks),
+        out_shape=jax.ShapeDtypeStruct(shape, jnp.bfloat16),
+        in_specs=[SMEM] + [ANY] * (len(blocks) + len(given)),
         out_specs=ANY,
-        input_output_aliases={count + 1: 0} if given else {},
-        scratch_shapes=[pltpu.SemaphoreType.DMA((count,))],
+        input_output_aliases={len(blocks) + 1: 0} if given else {},
+        scratch_shapes=[pltpu.SemaphoreType.DMA((len(entries),))],
         compiler_params=params(16),
         name="collect",
     )(scalars, *blocks, *given)
@@ -626,24 +637,33 @@
             + [tm_permute(blocks[j], lambda i: i ^ (pair * j)) for j in range(1, levels)]
             for blocks in spatials
         ]
-        returns = []
-        for gathered in gathers:
+        far = devices // 2
+        near = far - 1
+        whole, waiting = None, []
+        for k, gathered in enumerate(gathers):
             gathered[0] = after(gathered[0], newest)
-            results = attend(scalars, gathered, *attention)
+            final = k == chunks - 1
+            results = attend(
+                scalars, gathered, near if final else 0, waiting if final else [], *attention
+            )
             newest = results[0]
-            returns.append(
-                [results[0]]
-                + [tm_permute(results[m], lambda i: i ^ m) for m in range(1, devices)]
-            )
-        whole = None
-        for k, blocks in enumerate(returns):
-            whole = collect(scalars, blocks, k, chunks, whole)
+            blocks = [tm_permute(results[m], lambda i: i ^ m) for m in range(far, devices)]
+            entries = [(m - far, None, k, m) for m in range(far, devices)]
+            if final:
+                for m in range(1, far):
+                    entries += [(len(blocks), c, c, m) for c in range(chunks)]
+                    blocks.append(tm_permute(results[m], lambda i: i ^ m))
+            else:
+                waiting += results[1:far]
+            entries.append((len(blocks), None, k, 0))
+            blocks.append(results[0])
+            whole = collect(scalars, blocks, entries, levels, chunks, whole)
         return whole.reshape(frames // 2, height, width, channels)
     sets = [[pair * z + s for z in range(levels)] for s in range(pair)]
     returns = []
     for (block,) in spatials:
         gathered = lax.all_to_all(block, "tm", 1, 0, axis_index_groups=sets, tiled=True)
-        (result,) = attend(scalars, [gathered], *attention)
+        (result,) = attend(scalars, [gathered], 0, [], *attention)
         result = lax.all_to_all(result, "tm", 0, 1, tiled=True)
         result = result.reshape(frames // 2, levels, pair, each, channels)
         returns.append(result.transpose(0, 2, 1, 3, 4).reshape(frames // 2, pair, -1, channels))

time: 95.9 us -> 95.1 us (level)
  starting transfers between devices: 42.1 us -> 40.3 us
  waiting for transfers between devices: 18.7 us -> 19.7 us
    ppermute x26 -> x23, starting transfers between devices: 41.9 us -> 40.1 us  [tm_permute(): lax.ppermute(value, 'tm', [(i, move(i)) for i in range(devices) if move(i...]
    ppermute x26 -> x23, waiting for transfers between devices: 12.2 us -> 13.2 us  [tm_permute(): lax.ppermute(value, 'tm', [(i, move(i)) for i in range(devices) if move(i...]
  transfers between devices with their start and end apart: 28 -> 25, of which waited for: 9 -> 10; matrix products, arithmetic and copies ran while one was open for 5% -> 5% of each run, Pallas kernels for 27% -> 27%
where the time goes in v15:
time: 95.1 us; the launch traced here: 94.9 us
  starting transfers between devices  40.3 us (42%)
  Pallas kernels  27.7 us (29%)
  waiting for transfers between devices  19.7 us (21%)
  local copies, waits for them, and re-layouts  3.73 us (4%)
  other arithmetic  2.99 us (3%)
    ppermute x23, starting transfers between devices, tm_permute(): lax.ppermute(value, 'tm', [(i, move(i)) for i in range(devices) if move(i...  40.1 us
    ppermute x23, waiting for transfers between devices, tm_permute(): lax.ppermute(value, 'tm', [(i, move(i)) for i in range(devices) if move(i...  13.2 us
    pallas_call x1, Pallas kernels, full(): pl.pallas_call(partial(full_kernel, owners, final, rows), out_shape=[jax....  7.33 us
    ppermute x1, waiting for transfers between devices, per_device(): other_edge = lax.ppermute(other_edge, ('tm', 'cols'), aslant)  6.52 us
    pallas_call x2, Pallas kernels, attend(): pl.pallas_call(partial(attend_kernel, frames_per, lanes, count, near, chu...  5.6 us
    pallas_call x1, Pallas kernels, early(): pl.pallas_call(partial(early_kernel, final, rows), out_shape=shapes, in_s...  5.03 us
    pallas_call x1, Pallas kernels, late(): pl.pallas_call(partial(late_kernel, owners, final, rows), out_shape=[jax....  3.91 us
    select_n x1, other arithmetic, per_device(): w_space = jnp.where(after(place, video) >= 0, w_space, 0)  2.79 us
  transfers between devices with their start and end apart: 25, of which 10 were waited for; matrix products, arithmetic and copies ran while one was open for 5% of the time, Pallas kernels for 27%

profile of v15, /device:TPU:0, one launch (start us, length us, event | category | flops | bytes accessed | tf_op | source)
XLA Modules:
  0.0 94.9 jit_solution(4387419223636897030)
XLA Ops:
  0.1 1.6 %copy-done = bf16[4,32,16,512]{3,2,1,0:T(8,128)(2,1)S(1)} copy-done((bf16[4,32,16,512]{3,2,1,0:T(8,128)(2,1)S(1)}, bf16[4,32,16,512]{3,2,1,0:T(8,128)(2,1)}, u32[]{:S(2)}) %copy-start) | copy-done | bytes 2097176
  2.3 3.0 %collective-permute-start.1 = (bf16[3,10,16,512]{3,2,1,0:T(8,128)(2,1)S(1)}, bf16[3,10,16,512]{3,2,1,0:T(8,128)(2,1)S(1)}, u32[]{:S(2)}, u32[]{:S(2)}) collective-permute-start(bf16[3,10,16,512]{3,2,1,0:T(8,128)(2,1)S(1)} %get-tuple-element.47), channel_id=1, source_target_pairs={{0,2},{2,0},{4,6},{6,4},{8,10},{10,8},{12,14},{14,12},{1,3},{3,1},... | collective-permute-start | bytes 1474568 | tf_op jit(solution)/shard_map/ppermute | solution.py:569
  5.3 1.9 %fusion.3 = (bf16[4,32,1,512]{3,2,1,0:T(2,128)(2,1)S(1)}, bf16[4,32,1,512]{3,2,1,0:T(2,128)(2,1)S(1)}) fusion(bf16[4,32,16,512]{3,2,1,0:T(8,128)(2,1)} %video.9), kind=kLoop, calls=%fused_computation.12 | loop fusion | bytes 524288 | tf_op jit(solution)/shard_map/slice | solution.py:573
  7.6 2.0 %collective-permute-start.2 = (bf16[1,10,16,512]{3,2,1,0:T(8,128)(2,1)S(1)}, bf16[1,10,16,512]{3,2,1,0:T(8,128)(2,1)S(1)}, u32[]{:S(2)}, u32[]{:S(2)}) collective-permute-start(bf16[1,10,16,512]{3,2,1,0:T(8,128)(2,1)S(1)} %get-tuple-element.50), channel_id=1, source_target_pairs={{0,2},{2,0},{4,6},{6,4},{8,10},{10,8},{12,14},{14,12},{1,3},{3,1},... | collective-permute-start | bytes 491528 | tf_op jit(solution)/shard_map/ppermute | solution.py:569
  9.7 2.8 %broadcast_select_fusion.w_space = bf16[9,512,512]{2,1,0:T(8,128)(2,1)S(1)} fusion(bf16[9,512,512]{2,1,0:T(8,128)(2,1)} %param.17, pred[]{:T(512)S(6)} %ge.3), kind=kLoop, calls=%fused_computation | loop fusion | flops 2359296 | bytes 9437185 | tf_op jit(solution)/shard_map/jit(_where)/select_n | solution.py:554
  12.5 6.5 %collective-permute-done.4 = bf16[4,18,512]{2,1,0:T(8,128)(2,1)S(1)} collective-permute-done((bf16[4,18,512]{2,1,0:T(8,128)(2,1)S(1)}, bf16[4,18,512]{2,1,0:T(8,128)(2,1)S(1)}, u32[]{:S(2)}, u32[]{:S(2)}) %collective-permute-start.4) | collective-permute-done | bytes 73760 | tf_op jit(solution)/shard_map/ppermute | solution.py:584
  19.9 1.6 %collective-permute-start.7 = (bf16[3,11,16,512]{3,2,1,0:T(8,128)(2,1)S(1)}, bf16[3,11,16,512]{3,2,1,0:T(8,128)(2,1)S(1)}, u32[]{:S(2)}, u32[]{:S(2)}) collective-permute-start(bf16[3,11,16,512]{3,2,1,0:T(8,128)(2,1)S(1)} %join_last.2.last), channel_id=1, source_target_pairs={{0,4},{2,6},{4,8},{6,10},{8,12},{10,14},{12,0},{14,2},{1,5},{3,7},... | collective-permute-start | bytes 1622024 | tf_op jit(solution)/shard_map/ppermute | solution.py:569
  21.5 1.5 %collective-permute-done.2.others = bf16[1,10,16,512]{3,2,1,0:T(8,128)(2,1)S(1)} collective-permute-done((bf16[1,10,16,512]{3,2,1,0:T(8,128)(2,1)S(1)}, bf16[1,10,16,512]{3,2,1,0:T(8,128)(2,1)S(1)}, u32[]{:S(2)}, u32[]{:S(2)}) %collective-permute-start.2) | collective-permute-done | bytes 163872 | tf_op jit(solution)/shard_map/ppermute | solution.py:569
  23.7 5.0 %early.1 = (f32[176,512]{1,0:T(8,128)S(1)}, bf16[2,128,512]{2,1,0:T(8,128)(2,1)S(1)}, bf16[3,2,2,16,512]{4,3,2,1,0:T(8,128)(2,1)S(1)}) custom-call(s32[3]{0:T(128)S(1)} %pad_add_fusion.scalars, bf16[5,11,16,512]{3,2,1,0:T(8,128)(2,1)S(1)} %join_first.2.first, bf16[3,11,16,512]{3,2,1,0:T(8,128)(2,1)S(1)} %join_last.2.last, bf16[1536,512]{1,0:T(8,128)(2,1)S(1)} %bitcast.26, ...), custom_call_target="tpu_custom_call" | custom-call | flops 3607101440 | bytes 9312256 | tf_op jit(solution)/shard_map/early/pallas_call | solution.py:239
  28.7 1.9 %collective-permute-done.received = bf16[3,8,16,512]{3,2,1,0:T(8,128)(2,1)S(1)} collective-permute-done((bf16[3,8,16,512]{3,2,1,0:T(8,128)(2,1)S(1)}, bf16[3,8,16,512]{3,2,1,0:T(8,128)(2,1)S(1)}, u32[]{:S(2)}, u32[]{:S(2)}) %collective-permute-start) | collective-permute-done | bytes 393248 | tf_op jit(solution)/shard_map/ppermute | solution.py:569
  31.2 1.8 %collective-permute-start.5 = (bf16[3,9,16,512]{3,2,1,0:T(8,128)(2,1)S(1)}, bf16[3,9,16,512]{3,2,1,0:T(8,128)(2,1)S(1)}, u32[]{:S(2)}, u32[]{:S(2)}) collective-permute-start(bf16[3,9,16,512]{3,2,1,0:T(8,128)(2,1)S(1)} %join_last.3.last), channel_id=1, source_target_pairs={{0,4},{2,6},{4,8},{6,10},{8,12},{10,14},{12,0},{14,2},{1,5},{3,7},... | collective-permute-start | bytes 1327112 | tf_op jit(solution)/shard_map/ppermute | solution.py:569
  33.0 1.5 %collective-permute-start.6 = (bf16[1,8,16,512]{3,2,1,0:T(8,128)(2,1)S(1)}, bf16[1,8,16,512]{3,2,1,0:T(8,128)(2,1)S(1)}, u32[]{:S(2)}, u32[]{:S(2)}) collective-permute-start(bf16[1,8,16,512]{3,2,1,0:T(8,128)(2,1)S(1)} %get-tuple-element.55), channel_id=1, source_target_pairs={{0,2},{2,0},{4,6},{6,4},{8,10},{10,8},{12,14},{14,12},{1,3},{3,1},... | collective-permute-start | bytes 393224 | tf_op jit(solution)/shard_map/ppermute | solution.py:569
  34.6 2.3 %collective-permute-done.7.halo = bf16[3,11,16,512]{3,2,1,0:T(8,128)(2,1)S(1)} collective-permute-done((bf16[3,11,16,512]{3,2,1,0:T(8,128)(2,1)S(1)}, bf16[3,11,16,512]{3,2,1,0:T(8,128)(2,1)S(1)}, u32[]{:S(2)}, u32[]{:S(2)}) %collective-permute-start.7) | collective-permute-done | bytes 540704 | tf_op jit(solution)/shard_map/ppermute | solution.py:569
  36.9 3.9 %late.1 = (bf16[4,32,512]{2,1,0:T(8,128)(2,1)S(1)}, bf16[4,32,512]{2,1,0:T(8,128)(2,1)S(1)}, bf16[4,32,512]{2,1,0:T(8,128)(2,1)S(1)}, bf16[4,32,512]{2,1,0:T(8,128)(2,1)S(1)}, bf16[3,2,2,16,512]{4,3,2,1,0:T(8,128)(2,1)S(1)}) custom-call(s32[3]{0:T(128)S(1)} %pad_add_fusion.scalars, bf16[3,11,16,512]{3,2,1,0:T(8,128)(2,1)S(1)} %collective-permute-done.7.halo, ...), custom_call_target="tpu_custom_call" | custom-call | flops 2407530496 | bytes 9672704 | tf_op jit(solution)/shard_map/late/pallas_call | solution.py:397
  40.9 2.4 %collective-permute-start.9 = (bf16[4,32,512]{2,1,0:T(8,128)(2,1)S(1)}, bf16[4,32,512]{2,1,0:T(8,128)(2,1)S(1)}, u32[]{:S(2)}, u32[]{:S(2)}) collective-permute-start(bf16[4,32,512]{2,1,0:T(8,128)(2,1)S(1)} %get-tuple-element.65), channel_id=1, source_target_pairs={{0,8},{2,10},{4,12},{6,14},{8,0},{10,2},{12,4},{14,6},{1,9},{3,11}... | collective-permute-start | bytes 393224 | tf_op jit(solution)/shard_map/ppermute | solution.py:569
  43.2 2.0 %collective-permute-start.10 = (bf16[4,32,512]{2,1,0:T(8,128)(2,1)S(1)}, bf16[4,32,512]{2,1,0:T(8,128)(2,1)S(1)}, u32[]{:S(2)}, u32[]{:S(2)}) collective-permute-start(bf16[4,32,512]{2,1,0:T(8,128)(2,1)S(1)} %get-tuple-element.66), channel_id=1, source_target_pairs={{0,12},{2,14},{4,8},{6,10},{8,4},{10,6},{12,0},{14,2},{1,13},{3,15... | collective-permute-start | bytes 393224 | tf_op jit(solution)/shard_map/ppermute | solution.py:569
  46.5 7.3 %full.1 = (bf16[4,32,512]{2,1,0:T(8,128)(2,1)S(1)}, bf16[4,32,512]{2,1,0:T(8,128)(2,1)S(1)}, bf16[4,32,512]{2,1,0:T(8,128)(2,1)S(1)}, bf16[4,32,512]{2,1,0:T(8,128)(2,1)S(1)}) custom-call(s32[3]{0:T(128)S(1)} %pad_add_fusion.scalars, bf16[3,9,16,512]{3,2,1,0:T(8,128)(2,1)S(1)} %collective-permute-done.5.halo, bf16[5,9,16,512]{3,2,1,0:T(8,128)(2,1)S(1)} %join_first.3.first, ...), custom_call_target="tpu_custom_call" | custom-call | flops 5360320512 | bytes 9492480 | tf_op jit(solution)/shard_map/full/pallas_call | solution.py:326
  53.9 4.9 %collective-permute-start.12 = (bf16[4,32,512]{2,1,0:T(8,128)(2,1)S(1)}, bf16[4,32,512]{2,1,0:T(8,128)(2,1)S(1)}, u32[]{:S(2)}, u32[]{:S(2)}) collective-permute-start(bf16[4,32,512]{2,1,0:T(8,128)(2,1)S(1)} %get-tuple-element.70), channel_id=1, source_target_pairs={{0,8},{2,10},{4,12},{6,14},{8,0},{10,2},{12,4},{14,6},{1,9},{3,11}... | collective-permute-start | bytes 393224 | tf_op jit(solution)/shard_map/ppermute | solution.py:569
  58.9 2.8 %attend.2 = (bf16[2,32,512]{2,1,0:T(8,128)(2,1)S(1)}, bf16[2,32,512]{2,1,0:T(8,128)(2,1)S(1)}, bf16[2,32,512]{2,1,0:T(8,128)(2,1)S(1)}, bf16[2,32,512]{2,1,0:T(8...) custom-call(s32[3]{0:T(128)S(1)} %pad_add_fusion.scalars, ...), custom_call_target="tpu_custom_call" | custom-call | flops 1342177280 | bytes 2621440 | tf_op jit(solution)/shard_map/attend/pallas_call | solution.py:498
  61.7 1.6 %collective-permute-start.21 = (bf16[2,32,512]{2,1,0:T(8,128)(2,1)S(1)}, bf16[2,32,512]{2,1,0:T(8,128)(2,1)S(1)}, u32[]{:S(2)}, u32[]{:S(2)}) collective-permute-start(bf16[2,32,512]{2,1,0:T(8,128)(2,1)S(1)} %get-tuple-element.83), channel_id=1, source_target_pairs={{0,8},{2,10},{4,12},{6,14},{8,0},{10,2},{12,4},{14,6},{1,9},{3,11}... | collective-permute-start | bytes 196616 | tf_op jit(solution)/shard_map/ppermute | solution.py:569
  63.3 1.8 %collective-permute-start.22 = (bf16[2,32,512]{2,1,0:T(8,128)(2,1)S(1)}, bf16[2,32,512]{2,1,0:T(8,128)(2,1)S(1)}, u32[]{:S(2)}, u32[]{:S(2)}) collective-permute-start(bf16[2,32,512]{2,1,0:T(8,128)(2,1)S(1)} %get-tuple-element.84), channel_id=1, source_target_pairs={{0,10},{2,8},{4,14},{6,12},{8,2},{10,0},{12,6},{14,4},{1,11},{3,9}... | collective-permute-start | bytes 196616 | tf_op jit(solution)/shard_map/ppermute | solution.py:569
  65.1 3.8 %collective-permute-start.23 = (bf16[2,32,512]{2,1,0:T(8,128)(2,1)S(1)}, bf16[2,32,512]{2,1,0:T(8,128)(2,1)S(1)}, u32[]{:S(2)}, u32[]{:S(2)}) collective-permute-start(bf16[2,32,512]{2,1,0:T(8,128)(2,1)S(1)} %get-tuple-element.85), channel_id=1, source_target_pairs={{0,12},{2,14},{4,8},{6,10},{8,4},{10,6},{12,0},{14,2},{1,13},{3,15... | collective-permute-start | bytes 196616 | tf_op jit(solution)/shard_map/ppermute | solution.py:569
  68.9 3.2 %collective-permute-done.12.refs_2_ = bf16[4,32,512]{2,1,0:T(8,128)(2,1)S(1)} collective-permute-done((bf16[4,32,512]{2,1,0:T(8,128)(2,1)S(1)}, bf16[4,32,512]{2,1,0:T(8,128)(2,1)S(1)}, u32[]{:S(2)}, u32[]{:S(2)}) %collective-permute-start.12) | collective-permute-done | bytes 131104 | tf_op jit(solution)/shard_map/ppermute | solution.py:569
  72.1 1.4 %collective-permute-start.24 = (bf16[2,32,512]{2,1,0:T(8,128)(2,1)S(1)}, bf16[2,32,512]{2,1,0:T(8,128)(2,1)S(1)}, u32[]{:S(2)}, u32[]{:S(2)}) collective-permute-start(bf16[2,32,512]{2,1,0:T(8,128)(2,1)S(1)} %get-tuple-element.86), channel_id=1, source_target_pairs={{0,14},{2,12},{4,10},{6,8},{8,6},{10,4},{12,2},{14,0},{1,15},{3,13... | collective-permute-start | bytes 196616 | tf_op jit(solution)/shard_map/ppermute | solution.py:569
  73.5 2.8 %attend.3 = (bf16[2,32,512]{2,1,0:T(8,128)(2,1)S(1)}, bf16[2,2,32,512]{3,2,1,0:T(8,128)(2,1)S(1)}, bf16[2,2,32,512]{3,2,1,0:T(8,128)(2,1)S(1)}, bf16[2,2,32,512]...) custom-call(s32[3]{0:T(128)S(1)} %pad_add_fusion.scalars, ...), custom_call_target="tpu_custom_call" | custom-call | flops 1342177280 | bytes 2621440 | tf_op jit(solution)/shard_map/attend/pallas_call | solution.py:498
  76.3 3.2 %collective-permute-start.14 = (bf16[2,32,512]{2,1,0:T(8,128)(2,1)S(1)}, bf16[2,32,512]{2,1,0:T(8,128)(2,1)S(1)}, u32[]{:S(2)}, u32[]{:S(2)}) collective-permute-start(bf16[2,32,512]{2,1,0:T(8,128)(2,1)S(1)} %get-tuple-element.75), channel_id=1, source_target_pairs={{0,8},{2,10},{4,12},{6,14},{8,0},{10,2},{12,4},{14,6},{1,9},{3,11}... | collective-permute-start | bytes 196616 | tf_op jit(solution)/shard_map/ppermute | solution.py:569
  81.0 1.7 %collective-permute-start.19 = (bf16[2,2,32,512]{3,2,1,0:T(8,128)(2,1)S(1)}, bf16[2,2,32,512]{3,2,1,0:T(8,128)(2,1)S(1)}, u32[]{:S(2)}, u32[]{:S(2)}) collective-permute-start(bf16[2,2,32,512]{3,2,1,0:T(8,128)(2,1)S(1)} %get-tuple-element.80), channel_id=1, source_target_pairs={{0,4},{2,6},{4,0},{6,2},{8,12},{10,14},{12,8},{14,10},{1,5},{3,7},... | collective-permute-start | bytes 393224 | tf_op jit(solution)/shard_map/ppermute | solution.py:569
  82.8 1.7 %collective-permute-start.20 = (bf16[2,2,32,512]{3,2,1,0:T(8,128)(2,1)S(1)}, bf16[2,2,32,512]{3,2,1,0:T(8,128)(2,1)S(1)}, u32[]{:S(2)}, u32[]{:S(2)}) collective-permute-start(bf16[2,2,32,512]{3,2,1,0:T(8,128)(2,1)S(1)} %get-tuple-element.81), channel_id=1, source_target_pairs={{0,6},{2,4},{4,2},{6,0},{8,14},{10,12},{12,10},{14,8},{1,7},{3,5},... | collective-permute-start | bytes 393224 | tf_op jit(solution)/shard_map/ppermute | solution.py:569
  86.3 3.1 %collective-permute-start.17 = (bf16[2,32,512]{2,1,0:T(8,128)(2,1)S(1)}, bf16[2,32,512]{2,1,0:T(8,128)(2,1)S(1)}, u32[]{:S(2)}, u32[]{:S(2)}) collective-permute-start(bf16[2,32,512]{2,1,0:T(8,128)(2,1)S(1)} %get-tuple-element.78), channel_id=1, source_target_pairs={{0,14},{2,12},{4,10},{6,8},{8,6},{10,4},{12,2},{14,0},{1,15},{3,13... | collective-permute-start | bytes 196616 | tf_op jit(solution)/shard_map/ppermute | solution.py:569
  89.4 1.3 %collect.2.refs_8_ = bf16[2,16,32,512]{3,2,1,0:T(8,128)(2,1)} custom-call(s32[3]{0:T(128)S(1)} %pad_add_fusion.scalars, bf16[2,32,512]{2,1,0:T(8,128)(2,1)S(1)} %collective-permute-done.21.refs_0_, bf16[2,32,512]{2,1,0:T(8,128)(2,1)S(1)} %collective-permute-done.22.refs_1_, bf16[2,32,512]{2,1,0:T(8,128)(2,1)S(1)} %collective-permute-done.23.refs_2_, ...), custom_call_target="tpu_custom_call" | custom-call | tf_op jit(solution)/shard_map/collect/pallas_call | solution.py:524
  91.6 1.7 %collective-permute-done.17.refs_3_ = bf16[2,32,512]{2,1,0:T(8,128)(2,1)S(1)} collective-permute-done((bf16[2,32,512]{2,1,0:T(8,128)(2,1)S(1)}, bf16[2,32,512]{2,1,0:T(8,128)(2,1)S(1)}, u32[]{:S(2)}, u32[]{:S(2)}) %collective-permute-start.17) | collective-permute-done | bytes 65568 | tf_op jit(solution)/shard_map/ppermute | solution.py:569
  93.3 1.5 %collect.3 = bf16[2,16,32,512]{3,2,1,0:T(8,128)(2,1)} custom-call(s32[3]{0:T(128)S(1)} %pad_add_fusion.scalars, bf16[2,32,512]{2,1,0:T(8,128)(2,1)S(1)} %collective-permute-done.14.refs_0_, bf16[2,32,512]{2,1,0:T(8,128)(2,1)S(1)} %collective-permute-done.15.refs_1_, ...), custom_call_target="tpu_custom_call", output_to_operand_aliasing={{}: (9, {})} | custom-call | tf_op jit(solution)/shard_map/collect/pallas_call | solution.py:524
  (66 shorter events, 8.7 us)
Async XLA Ops:
  2.3 16.9 %collective-permute-start.1 = (bf16[3,10,16,512]{3,2,1,0:T(8,128)(2,1)S(1)}, bf16[3,10,16,512]{3,2,1,0:T(8,128)(2,1)S(1)}, u32[]{:S(2)}, u32[]{:S(2)}) collective-permute-start(bf16[3,10,16,512]{3,2,1,0:T(8,128)(2,1)S(1)} %get-tuple-element.47), channel_id=1, source_target_pairs={{0,2},{2,0},{4,6},{6,4},{8,10},{10,8},{12,14},{14,12},{1,3},{3,1},... | collective-permute-start | bytes 1474568 | tf_op jit(solution)/shard_map/ppermute | solution.py:569
  7.4 11.6 %collective-permute-start.4 = (bf16[4,18,512]{2,1,0:T(8,128)(2,1)S(1)}, bf16[4,18,512]{2,1,0:T(8,128)(2,1)S(1)}, u32[]{:S(2)}, u32[]{:S(2)}) collective-permute-start(bf16[4,18,512]{2,1,0:T(8,128)(2,1)S(1)} %get-tuple-element.89), channel_id=1, source_target_pairs={{0,3},{1,2},{2,1},{3,0},{4,7},{5,6},{6,5},{7,4},{8,11},{9,10},{10,... | collective-permute-start | bytes 221192 | tf_op jit(solution)/shard_map/ppermute | solution.py:584
  7.5 11.6 %collective-permute-start.3 = (bf16[4,18,512]{2,1,0:T(8,128)(2,1)S(1)}, bf16[4,18,512]{2,1,0:T(8,128)(2,1)S(1)}, u32[]{:S(2)}, u32[]{:S(2)}) collective-permute-start(bf16[4,18,512]{2,1,0:T(8,128)(2,1)S(1)} %get-tuple-element.90), channel_id=1, source_target_pairs={{0,1},{1,0},{2,3},{3,2},{4,5},{5,4},{6,7},{7,6},{8,9},{9,8},{10,11... | collective-permute-start | bytes 221192 | tf_op jit(solution)/shard_map/ppermute | solution.py:578
  7.6 15.4 %collective-permute-start.2 = (bf16[1,10,16,512]{3,2,1,0:T(8,128)(2,1)S(1)}, bf16[1,10,16,512]{3,2,1,0:T(8,128)(2,1)S(1)}, u32[]{:S(2)}, u32[]{:S(2)}) collective-permute-start(bf16[1,10,16,512]{3,2,1,0:T(8,128)(2,1)S(1)} %get-tuple-element.50), channel_id=1, source_target_pairs={{0,2},{2,0},{4,6},{6,4},{8,10},{10,8},{12,14},{14,12},{1,3},{3,1},... | collective-permute-start | bytes 491528 | tf_op jit(solution)/shard_map/ppermute | solution.py:569
  9.6 21.0 %collective-permute-start = (bf16[3,8,16,512]{3,2,1,0:T(8,128)(2,1)S(1)}, bf16[3,8,16,512]{3,2,1,0:T(8,128)(2,1)S(1)}, u32[]{:S(2)}, u32[]{:S(2)}) collective-permute-start(bf16[3,8,16,512]{3,2,1,0:T(8,128)(2,1)S(1)} %get-tuple-element.46), channel_id=1, source_target_pairs={{0,2},{2,0},{4,6},{6,4},{8,10},{10,8},{12,14},{14,12},{1,3},{3,1},... | collective-permute-start | bytes 1179656 | tf_op jit(solution)/shard_map/ppermute | solution.py:569
  12.5 11.1 %copy-start.2 = (bf16[3,512,512]{2,1,0:T(8,128)(2,1)S(1)}, bf16[3,512,512]{2,1,0:T(8,128)(2,1)}, u32[]{:S(2)}) copy-start(bf16[3,512,512]{2,1,0:T(8,128)(2,1)} %param.13) | copy-start | bytes 4718596
  12.5 11.1 %copy-start.3 = (bf16[3,512,512]{2,1,0:T(8,128)(2,1)S(1)}, bf16[3,512,512]{2,1,0:T(8,128)(2,1)}, u32[]{:S(2)}) copy-start(bf16[3,512,512]{2,1,0:T(8,128)(2,1)} %param.15) | copy-start | bytes 4718596
  19.9 17.0 %collective-permute-start.7 = (bf16[3,11,16,512]{3,2,1,0:T(8,128)(2,1)S(1)}, bf16[3,11,16,512]{3,2,1,0:T(8,128)(2,1)S(1)}, u32[]{:S(2)}, u32[]{:S(2)}) collective-permute-start(bf16[3,11,16,512]{3,2,1,0:T(8,128)(2,1)S(1)} %join_last.2.last), channel_id=1, source_target_pairs={{0,4},{2,6},{4,8},{6,10},{8,12},{10,14},{12,0},{14,2},{1,5},{3,7},... | collective-permute-start | bytes 1622024 | tf_op jit(solution)/shard_map/ppermute | solution.py:569
  31.2 15.3 %collective-permute-start.5 = (bf16[3,9,16,512]{3,2,1,0:T(8,128)(2,1)S(1)}, bf16[3,9,16,512]{3,2,1,0:T(8,128)(2,1)S(1)}, u32[]{:S(2)}, u32[]{:S(2)}) collective-permute-start(bf16[3,9,16,512]{3,2,1,0:T(8,128)(2,1)S(1)} %join_last.3.last), channel_id=1, source_target_pairs={{0,4},{2,6},{4,8},{6,10},{8,12},{10,14},{12,0},{14,2},{1,5},{3,7},... | collective-permute-start | bytes 1327112 | tf_op jit(solution)/shard_map/ppermute | solution.py:569
  33.0 7.7 %collective-permute-start.6 = (bf16[1,8,16,512]{3,2,1,0:T(8,128)(2,1)S(1)}, bf16[1,8,16,512]{3,2,1,0:T(8,128)(2,1)S(1)}, u32[]{:S(2)}, u32[]{:S(2)}) collective-permute-start(bf16[1,8,16,512]{3,2,1,0:T(8,128)(2,1)S(1)} %get-tuple-element.55), channel_id=1, source_target_pairs={{0,2},{2,0},{4,6},{6,4},{8,10},{10,8},{12,14},{14,12},{1,3},{3,1},... | collective-permute-start | bytes 393224 | tf_op jit(solution)/shard_map/ppermute | solution.py:569
  40.8 18.0 %collective-permute-start.8 = (bf16[4,32,512]{2,1,0:T(8,128)(2,1)S(1)}, bf16[4,32,512]{2,1,0:T(8,128)(2,1)S(1)}, u32[]{:S(2)}, u32[]{:S(2)}) collective-permute-start(bf16[4,32,512]{2,1,0:T(8,128)(2,1)S(1)} %get-tuple-element.64), channel_id=1, source_target_pairs={{0,4},{2,6},{4,0},{6,2},{8,12},{10,14},{12,8},{14,10},{1,5},{3,7},... | collective-permute-start | bytes 393224 | tf_op jit(solution)/shard_map/ppermute | solution.py:569
  40.9 18.0 %collective-permute-start.9 = (bf16[4,32,512]{2,1,0:T(8,128)(2,1)S(1)}, bf16[4,32,512]{2,1,0:T(8,128)(2,1)S(1)}, u32[]{:S(2)}, u32[]{:S(2)}) collective-permute-start(bf16[4,32,512]{2,1,0:T(8,128)(2,1)S(1)} %get-tuple-element.65), channel_id=1, source_target_pairs={{0,8},{2,10},{4,12},{6,14},{8,0},{10,2},{12,4},{14,6},{1,9},{3,11}... | collective-permute-start | bytes 393224 | tf_op jit(solution)/shard_map/ppermute | solution.py:569
  43.2 15.6 %collective-permute-start.10 = (bf16[4,32,512]{2,1,0:T(8,128)(2,1)S(1)}, bf16[4,32,512]{2,1,0:T(8,128)(2,1)S(1)}, u32[]{:S(2)}, u32[]{:S(2)}) collective-permute-start(bf16[4,32,512]{2,1,0:T(8,128)(2,1)S(1)} %get-tuple-element.66), channel_id=1, source_target_pairs={{0,12},{2,14},{4,8},{6,10},{8,4},{10,6},{12,0},{14,2},{1,13},{3,15... | collective-permute-start | bytes 393224 | tf_op jit(solution)/shard_map/ppermute | solution.py:569
  46.5 12.4 %copy-start.7 = (bf16[512,512]{1,0:T(8,128)(2,1)S(1)}, bf16[512,512]{1,0:T(8,128)(2,1)}, u32[]{:S(2)}) copy-start(bf16[512,512]{1,0:T(8,128)(2,1)} %refs_5_.3) | copy-start | bytes 1572868
  46.5 12.4 %copy-start.8 = (bf16[512,512]{1,0:T(8,128)(2,1)S(1)}, bf16[512,512]{1,0:T(8,128)(2,1)}, u32[]{:S(2)}) copy-start(bf16[512,512]{1,0:T(8,128)(2,1)} %refs_6_.3) | copy-start | bytes 1572868
  46.5 12.4 %copy-start.9 = (bf16[512,512]{1,0:T(8,128)(2,1)S(1)}, bf16[512,512]{1,0:T(8,128)(2,1)}, u32[]{:S(2)}) copy-start(bf16[512,512]{1,0:T(8,128)(2,1)} %refs_7_.3) | copy-start | bytes 1572868
  46.5 12.4 %copy-start.10 = (bf16[512,512]{1,0:T(8,128)(2,1)S(1)}, bf16[512,512]{1,0:T(8,128)(2,1)}, u32[]{:S(2)}) copy-start(bf16[512,512]{1,0:T(8,128)(2,1)} %refs_8_.3) | copy-start | bytes 1572868
  46.5 12.4 %copy-start.11 = (f32[512]{0:T(512)S(1)}, f32[512]{0:T(512)}, u32[]{:S(2)}) copy-start(f32[512]{0:T(512)} %param.19) | copy-start | bytes 6148
  53.8 11.3 %collective-permute-start.11 = (bf16[4,32,512]{2,1,0:T(8,128)(2,1)S(1)}, bf16[4,32,512]{2,1,0:T(8,128)(2,1)S(1)}, u32[]{:S(2)}, u32[]{:S(2)}) collective-permute-start(bf16[4,32,512]{2,1,0:T(8,128)(2,1)S(1)} %get-tuple-element.69), channel_id=1, source_target_pairs={{0,4},{2,6},{4,0},{6,2},{8,12},{10,14},{12,8},{14,10},{1,5},{3,7},... | collective-permute-start | bytes 393224 | tf_op jit(solution)/shard_map/ppermute | solution.py:569
  53.9 18.2 %collective-permute-start.12 = (bf16[4,32,512]{2,1,0:T(8,128)(2,1)S(1)}, bf16[4,32,512]{2,1,0:T(8,128)(2,1)S(1)}, u32[]{:S(2)}, u32[]{:S(2)}) collective-permute-start(bf16[4,32,512]{2,1,0:T(8,128)(2,1)S(1)} %get-tuple-element.70), channel_id=1, source_target_pairs={{0,8},{2,10},{4,12},{6,14},{8,0},{10,2},{12,4},{14,6},{1,9},{3,11}... | collective-permute-start | bytes 393224 | tf_op jit(solution)/shard_map/ppermute | solution.py:569
  58.8 14.7 %collective-permute-start.13 = (bf16[4,32,512]{2,1,0:T(8,128)(2,1)S(1)}, bf16[4,32,512]{2,1,0:T(8,128)(2,1)S(1)}, u32[]{:S(2)}, u32[]{:S(2)}) collective-permute-start(bf16[4,32,512]{2,1,0:T(8,128)(2,1)S(1)} %get-tuple-element.71), channel_id=1, source_target_pairs={{0,12},{2,14},{4,8},{6,10},{8,4},{10,6},{12,0},{14,2},{1,13},{3,15... | collective-permute-start | bytes 393224 | tf_op jit(solution)/shard_map/ppermute | solution.py:569
  61.7 17.8 %collective-permute-start.21 = (bf16[2,32,512]{2,1,0:T(8,128)(2,1)S(1)}, bf16[2,32,512]{2,1,0:T(8,128)(2,1)S(1)}, u32[]{:S(2)}, u32[]{:S(2)}) collective-permute-start(bf16[2,32,512]{2,1,0:T(8,128)(2,1)S(1)} %get-tuple-element.83), channel_id=1, source_target_pairs={{0,8},{2,10},{4,12},{6,14},{8,0},{10,2},{12,4},{14,6},{1,9},{3,11}... | collective-permute-start | bytes 196616 | tf_op jit(solution)/shard_map/ppermute | solution.py:569
  63.3 17.4 %collective-permute-start.22 = (bf16[2,32,512]{2,1,0:T(8,128)(2,1)S(1)}, bf16[2,32,512]{2,1,0:T(8,128)(2,1)S(1)}, u32[]{:S(2)}, u32[]{:S(2)}) collective-permute-start(bf16[2,32,512]{2,1,0:T(8,128)(2,1)S(1)} %get-tuple-element.84), channel_id=1, source_target_pairs={{0,10},{2,8},{4,14},{6,12},{8,2},{10,0},{12,6},{14,4},{1,11},{3,9}... | collective-permute-start | bytes 196616 | tf_op jit(solution)/shard_map/ppermute | solution.py:569
  65.1 16.0 %collective-permute-start.23 = (bf16[2,32,512]{2,1,0:T(8,128)(2,1)S(1)}, bf16[2,32,512]{2,1,0:T(8,128)(2,1)S(1)}, u32[]{:S(2)}, u32[]{:S(2)}) collective-permute-start(bf16[2,32,512]{2,1,0:T(8,128)(2,1)S(1)} %get-tuple-element.85), channel_id=1, source_target_pairs={{0,12},{2,14},{4,8},{6,10},{8,4},{10,6},{12,0},{14,2},{1,13},{3,15... | collective-permute-start | bytes 196616 | tf_op jit(solution)/shard_map/ppermute | solution.py:569
  72.1 10.7 %collective-permute-start.24 = (bf16[2,32,512]{2,1,0:T(8,128)(2,1)S(1)}, bf16[2,32,512]{2,1,0:T(8,128)(2,1)S(1)}, u32[]{:S(2)}, u32[]{:S(2)}) collective-permute-start(bf16[2,32,512]{2,1,0:T(8,128)(2,1)S(1)} %get-tuple-element.86), channel_id=1, source_target_pairs={{0,14},{2,12},{4,10},{6,8},{8,6},{10,4},{12,2},{14,0},{1,15},{3,13... | collective-permute-start | bytes 196616 | tf_op jit(solution)/shard_map/ppermute | solution.py:569
  76.3 9.2 %collective-permute-start.14 = (bf16[2,32,512]{2,1,0:T(8,128)(2,1)S(1)}, bf16[2,32,512]{2,1,0:T(8,128)(2,1)S(1)}, u32[]{:S(2)}, u32[]{:S(2)}) collective-permute-start(bf16[2,32,512]{2,1,0:T(8,128)(2,1)S(1)} %get-tuple-element.75), channel_id=1, source_target_pairs={{0,8},{2,10},{4,12},{6,14},{8,0},{10,2},{12,4},{14,6},{1,9},{3,11}... | collective-permute-start | bytes 196616 | tf_op jit(solution)/shard_map/ppermute | solution.py:569
  79.5 6.8 %collective-permute-start.15 = (bf16[2,32,512]{2,1,0:T(8,128)(2,1)S(1)}, bf16[2,32,512]{2,1,0:T(8,128)(2,1)S(1)}, u32[]{:S(2)}, u32[]{:S(2)}) collective-permute-start(bf16[2,32,512]{2,1,0:T(8,128)(2,1)S(1)} %get-tuple-element.76), channel_id=1, source_target_pairs={{0,10},{2,8},{4,14},{6,12},{8,2},{10,0},{12,6},{14,4},{1,11},{3,9}... | collective-permute-start | bytes 196616 | tf_op jit(solution)/shard_map/ppermute | solution.py:569
  80.7 12.6 %collective-permute-start.18 = (bf16[2,2,32,512]{3,2,1,0:T(8,128)(2,1)S(1)}, bf16[2,2,32,512]{3,2,1,0:T(8,128)(2,1)S(1)}, u32[]{:S(2)}, u32[]{:S(2)}) collective-permute-start(bf16[2,2,32,512]{3,2,1,0:T(8,128)(2,1)S(1)} %get-tuple-element.79), channel_id=1, source_target_pairs={{0,2},{2,0},{4,6},{6,4},{8,10},{10,8},{12,14},{14,12},{1,3},{3,1},... | collective-permute-start | bytes 393224 | tf_op jit(solution)/shard_map/ppermute | solution.py:569
  81.0 12.2 %collective-permute-start.19 = (bf16[2,2,32,512]{3,2,1,0:T(8,128)(2,1)S(1)}, bf16[2,2,32,512]{3,2,1,0:T(8,128)(2,1)S(1)}, u32[]{:S(2)}, u32[]{:S(2)}) collective-permute-start(bf16[2,2,32,512]{3,2,1,0:T(8,128)(2,1)S(1)} %get-tuple-element.80), channel_id=1, source_target_pairs={{0,4},{2,6},{4,0},{6,2},{8,12},{10,14},{12,8},{14,10},{1,5},{3,7},... | collective-permute-start | bytes 393224 | tf_op jit(solution)/shard_map/ppermute | solution.py:569
  82.8 10.5 %collective-permute-start.20 = (bf16[2,2,32,512]{3,2,1,0:T(8,128)(2,1)S(1)}, bf16[2,2,32,512]{3,2,1,0:T(8,128)(2,1)S(1)}, u32[]{:S(2)}, u32[]{:S(2)}) collective-permute-start(bf16[2,2,32,512]{3,2,1,0:T(8,128)(2,1)S(1)} %get-tuple-element.81), channel_id=1, source_target_pairs={{0,6},{2,4},{4,2},{6,0},{8,14},{10,12},{12,10},{14,8},{1,7},{3,5},... | collective-permute-start | bytes 393224 | tf_op jit(solution)/shard_map/ppermute | solution.py:569
  85.5 6.2 %collective-permute-start.16 = (bf16[2,32,512]{2,1,0:T(8,128)(2,1)S(1)}, bf16[2,32,512]{2,1,0:T(8,128)(2,1)S(1)}, u32[]{:S(2)}, u32[]{:S(2)}) collective-permute-start(bf16[2,32,512]{2,1,0:T(8,128)(2,1)S(1)} %get-tuple-element.77), channel_id=1, source_target_pairs={{0,12},{2,14},{4,8},{6,10},{8,4},{10,6},{12,0},{14,2},{1,13},{3,15... | collective-permute-start | bytes 196616 | tf_op jit(solution)/shard_map/ppermute | solution.py:569
  86.3 7.0 %collective-permute-start.17 = (bf16[2,32,512]{2,1,0:T(8,128)(2,1)S(1)}, bf16[2,32,512]{2,1,0:T(8,128)(2,1)S(1)}, u32[]{:S(2)}, u32[]{:S(2)}) collective-permute-start(bf16[2,32,512]{2,1,0:T(8,128)(2,1)S(1)} %get-tuple-element.78), channel_id=1, source_target_pairs={{0,14},{2,12},{4,10},{6,8},{8,6},{10,4},{12,2},{14,0},{1,15},{3,13... | collective-permute-start | bytes 196616 | tf_op jit(solution)/shard_map/ppermute | solution.py:569
  (6 other events, 54.0 us)

commit v16 on v15

--- a/solution.py
+++ b/solution.py
@@ -59,16 +59,22 @@
 
 
 def send_kernel(spans, half, scalars, video, *outs):
-    frames = video.shape[0]
+    frames = pl.num_programs(0)
     rest = frames - taps
+    step = pl.program_id(0)
     for k, (begin, end) in enumerate(spans):
-        for t in range(frames):
-            target = outs[2 * k].at[t - rest] if t >= rest else outs[2 * k + 1].at[t]
-            cut(target, video, t, 1 - scalars[0], begin, end, half)
+
+        @pl.when(step < rest)
+        def _():
+            cut(outs[2 * k + 1].at[step], video, 0, 1 - scalars[0], begin, end, half)
+
+        @pl.when(step >= rest)
+        def _():
+            cut(outs[2 * k].at[step - rest], video, 0, 1 - scalars[0], begin, end, half)
 
 
 def send(scalars, video, spans, half):
-    frames, _, width, channels = video.shape
+    frames, height, width, channels = video.shape
     shapes = [
         (count, end - begin, width, channels)
         for begin, end in spans
@@ -76,10 +82,14 @@
     ]
     return pl.pallas_call(
         partial(send_kernel, spans, half),
+        grid=(frames,),
         out_shape=[jax.ShapeDtypeStruct(shape, video.dtype) for shape in shapes],
-        in_specs=[SMEM, VMEM],
-        out_specs=[VMEM] * len(shapes),
-        compiler_params=params(12),
+        in_specs=[
+            SMEM,
+            pl.BlockSpec((1, height, width, channels), lambda t: (t, 0, 0, 0)),
+        ],
+        out_specs=[pl.BlockSpec(shape, lambda t: (0, 0, 0, 0)) for shape in shapes],
+        compiler_params=params(56),
         name="send",
     )(scalars, video)
 

time: 95.1 us -> 97 us (1.020)
  Pallas kernels: 27.7 us -> 30.4 us
  local copies, waits for them, and re-layouts: 3.73 us -> 2.14 us
    pallas_call x1, Pallas kernels: 0.62 us -> 3.39 us  [send(): pl.pallas_call(partial(send_kernel, spans, half), grid=(frames,), out_sha...]
    unnamed x26 -> x28, local copies, waits for them, and re-layouts: 1.65 us -> 0.07 us
  transfers between devices with their start and end apart: 25 -> 25, of which waited for: 10 -> 10; matrix products, arithmetic and copies ran while one was open for 5% -> 5% of each run, Pallas kernels for 27% -> 26%
where the time goes in v16:
time: 97 us; the launch traced here: 96.9 us
  starting transfers between devices  40.3 us (42%)
  Pallas kernels  30.4 us (31%)
  waiting for transfers between devices  19.9 us (21%)
  other arithmetic  3.56 us (4%)
  local copies, waits for them, and re-layouts  2.14 us (2%)
    ppermute x23, starting transfers between devices, tm_permute(): lax.ppermute(value, 'tm', [(i, move(i)) for i in range(devices) if move(i...  40.1 us
    ppermute x23, waiting for transfers between devices, tm_permute(): lax.ppermute(value, 'tm', [(i, move(i)) for i in range(devices) if move(i...  13.2 us
    pallas_call x1, Pallas kernels, full(): pl.pallas_call(partial(full_kernel, owners, final, rows), out_shape=[jax....  7.33 us
    ppermute x1, waiting for transfers between devices, per_device(): other_edge = lax.ppermute(other_edge, ('tm', 'cols'), aslant)  6.73 us
    pallas_call x2, Pallas kernels, attend(): pl.pallas_call(partial(attend_kernel, frames_per, lanes, count, near, chu...  5.61 us
    pallas_call x1, Pallas kernels, early(): pl.pallas_call(partial(early_kernel, final, rows), out_shape=shapes, in_s...  5.03 us
    pallas_call x1, Pallas kernels, late(): pl.pallas_call(partial(late_kernel, owners, final, rows), out_shape=[jax....  3.91 us
    pallas_call x1, Pallas kernels, send(): pl.pallas_call(partial(send_kernel, spans, half), grid=(frames,), out_sha...  3.39 us
  transfers between devices with their start and end apart: 25, of which 10 were waited for; matrix products, arithmetic and copies ran while one was open for 5% of the time, Pallas kernels for 26%

profile of v16, /device:TPU:0, one launch (start us, length us, event | category | flops | bytes accessed | tf_op | source)
XLA Modules:
  0.0 96.9 jit_solution(2994321736936742938)
XLA Ops:
  0.6 3.4 %send.1 = (bf16[3,10,16,512]{3,2,1,0:T(8,128)(2,1)}, bf16[1,10,16,512]{3,2,1,0:T(8,128)(2,1)}, bf16[3,8,16,512]{3,2,1,0:T(8,128)(2,1)}, bf16[1,8,16,512]{3,2,1,0:T(8,128)(2,1)}) custom-call(s32[3]{0:T(128)} %pad_add_fusion.scalars, bf16[4,32,16,512]{3,2,1,0:T(8,128)(2,1)} %video.9), custom_call_target="tpu_custom_call" | custom-call | tf_op jit(solution)/shard_map/send/pallas_call | solution.py:83
  4.0 3.0 %collective-permute-start.1 = (bf16[3,10,16,512]{3,2,1,0:T(8,128)(2,1)}, bf16[3,10,16,512]{3,2,1,0:T(8,128)(2,1)S(1)}, u32[]{:S(2)}, u32[]{:S(2)}) collective-permute-start(bf16[3,10,16,512]{3,2,1,0:T(8,128)(2,1)} %get-tuple-element.47), channel_id=1, source_target_pairs={{0,2},{2,0},{4,6},{6,4},{8,10},{10,8},{12,14},{14,12},{1,3},{3,1},... | collective-permute-start | bytes 1474568 | tf_op jit(solution)/shard_map/ppermute | solution.py:579
  7.0 1.9 %fusion.3 = (bf16[4,32,1,512]{3,2,1,0:T(2,128)(2,1)S(1)}, bf16[4,32,1,512]{3,2,1,0:T(2,128)(2,1)S(1)}) fusion(bf16[4,32,16,512]{3,2,1,0:T(8,128)(2,1)} %video.9), kind=kLoop, calls=%fused_computation.12 | loop fusion | bytes 524288 | tf_op jit(solution)/shard_map/slice | solution.py:583
  9.3 2.0 %collective-permute-start.2 = (bf16[1,10,16,512]{3,2,1,0:T(8,128)(2,1)}, bf16[1,10,16,512]{3,2,1,0:T(8,128)(2,1)S(1)}, u32[]{:S(2)}, u32[]{:S(2)}) collective-permute-start(bf16[1,10,16,512]{3,2,1,0:T(8,128)(2,1)} %get-tuple-element.50), channel_id=1, source_target_pairs={{0,2},{2,0},{4,6},{6,4},{8,10},{10,8},{12,14},{14,12},{1,3},{3,1},... | collective-permute-start | bytes 491528 | tf_op jit(solution)/shard_map/ppermute | solution.py:579
  11.4 2.8 %broadcast_select_fusion.w_space = bf16[9,512,512]{2,1,0:T(8,128)(2,1)S(1)} fusion(bf16[9,512,512]{2,1,0:T(8,128)(2,1)} %param.17, pred[]{:T(512)S(6)} %ge.3), kind=kLoop, calls=%fused_computation | loop fusion | flops 2359296 | bytes 9437185 | tf_op jit(solution)/shard_map/jit(_where)/select_n | solution.py:564
  14.2 6.7 %collective-permute-done.4 = bf16[4,18,512]{2,1,0:T(8,128)(2,1)S(1)} collective-permute-done((bf16[4,18,512]{2,1,0:T(8,128)(2,1)S(1)}, bf16[4,18,512]{2,1,0:T(8,128)(2,1)S(1)}, u32[]{:S(2)}, u32[]{:S(2)}) %collective-permute-start.4) | collective-permute-done | bytes 73760 | tf_op jit(solution)/shard_map/ppermute | solution.py:594
  21.8 1.6 %collective-permute-start.7 = (bf16[3,11,16,512]{3,2,1,0:T(8,128)(2,1)S(1)}, bf16[3,11,16,512]{3,2,1,0:T(8,128)(2,1)S(1)}, u32[]{:S(2)}, u32[]{:S(2)}) collective-permute-start(bf16[3,11,16,512]{3,2,1,0:T(8,128)(2,1)S(1)} %join_last.2.last), channel_id=1, source_target_pairs={{0,4},{2,6},{4,8},{6,10},{8,12},{10,14},{12,0},{14,2},{1,5},{3,7},... | collective-permute-start | bytes 1622024 | tf_op jit(solution)/shard_map/ppermute | solution.py:579
  23.4 1.5 %collective-permute-done.2.others = bf16[1,10,16,512]{3,2,1,0:T(8,128)(2,1)S(1)} collective-permute-done((bf16[1,10,16,512]{3,2,1,0:T(8,128)(2,1)}, bf16[1,10,16,512]{3,2,1,0:T(8,128)(2,1)S(1)}, u32[]{:S(2)}, u32[]{:S(2)}) %collective-permute-start.2) | collective-permute-done | bytes 163872 | tf_op jit(solution)/shard_map/ppermute | solution.py:579
  25.6 5.0 %early.1 = (f32[176,512]{1,0:T(8,128)S(1)}, bf16[2,128,512]{2,1,0:T(8,128)(2,1)S(1)}, bf16[3,2,2,16,512]{4,3,2,1,0:T(8,128)(2,1)S(1)}) custom-call(s32[3]{0:T(128)S(1)} %copy-done.3, bf16[5,11,16,512]{3,2,1,0:T(8,128)(2,1)S(1)} %join_first.2.first, bf16[3,11,16,512]{3,2,1,0:T(8,128)(2,1)S(1)} %join_last.2.last, bf16[1536,512]{1,0:T(8,128)(2,1)S(1)} %bitcast.26, ...), custom_call_target="tpu_custom_call" | custom-call | flops 3607101440 | bytes 9312256 | tf_op jit(solution)/shard_map/early/pallas_call | solution.py:249
  30.6 1.9 %collective-permute-done.received = bf16[3,8,16,512]{3,2,1,0:T(8,128)(2,1)S(1)} collective-permute-done((bf16[3,8,16,512]{3,2,1,0:T(8,128)(2,1)}, bf16[3,8,16,512]{3,2,1,0:T(8,128)(2,1)S(1)}, u32[]{:S(2)}, u32[]{:S(2)}) %collective-permute-start) | collective-permute-done | bytes 393248 | tf_op jit(solution)/shard_map/ppermute | solution.py:579
  33.1 1.9 %collective-permute-start.5 = (bf16[3,9,16,512]{3,2,1,0:T(8,128)(2,1)S(1)}, bf16[3,9,16,512]{3,2,1,0:T(8,128)(2,1)S(1)}, u32[]{:S(2)}, u32[]{:S(2)}) collective-permute-start(bf16[3,9,16,512]{3,2,1,0:T(8,128)(2,1)S(1)} %join_last.3.last), channel_id=1, source_target_pairs={{0,4},{2,6},{4,8},{6,10},{8,12},{10,14},{12,0},{14,2},{1,5},{3,7},... | collective-permute-start | bytes 1327112 | tf_op jit(solution)/shard_map/ppermute | solution.py:579
  34.9 1.5 %collective-permute-start.6 = (bf16[1,8,16,512]{3,2,1,0:T(8,128)(2,1)S(1)}, bf16[1,8,16,512]{3,2,1,0:T(8,128)(2,1)S(1)}, u32[]{:S(2)}, u32[]{:S(2)}) collective-permute-start(bf16[1,8,16,512]{3,2,1,0:T(8,128)(2,1)S(1)} %copy-done.13), channel_id=1, source_target_pairs={{0,2},{2,0},{4,6},{6,4},{8,10},{10,8},{12,14},{14,12},{1,3},{3,1},... | collective-permute-start | bytes 393224 | tf_op jit(solution)/shard_map/ppermute | solution.py:579
  36.4 2.3 %collective-permute-done.7.halo = bf16[3,11,16,512]{3,2,1,0:T(8,128)(2,1)S(1)} collective-permute-done((bf16[3,11,16,512]{3,2,1,0:T(8,128)(2,1)S(1)}, bf16[3,11,16,512]{3,2,1,0:T(8,128)(2,1)S(1)}, u32[]{:S(2)}, u32[]{:S(2)}) %collective-permute-start.7) | collective-permute-done | bytes 540704 | tf_op jit(solution)/shard_map/ppermute | solution.py:579
  38.7 3.9 %late.1 = (bf16[4,32,512]{2,1,0:T(8,128)(2,1)S(1)}, bf16[4,32,512]{2,1,0:T(8,128)(2,1)S(1)}, bf16[4,32,512]{2,1,0:T(8,128)(2,1)S(1)}, bf16[4,32,512]{2,1,0:T(8,128)(2,1)S(1)}, bf16[3,2,2,16,512]{4,3,2,1,0:T(8,128)(2,1)S(1)}) custom-call(s32[3]{0:T(128)S(1)} %copy-done.3, bf16[3,11,16,512]{3,2,1,0:T(8,128)(2,1)S(1)} %collective-permute-done.7.halo, ...), custom_call_target="tpu_custom_call" | custom-call | flops 2407530496 | bytes 9672704 | tf_op jit(solution)/shard_map/late/pallas_call | solution.py:407
  42.8 2.4 %collective-permute-start.9 = (bf16[4,32,512]{2,1,0:T(8,128)(2,1)S(1)}, bf16[4,32,512]{2,1,0:T(8,128)(2,1)S(1)}, u32[]{:S(2)}, u32[]{:S(2)}) collective-permute-start(bf16[4,32,512]{2,1,0:T(8,128)(2,1)S(1)} %get-tuple-element.65), channel_id=1, source_target_pairs={{0,8},{2,10},{4,12},{6,14},{8,0},{10,2},{12,4},{14,6},{1,9},{3,11}... | collective-permute-start | bytes 393224 | tf_op jit(solution)/shard_map/ppermute | solution.py:579
  45.1 2.0 %collective-permute-start.10 = (bf16[4,32,512]{2,1,0:T(8,128)(2,1)S(1)}, bf16[4,32,512]{2,1,0:T(8,128)(2,1)S(1)}, u32[]{:S(2)}, u32[]{:S(2)}) collective-permute-start(bf16[4,32,512]{2,1,0:T(8,128)(2,1)S(1)} %get-tuple-element.66), channel_id=1, source_target_pairs={{0,12},{2,14},{4,8},{6,10},{8,4},{10,6},{12,0},{14,2},{1,13},{3,15... | collective-permute-start | bytes 393224 | tf_op jit(solution)/shard_map/ppermute | solution.py:579
  48.4 7.3 %full.1 = (bf16[4,32,512]{2,1,0:T(8,128)(2,1)S(1)}, bf16[4,32,512]{2,1,0:T(8,128)(2,1)S(1)}, bf16[4,32,512]{2,1,0:T(8,128)(2,1)S(1)}, bf16[4,32,512]{2,1,0:T(8,128)(2,1)S(1)}) custom-call(s32[3]{0:T(128)S(1)} %copy-done.3, bf16[3,9,16,512]{3,2,1,0:T(8,128)(2,1)S(1)} %collective-permute-done.5.halo, bf16[5,9,16,512]{3,2,1,0:T(8,128)(2,1)S(1)} %join_first.3.first, ...), custom_call_target="tpu_custom_call" | custom-call | flops 5360320512 | bytes 9492480 | tf_op jit(solution)/shard_map/full/pallas_call | solution.py:336
  55.8 4.9 %collective-permute-start.12 = (bf16[4,32,512]{2,1,0:T(8,128)(2,1)S(1)}, bf16[4,32,512]{2,1,0:T(8,128)(2,1)S(1)}, u32[]{:S(2)}, u32[]{:S(2)}) collective-permute-start(bf16[4,32,512]{2,1,0:T(8,128)(2,1)S(1)} %get-tuple-element.70), channel_id=1, source_target_pairs={{0,8},{2,10},{4,12},{6,14},{8,0},{10,2},{12,4},{14,6},{1,9},{3,11}... | collective-permute-start | bytes 393224 | tf_op jit(solution)/shard_map/ppermute | solution.py:579
  60.8 2.8 %attend.2 = (bf16[2,32,512]{2,1,0:T(8,128)(2,1)S(1)}, bf16[2,32,512]{2,1,0:T(8,128)(2,1)S(1)}, bf16[2,32,512]{2,1,0:T(8,128)(2,1)S(1)}, bf16[2,32,512]{2,1,0:T(8...) custom-call(s32[3]{0:T(128)S(1)} %copy-done.3, ...), custom_call_target="tpu_custom_call" | custom-call | flops 1342177280 | bytes 2621440 | tf_op jit(solution)/shard_map/attend/pallas_call | solution.py:508
  63.6 1.6 %collective-permute-start.21 = (bf16[2,32,512]{2,1,0:T(8,128)(2,1)S(1)}, bf16[2,32,512]{2,1,0:T(8,128)(2,1)S(1)}, u32[]{:S(2)}, u32[]{:S(2)}) collective-permute-start(bf16[2,32,512]{2,1,0:T(8,128)(2,1)S(1)} %get-tuple-element.83), channel_id=1, source_target_pairs={{0,8},{2,10},{4,12},{6,14},{8,0},{10,2},{12,4},{14,6},{1,9},{3,11}... | collective-permute-start | bytes 196616 | tf_op jit(solution)/shard_map/ppermute | solution.py:579
  65.2 1.8 %collective-permute-start.22 = (bf16[2,32,512]{2,1,0:T(8,128)(2,1)S(1)}, bf16[2,32,512]{2,1,0:T(8,128)(2,1)S(1)}, u32[]{:S(2)}, u32[]{:S(2)}) collective-permute-start(bf16[2,32,512]{2,1,0:T(8,128)(2,1)S(1)} %get-tuple-element.84), channel_id=1, source_target_pairs={{0,10},{2,8},{4,14},{6,12},{8,2},{10,0},{12,6},{14,4},{1,11},{3,9}... | collective-permute-start | bytes 196616 | tf_op jit(solution)/shard_map/ppermute | solution.py:579
  67.0 3.8 %collective-permute-start.23 = (bf16[2,32,512]{2,1,0:T(8,128)(2,1)S(1)}, bf16[2,32,512]{2,1,0:T(8,128)(2,1)S(1)}, u32[]{:S(2)}, u32[]{:S(2)}) collective-permute-start(bf16[2,32,512]{2,1,0:T(8,128)(2,1)S(1)} %get-tuple-element.85), channel_id=1, source_target_pairs={{0,12},{2,14},{4,8},{6,10},{8,4},{10,6},{12,0},{14,2},{1,13},{3,15... | collective-permute-start | bytes 196616 | tf_op jit(solution)/shard_map/ppermute | solution.py:579
  70.8 3.2 %collective-permute-done.12.refs_2_ = bf16[4,32,512]{2,1,0:T(8,128)(2,1)S(1)} collective-permute-done((bf16[4,32,512]{2,1,0:T(8,128)(2,1)S(1)}, bf16[4,32,512]{2,1,0:T(8,128)(2,1)S(1)}, u32[]{:S(2)}, u32[]{:S(2)}) %collective-permute-start.12) | collective-permute-done | bytes 131104 | tf_op jit(solution)/shard_map/ppermute | solution.py:579
  74.0 1.4 %collective-permute-start.24 = (bf16[2,32,512]{2,1,0:T(8,128)(2,1)S(1)}, bf16[2,32,512]{2,1,0:T(8,128)(2,1)S(1)}, u32[]{:S(2)}, u32[]{:S(2)}) collective-permute-start(bf16[2,32,512]{2,1,0:T(8,128)(2,1)S(1)} %get-tuple-element.86), channel_id=1, source_target_pairs={{0,14},{2,12},{4,10},{6,8},{8,6},{10,4},{12,2},{14,0},{1,15},{3,13... | collective-permute-start | bytes 196616 | tf_op jit(solution)/shard_map/ppermute | solution.py:579
  75.4 2.8 %attend.3 = (bf16[2,32,512]{2,1,0:T(8,128)(2,1)S(1)}, bf16[2,2,32,512]{3,2,1,0:T(8,128)(2,1)S(1)}, bf16[2,2,32,512]{3,2,1,0:T(8,128)(2,1)S(1)}, bf16[2,2,32,512]...) custom-call(s32[3]{0:T(128)S(1)} %copy-done.3, ...), custom_call_target="tpu_custom_call" | custom-call | flops 1342177280 | bytes 2621440 | tf_op jit(solution)/shard_map/attend/pallas_call | solution.py:508
  78.2 3.2 %collective-permute-start.14 = (bf16[2,32,512]{2,1,0:T(8,128)(2,1)S(1)}, bf16[2,32,512]{2,1,0:T(8,128)(2,1)S(1)}, u32[]{:S(2)}, u32[]{:S(2)}) collective-permute-start(bf16[2,32,512]{2,1,0:T(8,128)(2,1)S(1)} %get-tuple-element.75), channel_id=1, source_target_pairs={{0,8},{2,10},{4,12},{6,14},{8,0},{10,2},{12,4},{14,6},{1,9},{3,11}... | collective-permute-start | bytes 196616 | tf_op jit(solution)/shard_map/ppermute | solution.py:579
  83.0 1.7 %collective-permute-start.19 = (bf16[2,2,32,512]{3,2,1,0:T(8,128)(2,1)S(1)}, bf16[2,2,32,512]{3,2,1,0:T(8,128)(2,1)S(1)}, u32[]{:S(2)}, u32[]{:S(2)}) collective-permute-start(bf16[2,2,32,512]{3,2,1,0:T(8,128)(2,1)S(1)} %get-tuple-element.80), channel_id=1, source_target_pairs={{0,4},{2,6},{4,0},{6,2},{8,12},{10,14},{12,8},{14,10},{1,5},{3,7},... | collective-permute-start | bytes 393224 | tf_op jit(solution)/shard_map/ppermute | solution.py:579
  84.7 1.7 %collective-permute-start.20 = (bf16[2,2,32,512]{3,2,1,0:T(8,128)(2,1)S(1)}, bf16[2,2,32,512]{3,2,1,0:T(8,128)(2,1)S(1)}, u32[]{:S(2)}, u32[]{:S(2)}) collective-permute-start(bf16[2,2,32,512]{3,2,1,0:T(8,128)(2,1)S(1)} %get-tuple-element.81), channel_id=1, source_target_pairs={{0,6},{2,4},{4,2},{6,0},{8,14},{10,12},{12,10},{14,8},{1,7},{3,5},... | collective-permute-start | bytes 393224 | tf_op jit(solution)/shard_map/ppermute | solution.py:579
  88.2 3.1 %collective-permute-start.17 = (bf16[2,32,512]{2,1,0:T(8,128)(2,1)S(1)}, bf16[2,32,512]{2,1,0:T(8,128)(2,1)S(1)}, u32[]{:S(2)}, u32[]{:S(2)}) collective-permute-start(bf16[2,32,512]{2,1,0:T(8,128)(2,1)S(1)} %get-tuple-element.78), channel_id=1, source_target_pairs={{0,14},{2,12},{4,10},{6,8},{8,6},{10,4},{12,2},{14,0},{1,15},{3,13... | collective-permute-start | bytes 196616 | tf_op jit(solution)/shard_map/ppermute | solution.py:579
  91.3 1.3 %collect.2.refs_8_ = bf16[2,16,32,512]{3,2,1,0:T(8,128)(2,1)} custom-call(s32[3]{0:T(128)S(1)} %copy-done.3, bf16[2,32,512]{2,1,0:T(8,128)(2,1)S(1)} %collective-permute-done.21.refs_0_, bf16[2,32,512]{2,1,0:T(8,128)(2,1)S(1)} %collective-permute-done.22.refs_1_, bf16[2,32,512]{2,1,0:T(8,128)(2,1)S(1)} %collective-permute-done.23.refs_2_, ...), custom_call_target="tpu_custom_call" | custom-call | tf_op jit(solution)/shard_map/collect/pallas_call | solution.py:534
  93.5 1.7 %collective-permute-done.17.refs_3_ = bf16[2,32,512]{2,1,0:T(8,128)(2,1)S(1)} collective-permute-done((bf16[2,32,512]{2,1,0:T(8,128)(2,1)S(1)}, bf16[2,32,512]{2,1,0:T(8,128)(2,1)S(1)}, u32[]{:S(2)}, u32[]{:S(2)}) %collective-permute-start.17) | collective-permute-done | bytes 65568 | tf_op jit(solution)/shard_map/ppermute | solution.py:579
  95.2 1.5 %collect.3 = bf16[2,16,32,512]{3,2,1,0:T(8,128)(2,1)} custom-call(s32[3]{0:T(128)S(1)} %copy-done.3, bf16[2,32,512]{2,1,0:T(8,128)(2,1)S(1)} %collective-permute-done.14.refs_0_, bf16[2,32,512]{2,1,0:T(8,128)(2,1)S(1)} %collective-permute-done.15.refs_1_, bf16[2,32,512]{2,1,0:T(8,128)(2,1)S(1)} %collective-permute-done.16.refs_2_, ...), custom_call_target="tpu_custom_call", output_to_operand_aliasing={{}: (9, {})} | custom-call | tf_op jit(solution)/shard_map/collect/pallas_call | solution.py:534
  (68 shorter events, 8.6 us)
Async XLA Ops:
  4.0 17.1 %collective-permute-start.1 = (bf16[3,10,16,512]{3,2,1,0:T(8,128)(2,1)}, bf16[3,10,16,512]{3,2,1,0:T(8,128)(2,1)S(1)}, u32[]{:S(2)}, u32[]{:S(2)}) collective-permute-start(bf16[3,10,16,512]{3,2,1,0:T(8,128)(2,1)} %get-tuple-element.47), channel_id=1, source_target_pairs={{0,2},{2,0},{4,6},{6,4},{8,10},{10,8},{12,14},{14,12},{1,3},{3,1},... | collective-permute-start | bytes 1474568 | tf_op jit(solution)/shard_map/ppermute | solution.py:579
  9.1 11.8 %collective-permute-start.4 = (bf16[4,18,512]{2,1,0:T(8,128)(2,1)S(1)}, bf16[4,18,512]{2,1,0:T(8,128)(2,1)S(1)}, u32[]{:S(2)}, u32[]{:S(2)}) collective-permute-start(bf16[4,18,512]{2,1,0:T(8,128)(2,1)S(1)} %get-tuple-element.89), channel_id=1, source_target_pairs={{0,3},{1,2},{2,1},{3,0},{4,7},{5,6},{6,5},{7,4},{8,11},{9,10},{10,... | collective-permute-start | bytes 221192 | tf_op jit(solution)/shard_map/ppermute | solution.py:594
  9.2 11.8 %collective-permute-start.3 = (bf16[4,18,512]{2,1,0:T(8,128)(2,1)S(1)}, bf16[4,18,512]{2,1,0:T(8,128)(2,1)S(1)}, u32[]{:S(2)}, u32[]{:S(2)}) collective-permute-start(bf16[4,18,512]{2,1,0:T(8,128)(2,1)S(1)} %get-tuple-element.90), channel_id=1, source_target_pairs={{0,1},{1,0},{2,3},{3,2},{4,5},{5,4},{6,7},{7,6},{8,9},{9,8},{10,11... | collective-permute-start | bytes 221192 | tf_op jit(solution)/shard_map/ppermute | solution.py:588
  9.3 15.6 %collective-permute-start.2 = (bf16[1,10,16,512]{3,2,1,0:T(8,128)(2,1)}, bf16[1,10,16,512]{3,2,1,0:T(8,128)(2,1)S(1)}, u32[]{:S(2)}, u32[]{:S(2)}) collective-permute-start(bf16[1,10,16,512]{3,2,1,0:T(8,128)(2,1)} %get-tuple-element.50), channel_id=1, source_target_pairs={{0,2},{2,0},{4,6},{6,4},{8,10},{10,8},{12,14},{14,12},{1,3},{3,1},... | collective-permute-start | bytes 491528 | tf_op jit(solution)/shard_map/ppermute | solution.py:579
  11.3 21.2 %collective-permute-start = (bf16[3,8,16,512]{3,2,1,0:T(8,128)(2,1)}, bf16[3,8,16,512]{3,2,1,0:T(8,128)(2,1)S(1)}, u32[]{:S(2)}, u32[]{:S(2)}) collective-permute-start(bf16[3,8,16,512]{3,2,1,0:T(8,128)(2,1)} %get-tuple-element.46), channel_id=1, source_target_pairs={{0,2},{2,0},{4,6},{6,4},{8,10},{10,8},{12,14},{14,12},{1,3},{3,1},... | collective-permute-start | bytes 1179656 | tf_op jit(solution)/shard_map/ppermute | solution.py:579
  14.2 11.3 %copy-start.1 = (bf16[3,512,512]{2,1,0:T(8,128)(2,1)S(1)}, bf16[3,512,512]{2,1,0:T(8,128)(2,1)}, u32[]{:S(2)}) copy-start(bf16[3,512,512]{2,1,0:T(8,128)(2,1)} %param.13) | copy-start | bytes 4718596
  14.2 11.3 %copy-start.2 = (bf16[3,512,512]{2,1,0:T(8,128)(2,1)S(1)}, bf16[3,512,512]{2,1,0:T(8,128)(2,1)}, u32[]{:S(2)}) copy-start(bf16[3,512,512]{2,1,0:T(8,128)(2,1)} %param.15) | copy-start | bytes 4718596
  21.8 17.0 %collective-permute-start.7 = (bf16[3,11,16,512]{3,2,1,0:T(8,128)(2,1)S(1)}, bf16[3,11,16,512]{3,2,1,0:T(8,128)(2,1)S(1)}, u32[]{:S(2)}, u32[]{:S(2)}) collective-permute-start(bf16[3,11,16,512]{3,2,1,0:T(8,128)(2,1)S(1)} %join_last.2.last), channel_id=1, source_target_pairs={{0,4},{2,6},{4,8},{6,10},{8,12},{10,14},{12,0},{14,2},{1,5},{3,7},... | collective-permute-start | bytes 1622024 | tf_op jit(solution)/shard_map/ppermute | solution.py:579
  33.1 15.3 %collective-permute-start.5 = (bf16[3,9,16,512]{3,2,1,0:T(8,128)(2,1)S(1)}, bf16[3,9,16,512]{3,2,1,0:T(8,128)(2,1)S(1)}, u32[]{:S(2)}, u32[]{:S(2)}) collective-permute-start(bf16[3,9,16,512]{3,2,1,0:T(8,128)(2,1)S(1)} %join_last.3.last), channel_id=1, source_target_pairs={{0,4},{2,6},{4,8},{6,10},{8,12},{10,14},{12,0},{14,2},{1,5},{3,7},... | collective-permute-start | bytes 1327112 | tf_op jit(solution)/shard_map/ppermute | solution.py:579
  34.9 7.7 %collective-permute-start.6 = (bf16[1,8,16,512]{3,2,1,0:T(8,128)(2,1)S(1)}, bf16[1,8,16,512]{3,2,1,0:T(8,128)(2,1)S(1)}, u32[]{:S(2)}, u32[]{:S(2)}) collective-permute-start(bf16[1,8,16,512]{3,2,1,0:T(8,128)(2,1)S(1)} %copy-done.13), channel_id=1, source_target_pairs={{0,2},{2,0},{4,6},{6,4},{8,10},{10,8},{12,14},{14,12},{1,3},{3,1},... | collective-permute-start | bytes 393224 | tf_op jit(solution)/shard_map/ppermute | solution.py:579
  42.7 18.0 %collective-permute-start.8 = (bf16[4,32,512]{2,1,0:T(8,128)(2,1)S(1)}, bf16[4,32,512]{2,1,0:T(8,128)(2,1)S(1)}, u32[]{:S(2)}, u32[]{:S(2)}) collective-permute-start(bf16[4,32,512]{2,1,0:T(8,128)(2,1)S(1)} %get-tuple-element.64), channel_id=1, source_target_pairs={{0,4},{2,6},{4,0},{6,2},{8,12},{10,14},{12,8},{14,10},{1,5},{3,7},... | collective-permute-start | bytes 393224 | tf_op jit(solution)/shard_map/ppermute | solution.py:579
  42.8 17.9 %collective-permute-start.9 = (bf16[4,32,512]{2,1,0:T(8,128)(2,1)S(1)}, bf16[4,32,512]{2,1,0:T(8,128)(2,1)S(1)}, u32[]{:S(2)}, u32[]{:S(2)}) collective-permute-start(bf16[4,32,512]{2,1,0:T(8,128)(2,1)S(1)} %get-tuple-element.65), channel_id=1, source_target_pairs={{0,8},{2,10},{4,12},{6,14},{8,0},{10,2},{12,4},{14,6},{1,9},{3,11}... | collective-permute-start | bytes 393224 | tf_op jit(solution)/shard_map/ppermute | solution.py:579
  45.1 15.6 %collective-permute-start.10 = (bf16[4,32,512]{2,1,0:T(8,128)(2,1)S(1)}, bf16[4,32,512]{2,1,0:T(8,128)(2,1)S(1)}, u32[]{:S(2)}, u32[]{:S(2)}) collective-permute-start(bf16[4,32,512]{2,1,0:T(8,128)(2,1)S(1)} %get-tuple-element.66), channel_id=1, source_target_pairs={{0,12},{2,14},{4,8},{6,10},{8,4},{10,6},{12,0},{14,2},{1,13},{3,15... | collective-permute-start | bytes 393224 | tf_op jit(solution)/shard_map/ppermute | solution.py:579
  48.4 12.4 %copy-start.7 = (bf16[512,512]{1,0:T(8,128)(2,1)S(1)}, bf16[512,512]{1,0:T(8,128)(2,1)}, u32[]{:S(2)}) copy-start(bf16[512,512]{1,0:T(8,128)(2,1)} %refs_5_.3) | copy-start | bytes 1572868
  48.4 12.4 %copy-start.8 = (bf16[512,512]{1,0:T(8,128)(2,1)S(1)}, bf16[512,512]{1,0:T(8,128)(2,1)}, u32[]{:S(2)}) copy-start(bf16[512,512]{1,0:T(8,128)(2,1)} %refs_6_.3) | copy-start | bytes 1572868
  48.4 12.4 %copy-start.9 = (bf16[512,512]{1,0:T(8,128)(2,1)S(1)}, bf16[512,512]{1,0:T(8,128)(2,1)}, u32[]{:S(2)}) copy-start(bf16[512,512]{1,0:T(8,128)(2,1)} %refs_7_.3) | copy-start | bytes 1572868
  48.4 12.4 %copy-start.10 = (bf16[512,512]{1,0:T(8,128)(2,1)S(1)}, bf16[512,512]{1,0:T(8,128)(2,1)}, u32[]{:S(2)}) copy-start(bf16[512,512]{1,0:T(8,128)(2,1)} %refs_8_.3) | copy-start | bytes 1572868
  48.4 12.4 %copy-start.11 = (f32[512]{0:T(512)S(1)}, f32[512]{0:T(512)}, u32[]{:S(2)}) copy-start(f32[512]{0:T(512)} %param.19) | copy-start | bytes 6148
  55.7 11.3 %collective-permute-start.11 = (bf16[4,32,512]{2,1,0:T(8,128)(2,1)S(1)}, bf16[4,32,512]{2,1,0:T(8,128)(2,1)S(1)}, u32[]{:S(2)}, u32[]{:S(2)}) collective-permute-start(bf16[4,32,512]{2,1,0:T(8,128)(2,1)S(1)} %get-tuple-element.69), channel_id=1, source_target_pairs={{0,4},{2,6},{4,0},{6,2},{8,12},{10,14},{12,8},{14,10},{1,5},{3,7},... | collective-permute-start | bytes 393224 | tf_op jit(solution)/shard_map/ppermute | solution.py:579
  55.8 18.2 %collective-permute-start.12 = (bf16[4,32,512]{2,1,0:T(8,128)(2,1)S(1)}, bf16[4,32,512]{2,1,0:T(8,128)(2,1)S(1)}, u32[]{:S(2)}, u32[]{:S(2)}) collective-permute-start(bf16[4,32,512]{2,1,0:T(8,128)(2,1)S(1)} %get-tuple-element.70), channel_id=1, source_target_pairs={{0,8},{2,10},{4,12},{6,14},{8,0},{10,2},{12,4},{14,6},{1,9},{3,11}... | collective-permute-start | bytes 393224 | tf_op jit(solution)/shard_map/ppermute | solution.py:579
  60.7 14.7 %collective-permute-start.13 = (bf16[4,32,512]{2,1,0:T(8,128)(2,1)S(1)}, bf16[4,32,512]{2,1,0:T(8,128)(2,1)S(1)}, u32[]{:S(2)}, u32[]{:S(2)}) collective-permute-start(bf16[4,32,512]{2,1,0:T(8,128)(2,1)S(1)} %get-tuple-element.71), channel_id=1, source_target_pairs={{0,12},{2,14},{4,8},{6,10},{8,4},{10,6},{12,0},{14,2},{1,13},{3,15... | collective-permute-start | bytes 393224 | tf_op jit(solution)/shard_map/ppermute | solution.py:579
  63.6 17.8 %collective-permute-start.21 = (bf16[2,32,512]{2,1,0:T(8,128)(2,1)S(1)}, bf16[2,32,512]{2,1,0:T(8,128)(2,1)S(1)}, u32[]{:S(2)}, u32[]{:S(2)}) collective-permute-start(bf16[2,32,512]{2,1,0:T(8,128)(2,1)S(1)} %get-tuple-element.83), channel_id=1, source_target_pairs={{0,8},{2,10},{4,12},{6,14},{8,0},{10,2},{12,4},{14,6},{1,9},{3,11}... | collective-permute-start | bytes 196616 | tf_op jit(solution)/shard_map/ppermute | solution.py:579
  65.2 17.4 %collective-permute-start.22 = (bf16[2,32,512]{2,1,0:T(8,128)(2,1)S(1)}, bf16[2,32,512]{2,1,0:T(8,128)(2,1)S(1)}, u32[]{:S(2)}, u32[]{:S(2)}) collective-permute-start(bf16[2,32,512]{2,1,0:T(8,128)(2,1)S(1)} %get-tuple-element.84), channel_id=1, source_target_pairs={{0,10},{2,8},{4,14},{6,12},{8,2},{10,0},{12,6},{14,4},{1,11},{3,9}... | collective-permute-start | bytes 196616 | tf_op jit(solution)/shard_map/ppermute | solution.py:579
  67.0 16.0 %collective-permute-start.23 = (bf16[2,32,512]{2,1,0:T(8,128)(2,1)S(1)}, bf16[2,32,512]{2,1,0:T(8,128)(2,1)S(1)}, u32[]{:S(2)}, u32[]{:S(2)}) collective-permute-start(bf16[2,32,512]{2,1,0:T(8,128)(2,1)S(1)} %get-tuple-element.85), channel_id=1, source_target_pairs={{0,12},{2,14},{4,8},{6,10},{8,4},{10,6},{12,0},{14,2},{1,13},{3,15... | collective-permute-start | bytes 196616 | tf_op jit(solution)/shard_map/ppermute | solution.py:579
  74.0 10.7 %collective-permute-start.24 = (bf16[2,32,512]{2,1,0:T(8,128)(2,1)S(1)}, bf16[2,32,512]{2,1,0:T(8,128)(2,1)S(1)}, u32[]{:S(2)}, u32[]{:S(2)}) collective-permute-start(bf16[2,32,512]{2,1,0:T(8,128)(2,1)S(1)} %get-tuple-element.86), channel_id=1, source_target_pairs={{0,14},{2,12},{4,10},{6,8},{8,6},{10,4},{12,2},{14,0},{1,15},{3,13... | collective-permute-start | bytes 196616 | tf_op jit(solution)/shard_map/ppermute | solution.py:579
  78.2 9.2 %collective-permute-start.14 = (bf16[2,32,512]{2,1,0:T(8,128)(2,1)S(1)}, bf16[2,32,512]{2,1,0:T(8,128)(2,1)S(1)}, u32[]{:S(2)}, u32[]{:S(2)}) collective-permute-start(bf16[2,32,512]{2,1,0:T(8,128)(2,1)S(1)} %get-tuple-element.75), channel_id=1, source_target_pairs={{0,8},{2,10},{4,12},{6,14},{8,0},{10,2},{12,4},{14,6},{1,9},{3,11}... | collective-permute-start | bytes 196616 | tf_op jit(solution)/shard_map/ppermute | solution.py:579
  81.4 6.8 %collective-permute-start.15 = (bf16[2,32,512]{2,1,0:T(8,128)(2,1)S(1)}, bf16[2,32,512]{2,1,0:T(8,128)(2,1)S(1)}, u32[]{:S(2)}, u32[]{:S(2)}) collective-permute-start(bf16[2,32,512]{2,1,0:T(8,128)(2,1)S(1)} %get-tuple-element.76), channel_id=1, source_target_pairs={{0,10},{2,8},{4,14},{6,12},{8,2},{10,0},{12,6},{14,4},{1,11},{3,9}... | collective-permute-start | bytes 196616 | tf_op jit(solution)/shard_map/ppermute | solution.py:579
  82.6 12.6 %collective-permute-start.18 = (bf16[2,2,32,512]{3,2,1,0:T(8,128)(2,1)S(1)}, bf16[2,2,32,512]{3,2,1,0:T(8,128)(2,1)S(1)}, u32[]{:S(2)}, u32[]{:S(2)}) collective-permute-start(bf16[2,2,32,512]{3,2,1,0:T(8,128)(2,1)S(1)} %get-tuple-element.79), channel_id=1, source_target_pairs={{0,2},{2,0},{4,6},{6,4},{8,10},{10,8},{12,14},{14,12},{1,3},{3,1},... | collective-permute-start | bytes 393224 | tf_op jit(solution)/shard_map/ppermute | solution.py:579
  83.0 12.2 %collective-permute-start.19 = (bf16[2,2,32,512]{3,2,1,0:T(8,128)(2,1)S(1)}, bf16[2,2,32,512]{3,2,1,0:T(8,128)(2,1)S(1)}, u32[]{:S(2)}, u32[]{:S(2)}) collective-permute-start(bf16[2,2,32,512]{3,2,1,0:T(8,128)(2,1)S(1)} %get-tuple-element.80), channel_id=1, source_target_pairs={{0,4},{2,6},{4,0},{6,2},{8,12},{10,14},{12,8},{14,10},{1,5},{3,7},... | collective-permute-start | bytes 393224 | tf_op jit(solution)/shard_map/ppermute | solution.py:579
  84.7 10.5 %collective-permute-start.20 = (bf16[2,2,32,512]{3,2,1,0:T(8,128)(2,1)S(1)}, bf16[2,2,32,512]{3,2,1,0:T(8,128)(2,1)S(1)}, u32[]{:S(2)}, u32[]{:S(2)}) collective-permute-start(bf16[2,2,32,512]{3,2,1,0:T(8,128)(2,1)S(1)} %get-tuple-element.81), channel_id=1, source_target_pairs={{0,6},{2,4},{4,2},{6,0},{8,14},{10,12},{12,10},{14,8},{1,7},{3,5},... | collective-permute-start | bytes 393224 | tf_op jit(solution)/shard_map/ppermute | solution.py:579
  87.4 6.2 %collective-permute-start.16 = (bf16[2,32,512]{2,1,0:T(8,128)(2,1)S(1)}, bf16[2,32,512]{2,1,0:T(8,128)(2,1)S(1)}, u32[]{:S(2)}, u32[]{:S(2)}) collective-permute-start(bf16[2,32,512]{2,1,0:T(8,128)(2,1)S(1)} %get-tuple-element.77), channel_id=1, source_target_pairs={{0,12},{2,14},{4,8},{6,10},{8,4},{10,6},{12,0},{14,2},{1,13},{3,15... | collective-permute-start | bytes 196616 | tf_op jit(solution)/shard_map/ppermute | solution.py:579
  88.2 7.0 %collective-permute-start.17 = (bf16[2,32,512]{2,1,0:T(8,128)(2,1)S(1)}, bf16[2,32,512]{2,1,0:T(8,128)(2,1)S(1)}, u32[]{:S(2)}, u32[]{:S(2)}) collective-permute-start(bf16[2,32,512]{2,1,0:T(8,128)(2,1)S(1)} %get-tuple-element.78), channel_id=1, source_target_pairs={{0,14},{2,12},{4,10},{6,8},{8,6},{10,4},{12,2},{14,0},{1,15},{3,13... | collective-permute-start | bytes 196616 | tf_op jit(solution)/shard_map/ppermute | solution.py:579
  (7 other events, 72.6 us)

commit v17 on v15

--- a/solution.py
+++ b/solution.py
@@ -410,7 +410,8 @@
     )(scalars, halo, first, part, spatial, *weights)
 
 
-def attend_kernel(frames_per, lanes, count, near, chunks, scalars, *refs):
+def attend_kernel(frames_per, lanes, turns, near, chunks, scalars, *refs):
+    count = len(turns)
     blocks, refs = refs[:count], refs[count:]
     gain, w_query, w_key, w_value, w_out = refs[:5]
     waiting, outs = refs[5 : 5 + near * (chunks - 1)], refs[5 + near * (chunks - 1) :]
@@ -431,7 +432,7 @@
         block = index // each
         time = index // lanes % frames_per
         for j in range(count):
-            level = 0 if flat else scalars[2] ^ j
+            level = 0 if flat else scalars[2] ^ turns[j]
             time = time + jnp.where(block == j, level * frames_per, 0)
         return time, index % lanes
 
@@ -472,14 +473,14 @@
                 def _():
                     part = slice(g * lanes, (g + 1) * lanes)
                     for x in range(pair):
-                        m = pair * j + x
+                        m = pair * turns[j] + x
                         if 0 < m <= near:
                             outs[m][chunks - 1, :, part] = rows[side ^ x]
                         else:
                             outs[m][:, part] = rows[side ^ x]
 
 
-def attend(scalars, blocks, near, waiting, gain, w_query, w_key, w_value, w_out):
+def attend(scalars, blocks, turns, near, waiting, gain, w_query, w_key, w_value, w_out):
     frames_per, pixels, channels = blocks[0].shape
     flat = pixels % 16 != 0
     lanes = pixels if flat else 16
@@ -496,7 +497,7 @@
         shapes = [blocks[0].shape]
     flops = 2 * frames_per * pixels * count * channels * (4 * channels + 2 * size)
     outs = pl.pallas_call(
-        partial(attend_kernel, frames_per, lanes, count, near, chunks),
+        partial(attend_kernel, frames_per, lanes, turns, near, chunks),
         out_shape=[jax.ShapeDtypeStruct(shape, jnp.bfloat16) for shape in shapes],
         in_specs=[SMEM] + [VMEM] * (count + 5 + len(waiting)),
         out_specs=[VMEM] * len(shapes),
@@ -643,8 +644,12 @@
         for k, gathered in enumerate(gathers):
             gathered[0] = after(gathered[0], newest)
             final = k == chunks - 1
+            turns = tuple(range(levels))
+            if final:
+                turns = turns[levels // 2 :] + turns[: levels // 2][::-1]
             results = attend(
-                scalars, gathered, near if final else 0, waiting if final else [], *attention
+                scalars, [gathered[j] for j in turns], turns, near if final else 0,
+                waiting if final else [], *attention
             )
             newest = results[0]
             blocks = [tm_permute(results[m], lambda i: i ^ m) for m in range(far, devices)]
@@ -663,7 +668,7 @@
     returns = []
     for (block,) in spatials:
         gathered = lax.all_to_all(block, "tm", 1, 0, axis_index_groups=sets, tiled=True)
-        (result,) = attend(scalars, [gathered], 0, [], *attention)
+        (result,) = attend(scalars, [gathered], (0,), 0, [], *attention)
         result = lax.all_to_all(result, "tm", 0, 1, tiled=True)
         result = result.reshape(frames // 2, levels, pair, each, channels)
         returns.append(result.transpose(0, 2, 1, 3, 4).reshape(frames // 2, pair, -1, channels))

time: 95.1 us -> 95 us (level)
  starting transfers between devices: 40.3 us -> 43.5 us
  waiting for transfers between devices: 19.7 us -> 16.5 us
    ppermute x23, waiting for transfers between devices: 13.2 us -> 9.94 us  [tm_permute(): lax.ppermute(value, 'tm', [(i, move(i)) for i in range(devices) if move(i...]
    ppermute x23, starting transfers between devices: 40.1 us -> 43.3 us  [tm_permute(): lax.ppermute(value, 'tm', [(i, move(i)) for i in range(devices) if move(i...]
  transfers between devices with their start and end apart: 25 -> 25, of which waited for: 10 -> 8; matrix products, arithmetic and copies ran while one was open for 5% -> 5% of each run, Pallas kernels for 27% -> 27%
where the time goes in v17:
time: 95 us; the launch traced here: 94.8 us
  starting transfers between devices  43.5 us (46%)
  Pallas kernels  27.6 us (29%)
  waiting for transfers between devices  16.5 us (17%)
  local copies, waits for them, and re-layouts  3.73 us (4%)
  other arithmetic  2.99 us (3%)
    ppermute x23, starting transfers between devices, tm_permute(): lax.ppermute(value, 'tm', [(i, move(i)) for i in range(devices) if move(i...  43.3 us
    ppermute x23, waiting for transfers between devices, tm_permute(): lax.ppermute(value, 'tm', [(i, move(i)) for i in range(devices) if move(i...  9.94 us
    pallas_call x1, Pallas kernels, full(): pl.pallas_call(partial(full_kernel, owners, final, rows), out_shape=[jax....  7.33 us
    ppermute x1, waiting for transfers between devices, per_device(): other_edge = lax.ppermute(other_edge, ('tm', 'cols'), aslant)  6.52 us
    pallas_call x2, Pallas kernels, attend(): pl.pallas_call(partial(attend_kernel, frames_per, lanes, turns, near, chu...  5.6 us
    pallas_call x1, Pallas kernels, early(): pl.pallas_call(partial(early_kernel, final, rows), out_shape=shapes, in_s...  5.03 us
    pallas_call x1, Pallas kernels, late(): pl.pallas_call(partial(late_kernel, owners, final, rows), out_shape=[jax....  3.91 us
    select_n x1, other arithmetic, per_device(): w_space = jnp.where(after(place, video) >= 0, w_space, 0)  2.79 us
  transfers between devices with their start and end apart: 25, of which 8 were waited for; matrix products, arithmetic and copies ran while one was open for 5% of the time, Pallas kernels for 27%

profile of v17, /device:TPU:0, one launch (start us, length us, event | category | flops | bytes accessed | tf_op | source)
XLA Modules:
  0.0 94.8 jit_solution(4615385363198233197)
XLA Ops:
  0.1 1.6 %copy-done = bf16[4,32,16,512]{3,2,1,0:T(8,128)(2,1)S(1)} copy-done((bf16[4,32,16,512]{3,2,1,0:T(8,128)(2,1)S(1)}, bf16[4,32,16,512]{3,2,1,0:T(8,128)(2,1)}, u32[]{:S(2)}) %copy-start) | copy-done | bytes 2097176
  2.3 3.0 %collective-permute-start.1 = (bf16[3,10,16,512]{3,2,1,0:T(8,128)(2,1)S(1)}, bf16[3,10,16,512]{3,2,1,0:T(8,128)(2,1)S(1)}, u32[]{:S(2)}, u32[]{:S(2)}) collective-permute-start(bf16[3,10,16,512]{3,2,1,0:T(8,128)(2,1)S(1)} %get-tuple-element.47), channel_id=1, source_target_pairs={{0,2},{2,0},{4,6},{6,4},{8,10},{10,8},{12,14},{14,12},{1,3},{3,1},... | collective-permute-start | bytes 1474568 | tf_op jit(solution)/shard_map/ppermute | solution.py:570
  5.3 1.9 %fusion.3 = (bf16[4,32,1,512]{3,2,1,0:T(2,128)(2,1)S(1)}, bf16[4,32,1,512]{3,2,1,0:T(2,128)(2,1)S(1)}) fusion(bf16[4,32,16,512]{3,2,1,0:T(8,128)(2,1)} %video.9), kind=kLoop, calls=%fused_computation.12 | loop fusion | bytes 524288 | tf_op jit(solution)/shard_map/slice | solution.py:574
  7.6 2.0 %collective-permute-start.2 = (bf16[1,10,16,512]{3,2,1,0:T(8,128)(2,1)S(1)}, bf16[1,10,16,512]{3,2,1,0:T(8,128)(2,1)S(1)}, u32[]{:S(2)}, u32[]{:S(2)}) collective-permute-start(bf16[1,10,16,512]{3,2,1,0:T(8,128)(2,1)S(1)} %get-tuple-element.50), channel_id=1, source_target_pairs={{0,2},{2,0},{4,6},{6,4},{8,10},{10,8},{12,14},{14,12},{1,3},{3,1},... | collective-permute-start | bytes 491528 | tf_op jit(solution)/shard_map/ppermute | solution.py:570
  9.7 2.8 %broadcast_select_fusion.w_space = bf16[9,512,512]{2,1,0:T(8,128)(2,1)S(1)} fusion(bf16[9,512,512]{2,1,0:T(8,128)(2,1)} %param.17, pred[]{:T(512)S(6)} %ge.3), kind=kLoop, calls=%fused_computation | loop fusion | flops 2359296 | bytes 9437185 | tf_op jit(solution)/shard_map/jit(_where)/select_n | solution.py:555
  12.5 6.5 %collective-permute-done.4 = bf16[4,18,512]{2,1,0:T(8,128)(2,1)S(1)} collective-permute-done((bf16[4,18,512]{2,1,0:T(8,128)(2,1)S(1)}, bf16[4,18,512]{2,1,0:T(8,128)(2,1)S(1)}, u32[]{:S(2)}, u32[]{:S(2)}) %collective-permute-start.4) | collective-permute-done | bytes 73760 | tf_op jit(solution)/shard_map/ppermute | solution.py:585
  19.9 1.6 %collective-permute-start.7 = (bf16[3,11,16,512]{3,2,1,0:T(8,128)(2,1)S(1)}, bf16[3,11,16,512]{3,2,1,0:T(8,128)(2,1)S(1)}, u32[]{:S(2)}, u32[]{:S(2)}) collective-permute-start(bf16[3,11,16,512]{3,2,1,0:T(8,128)(2,1)S(1)} %join_last.2.last), channel_id=1, source_target_pairs={{0,4},{2,6},{4,8},{6,10},{8,12},{10,14},{12,0},{14,2},{1,5},{3,7},... | collective-permute-start | bytes 1622024 | tf_op jit(solution)/shard_map/ppermute | solution.py:570
  21.5 1.5 %collective-permute-done.2.others = bf16[1,10,16,512]{3,2,1,0:T(8,128)(2,1)S(1)} collective-permute-done((bf16[1,10,16,512]{3,2,1,0:T(8,128)(2,1)S(1)}, bf16[1,10,16,512]{3,2,1,0:T(8,128)(2,1)S(1)}, u32[]{:S(2)}, u32[]{:S(2)}) %collective-permute-start.2) | collective-permute-done | bytes 163872 | tf_op jit(solution)/shard_map/ppermute | solution.py:570
  23.7 5.0 %early.1 = (f32[176,512]{1,0:T(8,128)S(1)}, bf16[2,128,512]{2,1,0:T(8,128)(2,1)S(1)}, bf16[3,2,2,16,512]{4,3,2,1,0:T(8,128)(2,1)S(1)}) custom-call(s32[3]{0:T(128)S(1)} %pad_add_fusion.scalars, bf16[5,11,16,512]{3,2,1,0:T(8,128)(2,1)S(1)} %join_first.2.first, bf16[3,11,16,512]{3,2,1,0:T(8,128)(2,1)S(1)} %join_last.2.last, bf16[1536,512]{1,0:T(8,128)(2,1)S(1)} %bitcast.26, ...), custom_call_target="tpu_custom_call" | custom-call | flops 3607101440 | bytes 9312256 | tf_op jit(solution)/shard_map/early/pallas_call | solution.py:239
  28.7 1.9 %collective-permute-done.received = bf16[3,8,16,512]{3,2,1,0:T(8,128)(2,1)S(1)} collective-permute-done((bf16[3,8,16,512]{3,2,1,0:T(8,128)(2,1)S(1)}, bf16[3,8,16,512]{3,2,1,0:T(8,128)(2,1)S(1)}, u32[]{:S(2)}, u32[]{:S(2)}) %collective-permute-start) | collective-permute-done | bytes 393248 | tf_op jit(solution)/shard_map/ppermute | solution.py:570
  31.2 1.8 %collective-permute-start.5 = (bf16[3,9,16,512]{3,2,1,0:T(8,128)(2,1)S(1)}, bf16[3,9,16,512]{3,2,1,0:T(8,128)(2,1)S(1)}, u32[]{:S(2)}, u32[]{:S(2)}) collective-permute-start(bf16[3,9,16,512]{3,2,1,0:T(8,128)(2,1)S(1)} %join_last.3.last), channel_id=1, source_target_pairs={{0,4},{2,6},{4,8},{6,10},{8,12},{10,14},{12,0},{14,2},{1,5},{3,7},... | collective-permute-start | bytes 1327112 | tf_op jit(solution)/shard_map/ppermute | solution.py:570
  33.0 1.5 %collective-permute-start.6 = (bf16[1,8,16,512]{3,2,1,0:T(8,128)(2,1)S(1)}, bf16[1,8,16,512]{3,2,1,0:T(8,128)(2,1)S(1)}, u32[]{:S(2)}, u32[]{:S(2)}) collective-permute-start(bf16[1,8,16,512]{3,2,1,0:T(8,128)(2,1)S(1)} %get-tuple-element.55), channel_id=1, source_target_pairs={{0,2},{2,0},{4,6},{6,4},{8,10},{10,8},{12,14},{14,12},{1,3},{3,1},... | collective-permute-start | bytes 393224 | tf_op jit(solution)/shard_map/ppermute | solution.py:570
  34.6 2.3 %collective-permute-done.7.halo = bf16[3,11,16,512]{3,2,1,0:T(8,128)(2,1)S(1)} collective-permute-done((bf16[3,11,16,512]{3,2,1,0:T(8,128)(2,1)S(1)}, bf16[3,11,16,512]{3,2,1,0:T(8,128)(2,1)S(1)}, u32[]{:S(2)}, u32[]{:S(2)}) %collective-permute-start.7) | collective-permute-done | bytes 540704 | tf_op jit(solution)/shard_map/ppermute | solution.py:570
  36.9 3.9 %late.1 = (bf16[4,32,512]{2,1,0:T(8,128)(2,1)S(1)}, bf16[4,32,512]{2,1,0:T(8,128)(2,1)S(1)}, bf16[4,32,512]{2,1,0:T(8,128)(2,1)S(1)}, bf16[4,32,512]{2,1,0:T(8,128)(2,1)S(1)}, bf16[3,2,2,16,512]{4,3,2,1,0:T(8,128)(2,1)S(1)}) custom-call(s32[3]{0:T(128)S(1)} %pad_add_fusion.scalars, bf16[3,11,16,512]{3,2,1,0:T(8,128)(2,1)S(1)} %collective-permute-done.7.halo, ...), custom_call_target="tpu_custom_call" | custom-call | flops 2407530496 | bytes 9672704 | tf_op jit(solution)/shard_map/late/pallas_call | solution.py:397
  40.9 2.4 %collective-permute-start.12 = (bf16[4,32,512]{2,1,0:T(8,128)(2,1)S(1)}, bf16[4,32,512]{2,1,0:T(8,128)(2,1)S(1)}, u32[]{:S(2)}, u32[]{:S(2)}) collective-permute-start(bf16[4,32,512]{2,1,0:T(8,128)(2,1)S(1)} %get-tuple-element.68), channel_id=1, source_target_pairs={{0,8},{2,10},{4,12},{6,14},{8,0},{10,2},{12,4},{14,6},{1,9},{3,11}... | collective-permute-start | bytes 393224 | tf_op jit(solution)/shard_map/ppermute | solution.py:570
  43.2 2.0 %collective-permute-start.13 = (bf16[4,32,512]{2,1,0:T(8,128)(2,1)S(1)}, bf16[4,32,512]{2,1,0:T(8,128)(2,1)S(1)}, u32[]{:S(2)}, u32[]{:S(2)}) collective-permute-start(bf16[4,32,512]{2,1,0:T(8,128)(2,1)S(1)} %get-tuple-element.69), channel_id=1, source_target_pairs={{0,12},{2,14},{4,8},{6,10},{8,4},{10,6},{12,0},{14,2},{1,13},{3,15... | collective-permute-start | bytes 393224 | tf_op jit(solution)/shard_map/ppermute | solution.py:570
  46.5 7.3 %full.1 = (bf16[4,32,512]{2,1,0:T(8,128)(2,1)S(1)}, bf16[4,32,512]{2,1,0:T(8,128)(2,1)S(1)}, bf16[4,32,512]{2,1,0:T(8,128)(2,1)S(1)}, bf16[4,32,512]{2,1,0:T(8,128)(2,1)S(1)}) custom-call(s32[3]{0:T(128)S(1)} %pad_add_fusion.scalars, bf16[3,9,16,512]{3,2,1,0:T(8,128)(2,1)S(1)} %collective-permute-done.5.halo, bf16[5,9,16,512]{3,2,1,0:T(8,128)(2,1)S(1)} %join_first.3.first, ...), custom_call_target="tpu_custom_call" | custom-call | flops 5360320512 | bytes 9492480 | tf_op jit(solution)/shard_map/full/pallas_call | solution.py:326
  54.5 3.8 %collective-permute-start.9 = (bf16[4,32,512]{2,1,0:T(8,128)(2,1)S(1)}, bf16[4,32,512]{2,1,0:T(8,128)(2,1)S(1)}, u32[]{:S(2)}, u32[]{:S(2)}) collective-permute-start(bf16[4,32,512]{2,1,0:T(8,128)(2,1)S(1)} %get-tuple-element.63), channel_id=1, source_target_pairs={{0,12},{2,14},{4,8},{6,10},{8,4},{10,6},{12,0},{14,2},{1,13},{3,15... | collective-permute-start | bytes 393224 | tf_op jit(solution)/shard_map/ppermute | solution.py:570
  58.9 2.8 %attend.2 = (bf16[2,32,512]{2,1,0:T(8,128)(2,1)S(1)}, bf16[2,32,512]{2,1,0:T(8,128)(2,1)S(1)}, bf16[2,32,512]{2,1,0:T(8,128)(2,1)S(1)}, bf16[2,32,512]{2,1,0:T(8...) custom-call(s32[3]{0:T(128)S(1)} %pad_add_fusion.scalars, ...), custom_call_target="tpu_custom_call" | custom-call | flops 1342177280 | bytes 2621440 | tf_op jit(solution)/shard_map/attend/pallas_call | solution.py:499
  61.7 3.9 %collective-permute-start.21 = (bf16[2,32,512]{2,1,0:T(8,128)(2,1)S(1)}, bf16[2,32,512]{2,1,0:T(8,128)(2,1)S(1)}, u32[]{:S(2)}, u32[]{:S(2)}) collective-permute-start(bf16[2,32,512]{2,1,0:T(8,128)(2,1)S(1)} %get-tuple-element.83), channel_id=1, source_target_pairs={{0,8},{2,10},{4,12},{6,14},{8,0},{10,2},{12,4},{14,6},{1,9},{3,11}... | collective-permute-start | bytes 196616 | tf_op jit(solution)/shard_map/ppermute | solution.py:570
  65.5 2.5 %collective-permute-start.22 = (bf16[2,32,512]{2,1,0:T(8,128)(2,1)S(1)}, bf16[2,32,512]{2,1,0:T(8,128)(2,1)S(1)}, u32[]{:S(2)}, u32[]{:S(2)}) collective-permute-start(bf16[2,32,512]{2,1,0:T(8,128)(2,1)S(1)} %get-tuple-element.84), channel_id=1, source_target_pairs={{0,10},{2,8},{4,14},{6,12},{8,2},{10,0},{12,6},{14,4},{1,11},{3,9}... | collective-permute-start | bytes 196616 | tf_op jit(solution)/shard_map/ppermute | solution.py:570
  68.0 3.7 %collective-permute-start.24 = (bf16[2,32,512]{2,1,0:T(8,128)(2,1)S(1)}, bf16[2,32,512]{2,1,0:T(8,128)(2,1)S(1)}, u32[]{:S(2)}, u32[]{:S(2)}) collective-permute-start(bf16[2,32,512]{2,1,0:T(8,128)(2,1)S(1)} %get-tuple-element.86), channel_id=1, source_target_pairs={{0,14},{2,12},{4,10},{6,8},{8,6},{10,4},{12,2},{14,0},{1,15},{3,13... | collective-permute-start | bytes 196616 | tf_op jit(solution)/shard_map/ppermute | solution.py:570
  71.7 2.8 %attend.3 = (bf16[2,32,512]{2,1,0:T(8,128)(2,1)S(1)}, bf16[2,2,32,512]{3,2,1,0:T(8,128)(2,1)S(1)}, bf16[2,2,32,512]{3,2,1,0:T(8,128)(2,1)S(1)}, bf16[2,2,32,512]...) custom-call(s32[3]{0:T(128)S(1)} %pad_add_fusion.scalars, ...), custom_call_target="tpu_custom_call" | custom-call | flops 1342177280 | bytes 2621440 | tf_op jit(solution)/shard_map/attend/pallas_call | solution.py:499
  74.6 2.6 %collective-permute-start.14 = (bf16[2,32,512]{2,1,0:T(8,128)(2,1)S(1)}, bf16[2,32,512]{2,1,0:T(8,128)(2,1)S(1)}, u32[]{:S(2)}, u32[]{:S(2)}) collective-permute-start(bf16[2,32,512]{2,1,0:T(8,128)(2,1)S(1)} %get-tuple-element.75), channel_id=1, source_target_pairs={{0,8},{2,10},{4,12},{6,14},{8,0},{10,2},{12,4},{14,6},{1,9},{3,11}... | collective-permute-start | bytes 196616 | tf_op jit(solution)/shard_map/ppermute | solution.py:570
  77.1 1.8 %collective-permute-start.15 = (bf16[2,32,512]{2,1,0:T(8,128)(2,1)S(1)}, bf16[2,32,512]{2,1,0:T(8,128)(2,1)S(1)}, u32[]{:S(2)}, u32[]{:S(2)}) collective-permute-start(bf16[2,32,512]{2,1,0:T(8,128)(2,1)S(1)} %get-tuple-element.76), channel_id=1, source_target_pairs={{0,10},{2,8},{4,14},{6,12},{8,2},{10,0},{12,6},{14,4},{1,11},{3,9}... | collective-permute-start | bytes 196616 | tf_op jit(solution)/shard_map/ppermute | solution.py:570
  79.5 3.9 %collective-permute-start.19 = (bf16[2,2,32,512]{3,2,1,0:T(8,128)(2,1)S(1)}, bf16[2,2,32,512]{3,2,1,0:T(8,128)(2,1)S(1)}, u32[]{:S(2)}, u32[]{:S(2)}) collective-permute-start(bf16[2,2,32,512]{3,2,1,0:T(8,128)(2,1)S(1)} %get-tuple-element.80), channel_id=1, source_target_pairs={{0,4},{2,6},{4,0},{6,2},{8,12},{10,14},{12,8},{14,10},{1,5},{3,7},... | collective-permute-start | bytes 393224 | tf_op jit(solution)/shard_map/ppermute | solution.py:570
  83.4 2.8 %collective-permute-start.16 = (bf16[2,32,512]{2,1,0:T(8,128)(2,1)S(1)}, bf16[2,32,512]{2,1,0:T(8,128)(2,1)S(1)}, u32[]{:S(2)}, u32[]{:S(2)}) collective-permute-start(bf16[2,32,512]{2,1,0:T(8,128)(2,1)S(1)} %get-tuple-element.77), channel_id=1, source_target_pairs={{0,12},{2,14},{4,8},{6,10},{8,4},{10,6},{12,0},{14,2},{1,13},{3,15... | collective-permute-start | bytes 196616 | tf_op jit(solution)/shard_map/ppermute | solution.py:570
  86.2 2.1 %collective-permute-start.17 = (bf16[2,32,512]{2,1,0:T(8,128)(2,1)S(1)}, bf16[2,32,512]{2,1,0:T(8,128)(2,1)S(1)}, u32[]{:S(2)}, u32[]{:S(2)}) collective-permute-start(bf16[2,32,512]{2,1,0:T(8,128)(2,1)S(1)} %get-tuple-element.78), channel_id=1, source_target_pairs={{0,14},{2,12},{4,10},{6,8},{8,6},{10,4},{12,2},{14,0},{1,15},{3,13... | collective-permute-start | bytes 196616 | tf_op jit(solution)/shard_map/ppermute | solution.py:570
  88.3 1.3 %collect.2.refs_8_ = bf16[2,16,32,512]{3,2,1,0:T(8,128)(2,1)} custom-call(s32[3]{0:T(128)S(1)} %pad_add_fusion.scalars, bf16[2,32,512]{2,1,0:T(8,128)(2,1)S(1)} %collective-permute-done.21.refs_0_, bf16[2,32,512]{2,1,0:T(8,128)(2,1)S(1)} %collective-permute-done.22.refs_1_, bf16[2,32,512]{2,1,0:T(8,128)(2,1)S(1)} %collective-permute-done.23.refs_2_, ...), custom_call_target="tpu_custom_call" | custom-call | tf_op jit(solution)/shard_map/collect/pallas_call | solution.py:525
  89.6 2.4 %collective-permute-done.16.refs_2_ = bf16[2,32,512]{2,1,0:T(8,128)(2,1)S(1)} collective-permute-done((bf16[2,32,512]{2,1,0:T(8,128)(2,1)S(1)}, bf16[2,32,512]{2,1,0:T(8,128)(2,1)S(1)}, u32[]{:S(2)}, u32[]{:S(2)}) %collective-permute-start.16) | collective-permute-done | bytes 65568 | tf_op jit(solution)/shard_map/ppermute | solution.py:570
  92.0 1.1 %collective-permute-done.17.refs_3_ = bf16[2,32,512]{2,1,0:T(8,128)(2,1)S(1)} collective-permute-done((bf16[2,32,512]{2,1,0:T(8,128)(2,1)S(1)}, bf16[2,32,512]{2,1,0:T(8,128)(2,1)S(1)}, u32[]{:S(2)}, u32[]{:S(2)}) %collective-permute-start.17) | collective-permute-done | bytes 65568 | tf_op jit(solution)/shard_map/ppermute | solution.py:570
  93.2 1.5 %collect.3 = bf16[2,16,32,512]{3,2,1,0:T(8,128)(2,1)} custom-call(s32[3]{0:T(128)S(1)} %pad_add_fusion.scalars, bf16[2,32,512]{2,1,0:T(8,128)(2,1)S(1)} %collective-permute-done.14.refs_0_, bf16[2,32,512]{2,1,0:T(8,128)(2,1)S(1)} %collective-permute-done.15.refs_1_, ...), custom_call_target="tpu_custom_call", output_to_operand_aliasing={{}: (9, {})} | custom-call | tf_op jit(solution)/shard_map/collect/pallas_call | solution.py:525
  (66 shorter events, 6.2 us)
Async XLA Ops:
  2.3 16.9 %collective-permute-start.1 = (bf16[3,10,16,512]{3,2,1,0:T(8,128)(2,1)S(1)}, bf16[3,10,16,512]{3,2,1,0:T(8,128)(2,1)S(1)}, u32[]{:S(2)}, u32[]{:S(2)}) collective-permute-start(bf16[3,10,16,512]{3,2,1,0:T(8,128)(2,1)S(1)} %get-tuple-element.47), channel_id=1, source_target_pairs={{0,2},{2,0},{4,6},{6,4},{8,10},{10,8},{12,14},{14,12},{1,3},{3,1},... | collective-permute-start | bytes 1474568 | tf_op jit(solution)/shard_map/ppermute | solution.py:570
  7.4 11.6 %collective-permute-start.4 = (bf16[4,18,512]{2,1,0:T(8,128)(2,1)S(1)}, bf16[4,18,512]{2,1,0:T(8,128)(2,1)S(1)}, u32[]{:S(2)}, u32[]{:S(2)}) collective-permute-start(bf16[4,18,512]{2,1,0:T(8,128)(2,1)S(1)} %get-tuple-element.89), channel_id=1, source_target_pairs={{0,3},{1,2},{2,1},{3,0},{4,7},{5,6},{6,5},{7,4},{8,11},{9,10},{10,... | collective-permute-start | bytes 221192 | tf_op jit(solution)/shard_map/ppermute | solution.py:585
  7.5 11.6 %collective-permute-start.3 = (bf16[4,18,512]{2,1,0:T(8,128)(2,1)S(1)}, bf16[4,18,512]{2,1,0:T(8,128)(2,1)S(1)}, u32[]{:S(2)}, u32[]{:S(2)}) collective-permute-start(bf16[4,18,512]{2,1,0:T(8,128)(2,1)S(1)} %get-tuple-element.90), channel_id=1, source_target_pairs={{0,1},{1,0},{2,3},{3,2},{4,5},{5,4},{6,7},{7,6},{8,9},{9,8},{10,11... | collective-permute-start | bytes 221192 | tf_op jit(solution)/shard_map/ppermute | solution.py:579
  7.6 15.4 %collective-permute-start.2 = (bf16[1,10,16,512]{3,2,1,0:T(8,128)(2,1)S(1)}, bf16[1,10,16,512]{3,2,1,0:T(8,128)(2,1)S(1)}, u32[]{:S(2)}, u32[]{:S(2)}) collective-permute-start(bf16[1,10,16,512]{3,2,1,0:T(8,128)(2,1)S(1)} %get-tuple-element.50), channel_id=1, source_target_pairs={{0,2},{2,0},{4,6},{6,4},{8,10},{10,8},{12,14},{14,12},{1,3},{3,1},... | collective-permute-start | bytes 491528 | tf_op jit(solution)/shard_map/ppermute | solution.py:570
  9.6 21.0 %collective-permute-start = (bf16[3,8,16,512]{3,2,1,0:T(8,128)(2,1)S(1)}, bf16[3,8,16,512]{3,2,1,0:T(8,128)(2,1)S(1)}, u32[]{:S(2)}, u32[]{:S(2)}) collective-permute-start(bf16[3,8,16,512]{3,2,1,0:T(8,128)(2,1)S(1)} %get-tuple-element.46), channel_id=1, source_target_pairs={{0,2},{2,0},{4,6},{6,4},{8,10},{10,8},{12,14},{14,12},{1,3},{3,1},... | collective-permute-start | bytes 1179656 | tf_op jit(solution)/shard_map/ppermute | solution.py:570
  12.5 11.1 %copy-start.2 = (bf16[3,512,512]{2,1,0:T(8,128)(2,1)S(1)}, bf16[3,512,512]{2,1,0:T(8,128)(2,1)}, u32[]{:S(2)}) copy-start(bf16[3,512,512]{2,1,0:T(8,128)(2,1)} %param.13) | copy-start | bytes 4718596
  12.5 11.1 %copy-start.3 = (bf16[3,512,512]{2,1,0:T(8,128)(2,1)S(1)}, bf16[3,512,512]{2,1,0:T(8,128)(2,1)}, u32[]{:S(2)}) copy-start(bf16[3,512,512]{2,1,0:T(8,128)(2,1)} %param.15) | copy-start | bytes 4718596
  19.9 17.0 %collective-permute-start.7 = (bf16[3,11,16,512]{3,2,1,0:T(8,128)(2,1)S(1)}, bf16[3,11,16,512]{3,2,1,0:T(8,128)(2,1)S(1)}, u32[]{:S(2)}, u32[]{:S(2)}) collective-permute-start(bf16[3,11,16,512]{3,2,1,0:T(8,128)(2,1)S(1)} %join_last.2.last), channel_id=1, source_target_pairs={{0,4},{2,6},{4,8},{6,10},{8,12},{10,14},{12,0},{14,2},{1,5},{3,7},... | collective-permute-start | bytes 1622024 | tf_op jit(solution)/shard_map/ppermute | solution.py:570
  31.2 15.3 %collective-permute-start.5 = (bf16[3,9,16,512]{3,2,1,0:T(8,128)(2,1)S(1)}, bf16[3,9,16,512]{3,2,1,0:T(8,128)(2,1)S(1)}, u32[]{:S(2)}, u32[]{:S(2)}) collective-permute-start(bf16[3,9,16,512]{3,2,1,0:T(8,128)(2,1)S(1)} %join_last.3.last), channel_id=1, source_target_pairs={{0,4},{2,6},{4,8},{6,10},{8,12},{10,14},{12,0},{14,2},{1,5},{3,7},... | collective-permute-start | bytes 1327112 | tf_op jit(solution)/shard_map/ppermute | solution.py:570
  33.0 7.7 %collective-permute-start.6 = (bf16[1,8,16,512]{3,2,1,0:T(8,128)(2,1)S(1)}, bf16[1,8,16,512]{3,2,1,0:T(8,128)(2,1)S(1)}, u32[]{:S(2)}, u32[]{:S(2)}) collective-permute-start(bf16[1,8,16,512]{3,2,1,0:T(8,128)(2,1)S(1)} %get-tuple-element.55), channel_id=1, source_target_pairs={{0,2},{2,0},{4,6},{6,4},{8,10},{10,8},{12,14},{14,12},{1,3},{3,1},... | collective-permute-start | bytes 393224 | tf_op jit(solution)/shard_map/ppermute | solution.py:570
  40.8 17.5 %collective-permute-start.11 = (bf16[4,32,512]{2,1,0:T(8,128)(2,1)S(1)}, bf16[4,32,512]{2,1,0:T(8,128)(2,1)S(1)}, u32[]{:S(2)}, u32[]{:S(2)}) collective-permute-start(bf16[4,32,512]{2,1,0:T(8,128)(2,1)S(1)} %get-tuple-element.67), channel_id=1, source_target_pairs={{0,4},{2,6},{4,0},{6,2},{8,12},{10,14},{12,8},{14,10},{1,5},{3,7},... | collective-permute-start | bytes 393224 | tf_op jit(solution)/shard_map/ppermute | solution.py:570
  40.9 18.0 %collective-permute-start.12 = (bf16[4,32,512]{2,1,0:T(8,128)(2,1)S(1)}, bf16[4,32,512]{2,1,0:T(8,128)(2,1)S(1)}, u32[]{:S(2)}, u32[]{:S(2)}) collective-permute-start(bf16[4,32,512]{2,1,0:T(8,128)(2,1)S(1)} %get-tuple-element.68), channel_id=1, source_target_pairs={{0,8},{2,10},{4,12},{6,14},{8,0},{10,2},{12,4},{14,6},{1,9},{3,11}... | collective-permute-start | bytes 393224 | tf_op jit(solution)/shard_map/ppermute | solution.py:570
  43.2 15.6 %collective-permute-start.13 = (bf16[4,32,512]{2,1,0:T(8,128)(2,1)S(1)}, bf16[4,32,512]{2,1,0:T(8,128)(2,1)S(1)}, u32[]{:S(2)}, u32[]{:S(2)}) collective-permute-start(bf16[4,32,512]{2,1,0:T(8,128)(2,1)S(1)} %get-tuple-element.69), channel_id=1, source_target_pairs={{0,12},{2,14},{4,8},{6,10},{8,4},{10,6},{12,0},{14,2},{1,13},{3,15... | collective-permute-start | bytes 393224 | tf_op jit(solution)/shard_map/ppermute | solution.py:570
  46.5 12.4 %copy-start.7 = (bf16[512,512]{1,0:T(8,128)(2,1)S(1)}, bf16[512,512]{1,0:T(8,128)(2,1)}, u32[]{:S(2)}) copy-start(bf16[512,512]{1,0:T(8,128)(2,1)} %refs_5_.3) | copy-start | bytes 1572868
  46.5 12.4 %copy-start.8 = (bf16[512,512]{1,0:T(8,128)(2,1)S(1)}, bf16[512,512]{1,0:T(8,128)(2,1)}, u32[]{:S(2)}) copy-start(bf16[512,512]{1,0:T(8,128)(2,1)} %refs_6_.3) | copy-start | bytes 1572868
  46.5 12.4 %copy-start.9 = (bf16[512,512]{1,0:T(8,128)(2,1)S(1)}, bf16[512,512]{1,0:T(8,128)(2,1)}, u32[]{:S(2)}) copy-start(bf16[512,512]{1,0:T(8,128)(2,1)} %refs_7_.3) | copy-start | bytes 1572868
  46.5 12.4 %copy-start.10 = (bf16[512,512]{1,0:T(8,128)(2,1)S(1)}, bf16[512,512]{1,0:T(8,128)(2,1)}, u32[]{:S(2)}) copy-start(bf16[512,512]{1,0:T(8,128)(2,1)} %refs_8_.3) | copy-start | bytes 1572868
  46.5 12.4 %copy-start.11 = (f32[512]{0:T(512)S(1)}, f32[512]{0:T(512)}, u32[]{:S(2)}) copy-start(f32[512]{0:T(512)} %param.19) | copy-start | bytes 6148
  53.8 14.2 %collective-permute-start.8 = (bf16[4,32,512]{2,1,0:T(8,128)(2,1)S(1)}, bf16[4,32,512]{2,1,0:T(8,128)(2,1)S(1)}, u32[]{:S(2)}, u32[]{:S(2)}) collective-permute-start(bf16[4,32,512]{2,1,0:T(8,128)(2,1)S(1)} %get-tuple-element.62), channel_id=1, source_target_pairs={{0,8},{2,10},{4,12},{6,14},{8,0},{10,2},{12,4},{14,6},{1,9},{3,11}... | collective-permute-start | bytes 393224 | tf_op jit(solution)/shard_map/ppermute | solution.py:570
  54.5 13.5 %collective-permute-start.9 = (bf16[4,32,512]{2,1,0:T(8,128)(2,1)S(1)}, bf16[4,32,512]{2,1,0:T(8,128)(2,1)S(1)}, u32[]{:S(2)}, u32[]{:S(2)}) collective-permute-start(bf16[4,32,512]{2,1,0:T(8,128)(2,1)S(1)} %get-tuple-element.63), channel_id=1, source_target_pairs={{0,12},{2,14},{4,8},{6,10},{8,4},{10,6},{12,0},{14,2},{1,13},{3,15... | collective-permute-start | bytes 393224 | tf_op jit(solution)/shard_map/ppermute | solution.py:570
  58.3 13.4 %collective-permute-start.10 = (bf16[4,32,512]{2,1,0:T(8,128)(2,1)S(1)}, bf16[4,32,512]{2,1,0:T(8,128)(2,1)S(1)}, u32[]{:S(2)}, u32[]{:S(2)}) collective-permute-start(bf16[4,32,512]{2,1,0:T(8,128)(2,1)S(1)} %get-tuple-element.64), channel_id=1, source_target_pairs={{0,4},{2,6},{4,0},{6,2},{8,12},{10,14},{12,8},{14,10},{1,5},{3,7},... | collective-permute-start | bytes 393224 | tf_op jit(solution)/shard_map/ppermute | solution.py:570
  61.7 15.5 %collective-permute-start.21 = (bf16[2,32,512]{2,1,0:T(8,128)(2,1)S(1)}, bf16[2,32,512]{2,1,0:T(8,128)(2,1)S(1)}, u32[]{:S(2)}, u32[]{:S(2)}) collective-permute-start(bf16[2,32,512]{2,1,0:T(8,128)(2,1)S(1)} %get-tuple-element.83), channel_id=1, source_target_pairs={{0,8},{2,10},{4,12},{6,14},{8,0},{10,2},{12,4},{14,6},{1,9},{3,11}... | collective-permute-start | bytes 196616 | tf_op jit(solution)/shard_map/ppermute | solution.py:570
  65.5 13.5 %collective-permute-start.22 = (bf16[2,32,512]{2,1,0:T(8,128)(2,1)S(1)}, bf16[2,32,512]{2,1,0:T(8,128)(2,1)S(1)}, u32[]{:S(2)}, u32[]{:S(2)}) collective-permute-start(bf16[2,32,512]{2,1,0:T(8,128)(2,1)S(1)} %get-tuple-element.84), channel_id=1, source_target_pairs={{0,10},{2,8},{4,14},{6,12},{8,2},{10,0},{12,6},{14,4},{1,11},{3,9}... | collective-permute-start | bytes 196616 | tf_op jit(solution)/shard_map/ppermute | solution.py:570
  68.0 11.5 %collective-permute-start.23 = (bf16[2,32,512]{2,1,0:T(8,128)(2,1)S(1)}, bf16[2,32,512]{2,1,0:T(8,128)(2,1)S(1)}, u32[]{:S(2)}, u32[]{:S(2)}) collective-permute-start(bf16[2,32,512]{2,1,0:T(8,128)(2,1)S(1)} %get-tuple-element.85), channel_id=1, source_target_pairs={{0,12},{2,14},{4,8},{6,10},{8,4},{10,6},{12,0},{14,2},{1,13},{3,15... | collective-permute-start | bytes 196616 | tf_op jit(solution)/shard_map/ppermute | solution.py:570
  68.0 15.4 %collective-permute-start.24 = (bf16[2,32,512]{2,1,0:T(8,128)(2,1)S(1)}, bf16[2,32,512]{2,1,0:T(8,128)(2,1)S(1)}, u32[]{:S(2)}, u32[]{:S(2)}) collective-permute-start(bf16[2,32,512]{2,1,0:T(8,128)(2,1)S(1)} %get-tuple-element.86), channel_id=1, source_target_pairs={{0,14},{2,12},{4,10},{6,8},{8,6},{10,4},{12,2},{14,0},{1,15},{3,13... | collective-permute-start | bytes 196616 | tf_op jit(solution)/shard_map/ppermute | solution.py:570
  74.6 8.8 %collective-permute-start.14 = (bf16[2,32,512]{2,1,0:T(8,128)(2,1)S(1)}, bf16[2,32,512]{2,1,0:T(8,128)(2,1)S(1)}, u32[]{:S(2)}, u32[]{:S(2)}) collective-permute-start(bf16[2,32,512]{2,1,0:T(8,128)(2,1)S(1)} %get-tuple-element.75), channel_id=1, source_target_pairs={{0,8},{2,10},{4,12},{6,14},{8,0},{10,2},{12,4},{14,6},{1,9},{3,11}... | collective-permute-start | bytes 196616 | tf_op jit(solution)/shard_map/ppermute | solution.py:570
  77.1 9.0 %collective-permute-start.15 = (bf16[2,32,512]{2,1,0:T(8,128)(2,1)S(1)}, bf16[2,32,512]{2,1,0:T(8,128)(2,1)S(1)}, u32[]{:S(2)}, u32[]{:S(2)}) collective-permute-start(bf16[2,32,512]{2,1,0:T(8,128)(2,1)S(1)} %get-tuple-element.76), channel_id=1, source_target_pairs={{0,10},{2,8},{4,14},{6,12},{8,2},{10,0},{12,6},{14,4},{1,11},{3,9}... | collective-permute-start | bytes 196616 | tf_op jit(solution)/shard_map/ppermute | solution.py:570
  79.0 14.2 %collective-permute-start.18 = (bf16[2,2,32,512]{3,2,1,0:T(8,128)(2,1)S(1)}, bf16[2,2,32,512]{3,2,1,0:T(8,128)(2,1)S(1)}, u32[]{:S(2)}, u32[]{:S(2)}) collective-permute-start(bf16[2,2,32,512]{3,2,1,0:T(8,128)(2,1)S(1)} %get-tuple-element.79), channel_id=1, source_target_pairs={{0,2},{2,0},{4,6},{6,4},{8,10},{10,8},{12,14},{14,12},{1,3},{3,1},... | collective-permute-start | bytes 393224 | tf_op jit(solution)/shard_map/ppermute | solution.py:570
  79.5 13.6 %collective-permute-start.19 = (bf16[2,2,32,512]{3,2,1,0:T(8,128)(2,1)S(1)}, bf16[2,2,32,512]{3,2,1,0:T(8,128)(2,1)S(1)}, u32[]{:S(2)}, u32[]{:S(2)}) collective-permute-start(bf16[2,2,32,512]{3,2,1,0:T(8,128)(2,1)S(1)} %get-tuple-element.80), channel_id=1, source_target_pairs={{0,4},{2,6},{4,0},{6,2},{8,12},{10,14},{12,8},{14,10},{1,5},{3,7},... | collective-permute-start | bytes 393224 | tf_op jit(solution)/shard_map/ppermute | solution.py:570
  83.4 9.8 %collective-permute-start.20 = (bf16[2,2,32,512]{3,2,1,0:T(8,128)(2,1)S(1)}, bf16[2,2,32,512]{3,2,1,0:T(8,128)(2,1)S(1)}, u32[]{:S(2)}, u32[]{:S(2)}) collective-permute-start(bf16[2,2,32,512]{3,2,1,0:T(8,128)(2,1)S(1)} %get-tuple-element.81), channel_id=1, source_target_pairs={{0,6},{2,4},{4,2},{6,0},{8,14},{10,12},{12,10},{14,8},{1,7},{3,5},... | collective-permute-start | bytes 393224 | tf_op jit(solution)/shard_map/ppermute | solution.py:570
  83.4 8.6 %collective-permute-start.16 = (bf16[2,32,512]{2,1,0:T(8,128)(2,1)S(1)}, bf16[2,32,512]{2,1,0:T(8,128)(2,1)S(1)}, u32[]{:S(2)}, u32[]{:S(2)}) collective-permute-start(bf16[2,32,512]{2,1,0:T(8,128)(2,1)S(1)} %get-tuple-element.77), channel_id=1, source_target_pairs={{0,12},{2,14},{4,8},{6,10},{8,4},{10,6},{12,0},{14,2},{1,13},{3,15... | collective-permute-start | bytes 196616 | tf_op jit(solution)/shard_map/ppermute | solution.py:570
  86.2 7.0 %collective-permute-start.17 = (bf16[2,32,512]{2,1,0:T(8,128)(2,1)S(1)}, bf16[2,32,512]{2,1,0:T(8,128)(2,1)S(1)}, u32[]{:S(2)}, u32[]{:S(2)}) collective-permute-start(bf16[2,32,512]{2,1,0:T(8,128)(2,1)S(1)} %get-tuple-element.78), channel_id=1, source_target_pairs={{0,14},{2,12},{4,10},{6,8},{8,6},{10,4},{12,2},{14,0},{1,15},{3,13... | collective-permute-start | bytes 196616 | tf_op jit(solution)/shard_map/ppermute | solution.py:570
  (6 other events, 54.0 us)

commit v18 on v17

--- a/solution.py
+++ b/solution.py
@@ -58,24 +58,20 @@
         target[here : here + count] = video[frame, pl.ds(source, count)]
 
 
-def send_kernel(spans, half, scalars, video, *outs):
-    frames = video.shape[0]
-    rest = frames - taps
-    for k, (begin, end) in enumerate(spans):
-        for t in range(frames):
-            target = outs[2 * k].at[t - rest] if t >= rest else outs[2 * k + 1].at[t]
-            cut(target, video, t, 1 - scalars[0], begin, end, half)
-
-
-def send(scalars, video, spans, half):
-    frames, _, width, channels = video.shape
+def send_kernel(spans, pieces, half, scalars, video, *outs):
+    for out, (k, low, high) in zip(outs, pieces):
+        begin, end = spans[k]
+        for t in range(low, high):
+            cut(out.at[t - low], video, t, 1 - scalars[0], begin, end, half)
+
+
+def send(scalars, video, spans, pieces, half):
+    width, channels = video.shape[2:]
     shapes = [
-        (count, end - begin, width, channels)
-        for begin, end in spans
-        for count in (taps, frames - taps)
+        (high - low, spans[k][1] - spans[k][0], width, channels) for k, low, high in pieces
     ]
     return pl.pallas_call(
-        partial(send_kernel, spans, half),
+        partial(send_kernel, spans, pieces, half),
         out_shape=[jax.ShapeDtypeStruct(shape, video.dtype) for shape in shapes],
         in_specs=[SMEM, VMEM],
         out_specs=[VMEM] * len(shapes),
@@ -569,7 +565,10 @@
     def tm_permute(value, move):
         return lax.ppermute(value, "tm", [(i, move(i)) for i in range(devices) if move(i) < devices])
 
-    sent = send(scalars, video, spans, half)
+    rest = frames - taps
+    pieces = [(k,) + cut for k in range(chunks) for cut in ((rest, frames), (0, rest))]
+    sent = send(scalars, video, spans, pieces[:1], half)
+    sent = [*sent, *send(after(scalars, sent[0]), video, spans, pieces[1:], half)]
     received = [tm_permute(value, lambda i: i ^ 1) for value in sent]
     border = jnp.where(column == 0, video[:, :, -1], video[:, :, 0])
     border = jnp.pad(after(border, sent[0]), ((0, 0), (1, 1), (0, 0)))

time: 95 us -> 98.1 us (1.033)
  local copies, waits for them, and re-layouts: 3.73 us -> 6.74 us
  Pallas kernels: 27.6 us -> 29.4 us
  starting transfers between devices: 43.5 us -> 42 us
  waiting for transfers between devices: 16.5 us -> 15.4 us
    ppermute x1, waiting for transfers between devices: 6.52 us -> 4.11 us  [per_device(): other_edge = lax.ppermute(other_edge, ('tm', 'cols'), aslant)]
    slice x2, local copies, waits for them, and re-layouts: 0.03 us -> 1.71 us  [edge_rows(): edge[:, begin:end]]
    ppermute x23, starting transfers between devices: 43.3 us -> 41.8 us  [tm_permute(): lax.ppermute(value, 'tm', [(i, move(i)) for i in range(devices) if move(i...]
    ppermute x23, waiting for transfers between devices: 9.94 us -> 11.3 us  [tm_permute(): lax.ppermute(value, 'tm', [(i, move(i)) for i in range(devices) if move(i...]
    pallas_call x1 -> x2, Pallas kernels: 0.62 us -> 1.97 us  [send(): pl.pallas_call(partial(send_kernel, spans, pieces, half), out_shape=[jax....]
    unnamed x26 -> x30, local copies, waits for them, and re-layouts: 1.65 us -> 2.3 us
  transfers between devices with their start and end apart: 25 -> 25, of which waited for: 8 -> 9; matrix products, arithmetic and copies ran while one was open for 5% -> 8% of each run, Pallas kernels for 27% -> 27%
where the time goes in v18:
time: 98.1 us; the launch traced here: 97.7 us
  starting transfers between devices  42 us (43%)
  Pallas kernels  29.4 us (30%)
  waiting for transfers between devices  15.4 us (16%)
  local copies, waits for them, and re-layouts  6.74 us (7%)
  other arithmetic  3.73 us (4%)
    ppermute x23, starting transfers between devices, tm_permute(): lax.ppermute(value, 'tm', [(i, move(i)) for i in range(devices) if move(i...  41.8 us
    ppermute x23, waiting for transfers between devices, tm_permute(): lax.ppermute(value, 'tm', [(i, move(i)) for i in range(devices) if move(i...  11.3 us
    pallas_call x1, Pallas kernels, full(): pl.pallas_call(partial(full_kernel, owners, final, rows), out_shape=[jax....  7.33 us
    pallas_call x2, Pallas kernels, attend(): pl.pallas_call(partial(attend_kernel, frames_per, lanes, turns, near, chu...  5.6 us
    pallas_call x1, Pallas kernels, early(): pl.pallas_call(partial(early_kernel, final, rows), out_shape=shapes, in_s...  5.03 us
    ppermute x1, waiting for transfers between devices, per_device(): other_edge = lax.ppermute(other_edge, ('tm', 'cols'), aslant)  4.11 us
    pallas_call x1, Pallas kernels, late(): pl.pallas_call(partial(late_kernel, owners, final, rows), out_shape=[jax....  3.91 us
    pallas_call x2, Pallas kernels, collect(): pl.pallas_call(partial(collect_kernel, entries, levels, chunks), out_shap...  2.79 us
  transfers between devices with their start and end apart: 25, of which 9 were waited for; matrix products, arithmetic and copies ran while one was open for 8% of the time, Pallas kernels for 27%

profile of v18, /device:TPU:0, one launch (start us, length us, event | category | flops | bytes accessed | tf_op | source)
XLA Modules:
  0.0 97.7 jit_solution(13435745270980639107)
XLA Ops:
  0.1 1.6 %copy-done = bf16[4,32,16,512]{3,2,1,0:T(8,128)(2,1)S(1)} copy-done((bf16[4,32,16,512]{3,2,1,0:T(8,128)(2,1)S(1)}, bf16[4,32,16,512]{3,2,1,0:T(8,128)(2,1)}, u32[]{:S(2)}) %copy-start) | copy-done | bytes 2097176
  2.3 3.0 %collective-permute-start.1 = (bf16[3,10,16,512]{3,2,1,0:T(8,128)(2,1)S(1)}, bf16[3,10,16,512]{3,2,1,0:T(8,128)(2,1)S(1)}, u32[]{:S(2)}, u32[]{:S(2)}) collective-permute-start(bf16[3,10,16,512]{3,2,1,0:T(8,128)(2,1)S(1)} %send.2), channel_id=1, source_target_pairs={{0,2},{2,0},{4,6},{6,4},{8,10},{10,8},{12,14},{14,12},{1,3},{3,1},... | collective-permute-start | bytes 1474568 | tf_op jit(solution)/shard_map/ppermute | solution.py:566
  5.3 1.9 %fusion.3 = (bf16[4,32,1,512]{3,2,1,0:T(2,128)(2,1)S(1)}, bf16[4,32,1,512]{3,2,1,0:T(2,128)(2,1)S(1)}) fusion(bf16[4,32,16,512]{3,2,1,0:T(8,128)(2,1)} %video.11), kind=kLoop, calls=%fused_computation.12 | loop fusion | bytes 524288 | tf_op jit(solution)/shard_map/slice | solution.py:573
  8.2 1.4 %send.3 = (bf16[1,10,16,512]{3,2,1,0:T(8,128)(2,1)}, bf16[3,8,16,512]{3,2,1,0:T(8,128)(2,1)}, bf16[1,8,16,512]{3,2,1,0:T(8,128)(2,1)S(1)}) custom-call(s32[3]{0:T(128)S(1)} %pad_add_fusion.scalars, bf16[4,32,16,512]{3,2,1,0:T(8,128)(2,1)S(1)} %copy-done.1), custom_call_target="tpu_custom_call" | custom-call | tf_op jit(solution)/shard_map/send/pallas_call | solution.py:73
  10.2 2.0 %collective-permute-start.2 = (bf16[1,10,16,512]{3,2,1,0:T(8,128)(2,1)}, bf16[1,10,16,512]{3,2,1,0:T(8,128)(2,1)}, u32[]{:S(2)}, u32[]{:S(2)}) collective-permute-start(bf16[1,10,16,512]{3,2,1,0:T(8,128)(2,1)} %get-tuple-element.50), channel_id=1, source_target_pairs={{0,2},{2,0},{4,6},{6,4},{8,10},{10,8},{12,14},{14,12},{1,3},{3,1},... | collective-permute-start | bytes 491528 | tf_op jit(solution)/shard_map/ppermute | solution.py:566
  12.3 2.7 %broadcast_select_fusion.w_space = bf16[9,512,512]{2,1,0:T(8,128)(2,1)S(1)} fusion(bf16[9,512,512]{2,1,0:T(8,128)(2,1)} %param.17, pred[]{:T(512)S(6)} %ge.3), kind=kLoop, calls=%fused_computation | loop fusion | flops 2359296 | bytes 9437185 | tf_op jit(solution)/shard_map/jit(_where)/select_n | solution.py:551
  15.0 4.1 %collective-permute-done.4 = bf16[4,18,512]{2,1,0:T(8,128)(2,1)} collective-permute-done((bf16[4,18,512]{2,1,0:T(8,128)(2,1)}, bf16[4,18,512]{2,1,0:T(8,128)(2,1)}, u32[]{:S(2)}, u32[]{:S(2)}) %collective-permute-start.4) | collective-permute-done | bytes 73760 | tf_op jit(solution)/shard_map/ppermute | solution.py:584
  22.5 1.6 %collective-permute-start.7 = (bf16[3,11,16,512]{3,2,1,0:T(8,128)(2,1)S(1)}, bf16[3,11,16,512]{3,2,1,0:T(8,128)(2,1)S(1)}, u32[]{:S(2)}, u32[]{:S(2)}) collective-permute-start(bf16[3,11,16,512]{3,2,1,0:T(8,128)(2,1)S(1)} %join_last.2.last), channel_id=1, source_target_pairs={{0,4},{2,6},{4,8},{6,10},{8,12},{10,14},{12,0},{14,2},{1,5},{3,7},... | collective-permute-start | bytes 1622024 | tf_op jit(solution)/shard_map/ppermute | solution.py:566
  24.1 1.0 %join_first.2.first = bf16[5,11,16,512]{3,2,1,0:T(8,128)(2,1)S(1)} custom-call(s32[3]{0:T(128)S(1)} %pad_add_fusion.scalars, bf16[4,32,16,512]{3,2,1,0:T(8,128)(2,1)S(1)} %copy-done.1, bf16[3,10,16,512]{3,2,1,0:T(8,128)(2,1)S(1)} %collective-permute-done.1.received, bf16[1,10,16,512]{3,2,1,0:T(8,128)(2,1)} %collective-permute-done.2.others, ...), custom_call_target="tpu_custom_call" | custom-call | tf_op jit(solution)/shard_map/join_first/pallas_call | solution.py:125
  25.2 5.0 %early.1 = (f32[176,512]{1,0:T(8,128)S(1)}, bf16[2,128,512]{2,1,0:T(8,128)(2,1)S(1)}, bf16[3,2,2,16,512]{4,3,2,1,0:T(8,128)(2,1)S(1)}) custom-call(s32[3]{0:T(128)S(1)} %pad_add_fusion.scalars, bf16[5,11,16,512]{3,2,1,0:T(8,128)(2,1)S(1)} %join_first.2.first, bf16[3,11,16,512]{3,2,1,0:T(8,128)(2,1)S(1)} %join_last.2.last, bf16[1536,512]{1,0:T(8,128)(2,1)S(1)} %bitcast.26, ...), custom_call_target="tpu_custom_call" | custom-call | flops 3607101440 | bytes 9312256 | tf_op jit(solution)/shard_map/early/pallas_call | solution.py:235
  31.1 1.8 %collective-permute-start.5 = (bf16[3,9,16,512]{3,2,1,0:T(8,128)(2,1)S(1)}, bf16[3,9,16,512]{3,2,1,0:T(8,128)(2,1)S(1)}, u32[]{:S(2)}, u32[]{:S(2)}) collective-permute-start(bf16[3,9,16,512]{3,2,1,0:T(8,128)(2,1)S(1)} %join_last.3.last), channel_id=1, source_target_pairs={{0,4},{2,6},{4,8},{6,10},{8,12},{10,14},{12,0},{14,2},{1,5},{3,7},... | collective-permute-start | bytes 1327112 | tf_op jit(solution)/shard_map/ppermute | solution.py:566
  33.0 1.5 %collective-permute-start.6 = (bf16[1,8,16,512]{3,2,1,0:T(8,128)(2,1)S(1)}, bf16[1,8,16,512]{3,2,1,0:T(8,128)(2,1)S(1)}, u32[]{:S(2)}, u32[]{:S(2)}) collective-permute-start(bf16[1,8,16,512]{3,2,1,0:T(8,128)(2,1)S(1)} %copy-done.12), channel_id=1, source_target_pairs={{0,2},{2,0},{4,6},{6,4},{8,10},{10,8},{12,14},{14,12},{1,3},{3,1},... | collective-permute-start | bytes 393224 | tf_op jit(solution)/shard_map/ppermute | solution.py:566
  34.5 4.9 %collective-permute-done.7.halo = bf16[3,11,16,512]{3,2,1,0:T(8,128)(2,1)S(1)} collective-permute-done((bf16[3,11,16,512]{3,2,1,0:T(8,128)(2,1)S(1)}, bf16[3,11,16,512]{3,2,1,0:T(8,128)(2,1)S(1)}, u32[]{:S(2)}, u32[]{:S(2)}) %collective-permute-start.7) | collective-permute-done | bytes 540704 | tf_op jit(solution)/shard_map/ppermute | solution.py:566
  39.5 3.9 %late.1 = (bf16[4,32,512]{2,1,0:T(8,128)(2,1)S(1)}, bf16[4,32,512]{2,1,0:T(8,128)(2,1)S(1)}, bf16[4,32,512]{2,1,0:T(8,128)(2,1)S(1)}, bf16[4,32,512]{2,1,0:T(8,128)(2,1)S(1)}, bf16[3,2,2,16,512]{4,3,2,1,0:T(8,128)(2,1)S(1)}) custom-call(s32[3]{0:T(128)S(1)} %pad_add_fusion.scalars, bf16[3,11,16,512]{3,2,1,0:T(8,128)(2,1)S(1)} %collective-permute-done.7.halo, ...), custom_call_target="tpu_custom_call" | custom-call | flops 2407530496 | bytes 9672704 | tf_op jit(solution)/shard_map/late/pallas_call | solution.py:393
  43.5 2.4 %collective-permute-start.12 = (bf16[4,32,512]{2,1,0:T(8,128)(2,1)S(1)}, bf16[4,32,512]{2,1,0:T(8,128)(2,1)S(1)}, u32[]{:S(2)}, u32[]{:S(2)}) collective-permute-start(bf16[4,32,512]{2,1,0:T(8,128)(2,1)S(1)} %get-tuple-element.68), channel_id=1, source_target_pairs={{0,8},{2,10},{4,12},{6,14},{8,0},{10,2},{12,4},{14,6},{1,9},{3,11}... | collective-permute-start | bytes 393224 | tf_op jit(solution)/shard_map/ppermute | solution.py:566
  45.8 2.0 %collective-permute-start.13 = (bf16[4,32,512]{2,1,0:T(8,128)(2,1)S(1)}, bf16[4,32,512]{2,1,0:T(8,128)(2,1)S(1)}, u32[]{:S(2)}, u32[]{:S(2)}) collective-permute-start(bf16[4,32,512]{2,1,0:T(8,128)(2,1)S(1)} %get-tuple-element.69), channel_id=1, source_target_pairs={{0,12},{2,14},{4,8},{6,10},{8,4},{10,6},{12,0},{14,2},{1,13},{3,15... | collective-permute-start | bytes 393224 | tf_op jit(solution)/shard_map/ppermute | solution.py:566
  49.1 7.3 %full.1 = (bf16[4,32,512]{2,1,0:T(8,128)(2,1)S(1)}, bf16[4,32,512]{2,1,0:T(8,128)(2,1)S(1)}, bf16[4,32,512]{2,1,0:T(8,128)(2,1)S(1)}, bf16[4,32,512]{2,1,0:T(8,128)(2,1)S(1)}) custom-call(s32[3]{0:T(128)S(1)} %pad_add_fusion.scalars, bf16[3,9,16,512]{3,2,1,0:T(8,128)(2,1)S(1)} %collective-permute-done.5.halo, bf16[5,9,16,512]{3,2,1,0:T(8,128)(2,1)S(1)} %join_first.3.first, ...), custom_call_target="tpu_custom_call" | custom-call | flops 5360320512 | bytes 9492480 | tf_op jit(solution)/shard_map/full/pallas_call | solution.py:322
  57.2 3.8 %collective-permute-start.9 = (bf16[4,32,512]{2,1,0:T(8,128)(2,1)S(1)}, bf16[4,32,512]{2,1,0:T(8,128)(2,1)S(1)}, u32[]{:S(2)}, u32[]{:S(2)}) collective-permute-start(bf16[4,32,512]{2,1,0:T(8,128)(2,1)S(1)} %get-tuple-element.63), channel_id=1, source_target_pairs={{0,12},{2,14},{4,8},{6,10},{8,4},{10,6},{12,0},{14,2},{1,13},{3,15... | collective-permute-start | bytes 393224 | tf_op jit(solution)/shard_map/ppermute | solution.py:566
  61.5 2.8 %attend.2 = (bf16[2,32,512]{2,1,0:T(8,128)(2,1)S(1)}, bf16[2,32,512]{2,1,0:T(8,128)(2,1)S(1)}, bf16[2,32,512]{2,1,0:T(8,128)(2,1)S(1)}, bf16[2,32,512]{2,1,0:T(8...) custom-call(s32[3]{0:T(128)S(1)} %pad_add_fusion.scalars, ...), custom_call_target="tpu_custom_call" | custom-call | flops 1342177280 | bytes 2621440 | tf_op jit(solution)/shard_map/attend/pallas_call | solution.py:495
  64.3 3.9 %collective-permute-start.21 = (bf16[2,32,512]{2,1,0:T(8,128)(2,1)S(1)}, bf16[2,32,512]{2,1,0:T(8,128)(2,1)S(1)}, u32[]{:S(2)}, u32[]{:S(2)}) collective-permute-start(bf16[2,32,512]{2,1,0:T(8,128)(2,1)S(1)} %get-tuple-element.83), channel_id=1, source_target_pairs={{0,8},{2,10},{4,12},{6,14},{8,0},{10,2},{12,4},{14,6},{1,9},{3,11}... | collective-permute-start | bytes 196616 | tf_op jit(solution)/shard_map/ppermute | solution.py:566
  68.7 1.7 %collective-permute-start.23 = (bf16[2,32,512]{2,1,0:T(8,128)(2,1)S(1)}, bf16[2,32,512]{2,1,0:T(8,128)(2,1)S(1)}, u32[]{:S(2)}, u32[]{:S(2)}) collective-permute-start(bf16[2,32,512]{2,1,0:T(8,128)(2,1)S(1)} %get-tuple-element.85), channel_id=1, source_target_pairs={{0,12},{2,14},{4,8},{6,10},{8,4},{10,6},{12,0},{14,2},{1,13},{3,15... | collective-permute-start | bytes 196616 | tf_op jit(solution)/shard_map/ppermute | solution.py:566
  70.4 2.6 %collective-permute-start.24 = (bf16[2,32,512]{2,1,0:T(8,128)(2,1)S(1)}, bf16[2,32,512]{2,1,0:T(8,128)(2,1)S(1)}, u32[]{:S(2)}, u32[]{:S(2)}) collective-permute-start(bf16[2,32,512]{2,1,0:T(8,128)(2,1)S(1)} %get-tuple-element.86), channel_id=1, source_target_pairs={{0,14},{2,12},{4,10},{6,8},{8,6},{10,4},{12,2},{14,0},{1,15},{3,13... | collective-permute-start | bytes 196616 | tf_op jit(solution)/shard_map/ppermute | solution.py:566
  72.9 2.8 %attend.3 = (bf16[2,32,512]{2,1,0:T(8,128)(2,1)S(1)}, bf16[2,2,32,512]{3,2,1,0:T(8,128)(2,1)S(1)}, bf16[2,2,32,512]{3,2,1,0:T(8,128)(2,1)S(1)}, bf16[2,2,32,512]...) custom-call(s32[3]{0:T(128)S(1)} %pad_add_fusion.scalars, ...), custom_call_target="tpu_custom_call" | custom-call | flops 1342177280 | bytes 2621440 | tf_op jit(solution)/shard_map/attend/pallas_call | solution.py:495
  75.8 4.3 %collective-permute-start.14 = (bf16[2,32,512]{2,1,0:T(8,128)(2,1)S(1)}, bf16[2,32,512]{2,1,0:T(8,128)(2,1)S(1)}, u32[]{:S(2)}, u32[]{:S(2)}) collective-permute-start(bf16[2,32,512]{2,1,0:T(8,128)(2,1)S(1)} %get-tuple-element.75), channel_id=1, source_target_pairs={{0,8},{2,10},{4,12},{6,14},{8,0},{10,2},{12,4},{14,6},{1,9},{3,11}... | collective-permute-start | bytes 196616 | tf_op jit(solution)/shard_map/ppermute | solution.py:566
  80.1 2.2 %collective-permute-start.15 = (bf16[2,32,512]{2,1,0:T(8,128)(2,1)S(1)}, bf16[2,32,512]{2,1,0:T(8,128)(2,1)S(1)}, u32[]{:S(2)}, u32[]{:S(2)}) collective-permute-start(bf16[2,32,512]{2,1,0:T(8,128)(2,1)S(1)} %get-tuple-element.76), channel_id=1, source_target_pairs={{0,10},{2,8},{4,14},{6,12},{8,2},{10,0},{12,6},{14,4},{1,11},{3,9}... | collective-permute-start | bytes 196616 | tf_op jit(solution)/shard_map/ppermute | solution.py:566
  82.8 1.7 %collective-permute-start.19 = (bf16[2,2,32,512]{3,2,1,0:T(8,128)(2,1)S(1)}, bf16[2,2,32,512]{3,2,1,0:T(8,128)(2,1)S(1)}, u32[]{:S(2)}, u32[]{:S(2)}) collective-permute-start(bf16[2,2,32,512]{3,2,1,0:T(8,128)(2,1)S(1)} %get-tuple-element.80), channel_id=1, source_target_pairs={{0,4},{2,6},{4,0},{6,2},{8,12},{10,14},{12,8},{14,10},{1,5},{3,7},... | collective-permute-start | bytes 393224 | tf_op jit(solution)/shard_map/ppermute | solution.py:566
  84.6 1.5 %collective-permute-start.20 = (bf16[2,2,32,512]{3,2,1,0:T(8,128)(2,1)S(1)}, bf16[2,2,32,512]{3,2,1,0:T(8,128)(2,1)S(1)}, u32[]{:S(2)}, u32[]{:S(2)}) collective-permute-start(bf16[2,2,32,512]{3,2,1,0:T(8,128)(2,1)S(1)} %get-tuple-element.81), channel_id=1, source_target_pairs={{0,6},{2,4},{4,2},{6,0},{8,14},{10,12},{12,10},{14,8},{1,7},{3,5},... | collective-permute-start | bytes 393224 | tf_op jit(solution)/shard_map/ppermute | solution.py:566
  87.0 1.4 %collective-permute-start.16 = (bf16[2,32,512]{2,1,0:T(8,128)(2,1)S(1)}, bf16[2,32,512]{2,1,0:T(8,128)(2,1)S(1)}, u32[]{:S(2)}, u32[]{:S(2)}) collective-permute-start(bf16[2,32,512]{2,1,0:T(8,128)(2,1)S(1)} %get-tuple-element.77), channel_id=1, source_target_pairs={{0,12},{2,14},{4,8},{6,10},{8,4},{10,6},{12,0},{14,2},{1,13},{3,15... | collective-permute-start | bytes 196616 | tf_op jit(solution)/shard_map/ppermute | solution.py:566
  89.1 2.5 %collective-permute-start.17 = (bf16[2,32,512]{2,1,0:T(8,128)(2,1)S(1)}, bf16[2,32,512]{2,1,0:T(8,128)(2,1)S(1)}, u32[]{:S(2)}, u32[]{:S(2)}) collective-permute-start(bf16[2,32,512]{2,1,0:T(8,128)(2,1)S(1)} %get-tuple-element.78), channel_id=1, source_target_pairs={{0,14},{2,12},{4,10},{6,8},{8,6},{10,4},{12,2},{14,0},{1,15},{3,13... | collective-permute-start | bytes 196616 | tf_op jit(solution)/shard_map/ppermute | solution.py:566
  91.6 1.3 %collect.2.refs_8_ = bf16[2,16,32,512]{3,2,1,0:T(8,128)(2,1)} custom-call(s32[3]{0:T(128)S(1)} %pad_add_fusion.scalars, bf16[2,32,512]{2,1,0:T(8,128)(2,1)S(1)} %collective-permute-done.21.refs_0_, bf16[2,32,512]{2,1,0:T(8,128)(2,1)S(1)} %collective-permute-done.22.refs_1_, bf16[2,32,512]{2,1,0:T(8,128)(2,1)S(1)} %collective-permute-done.23.refs_2_, ...), custom_call_target="tpu_custom_call" | custom-call | tf_op jit(solution)/shard_map/collect/pallas_call | solution.py:521
  93.4 2.6 %collective-permute-done.17.refs_3_ = bf16[2,32,512]{2,1,0:T(8,128)(2,1)S(1)} collective-permute-done((bf16[2,32,512]{2,1,0:T(8,128)(2,1)S(1)}, bf16[2,32,512]{2,1,0:T(8,128)(2,1)S(1)}, u32[]{:S(2)}, u32[]{:S(2)}) %collective-permute-start.17) | collective-permute-done | bytes 65568 | tf_op jit(solution)/shard_map/ppermute | solution.py:566
  96.1 1.5 %collect.3 = bf16[2,16,32,512]{3,2,1,0:T(8,128)(2,1)} custom-call(s32[3]{0:T(128)S(1)} %pad_add_fusion.scalars, bf16[2,32,512]{2,1,0:T(8,128)(2,1)S(1)} %collective-permute-done.14.refs_0_, bf16[2,32,512]{2,1,0:T(8,128)(2,1)S(1)} %collective-permute-done.15.refs_1_, ...), custom_call_target="tpu_custom_call", output_to_operand_aliasing={{}: (9, {})} | custom-call | tf_op jit(solution)/shard_map/collect/pallas_call | solution.py:521
  (71 shorter events, 12.4 us)
Async XLA Ops:
  2.3 19.6 %collective-permute-start.1 = (bf16[3,10,16,512]{3,2,1,0:T(8,128)(2,1)S(1)}, bf16[3,10,16,512]{3,2,1,0:T(8,128)(2,1)S(1)}, u32[]{:S(2)}, u32[]{:S(2)}) collective-permute-start(bf16[3,10,16,512]{3,2,1,0:T(8,128)(2,1)S(1)} %send.2), channel_id=1, source_target_pairs={{0,2},{2,0},{4,6},{6,4},{8,10},{10,8},{12,14},{14,12},{1,3},{3,1},... | collective-permute-start | bytes 1474568 | tf_op jit(solution)/shard_map/ppermute | solution.py:566
  8.1 11.1 %collective-permute-start.4 = (bf16[4,18,512]{2,1,0:T(8,128)(2,1)}, bf16[4,18,512]{2,1,0:T(8,128)(2,1)}, u32[]{:S(2)}, u32[]{:S(2)}) collective-permute-start(bf16[4,18,512]{2,1,0:T(8,128)(2,1)} %get-tuple-element.89), channel_id=1, source_target_pairs={{0,3},{1,2},{2,1},{3,0},{4,7},{5,6},{6,5},{7,4},{8,11},{9,10},{10,... | collective-permute-start | bytes 221192 | tf_op jit(solution)/shard_map/ppermute | solution.py:584
  8.1 11.9 %collective-permute-start.3 = (bf16[4,18,512]{2,1,0:T(8,128)(2,1)}, bf16[4,18,512]{2,1,0:T(8,128)(2,1)}, u32[]{:S(2)}, u32[]{:S(2)}) collective-permute-start(bf16[4,18,512]{2,1,0:T(8,128)(2,1)} %get-tuple-element.90), channel_id=1, source_target_pairs={{0,1},{1,0},{2,3},{3,2},{4,5},{5,4},{6,7},{7,6},{8,9},{9,8},{10,11... | collective-permute-start | bytes 221192 | tf_op jit(solution)/shard_map/ppermute | solution.py:578
  10.2 13.8 %collective-permute-start.2 = (bf16[1,10,16,512]{3,2,1,0:T(8,128)(2,1)}, bf16[1,10,16,512]{3,2,1,0:T(8,128)(2,1)}, u32[]{:S(2)}, u32[]{:S(2)}) collective-permute-start(bf16[1,10,16,512]{3,2,1,0:T(8,128)(2,1)} %get-tuple-element.50), channel_id=1, source_target_pairs={{0,2},{2,0},{4,6},{6,4},{8,10},{10,8},{12,14},{14,12},{1,3},{3,1},... | collective-permute-start | bytes 491528 | tf_op jit(solution)/shard_map/ppermute | solution.py:566
  12.2 18.3 %collective-permute-start = (bf16[3,8,16,512]{3,2,1,0:T(8,128)(2,1)}, bf16[3,8,16,512]{3,2,1,0:T(8,128)(2,1)S(1)}, u32[]{:S(2)}, u32[]{:S(2)}) collective-permute-start(bf16[3,8,16,512]{3,2,1,0:T(8,128)(2,1)} %get-tuple-element.47), channel_id=1, source_target_pairs={{0,2},{2,0},{4,6},{6,4},{8,10},{10,8},{12,14},{14,12},{1,3},{3,1},... | collective-permute-start | bytes 1179656 | tf_op jit(solution)/shard_map/ppermute | solution.py:566
  15.0 10.1 %copy-start.2 = (bf16[3,512,512]{2,1,0:T(8,128)(2,1)S(1)}, bf16[3,512,512]{2,1,0:T(8,128)(2,1)}, u32[]{:S(2)}) copy-start(bf16[3,512,512]{2,1,0:T(8,128)(2,1)} %param.13) | copy-start | bytes 4718596
  15.0 10.1 %copy-start.3 = (bf16[3,512,512]{2,1,0:T(8,128)(2,1)S(1)}, bf16[3,512,512]{2,1,0:T(8,128)(2,1)}, u32[]{:S(2)}) copy-start(bf16[3,512,512]{2,1,0:T(8,128)(2,1)} %param.15) | copy-start | bytes 4718596
  22.5 17.0 %collective-permute-start.7 = (bf16[3,11,16,512]{3,2,1,0:T(8,128)(2,1)S(1)}, bf16[3,11,16,512]{3,2,1,0:T(8,128)(2,1)S(1)}, u32[]{:S(2)}, u32[]{:S(2)}) collective-permute-start(bf16[3,11,16,512]{3,2,1,0:T(8,128)(2,1)S(1)} %join_last.2.last), channel_id=1, source_target_pairs={{0,4},{2,6},{4,8},{6,10},{8,12},{10,14},{12,0},{14,2},{1,5},{3,7},... | collective-permute-start | bytes 1622024 | tf_op jit(solution)/shard_map/ppermute | solution.py:566
  31.1 17.9 %collective-permute-start.5 = (bf16[3,9,16,512]{3,2,1,0:T(8,128)(2,1)S(1)}, bf16[3,9,16,512]{3,2,1,0:T(8,128)(2,1)S(1)}, u32[]{:S(2)}, u32[]{:S(2)}) collective-permute-start(bf16[3,9,16,512]{3,2,1,0:T(8,128)(2,1)S(1)} %join_last.3.last), channel_id=1, source_target_pairs={{0,4},{2,6},{4,8},{6,10},{8,12},{10,14},{12,0},{14,2},{1,5},{3,7},... | collective-permute-start | bytes 1327112 | tf_op jit(solution)/shard_map/ppermute | solution.py:566
  33.0 10.4 %collective-permute-start.6 = (bf16[1,8,16,512]{3,2,1,0:T(8,128)(2,1)S(1)}, bf16[1,8,16,512]{3,2,1,0:T(8,128)(2,1)S(1)}, u32[]{:S(2)}, u32[]{:S(2)}) collective-permute-start(bf16[1,8,16,512]{3,2,1,0:T(8,128)(2,1)S(1)} %copy-done.12), channel_id=1, source_target_pairs={{0,2},{2,0},{4,6},{6,4},{8,10},{10,8},{12,14},{14,12},{1,3},{3,1},... | collective-permute-start | bytes 393224 | tf_op jit(solution)/shard_map/ppermute | solution.py:566
  43.4 17.5 %collective-permute-start.11 = (bf16[4,32,512]{2,1,0:T(8,128)(2,1)S(1)}, bf16[4,32,512]{2,1,0:T(8,128)(2,1)S(1)}, u32[]{:S(2)}, u32[]{:S(2)}) collective-permute-start(bf16[4,32,512]{2,1,0:T(8,128)(2,1)S(1)} %get-tuple-element.67), channel_id=1, source_target_pairs={{0,4},{2,6},{4,0},{6,2},{8,12},{10,14},{12,8},{14,10},{1,5},{3,7},... | collective-permute-start | bytes 393224 | tf_op jit(solution)/shard_map/ppermute | solution.py:566
  43.5 17.9 %collective-permute-start.12 = (bf16[4,32,512]{2,1,0:T(8,128)(2,1)S(1)}, bf16[4,32,512]{2,1,0:T(8,128)(2,1)S(1)}, u32[]{:S(2)}, u32[]{:S(2)}) collective-permute-start(bf16[4,32,512]{2,1,0:T(8,128)(2,1)S(1)} %get-tuple-element.68), channel_id=1, source_target_pairs={{0,8},{2,10},{4,12},{6,14},{8,0},{10,2},{12,4},{14,6},{1,9},{3,11}... | collective-permute-start | bytes 393224 | tf_op jit(solution)/shard_map/ppermute | solution.py:566
  45.8 15.6 %collective-permute-start.13 = (bf16[4,32,512]{2,1,0:T(8,128)(2,1)S(1)}, bf16[4,32,512]{2,1,0:T(8,128)(2,1)S(1)}, u32[]{:S(2)}, u32[]{:S(2)}) collective-permute-start(bf16[4,32,512]{2,1,0:T(8,128)(2,1)S(1)} %get-tuple-element.69), channel_id=1, source_target_pairs={{0,12},{2,14},{4,8},{6,10},{8,4},{10,6},{12,0},{14,2},{1,13},{3,15... | collective-permute-start | bytes 393224 | tf_op jit(solution)/shard_map/ppermute | solution.py:566
  49.1 12.4 %copy-start.7 = (bf16[512,512]{1,0:T(8,128)(2,1)S(1)}, bf16[512,512]{1,0:T(8,128)(2,1)}, u32[]{:S(2)}) copy-start(bf16[512,512]{1,0:T(8,128)(2,1)} %refs_5_.3) | copy-start | bytes 1572868
  49.1 12.4 %copy-start.8 = (bf16[512,512]{1,0:T(8,128)(2,1)S(1)}, bf16[512,512]{1,0:T(8,128)(2,1)}, u32[]{:S(2)}) copy-start(bf16[512,512]{1,0:T(8,128)(2,1)} %refs_6_.3) | copy-start | bytes 1572868
  49.1 12.4 %copy-start.9 = (bf16[512,512]{1,0:T(8,128)(2,1)S(1)}, bf16[512,512]{1,0:T(8,128)(2,1)}, u32[]{:S(2)}) copy-start(bf16[512,512]{1,0:T(8,128)(2,1)} %refs_7_.3) | copy-start | bytes 1572868
  49.1 12.4 %copy-start.10 = (bf16[512,512]{1,0:T(8,128)(2,1)S(1)}, bf16[512,512]{1,0:T(8,128)(2,1)}, u32[]{:S(2)}) copy-start(bf16[512,512]{1,0:T(8,128)(2,1)} %refs_8_.3) | copy-start | bytes 1572868
  49.1 12.4 %copy-start.13 = (f32[512]{0:T(512)S(1)}, f32[512]{0:T(512)}, u32[]{:S(2)}) copy-start(f32[512]{0:T(512)} %param.19) | copy-start | bytes 6148
  56.4 12.2 %collective-permute-start.8 = (bf16[4,32,512]{2,1,0:T(8,128)(2,1)S(1)}, bf16[4,32,512]{2,1,0:T(8,128)(2,1)S(1)}, u32[]{:S(2)}, u32[]{:S(2)}) collective-permute-start(bf16[4,32,512]{2,1,0:T(8,128)(2,1)S(1)} %get-tuple-element.62), channel_id=1, source_target_pairs={{0,8},{2,10},{4,12},{6,14},{8,0},{10,2},{12,4},{14,6},{1,9},{3,11}... | collective-permute-start | bytes 393224 | tf_op jit(solution)/shard_map/ppermute | solution.py:566
  57.2 13.2 %collective-permute-start.9 = (bf16[4,32,512]{2,1,0:T(8,128)(2,1)S(1)}, bf16[4,32,512]{2,1,0:T(8,128)(2,1)S(1)}, u32[]{:S(2)}, u32[]{:S(2)}) collective-permute-start(bf16[4,32,512]{2,1,0:T(8,128)(2,1)S(1)} %get-tuple-element.63), channel_id=1, source_target_pairs={{0,12},{2,14},{4,8},{6,10},{8,4},{10,6},{12,0},{14,2},{1,13},{3,15... | collective-permute-start | bytes 393224 | tf_op jit(solution)/shard_map/ppermute | solution.py:566
  60.9 12.0 %collective-permute-start.10 = (bf16[4,32,512]{2,1,0:T(8,128)(2,1)S(1)}, bf16[4,32,512]{2,1,0:T(8,128)(2,1)S(1)}, u32[]{:S(2)}, u32[]{:S(2)}) collective-permute-start(bf16[4,32,512]{2,1,0:T(8,128)(2,1)S(1)} %get-tuple-element.64), channel_id=1, source_target_pairs={{0,4},{2,6},{4,0},{6,2},{8,12},{10,14},{12,8},{14,10},{1,5},{3,7},... | collective-permute-start | bytes 393224 | tf_op jit(solution)/shard_map/ppermute | solution.py:566
  64.3 15.8 %collective-permute-start.21 = (bf16[2,32,512]{2,1,0:T(8,128)(2,1)S(1)}, bf16[2,32,512]{2,1,0:T(8,128)(2,1)S(1)}, u32[]{:S(2)}, u32[]{:S(2)}) collective-permute-start(bf16[2,32,512]{2,1,0:T(8,128)(2,1)S(1)} %get-tuple-element.83), channel_id=1, source_target_pairs={{0,8},{2,10},{4,12},{6,14},{8,0},{10,2},{12,4},{14,6},{1,9},{3,11}... | collective-permute-start | bytes 196616 | tf_op jit(solution)/shard_map/ppermute | solution.py:566
  68.1 14.2 %collective-permute-start.22 = (bf16[2,32,512]{2,1,0:T(8,128)(2,1)S(1)}, bf16[2,32,512]{2,1,0:T(8,128)(2,1)S(1)}, u32[]{:S(2)}, u32[]{:S(2)}) collective-permute-start(bf16[2,32,512]{2,1,0:T(8,128)(2,1)S(1)} %get-tuple-element.84), channel_id=1, source_target_pairs={{0,10},{2,8},{4,14},{6,12},{8,2},{10,0},{12,6},{14,4},{1,11},{3,9}... | collective-permute-start | bytes 196616 | tf_op jit(solution)/shard_map/ppermute | solution.py:566
  68.7 14.2 %collective-permute-start.23 = (bf16[2,32,512]{2,1,0:T(8,128)(2,1)S(1)}, bf16[2,32,512]{2,1,0:T(8,128)(2,1)S(1)}, u32[]{:S(2)}, u32[]{:S(2)}) collective-permute-start(bf16[2,32,512]{2,1,0:T(8,128)(2,1)S(1)} %get-tuple-element.85), channel_id=1, source_target_pairs={{0,12},{2,14},{4,8},{6,10},{8,4},{10,6},{12,0},{14,2},{1,13},{3,15... | collective-permute-start | bytes 196616 | tf_op jit(solution)/shard_map/ppermute | solution.py:566
  70.4 14.2 %collective-permute-start.24 = (bf16[2,32,512]{2,1,0:T(8,128)(2,1)S(1)}, bf16[2,32,512]{2,1,0:T(8,128)(2,1)S(1)}, u32[]{:S(2)}, u32[]{:S(2)}) collective-permute-start(bf16[2,32,512]{2,1,0:T(8,128)(2,1)S(1)} %get-tuple-element.86), channel_id=1, source_target_pairs={{0,14},{2,12},{4,10},{6,8},{8,6},{10,4},{12,2},{14,0},{1,15},{3,13... | collective-permute-start | bytes 196616 | tf_op jit(solution)/shard_map/ppermute | solution.py:566
  75.8 11.3 %collective-permute-start.14 = (bf16[2,32,512]{2,1,0:T(8,128)(2,1)S(1)}, bf16[2,32,512]{2,1,0:T(8,128)(2,1)S(1)}, u32[]{:S(2)}, u32[]{:S(2)}) collective-permute-start(bf16[2,32,512]{2,1,0:T(8,128)(2,1)S(1)} %get-tuple-element.75), channel_id=1, source_target_pairs={{0,8},{2,10},{4,12},{6,14},{8,0},{10,2},{12,4},{14,6},{1,9},{3,11}... | collective-permute-start | bytes 196616 | tf_op jit(solution)/shard_map/ppermute | solution.py:566
  80.1 9.0 %collective-permute-start.15 = (bf16[2,32,512]{2,1,0:T(8,128)(2,1)S(1)}, bf16[2,32,512]{2,1,0:T(8,128)(2,1)S(1)}, u32[]{:S(2)}, u32[]{:S(2)}) collective-permute-start(bf16[2,32,512]{2,1,0:T(8,128)(2,1)S(1)} %get-tuple-element.76), channel_id=1, source_target_pairs={{0,10},{2,8},{4,14},{6,12},{8,2},{10,0},{12,6},{14,4},{1,11},{3,9}... | collective-permute-start | bytes 196616 | tf_op jit(solution)/shard_map/ppermute | solution.py:566
  82.3 13.8 %collective-permute-start.18 = (bf16[2,2,32,512]{3,2,1,0:T(8,128)(2,1)S(1)}, bf16[2,2,32,512]{3,2,1,0:T(8,128)(2,1)S(1)}, u32[]{:S(2)}, u32[]{:S(2)}) collective-permute-start(bf16[2,2,32,512]{3,2,1,0:T(8,128)(2,1)S(1)} %get-tuple-element.79), channel_id=1, source_target_pairs={{0,2},{2,0},{4,6},{6,4},{8,10},{10,8},{12,14},{14,12},{1,3},{3,1},... | collective-permute-start | bytes 393224 | tf_op jit(solution)/shard_map/ppermute | solution.py:566
  82.8 13.2 %collective-permute-start.19 = (bf16[2,2,32,512]{3,2,1,0:T(8,128)(2,1)S(1)}, bf16[2,2,32,512]{3,2,1,0:T(8,128)(2,1)S(1)}, u32[]{:S(2)}, u32[]{:S(2)}) collective-permute-start(bf16[2,2,32,512]{3,2,1,0:T(8,128)(2,1)S(1)} %get-tuple-element.80), channel_id=1, source_target_pairs={{0,4},{2,6},{4,0},{6,2},{8,12},{10,14},{12,8},{14,10},{1,5},{3,7},... | collective-permute-start | bytes 393224 | tf_op jit(solution)/shard_map/ppermute | solution.py:566
  84.6 11.5 %collective-permute-start.20 = (bf16[2,2,32,512]{3,2,1,0:T(8,128)(2,1)S(1)}, bf16[2,2,32,512]{3,2,1,0:T(8,128)(2,1)S(1)}, u32[]{:S(2)}, u32[]{:S(2)}) collective-permute-start(bf16[2,2,32,512]{3,2,1,0:T(8,128)(2,1)S(1)} %get-tuple-element.81), channel_id=1, source_target_pairs={{0,6},{2,4},{4,2},{6,0},{8,14},{10,12},{12,10},{14,8},{1,7},{3,5},... | collective-permute-start | bytes 393224 | tf_op jit(solution)/shard_map/ppermute | solution.py:566
  87.0 6.4 %collective-permute-start.16 = (bf16[2,32,512]{2,1,0:T(8,128)(2,1)S(1)}, bf16[2,32,512]{2,1,0:T(8,128)(2,1)S(1)}, u32[]{:S(2)}, u32[]{:S(2)}) collective-permute-start(bf16[2,32,512]{2,1,0:T(8,128)(2,1)S(1)} %get-tuple-element.77), channel_id=1, source_target_pairs={{0,12},{2,14},{4,8},{6,10},{8,4},{10,6},{12,0},{14,2},{1,13},{3,15... | collective-permute-start | bytes 196616 | tf_op jit(solution)/shard_map/ppermute | solution.py:566
  89.1 7.0 %collective-permute-start.17 = (bf16[2,32,512]{2,1,0:T(8,128)(2,1)S(1)}, bf16[2,32,512]{2,1,0:T(8,128)(2,1)S(1)}, u32[]{:S(2)}, u32[]{:S(2)}) collective-permute-start(bf16[2,32,512]{2,1,0:T(8,128)(2,1)S(1)} %get-tuple-element.78), channel_id=1, source_target_pairs={{0,14},{2,12},{4,10},{6,8},{8,6},{10,4},{12,2},{14,0},{1,15},{3,13... | collective-permute-start | bytes 196616 | tf_op jit(solution)/shard_map/ppermute | solution.py:566
  (8 other events, 54.8 us)

commit v19 on v17

--- a/solution.py
+++ b/solution.py
@@ -582,14 +582,22 @@
         for i in range(devices)
         for c in range(columns)
     ]
-    other_edge = lax.ppermute(other_edge, ("tm", "cols"), aslant)
+    other_edges = []
+    for k, (begin, end) in enumerate(spans):
+        cut_edge = other_edge[:, begin:end]
+        if k:
+            cut_edge = after(cut_edge, received[1])
+        other_edges.append(lax.ppermute(cut_edge, ("tm", "cols"), aslant))
 
     def edge_rows(edge, begin, end):
         cut = jnp.pad(edge[:, begin:end], ((0, 0), (0, -(end - begin) % width), (0, 0)))
         return cut.reshape(frames, -1, width, channels)
 
     owners = levels if direct else 1
-    edges = [[edge_rows(e, begin, end) for e in (own_edge, other_edge)] for begin, end in spans]
+    edges = [
+        [edge_rows(own_edge, begin, end), edge_rows(other, 0, end - begin)]
+        for other, (begin, end) in zip(other_edges, spans)
+    ]
     lasts, firsts, halos = [], [], []
     newest = w_space
     for k, (begin, end) in enumerate(spans):

time: 95 us -> 107 us (1.13)
  waiting for transfers between devices: 16.5 us -> 28.5 us
    ppermute x1 -> x2, waiting for transfers between devices: 6.52 us -> 13.3 us  [per_device(): other_edges.append(lax.ppermute(cut_edge, ('tm', 'cols'), aslant))]
    ppermute x23, waiting for transfers between devices: 9.94 us -> 15.2 us  [tm_permute(): lax.ppermute(value, 'tm', [(i, move(i)) for i in range(devices) if move(i...]
  transfers between devices with their start and end apart: 25 -> 26, of which waited for: 8 -> 9; matrix products, arithmetic and copies ran while one was open for 5% -> 5% of each run, Pallas kernels for 27% -> 24%
where the time goes in v19:
time: 107 us
  starting transfers between devices  43.2 us (40%)
  waiting for transfers between devices  28.5 us (27%)
  Pallas kernels  27.7 us (26%)
  local copies, waits for them, and re-layouts  3.75 us (4%)
  other arithmetic  2.98 us (3%)
    ppermute x23, starting transfers between devices, tm_permute(): lax.ppermute(value, 'tm', [(i, move(i)) for i in range(devices) if move(i...  42.9 us
    ppermute x23, waiting for transfers between devices, tm_permute(): lax.ppermute(value, 'tm', [(i, move(i)) for i in range(devices) if move(i...  15.2 us
    ppermute x2, waiting for transfers between devices, per_device(): other_edges.append(lax.ppermute(cut_edge, ('tm', 'cols'), aslant))  13.3 us
    pallas_call x1, Pallas kernels, full(): pl.pallas_call(partial(full_kernel, owners, final, rows), out_shape=[jax....  7.33 us
    pallas_call x2, Pallas kernels, attend(): pl.pallas_call(partial(attend_kernel, frames_per, lanes, turns, near, chu...  5.6 us
    pallas_call x1, Pallas kernels, early(): pl.pallas_call(partial(early_kernel, final, rows), out_shape=shapes, in_s...  5.05 us
    pallas_call x1, Pallas kernels, late(): pl.pallas_call(partial(late_kernel, owners, final, rows), out_shape=[jax....  3.92 us
    select_n x1, other arithmetic, per_device(): w_space = jnp.where(after(place, video) >= 0, w_space, 0)  2.79 us
  transfers between devices with their start and end apart: 26, of which 9 were waited for; matrix products, arithmetic and copies ran while one was open for 5% of the time, Pallas kernels for 24%

profile of v19, /device:TPU:0, one launch (start us, length us, event | category | flops | bytes accessed | tf_op | source)
XLA Modules:
  0.0 106.6 jit_solution(9894103403059823938)
XLA Ops:
  0.1 1.6 %copy-done = bf16[4,32,16,512]{3,2,1,0:T(8,128)(2,1)S(1)} copy-done((bf16[4,32,16,512]{3,2,1,0:T(8,128)(2,1)S(1)}, bf16[4,32,16,512]{3,2,1,0:T(8,128)(2,1)}, u32[]{:S(2)}) %copy-start) | copy-done | bytes 2097176
  2.3 3.0 %collective-permute-start.1 = (bf16[3,10,16,512]{3,2,1,0:T(8,128)(2,1)S(1)}, bf16[3,10,16,512]{3,2,1,0:T(8,128)(2,1)S(1)}, u32[]{:S(2)}, u32[]{:S(2)}) collective-permute-start(bf16[3,10,16,512]{3,2,1,0:T(8,128)(2,1)S(1)} %get-tuple-element.48), channel_id=1, source_target_pairs={{0,2},{2,0},{4,6},{6,4},{8,10},{10,8},{12,14},{14,12},{1,3},{3,1},... | collective-permute-start | bytes 1474568 | tf_op jit(solution)/shard_map/ppermute | solution.py:570
  5.3 1.9 %fusion.2 = (bf16[4,32,1,512]{3,2,1,0:T(2,128)(2,1)S(1)}, bf16[4,32,1,512]{3,2,1,0:T(2,128)(2,1)S(1)}) fusion(bf16[4,32,16,512]{3,2,1,0:T(8,128)(2,1)} %video.9), kind=kLoop, calls=%fused_computation.12 | loop fusion | bytes 524288 | tf_op jit(solution)/shard_map/slice | solution.py:574
  7.7 2.0 %collective-permute-start.2 = (bf16[1,10,16,512]{3,2,1,0:T(8,128)(2,1)S(1)}, bf16[1,10,16,512]{3,2,1,0:T(8,128)(2,1)S(1)}, u32[]{:S(2)}, u32[]{:S(2)}) collective-permute-start(bf16[1,10,16,512]{3,2,1,0:T(8,128)(2,1)S(1)} %get-tuple-element.51), channel_id=1, source_target_pairs={{0,2},{2,0},{4,6},{6,4},{8,10},{10,8},{12,14},{14,12},{1,3},{3,1},... | collective-permute-start | bytes 491528 | tf_op jit(solution)/shard_map/ppermute | solution.py:570
  9.7 2.8 %broadcast_select_fusion.w_space = bf16[9,512,512]{2,1,0:T(8,128)(2,1)S(1)} fusion(bf16[9,512,512]{2,1,0:T(8,128)(2,1)} %param.17, pred[]{:T(512)S(6)} %ge.3), kind=kLoop, calls=%fused_computation | loop fusion | flops 2359296 | bytes 9437185 | tf_op jit(solution)/shard_map/jit(_where)/select_n | solution.py:555
  12.6 5.7 %collective-permute-done.4 = bf16[4,10,512]{2,1,0:T(8,128)(2,1)S(1)} collective-permute-done((bf16[4,10,512]{2,1,0:T(8,128)(2,1)S(1)}, bf16[4,10,512]{2,1,0:T(8,128)(2,1)S(1)}, u32[]{:S(2)}, u32[]{:S(2)}) %collective-permute-start.4) | collective-permute-done | bytes 40992 | tf_op jit(solution)/shard_map/ppermute | solution.py:590
  18.5 3.8 %collective-permute-done.2.others = bf16[1,10,16,512]{3,2,1,0:T(8,128)(2,1)S(1)} collective-permute-done((bf16[1,10,16,512]{3,2,1,0:T(8,128)(2,1)S(1)}, bf16[1,10,16,512]{3,2,1,0:T(8,128)(2,1)S(1)}, u32[]{:S(2)}, u32[]{:S(2)}) %collective-permute-start.2) | collective-permute-done | bytes 163872 | tf_op jit(solution)/shard_map/ppermute | solution.py:570
  22.3 7.5 %collective-permute-done.5 = bf16[4,8,512]{2,1,0:T(8,128)(2,1)S(1)} collective-permute-done((bf16[4,8,512]{2,1,0:T(8,128)(2,1)S(1)}, bf16[4,8,512]{2,1,0:T(8,128)(2,1)S(1)}, u32[]{:S(2)}, u32[]{:S(2)}) %collective-permute-start.5) | collective-permute-done | bytes 32800 | tf_op jit(solution)/shard_map/ppermute | solution.py:590
  30.5 1.6 %collective-permute-start.8 = (bf16[3,11,16,512]{3,2,1,0:T(8,128)(2,1)S(1)}, bf16[3,11,16,512]{3,2,1,0:T(8,128)(2,1)S(1)}, u32[]{:S(2)}, u32[]{:S(2)}) collective-permute-start(bf16[3,11,16,512]{3,2,1,0:T(8,128)(2,1)S(1)} %join_last.2.last), channel_id=1, source_target_pairs={{0,4},{2,6},{4,8},{6,10},{8,12},{10,14},{12,0},{14,2},{1,5},{3,7},... | collective-permute-start | bytes 1622024 | tf_op jit(solution)/shard_map/ppermute | solution.py:570
  32.8 5.1 %early.1 = (f32[176,512]{1,0:T(8,128)S(1)}, bf16[2,128,512]{2,1,0:T(8,128)(2,1)S(1)}, bf16[3,2,2,16,512]{4,3,2,1,0:T(8,128)(2,1)S(1)}) custom-call(s32[3]{0:T(128)S(1)} %pad_add_fusion.scalars, bf16[5,11,16,512]{3,2,1,0:T(8,128)(2,1)S(1)} %join_first.2.first, bf16[3,11,16,512]{3,2,1,0:T(8,128)(2,1)S(1)} %join_last.2.last, bf16[1536,512]{1,0:T(8,128)(2,1)S(1)} %bitcast.26, ...), custom_call_target="tpu_custom_call" | custom-call | flops 3607101440 | bytes 9312256 | tf_op jit(solution)/shard_map/early/pallas_call | solution.py:239
  38.4 1.6 %collective-permute-start.6 = (bf16[3,9,16,512]{3,2,1,0:T(8,128)(2,1)S(1)}, bf16[3,9,16,512]{3,2,1,0:T(8,128)(2,1)S(1)}, u32[]{:S(2)}, u32[]{:S(2)}) collective-permute-start(bf16[3,9,16,512]{3,2,1,0:T(8,128)(2,1)S(1)} %join_last.3.last), channel_id=1, source_target_pairs={{0,4},{2,6},{4,8},{6,10},{8,12},{10,14},{12,0},{14,2},{1,5},{3,7},... | collective-permute-start | bytes 1327112 | tf_op jit(solution)/shard_map/ppermute | solution.py:570
  40.1 1.3 %collective-permute-start.7 = (bf16[1,8,16,512]{3,2,1,0:T(8,128)(2,1)S(1)}, bf16[1,8,16,512]{3,2,1,0:T(8,128)(2,1)S(1)}, u32[]{:S(2)}, u32[]{:S(2)}) collective-permute-start(bf16[1,8,16,512]{3,2,1,0:T(8,128)(2,1)S(1)} %get-tuple-element.57), channel_id=1, source_target_pairs={{0,2},{2,0},{4,6},{6,4},{8,10},{10,8},{12,14},{14,12},{1,3},{3,1},... | collective-permute-start | bytes 393224 | tf_op jit(solution)/shard_map/ppermute | solution.py:570
  41.4 6.1 %collective-permute-done.8.halo = bf16[3,11,16,512]{3,2,1,0:T(8,128)(2,1)S(1)} collective-permute-done((bf16[3,11,16,512]{3,2,1,0:T(8,128)(2,1)S(1)}, bf16[3,11,16,512]{3,2,1,0:T(8,128)(2,1)S(1)}, u32[]{:S(2)}, u32[]{:S(2)}) %collective-permute-start.8) | collective-permute-done | bytes 540704 | tf_op jit(solution)/shard_map/ppermute | solution.py:570
  47.5 3.9 %late.1 = (bf16[4,32,512]{2,1,0:T(8,128)(2,1)S(1)}, bf16[4,32,512]{2,1,0:T(8,128)(2,1)S(1)}, bf16[4,32,512]{2,1,0:T(8,128)(2,1)S(1)}, bf16[4,32,512]{2,1,0:T(8,128)(2,1)S(1)}, bf16[3,2,2,16,512]{4,3,2,1,0:T(8,128)(2,1)S(1)}) custom-call(s32[3]{0:T(128)S(1)} %pad_add_fusion.scalars, bf16[3,11,16,512]{3,2,1,0:T(8,128)(2,1)S(1)} %collective-permute-done.8.halo, ...), custom_call_target="tpu_custom_call" | custom-call | flops 2407530496 | bytes 9672704 | tf_op jit(solution)/shard_map/late/pallas_call | solution.py:397
  51.5 2.4 %collective-permute-start.13 = (bf16[4,32,512]{2,1,0:T(8,128)(2,1)S(1)}, bf16[4,32,512]{2,1,0:T(8,128)(2,1)S(1)}, u32[]{:S(2)}, u32[]{:S(2)}) collective-permute-start(bf16[4,32,512]{2,1,0:T(8,128)(2,1)S(1)} %get-tuple-element.70), channel_id=1, source_target_pairs={{0,8},{2,10},{4,12},{6,14},{8,0},{10,2},{12,4},{14,6},{1,9},{3,11}... | collective-permute-start | bytes 393224 | tf_op jit(solution)/shard_map/ppermute | solution.py:570
  53.8 2.0 %collective-permute-start.14 = (bf16[4,32,512]{2,1,0:T(8,128)(2,1)S(1)}, bf16[4,32,512]{2,1,0:T(8,128)(2,1)S(1)}, u32[]{:S(2)}, u32[]{:S(2)}) collective-permute-start(bf16[4,32,512]{2,1,0:T(8,128)(2,1)S(1)} %get-tuple-element.71), channel_id=1, source_target_pairs={{0,12},{2,14},{4,8},{6,10},{8,4},{10,6},{12,0},{14,2},{1,13},{3,15... | collective-permute-start | bytes 393224 | tf_op jit(solution)/shard_map/ppermute | solution.py:570
  57.1 7.3 %full.1 = (bf16[4,32,512]{2,1,0:T(8,128)(2,1)S(1)}, bf16[4,32,512]{2,1,0:T(8,128)(2,1)S(1)}, bf16[4,32,512]{2,1,0:T(8,128)(2,1)S(1)}, bf16[4,32,512]{2,1,0:T(8,128)(2,1)S(1)}) custom-call(s32[3]{0:T(128)S(1)} %pad_add_fusion.scalars, bf16[3,9,16,512]{3,2,1,0:T(8,128)(2,1)S(1)} %collective-permute-done.6.halo, bf16[5,9,16,512]{3,2,1,0:T(8,128)(2,1)S(1)} %join_first.3.first, ...), custom_call_target="tpu_custom_call" | custom-call | flops 5360320512 | bytes 9492480 | tf_op jit(solution)/shard_map/full/pallas_call | solution.py:326
  65.2 3.8 %collective-permute-start.10 = (bf16[4,32,512]{2,1,0:T(8,128)(2,1)S(1)}, bf16[4,32,512]{2,1,0:T(8,128)(2,1)S(1)}, u32[]{:S(2)}, u32[]{:S(2)}) collective-permute-start(bf16[4,32,512]{2,1,0:T(8,128)(2,1)S(1)} %get-tuple-element.65), channel_id=1, source_target_pairs={{0,12},{2,14},{4,8},{6,10},{8,4},{10,6},{12,0},{14,2},{1,13},{3,15... | collective-permute-start | bytes 393224 | tf_op jit(solution)/shard_map/ppermute | solution.py:570
  69.5 2.8 %attend.2 = (bf16[2,32,512]{2,1,0:T(8,128)(2,1)S(1)}, bf16[2,32,512]{2,1,0:T(8,128)(2,1)S(1)}, bf16[2,32,512]{2,1,0:T(8,128)(2,1)S(1)}, bf16[2,32,512]{2,1,0:T(8...) custom-call(s32[3]{0:T(128)S(1)} %pad_add_fusion.scalars, ...), custom_call_target="tpu_custom_call" | custom-call | flops 1342177280 | bytes 2621440 | tf_op jit(solution)/shard_map/attend/pallas_call | solution.py:499
  72.3 3.9 %collective-permute-start.22 = (bf16[2,32,512]{2,1,0:T(8,128)(2,1)S(1)}, bf16[2,32,512]{2,1,0:T(8,128)(2,1)S(1)}, u32[]{:S(2)}, u32[]{:S(2)}) collective-permute-start(bf16[2,32,512]{2,1,0:T(8,128)(2,1)S(1)} %get-tuple-element.85), channel_id=1, source_target_pairs={{0,8},{2,10},{4,12},{6,14},{8,0},{10,2},{12,4},{14,6},{1,9},{3,11}... | collective-permute-start | bytes 196616 | tf_op jit(solution)/shard_map/ppermute | solution.py:570
  76.7 2.3 %collective-permute-start.24 = (bf16[2,32,512]{2,1,0:T(8,128)(2,1)S(1)}, bf16[2,32,512]{2,1,0:T(8,128)(2,1)S(1)}, u32[]{:S(2)}, u32[]{:S(2)}) collective-permute-start(bf16[2,32,512]{2,1,0:T(8,128)(2,1)S(1)} %get-tuple-element.87), channel_id=1, source_target_pairs={{0,12},{2,14},{4,8},{6,10},{8,4},{10,6},{12,0},{14,2},{1,13},{3,15... | collective-permute-start | bytes 196616 | tf_op jit(solution)/shard_map/ppermute | solution.py:570
  78.9 3.2 %collective-permute-start.25 = (bf16[2,32,512]{2,1,0:T(8,128)(2,1)S(1)}, bf16[2,32,512]{2,1,0:T(8,128)(2,1)S(1)}, u32[]{:S(2)}, u32[]{:S(2)}) collective-permute-start(bf16[2,32,512]{2,1,0:T(8,128)(2,1)S(1)} %get-tuple-element.88), channel_id=1, source_target_pairs={{0,14},{2,12},{4,10},{6,8},{8,6},{10,4},{12,2},{14,0},{1,15},{3,13... | collective-permute-start | bytes 196616 | tf_op jit(solution)/shard_map/ppermute | solution.py:570
  82.1 2.8 %attend.3 = (bf16[2,32,512]{2,1,0:T(8,128)(2,1)S(1)}, bf16[2,2,32,512]{3,2,1,0:T(8,128)(2,1)S(1)}, bf16[2,2,32,512]{3,2,1,0:T(8,128)(2,1)S(1)}, bf16[2,2,32,512]...) custom-call(s32[3]{0:T(128)S(1)} %pad_add_fusion.scalars, ...), custom_call_target="tpu_custom_call" | custom-call | flops 1342177280 | bytes 2621440 | tf_op jit(solution)/shard_map/attend/pallas_call | solution.py:499
  84.9 6.7 %collective-permute-start.15 = (bf16[2,32,512]{2,1,0:T(8,128)(2,1)S(1)}, bf16[2,32,512]{2,1,0:T(8,128)(2,1)S(1)}, u32[]{:S(2)}, u32[]{:S(2)}) collective-permute-start(bf16[2,32,512]{2,1,0:T(8,128)(2,1)S(1)} %get-tuple-element.77), channel_id=1, source_target_pairs={{0,8},{2,10},{4,12},{6,14},{8,0},{10,2},{12,4},{14,6},{1,9},{3,11}... | collective-permute-start | bytes 196616 | tf_op jit(solution)/shard_map/ppermute | solution.py:570
  91.6 1.5 %collective-permute-start.19 = (bf16[2,2,32,512]{3,2,1,0:T(8,128)(2,1)S(1)}, bf16[2,2,32,512]{3,2,1,0:T(8,128)(2,1)S(1)}, u32[]{:S(2)}, u32[]{:S(2)}) collective-permute-start(bf16[2,2,32,512]{3,2,1,0:T(8,128)(2,1)S(1)} %get-tuple-element.81), channel_id=1, source_target_pairs={{0,2},{2,0},{4,6},{6,4},{8,10},{10,8},{12,14},{14,12},{1,3},{3,1},... | collective-permute-start | bytes 393224 | tf_op jit(solution)/shard_map/ppermute | solution.py:570
  93.2 2.0 %collective-permute-start.20 = (bf16[2,2,32,512]{3,2,1,0:T(8,128)(2,1)S(1)}, bf16[2,2,32,512]{3,2,1,0:T(8,128)(2,1)S(1)}, u32[]{:S(2)}, u32[]{:S(2)}) collective-permute-start(bf16[2,2,32,512]{3,2,1,0:T(8,128)(2,1)S(1)} %get-tuple-element.82), channel_id=1, source_target_pairs={{0,4},{2,6},{4,0},{6,2},{8,12},{10,14},{12,8},{14,10},{1,5},{3,7},... | collective-permute-start | bytes 393224 | tf_op jit(solution)/shard_map/ppermute | solution.py:570
  95.2 2.4 %collective-permute-start.17 = (bf16[2,32,512]{2,1,0:T(8,128)(2,1)S(1)}, bf16[2,32,512]{2,1,0:T(8,128)(2,1)S(1)}, u32[]{:S(2)}, u32[]{:S(2)}) collective-permute-start(bf16[2,32,512]{2,1,0:T(8,128)(2,1)S(1)} %get-tuple-element.79), channel_id=1, source_target_pairs={{0,12},{2,14},{4,8},{6,10},{8,4},{10,6},{12,0},{14,2},{1,13},{3,15... | collective-permute-start | bytes 196616 | tf_op jit(solution)/shard_map/ppermute | solution.py:570
  98.0 2.0 %collective-permute-start.18 = (bf16[2,32,512]{2,1,0:T(8,128)(2,1)S(1)}, bf16[2,32,512]{2,1,0:T(8,128)(2,1)S(1)}, u32[]{:S(2)}, u32[]{:S(2)}) collective-permute-start(bf16[2,32,512]{2,1,0:T(8,128)(2,1)S(1)} %get-tuple-element.80), channel_id=1, source_target_pairs={{0,14},{2,12},{4,10},{6,8},{8,6},{10,4},{12,2},{14,0},{1,15},{3,13... | collective-permute-start | bytes 196616 | tf_op jit(solution)/shard_map/ppermute | solution.py:570
  100.0 1.3 %collect.2.refs_8_ = bf16[2,16,32,512]{3,2,1,0:T(8,128)(2,1)} custom-call(s32[3]{0:T(128)S(1)} %pad_add_fusion.scalars, bf16[2,32,512]{2,1,0:T(8,128)(2,1)S(1)} %collective-permute-done.22.refs_0_, bf16[2,32,512]{2,1,0:T(8,128)(2,1)S(1)} %collective-permute-done.23.refs_1_, bf16[2,32,512]{2,1,0:T(8,128)(2,1)S(1)} %collective-permute-done.24.refs_2_, ...), custom_call_target="tpu_custom_call" | custom-call | tf_op jit(solution)/shard_map/collect/pallas_call | solution.py:525
  101.3 2.3 %collective-permute-done.17.refs_2_ = bf16[2,32,512]{2,1,0:T(8,128)(2,1)S(1)} collective-permute-done((bf16[2,32,512]{2,1,0:T(8,128)(2,1)S(1)}, bf16[2,32,512]{2,1,0:T(8,128)(2,1)S(1)}, u32[]{:S(2)}, u32[]{:S(2)}) %collective-permute-start.17) | collective-permute-done | bytes 65568 | tf_op jit(solution)/shard_map/ppermute | solution.py:570
  103.6 1.4 %collective-permute-done.18.refs_3_ = bf16[2,32,512]{2,1,0:T(8,128)(2,1)S(1)} collective-permute-done((bf16[2,32,512]{2,1,0:T(8,128)(2,1)S(1)}, bf16[2,32,512]{2,1,0:T(8,128)(2,1)S(1)}, u32[]{:S(2)}, u32[]{:S(2)}) %collective-permute-start.18) | collective-permute-done | bytes 65568 | tf_op jit(solution)/shard_map/ppermute | solution.py:570
  105.0 1.5 %collect.3 = bf16[2,16,32,512]{3,2,1,0:T(8,128)(2,1)} custom-call(s32[3]{0:T(128)S(1)} %pad_add_fusion.scalars, bf16[2,32,512]{2,1,0:T(8,128)(2,1)S(1)} %collective-permute-done.15.refs_0_, bf16[2,32,512]{2,1,0:T(8,128)(2,1)S(1)} %collective-permute-done.16.refs_1_, ...), custom_call_target="tpu_custom_call", output_to_operand_aliasing={{}: (9, {})} | custom-call | tf_op jit(solution)/shard_map/collect/pallas_call | solution.py:525
  (70 shorter events, 6.6 us)
Async XLA Ops:
  2.3 27.6 %collective-permute-start.1 = (bf16[3,10,16,512]{3,2,1,0:T(8,128)(2,1)S(1)}, bf16[3,10,16,512]{3,2,1,0:T(8,128)(2,1)S(1)}, u32[]{:S(2)}, u32[]{:S(2)}) collective-permute-start(bf16[3,10,16,512]{3,2,1,0:T(8,128)(2,1)S(1)} %get-tuple-element.48), channel_id=1, source_target_pairs={{0,2},{2,0},{4,6},{6,4},{8,10},{10,8},{12,14},{14,12},{1,3},{3,1},... | collective-permute-start | bytes 1474568 | tf_op jit(solution)/shard_map/ppermute | solution.py:570
  7.4 11.0 %collective-permute-start.4 = (bf16[4,10,512]{2,1,0:T(8,128)(2,1)S(1)}, bf16[4,10,512]{2,1,0:T(8,128)(2,1)S(1)}, u32[]{:S(2)}, u32[]{:S(2)}) collective-permute-start(bf16[4,10,512]{2,1,0:T(8,128)(2,1)S(1)} %pad_dynamic-slice_fusion), channel_id=1, source_target_pairs={{0,3},{1,2},{2,1},{3,0},{4,7},{5,6},{6,5},{7,4},{8,11},{9,10},{10,... | collective-permute-start | bytes 122888 | tf_op jit(solution)/shard_map/ppermute | solution.py:590
  7.5 10.8 %collective-permute-start.3 = (bf16[4,18,512]{2,1,0:T(8,128)(2,1)S(1)}, bf16[4,18,512]{2,1,0:T(8,128)(2,1)S(1)}, u32[]{:S(2)}, u32[]{:S(2)}) collective-permute-start(bf16[4,18,512]{2,1,0:T(8,128)(2,1)S(1)} %pad_dynamic-slice_fusion.2), channel_id=1, source_target_pairs={{0,1},{1,0},{2,3},{3,2},{4,5},{5,4},{6,7},{7,6},{8,9},{9,8},{10,11... | collective-permute-start | bytes 221192 | tf_op jit(solution)/shard_map/ppermute | solution.py:579
  7.7 14.6 %collective-permute-start.2 = (bf16[1,10,16,512]{3,2,1,0:T(8,128)(2,1)S(1)}, bf16[1,10,16,512]{3,2,1,0:T(8,128)(2,1)S(1)}, u32[]{:S(2)}, u32[]{:S(2)}) collective-permute-start(bf16[1,10,16,512]{3,2,1,0:T(8,128)(2,1)S(1)} %get-tuple-element.51), channel_id=1, source_target_pairs={{0,2},{2,0},{4,6},{6,4},{8,10},{10,8},{12,14},{14,12},{1,3},{3,1},... | collective-permute-start | bytes 491528 | tf_op jit(solution)/shard_map/ppermute | solution.py:570
  9.7 28.1 %collective-permute-start = (bf16[3,8,16,512]{3,2,1,0:T(8,128)(2,1)S(1)}, bf16[3,8,16,512]{3,2,1,0:T(8,128)(2,1)S(1)}, u32[]{:S(2)}, u32[]{:S(2)}) collective-permute-start(bf16[3,8,16,512]{3,2,1,0:T(8,128)(2,1)S(1)} %get-tuple-element.47), channel_id=1, source_target_pairs={{0,2},{2,0},{4,6},{6,4},{8,10},{10,8},{12,14},{14,12},{1,3},{3,1},... | collective-permute-start | bytes 1179656 | tf_op jit(solution)/shard_map/ppermute | solution.py:570
  9.7 20.1 %copy-start.1 = (bf16[4,32,16,512]{3,2,1,0:T(8,128)(2,1)S(1)}, bf16[4,32,16,512]{3,2,1,0:T(8,128)(2,1)}, u32[]{:S(2)}) copy-start(bf16[4,32,16,512]{3,2,1,0:T(8,128)(2,1)} %video.9) | copy-start | bytes 6291460
  12.5 20.2 %copy-start.2 = (bf16[3,512,512]{2,1,0:T(8,128)(2,1)S(1)}, bf16[3,512,512]{2,1,0:T(8,128)(2,1)}, u32[]{:S(2)}) copy-start(bf16[3,512,512]{2,1,0:T(8,128)(2,1)} %param.13) | copy-start | bytes 4718596
  12.6 20.2 %copy-start.3 = (bf16[3,512,512]{2,1,0:T(8,128)(2,1)S(1)}, bf16[3,512,512]{2,1,0:T(8,128)(2,1)}, u32[]{:S(2)}) copy-start(bf16[3,512,512]{2,1,0:T(8,128)(2,1)} %param.15) | copy-start | bytes 4718596
  12.6 20.2 %copy-start.4 = (f32[512]{0:T(512)S(1)}, f32[512]{0:T(512)}, u32[]{:S(2)}) copy-start(f32[512]{0:T(512)} %param.14) | copy-start | bytes 6148
  12.6 20.2 %copy-start.5 = (f32[512]{0:T(512)S(1)}, f32[512]{0:T(512)}, u32[]{:S(2)}) copy-start(f32[512]{0:T(512)} %param.16) | copy-start | bytes 6148
  12.6 20.2 %copy-start.6 = (f32[512]{0:T(512)S(1)}, f32[512]{0:T(512)}, u32[]{:S(2)}) copy-start(f32[512]{0:T(512)} %param.18) | copy-start | bytes 6148
  22.3 7.6 %collective-permute-start.5 = (bf16[4,8,512]{2,1,0:T(8,128)(2,1)S(1)}, bf16[4,8,512]{2,1,0:T(8,128)(2,1)S(1)}, u32[]{:S(2)}, u32[]{:S(2)}) collective-permute-start(bf16[4,8,512]{2,1,0:T(8,128)(2,1)S(1)} %pad_dynamic-slice_fusion.1), channel_id=1, source_target_pairs={{0,3},{1,2},{2,1},{3,0},{4,7},{5,6},{6,5},{7,4},{8,11},{9,10},{10,... | collective-permute-start | bytes 98312 | tf_op jit(solution)/shard_map/ppermute | solution.py:590
  30.5 17.0 %collective-permute-start.8 = (bf16[3,11,16,512]{3,2,1,0:T(8,128)(2,1)S(1)}, bf16[3,11,16,512]{3,2,1,0:T(8,128)(2,1)S(1)}, u32[]{:S(2)}, u32[]{:S(2)}) collective-permute-start(bf16[3,11,16,512]{3,2,1,0:T(8,128)(2,1)S(1)} %join_last.2.last), channel_id=1, source_target_pairs={{0,4},{2,6},{4,8},{6,10},{8,12},{10,14},{12,0},{14,2},{1,5},{3,7},... | collective-permute-start | bytes 1622024 | tf_op jit(solution)/shard_map/ppermute | solution.py:570
  38.4 18.7 %collective-permute-start.6 = (bf16[3,9,16,512]{3,2,1,0:T(8,128)(2,1)S(1)}, bf16[3,9,16,512]{3,2,1,0:T(8,128)(2,1)S(1)}, u32[]{:S(2)}, u32[]{:S(2)}) collective-permute-start(bf16[3,9,16,512]{3,2,1,0:T(8,128)(2,1)S(1)} %join_last.3.last), channel_id=1, source_target_pairs={{0,4},{2,6},{4,8},{6,10},{8,12},{10,14},{12,0},{14,2},{1,5},{3,7},... | collective-permute-start | bytes 1327112 | tf_op jit(solution)/shard_map/ppermute | solution.py:570
  40.1 11.3 %collective-permute-start.7 = (bf16[1,8,16,512]{3,2,1,0:T(8,128)(2,1)S(1)}, bf16[1,8,16,512]{3,2,1,0:T(8,128)(2,1)S(1)}, u32[]{:S(2)}, u32[]{:S(2)}) collective-permute-start(bf16[1,8,16,512]{3,2,1,0:T(8,128)(2,1)S(1)} %get-tuple-element.57), channel_id=1, source_target_pairs={{0,2},{2,0},{4,6},{6,4},{8,10},{10,8},{12,14},{14,12},{1,3},{3,1},... | collective-permute-start | bytes 393224 | tf_op jit(solution)/shard_map/ppermute | solution.py:570
  51.4 17.5 %collective-permute-start.12 = (bf16[4,32,512]{2,1,0:T(8,128)(2,1)S(1)}, bf16[4,32,512]{2,1,0:T(8,128)(2,1)S(1)}, u32[]{:S(2)}, u32[]{:S(2)}) collective-permute-start(bf16[4,32,512]{2,1,0:T(8,128)(2,1)S(1)} %get-tuple-element.69), channel_id=1, source_target_pairs={{0,4},{2,6},{4,0},{6,2},{8,12},{10,14},{12,8},{14,10},{1,5},{3,7},... | collective-permute-start | bytes 393224 | tf_op jit(solution)/shard_map/ppermute | solution.py:570
  51.5 17.9 %collective-permute-start.13 = (bf16[4,32,512]{2,1,0:T(8,128)(2,1)S(1)}, bf16[4,32,512]{2,1,0:T(8,128)(2,1)S(1)}, u32[]{:S(2)}, u32[]{:S(2)}) collective-permute-start(bf16[4,32,512]{2,1,0:T(8,128)(2,1)S(1)} %get-tuple-element.70), channel_id=1, source_target_pairs={{0,8},{2,10},{4,12},{6,14},{8,0},{10,2},{12,4},{14,6},{1,9},{3,11}... | collective-permute-start | bytes 393224 | tf_op jit(solution)/shard_map/ppermute | solution.py:570
  53.8 15.6 %collective-permute-start.14 = (bf16[4,32,512]{2,1,0:T(8,128)(2,1)S(1)}, bf16[4,32,512]{2,1,0:T(8,128)(2,1)S(1)}, u32[]{:S(2)}, u32[]{:S(2)}) collective-permute-start(bf16[4,32,512]{2,1,0:T(8,128)(2,1)S(1)} %get-tuple-element.71), channel_id=1, source_target_pairs={{0,12},{2,14},{4,8},{6,10},{8,4},{10,6},{12,0},{14,2},{1,13},{3,15... | collective-permute-start | bytes 393224 | tf_op jit(solution)/shard_map/ppermute | solution.py:570
  64.4 12.2 %collective-permute-start.9 = (bf16[4,32,512]{2,1,0:T(8,128)(2,1)S(1)}, bf16[4,32,512]{2,1,0:T(8,128)(2,1)S(1)}, u32[]{:S(2)}, u32[]{:S(2)}) collective-permute-start(bf16[4,32,512]{2,1,0:T(8,128)(2,1)S(1)} %get-tuple-element.64), channel_id=1, source_target_pairs={{0,8},{2,10},{4,12},{6,14},{8,0},{10,2},{12,4},{14,6},{1,9},{3,11}... | collective-permute-start | bytes 393224 | tf_op jit(solution)/shard_map/ppermute | solution.py:570
  65.2 13.8 %collective-permute-start.10 = (bf16[4,32,512]{2,1,0:T(8,128)(2,1)S(1)}, bf16[4,32,512]{2,1,0:T(8,128)(2,1)S(1)}, u32[]{:S(2)}, u32[]{:S(2)}) collective-permute-start(bf16[4,32,512]{2,1,0:T(8,128)(2,1)S(1)} %get-tuple-element.65), channel_id=1, source_target_pairs={{0,12},{2,14},{4,8},{6,10},{8,4},{10,6},{12,0},{14,2},{1,13},{3,15... | collective-permute-start | bytes 393224 | tf_op jit(solution)/shard_map/ppermute | solution.py:570
  68.9 13.2 %collective-permute-start.11 = (bf16[4,32,512]{2,1,0:T(8,128)(2,1)S(1)}, bf16[4,32,512]{2,1,0:T(8,128)(2,1)S(1)}, u32[]{:S(2)}, u32[]{:S(2)}) collective-permute-start(bf16[4,32,512]{2,1,0:T(8,128)(2,1)S(1)} %get-tuple-element.66), channel_id=1, source_target_pairs={{0,4},{2,6},{4,0},{6,2},{8,12},{10,14},{12,8},{14,10},{1,5},{3,7},... | collective-permute-start | bytes 393224 | tf_op jit(solution)/shard_map/ppermute | solution.py:570
  72.3 19.3 %collective-permute-start.22 = (bf16[2,32,512]{2,1,0:T(8,128)(2,1)S(1)}, bf16[2,32,512]{2,1,0:T(8,128)(2,1)S(1)}, u32[]{:S(2)}, u32[]{:S(2)}) collective-permute-start(bf16[2,32,512]{2,1,0:T(8,128)(2,1)S(1)} %get-tuple-element.85), channel_id=1, source_target_pairs={{0,8},{2,10},{4,12},{6,14},{8,0},{10,2},{12,4},{14,6},{1,9},{3,11}... | collective-permute-start | bytes 196616 | tf_op jit(solution)/shard_map/ppermute | solution.py:570
  76.1 15.5 %collective-permute-start.23 = (bf16[2,32,512]{2,1,0:T(8,128)(2,1)S(1)}, bf16[2,32,512]{2,1,0:T(8,128)(2,1)S(1)}, u32[]{:S(2)}, u32[]{:S(2)}) collective-permute-start(bf16[2,32,512]{2,1,0:T(8,128)(2,1)S(1)} %get-tuple-element.86), channel_id=1, source_target_pairs={{0,10},{2,8},{4,14},{6,12},{8,2},{10,0},{12,6},{14,4},{1,11},{3,9}... | collective-permute-start | bytes 196616 | tf_op jit(solution)/shard_map/ppermute | solution.py:570
  76.7 16.5 %collective-permute-start.24 = (bf16[2,32,512]{2,1,0:T(8,128)(2,1)S(1)}, bf16[2,32,512]{2,1,0:T(8,128)(2,1)S(1)}, u32[]{:S(2)}, u32[]{:S(2)}) collective-permute-start(bf16[2,32,512]{2,1,0:T(8,128)(2,1)S(1)} %get-tuple-element.87), channel_id=1, source_target_pairs={{0,12},{2,14},{4,8},{6,10},{8,4},{10,6},{12,0},{14,2},{1,13},{3,15... | collective-permute-start | bytes 196616 | tf_op jit(solution)/shard_map/ppermute | solution.py:570
  78.9 16.2 %collective-permute-start.25 = (bf16[2,32,512]{2,1,0:T(8,128)(2,1)S(1)}, bf16[2,32,512]{2,1,0:T(8,128)(2,1)S(1)}, u32[]{:S(2)}, u32[]{:S(2)}) collective-permute-start(bf16[2,32,512]{2,1,0:T(8,128)(2,1)S(1)} %get-tuple-element.88), channel_id=1, source_target_pairs={{0,14},{2,12},{4,10},{6,8},{8,6},{10,4},{12,2},{14,0},{1,15},{3,13... | collective-permute-start | bytes 196616 | tf_op jit(solution)/shard_map/ppermute | solution.py:570
  84.9 10.3 %collective-permute-start.15 = (bf16[2,32,512]{2,1,0:T(8,128)(2,1)S(1)}, bf16[2,32,512]{2,1,0:T(8,128)(2,1)S(1)}, u32[]{:S(2)}, u32[]{:S(2)}) collective-permute-start(bf16[2,32,512]{2,1,0:T(8,128)(2,1)S(1)} %get-tuple-element.77), channel_id=1, source_target_pairs={{0,8},{2,10},{4,12},{6,14},{8,0},{10,2},{12,4},{14,6},{1,9},{3,11}... | collective-permute-start | bytes 196616 | tf_op jit(solution)/shard_map/ppermute | solution.py:570
  91.6 6.4 %collective-permute-start.16 = (bf16[2,32,512]{2,1,0:T(8,128)(2,1)S(1)}, bf16[2,32,512]{2,1,0:T(8,128)(2,1)S(1)}, u32[]{:S(2)}, u32[]{:S(2)}) collective-permute-start(bf16[2,32,512]{2,1,0:T(8,128)(2,1)S(1)} %get-tuple-element.78), channel_id=1, source_target_pairs={{0,10},{2,8},{4,14},{6,12},{8,2},{10,0},{12,6},{14,4},{1,11},{3,9}... | collective-permute-start | bytes 196616 | tf_op jit(solution)/shard_map/ppermute | solution.py:570
  91.6 13.3 %collective-permute-start.19 = (bf16[2,2,32,512]{3,2,1,0:T(8,128)(2,1)S(1)}, bf16[2,2,32,512]{3,2,1,0:T(8,128)(2,1)S(1)}, u32[]{:S(2)}, u32[]{:S(2)}) collective-permute-start(bf16[2,2,32,512]{3,2,1,0:T(8,128)(2,1)S(1)} %get-tuple-element.81), channel_id=1, source_target_pairs={{0,2},{2,0},{4,6},{6,4},{8,10},{10,8},{12,14},{14,12},{1,3},{3,1},... | collective-permute-start | bytes 393224 | tf_op jit(solution)/shard_map/ppermute | solution.py:570
  93.2 11.8 %collective-permute-start.20 = (bf16[2,2,32,512]{3,2,1,0:T(8,128)(2,1)S(1)}, bf16[2,2,32,512]{3,2,1,0:T(8,128)(2,1)S(1)}, u32[]{:S(2)}, u32[]{:S(2)}) collective-permute-start(bf16[2,2,32,512]{3,2,1,0:T(8,128)(2,1)S(1)} %get-tuple-element.82), channel_id=1, source_target_pairs={{0,4},{2,6},{4,0},{6,2},{8,12},{10,14},{12,8},{14,10},{1,5},{3,7},... | collective-permute-start | bytes 393224 | tf_op jit(solution)/shard_map/ppermute | solution.py:570
  95.2 9.8 %collective-permute-start.21 = (bf16[2,2,32,512]{3,2,1,0:T(8,128)(2,1)S(1)}, bf16[2,2,32,512]{3,2,1,0:T(8,128)(2,1)S(1)}, u32[]{:S(2)}, u32[]{:S(2)}) collective-permute-start(bf16[2,2,32,512]{3,2,1,0:T(8,128)(2,1)S(1)} %get-tuple-element.83), channel_id=1, source_target_pairs={{0,6},{2,4},{4,2},{6,0},{8,14},{10,12},{12,10},{14,8},{1,7},{3,5},... | collective-permute-start | bytes 393224 | tf_op jit(solution)/shard_map/ppermute | solution.py:570
  95.2 8.4 %collective-permute-start.17 = (bf16[2,32,512]{2,1,0:T(8,128)(2,1)S(1)}, bf16[2,32,512]{2,1,0:T(8,128)(2,1)S(1)}, u32[]{:S(2)}, u32[]{:S(2)}) collective-permute-start(bf16[2,32,512]{2,1,0:T(8,128)(2,1)S(1)} %get-tuple-element.79), channel_id=1, source_target_pairs={{0,12},{2,14},{4,8},{6,10},{8,4},{10,6},{12,0},{14,2},{1,13},{3,15... | collective-permute-start | bytes 196616 | tf_op jit(solution)/shard_map/ppermute | solution.py:570
  98.0 7.0 %collective-permute-start.18 = (bf16[2,32,512]{2,1,0:T(8,128)(2,1)S(1)}, bf16[2,32,512]{2,1,0:T(8,128)(2,1)S(1)}, u32[]{:S(2)}, u32[]{:S(2)}) collective-permute-start(bf16[2,32,512]{2,1,0:T(8,128)(2,1)S(1)} %get-tuple-element.80), channel_id=1, source_target_pairs={{0,14},{2,12},{4,10},{6,8},{8,6},{10,4},{12,2},{14,0},{1,15},{3,13... | collective-permute-start | bytes 196616 | tf_op jit(solution)/shard_map/ppermute | solution.py:570
  (7 other events, 72.1 us)

commit v20 on v17

--- a/solution.py
+++ b/solution.py
@@ -645,8 +645,7 @@
             gathered[0] = after(gathered[0], newest)
             final = k == chunks - 1
             turns = tuple(range(levels))
-            if final:
-                turns = turns[levels // 2 :] + turns[: levels // 2][::-1]
+            turns = turns[levels // 2 :] + turns[: levels // 2][::-1]
             results = attend(
                 scalars, [gathered[j] for j in turns], turns, near if final else 0,
                 waiting if final else [], *attention

time: 95 us -> 96.4 us (1.015)
  waiting for transfers between devices: 16.5 us -> 20.3 us
  starting transfers between devices: 43.5 us -> 41.1 us
    ppermute x23, waiting for transfers between devices: 9.94 us -> 13.8 us  [tm_permute(): lax.ppermute(value, 'tm', [(i, move(i)) for i in range(devices) if move(i...]
    ppermute x23, starting transfers between devices: 43.3 us -> 40.9 us  [tm_permute(): lax.ppermute(value, 'tm', [(i, move(i)) for i in range(devices) if move(i...]
  transfers between devices with their start and end apart: 25 -> 25, of which waited for: 8 -> 9; matrix products, arithmetic and copies ran while one was open for 5% -> 5% of each run, Pallas kernels for 27% -> 27%
where the time goes in v20:
time: 96.4 us; the launch traced here: 96.3 us
  starting transfers between devices  41.1 us (43%)
  Pallas kernels  27.7 us (29%)
  waiting for transfers between devices  20.3 us (21%)
  local copies, waits for them, and re-layouts  3.73 us (4%)
  other arithmetic  2.99 us (3%)
    ppermute x23, starting transfers between devices, tm_permute(): lax.ppermute(value, 'tm', [(i, move(i)) for i in range(devices) if move(i...  40.9 us
    ppermute x23, waiting for transfers between devices, tm_permute(): lax.ppermute(value, 'tm', [(i, move(i)) for i in range(devices) if move(i...  13.8 us
    pallas_call x1, Pallas kernels, full(): pl.pallas_call(partial(full_kernel, owners, final, rows), out_shape=[jax....  7.33 us
    ppermute x1, waiting for transfers between devices, per_device(): other_edge = lax.ppermute(other_edge, ('tm', 'cols'), aslant)  6.52 us
    pallas_call x2, Pallas kernels, attend(): pl.pallas_call(partial(attend_kernel, frames_per, lanes, turns, near, chu...  5.61 us
    pallas_call x1, Pallas kernels, early(): pl.pallas_call(partial(early_kernel, final, rows), out_shape=shapes, in_s...  5.03 us
    pallas_call x1, Pallas kernels, late(): pl.pallas_call(partial(late_kernel, owners, final, rows), out_shape=[jax....  3.91 us
    select_n x1, other arithmetic, per_device(): w_space = jnp.where(after(place, video) >= 0, w_space, 0)  2.79 us
  transfers between devices with their start and end apart: 25, of which 9 were waited for; matrix products, arithmetic and copies ran while one was open for 5% of the time, Pallas kernels for 27%

profile of v20, /device:TPU:0, one launch (start us, length us, event | category | flops | bytes accessed | tf_op | source)
XLA Modules:
  0.0 96.3 jit_solution(15738766300012624111)
XLA Ops:
  0.1 1.6 %copy-done = bf16[4,32,16,512]{3,2,1,0:T(8,128)(2,1)S(1)} copy-done((bf16[4,32,16,512]{3,2,1,0:T(8,128)(2,1)S(1)}, bf16[4,32,16,512]{3,2,1,0:T(8,128)(2,1)}, u32[]{:S(2)}) %copy-start) | copy-done | bytes 2097176
  2.3 3.0 %collective-permute-start.1 = (bf16[3,10,16,512]{3,2,1,0:T(8,128)(2,1)S(1)}, bf16[3,10,16,512]{3,2,1,0:T(8,128)(2,1)S(1)}, u32[]{:S(2)}, u32[]{:S(2)}) collective-permute-start(bf16[3,10,16,512]{3,2,1,0:T(8,128)(2,1)S(1)} %get-tuple-element.47), channel_id=1, source_target_pairs={{0,2},{2,0},{4,6},{6,4},{8,10},{10,8},{12,14},{14,12},{1,3},{3,1},... | collective-permute-start | bytes 1474568 | tf_op jit(solution)/shard_map/ppermute | solution.py:570
  5.3 1.9 %fusion.3 = (bf16[4,32,1,512]{3,2,1,0:T(2,128)(2,1)S(1)}, bf16[4,32,1,512]{3,2,1,0:T(2,128)(2,1)S(1)}) fusion(bf16[4,32,16,512]{3,2,1,0:T(8,128)(2,1)} %video.9), kind=kLoop, calls=%fused_computation.12 | loop fusion | bytes 524288 | tf_op jit(solution)/shard_map/slice | solution.py:574
  7.6 2.0 %collective-permute-start.2 = (bf16[1,10,16,512]{3,2,1,0:T(8,128)(2,1)S(1)}, bf16[1,10,16,512]{3,2,1,0:T(8,128)(2,1)S(1)}, u32[]{:S(2)}, u32[]{:S(2)}) collective-permute-start(bf16[1,10,16,512]{3,2,1,0:T(8,128)(2,1)S(1)} %get-tuple-element.50), channel_id=1, source_target_pairs={{0,2},{2,0},{4,6},{6,4},{8,10},{10,8},{12,14},{14,12},{1,3},{3,1},... | collective-permute-start | bytes 491528 | tf_op jit(solution)/shard_map/ppermute | solution.py:570
  9.7 2.8 %broadcast_select_fusion.w_space = bf16[9,512,512]{2,1,0:T(8,128)(2,1)S(1)} fusion(bf16[9,512,512]{2,1,0:T(8,128)(2,1)} %param.17, pred[]{:T(512)S(6)} %ge.3), kind=kLoop, calls=%fused_computation | loop fusion | flops 2359296 | bytes 9437185 | tf_op jit(solution)/shard_map/jit(_where)/select_n | solution.py:555
  12.5 6.5 %collective-permute-done.4 = bf16[4,18,512]{2,1,0:T(8,128)(2,1)S(1)} collective-permute-done((bf16[4,18,512]{2,1,0:T(8,128)(2,1)S(1)}, bf16[4,18,512]{2,1,0:T(8,128)(2,1)S(1)}, u32[]{:S(2)}, u32[]{:S(2)}) %collective-permute-start.4) | collective-permute-done | bytes 73760 | tf_op jit(solution)/shard_map/ppermute | solution.py:585
  19.9 1.6 %collective-permute-start.7 = (bf16[3,11,16,512]{3,2,1,0:T(8,128)(2,1)S(1)}, bf16[3,11,16,512]{3,2,1,0:T(8,128)(2,1)S(1)}, u32[]{:S(2)}, u32[]{:S(2)}) collective-permute-start(bf16[3,11,16,512]{3,2,1,0:T(8,128)(2,1)S(1)} %join_last.2.last), channel_id=1, source_target_pairs={{0,4},{2,6},{4,8},{6,10},{8,12},{10,14},{12,0},{14,2},{1,5},{3,7},... | collective-permute-start | bytes 1622024 | tf_op jit(solution)/shard_map/ppermute | solution.py:570
  21.5 1.5 %collective-permute-done.2.others = bf16[1,10,16,512]{3,2,1,0:T(8,128)(2,1)S(1)} collective-permute-done((bf16[1,10,16,512]{3,2,1,0:T(8,128)(2,1)S(1)}, bf16[1,10,16,512]{3,2,1,0:T(8,128)(2,1)S(1)}, u32[]{:S(2)}, u32[]{:S(2)}) %collective-permute-start.2) | collective-permute-done | bytes 163872 | tf_op jit(solution)/shard_map/ppermute | solution.py:570
  23.7 5.0 %early.1 = (f32[176,512]{1,0:T(8,128)S(1)}, bf16[2,128,512]{2,1,0:T(8,128)(2,1)S(1)}, bf16[3,2,2,16,512]{4,3,2,1,0:T(8,128)(2,1)S(1)}) custom-call(s32[3]{0:T(128)S(1)} %pad_add_fusion.scalars, bf16[5,11,16,512]{3,2,1,0:T(8,128)(2,1)S(1)} %join_first.2.first, bf16[3,11,16,512]{3,2,1,0:T(8,128)(2,1)S(1)} %join_last.2.last, bf16[1536,512]{1,0:T(8,128)(2,1)S(1)} %bitcast.26, ...), custom_call_target="tpu_custom_call" | custom-call | flops 3607101440 | bytes 9312256 | tf_op jit(solution)/shard_map/early/pallas_call | solution.py:239
  28.7 1.9 %collective-permute-done.received = bf16[3,8,16,512]{3,2,1,0:T(8,128)(2,1)S(1)} collective-permute-done((bf16[3,8,16,512]{3,2,1,0:T(8,128)(2,1)S(1)}, bf16[3,8,16,512]{3,2,1,0:T(8,128)(2,1)S(1)}, u32[]{:S(2)}, u32[]{:S(2)}) %collective-permute-start) | collective-permute-done | bytes 393248 | tf_op jit(solution)/shard_map/ppermute | solution.py:570
  31.2 1.8 %collective-permute-start.5 = (bf16[3,9,16,512]{3,2,1,0:T(8,128)(2,1)S(1)}, bf16[3,9,16,512]{3,2,1,0:T(8,128)(2,1)S(1)}, u32[]{:S(2)}, u32[]{:S(2)}) collective-permute-start(bf16[3,9,16,512]{3,2,1,0:T(8,128)(2,1)S(1)} %join_last.3.last), channel_id=1, source_target_pairs={{0,4},{2,6},{4,8},{6,10},{8,12},{10,14},{12,0},{14,2},{1,5},{3,7},... | collective-permute-start | bytes 1327112 | tf_op jit(solution)/shard_map/ppermute | solution.py:570
  33.0 1.5 %collective-permute-start.6 = (bf16[1,8,16,512]{3,2,1,0:T(8,128)(2,1)S(1)}, bf16[1,8,16,512]{3,2,1,0:T(8,128)(2,1)S(1)}, u32[]{:S(2)}, u32[]{:S(2)}) collective-permute-start(bf16[1,8,16,512]{3,2,1,0:T(8,128)(2,1)S(1)} %get-tuple-element.55), channel_id=1, source_target_pairs={{0,2},{2,0},{4,6},{6,4},{8,10},{10,8},{12,14},{14,12},{1,3},{3,1},... | collective-permute-start | bytes 393224 | tf_op jit(solution)/shard_map/ppermute | solution.py:570
  34.6 2.3 %collective-permute-done.7.halo = bf16[3,11,16,512]{3,2,1,0:T(8,128)(2,1)S(1)} collective-permute-done((bf16[3,11,16,512]{3,2,1,0:T(8,128)(2,1)S(1)}, bf16[3,11,16,512]{3,2,1,0:T(8,128)(2,1)S(1)}, u32[]{:S(2)}, u32[]{:S(2)}) %collective-permute-start.7) | collective-permute-done | bytes 540704 | tf_op jit(solution)/shard_map/ppermute | solution.py:570
  36.9 3.9 %late.1 = (bf16[4,32,512]{2,1,0:T(8,128)(2,1)S(1)}, bf16[4,32,512]{2,1,0:T(8,128)(2,1)S(1)}, bf16[4,32,512]{2,1,0:T(8,128)(2,1)S(1)}, bf16[4,32,512]{2,1,0:T(8,128)(2,1)S(1)}, bf16[3,2,2,16,512]{4,3,2,1,0:T(8,128)(2,1)S(1)}) custom-call(s32[3]{0:T(128)S(1)} %pad_add_fusion.scalars, bf16[3,11,16,512]{3,2,1,0:T(8,128)(2,1)S(1)} %collective-permute-done.7.halo, ...), custom_call_target="tpu_custom_call" | custom-call | flops 2407530496 | bytes 9672704 | tf_op jit(solution)/shard_map/late/pallas_call | solution.py:397
  41.6 1.3 %collective-permute-start.12 = (bf16[4,32,512]{2,1,0:T(8,128)(2,1)S(1)}, bf16[4,32,512]{2,1,0:T(8,128)(2,1)S(1)}, u32[]{:S(2)}, u32[]{:S(2)}) collective-permute-start(bf16[4,32,512]{2,1,0:T(8,128)(2,1)S(1)} %get-tuple-element.67), channel_id=1, source_target_pairs={{0,12},{2,14},{4,8},{6,10},{8,4},{10,6},{12,0},{14,2},{1,13},{3,15... | collective-permute-start | bytes 393224 | tf_op jit(solution)/shard_map/ppermute | solution.py:570
  43.0 1.3 %collective-permute-start.13 = (bf16[4,32,512]{2,1,0:T(8,128)(2,1)S(1)}, bf16[4,32,512]{2,1,0:T(8,128)(2,1)S(1)}, u32[]{:S(2)}, u32[]{:S(2)}) collective-permute-start(bf16[4,32,512]{2,1,0:T(8,128)(2,1)S(1)} %get-tuple-element.68), channel_id=1, source_target_pairs={{0,4},{2,6},{4,0},{6,2},{8,12},{10,14},{12,8},{14,10},{1,5},{3,7},... | collective-permute-start | bytes 393224 | tf_op jit(solution)/shard_map/ppermute | solution.py:570
  44.9 1.5 %collective-permute-done.5.halo = bf16[3,9,16,512]{3,2,1,0:T(8,128)(2,1)S(1)} collective-permute-done((bf16[3,9,16,512]{3,2,1,0:T(8,128)(2,1)S(1)}, bf16[3,9,16,512]{3,2,1,0:T(8,128)(2,1)S(1)}, u32[]{:S(2)}, u32[]{:S(2)}) %collective-permute-start.5) | collective-permute-done | bytes 442400 | tf_op jit(solution)/shard_map/ppermute | solution.py:570
  46.5 7.3 %full.1 = (bf16[4,32,512]{2,1,0:T(8,128)(2,1)S(1)}, bf16[4,32,512]{2,1,0:T(8,128)(2,1)S(1)}, bf16[4,32,512]{2,1,0:T(8,128)(2,1)S(1)}, bf16[4,32,512]{2,1,0:T(8,128)(2,1)S(1)}) custom-call(s32[3]{0:T(128)S(1)} %pad_add_fusion.scalars, bf16[3,9,16,512]{3,2,1,0:T(8,128)(2,1)S(1)} %collective-permute-done.5.halo, bf16[5,9,16,512]{3,2,1,0:T(8,128)(2,1)S(1)} %join_first.3.first, ...), custom_call_target="tpu_custom_call" | custom-call | flops 5360320512 | bytes 9492480 | tf_op jit(solution)/shard_map/full/pallas_call | solution.py:326
  53.8 6.4 %collective-permute-start.8 = (bf16[4,32,512]{2,1,0:T(8,128)(2,1)S(1)}, bf16[4,32,512]{2,1,0:T(8,128)(2,1)S(1)}, u32[]{:S(2)}, u32[]{:S(2)}) collective-permute-start(bf16[4,32,512]{2,1,0:T(8,128)(2,1)S(1)} %get-tuple-element.62), channel_id=1, source_target_pairs={{0,8},{2,10},{4,12},{6,14},{8,0},{10,2},{12,4},{14,6},{1,9},{3,11}... | collective-permute-start | bytes 393224 | tf_op jit(solution)/shard_map/ppermute | solution.py:570
  60.9 2.8 %attend.2 = (bf16[2,32,512]{2,1,0:T(8,128)(2,1)S(1)}, bf16[2,32,512]{2,1,0:T(8,128)(2,1)S(1)}, bf16[2,32,512]{2,1,0:T(8,128)(2,1)S(1)}, bf16[2,32,512]{2,1,0:T(8...) custom-call(s32[3]{0:T(128)S(1)} %pad_add_fusion.scalars, ...), custom_call_target="tpu_custom_call" | custom-call | flops 1342177280 | bytes 2621440 | tf_op jit(solution)/shard_map/attend/pallas_call | solution.py:499
  63.7 3.8 %collective-permute-start.21 = (bf16[2,32,512]{2,1,0:T(8,128)(2,1)S(1)}, bf16[2,32,512]{2,1,0:T(8,128)(2,1)S(1)}, u32[]{:S(2)}, u32[]{:S(2)}) collective-permute-start(bf16[2,32,512]{2,1,0:T(8,128)(2,1)S(1)} %get-tuple-element.83), channel_id=1, source_target_pairs={{0,8},{2,10},{4,12},{6,14},{8,0},{10,2},{12,4},{14,6},{1,9},{3,11}... | collective-permute-start | bytes 196616 | tf_op jit(solution)/shard_map/ppermute | solution.py:570
  68.5 2.3 %collective-permute-start.23 = (bf16[2,32,512]{2,1,0:T(8,128)(2,1)S(1)}, bf16[2,32,512]{2,1,0:T(8,128)(2,1)S(1)}, u32[]{:S(2)}, u32[]{:S(2)}) collective-permute-start(bf16[2,32,512]{2,1,0:T(8,128)(2,1)S(1)} %get-tuple-element.85), channel_id=1, source_target_pairs={{0,12},{2,14},{4,8},{6,10},{8,4},{10,6},{12,0},{14,2},{1,13},{3,15... | collective-permute-start | bytes 196616 | tf_op jit(solution)/shard_map/ppermute | solution.py:570
  70.8 1.5 %collective-permute-start.24 = (bf16[2,32,512]{2,1,0:T(8,128)(2,1)S(1)}, bf16[2,32,512]{2,1,0:T(8,128)(2,1)S(1)}, u32[]{:S(2)}, u32[]{:S(2)}) collective-permute-start(bf16[2,32,512]{2,1,0:T(8,128)(2,1)S(1)} %get-tuple-element.86), channel_id=1, source_target_pairs={{0,14},{2,12},{4,10},{6,8},{8,6},{10,4},{12,2},{14,0},{1,15},{3,13... | collective-permute-start | bytes 196616 | tf_op jit(solution)/shard_map/ppermute | solution.py:570
  72.3 2.8 %attend.3 = (bf16[2,32,512]{2,1,0:T(8,128)(2,1)S(1)}, bf16[2,2,32,512]{3,2,1,0:T(8,128)(2,1)S(1)}, bf16[2,2,32,512]{3,2,1,0:T(8,128)(2,1)S(1)}, bf16[2,2,32,512]...) custom-call(s32[3]{0:T(128)S(1)} %pad_add_fusion.scalars, ...), custom_call_target="tpu_custom_call" | custom-call | flops 1342177280 | bytes 2621440 | tf_op jit(solution)/shard_map/attend/pallas_call | solution.py:499
  75.2 5.1 %collective-permute-start.14 = (bf16[2,32,512]{2,1,0:T(8,128)(2,1)S(1)}, bf16[2,32,512]{2,1,0:T(8,128)(2,1)S(1)}, u32[]{:S(2)}, u32[]{:S(2)}) collective-permute-start(bf16[2,32,512]{2,1,0:T(8,128)(2,1)S(1)} %get-tuple-element.75), channel_id=1, source_target_pairs={{0,8},{2,10},{4,12},{6,14},{8,0},{10,2},{12,4},{14,6},{1,9},{3,11}... | collective-permute-start | bytes 196616 | tf_op jit(solution)/shard_map/ppermute | solution.py:570
  80.3 1.5 %collective-permute-start.18 = (bf16[2,2,32,512]{3,2,1,0:T(8,128)(2,1)S(1)}, bf16[2,2,32,512]{3,2,1,0:T(8,128)(2,1)S(1)}, u32[]{:S(2)}, u32[]{:S(2)}) collective-permute-start(bf16[2,2,32,512]{3,2,1,0:T(8,128)(2,1)S(1)} %get-tuple-element.79), channel_id=1, source_target_pairs={{0,2},{2,0},{4,6},{6,4},{8,10},{10,8},{12,14},{14,12},{1,3},{3,1},... | collective-permute-start | bytes 393224 | tf_op jit(solution)/shard_map/ppermute | solution.py:570
  84.7 1.5 %collective-permute-start.16 = (bf16[2,32,512]{2,1,0:T(8,128)(2,1)S(1)}, bf16[2,32,512]{2,1,0:T(8,128)(2,1)S(1)}, u32[]{:S(2)}, u32[]{:S(2)}) collective-permute-start(bf16[2,32,512]{2,1,0:T(8,128)(2,1)S(1)} %get-tuple-element.77), channel_id=1, source_target_pairs={{0,12},{2,14},{4,8},{6,10},{8,4},{10,6},{12,0},{14,2},{1,13},{3,15... | collective-permute-start | bytes 196616 | tf_op jit(solution)/shard_map/ppermute | solution.py:570
  86.2 1.5 %collective-permute-done.15.refs_1_ = bf16[2,32,512]{2,1,0:T(8,128)(2,1)S(1)} collective-permute-done((bf16[2,32,512]{2,1,0:T(8,128)(2,1)S(1)}, bf16[2,32,512]{2,1,0:T(8,128)(2,1)S(1)}, u32[]{:S(2)}, u32[]{:S(2)}) %collective-permute-start.15) | collective-permute-done | bytes 65568 | tf_op jit(solution)/shard_map/ppermute | solution.py:570
  87.6 1.4 %collective-permute-start.17 = (bf16[2,32,512]{2,1,0:T(8,128)(2,1)S(1)}, bf16[2,32,512]{2,1,0:T(8,128)(2,1)S(1)}, u32[]{:S(2)}, u32[]{:S(2)}) collective-permute-start(bf16[2,32,512]{2,1,0:T(8,128)(2,1)S(1)} %get-tuple-element.78), channel_id=1, source_target_pairs={{0,14},{2,12},{4,10},{6,8},{8,6},{10,4},{12,2},{14,0},{1,15},{3,13... | collective-permute-start | bytes 196616 | tf_op jit(solution)/shard_map/ppermute | solution.py:570
  90.4 1.6 %collective-permute-done.16.refs_2_ = bf16[2,32,512]{2,1,0:T(8,128)(2,1)S(1)} collective-permute-done((bf16[2,32,512]{2,1,0:T(8,128)(2,1)S(1)}, bf16[2,32,512]{2,1,0:T(8,128)(2,1)S(1)}, u32[]{:S(2)}, u32[]{:S(2)}) %collective-permute-start.16) | collective-permute-done | bytes 65568 | tf_op jit(solution)/shard_map/ppermute | solution.py:570
  92.0 2.6 %collective-permute-done.17.refs_3_ = bf16[2,32,512]{2,1,0:T(8,128)(2,1)S(1)} collective-permute-done((bf16[2,32,512]{2,1,0:T(8,128)(2,1)S(1)}, bf16[2,32,512]{2,1,0:T(8,128)(2,1)S(1)}, u32[]{:S(2)}, u32[]{:S(2)}) %collective-permute-start.17) | collective-permute-done | bytes 65568 | tf_op jit(solution)/shard_map/ppermute | solution.py:570
  94.6 1.5 %collect.3 = bf16[2,16,32,512]{3,2,1,0:T(8,128)(2,1)} custom-call(s32[3]{0:T(128)S(1)} %pad_add_fusion.scalars, bf16[2,32,512]{2,1,0:T(8,128)(2,1)S(1)} %collective-permute-done.14.refs_0_, bf16[2,32,512]{2,1,0:T(8,128)(2,1)S(1)} %collective-permute-done.15.refs_1_, ...), custom_call_target="tpu_custom_call", output_to_operand_aliasing={{}: (9, {})} | custom-call | tf_op jit(solution)/shard_map/collect/pallas_call | solution.py:525
  (66 shorter events, 10.3 us)
Async XLA Ops:
  2.3 16.9 %collective-permute-start.1 = (bf16[3,10,16,512]{3,2,1,0:T(8,128)(2,1)S(1)}, bf16[3,10,16,512]{3,2,1,0:T(8,128)(2,1)S(1)}, u32[]{:S(2)}, u32[]{:S(2)}) collective-permute-start(bf16[3,10,16,512]{3,2,1,0:T(8,128)(2,1)S(1)} %get-tuple-element.47), channel_id=1, source_target_pairs={{0,2},{2,0},{4,6},{6,4},{8,10},{10,8},{12,14},{14,12},{1,3},{3,1},... | collective-permute-start | bytes 1474568 | tf_op jit(solution)/shard_map/ppermute | solution.py:570
  7.4 11.6 %collective-permute-start.4 = (bf16[4,18,512]{2,1,0:T(8,128)(2,1)S(1)}, bf16[4,18,512]{2,1,0:T(8,128)(2,1)S(1)}, u32[]{:S(2)}, u32[]{:S(2)}) collective-permute-start(bf16[4,18,512]{2,1,0:T(8,128)(2,1)S(1)} %get-tuple-element.89), channel_id=1, source_target_pairs={{0,3},{1,2},{2,1},{3,0},{4,7},{5,6},{6,5},{7,4},{8,11},{9,10},{10,... | collective-permute-start | bytes 221192 | tf_op jit(solution)/shard_map/ppermute | solution.py:585
  7.5 11.6 %collective-permute-start.3 = (bf16[4,18,512]{2,1,0:T(8,128)(2,1)S(1)}, bf16[4,18,512]{2,1,0:T(8,128)(2,1)S(1)}, u32[]{:S(2)}, u32[]{:S(2)}) collective-permute-start(bf16[4,18,512]{2,1,0:T(8,128)(2,1)S(1)} %get-tuple-element.90), channel_id=1, source_target_pairs={{0,1},{1,0},{2,3},{3,2},{4,5},{5,4},{6,7},{7,6},{8,9},{9,8},{10,11... | collective-permute-start | bytes 221192 | tf_op jit(solution)/shard_map/ppermute | solution.py:579
  7.6 15.4 %collective-permute-start.2 = (bf16[1,10,16,512]{3,2,1,0:T(8,128)(2,1)S(1)}, bf16[1,10,16,512]{3,2,1,0:T(8,128)(2,1)S(1)}, u32[]{:S(2)}, u32[]{:S(2)}) collective-permute-start(bf16[1,10,16,512]{3,2,1,0:T(8,128)(2,1)S(1)} %get-tuple-element.50), channel_id=1, source_target_pairs={{0,2},{2,0},{4,6},{6,4},{8,10},{10,8},{12,14},{14,12},{1,3},{3,1},... | collective-permute-start | bytes 491528 | tf_op jit(solution)/shard_map/ppermute | solution.py:570
  9.6 21.0 %collective-permute-start = (bf16[3,8,16,512]{3,2,1,0:T(8,128)(2,1)S(1)}, bf16[3,8,16,512]{3,2,1,0:T(8,128)(2,1)S(1)}, u32[]{:S(2)}, u32[]{:S(2)}) collective-permute-start(bf16[3,8,16,512]{3,2,1,0:T(8,128)(2,1)S(1)} %get-tuple-element.46), channel_id=1, source_target_pairs={{0,2},{2,0},{4,6},{6,4},{8,10},{10,8},{12,14},{14,12},{1,3},{3,1},... | collective-permute-start | bytes 1179656 | tf_op jit(solution)/shard_map/ppermute | solution.py:570
  12.5 11.1 %copy-start.2 = (bf16[3,512,512]{2,1,0:T(8,128)(2,1)S(1)}, bf16[3,512,512]{2,1,0:T(8,128)(2,1)}, u32[]{:S(2)}) copy-start(bf16[3,512,512]{2,1,0:T(8,128)(2,1)} %param.13) | copy-start | bytes 4718596
  12.5 11.1 %copy-start.3 = (bf16[3,512,512]{2,1,0:T(8,128)(2,1)S(1)}, bf16[3,512,512]{2,1,0:T(8,128)(2,1)}, u32[]{:S(2)}) copy-start(bf16[3,512,512]{2,1,0:T(8,128)(2,1)} %param.15) | copy-start | bytes 4718596
  19.9 17.0 %collective-permute-start.7 = (bf16[3,11,16,512]{3,2,1,0:T(8,128)(2,1)S(1)}, bf16[3,11,16,512]{3,2,1,0:T(8,128)(2,1)S(1)}, u32[]{:S(2)}, u32[]{:S(2)}) collective-permute-start(bf16[3,11,16,512]{3,2,1,0:T(8,128)(2,1)S(1)} %join_last.2.last), channel_id=1, source_target_pairs={{0,4},{2,6},{4,8},{6,10},{8,12},{10,14},{12,0},{14,2},{1,5},{3,7},... | collective-permute-start | bytes 1622024 | tf_op jit(solution)/shard_map/ppermute | solution.py:570
  31.2 15.2 %collective-permute-start.5 = (bf16[3,9,16,512]{3,2,1,0:T(8,128)(2,1)S(1)}, bf16[3,9,16,512]{3,2,1,0:T(8,128)(2,1)S(1)}, u32[]{:S(2)}, u32[]{:S(2)}) collective-permute-start(bf16[3,9,16,512]{3,2,1,0:T(8,128)(2,1)S(1)} %join_last.3.last), channel_id=1, source_target_pairs={{0,4},{2,6},{4,8},{6,10},{8,12},{10,14},{12,0},{14,2},{1,5},{3,7},... | collective-permute-start | bytes 1327112 | tf_op jit(solution)/shard_map/ppermute | solution.py:570
  33.0 7.7 %collective-permute-start.6 = (bf16[1,8,16,512]{3,2,1,0:T(8,128)(2,1)S(1)}, bf16[1,8,16,512]{3,2,1,0:T(8,128)(2,1)S(1)}, u32[]{:S(2)}, u32[]{:S(2)}) collective-permute-start(bf16[1,8,16,512]{3,2,1,0:T(8,128)(2,1)S(1)} %get-tuple-element.55), channel_id=1, source_target_pairs={{0,2},{2,0},{4,6},{6,4},{8,10},{10,8},{12,14},{14,12},{1,3},{3,1},... | collective-permute-start | bytes 393224 | tf_op jit(solution)/shard_map/ppermute | solution.py:570
  40.8 19.4 %collective-permute-start.11 = (bf16[4,32,512]{2,1,0:T(8,128)(2,1)S(1)}, bf16[4,32,512]{2,1,0:T(8,128)(2,1)S(1)}, u32[]{:S(2)}, u32[]{:S(2)}) collective-permute-start(bf16[4,32,512]{2,1,0:T(8,128)(2,1)S(1)} %get-tuple-element.66), channel_id=1, source_target_pairs={{0,8},{2,10},{4,12},{6,14},{8,0},{10,2},{12,4},{14,6},{1,9},{3,11}... | collective-permute-start | bytes 393224 | tf_op jit(solution)/shard_map/ppermute | solution.py:570
  41.6 19.2 %collective-permute-start.12 = (bf16[4,32,512]{2,1,0:T(8,128)(2,1)S(1)}, bf16[4,32,512]{2,1,0:T(8,128)(2,1)S(1)}, u32[]{:S(2)}, u32[]{:S(2)}) collective-permute-start(bf16[4,32,512]{2,1,0:T(8,128)(2,1)S(1)} %get-tuple-element.67), channel_id=1, source_target_pairs={{0,12},{2,14},{4,8},{6,10},{8,4},{10,6},{12,0},{14,2},{1,13},{3,15... | collective-permute-start | bytes 393224 | tf_op jit(solution)/shard_map/ppermute | solution.py:570
  43.0 17.9 %collective-permute-start.13 = (bf16[4,32,512]{2,1,0:T(8,128)(2,1)S(1)}, bf16[4,32,512]{2,1,0:T(8,128)(2,1)S(1)}, u32[]{:S(2)}, u32[]{:S(2)}) collective-permute-start(bf16[4,32,512]{2,1,0:T(8,128)(2,1)S(1)} %get-tuple-element.68), channel_id=1, source_target_pairs={{0,4},{2,6},{4,0},{6,2},{8,12},{10,14},{12,8},{14,10},{1,5},{3,7},... | collective-permute-start | bytes 393224 | tf_op jit(solution)/shard_map/ppermute | solution.py:570
  46.4 14.4 %copy-start.7 = (bf16[512,512]{1,0:T(8,128)(2,1)S(1)}, bf16[512,512]{1,0:T(8,128)(2,1)}, u32[]{:S(2)}) copy-start(bf16[512,512]{1,0:T(8,128)(2,1)} %refs_5_.3) | copy-start | bytes 1572868
  46.4 14.4 %copy-start.8 = (bf16[512,512]{1,0:T(8,128)(2,1)S(1)}, bf16[512,512]{1,0:T(8,128)(2,1)}, u32[]{:S(2)}) copy-start(bf16[512,512]{1,0:T(8,128)(2,1)} %refs_6_.3) | copy-start | bytes 1572868
  46.4 14.4 %copy-start.9 = (bf16[512,512]{1,0:T(8,128)(2,1)S(1)}, bf16[512,512]{1,0:T(8,128)(2,1)}, u32[]{:S(2)}) copy-start(bf16[512,512]{1,0:T(8,128)(2,1)} %refs_7_.3) | copy-start | bytes 1572868
  46.4 14.5 %copy-start.10 = (bf16[512,512]{1,0:T(8,128)(2,1)S(1)}, bf16[512,512]{1,0:T(8,128)(2,1)}, u32[]{:S(2)}) copy-start(bf16[512,512]{1,0:T(8,128)(2,1)} %refs_8_.3) | copy-start | bytes 1572868
  46.4 14.5 %copy-start.11 = (f32[512]{0:T(512)S(1)}, f32[512]{0:T(512)}, u32[]{:S(2)}) copy-start(f32[512]{0:T(512)} %param.19) | copy-start | bytes 6148
  53.8 14.8 %collective-permute-start.8 = (bf16[4,32,512]{2,1,0:T(8,128)(2,1)S(1)}, bf16[4,32,512]{2,1,0:T(8,128)(2,1)S(1)}, u32[]{:S(2)}, u32[]{:S(2)}) collective-permute-start(bf16[4,32,512]{2,1,0:T(8,128)(2,1)S(1)} %get-tuple-element.62), channel_id=1, source_target_pairs={{0,8},{2,10},{4,12},{6,14},{8,0},{10,2},{12,4},{14,6},{1,9},{3,11}... | collective-permute-start | bytes 393224 | tf_op jit(solution)/shard_map/ppermute | solution.py:570
  60.2 10.6 %collective-permute-start.9 = (bf16[4,32,512]{2,1,0:T(8,128)(2,1)S(1)}, bf16[4,32,512]{2,1,0:T(8,128)(2,1)S(1)}, u32[]{:S(2)}, u32[]{:S(2)}) collective-permute-start(bf16[4,32,512]{2,1,0:T(8,128)(2,1)S(1)} %get-tuple-element.63), channel_id=1, source_target_pairs={{0,12},{2,14},{4,8},{6,10},{8,4},{10,6},{12,0},{14,2},{1,13},{3,15... | collective-permute-start | bytes 393224 | tf_op jit(solution)/shard_map/ppermute | solution.py:570
  60.2 12.1 %collective-permute-start.10 = (bf16[4,32,512]{2,1,0:T(8,128)(2,1)S(1)}, bf16[4,32,512]{2,1,0:T(8,128)(2,1)S(1)}, u32[]{:S(2)}, u32[]{:S(2)}) collective-permute-start(bf16[4,32,512]{2,1,0:T(8,128)(2,1)S(1)} %get-tuple-element.64), channel_id=1, source_target_pairs={{0,4},{2,6},{4,0},{6,2},{8,12},{10,14},{12,8},{14,10},{1,5},{3,7},... | collective-permute-start | bytes 393224 | tf_op jit(solution)/shard_map/ppermute | solution.py:570
  63.7 16.5 %collective-permute-start.21 = (bf16[2,32,512]{2,1,0:T(8,128)(2,1)S(1)}, bf16[2,32,512]{2,1,0:T(8,128)(2,1)S(1)}, u32[]{:S(2)}, u32[]{:S(2)}) collective-permute-start(bf16[2,32,512]{2,1,0:T(8,128)(2,1)S(1)} %get-tuple-element.83), channel_id=1, source_target_pairs={{0,8},{2,10},{4,12},{6,14},{8,0},{10,2},{12,4},{14,6},{1,9},{3,11}... | collective-permute-start | bytes 196616 | tf_op jit(solution)/shard_map/ppermute | solution.py:570
  67.5 12.7 %collective-permute-start.22 = (bf16[2,32,512]{2,1,0:T(8,128)(2,1)S(1)}, bf16[2,32,512]{2,1,0:T(8,128)(2,1)S(1)}, u32[]{:S(2)}, u32[]{:S(2)}) collective-permute-start(bf16[2,32,512]{2,1,0:T(8,128)(2,1)S(1)} %get-tuple-element.84), channel_id=1, source_target_pairs={{0,10},{2,8},{4,14},{6,12},{8,2},{10,0},{12,6},{14,4},{1,11},{3,9}... | collective-permute-start | bytes 196616 | tf_op jit(solution)/shard_map/ppermute | solution.py:570
  68.5 13.3 %collective-permute-start.23 = (bf16[2,32,512]{2,1,0:T(8,128)(2,1)S(1)}, bf16[2,32,512]{2,1,0:T(8,128)(2,1)S(1)}, u32[]{:S(2)}, u32[]{:S(2)}) collective-permute-start(bf16[2,32,512]{2,1,0:T(8,128)(2,1)S(1)} %get-tuple-element.85), channel_id=1, source_target_pairs={{0,12},{2,14},{4,8},{6,10},{8,4},{10,6},{12,0},{14,2},{1,13},{3,15... | collective-permute-start | bytes 196616 | tf_op jit(solution)/shard_map/ppermute | solution.py:570
  70.8 11.8 %collective-permute-start.24 = (bf16[2,32,512]{2,1,0:T(8,128)(2,1)S(1)}, bf16[2,32,512]{2,1,0:T(8,128)(2,1)S(1)}, u32[]{:S(2)}, u32[]{:S(2)}) collective-permute-start(bf16[2,32,512]{2,1,0:T(8,128)(2,1)S(1)} %get-tuple-element.86), channel_id=1, source_target_pairs={{0,14},{2,12},{4,10},{6,8},{8,6},{10,4},{12,2},{14,0},{1,15},{3,13... | collective-permute-start | bytes 196616 | tf_op jit(solution)/shard_map/ppermute | solution.py:570
  75.2 9.5 %collective-permute-start.14 = (bf16[2,32,512]{2,1,0:T(8,128)(2,1)S(1)}, bf16[2,32,512]{2,1,0:T(8,128)(2,1)S(1)}, u32[]{:S(2)}, u32[]{:S(2)}) collective-permute-start(bf16[2,32,512]{2,1,0:T(8,128)(2,1)S(1)} %get-tuple-element.75), channel_id=1, source_target_pairs={{0,8},{2,10},{4,12},{6,14},{8,0},{10,2},{12,4},{14,6},{1,9},{3,11}... | collective-permute-start | bytes 196616 | tf_op jit(solution)/shard_map/ppermute | solution.py:570
  80.3 7.4 %collective-permute-start.15 = (bf16[2,32,512]{2,1,0:T(8,128)(2,1)S(1)}, bf16[2,32,512]{2,1,0:T(8,128)(2,1)S(1)}, u32[]{:S(2)}, u32[]{:S(2)}) collective-permute-start(bf16[2,32,512]{2,1,0:T(8,128)(2,1)S(1)} %get-tuple-element.76), channel_id=1, source_target_pairs={{0,10},{2,8},{4,14},{6,12},{8,2},{10,0},{12,6},{14,4},{1,11},{3,9}... | collective-permute-start | bytes 196616 | tf_op jit(solution)/shard_map/ppermute | solution.py:570
  80.3 14.4 %collective-permute-start.18 = (bf16[2,2,32,512]{3,2,1,0:T(8,128)(2,1)S(1)}, bf16[2,2,32,512]{3,2,1,0:T(8,128)(2,1)S(1)}, u32[]{:S(2)}, u32[]{:S(2)}) collective-permute-start(bf16[2,2,32,512]{3,2,1,0:T(8,128)(2,1)S(1)} %get-tuple-element.79), channel_id=1, source_target_pairs={{0,2},{2,0},{4,6},{6,4},{8,10},{10,8},{12,14},{14,12},{1,3},{3,1},... | collective-permute-start | bytes 393224 | tf_op jit(solution)/shard_map/ppermute | solution.py:570
  81.8 12.8 %collective-permute-start.19 = (bf16[2,2,32,512]{3,2,1,0:T(8,128)(2,1)S(1)}, bf16[2,2,32,512]{3,2,1,0:T(8,128)(2,1)S(1)}, u32[]{:S(2)}, u32[]{:S(2)}) collective-permute-start(bf16[2,2,32,512]{3,2,1,0:T(8,128)(2,1)S(1)} %get-tuple-element.80), channel_id=1, source_target_pairs={{0,4},{2,6},{4,0},{6,2},{8,12},{10,14},{12,8},{14,10},{1,5},{3,7},... | collective-permute-start | bytes 393224 | tf_op jit(solution)/shard_map/ppermute | solution.py:570
  82.7 11.9 %collective-permute-start.20 = (bf16[2,2,32,512]{3,2,1,0:T(8,128)(2,1)S(1)}, bf16[2,2,32,512]{3,2,1,0:T(8,128)(2,1)S(1)}, u32[]{:S(2)}, u32[]{:S(2)}) collective-permute-start(bf16[2,2,32,512]{3,2,1,0:T(8,128)(2,1)S(1)} %get-tuple-element.81), channel_id=1, source_target_pairs={{0,6},{2,4},{4,2},{6,0},{8,14},{10,12},{12,10},{14,8},{1,7},{3,5},... | collective-permute-start | bytes 393224 | tf_op jit(solution)/shard_map/ppermute | solution.py:570
  84.7 7.3 %collective-permute-start.16 = (bf16[2,32,512]{2,1,0:T(8,128)(2,1)S(1)}, bf16[2,32,512]{2,1,0:T(8,128)(2,1)S(1)}, u32[]{:S(2)}, u32[]{:S(2)}) collective-permute-start(bf16[2,32,512]{2,1,0:T(8,128)(2,1)S(1)} %get-tuple-element.77), channel_id=1, source_target_pairs={{0,12},{2,14},{4,8},{6,10},{8,4},{10,6},{12,0},{14,2},{1,13},{3,15... | collective-permute-start | bytes 196616 | tf_op jit(solution)/shard_map/ppermute | solution.py:570
  87.6 7.0 %collective-permute-start.17 = (bf16[2,32,512]{2,1,0:T(8,128)(2,1)S(1)}, bf16[2,32,512]{2,1,0:T(8,128)(2,1)S(1)}, u32[]{:S(2)}, u32[]{:S(2)}) collective-permute-start(bf16[2,32,512]{2,1,0:T(8,128)(2,1)S(1)} %get-tuple-element.78), channel_id=1, source_target_pairs={{0,14},{2,12},{4,10},{6,8},{8,6},{10,4},{12,2},{14,0},{1,15},{3,13... | collective-permute-start | bytes 196616 | tf_op jit(solution)/shard_map/ppermute | solution.py:570
  (6 other events, 54.0 us)
